TPU v7x, 32 devices: a whole 2x2x4 slice. The times are simulated.
32 devices in a mesh: groups: 2 (over y), hid: 4 (over z), wid: 2 (over x), tok: 2 (over core).
Axes of the slice: x: 2, y: 2, z: 4, core: 2. Of those that a mesh axis runs over, the one named last changes fastest.
Arguments:
- acts: bfloat16 [768, 4096], P(('groups', 'tok'), ('wid', 'hid')), parts along dimension 0, may hold values from -6 to 6
- grad_out: bfloat16 [768, 4096], P(('groups', 'tok'), ('wid', 'hid')), parts along dimension 0, may hold values from -4 to 4
- w_gate: bfloat16 [4096, 14336], P('wid', ('hid', 'tok')), may hold values from -0.125 to 0.125
- w_up: bfloat16 [4096, 14336], P('wid', ('hid', 'tok')), may hold values from -0.09375 to 0.09375
- w_down: bfloat16 [14336, 4096], P(('hid', 'tok'), 'wid'), may hold values from -0.046875 to 0.046875
Outputs:
- input_grad: bfloat16 [768, 4096], P(('groups', 'tok'), ('wid', 'hid')), parts along dimension 0
- grad_gate: bfloat16 [8192, 14336], P(('groups', 'wid'), ('hid', 'tok')), parts along dimension 0
- grad_up: bfloat16 [8192, 14336], P(('groups', 'wid'), ('hid', 'tok')), parts along dimension 0
- grad_down: bfloat16 [28672, 4096], P(('groups', 'hid', 'tok'), 'wid'), parts along dimension 0
There are 2 independent parts, one for each index of `groups`. A program takes and returns all parts, laid end to end along the dimension named above; an argument that names none is the same for every part. Nothing has to cross between parts.
All inputs are finite; a program needn't handle non-finite values.
Results may differ from a plain program's by a relative error of at most 0.02.
Values may be sent and summed in bfloat16 or wider, within the bound.
No kernel may reach another device: no remote copies, remote signals or barrier semaphores. Data moves between devices by JAX's collectives and lax.ppermute only.
A program may use at most 256 MiB of HBM per device.

v0:
```python
import jax
import jax.numpy as jnp
from jax import lax
from jax.sharding import PartitionSpec as P


def swiglu_grads(gate, up, dhid):
    sig = jax.nn.sigmoid(gate)
    hidden = (gate * sig * up).astype(jnp.bfloat16)
    d_gate = (dhid * up * sig * (1.0 + gate * (1.0 - sig))).astype(jnp.bfloat16)
    d_up = (dhid * gate * sig).astype(jnp.bfloat16)
    return (hidden, d_gate, d_up)


def over_rows(left, right):
    return lax.dot_general(
        left, right, (((0,), (0,)), ((), ())), preferred_element_type=jnp.float32
    )


def over_cols(left, right):
    return lax.dot_general(
        left, right, (((1,), (1,)), ((), ())), preferred_element_type=jnp.float32
    )


def blockwise(left, right, count, height):
    total = jnp.zeros((left.shape[1], right.shape[1]), jnp.float32)
    for block in range(count):
        lower = block * height
        piece = over_rows(left[lower : lower + height], right[lower : lower + height])
        total = total + lax.optimization_barrier(piece.astype(jnp.bfloat16)).astype(jnp.float32)
    return total.astype(jnp.bfloat16)


def shards(acts, grad_out, w_gate, w_up, w_down):
    x_cols, dy_cols = (
        lax.all_gather(acts, "hid", axis=1, tiled=True),
        lax.all_gather(grad_out, "hid", axis=1, tiled=True),
    )
    x_rows, dy_rows = (
        lax.all_gather(x_cols, "tok", axis=0, tiled=True),
        lax.all_gather(dy_cols, "tok", axis=0, tiled=True),
    )
    gate_cols, up_cols, down_part = (w_gate, w_up, w_down)
    gate_part = jnp.dot(x_rows, gate_cols, preferred_element_type=jnp.float32)
    up_part = jnp.dot(x_rows, up_cols, preferred_element_type=jnp.float32)
    dhid_part = over_cols(dy_rows, down_part)
    gate, up, dhid = (
        lax.psum(gate_part.astype(jnp.bfloat16), "wid").astype(jnp.float32),
        lax.psum(up_part.astype(jnp.bfloat16), "wid").astype(jnp.float32),
        lax.psum(dhid_part.astype(jnp.bfloat16), "wid").astype(jnp.float32),
    )
    hidden, d_gate, d_up = swiglu_grads(gate, up, dhid)
    input_part = over_cols(d_gate, gate_cols) + over_cols(d_up, up_cols)
    input_part = lax.psum_scatter(
        input_part.astype(jnp.bfloat16), "tok", scatter_dimension=0, tiled=True
    ).astype(jnp.float32)
    input_part = input_part.astype(jnp.bfloat16)
    input_grad = (
        lax.psum_scatter(input_part, "hid", scatter_dimension=1, tiled=True)
        .astype(jnp.float32)
        .astype(jnp.bfloat16)
    )
    count = lax.axis_size("tok")
    height = x_cols.shape[0]
    grad_gate = blockwise(x_rows, d_gate, count, height)
    grad_up = blockwise(x_rows, d_up, count, height)
    grad_down = blockwise(hidden, dy_rows, count, height)
    return (input_grad, grad_gate, grad_up, grad_down)


def solution(mesh):
    placed = (
        P(("groups", "tok"), ("wid", "hid")),
        P(("groups", "tok"), ("wid", "hid")),
        P("wid", ("hid", "tok")),
        P("wid", ("hid", "tok")),
        P(("hid", "tok"), "wid"),
    )
    return jax.shard_map(
        shards,
        mesh=mesh,
        in_specs=placed,
        out_specs=(
            P(("groups", "tok"), ("wid", "hid")),
            P(("groups", "wid"), ("hid", "tok")),
            P(("groups", "wid"), ("hid", "tok")),
            P(("groups", "hid", "tok"), "wid"),
        ),
        check_vma=False,
    )
```

profile of v0, /device:TPU:0, one launch (start us, length us, event | category | flops | bytes accessed | tf_op | source)
XLA Modules:
  0.0 289.5 jit_solution(9746527330577285281)
XLA Ops:
  7.2 0.0 all-gather.5.cloned.1.call-start
  7.2 21.8 %all_gather.14 = bf16[192,2048]{1,0:T(8,128)(2,1)} all-gather(bf16[192,512]{1,0:T(8,128)(2,1)} %param.5), channel_id=1, replica_groups=mesh['groups'=2,'hid'=4,'wid'=2,'tok'=2] {'hid'}, dimensions={1}, use_global_device_ids=true | all-gather | bytes 983040 | tf_op jit(solution)/shard_map/all_gather | solution.py:38
  29.0 0.0 all-gather.5.cloned.1.call-update
  29.1 0.0 all-gather.3.cloned.1.call-start
  29.1 18.6 %all_gather.12 = bf16[192,2048]{1,0:T(8,128)(2,1)} all-gather(bf16[192,512]{1,0:T(8,128)(2,1)} %param.6), channel_id=1, replica_groups=mesh['groups'=2,'hid'=4,'wid'=2,'tok'=2] {'hid'}, dimensions={1}, use_global_device_ids=true | all-gather | bytes 983040 | tf_op jit(solution)/shard_map/all_gather | solution.py:39
  47.7 0.0 all-gather.3.cloned.1.call-update
  47.7 0.0 all-reduce.3.cloned.1.call-start
  47.8 0.0 all-gather.5.cloned.1.call-done
  47.8 0.0 copy-start.2
  47.8 7.8 %convolution_convert_fusion.6 = bf16[384,1792]{1,0:T(8,128)(2,1)} fusion(bf16[384,2048]{1,0:T(8,128)(2,1)} %all-gather.5.cloned.1.call-done, bf16[2048,1792]{1,0:T(8,128)(2,1)} %param.7), kind=kOutput, calls=%fused_computation.20 | convolution fusion | flops 2819260416 | bytes 10289152 | tf_op jit(solution)/shard_map/dot_general | solution.py:46
  55.6 0.0 copy-done.2
  55.6 7.4 %convolution_convert_fusion.7 = bf16[384,1792]{1,0:T(8,128)(2,1)} fusion(bf16[384,2048]{1,0:T(8,128)(2,1)S(1)} %copy-done.2, bf16[2048,1792]{1,0:T(8,128)(2,1)} %param.8), kind=kOutput, calls=%fused_computation.21 | convolution fusion | flops 2819260416 | bytes 10289152 | tf_op jit(solution)/shard_map/dot_general | solution.py:47
  63.0 7.7 %convolution_convert_fusion.8 = bf16[384,1792]{1,0:T(8,128)(2,1)} fusion(bf16[384,2048]{1,0:T(8,128)(2,1)} %all-gather.3.cloned.1.call-done, bf16[1792,2048]{1,0:T(8,128)(2,1)} %param.9), kind=kOutput, calls=%fused_computation.22 | convolution fusion | flops 2819260416 | bytes 10289152 | tf_op jit(solution)/shard_map/dot_general | solution.py:22
  70.7 0.0 all-reduce.3.cloned.1.call-update
  70.7 0.0 reduce-scatter.3.cloned.1.call-start
  70.7 107.5 %all-reduce.3.cloned.1.call-done = (bf16[384,1792]{1,0:T(8,128)(2,1)}, bf16[384,1792]{1,0:T(8,128)(2,1)}, bf16[384,1792]{1,0:T(8,128)(2,1)}) async-done(((bf16[384,1792]{1,0:T(8,128)(2,1)}, bf16[384,1792]{1,0:T(8,128)(2,1)}, bf16[384,1792]{1,0:T(8,128)(2,1)}), (bf16[384,1792]{1,0:T(8,128)(2,1)}, bf16[384,1792]{1,0:T(8,128)(2,1)}, bf16[384,1792]{1,0:T(8,128)(2,1)})) %all-reduce.3.cloned.1.call-update) | async-done | bytes 4128784 | tf_op jit(solution)/shard_map/psum | solution.py:51
  178.2 0.0 slice-start
  178.2 4.0 %fusion.7 = (bf16[384,1792]{1,0:T(8,128)(2,1)S(1)}, bf16[384,1792]{1,0:T(8,128)(2,1)S(1)}, bf16[384,1792]{1,0:T(8,128)(2,1)S(1)}) fusion(bf16[384,1792]{1,0:T(8,128)(2,1)} %get-tuple-element.8, bf16[384,1792]{1,0:T(8,128)(2,1)} %get-tuple-element.10, bf16[384,1792]{1,0:T(8,128)(2,1)} %get-tuple-element.9), kind=kLoop, calls=%fused_computation.26 | loop fusion | flops 13074432 | bytes 8257536 | tf_op jit(solution)/shard_map/convert_element_type | solution.py:9
  182.2 0.0 copy-start
  182.2 0.0 slice-start.1
  182.2 5.8 %fusion.26 = f32[384,2048]{1,0:T(8,128)S(1)} fusion(bf16[384,1792]{1,0:T(8,128)(2,1)S(1)} %get-tuple-element.12, bf16[2048,1792]{1,0:T(8,128)(2,1)} %param.7), kind=kOutput, calls=%fused_computation.45 | convolution fusion | flops 2818572288 | bytes 11862016 | tf_op jit(solution)/shard_map/dot_general | solution.py:22
  188.1 0.0 copy-done
  188.1 0.0 slice-done
  188.1 0.0 slice-done.1
  188.1 4.2 %add_convert_fusion.3 = bf16[384,2048]{1,0:T(8,128)(2,1)} fusion(f32[384,2048]{1,0:T(8,128)S(1)} %fusion.26, bf16[384,1792]{1,0:T(8,128)(2,1)S(1)} %get-tuple-element.13, bf16[2048,1792]{1,0:T(8,128)(2,1)S(1)} %bitcast.19), kind=kOutput, calls=%fused_computation.19 | convolution fusion | flops 2820145152 | bytes 13434880 | tf_op jit(solution)/shard_map/dot_general | solution.py:22
  192.3 0.0 reduce-scatter.3.cloned.1.call-update
  192.3 0.2 reduce-scatter.5.cloned.1.call-start
  192.6 0.0 copy-start.1
  192.6 0.0 copy-start.3
  192.6 6.7 %fusion.1 = bf16[2048,1792]{0,1:T(8,128)(2,1)} fusion(bf16[384,2048]{1,0:T(8,128)(2,1)} %all-gather.5.cloned.1.call-done, bf16[384,1792]{1,0:T(8,128)(2,1)} %copy-done), kind=kOutput, calls=%fused_computation.10 | convolution fusion | flops 1412956160 | bytes 8814592 | tf_op jit(solution)/shard_map/dot_general | solution.py:16
  199.2 0.0 copy-done.1
  199.2 0.0 copy-done.3
  199.2 5.2 %fusion = bf16[2048,1792]{0,1:T(8,128)(2,1)} fusion(bf16[384,2048]{1,0:T(8,128)(2,1)S(1)} %copy-done.3, bf16[384,1792]{1,0:T(8,128)(2,1)S(1)} %copy-done.1), kind=kOutput, calls=%fused_computation.9 | convolution fusion | flops 1412956160 | bytes 8814592 | tf_op jit(solution)/shard_map/dot_general | solution.py:16
  204.4 5.2 %fusion.3 = bf16[2048,1792]{0,1:T(8,128)(2,1)} fusion(bf16[384,2048]{1,0:T(8,128)(2,1)S(1)} %copy-done.3, bf16[384,1792]{1,0:T(8,128)(2,1)S(1)} %get-tuple-element.13), kind=kOutput, calls=%fused_computation.12 | convolution fusion | flops 1412956160 | bytes 8814592 | tf_op jit(solution)/shard_map/dot_general | solution.py:16
  209.6 0.0 copy-start.4
  209.6 5.1 %fusion.2 = bf16[2048,1792]{0,1:T(8,128)(2,1)} fusion(bf16[384,2048]{1,0:T(8,128)(2,1)S(1)} %copy-done.3, bf16[384,1792]{1,0:T(8,128)(2,1)S(1)} %get-tuple-element.13), kind=kOutput, calls=%fused_computation.11 | convolution fusion | flops 1412956160 | bytes 8814592 | tf_op jit(solution)/shard_map/dot_general | solution.py:16
  214.7 0.0 copy-done.4
  214.7 5.1 %convolution_convert_fusion = bf16[1792,2048]{1,0:T(8,128)(2,1)} fusion(bf16[384,2048]{1,0:T(8,128)(2,1)S(1)} %copy-done.4, bf16[384,1792]{1,0:T(8,128)(2,1)S(1)} %get-tuple-element.11), kind=kOutput, calls=%fused_computation.3 | convolution fusion | flops 1412956160 | bytes 8814592 | tf_op jit(solution)/shard_map/dot_general | solution.py:16
  219.8 12.8 %add_convert_fusion.2 = bf16[2048,1792]{0,1:T(8,128)(2,1)} fusion(bf16[2048,1792]{0,1:T(8,128)(2,1)} %fusion.1, bf16[2048,1792]{0,1:T(8,128)(2,1)} %fusion), kind=kLoop, calls=%fused_computation.2 | loop fusion | flops 14680064 | bytes 22020096 | tf_op jit(solution)/shard_map/convert_element_type | solution.py:33
  232.6 0.0 copy-start.5
  232.6 12.6 %add_convert_fusion.1 = bf16[2048,1792]{0,1:T(8,128)(2,1)} fusion(bf16[2048,1792]{0,1:T(8,128)(2,1)} %fusion.3, bf16[2048,1792]{0,1:T(8,128)(2,1)} %fusion.2), kind=kLoop, calls=%fused_computation.1 | loop fusion | flops 14680064 | bytes 22020096 | tf_op jit(solution)/shard_map/convert_element_type | solution.py:33
  245.2 0.0 reduce-scatter.3.cloned.1.call-done
  245.2 0.0 reduce-scatter.5.cloned.1.call-update
  245.3 0.0 copy-done.5
  245.3 5.1 %convolution_convert_fusion.1 = bf16[1792,2048]{1,0:T(8,128)(2,1)} fusion(bf16[384,2048]{1,0:T(8,128)(2,1)S(1)} %copy-done.5, bf16[384,1792]{1,0:T(8,128)(2,1)S(1)} %get-tuple-element.11), kind=kOutput, calls=%fused_computation.4 | convolution fusion | flops 1412956160 | bytes 8814592 | tf_op jit(solution)/shard_map/dot_general | solution.py:16
  250.4 10.0 %copy.9 = bf16[2048,1792]{1,0:T(8,128)(2,1)} copy(bf16[2048,1792]{0,1:T(8,128)(2,1)} %add_convert_fusion.2) | data formatting | bytes 14680064
  260.4 10.0 %copy.10 = bf16[2048,1792]{1,0:T(8,128)(2,1)} copy(bf16[2048,1792]{0,1:T(8,128)(2,1)} %add_convert_fusion.1) | data formatting | bytes 14680064
  270.4 12.6 %add_convert_fusion = bf16[1792,2048]{1,0:T(8,128)(2,1)} fusion(bf16[1792,2048]{1,0:T(8,128)(2,1)} %convolution_convert_fusion, bf16[1792,2048]{1,0:T(8,128)(2,1)} %convolution_convert_fusion.1), kind=kLoop, calls=%fused_computation | loop fusion | flops 14680064 | bytes 22020096 | tf_op jit(solution)/shard_map/convert_element_type | solution.py:33
  (3 shorter events, 0.0 us)
Async XLA Ops:
  7.2 40.6 %all-gather.5.cloned.1.call-start = ((), (), s32[]{:S(2)}) async-start(), calls=%async_computation.3 | async-start | bytes 2359296 | tf_op jit(solution)/shard_map/all_gather | solution.py:42
  29.1 33.9 %all-gather.3.cloned.1.call-start = ((), (), s32[]{:S(2)}) async-start(), calls=%async_computation.2 | async-start | bytes 2359296 | tf_op jit(solution)/shard_map/all_gather | solution.py:43
  47.7 130.5 %all-reduce.3.cloned.1.call-start = ((), (), s32[]{:S(2)}) async-start(), calls=%async_computation.6 | async-start | bytes 8257536 | tf_op jit(solution)/shard_map/psum | solution.py:51
  47.8 7.8 %copy-start.2 = (bf16[384,2048]{1,0:T(8,128)(2,1)S(1)}, bf16[384,2048]{1,0:T(8,128)(2,1)}, u32[]{:S(2)}) copy-start(bf16[384,2048]{1,0:T(8,128)(2,1)} %all-gather.5.cloned.1.call-done) | copy-start | bytes 4718596
  70.7 174.6 %reduce-scatter.3.cloned.1.call-start = ((), (), s32[]{:S(2)}) async-start(), calls=%async_computation.4 | async-start | bytes 2359296 | tf_op jit(solution)/shard_map/reduce_scatter | solution.py:56
  178.2 9.9 %slice-start = ((s8[7340032]{0:T(1024)(128)(4,1)}), s8[4194304]{0:T(1024)(128)(4,1)S(1)}, s32[]{:S(2)}) async-start(s8[7340032]{0:T(1024)(128)(4,1)} %bitcast.18), calls=%async_computation.7 | async-start | bytes 8388608
  182.2 5.9 %copy-start = (bf16[384,1792]{1,0:T(8,128)(2,1)}, bf16[384,1792]{1,0:T(8,128)(2,1)S(1)}, u32[]{:S(2)}) copy-start(bf16[384,1792]{1,0:T(8,128)(2,1)S(1)} %get-tuple-element.12) | copy-start | bytes 4128772
  182.2 5.9 %slice-start.1 = ((s8[7340032]{0:T(1024)(128)(4,1)}), s8[3145728]{0:T(1024)(128)(4,1)S(1)}, s32[]{:S(2)}) async-start(s8[7340032]{0:T(1024)(128)(4,1)} %bitcast.18), calls=%async_computation.8 | async-start | bytes 6291456
  192.3 90.7 %reduce-scatter.5.cloned.1.call-start = ((), (), s32[]{:S(2)}) async-start(), calls=%async_computation.5 | async-start | bytes 983040 | tf_op jit(solution)/shard_map/reduce_scatter | solution.py:61
  192.6 6.7 %copy-start.1 = (bf16[384,1792]{1,0:T(8,128)(2,1)S(1)}, bf16[384,1792]{1,0:T(8,128)(2,1)}, u32[]{:S(2)}) copy-start(bf16[384,1792]{1,0:T(8,128)(2,1)} %copy-done) | copy-start | bytes 4128772
  192.6 6.7 %copy-start.3 = (bf16[384,2048]{1,0:T(8,128)(2,1)S(1)}, bf16[384,2048]{1,0:T(8,128)(2,1)}, u32[]{:S(2)}) copy-start(bf16[384,2048]{1,0:T(8,128)(2,1)} %all-gather.5.cloned.1.call-done) | copy-start | bytes 4718596
  209.6 5.1 %copy-start.4 = (bf16[384,2048]{1,0:T(8,128)(2,1)S(1)}, bf16[384,2048]{1,0:T(8,128)(2,1)}, u32[]{:S(2)}) copy-start(bf16[384,2048]{1,0:T(8,128)(2,1)} %all-gather.3.cloned.1.call-done) | copy-start | bytes 4718596
  232.6 12.7 %copy-start.5 = (bf16[384,2048]{1,0:T(8,128)(2,1)S(1)}, bf16[384,2048]{1,0:T(8,128)(2,1)}, u32[]{:S(2)}) copy-start(bf16[384,2048]{1,0:T(8,128)(2,1)} %all-gather.3.cloned.1.call-done) | copy-start | bytes 4718596
Sparse Core Ops, SparseCore 0:
  29.2 9.5 all-gather.4
  47.9 9.7 all-gather.2
  70.8 107.3 all-reduce.2
  192.5 9.0 reduce-scatter.2
  245.4 23.3 reduce-scatter.4
where the time goes:
time: 290 us
  waiting for transfers between devices  108 us (37%)
  matrix products  65.1 us (22%)
  other arithmetic  42.1 us (15%)
  blocking collectives  40.4 us (14%)
  local copies, waits for them, and re-layouts  20 us (7%)
  between operations  13.9 us (5%)
    psum x1, waiting for transfers between devices, shards(): lax.psum(up_part.astype(jnp.bfloat16), 'wid').astype(jnp.float32)  107 us
    convert_element_type x3, other arithmetic, blockwise(): return total.astype(jnp.bfloat16)  38.1 us
    dot_general x6, matrix products, over_rows(): lax.dot_general(left, right, (((0,), (0,)), ((), ())), preferred_element_...  32.3 us
    all_gather x1, blocking collectives, shards(): lax.all_gather(acts, 'hid', axis=1, tiled=True)  21.8 us
    unnamed x18, local copies, waits for them, and re-layouts  20 us
    all_gather x1, blocking collectives, shards(): lax.all_gather(grad_out, 'hid', axis=1, tiled=True)  18.6 us
    dot_general x3, matrix products, over_cols(): lax.dot_general(left, right, (((1,), (1,)), ((), ())), preferred_element_...  17.7 us
    dot_general x1, matrix products, shards(): gate_part = jnp.dot(x_rows, gate_cols, preferred_element_type=jnp.float32)  7.75 us
  transfers between devices with their start and end apart: 5, of which 1 were waited for; matrix products, arithmetic and copies ran while one was open for 36% of the time, Pallas kernels for 0%

commit v1 on v0

v1 whole, which is shorter than its diff:
```python
import jax
import jax.numpy as jnp
from jax import lax
from jax.sharding import PartitionSpec as P

PIECES = (1, 2, 3)


def swiglu_grads(gate, up, dhid):
    sig = jax.nn.sigmoid(gate)
    hidden = (gate * sig * up).astype(jnp.bfloat16)
    d_gate = (dhid * up * sig * (1.0 + gate * (1.0 - sig))).astype(jnp.bfloat16)
    d_up = (dhid * gate * sig).astype(jnp.bfloat16)
    return hidden, d_gate, d_up


def dot(left, right, dims):
    return lax.dot_general(left, right, (dims, ((), ())), preferred_element_type=jnp.float32)


def shifted(value, axis, step):
    n = lax.axis_size(axis)
    return lax.ppermute(value, axis, [(i, (i + step) % n) for i in range(n)])


def gather_cols(value, axis):
    n = lax.axis_size(axis)
    if n > 4:
        return lax.all_gather(value, axis, axis=1, tiled=True)
    me = lax.axis_index(axis)
    width = value.shape[1]
    out = jnp.zeros((value.shape[0], n * width), value.dtype)
    for step in range(n):
        block = shifted(value, axis, step) if step else value
        out = lax.dynamic_update_slice(out, block, (0, lax.rem(me - step + n, n) * width))
    return out


def scatter_cols(value, axis):
    n = lax.axis_size(axis)
    if n > 4:
        return lax.psum_scatter(value, axis, scatter_dimension=1, tiled=True).astype(jnp.float32)
    me = lax.axis_index(axis)
    width = value.shape[1] // n
    total = None
    for step in range(n):
        block = lax.dynamic_slice(value, (0, lax.rem(me + step, n) * width), (value.shape[0], width))
        block = shifted(block, axis, step) if step else block
        block = block.astype(jnp.float32)
        total = block if total is None else total + block
    return total


def summed(value, axis):
    total = value.astype(jnp.float32)
    for step in range(1, lax.axis_size(axis)):
        total = total + shifted(value, axis, step).astype(jnp.float32)
    return total


def own_first(value, axis):
    return jnp.concatenate([value] + [shifted(value, axis, step) for step in range(1, lax.axis_size(axis))], axis=0)


def pieces(rows):
    unit = rows // sum(PIECES)
    bounds = [0]
    for part in PIECES:
        bounds.append(bounds[-1] + part * unit)
    return list(zip(bounds[:-1], bounds[1:]))


def shards(acts, grad_out, w_gate, w_up, w_down):
    ins, backs = [], []
    spans = pieces(acts.shape[0])
    for lower, upper in spans:
        x = own_first(gather_cols(acts[lower:upper], "hid"), "tok")
        dy = own_first(gather_cols(grad_out[lower:upper], "hid"), "tok")
        ins.append((x, dy))
    halves = []
    for x, dy in ins:
        gate = dot(x, w_gate, ((1,), (0,))).astype(jnp.bfloat16)
        up = dot(x, w_up, ((1,), (0,))).astype(jnp.bfloat16)
        dhid = dot(dy, w_down, ((1,), (1,))).astype(jnp.bfloat16)
        halves.append((gate, up, dhid))
    grads = []
    for (lower, upper), parts in zip(spans, halves):
        gate, up, dhid = [summed(part, "wid") for part in parts]
        hidden, d_gate, d_up = swiglu_grads(gate, up, dhid)
        grads.append((hidden, d_gate, d_up))
        back = dot(d_gate, w_gate, ((1,), (1,))) + dot(d_up, w_up, ((1,), (1,)))
        rows = upper - lower
        n = lax.axis_size("tok")
        back = back.astype(jnp.bfloat16)
        total = back[:rows].astype(jnp.float32)
        for step in range(1, n):
            block = back[step * rows : (step + 1) * rows]
            total = total + shifted(block, "tok", n - step).astype(jnp.float32)
        backs.append(scatter_cols(total.astype(jnp.bfloat16), "hid").astype(jnp.bfloat16))
    x_all = jnp.concatenate([x for x, _ in ins], axis=0)
    dy_all = jnp.concatenate([dy for _, dy in ins], axis=0)
    hidden, d_gate, d_up = [jnp.concatenate([g[i] for g in grads], axis=0) for i in range(3)]
    grad_gate = dot(x_all, d_gate, ((0,), (0,))).astype(jnp.bfloat16)
    grad_up = dot(x_all, d_up, ((0,), (0,))).astype(jnp.bfloat16)
    grad_down = dot(hidden, dy_all, ((0,), (0,))).astype(jnp.bfloat16)
    return jnp.concatenate(backs, axis=0), grad_gate, grad_up, grad_down


def solution(mesh):
    placed = (
        P(("groups", "tok"), ("wid", "hid")),
        P(("groups", "tok"), ("wid", "hid")),
        P("wid", ("hid", "tok")),
        P("wid", ("hid", "tok")),
        P(("hid", "tok"), "wid"),
    )
    return jax.shard_map(
        shards,
        mesh=mesh,
        in_specs=placed,
        out_specs=(
            P(("groups", "tok"), ("wid", "hid")),
            P(("groups", "wid"), ("hid", "tok")),
            P(("groups", "wid"), ("hid", "tok")),
            P(("groups", "hid", "tok"), "wid"),
        ),
        check_vma=False,
    )
```

time: 290 us -> 191 us (0.66)
  waiting for transfers between devices: 108 us -> 57.5 us
  starting transfers between devices: 0.39 us -> 48.7 us
  blocking collectives: 40.4 us -> 0 us
  other arithmetic: 42.1 us -> 4.28 us
  between operations: 13.9 us -> 1.3 us
  matrix products: 65.1 us -> 57.9 us
    psum x1 -> x0, waiting for transfers between devices: 107 us -> none  [shards(): lax.psum(up_part.astype(jnp.bfloat16), 'wid').astype(jnp.float32)]
    ppermute x0 -> x45, waiting for transfers between devices: none -> 57.5 us  [shifted(): return lax.ppermute(value, axis, [(i, (i + step) % n) for i in range(n)])]
    ppermute x0 -> x45, starting transfers between devices: none -> 48.7 us  [shifted(): return lax.ppermute(value, axis, [(i, (i + step) % n) for i in range(n)])]
    all_gather x2 -> x0, blocking collectives: 40.4 us -> none  [the longest x1 21.8 us: shards(): lax.all_gather(acts, 'hid', axis=1, tiled=True)]
    convert_element_type x3 -> x6, other arithmetic: 38.1 us -> 0.31 us  [the longest x3 0.2 us: shards(): total.astype(jnp.bfloat16)]
    unnamed x18 -> x48, local copies, waits for them, and re-layouts: 20 us -> 4.06 us
    slice x0 -> x9, local copies, waits for them, and re-layouts: none -> 8.22 us  [the longest x3 4.62 us: shards(): x = own_first(gather_cols(acts[lower:upper], 'hid'), 'tok')]
    dynamic_update_slice x0 -> x18, local copies, waits for them, and re-layouts: none -> 7.64 us  [gather_cols(): lax.dynamic_update_slice(out, block, (0, lax.rem(me - step + n, n) * width))]
  transfers between devices with their start and end apart: 5 -> 45, of which waited for: 1 -> 16; matrix products, arithmetic and copies ran while one was open for 36% -> 38% of each run, Pallas kernels for 0% -> 0%
where the time goes in v1:
time: 191 us
  matrix products  57.9 us (30%)
  waiting for transfers between devices  57.5 us (30%)
  starting transfers between devices  48.7 us (25%)
  local copies, waits for them, and re-layouts  20.9 us (11%)
  other arithmetic  4.28 us (2%)
    dot_general x18, matrix products, dot(): lax.dot_general(left, right, (dims, ((), ())), preferred_element_type=jnp...  57.9 us
    ppermute x45, waiting for transfers between devices, shifted(): return lax.ppermute(value, axis, [(i, (i + step) % n) for i in range(n)])  57.5 us
    ppermute x45, starting transfers between devices, shifted(): return lax.ppermute(value, axis, [(i, (i + step) % n) for i in range(n)])  48.7 us
    dynamic_update_slice x18, local copies, waits for them, and re-layouts, gather_cols(): lax.dynamic_update_slice(out, block, (0, lax.rem(me - step + n, n) * width))  7.64 us
    slice x3, local copies, waits for them, and re-layouts, shards(): x = own_first(gather_cols(acts[lower:upper], 'hid'), 'tok')  4.62 us
    unnamed x48, local copies, waits for them, and re-layouts  4.06 us
  transfers between devices with their start and end apart: 45, of which 16 were waited for; matrix products, arithmetic and copies ran while one was open for 38% of the time, Pallas kernels for 0%

profile of v1, /device:TPU:0, one launch (start us, length us, event | category | flops | bytes accessed | tf_op | source)
XLA Modules:
  0.0 190.6 jit_solution(16077892466703162738)
XLA Ops:
  0.7 1.4 fusion.39
  2.1 4.0 %collective-permute-start.6 = (bf16[32,512]{1,0:T(8,128)(2,1)}, bf16[32,512]{1,0:T(8,128)(2,1)}, u32[]{:S(2)}, u32[]{:S(2)}) collective-permute-start(bf16[32,512]{1,0:T(8,128)(2,1)} %get-tuple-element.19), channel_id=1, source_target_pairs={{0,8},{4,12},{8,0},{12,4},{1,9},{5,13},{9,1},{13,5},{2,10},{6,14},... | collective-permute-start | bytes 98312 | tf_op jit(solution)/shard_map/ppermute | solution.py:23
  6.1 1.6 collective-permute-start.5
  7.7 2.2 %collective-permute-start.7 = (bf16[32,512]{1,0:T(8,128)(2,1)}, bf16[32,512]{1,0:T(8,128)(2,1)}, u32[]{:S(2)}, u32[]{:S(2)}) collective-permute-start(bf16[32,512]{1,0:T(8,128)(2,1)} %get-tuple-element.19), channel_id=1, source_target_pairs={{0,12},{4,0},{8,4},{12,8},{1,13},{5,1},{9,5},{13,9},{2,14},{6,2},{... | collective-permute-start | bytes 98312 | tf_op jit(solution)/shard_map/ppermute | solution.py:23
  12.6 1.5 fusion.41
  14.2 1.7 fusion.43
  17.4 1.5 fusion.42
  18.9 3.3 %collective-permute-start.2 = (bf16[32,512]{1,0:T(8,128)(2,1)}, bf16[32,512]{1,0:T(8,128)(2,1)S(1)}, u32[]{:S(2)}, u32[]{:S(2)}) collective-permute-start(bf16[32,512]{1,0:T(8,128)(2,1)} %get-tuple-element.21), channel_id=1, source_target_pairs={{0,12},{4,0},{8,4},{12,8},{1,13},{5,1},{9,5},{13,9},{2,14},{6,2},{... | collective-permute-start | bytes 98312 | tf_op jit(solution)/shard_map/ppermute | solution.py:23
  28.3 3.2 %collective-permute-start.22 = (bf16[64,512]{1,0:T(8,128)(2,1)}, bf16[64,512]{1,0:T(8,128)(2,1)S(1)}, u32[]{:S(2)}, u32[]{:S(2)}) collective-permute-start(bf16[64,512]{1,0:T(8,128)(2,1)} %get-tuple-element.23), channel_id=1, source_target_pairs={{0,12},{4,0},{8,4},{12,8},{1,13},{5,1},{9,5},{13,9},{2,14},{6,2},{... | collective-permute-start | bytes 196616 | tf_op jit(solution)/shard_map/ppermute | solution.py:23
  35.0 2.7 %collective-permute-start.17 = (bf16[64,512]{1,0:T(8,128)(2,1)}, bf16[64,512]{1,0:T(8,128)(2,1)S(1)}, u32[]{:S(2)}, u32[]{:S(2)}) collective-permute-start(bf16[64,512]{1,0:T(8,128)(2,1)} %get-tuple-element.25), channel_id=1, source_target_pairs={{0,12},{4,0},{8,4},{12,8},{1,13},{5,1},{9,5},{13,9},{2,14},{6,2},{... | collective-permute-start | bytes 196616 | tf_op jit(solution)/shard_map/ppermute | solution.py:23
  40.8 3.8 %collective-permute-start.37 = (bf16[96,512]{1,0:T(8,128)(2,1)}, bf16[96,512]{1,0:T(8,128)(2,1)S(1)}, u32[]{:S(2)}, u32[]{:S(2)}) collective-permute-start(bf16[96,512]{1,0:T(8,128)(2,1)} %get-tuple-element.27), channel_id=1, source_target_pairs={{0,12},{4,0},{8,4},{12,8},{1,13},{5,1},{9,5},{13,9},{2,14},{6,2},{... | collective-permute-start | bytes 294920 | tf_op jit(solution)/shard_map/ppermute | solution.py:23
  45.3 2.1 %collective-permute-done.35 = bf16[96,512]{1,0:T(8,128)(2,1)S(1)} collective-permute-done((bf16[96,512]{1,0:T(8,128)(2,1)}, bf16[96,512]{1,0:T(8,128)(2,1)S(1)}, u32[]{:S(2)}, u32[]{:S(2)}) %collective-permute-start.35) | collective-permute-done | bytes 98336 | tf_op jit(solution)/shard_map/ppermute | solution.py:23
  47.4 1.5 collective-permute-start.32
  48.9 1.5 collective-permute-done.36
  51.6 3.7 %collective-permute-done.31 = bf16[96,512]{1,0:T(8,128)(2,1)S(1)} collective-permute-done((bf16[96,512]{1,0:T(8,128)(2,1)}, bf16[96,512]{1,0:T(8,128)(2,1)S(1)}, u32[]{:S(2)}, u32[]{:S(2)}) %collective-permute-start.31) | collective-permute-done | bytes 98336 | tf_op jit(solution)/shard_map/ppermute | solution.py:23
  56.6 5.6 %convolution_convert_fusion.11 = bf16[64,1792]{1,0:T(8,128)(2,1)S(1)} fusion(bf16[1792,2048]{1,0:T(8,128)(2,1)} %param.9, bf16[32,2048]{1,0:T(8,128)(2,1)S(1)} %collective-permute-done.3, bf16[32,2048]{1,0:T(8,128)(2,1)S(1)} %copy-done.5), kind=kOutput, calls=%fused_computation.16 | convolution fusion | flops 470401024 | bytes 7831552 | tf_op jit(solution)/shard_map/dot_general | solution.py:18
  62.2 1.6 collective-permute-start.4
  65.2 4.4 %convolution_convert_fusion.10 = bf16[64,1792]{1,0:T(8,128)(2,1)S(1)} fusion(bf16[2048,1792]{1,0:T(8,128)(2,1)} %param.8, bf16[32,2048]{1,0:T(8,128)(2,1)S(1)} %collective-permute-done.8, bf16[32,2048]{1,0:T(8,128)(2,1)S(1)} %constant_dynamic-update-slice_fusion.28), kind=kOutput, calls=%fused_computation.15 | convolution fusion | flops 470401024 | bytes 7831552 | tf_op jit(solution)/shard_map/dot_general | solution.py:18
  71.3 1.6 collective-permute-start.10
  72.9 2.9 %convolution_convert_fusion.6 = bf16[128,1792]{1,0:T(8,128)(2,1)S(1)} fusion(bf16[2048,1792]{1,0:T(8,128)(2,1)S(1)} %bitcast.25, bf16[64,2048]{1,0:T(8,128)(2,1)S(1)} %collective-permute-done.23, bf16[64,2048]{1,0:T(8,128)(2,1)} %constant_dynamic-update-slice_fusion.20), kind=kOutput, calls=%fused_computation.10 | convolution fusion | flops 940802048 | bytes 8323072 | tf_op jit(solution)/shard_map/dot_general | solution.py:18
  75.8 2.3 %convolution_convert_fusion.7 = bf16[128,1792]{1,0:T(8,128)(2,1)S(1)} fusion(bf16[2048,1792]{1,0:T(8,128)(2,1)S(1)} %bitcast.27, bf16[64,2048]{1,0:T(8,128)(2,1)S(1)} %collective-permute-done.23, bf16[64,2048]{1,0:T(8,128)(2,1)} %constant_dynamic-update-slice_fusion.20), kind=kOutput, calls=%fused_computation.11 | convolution fusion | flops 940802048 | bytes 8323072 | tf_op jit(solution)/shard_map/dot_general | solution.py:18
  78.1 2.6 %convolution_convert_fusion.8 = bf16[128,1792]{1,0:T(8,128)(2,1)S(1)} fusion(bf16[1792,2048]{1,0:T(8,128)(2,1)S(1)} %bitcast.29, bf16[64,2048]{1,0:T(8,128)(2,1)S(1)} %collective-permute-done.18, bf16[64,2048]{1,0:T(8,128)(2,1)S(1)} %constant_dynamic-update-slice_fusion.24), kind=kOutput, calls=%fused_computation.12 | convolution fusion | flops 940802048 | bytes 8323072 | tf_op jit(solution)/shard_map/dot_general | solution.py:18
  85.1 2.3 %fusion.45 = f32[64,2048]{1,0:T(8,128)S(1)} fusion(bf16[64,1792]{1,0:T(8,128)(2,1)S(1)} %get-tuple-element.11, bf16[2048,1792]{1,0:T(8,128)(2,1)S(1)} %bitcast.25), kind=kOutput, calls=%fused_computation.136 | convolution fusion | flops 469762048 | bytes 8093696 | tf_op jit(solution)/shard_map/dot_general | solution.py:18
  87.4 2.3 %fusion.2 = bf16[64,2048]{1,0:T(8,128)(2,1)S(1)} fusion(f32[64,2048]{1,0:T(8,128)S(1)} %fusion.45, bf16[64,1792]{1,0:T(8,128)(2,1)S(1)} %get-tuple-element.12, bf16[2048,1792]{1,0:T(8,128)(2,1)S(1)} %bitcast.27), kind=kOutput, calls=%fused_computation.17 | convolution fusion | flops 470024192 | bytes 8355840 | tf_op jit(solution)/shard_map/dot_general | solution.py:18
  89.9 2.8 %convolution_convert_fusion.5 = bf16[192,1792]{1,0:T(8,128)(2,1)S(1)} fusion(bf16[1792,2048]{1,0:T(8,128)(2,1)S(1)} %bitcast.29, bf16[96,2048]{1,0:T(8,128)(2,1)S(1)} %collective-permute-done.33, bf16[96,2048]{1,0:T(8,128)(2,1)S(1)} %constant_dynamic-update-slice_fusion.16), kind=kOutput, calls=%fused_computation.7 | convolution fusion | flops 1411203072 | bytes 8814592 | tf_op jit(solution)/shard_map/dot_general | solution.py:18
  93.9 1.6 convolution_convert_fusion.3
  95.6 1.6 convolution_convert_fusion.4
  98.1 7.0 %collective-permute-done.24 = bf16[128,1792]{1,0:T(8,128)(2,1)S(1)} collective-permute-done((bf16[128,1792]{1,0:T(8,128)(2,1)S(1)}, bf16[128,1792]{1,0:T(8,128)(2,1)S(1)}, u32[]{:S(2)}, u32[]{:S(2)}) %collective-permute-start.24) | collective-permute-done | bytes 458784 | tf_op jit(solution)/shard_map/ppermute | solution.py:23
  105.9 9.1 %collective-permute-done.25 = bf16[128,1792]{1,0:T(8,128)(2,1)} collective-permute-done((bf16[128,1792]{1,0:T(8,128)(2,1)S(1)}, bf16[128,1792]{1,0:T(8,128)(2,1)}, u32[]{:S(2)}, u32[]{:S(2)}) %collective-permute-start.25) | collective-permute-done | bytes 458784 | tf_op jit(solution)/shard_map/ppermute | solution.py:23
  115.1 1.8 multiply_convert_fusion.3
  116.8 2.5 %fusion.46 = f32[128,2048]{1,0:T(8,128)S(1)} fusion(bf16[128,1792]{1,0:T(8,128)(2,1)S(1)} %get-tuple-element.8, bf16[2048,1792]{1,0:T(8,128)(2,1)S(1)} %bitcast.25), kind=kOutput, calls=%fused_computation.137 | convolution fusion | flops 939524096 | bytes 8847360 | tf_op jit(solution)/shard_map/dot_general | solution.py:18
  119.3 2.5 %fusion.1 = bf16[128,2048]{1,0:T(8,128)(2,1)S(1)} fusion(f32[128,2048]{1,0:T(8,128)S(1)} %fusion.46, bf16[128,1792]{1,0:T(8,128)(2,1)S(1)} %get-tuple-element.9, bf16[2048,1792]{1,0:T(8,128)(2,1)S(1)} %bitcast.27), kind=kOutput, calls=%fused_computation.9 | convolution fusion | flops 940048384 | bytes 9371648 | tf_op jit(solution)/shard_map/dot_general | solution.py:18
  123.4 2.4 %collective-permute-start.14 = (bf16[32,512]{1,0:T(8,128)(2,1)S(1)}, bf16[32,512]{1,0:T(8,128)(2,1)S(1)}, u32[]{:S(2)}, u32[]{:S(2)}) collective-permute-start(bf16[32,512]{1,0:T(8,128)(2,1)S(1)} %get-tuple-element.32), channel_id=1, source_target_pairs={{0,12},{4,0},{8,4},{12,8},{1,13},{5,1},{9,5},{13,9},{2,14},{6,2},{... | collective-permute-start | bytes 98312 | tf_op jit(solution)/shard_map/ppermute | solution.py:23
  126.0 1.8 collective-permute-done.12
  129.3 4.0 %collective-permute-done.13 = bf16[32,512]{1,0:T(8,128)(2,1)S(1)} collective-permute-done((bf16[32,512]{1,0:T(8,128)(2,1)S(1)}, bf16[32,512]{1,0:T(8,128)(2,1)S(1)}, u32[]{:S(2)}, u32[]{:S(2)}) %collective-permute-start.13) | collective-permute-done | bytes 32800 | tf_op jit(solution)/shard_map/ppermute | solution.py:23
  133.6 2.0 %collective-permute-done.27 = bf16[64,512]{1,0:T(8,128)(2,1)S(1)} collective-permute-done((bf16[64,512]{1,0:T(8,128)(2,1)S(1)}, bf16[64,512]{1,0:T(8,128)(2,1)S(1)}, u32[]{:S(2)}, u32[]{:S(2)}) %collective-permute-start.27) | collective-permute-done | bytes 65568 | tf_op jit(solution)/shard_map/ppermute | solution.py:23
  135.6 2.5 %collective-permute-done.29 = bf16[64,512]{1,0:T(8,128)(2,1)S(1)} collective-permute-done((bf16[64,512]{1,0:T(8,128)(2,1)S(1)}, bf16[64,512]{1,0:T(8,128)(2,1)S(1)}, u32[]{:S(2)}, u32[]{:S(2)}) %collective-permute-start.29) | collective-permute-done | bytes 65568 | tf_op jit(solution)/shard_map/ppermute | solution.py:23
  138.1 2.6 %collective-permute-done.28 = bf16[64,512]{1,0:T(8,128)(2,1)S(1)} collective-permute-done((bf16[64,512]{1,0:T(8,128)(2,1)S(1)}, bf16[64,512]{1,0:T(8,128)(2,1)S(1)}, u32[]{:S(2)}, u32[]{:S(2)}) %collective-permute-start.28) | collective-permute-done | bytes 65568 | tf_op jit(solution)/shard_map/ppermute | solution.py:23
  140.8 3.6 %collective-permute-done.39 = bf16[192,1792]{1,0:T(8,128)(2,1)S(1)} collective-permute-done((bf16[192,1792]{1,0:T(8,128)(2,1)S(1)}, bf16[192,1792]{1,0:T(8,128)(2,1)S(1)}, u32[]{:S(2)}, u32[]{:S(2)}) %collective-permute-start.39) | collective-permute-done | bytes 688160 | tf_op jit(solution)/shard_map/ppermute | solution.py:23
  144.4 13.4 %collective-permute-done.40 = bf16[192,1792]{1,0:T(8,128)(2,1)S(1)} collective-permute-done((bf16[192,1792]{1,0:T(8,128)(2,1)S(1)}, bf16[192,1792]{1,0:T(8,128)(2,1)S(1)}, u32[]{:S(2)}, u32[]{:S(2)}) %collective-permute-start.40) | collective-permute-done | bytes 688160 | tf_op jit(solution)/shard_map/ppermute | solution.py:23
  159.0 2.5 %fusion.47 = f32[192,2048]{1,0:T(8,128)S(1)} fusion(bf16[192,1792]{1,0:T(8,128)(2,1)S(1)} %get-tuple-element.5, bf16[2048,1792]{1,0:T(8,128)(2,1)S(1)} %bitcast.25), kind=kOutput, calls=%fused_computation.138 | convolution fusion | flops 1409286144 | bytes 9601024 | tf_op jit(solution)/shard_map/dot_general | solution.py:18
  161.5 2.5 %fusion = bf16[192,2048]{1,0:T(8,128)(2,1)S(1)} fusion(f32[192,2048]{1,0:T(8,128)S(1)} %fusion.47, bf16[192,1792]{1,0:T(8,128)(2,1)S(1)} %get-tuple-element.6, bf16[2048,1792]{1,0:T(8,128)(2,1)S(1)} %bitcast.27), kind=kOutput, calls=%fused_computation.4 | convolution fusion | flops 1410072576 | bytes 10387456 | tf_op jit(solution)/shard_map/dot_general | solution.py:18
  164.2 6.1 %convolution_convert_fusion.1 = bf16[2048,1792]{1,0:T(8,128)(2,1)} fusion(bf16[384,2048]{1,0:T(8,128)(2,1)S(1)} %constant_dynamic-update-slice_fusion, bf16[192,1792]{1,0:T(8,128)(2,1)S(1)} %get-tuple-element.6, bf16[128,1792]{1,0:T(8,128)(2,1)S(1)} %get-tuple-element.9, bf16[64,1792]{1,0:T(8,128)(2,1)S(1)} %get-tuple-element.12), kind=kOutput, calls=%fused_computation.1 | convolution fusion | flops 2826371072 | bytes 10289152 | tf_op jit(solution)/shard_map/dot_general | solution.py:18
  170.3 6.1 %convolution_convert_fusion.2 = bf16[2048,1792]{1,0:T(8,128)(2,1)} fusion(bf16[384,2048]{1,0:T(8,128)(2,1)S(1)} %constant_dynamic-update-slice_fusion, bf16[192,1792]{1,0:T(8,128)(2,1)S(1)} %get-tuple-element.5, bf16[128,1792]{1,0:T(8,128)(2,1)S(1)} %get-tuple-element.8, bf16[64,1792]{1,0:T(8,128)(2,1)S(1)} %get-tuple-element.11), kind=kOutput, calls=%fused_computation.2 | convolution fusion | flops 2826371072 | bytes 10289152 | tf_op jit(solution)/shard_map/dot_general | solution.py:18
  176.5 1.5 collective-permute-start.42
  177.9 2.4 %collective-permute-start.44 = (bf16[96,512]{1,0:T(8,128)(2,1)S(1)}, bf16[96,512]{1,0:T(8,128)(2,1)S(1)}, u32[]{:S(2)}, u32[]{:S(2)}) collective-permute-start(bf16[96,512]{1,0:T(8,128)(2,1)S(1)} %get-tuple-element.14), channel_id=1, source_target_pairs={{0,12},{4,0},{8,4},{12,8},{1,13},{5,1},{9,5},{13,9},{2,14},{6,2},{... | collective-permute-start | bytes 294920 | tf_op jit(solution)/shard_map/ppermute | solution.py:23
  181.4 6.1 %convolution_convert_fusion = bf16[1792,2048]{1,0:T(8,128)(2,1)} fusion(bf16[384,2048]{1,0:T(8,128)(2,1)S(1)} %constant_dynamic-update-slice_fusion.6, bf16[192,1792]{1,0:T(8,128)(2,1)S(1)} %get-tuple-element.4, bf16[128,1792]{1,0:T(8,128)(2,1)S(1)} %get-tuple-element.7, bf16[64,1792]{1,0:T(8,128)(2,1)S(1)} %get-tuple-element.10), kind=kOutput, calls=%fused_computation | convolution fusion | flops 2826371072 | bytes 10289152 | tf_op jit(solution)/shard_map/dot_general | solution.py:18
  187.5 2.3 %collective-permute-done.43 = bf16[96,512]{1,0:T(8,128)(2,1)S(1)} collective-permute-done((bf16[96,512]{1,0:T(8,128)(2,1)S(1)}, bf16[96,512]{1,0:T(8,128)(2,1)S(1)}, u32[]{:S(2)}, u32[]{:S(2)}) %collective-permute-start.43) | collective-permute-done | bytes 98336 | tf_op jit(solution)/shard_map/ppermute | solution.py:23
  (159 shorter events, 37.4 us)
Async XLA Ops:
  2.1 30.2 %collective-permute-start.6 = (bf16[32,512]{1,0:T(8,128)(2,1)}, bf16[32,512]{1,0:T(8,128)(2,1)}, u32[]{:S(2)}, u32[]{:S(2)}) collective-permute-start(bf16[32,512]{1,0:T(8,128)(2,1)} %get-tuple-element.19), channel_id=1, source_target_pairs={{0,8},{4,12},{8,0},{12,4},{1,9},{5,13},{9,1},{13,5},{2,10},{6,14},... | collective-permute-start | bytes 98312 | tf_op jit(solution)/shard_map/ppermute | solution.py:23
  6.1 22.2 %collective-permute-start.5 = (bf16[32,512]{1,0:T(8,128)(2,1)}, bf16[32,512]{1,0:T(8,128)(2,1)}, u32[]{:S(2)}, u32[]{:S(2)}) collective-permute-start(bf16[32,512]{1,0:T(8,128)(2,1)} %get-tuple-element.19), channel_id=1, source_target_pairs={{0,4},{4,8},{8,12},{12,0},{1,5},{5,9},{9,13},{13,1},{2,6},{6,10},{... | collective-permute-start | bytes 98312 | tf_op jit(solution)/shard_map/ppermute | solution.py:23
  7.7 25.4 %collective-permute-start.7 = (bf16[32,512]{1,0:T(8,128)(2,1)}, bf16[32,512]{1,0:T(8,128)(2,1)}, u32[]{:S(2)}, u32[]{:S(2)}) collective-permute-start(bf16[32,512]{1,0:T(8,128)(2,1)} %get-tuple-element.19), channel_id=1, source_target_pairs={{0,12},{4,0},{8,4},{12,8},{1,13},{5,1},{9,5},{13,9},{2,14},{6,2},{... | collective-permute-start | bytes 98312 | tf_op jit(solution)/shard_map/ppermute | solution.py:23
  11.3 12.2 %collective-permute-start.1 = (bf16[32,512]{1,0:T(8,128)(2,1)}, bf16[32,512]{1,0:T(8,128)(2,1)}, u32[]{:S(2)}, u32[]{:S(2)}) collective-permute-start(bf16[32,512]{1,0:T(8,128)(2,1)} %get-tuple-element.21), channel_id=1, source_target_pairs={{0,8},{4,12},{8,0},{12,4},{1,9},{5,13},{9,1},{13,5},{2,10},{6,14},... | collective-permute-start | bytes 98312 | tf_op jit(solution)/shard_map/ppermute | solution.py:23
  11.3 7.5 %collective-permute-start = (bf16[32,512]{1,0:T(8,128)(2,1)}, bf16[32,512]{1,0:T(8,128)(2,1)}, u32[]{:S(2)}, u32[]{:S(2)}) collective-permute-start(bf16[32,512]{1,0:T(8,128)(2,1)} %get-tuple-element.21), channel_id=1, source_target_pairs={{0,4},{4,8},{8,12},{12,0},{1,5},{5,9},{9,13},{13,1},{2,6},{6,10},{... | collective-permute-start | bytes 98312 | tf_op jit(solution)/shard_map/ppermute | solution.py:23
  14.1 49.7 %slice-start = ((s8[7340032]{0:T(1024)(128)(4,1)}), s8[3145728]{0:T(1024)(128)(4,1)S(1)}, s32[]{:S(2)}) async-start(s8[7340032]{0:T(1024)(128)(4,1)} %bitcast.24), calls=%async_computation | async-start | bytes 6291456
  18.8 30.0 %copy-start.1 = (bf16[96,2048]{1,0:T(8,128)(2,1)S(1)}, bf16[96,2048]{1,0:T(8,128)(2,1)}, u32[]{:S(2)}) copy-start(bf16[96,2048]{1,0:T(8,128)(2,1)} %copy-done) | copy-start | bytes 1179652
  18.8 32.8 %copy-start.3 = (bf16[96,2048]{1,0:T(8,128)(2,1)S(1)}, bf16[96,2048]{1,0:T(8,128)(2,1)}, u32[]{:S(2)}) copy-start(bf16[96,2048]{1,0:T(8,128)(2,1)} %copy-done.2) | copy-start | bytes 1179652
  18.9 7.2 %collective-permute-start.2 = (bf16[32,512]{1,0:T(8,128)(2,1)}, bf16[32,512]{1,0:T(8,128)(2,1)S(1)}, u32[]{:S(2)}, u32[]{:S(2)}) collective-permute-start(bf16[32,512]{1,0:T(8,128)(2,1)} %get-tuple-element.21), channel_id=1, source_target_pairs={{0,12},{4,0},{8,4},{12,8},{1,13},{5,1},{9,5},{13,9},{2,14},{6,2},{... | collective-permute-start | bytes 98312 | tf_op jit(solution)/shard_map/ppermute | solution.py:23
  23.5 14.8 %collective-permute-start.21 = (bf16[64,512]{1,0:T(8,128)(2,1)}, bf16[64,512]{1,0:T(8,128)(2,1)S(1)}, u32[]{:S(2)}, u32[]{:S(2)}) collective-permute-start(bf16[64,512]{1,0:T(8,128)(2,1)} %get-tuple-element.23), channel_id=1, source_target_pairs={{0,8},{4,12},{8,0},{12,4},{1,9},{5,13},{9,1},{13,5},{2,10},{6,14},... | collective-permute-start | bytes 196616 | tf_op jit(solution)/shard_map/ppermute | solution.py:23
  26.0 9.0 %collective-permute-start.20 = (bf16[64,512]{1,0:T(8,128)(2,1)}, bf16[64,512]{1,0:T(8,128)(2,1)S(1)}, u32[]{:S(2)}, u32[]{:S(2)}) collective-permute-start(bf16[64,512]{1,0:T(8,128)(2,1)} %get-tuple-element.23), channel_id=1, source_target_pairs={{0,4},{4,8},{8,12},{12,0},{1,5},{5,9},{9,13},{13,1},{2,6},{6,10},{... | collective-permute-start | bytes 196616 | tf_op jit(solution)/shard_map/ppermute | solution.py:23
  28.3 11.8 %collective-permute-start.22 = (bf16[64,512]{1,0:T(8,128)(2,1)}, bf16[64,512]{1,0:T(8,128)(2,1)S(1)}, u32[]{:S(2)}, u32[]{:S(2)}) collective-permute-start(bf16[64,512]{1,0:T(8,128)(2,1)} %get-tuple-element.23), channel_id=1, source_target_pairs={{0,12},{4,0},{8,4},{12,8},{1,13},{5,1},{9,5},{13,9},{2,14},{6,2},{... | collective-permute-start | bytes 196616 | tf_op jit(solution)/shard_map/ppermute | solution.py:23
  32.3 12.3 %collective-permute-start.16 = (bf16[64,512]{1,0:T(8,128)(2,1)}, bf16[64,512]{1,0:T(8,128)(2,1)S(1)}, u32[]{:S(2)}, u32[]{:S(2)}) collective-permute-start(bf16[64,512]{1,0:T(8,128)(2,1)} %get-tuple-element.25), channel_id=1, source_target_pairs={{0,8},{4,12},{8,0},{12,4},{1,9},{5,13},{9,1},{13,5},{2,10},{6,14},... | collective-permute-start | bytes 196616 | tf_op jit(solution)/shard_map/ppermute | solution.py:23
  33.1 7.7 %collective-permute-start.15 = (bf16[64,512]{1,0:T(8,128)(2,1)}, bf16[64,512]{1,0:T(8,128)(2,1)S(1)}, u32[]{:S(2)}, u32[]{:S(2)}) collective-permute-start(bf16[64,512]{1,0:T(8,128)(2,1)} %get-tuple-element.25), channel_id=1, source_target_pairs={{0,4},{4,8},{8,12},{12,0},{1,5},{5,9},{9,13},{13,1},{2,6},{6,10},{... | collective-permute-start | bytes 196616 | tf_op jit(solution)/shard_map/ppermute | solution.py:23
  35.0 9.7 %collective-permute-start.17 = (bf16[64,512]{1,0:T(8,128)(2,1)}, bf16[64,512]{1,0:T(8,128)(2,1)S(1)}, u32[]{:S(2)}, u32[]{:S(2)}) collective-permute-start(bf16[64,512]{1,0:T(8,128)(2,1)} %get-tuple-element.25), channel_id=1, source_target_pairs={{0,12},{4,0},{8,4},{12,8},{1,13},{5,1},{9,5},{13,9},{2,14},{6,2},{... | collective-permute-start | bytes 196616 | tf_op jit(solution)/shard_map/ppermute | solution.py:23
  38.4 12.0 %collective-permute-start.36 = (bf16[96,512]{1,0:T(8,128)(2,1)}, bf16[96,512]{1,0:T(8,128)(2,1)S(1)}, u32[]{:S(2)}, u32[]{:S(2)}) collective-permute-start(bf16[96,512]{1,0:T(8,128)(2,1)} %get-tuple-element.27), channel_id=1, source_target_pairs={{0,8},{4,12},{8,0},{12,4},{1,9},{5,13},{9,1},{13,5},{2,10},{6,14},... | collective-permute-start | bytes 294920 | tf_op jit(solution)/shard_map/ppermute | solution.py:23
  40.1 7.3 %collective-permute-start.35 = (bf16[96,512]{1,0:T(8,128)(2,1)}, bf16[96,512]{1,0:T(8,128)(2,1)S(1)}, u32[]{:S(2)}, u32[]{:S(2)}) collective-permute-start(bf16[96,512]{1,0:T(8,128)(2,1)} %get-tuple-element.27), channel_id=1, source_target_pairs={{0,4},{4,8},{8,12},{12,0},{1,5},{5,9},{9,13},{13,1},{2,6},{6,10},{... | collective-permute-start | bytes 294920 | tf_op jit(solution)/shard_map/ppermute | solution.py:23
  40.8 15.1 %collective-permute-start.37 = (bf16[96,512]{1,0:T(8,128)(2,1)}, bf16[96,512]{1,0:T(8,128)(2,1)S(1)}, u32[]{:S(2)}, u32[]{:S(2)}) collective-permute-start(bf16[96,512]{1,0:T(8,128)(2,1)} %get-tuple-element.27), channel_id=1, source_target_pairs={{0,12},{4,0},{8,4},{12,8},{1,13},{5,1},{9,5},{13,9},{2,14},{6,2},{... | collective-permute-start | bytes 294920 | tf_op jit(solution)/shard_map/ppermute | solution.py:23
  44.6 10.7 %collective-permute-start.31 = (bf16[96,512]{1,0:T(8,128)(2,1)}, bf16[96,512]{1,0:T(8,128)(2,1)S(1)}, u32[]{:S(2)}, u32[]{:S(2)}) collective-permute-start(bf16[96,512]{1,0:T(8,128)(2,1)} %get-tuple-element.29), channel_id=1, source_target_pairs={{0,8},{4,12},{8,0},{12,4},{1,9},{5,13},{9,1},{13,5},{2,10},{6,14},... | collective-permute-start | bytes 294920 | tf_op jit(solution)/shard_map/ppermute | solution.py:23
  44.7 6.9 %collective-permute-start.30 = (bf16[96,512]{1,0:T(8,128)(2,1)}, bf16[96,512]{1,0:T(8,128)(2,1)S(1)}, u32[]{:S(2)}, u32[]{:S(2)}) collective-permute-start(bf16[96,512]{1,0:T(8,128)(2,1)} %get-tuple-element.29), channel_id=1, source_target_pairs={{0,4},{4,8},{8,12},{12,0},{1,5},{5,9},{9,13},{13,1},{2,6},{6,10},{... | collective-permute-start | bytes 294920 | tf_op jit(solution)/shard_map/ppermute | solution.py:23
  47.4 8.4 %collective-permute-start.32 = (bf16[96,512]{1,0:T(8,128)(2,1)}, bf16[96,512]{1,0:T(8,128)(2,1)S(1)}, u32[]{:S(2)}, u32[]{:S(2)}) collective-permute-start(bf16[96,512]{1,0:T(8,128)(2,1)} %get-tuple-element.29), channel_id=1, source_target_pairs={{0,12},{4,0},{8,4},{12,8},{1,13},{5,1},{9,5},{13,9},{2,14},{6,2},{... | collective-permute-start | bytes 294920 | tf_op jit(solution)/shard_map/ppermute | solution.py:23
  50.4 6.1 %collective-permute-start.3 = (bf16[32,2048]{1,0:T(8,128)(2,1)}, bf16[32,2048]{1,0:T(8,128)(2,1)S(1)}, u32[]{:S(2)}, u32[]{:S(2)}) collective-permute-start(bf16[32,2048]{1,0:T(8,128)(2,1)} %constant_dynamic-update-slice_fusion.32), channel_id=1, source_target_pairs={{0,1},{1,0},{2,3},{3,2},{4,5},{5,4},{6,7},{7,6},{8,9},{9,8},{10,11... | collective-permute-start | bytes 393224 | tf_op jit(solution)/shard_map/ppermute | solution.py:23
  51.6 10.6 %collective-permute-start.8 = (bf16[32,2048]{1,0:T(8,128)(2,1)S(1)}, bf16[32,2048]{1,0:T(8,128)(2,1)S(1)}, u32[]{:S(2)}, u32[]{:S(2)}) collective-permute-start(bf16[32,2048]{1,0:T(8,128)(2,1)S(1)} %constant_dynamic-update-slice_fusion.28), channel_id=1, source_target_pairs={{0,1},{1,0},{2,3},{3,2},{4,5},{5,4},{6,7},{7,6},{8,9},{9,8},{10,11... | collective-permute-start | bytes 393224 | tf_op jit(solution)/shard_map/ppermute | solution.py:23
  55.3 15.3 %collective-permute-start.18 = (bf16[64,2048]{1,0:T(8,128)(2,1)S(1)}, bf16[64,2048]{1,0:T(8,128)(2,1)S(1)}, u32[]{:S(2)}, u32[]{:S(2)}) collective-permute-start(bf16[64,2048]{1,0:T(8,128)(2,1)S(1)} %constant_dynamic-update-slice_fusion.24), channel_id=1, source_target_pairs={{0,1},{1,0},{2,3},{3,2},{4,5},{5,4},{6,7},{7,6},{8,9},{9,8},{10,11... | collective-permute-start | bytes 786440 | tf_op jit(solution)/shard_map/ppermute | solution.py:23
  55.8 15.5 %collective-permute-start.23 = (bf16[64,2048]{1,0:T(8,128)(2,1)}, bf16[64,2048]{1,0:T(8,128)(2,1)S(1)}, u32[]{:S(2)}, u32[]{:S(2)}) collective-permute-start(bf16[64,2048]{1,0:T(8,128)(2,1)} %constant_dynamic-update-slice_fusion.20), channel_id=1, source_target_pairs={{0,1},{1,0},{2,3},{3,2},{4,5},{5,4},{6,7},{7,6},{8,9},{9,8},{10,11... | collective-permute-start | bytes 786440 | tf_op jit(solution)/shard_map/ppermute | solution.py:23
  55.9 33.9 %collective-permute-start.33 = (bf16[96,2048]{1,0:T(8,128)(2,1)S(1)}, bf16[96,2048]{1,0:T(8,128)(2,1)S(1)}, u32[]{:S(2)}, u32[]{:S(2)}) collective-permute-start(bf16[96,2048]{1,0:T(8,128)(2,1)S(1)} %constant_dynamic-update-slice_fusion.16), channel_id=1, source_target_pairs={{0,1},{1,0},{2,3},{3,2},{4,5},{5,4},{6,7},{7,6},{8,9},{9,8},{10,11... | collective-permute-start | bytes 1179656 | tf_op jit(solution)/shard_map/ppermute | solution.py:23
  56.4 36.2 %collective-permute-start.38 = (bf16[96,2048]{1,0:T(8,128)(2,1)S(1)}, bf16[96,2048]{1,0:T(8,128)(2,1)S(1)}, u32[]{:S(2)}, u32[]{:S(2)}) collective-permute-start(bf16[96,2048]{1,0:T(8,128)(2,1)S(1)} %constant_dynamic-update-slice_fusion.12), channel_id=1, source_target_pairs={{0,1},{1,0},{2,3},{3,2},{4,5},{5,4},{6,7},{7,6},{8,9},{9,8},{10,11... | collective-permute-start | bytes 1179656 | tf_op jit(solution)/shard_map/ppermute | solution.py:23
  62.2 19.6 %collective-permute-start.4 = (bf16[64,1792]{1,0:T(8,128)(2,1)S(1)}, bf16[64,1792]{1,0:T(8,128)(2,1)S(1)}, u32[]{:S(2)}, u32[]{:S(2)}) collective-permute-start(bf16[64,1792]{1,0:T(8,128)(2,1)S(1)} %convolution_convert_fusion.11), channel_id=1, source_target_pairs={{0,2},{2,0},{1,3},{3,1},{4,6},{6,4},{5,7},{7,5},{8,10},{10,8},{9,1... | collective-permute-start | bytes 688136 | tf_op jit(solution)/shard_map/ppermute | solution.py:23
  70.6 12.1 %collective-permute-start.9 = (bf16[64,1792]{1,0:T(8,128)(2,1)S(1)}, bf16[64,1792]{1,0:T(8,128)(2,1)S(1)}, u32[]{:S(2)}, u32[]{:S(2)}) collective-permute-start(bf16[64,1792]{1,0:T(8,128)(2,1)S(1)} %convolution_convert_fusion.10), channel_id=1, source_target_pairs={{0,2},{2,0},{1,3},{3,1},{4,6},{6,4},{5,7},{7,5},{8,10},{10,8},{9,1... | collective-permute-start | bytes 688136 | tf_op jit(solution)/shard_map/ppermute | solution.py:23
  71.3 12.6 %collective-permute-start.10 = (bf16[64,1792]{1,0:T(8,128)(2,1)S(1)}, bf16[64,1792]{1,0:T(8,128)(2,1)S(1)}, u32[]{:S(2)}, u32[]{:S(2)}) collective-permute-start(bf16[64,1792]{1,0:T(8,128)(2,1)S(1)} %convolution_convert_fusion.9), channel_id=1, source_target_pairs={{0,2},{2,0},{1,3},{3,1},{4,6},{6,4},{5,7},{7,5},{8,10},{10,8},{9,1... | collective-permute-start | bytes 688136 | tf_op jit(solution)/shard_map/ppermute | solution.py:23
  81.9 15.4 %collective-permute-start.19 = (bf16[128,1792]{1,0:T(8,128)(2,1)S(1)}, bf16[128,1792]{1,0:T(8,128)(2,1)S(1)}, u32[]{:S(2)}, u32[]{:S(2)}) collective-permute-start(bf16[128,1792]{1,0:T(8,128)(2,1)S(1)} %convolution_convert_fusion.8), channel_id=1, source_target_pairs={{0,2},{2,0},{1,3},{3,1},{4,6},{6,4},{5,7},{7,5},{8,10},{10,8},{9,1... | collective-permute-start | bytes 1376264 | tf_op jit(solution)/shard_map/ppermute | solution.py:23
  82.7 22.4 %collective-permute-start.24 = (bf16[128,1792]{1,0:T(8,128)(2,1)S(1)}, bf16[128,1792]{1,0:T(8,128)(2,1)S(1)}, u32[]{:S(2)}, u32[]{:S(2)}) collective-permute-start(bf16[128,1792]{1,0:T(8,128)(2,1)S(1)} %convolution_convert_fusion.7), channel_id=1, source_target_pairs={{0,2},{2,0},{1,3},{3,1},{4,6},{6,4},{5,7},{7,5},{8,10},{10,8},{9,1... | collective-permute-start | bytes 1376264 | tf_op jit(solution)/shard_map/ppermute | solution.py:23
  83.9 31.2 %collective-permute-start.25 = (bf16[128,1792]{1,0:T(8,128)(2,1)S(1)}, bf16[128,1792]{1,0:T(8,128)(2,1)}, u32[]{:S(2)}, u32[]{:S(2)}) collective-permute-start(bf16[128,1792]{1,0:T(8,128)(2,1)S(1)} %convolution_convert_fusion.6), channel_id=1, source_target_pairs={{0,2},{2,0},{1,3},{3,1},{4,6},{6,4},{5,7},{7,5},{8,10},{10,8},{9,1... | collective-permute-start | bytes 1376264 | tf_op jit(solution)/shard_map/ppermute | solution.py:23
  89.8 32.1 %collective-permute-start.11 = (bf16[32,2048]{1,0:T(8,128)(2,1)S(1)}, bf16[32,2048]{1,0:T(8,128)(2,1)S(1)}, u32[]{:S(2)}, u32[]{:S(2)}) collective-permute-start(bf16[32,2048]{1,0:T(8,128)(2,1)S(1)} %slice.49), channel_id=1, source_target_pairs={{0,1},{1,0},{2,3},{3,2},{4,5},{5,4},{6,7},{7,6},{8,9},{9,8},{10,11... | collective-permute-start | bytes 393224 | tf_op jit(solution)/shard_map/ppermute | solution.py:23
  92.7 48.1 %collective-permute-start.34 = (bf16[192,1792]{1,0:T(8,128)(2,1)S(1)}, bf16[192,1792]{1,0:T(8,128)(2,1)S(1)}, u32[]{:S(2)}, u32[]{:S(2)}) collective-permute-start(bf16[192,1792]{1,0:T(8,128)(2,1)S(1)} %convolution_convert_fusion.5), channel_id=1, source_target_pairs={{0,2},{2,0},{1,3},{3,1},{4,6},{6,4},{5,7},{7,5},{8,10},{10,8},{9,1... | collective-permute-start | bytes 2064392 | tf_op jit(solution)/shard_map/ppermute | solution.py:23
  97.2 47.2 %collective-permute-start.39 = (bf16[192,1792]{1,0:T(8,128)(2,1)S(1)}, bf16[192,1792]{1,0:T(8,128)(2,1)S(1)}, u32[]{:S(2)}, u32[]{:S(2)}) collective-permute-start(bf16[192,1792]{1,0:T(8,128)(2,1)S(1)} %convolution_convert_fusion.4), channel_id=1, source_target_pairs={{0,2},{2,0},{1,3},{3,1},{4,6},{6,4},{5,7},{7,5},{8,10},{10,8},{9,1... | collective-permute-start | bytes 2064392 | tf_op jit(solution)/shard_map/ppermute | solution.py:23
  105.1 52.8 %collective-permute-start.40 = (bf16[192,1792]{1,0:T(8,128)(2,1)S(1)}, bf16[192,1792]{1,0:T(8,128)(2,1)S(1)}, u32[]{:S(2)}, u32[]{:S(2)}) collective-permute-start(bf16[192,1792]{1,0:T(8,128)(2,1)S(1)} %convolution_convert_fusion.3), channel_id=1, source_target_pairs={{0,2},{2,0},{1,3},{3,1},{4,6},{6,4},{5,7},{7,5},{8,10},{10,8},{9,1... | collective-permute-start | bytes 2064392 | tf_op jit(solution)/shard_map/ppermute | solution.py:23
  121.8 1.6 collective-permute-start.26
  122.0 5.8 %collective-permute-start.12 = (bf16[32,512]{1,0:T(8,128)(2,1)S(1)}, bf16[32,512]{1,0:T(8,128)(2,1)S(1)}, u32[]{:S(2)}, u32[]{:S(2)}) collective-permute-start(bf16[32,512]{1,0:T(8,128)(2,1)S(1)} %get-tuple-element.31), channel_id=1, source_target_pairs={{0,4},{4,8},{8,12},{12,0},{1,5},{5,9},{9,13},{13,1},{2,6},{6,10},{... | collective-permute-start | bytes 98312 | tf_op jit(solution)/shard_map/ppermute | solution.py:23
  123.4 5.3 %collective-permute-start.14 = (bf16[32,512]{1,0:T(8,128)(2,1)S(1)}, bf16[32,512]{1,0:T(8,128)(2,1)S(1)}, u32[]{:S(2)}, u32[]{:S(2)}) collective-permute-start(bf16[32,512]{1,0:T(8,128)(2,1)S(1)} %get-tuple-element.32), channel_id=1, source_target_pairs={{0,12},{4,0},{8,4},{12,8},{1,13},{5,1},{9,5},{13,9},{2,14},{6,2},{... | collective-permute-start | bytes 98312 | tf_op jit(solution)/shard_map/ppermute | solution.py:23
  127.8 5.6 %collective-permute-start.13 = (bf16[32,512]{1,0:T(8,128)(2,1)S(1)}, bf16[32,512]{1,0:T(8,128)(2,1)S(1)}, u32[]{:S(2)}, u32[]{:S(2)}) collective-permute-start(bf16[32,512]{1,0:T(8,128)(2,1)S(1)} %get-tuple-element.33), channel_id=1, source_target_pairs={{0,8},{4,12},{8,0},{12,4},{1,9},{5,13},{9,1},{13,5},{2,10},{6,14},... | collective-permute-start | bytes 98312 | tf_op jit(solution)/shard_map/ppermute | solution.py:23
  128.7 6.9 %collective-permute-start.27 = (bf16[64,512]{1,0:T(8,128)(2,1)S(1)}, bf16[64,512]{1,0:T(8,128)(2,1)S(1)}, u32[]{:S(2)}, u32[]{:S(2)}) collective-permute-start(bf16[64,512]{1,0:T(8,128)(2,1)S(1)} %get-tuple-element.16), channel_id=1, source_target_pairs={{0,4},{4,8},{8,12},{12,0},{1,5},{5,9},{9,13},{13,1},{2,6},{6,10},{... | collective-permute-start | bytes 196616 | tf_op jit(solution)/shard_map/ppermute | solution.py:23
  133.3 4.8 %collective-permute-start.29 = (bf16[64,512]{1,0:T(8,128)(2,1)S(1)}, bf16[64,512]{1,0:T(8,128)(2,1)S(1)}, u32[]{:S(2)}, u32[]{:S(2)}) collective-permute-start(bf16[64,512]{1,0:T(8,128)(2,1)S(1)} %get-tuple-element.17), channel_id=1, source_target_pairs={{0,12},{4,0},{8,4},{12,8},{1,13},{5,1},{9,5},{13,9},{2,14},{6,2},{... | collective-permute-start | bytes 196616 | tf_op jit(solution)/shard_map/ppermute | solution.py:23
  135.6 5.2 %collective-permute-start.28 = (bf16[64,512]{1,0:T(8,128)(2,1)S(1)}, bf16[64,512]{1,0:T(8,128)(2,1)S(1)}, u32[]{:S(2)}, u32[]{:S(2)}) collective-permute-start(bf16[64,512]{1,0:T(8,128)(2,1)S(1)} %get-tuple-element.18), channel_id=1, source_target_pairs={{0,8},{4,12},{8,0},{12,4},{1,9},{5,13},{9,1},{13,5},{2,10},{6,14},... | collective-permute-start | bytes 196616 | tf_op jit(solution)/shard_map/ppermute | solution.py:23
  164.1 12.3 %collective-permute-start.41 = (bf16[96,2048]{1,0:T(8,128)(2,1)S(1)}, bf16[96,2048]{1,0:T(8,128)(2,1)S(1)}, u32[]{:S(2)}, u32[]{:S(2)}) collective-permute-start(bf16[96,2048]{1,0:T(8,128)(2,1)S(1)} %slice.53), channel_id=1, source_target_pairs={{0,1},{1,0},{2,3},{3,2},{4,5},{5,4},{6,7},{7,6},{8,9},{9,8},{10,11... | collective-permute-start | bytes 1179656 | tf_op jit(solution)/shard_map/ppermute | solution.py:23
  176.5 11.0 %collective-permute-start.42 = (bf16[96,512]{1,0:T(8,128)(2,1)S(1)}, bf16[96,512]{1,0:T(8,128)(2,1)S(1)}, u32[]{:S(2)}, u32[]{:S(2)}) collective-permute-start(bf16[96,512]{1,0:T(8,128)(2,1)S(1)} %get-tuple-element.13), channel_id=1, source_target_pairs={{0,4},{4,8},{8,12},{12,0},{1,5},{5,9},{9,13},{13,1},{2,6},{6,10},{... | collective-permute-start | bytes 294920 | tf_op jit(solution)/shard_map/ppermute | solution.py:23
  177.9 9.6 %collective-permute-start.44 = (bf16[96,512]{1,0:T(8,128)(2,1)S(1)}, bf16[96,512]{1,0:T(8,128)(2,1)S(1)}, u32[]{:S(2)}, u32[]{:S(2)}) collective-permute-start(bf16[96,512]{1,0:T(8,128)(2,1)S(1)} %get-tuple-element.14), channel_id=1, source_target_pairs={{0,12},{4,0},{8,4},{12,8},{1,13},{5,1},{9,5},{13,9},{2,14},{6,2},{... | collective-permute-start | bytes 294920 | tf_op jit(solution)/shard_map/ppermute | solution.py:23
  180.4 9.5 %collective-permute-start.43 = (bf16[96,512]{1,0:T(8,128)(2,1)S(1)}, bf16[96,512]{1,0:T(8,128)(2,1)S(1)}, u32[]{:S(2)}, u32[]{:S(2)}) collective-permute-start(bf16[96,512]{1,0:T(8,128)(2,1)S(1)} %get-tuple-element.15), channel_id=1, source_target_pairs={{0,8},{4,12},{8,0},{12,4},{1,9},{5,13},{9,1},{13,5},{2,10},{6,14},... | collective-permute-start | bytes 294920 | tf_op jit(solution)/shard_map/ppermute | solution.py:23
  (16 other events, 97.6 us)

commit v2 on v1

--- a/solution.py
+++ b/solution.py
@@ -3,7 +3,7 @@
 from jax import lax
 from jax.sharding import PartitionSpec as P
 
-PIECES = (1, 2, 3)
+PIECES = (3, 5, 4)
 
 
 def swiglu_grads(gate, up, dhid):
@@ -23,32 +23,45 @@
     return lax.ppermute(value, axis, [(i, (i + step) % n) for i in range(n)])
 
 
+def swapped(value, axis, bit):
+    n = lax.axis_size(axis)
+    return lax.ppermute(value, axis, [(i, i ^ bit) for i in range(n)])
+
+
 def gather_cols(value, axis):
     n = lax.axis_size(axis)
-    if n > 4:
+    if n != 4:
         return lax.all_gather(value, axis, axis=1, tiled=True)
     me = lax.axis_index(axis)
     width = value.shape[1]
-    out = jnp.zeros((value.shape[0], n * width), value.dtype)
-    for step in range(n):
-        block = shifted(value, axis, step) if step else value
-        out = lax.dynamic_update_slice(out, block, (0, lax.rem(me - step + n, n) * width))
-    return out
+    far = swapped(value, axis, 2)
+    near = swapped(jnp.concatenate([value, far], axis=1), axis, 1)
+    own = (value, far)
+    other = (near[:, :width], near[:, width:])
+    odd, upper = lax.rem(me, 2) == 1, me >= 2
+    blocks = []
+    for pair in range(2):
+        blocks.append(jnp.where(odd, other[pair], own[pair]))
+        blocks.append(jnp.where(odd, own[pair], other[pair]))
+    blocks = [jnp.where(upper, blocks[i ^ 2], blocks[i]) for i in range(4)]
+    return jnp.concatenate(blocks, axis=1)
 
 
 def scatter_cols(value, axis):
     n = lax.axis_size(axis)
-    if n > 4:
-        return lax.psum_scatter(value, axis, scatter_dimension=1, tiled=True).astype(jnp.float32)
+    if n != 4:
+        return lax.psum_scatter(value.astype(jnp.bfloat16), axis, scatter_dimension=1, tiled=True)
     me = lax.axis_index(axis)
     width = value.shape[1] // n
-    total = None
-    for step in range(n):
-        block = lax.dynamic_slice(value, (0, lax.rem(me + step, n) * width), (value.shape[0], width))
-        block = shifted(block, axis, step) if step else block
-        block = block.astype(jnp.float32)
-        total = block if total is None else total + block
-    return total
+    odd, upper = lax.rem(me, 2) == 1, me >= 2
+    blocks = [value[:, i * width : (i + 1) * width] for i in range(4)]
+    keep = [jnp.where(odd, blocks[2 * i + 1], blocks[2 * i]) for i in range(2)]
+    give = [jnp.where(odd, blocks[2 * i], blocks[2 * i + 1]) for i in range(2)]
+    near = swapped(jnp.concatenate(give, axis=1).astype(jnp.bfloat16), axis, 1).astype(jnp.float32)
+    sums = [keep[i] + near[:, i * width : (i + 1) * width] for i in range(2)]
+    mine = jnp.where(upper, sums[1], sums[0])
+    theirs = jnp.where(upper, sums[0], sums[1])
+    return (mine + swapped(theirs.astype(jnp.bfloat16), axis, 2).astype(jnp.float32)).astype(jnp.bfloat16)
 
 
 def summed(value, axis):
@@ -71,11 +84,25 @@
 
 
 def shards(acts, grad_out, w_gate, w_up, w_down):
+    spans = pieces(acts.shape[0])
     ins, backs = [], []
-    spans = pieces(acts.shape[0])
-    for lower, upper in spans:
-        x = own_first(gather_cols(acts[lower:upper], "hid"), "tok")
-        dy = own_first(gather_cols(grad_out[lower:upper], "hid"), "tok")
+    held = None
+    for index, (lower, upper) in enumerate(spans):
+        rows = upper - lower
+        x, dy = acts[lower:upper], grad_out[lower:upper]
+        if index == 0:
+            x = gather_cols(x, "hid")
+            dy = gather_cols(dy, "hid")
+            held = dy
+            x, dy = own_first(x, "tok"), own_first(dy, "tok")
+        else:
+            both, held = lax.optimization_barrier((jnp.concatenate([x, dy], axis=0), held))
+            both = gather_cols(both, "hid")
+            held = both
+            blocks = own_first(both, "tok")
+            count = blocks.shape[0] // rows
+            x = jnp.concatenate([blocks[i * rows : (i + 1) * rows] for i in range(0, count, 2)], axis=0)
+            dy = jnp.concatenate([blocks[i * rows : (i + 1) * rows] for i in range(1, count, 2)], axis=0)
         ins.append((x, dy))
     halves = []
     for x, dy in ins:
@@ -96,7 +123,7 @@
         for step in range(1, n):
             block = back[step * rows : (step + 1) * rows]
             total = total + shifted(block, "tok", n - step).astype(jnp.float32)
-        backs.append(scatter_cols(total.astype(jnp.bfloat16), "hid").astype(jnp.bfloat16))
+        backs.append(scatter_cols(total, "hid"))
     x_all = jnp.concatenate([x for x, _ in ins], axis=0)
     dy_all = jnp.concatenate([dy for _, dy in ins], axis=0)
     hidden, d_gate, d_up = [jnp.concatenate([g[i] for g in grads], axis=0) for i in range(3)]

time: 191 us -> 196 us (1.026)
  waiting for transfers between devices: 57.5 us -> 86.5 us
  local copies, waits for them, and re-layouts: 20.9 us -> 9.16 us
  starting transfers between devices: 48.7 us -> 39 us
  matrix products: 57.9 us -> 53.1 us
  other arithmetic: 4.28 us -> 6.25 us
    ppermute x45 -> x16, starting transfers between devices: 48.7 us -> 12.1 us  [shifted(): return lax.ppermute(value, axis, [(i, (i + step) % n) for i in range(n)])]
    ppermute x0 -> x14, waiting for transfers between devices: none -> 27.6 us  [swapped(): return lax.ppermute(value, axis, [(i, i ^ bit) for i in range(n)])]
    ppermute x0 -> x14, starting transfers between devices: none -> 27 us  [swapped(): return lax.ppermute(value, axis, [(i, i ^ bit) for i in range(n)])]
    dynamic_update_slice x18 -> x0, local copies, waits for them, and re-layouts: 7.64 us -> none  [gather_cols(): lax.dynamic_update_slice(out, block, (0, lax.rem(me - step + n, n) * width))]
    dot_general x18, matrix products: 57.9 us -> 53.1 us  [dot(): lax.dot_general(left, right, (dims, ((), ())), preferred_element_type=jnp...]
    slice x6, local copies, waits for them, and re-layouts: 8.16 us -> 5.08 us  [shards(): x, dy = (acts[lower:upper], grad_out[lower:upper])]
    ppermute x45 -> x16, waiting for transfers between devices: 57.5 us -> 58.8 us  [shifted(): return lax.ppermute(value, axis, [(i, (i + step) % n) for i in range(n)])]
    unnamed x48 -> x15, local copies, waits for them, and re-layouts: 4.06 us -> 3.25 us
  transfers between devices with their start and end apart: 45 -> 30, of which waited for: 16 -> 16; matrix products, arithmetic and copies ran while one was open for 38% -> 34% of each run, Pallas kernels for 0% -> 0%
where the time goes in v2:
time: 196 us; the launch traced here: 195 us
  waiting for transfers between devices  86.5 us (44%)
  matrix products  53.1 us (27%)
  starting transfers between devices  39 us (20%)
  local copies, waits for them, and re-layouts  9.16 us (5%)
  other arithmetic  6.25 us (3%)
    ppermute x16, waiting for transfers between devices, shifted(): return lax.ppermute(value, axis, [(i, (i + step) % n) for i in range(n)])  58.8 us
    dot_general x18, matrix products, dot(): lax.dot_general(left, right, (dims, ((), ())), preferred_element_type=jnp...  53.1 us
    ppermute x14, waiting for transfers between devices, swapped(): return lax.ppermute(value, axis, [(i, i ^ bit) for i in range(n)])  27.6 us
    ppermute x14, starting transfers between devices, swapped(): return lax.ppermute(value, axis, [(i, i ^ bit) for i in range(n)])  27 us
    ppermute x16, starting transfers between devices, shifted(): return lax.ppermute(value, axis, [(i, (i + step) % n) for i in range(n)])  12.1 us
    slice x6, local copies, waits for them, and re-layouts, shards(): x, dy = (acts[lower:upper], grad_out[lower:upper])  5.08 us
  transfers between devices with their start and end apart: 30, of which 16 were waited for; matrix products, arithmetic and copies ran while one was open for 34% of the time, Pallas kernels for 0%

profile of v2, /device:TPU:0, one launch (start us, length us, event | category | flops | bytes accessed | tf_op | source)
XLA Modules:
  0.0 195.1 jit_solution(9662276164890355237)
XLA Ops:
  1.4 4.0 %collective-permute-start = (bf16[48,512]{1,0:T(8,128)(2,1)S(1)}, bf16[48,512]{1,0:T(8,128)(2,1)S(1)}, u32[]{:S(2)}, u32[]{:S(2)}) collective-permute-start(bf16[48,512]{1,0:T(8,128)(2,1)S(1)} %slice.138), channel_id=1, source_target_pairs={{0,8},{4,12},{8,0},{12,4},{1,9},{5,13},{9,1},{13,5},{2,10},{6,14},... | collective-permute-start | bytes 147464 | tf_op jit(solution)/shard_map/ppermute | solution.py:28
  9.8 2.0 %collective-permute-start.1 = (bf16[48,1024]{1,0:T(8,128)(2,1)S(1)}, bf16[48,1024]{1,0:T(8,128)(2,1)S(1)}, u32[]{:S(2)}, u32[]{:S(2)}) collective-permute-start(bf16[48,1024]{1,0:T(8,128)(2,1)S(1)} %pad_maximum_fusion.18), channel_id=1, source_target_pairs={{0,4},{4,0},{8,12},{12,8},{1,5},{5,1},{9,13},{13,9},{2,6},{6,2},{1... | collective-permute-start | bytes 294920 | tf_op jit(solution)/shard_map/ppermute | solution.py:28
  11.8 1.1 collective-permute-start.5
  12.9 2.6 %collective-permute-done.1 = bf16[48,1024]{1,0:T(8,128)(2,1)S(1)} collective-permute-done((bf16[48,1024]{1,0:T(8,128)(2,1)S(1)}, bf16[48,1024]{1,0:T(8,128)(2,1)S(1)}, u32[]{:S(2)}, u32[]{:S(2)}) %collective-permute-start.1) | collective-permute-done | bytes 98336 | tf_op jit(solution)/shard_map/ppermute | solution.py:28
  17.1 2.6 %collective-permute-start.12 = (bf16[160,512]{1,0:T(8,128)(2,1)S(1)}, bf16[160,512]{1,0:T(8,128)(2,1)S(1)}, u32[]{:S(2)}, u32[]{:S(2)}) collective-permute-start(bf16[160,512]{1,0:T(8,128)(2,1)S(1)} %pad_maximum_fusion.14), channel_id=1, source_target_pairs={{0,8},{4,12},{8,0},{12,4},{1,9},{5,13},{9,1},{13,5},{2,10},{6,14},... | collective-permute-start | bytes 491528 | tf_op jit(solution)/shard_map/ppermute | solution.py:28
  20.9 7.2 %collective-permute-done.12 = bf16[160,512]{1,0:T(8,128)(2,1)S(1)} collective-permute-done((bf16[160,512]{1,0:T(8,128)(2,1)S(1)}, bf16[160,512]{1,0:T(8,128)(2,1)S(1)}, u32[]{:S(2)}, u32[]{:S(2)}) %collective-permute-start.12) | collective-permute-done | bytes 163872 | tf_op jit(solution)/shard_map/ppermute | solution.py:28
  28.7 5.7 %convolution_convert_fusion.11 = bf16[96,1792]{1,0:T(8,128)(2,1)S(1)} fusion(bf16[1792,2048]{1,0:T(8,128)(2,1)} %param.9, bf16[48,2048]{1,0:T(8,128)(2,1)S(1)} %collective-permute-done.2, bf16[48,512]{1,0:T(8,128)(2,1)S(1)} %get-tuple-element.63, bf16[48,512]{1,0:T(8,128)(2,1)S(1)} %get-tuple-element.62, bf16[48,512]{1,0:T(8,128)(2,1)S(1)} %get-tuple-element.61, ...), kind=kOutput, calls=%fused_computation.16 | convolution fusion | flops 706781184 | bytes 8077312 | tf_op jit(solution)/shard_map/dot_general | solution.py:18
  34.4 1.5 collective-permute-start.3
  35.9 1.3 convolution_convert_fusion.10
  37.9 1.3 convolution_convert_fusion.9
  39.2 1.5 collective-permute-start.8
  41.5 3.4 %collective-permute-start.21 = (bf16[128,512]{1,0:T(8,128)(2,1)S(1)}, bf16[128,512]{1,0:T(8,128)(2,1)S(1)}, u32[]{:S(2)}, u32[]{:S(2)}) collective-permute-start(bf16[128,512]{1,0:T(8,128)(2,1)S(1)} %pad_maximum_fusion.16), channel_id=1, source_target_pairs={{0,8},{4,12},{8,0},{12,4},{1,9},{5,13},{9,1},{13,5},{2,10},{6,14},... | collective-permute-start | bytes 393224 | tf_op jit(solution)/shard_map/ppermute | solution.py:28
  45.5 7.4 %collective-permute-done.7 = bf16[96,1792]{1,0:T(8,128)(2,1)S(1)} collective-permute-done((bf16[96,1792]{1,0:T(8,128)(2,1)S(1)}, bf16[96,1792]{1,0:T(8,128)(2,1)S(1)}, u32[]{:S(2)}, u32[]{:S(2)}) %collective-permute-start.7) | collective-permute-done | bytes 344096 | tf_op jit(solution)/shard_map/ppermute | solution.py:23
  52.8 5.8 %collective-permute-done.8 = bf16[96,1792]{1,0:T(8,128)(2,1)S(1)} collective-permute-done((bf16[96,1792]{1,0:T(8,128)(2,1)S(1)}, bf16[96,1792]{1,0:T(8,128)(2,1)S(1)}, u32[]{:S(2)}, u32[]{:S(2)}) %collective-permute-start.8) | collective-permute-done | bytes 344096 | tf_op jit(solution)/shard_map/ppermute | solution.py:23
  59.2 2.3 %fusion.43 = f32[96,2048]{1,0:T(8,128)S(1)} fusion(bf16[96,1792]{1,0:T(8,128)(2,1)S(1)} %get-tuple-element.24, bf16[2048,1792]{1,0:T(8,128)(2,1)S(1)} %bitcast.25), kind=kOutput, calls=%fused_computation.161 | convolution fusion | flops 704643072 | bytes 8470528 | tf_op jit(solution)/shard_map/dot_general | solution.py:18
  61.5 2.3 %fusion.2 = bf16[96,2048]{1,0:T(8,128)(2,1)S(1)} fusion(f32[96,2048]{1,0:T(8,128)S(1)} %fusion.43, bf16[96,1792]{1,0:T(8,128)(2,1)S(1)} %get-tuple-element.25, bf16[2048,1792]{1,0:T(8,128)(2,1)S(1)} %copy-done), kind=kOutput, calls=%fused_computation.17 | convolution fusion | flops 705036288 | bytes 8863744 | tf_op jit(solution)/shard_map/dot_general | solution.py:18
  64.5 1.9 collective-permute-start.22
  68.2 6.8 %collective-permute-done.10 = bf16[48,1024]{1,0:T(8,128)(2,1)S(1)} collective-permute-done((bf16[48,1024]{1,0:T(8,128)(2,1)S(1)}, bf16[48,1024]{1,0:T(8,128)(2,1)S(1)}, u32[]{:S(2)}, u32[]{:S(2)}) %collective-permute-start.10) | collective-permute-done | bytes 98336 | tf_op jit(solution)/shard_map/ppermute | solution.py:28
  75.1 3.4 %collective-permute-start.11 = (bf16[48,512]{1,0:T(8,128)(2,1)S(1)}, bf16[48,512]{1,0:T(8,128)(2,1)S(1)}, u32[]{:S(2)}, u32[]{:S(2)}) collective-permute-start(bf16[48,512]{1,0:T(8,128)(2,1)S(1)} %get-tuple-element.8), channel_id=1, source_target_pairs={{0,8},{4,12},{8,0},{12,4},{1,9},{5,13},{9,1},{13,5},{2,10},{6,14},... | collective-permute-start | bytes 147464 | tf_op jit(solution)/shard_map/ppermute | solution.py:28
  78.7 1.9 collective-permute-done.11
  81.4 1.4 convolution_convert_fusion.3
  82.8 1.4 convolution_convert_fusion.4
  84.2 1.6 collective-permute-start.16
  86.3 2.7 %convolution_convert_fusion.5 = bf16[160,1792]{1,0:T(8,128)(2,1)S(1)} fusion(bf16[1792,2048]{1,0:T(8,128)(2,1)S(1)} %bitcast.27, bf16[80,2048]{1,0:T(8,128)(2,1)S(1)} %get-tuple-element.29, bf16[80,2048]{1,0:T(8,128)(2,1)S(1)} %get-tuple-element.33), kind=kOutput, calls=%fused_computation.7 | convolution fusion | flops 1176002560 | bytes 8568832 | tf_op jit(solution)/shard_map/dot_general | solution.py:18
  89.1 1.6 collective-permute-start.15
  92.2 1.1 convolution_convert_fusion.6
  93.3 1.1 convolution_convert_fusion.7
  95.1 1.5 collective-permute-start.26
  96.6 2.6 %convolution_convert_fusion.8 = bf16[128,1792]{1,0:T(8,128)(2,1)S(1)} fusion(bf16[1792,2048]{1,0:T(8,128)(2,1)S(1)} %bitcast.27, bf16[64,2048]{1,0:T(8,128)(2,1)S(1)} %get-tuple-element.43, bf16[64,2048]{1,0:T(8,128)(2,1)S(1)} %get-tuple-element.47), kind=kOutput, calls=%fused_computation.12 | convolution fusion | flops 940802048 | bytes 8323072 | tf_op jit(solution)/shard_map/dot_general | solution.py:18
  99.2 1.0 collective-permute-done.16
  100.2 1.5 collective-permute-start.24
  101.7 10.8 %collective-permute-done.17 = bf16[160,1792]{1,0:T(8,128)(2,1)S(1)} collective-permute-done((bf16[160,1792]{1,0:T(8,128)(2,1)S(1)}, bf16[160,1792]{1,0:T(8,128)(2,1)S(1)}, u32[]{:S(2)}, u32[]{:S(2)}) %collective-permute-start.17) | collective-permute-done | bytes 573472 | tf_op jit(solution)/shard_map/ppermute | solution.py:23
  112.5 12.3 %collective-permute-done.15 = bf16[160,1792]{1,0:T(8,128)(2,1)S(1)} collective-permute-done((bf16[160,1792]{1,0:T(8,128)(2,1)S(1)}, bf16[160,1792]{1,0:T(8,128)(2,1)S(1)}, u32[]{:S(2)}, u32[]{:S(2)}) %collective-permute-start.15) | collective-permute-done | bytes 573472 | tf_op jit(solution)/shard_map/ppermute | solution.py:23
  125.7 2.5 %fusion.44 = f32[160,2048]{1,0:T(8,128)S(1)} fusion(bf16[160,1792]{1,0:T(8,128)(2,1)S(1)} %get-tuple-element.18, bf16[2048,1792]{1,0:T(8,128)(2,1)S(1)} %bitcast.25), kind=kOutput, calls=%fused_computation.162 | convolution fusion | flops 1174405120 | bytes 9224192 | tf_op jit(solution)/shard_map/dot_general | solution.py:18
  128.2 2.5 %fusion = bf16[160,2048]{1,0:T(8,128)(2,1)S(1)} fusion(f32[160,2048]{1,0:T(8,128)S(1)} %fusion.44, bf16[160,1792]{1,0:T(8,128)(2,1)S(1)} %get-tuple-element.19, bf16[2048,1792]{1,0:T(8,128)(2,1)S(1)} %copy-done), kind=kOutput, calls=%fused_computation.4 | convolution fusion | flops 1175060480 | bytes 9879552 | tf_op jit(solution)/shard_map/dot_general | solution.py:18
  130.9 3.7 %collective-permute-done.25 = bf16[128,1792]{1,0:T(8,128)(2,1)S(1)} collective-permute-done((bf16[128,1792]{1,0:T(8,128)(2,1)S(1)}, bf16[128,1792]{1,0:T(8,128)(2,1)S(1)}, u32[]{:S(2)}, u32[]{:S(2)}) %collective-permute-start.25) | collective-permute-done | bytes 458784 | tf_op jit(solution)/shard_map/ppermute | solution.py:23
  134.6 9.8 %collective-permute-done.26 = bf16[128,1792]{1,0:T(8,128)(2,1)S(1)} collective-permute-done((bf16[128,1792]{1,0:T(8,128)(2,1)S(1)}, bf16[128,1792]{1,0:T(8,128)(2,1)S(1)}, u32[]{:S(2)}, u32[]{:S(2)}) %collective-permute-start.26) | collective-permute-done | bytes 458784 | tf_op jit(solution)/shard_map/ppermute | solution.py:23
  144.4 7.4 %collective-permute-done.24 = bf16[128,1792]{1,0:T(8,128)(2,1)S(1)} collective-permute-done((bf16[128,1792]{1,0:T(8,128)(2,1)S(1)}, bf16[128,1792]{1,0:T(8,128)(2,1)S(1)}, u32[]{:S(2)}, u32[]{:S(2)}) %collective-permute-start.24) | collective-permute-done | bytes 458784 | tf_op jit(solution)/shard_map/ppermute | solution.py:23
  152.6 2.4 %fusion.45 = f32[128,2048]{1,0:T(8,128)S(1)} fusion(bf16[128,1792]{1,0:T(8,128)(2,1)S(1)} %get-tuple-element.21, bf16[2048,1792]{1,0:T(8,128)(2,1)S(1)} %bitcast.25), kind=kOutput, calls=%fused_computation.163 | convolution fusion | flops 939524096 | bytes 8847360 | tf_op jit(solution)/shard_map/dot_general | solution.py:18
  155.0 6.3 %convolution_convert_fusion.2 = bf16[2048,1792]{1,0:T(8,128)(2,1)} fusion(bf16[384,2048]{1,0:T(8,128)(2,1)S(1)} %get-tuple-element.41, bf16[128,1792]{1,0:T(8,128)(2,1)S(1)} %get-tuple-element.21, bf16[160,1792]{1,0:T(8,128)(2,1)S(1)} %get-tuple-element.18, bf16[96,1792]{1,0:T(8,128)(2,1)S(1)} %get-tuple-element.24), kind=kOutput, calls=%fused_computation.2 | convolution fusion | flops 2826371072 | bytes 10289152 | tf_op jit(solution)/shard_map/dot_general | solution.py:18
  161.4 6.1 %convolution_convert_fusion.1 = bf16[2048,1792]{1,0:T(8,128)(2,1)} fusion(bf16[384,2048]{1,0:T(8,128)(2,1)S(1)} %get-tuple-element.41, bf16[128,1792]{1,0:T(8,128)(2,1)S(1)} %get-tuple-element.22, bf16[160,1792]{1,0:T(8,128)(2,1)S(1)} %get-tuple-element.19, bf16[96,1792]{1,0:T(8,128)(2,1)S(1)} %get-tuple-element.25), kind=kOutput, calls=%fused_computation.1 | convolution fusion | flops 2826371072 | bytes 10289152 | tf_op jit(solution)/shard_map/dot_general | solution.py:18
  167.4 2.5 %fusion.1 = bf16[128,2048]{1,0:T(8,128)(2,1)S(1)} fusion(f32[128,2048]{1,0:T(8,128)S(1)} %fusion.45, bf16[128,1792]{1,0:T(8,128)(2,1)S(1)} %get-tuple-element.22, bf16[2048,1792]{1,0:T(8,128)(2,1)S(1)} %copy-done), kind=kOutput, calls=%fused_computation.9 | convolution fusion | flops 940048384 | bytes 9371648 | tf_op jit(solution)/shard_map/dot_general | solution.py:18
  170.0 7.5 %convolution_convert_fusion = bf16[1792,2048]{1,0:T(8,128)(2,1)} fusion(bf16[384,2048]{1,0:T(8,128)(2,1)} %get-tuple-element.40, bf16[128,1792]{1,0:T(8,128)(2,1)S(1)} %get-tuple-element.20, bf16[160,1792]{1,0:T(8,128)(2,1)S(1)} %get-tuple-element.17, bf16[96,1792]{1,0:T(8,128)(2,1)S(1)} %get-tuple-element.23), kind=kOutput, calls=%fused_computation | convolution fusion | flops 2826371072 | bytes 10289152 | tf_op jit(solution)/shard_map/dot_general | solution.py:18
  178.6 1.3 collective-permute-start.28
  180.0 4.8 %collective-permute-done.19 = bf16[80,1024]{1,0:T(8,128)(2,1)S(1)} collective-permute-done((bf16[80,1024]{1,0:T(8,128)(2,1)S(1)}, bf16[80,1024]{1,0:T(8,128)(2,1)S(1)}, u32[]{:S(2)}, u32[]{:S(2)}) %collective-permute-start.19) | collective-permute-done | bytes 163872 | tf_op jit(solution)/shard_map/ppermute | solution.py:28
  184.9 2.4 %collective-permute-start.20 = (bf16[80,512]{1,0:T(8,128)(2,1)S(1)}, bf16[80,512]{1,0:T(8,128)(2,1)S(1)}, u32[]{:S(2)}, u32[]{:S(2)}) collective-permute-start(bf16[80,512]{1,0:T(8,128)(2,1)S(1)} %get-tuple-element.11), channel_id=1, source_target_pairs={{0,8},{4,12},{8,0},{12,4},{1,9},{5,13},{9,1},{13,5},{2,10},{6,14},... | collective-permute-start | bytes 245768 | tf_op jit(solution)/shard_map/ppermute | solution.py:28
  187.4 2.7 %collective-permute-start.29 = (bf16[64,512]{1,0:T(8,128)(2,1)S(1)}, bf16[64,512]{1,0:T(8,128)(2,1)S(1)}, u32[]{:S(2)}, u32[]{:S(2)}) collective-permute-start(bf16[64,512]{1,0:T(8,128)(2,1)S(1)} %get-tuple-element.14), channel_id=1, source_target_pairs={{0,8},{4,12},{8,0},{12,4},{1,9},{5,13},{9,1},{13,5},{2,10},{6,14},... | collective-permute-start | bytes 196616 | tf_op jit(solution)/shard_map/ppermute | solution.py:28
  190.0 3.6 %collective-permute-done.20 = bf16[80,512]{1,0:T(8,128)(2,1)S(1)} collective-permute-done((bf16[80,512]{1,0:T(8,128)(2,1)S(1)}, bf16[80,512]{1,0:T(8,128)(2,1)S(1)}, u32[]{:S(2)}, u32[]{:S(2)}) %collective-permute-start.20) | collective-permute-done | bytes 81952 | tf_op jit(solution)/shard_map/ppermute | solution.py:28
  (93 shorter events, 21.7 us)
Async XLA Ops:
  1.4 8.4 %collective-permute-start = (bf16[48,512]{1,0:T(8,128)(2,1)S(1)}, bf16[48,512]{1,0:T(8,128)(2,1)S(1)}, u32[]{:S(2)}, u32[]{:S(2)}) collective-permute-start(bf16[48,512]{1,0:T(8,128)(2,1)S(1)} %slice.138), channel_id=1, source_target_pairs={{0,8},{4,12},{8,0},{12,4},{1,9},{5,13},{9,1},{13,5},{2,10},{6,14},... | collective-permute-start | bytes 147464 | tf_op jit(solution)/shard_map/ppermute | solution.py:28
  6.3 5.5 %collective-permute-start.4 = (bf16[48,512]{1,0:T(8,128)(2,1)S(1)}, bf16[48,512]{1,0:T(8,128)(2,1)S(1)}, u32[]{:S(2)}, u32[]{:S(2)}) collective-permute-start(bf16[48,512]{1,0:T(8,128)(2,1)S(1)} %slice.141), channel_id=1, source_target_pairs={{0,8},{4,12},{8,0},{12,4},{1,9},{5,13},{9,1},{13,5},{2,10},{6,14},... | collective-permute-start | bytes 147464 | tf_op jit(solution)/shard_map/ppermute | solution.py:28
  9.8 5.7 %collective-permute-start.1 = (bf16[48,1024]{1,0:T(8,128)(2,1)S(1)}, bf16[48,1024]{1,0:T(8,128)(2,1)S(1)}, u32[]{:S(2)}, u32[]{:S(2)}) collective-permute-start(bf16[48,1024]{1,0:T(8,128)(2,1)S(1)} %pad_maximum_fusion.18), channel_id=1, source_target_pairs={{0,4},{4,0},{8,12},{12,8},{1,5},{5,1},{9,13},{13,9},{2,6},{6,2},{1... | collective-permute-start | bytes 294920 | tf_op jit(solution)/shard_map/ppermute | solution.py:28
  11.8 7.9 %collective-permute-start.5 = (bf16[48,1024]{1,0:T(8,128)(2,1)S(1)}, bf16[48,1024]{1,0:T(8,128)(2,1)S(1)}, u32[]{:S(2)}, u32[]{:S(2)}) collective-permute-start(bf16[48,1024]{1,0:T(8,128)(2,1)S(1)} %pad_maximum_fusion.19), channel_id=1, source_target_pairs={{0,4},{4,0},{8,12},{12,8},{1,5},{5,1},{9,13},{13,9},{2,6},{6,2},{1... | collective-permute-start | bytes 294920 | tf_op jit(solution)/shard_map/ppermute | solution.py:28
  17.1 11.6 %collective-permute-start.2 = (bf16[48,2048]{1,0:T(8,128)(2,1)S(1)}, bf16[48,2048]{1,0:T(8,128)(2,1)S(1)}, u32[]{:S(2)}, u32[]{:S(2)}) collective-permute-start(bf16[48,2048]{1,0:T(8,128)(2,1)S(1)} %get-tuple-element.65), channel_id=1, source_target_pairs={{0,1},{1,0},{2,3},{3,2},{4,5},{5,4},{6,7},{7,6},{8,9},{9,8},{10,11... | collective-permute-start | bytes 589832 | tf_op jit(solution)/shard_map/ppermute | solution.py:23
  17.1 11.0 %collective-permute-start.12 = (bf16[160,512]{1,0:T(8,128)(2,1)S(1)}, bf16[160,512]{1,0:T(8,128)(2,1)S(1)}, u32[]{:S(2)}, u32[]{:S(2)}) collective-permute-start(bf16[160,512]{1,0:T(8,128)(2,1)S(1)} %pad_maximum_fusion.14), channel_id=1, source_target_pairs={{0,8},{4,12},{8,0},{12,4},{1,9},{5,13},{9,1},{13,5},{2,10},{6,14},... | collective-permute-start | bytes 491528 | tf_op jit(solution)/shard_map/ppermute | solution.py:28
  20.6 15.4 %collective-permute-start.6 = (bf16[48,2048]{1,0:T(8,128)(2,1)S(1)}, bf16[48,2048]{1,0:T(8,128)(2,1)S(1)}, u32[]{:S(2)}, u32[]{:S(2)}) collective-permute-start(bf16[48,2048]{1,0:T(8,128)(2,1)S(1)} %get-tuple-element.67), channel_id=1, source_target_pairs={{0,1},{1,0},{2,3},{3,2},{4,5},{5,4},{6,7},{7,6},{8,9},{9,8},{10,11... | collective-permute-start | bytes 589832 | tf_op jit(solution)/shard_map/ppermute | solution.py:23
  28.1 7.8 %copy-start = (bf16[2048,1792]{1,0:T(8,128)(2,1)S(1)}, bf16[2048,1792]{1,0:T(8,128)(2,1)}, u32[]{:S(2)}) copy-start(bf16[2048,1792]{1,0:T(8,128)(2,1)} %param.8) | copy-start | bytes 22020100
  28.1 13.2 %collective-permute-start.13 = (bf16[160,1024]{1,0:T(8,128)(2,1)S(1)}, bf16[160,1024]{1,0:T(8,128)(2,1)S(1)}, u32[]{:S(2)}, u32[]{:S(2)}) collective-permute-start(bf16[160,1024]{1,0:T(8,128)(2,1)S(1)} %pad_maximum_fusion.9), channel_id=1, source_target_pairs={{0,4},{4,0},{8,12},{12,8},{1,5},{5,1},{9,13},{13,9},{2,6},{6,2},{1... | collective-permute-start | bytes 983048 | tf_op jit(solution)/shard_map/ppermute | solution.py:28
  28.7 9.2 %slice-start = ((s8[7340032]{0:T(1024)(128)(4,1)}), s8[4194304]{0:T(1024)(128)(4,1)S(1)}, s32[]{:S(2)}) async-start(s8[7340032]{0:T(1024)(128)(4,1)} %bitcast.24), calls=%async_computation | async-start | bytes 8388608
  34.4 3.5 %slice-start.1 = ((s8[7340032]{0:T(1024)(128)(4,1)}), s8[3145728]{0:T(1024)(128)(4,1)S(1)}, s32[]{:S(2)}) async-start(s8[7340032]{0:T(1024)(128)(4,1)} %bitcast.24), calls=%async_computation.1 | async-start | bytes 6291456
  34.4 11.1 %collective-permute-start.3 = (bf16[96,1792]{1,0:T(8,128)(2,1)S(1)}, bf16[96,1792]{1,0:T(8,128)(2,1)S(1)}, u32[]{:S(2)}, u32[]{:S(2)}) collective-permute-start(bf16[96,1792]{1,0:T(8,128)(2,1)S(1)} %convolution_convert_fusion.11), channel_id=1, source_target_pairs={{0,2},{2,0},{1,3},{3,1},{4,6},{6,4},{5,7},{7,5},{8,10},{10,8},{9,1... | collective-permute-start | bytes 1032200 | tf_op jit(solution)/shard_map/ppermute | solution.py:23
  37.2 15.6 %collective-permute-start.7 = (bf16[96,1792]{1,0:T(8,128)(2,1)S(1)}, bf16[96,1792]{1,0:T(8,128)(2,1)S(1)}, u32[]{:S(2)}, u32[]{:S(2)}) collective-permute-start(bf16[96,1792]{1,0:T(8,128)(2,1)S(1)} %convolution_convert_fusion.10), channel_id=1, source_target_pairs={{0,2},{2,0},{1,3},{3,1},{4,6},{6,4},{5,7},{7,5},{8,10},{10,8},{9,1... | collective-permute-start | bytes 1032200 | tf_op jit(solution)/shard_map/ppermute | solution.py:23
  39.2 19.5 %collective-permute-start.8 = (bf16[96,1792]{1,0:T(8,128)(2,1)S(1)}, bf16[96,1792]{1,0:T(8,128)(2,1)S(1)}, u32[]{:S(2)}, u32[]{:S(2)}) collective-permute-start(bf16[96,1792]{1,0:T(8,128)(2,1)S(1)} %convolution_convert_fusion.9), channel_id=1, source_target_pairs={{0,2},{2,0},{1,3},{3,1},{4,6},{6,4},{5,7},{7,5},{8,10},{10,8},{9,1... | collective-permute-start | bytes 1032200 | tf_op jit(solution)/shard_map/ppermute | solution.py:23
  41.5 23.0 %collective-permute-start.21 = (bf16[128,512]{1,0:T(8,128)(2,1)S(1)}, bf16[128,512]{1,0:T(8,128)(2,1)S(1)}, u32[]{:S(2)}, u32[]{:S(2)}) collective-permute-start(bf16[128,512]{1,0:T(8,128)(2,1)S(1)} %pad_maximum_fusion.16), channel_id=1, source_target_pairs={{0,8},{4,12},{8,0},{12,4},{1,9},{5,13},{9,1},{13,5},{2,10},{6,14},... | collective-permute-start | bytes 393224 | tf_op jit(solution)/shard_map/ppermute | solution.py:28
  63.9 2.6 %collective-permute-start.9 = (bf16[48,2048]{1,0:T(8,128)(2,1)S(1)}, bf16[48,2048]{1,0:T(8,128)(2,1)S(1)}, u32[]{:S(2)}, u32[]{:S(2)}) collective-permute-start(bf16[48,2048]{1,0:T(8,128)(2,1)S(1)} %slice.189), channel_id=1, source_target_pairs={{0,1},{1,0},{2,3},{3,2},{4,5},{5,4},{6,7},{7,6},{8,9},{9,8},{10,11... | collective-permute-start | bytes 589832 | tf_op jit(solution)/shard_map/ppermute | solution.py:23
  64.0 16.6 %collective-permute-start.14 = (bf16[160,2048]{1,0:T(8,128)(2,1)S(1)}, bf16[160,2048]{1,0:T(8,128)(2,1)S(1)}, u32[]{:S(2)}, u32[]{:S(2)}) collective-permute-start(bf16[160,2048]{1,0:T(8,128)(2,1)S(1)} %pad_maximum_fusion), channel_id=1, source_target_pairs={{0,1},{1,0},{2,3},{3,2},{4,5},{5,4},{6,7},{7,6},{8,9},{9,8},{10,11... | collective-permute-start | bytes 1966088 | tf_op jit(solution)/shard_map/ppermute | solution.py:23
  64.5 13.9 %collective-permute-start.22 = (bf16[128,1024]{1,0:T(8,128)(2,1)S(1)}, bf16[128,1024]{1,0:T(8,128)(2,1)S(1)}, u32[]{:S(2)}, u32[]{:S(2)}) collective-permute-start(bf16[128,1024]{1,0:T(8,128)(2,1)S(1)} %pad_maximum_fusion.10), channel_id=1, source_target_pairs={{0,4},{4,0},{8,12},{12,8},{1,5},{5,1},{9,13},{13,9},{2,6},{6,2},{1... | collective-permute-start | bytes 786440 | tf_op jit(solution)/shard_map/ppermute | solution.py:28
  66.5 8.5 %collective-permute-start.10 = (bf16[48,1024]{1,0:T(8,128)(2,1)S(1)}, bf16[48,1024]{1,0:T(8,128)(2,1)S(1)}, u32[]{:S(2)}, u32[]{:S(2)}) collective-permute-start(bf16[48,1024]{1,0:T(8,128)(2,1)S(1)} %pad_maximum_fusion.20), channel_id=1, source_target_pairs={{0,4},{4,0},{8,12},{12,8},{1,5},{5,1},{9,13},{13,9},{2,6},{6,2},{1... | collective-permute-start | bytes 294920 | tf_op jit(solution)/shard_map/ppermute | solution.py:28
  75.1 5.4 %collective-permute-start.11 = (bf16[48,512]{1,0:T(8,128)(2,1)S(1)}, bf16[48,512]{1,0:T(8,128)(2,1)S(1)}, u32[]{:S(2)}, u32[]{:S(2)}) collective-permute-start(bf16[48,512]{1,0:T(8,128)(2,1)S(1)} %get-tuple-element.8), channel_id=1, source_target_pairs={{0,8},{4,12},{8,0},{12,4},{1,9},{5,13},{9,1},{13,5},{2,10},{6,14},... | collective-permute-start | bytes 147464 | tf_op jit(solution)/shard_map/ppermute | solution.py:28
  78.6 12.8 %collective-permute-start.23 = (bf16[128,2048]{1,0:T(8,128)(2,1)S(1)}, bf16[128,2048]{1,0:T(8,128)(2,1)S(1)}, u32[]{:S(2)}, u32[]{:S(2)}) collective-permute-start(bf16[128,2048]{1,0:T(8,128)(2,1)S(1)} %pad_maximum_fusion.2), channel_id=1, source_target_pairs={{0,1},{1,0},{2,3},{3,2},{4,5},{5,4},{6,7},{7,6},{8,9},{9,8},{10,11... | collective-permute-start | bytes 1572872 | tf_op jit(solution)/shard_map/ppermute | solution.py:23
  81.4 4.9 %slice-start.2 = ((s8[7340032]{0:T(1024)(128)(4,1)}), s8[4194304]{0:T(1024)(128)(4,1)S(1)}, s32[]{:S(2)}) async-start(s8[7340032]{0:T(1024)(128)(4,1)} %bitcast.26), calls=%async_computation.2 | async-start | bytes 8388608
  82.8 3.5 %slice-start.3 = ((s8[7340032]{0:T(1024)(128)(4,1)}), s8[3145728]{0:T(1024)(128)(4,1)S(1)}, s32[]{:S(2)}) async-start(s8[7340032]{0:T(1024)(128)(4,1)} %bitcast.26), calls=%async_computation.3 | async-start | bytes 6291456
  84.2 16.0 %collective-permute-start.16 = (bf16[160,1792]{1,0:T(8,128)(2,1)S(1)}, bf16[160,1792]{1,0:T(8,128)(2,1)S(1)}, u32[]{:S(2)}, u32[]{:S(2)}) collective-permute-start(bf16[160,1792]{1,0:T(8,128)(2,1)S(1)} %convolution_convert_fusion.4), channel_id=1, source_target_pairs={{0,2},{2,0},{1,3},{3,1},{4,6},{6,4},{5,7},{7,5},{8,10},{10,8},{9,1... | collective-permute-start | bytes 1720328 | tf_op jit(solution)/shard_map/ppermute | solution.py:23
  85.8 26.7 %collective-permute-start.17 = (bf16[160,1792]{1,0:T(8,128)(2,1)S(1)}, bf16[160,1792]{1,0:T(8,128)(2,1)S(1)}, u32[]{:S(2)}, u32[]{:S(2)}) collective-permute-start(bf16[160,1792]{1,0:T(8,128)(2,1)S(1)} %convolution_convert_fusion.3), channel_id=1, source_target_pairs={{0,2},{2,0},{1,3},{3,1},{4,6},{6,4},{5,7},{7,5},{8,10},{10,8},{9,1... | collective-permute-start | bytes 1720328 | tf_op jit(solution)/shard_map/ppermute | solution.py:23
  89.1 35.7 %collective-permute-start.15 = (bf16[160,1792]{1,0:T(8,128)(2,1)S(1)}, bf16[160,1792]{1,0:T(8,128)(2,1)S(1)}, u32[]{:S(2)}, u32[]{:S(2)}) collective-permute-start(bf16[160,1792]{1,0:T(8,128)(2,1)S(1)} %convolution_convert_fusion.5), channel_id=1, source_target_pairs={{0,2},{2,0},{1,3},{3,1},{4,6},{6,4},{5,7},{7,5},{8,10},{10,8},{9,1... | collective-permute-start | bytes 1720328 | tf_op jit(solution)/shard_map/ppermute | solution.py:23
  94.5 40.1 %collective-permute-start.25 = (bf16[128,1792]{1,0:T(8,128)(2,1)S(1)}, bf16[128,1792]{1,0:T(8,128)(2,1)S(1)}, u32[]{:S(2)}, u32[]{:S(2)}) collective-permute-start(bf16[128,1792]{1,0:T(8,128)(2,1)S(1)} %convolution_convert_fusion.7), channel_id=1, source_target_pairs={{0,2},{2,0},{1,3},{3,1},{4,6},{6,4},{5,7},{7,5},{8,10},{10,8},{9,1... | collective-permute-start | bytes 1376264 | tf_op jit(solution)/shard_map/ppermute | solution.py:23
  95.1 49.4 %collective-permute-start.26 = (bf16[128,1792]{1,0:T(8,128)(2,1)S(1)}, bf16[128,1792]{1,0:T(8,128)(2,1)S(1)}, u32[]{:S(2)}, u32[]{:S(2)}) collective-permute-start(bf16[128,1792]{1,0:T(8,128)(2,1)S(1)} %convolution_convert_fusion.6), channel_id=1, source_target_pairs={{0,2},{2,0},{1,3},{3,1},{4,6},{6,4},{5,7},{7,5},{8,10},{10,8},{9,1... | collective-permute-start | bytes 1376264 | tf_op jit(solution)/shard_map/ppermute | solution.py:23
  100.2 51.7 %collective-permute-start.24 = (bf16[128,1792]{1,0:T(8,128)(2,1)S(1)}, bf16[128,1792]{1,0:T(8,128)(2,1)S(1)}, u32[]{:S(2)}, u32[]{:S(2)}) collective-permute-start(bf16[128,1792]{1,0:T(8,128)(2,1)S(1)} %convolution_convert_fusion.8), channel_id=1, source_target_pairs={{0,2},{2,0},{1,3},{3,1},{4,6},{6,4},{5,7},{7,5},{8,10},{10,8},{9,1... | collective-permute-start | bytes 1376264 | tf_op jit(solution)/shard_map/ppermute | solution.py:23
  130.8 46.8 %collective-permute-start.18 = (bf16[80,2048]{1,0:T(8,128)(2,1)S(1)}, bf16[80,2048]{1,0:T(8,128)(2,1)S(1)}, u32[]{:S(2)}, u32[]{:S(2)}) collective-permute-start(bf16[80,2048]{1,0:T(8,128)(2,1)S(1)} %slice.203), channel_id=1, source_target_pairs={{0,1},{1,0},{2,3},{3,2},{4,5},{5,4},{6,7},{7,6},{8,9},{9,8},{10,11... | collective-permute-start | bytes 983048 | tf_op jit(solution)/shard_map/ppermute | solution.py:23
  170.0 8.6 %collective-permute-start.27 = (bf16[64,2048]{1,0:T(8,128)(2,1)S(1)}, bf16[64,2048]{1,0:T(8,128)(2,1)S(1)}, u32[]{:S(2)}, u32[]{:S(2)}) collective-permute-start(bf16[64,2048]{1,0:T(8,128)(2,1)S(1)} %slice.217), channel_id=1, source_target_pairs={{0,1},{1,0},{2,3},{3,2},{4,5},{5,4},{6,7},{7,6},{8,9},{9,8},{10,11... | collective-permute-start | bytes 786440 | tf_op jit(solution)/shard_map/ppermute | solution.py:23
  177.7 7.1 %collective-permute-start.19 = (bf16[80,1024]{1,0:T(8,128)(2,1)S(1)}, bf16[80,1024]{1,0:T(8,128)(2,1)S(1)}, u32[]{:S(2)}, u32[]{:S(2)}) collective-permute-start(bf16[80,1024]{1,0:T(8,128)(2,1)S(1)} %pad_maximum_fusion.15), channel_id=1, source_target_pairs={{0,4},{4,0},{8,12},{12,8},{1,5},{5,1},{9,13},{13,9},{2,6},{6,2},{1... | collective-permute-start | bytes 491528 | tf_op jit(solution)/shard_map/ppermute | solution.py:28
  178.6 8.6 %collective-permute-start.28 = (bf16[64,1024]{1,0:T(8,128)(2,1)S(1)}, bf16[64,1024]{1,0:T(8,128)(2,1)S(1)}, u32[]{:S(2)}, u32[]{:S(2)}) collective-permute-start(bf16[64,1024]{1,0:T(8,128)(2,1)S(1)} %pad_maximum_fusion.17), channel_id=1, source_target_pairs={{0,4},{4,0},{8,12},{12,8},{1,5},{5,1},{9,13},{13,9},{2,6},{6,2},{1... | collective-permute-start | bytes 393224 | tf_op jit(solution)/shard_map/ppermute | solution.py:28
  184.9 8.8 %collective-permute-start.20 = (bf16[80,512]{1,0:T(8,128)(2,1)S(1)}, bf16[80,512]{1,0:T(8,128)(2,1)S(1)}, u32[]{:S(2)}, u32[]{:S(2)}) collective-permute-start(bf16[80,512]{1,0:T(8,128)(2,1)S(1)} %get-tuple-element.11), channel_id=1, source_target_pairs={{0,8},{4,12},{8,0},{12,4},{1,9},{5,13},{9,1},{13,5},{2,10},{6,14},... | collective-permute-start | bytes 245768 | tf_op jit(solution)/shard_map/ppermute | solution.py:28
  187.4 7.0 %collective-permute-start.29 = (bf16[64,512]{1,0:T(8,128)(2,1)S(1)}, bf16[64,512]{1,0:T(8,128)(2,1)S(1)}, u32[]{:S(2)}, u32[]{:S(2)}) collective-permute-start(bf16[64,512]{1,0:T(8,128)(2,1)S(1)} %get-tuple-element.14), channel_id=1, source_target_pairs={{0,8},{4,12},{8,0},{12,4},{1,9},{5,13},{9,1},{13,5},{2,10},{6,14},... | collective-permute-start | bytes 196616 | tf_op jit(solution)/shard_map/ppermute | solution.py:28

commit v3 on v0

v3 whole, which is shorter than its diff:
```python
import functools

import jax
import jax.numpy as jnp
from jax import lax
from jax.experimental import pallas as pl
from jax.experimental.pallas import tpu as pltpu
from jax.sharding import PartitionSpec as P

SIXTEENTHS = (2, 3, 4, 3)
MIB = 1 << 20


def dot(left, right, dims):
    return lax.dot_general(left, right, (dims, ((), ())), preferred_element_type=jnp.float32)


def rows_by_cols(left, right):
    return dot(left, right, ((1,), (0,)))


def over_cols(left, right):
    return dot(left, right, ((1,), (1,)))


def over_rows(left, right):
    return dot(left, right, ((0,), (0,)))


def swiglu_grads(gate, up, dhid):
    sig = jax.nn.sigmoid(gate)
    hidden = (gate * sig * up).astype(jnp.bfloat16)
    d_gate = (dhid * up * sig * (1.0 + gate * (1.0 - sig))).astype(jnp.bfloat16)
    d_up = (dhid * gate * sig).astype(jnp.bfloat16)
    return hidden, d_gate, d_up


def shifted(value, axis, step):
    n = lax.axis_size(axis)
    return lax.ppermute(value, axis, [(i, (i + step) % n) for i in range(n)])


def swapped(value, axis, bit):
    n = lax.axis_size(axis)
    return lax.ppermute(value, axis, [(i, i ^ bit) for i in range(n)])


def summed(value, axis):
    total = value.astype(jnp.float32)
    for step in range(1, lax.axis_size(axis)):
        total = total + shifted(value, axis, step).astype(jnp.float32)
    return total


def own_first(value, axis):
    return jnp.concatenate([value] + [shifted(value, axis, step) for step in range(1, lax.axis_size(axis))], axis=0)


def home_rows(back, axis):
    n = lax.axis_size(axis)
    rows = back.shape[0] // n
    sent = back.astype(jnp.bfloat16)
    total = back[:rows]
    for step in range(1, n):
        block = sent[step * rows : (step + 1) * rows]
        total = total + shifted(block, axis, n - step).astype(jnp.float32)
    return total


def plain(acts, grad_out, w_gate, w_up, w_down):
    x = own_first(lax.all_gather(acts, "hid", axis=1, tiled=True), "tok")
    dy = own_first(lax.all_gather(grad_out, "hid", axis=1, tiled=True), "tok")
    gate = summed(rows_by_cols(x, w_gate).astype(jnp.bfloat16), "wid")
    up = summed(rows_by_cols(x, w_up).astype(jnp.bfloat16), "wid")
    dhid = summed(over_cols(dy, w_down).astype(jnp.bfloat16), "wid")
    hidden, d_gate, d_up = swiglu_grads(gate, up, dhid)
    back = home_rows(over_cols(d_gate, w_gate) + over_cols(d_up, w_up), "tok").astype(jnp.bfloat16)
    back = lax.psum_scatter(back, "hid", scatter_dimension=1, tiled=True)
    return (
        back,
        over_rows(x, d_gate).astype(jnp.bfloat16),
        over_rows(x, d_up).astype(jnp.bfloat16),
        over_rows(hidden, dy).astype(jnp.bfloat16),
    )


def nothing(*refs):
    pass


def ordered(value, *after):
    anywhere = pl.BlockSpec(memory_space=pl.ANY)
    return pl.pallas_call(
        nothing,
        out_shape=jax.ShapeDtypeStruct(value.shape, value.dtype),
        in_specs=[anywhere] * (1 + len(after)),
        out_specs=anywhere,
        input_output_aliases={0: 0},
    )(value, *after)


def arrange(value, far, near):
    me = lax.axis_index("hid")
    width = value.shape[1]
    own = (value, far)
    other = (near[:, :width], near[:, width:])
    odd, upper = lax.rem(me, 2) == 1, me >= 2
    blocks = []
    for pair in range(2):
        blocks.append(jnp.where(odd, other[pair], own[pair]))
        blocks.append(jnp.where(odd, own[pair], other[pair]))
    return jnp.concatenate([jnp.where(upper, blocks[i ^ 2], blocks[i]) for i in range(4)], axis=1)


def scatter_cols(value):
    me = lax.axis_index("hid")
    width = value.shape[1] // 4
    odd, upper = lax.rem(me, 2) == 1, me >= 2
    blocks = [value[:, i * width : (i + 1) * width] for i in range(4)]
    keep = [jnp.where(odd, blocks[2 * i + 1], blocks[2 * i]) for i in range(2)]
    give = [jnp.where(odd, blocks[2 * i], blocks[2 * i + 1]) for i in range(2)]
    near = swapped(jnp.concatenate(give, axis=1).astype(jnp.bfloat16), "hid", 1).astype(jnp.float32)
    sums = [keep[i] + near[:, i * width : (i + 1) * width] for i in range(2)]
    mine = jnp.where(upper, sums[1], sums[0])
    theirs = jnp.where(upper, sums[0], sums[1])
    return (mine + swapped(theirs.astype(jnp.bfloat16), "hid", 2).astype(jnp.float32)).astype(jnp.bfloat16)


def load_all(pairs, sem):
    copies = [pltpu.make_async_copy(source, target, sem.at[i]) for i, (source, target) in enumerate(pairs)]
    for copy in copies:
        copy.start()
    for copy in copies:
        copy.wait()


def columns_kernel(heights, starts, width, n_old, *refs):
    count = len(heights)
    x_refs, g_refs, u_refs = refs[:count], refs[count : 2 * count], refs[2 * count : 3 * count]
    gate_ref, up_ref, x_all, g_all, u_all, sem = refs[3 * count + n_old :]
    step = pl.program_id(0)

    @pl.when(step == 0)
    def _():
        pairs, top = [], 0
        for c, height in enumerate(heights):
            rows = pl.ds(top, height)
            pairs.append((x_refs[c], x_all.at[rows]))
            pairs.append((g_refs[c].at[:, pl.ds(starts[c], width)], g_all.at[rows]))
            pairs.append((u_refs[c].at[:, pl.ds(starts[c], width)], u_all.at[rows]))
            top += height
        load_all(pairs, sem)

    block = gate_ref.shape[0]
    x = x_all[:, pl.ds(pl.multiple_of(step * block, block), block)]
    gate_ref[...] = over_rows(x, g_all[...]).astype(gate_ref.dtype)
    up_ref[...] = over_rows(x, u_all[...]).astype(up_ref.dtype)


def column_grads(xs, gs, us, starts, part, parts, total, old):
    heights = [x.shape[0] for x in xs]
    tokens, features, width = sum(heights), xs[0].shape[1], total // parts
    block = 256
    anywhere = pl.BlockSpec(memory_space=pl.ANY)
    shape = jax.ShapeDtypeStruct((features, total), jnp.bfloat16)
    spec = pl.BlockSpec((block, width), lambda i: (i, part))
    first = 3 * len(xs)
    return pl.pallas_call(
        functools.partial(columns_kernel, heights, starts, width, len(old)),
        grid=(features // block,),
        out_shape=(shape, shape),
        in_specs=[anywhere] * (first + len(old)),
        out_specs=(spec, spec),
        scratch_shapes=[
            pltpu.VMEM((tokens, features), jnp.bfloat16),
            pltpu.VMEM((tokens, width), jnp.bfloat16),
            pltpu.VMEM((tokens, width), jnp.bfloat16),
            pltpu.SemaphoreType.DMA((first,)),
        ],
        input_output_aliases={first + i: i for i in range(len(old))},
        compiler_params=pltpu.CompilerParams(vmem_limit_bytes=20 * MIB),
        cost_estimate=pl.CostEstimate(
            flops=4 * tokens * features * width, bytes_accessed=4 * features * width, transcendentals=0
        ),
    )(*xs, *gs, *us, *old)


def rows_kernel(heights, starts, width, n_old, *refs):
    count = len(heights)
    h_refs, y_refs = refs[:count], refs[count : 2 * count]
    out_ref, h_all, y_all, sem = refs[2 * count + n_old :]
    step = pl.program_id(0)

    @pl.when(step == 0)
    def _():
        pairs, top = [], 0
        for c, height in enumerate(heights):
            rows = pl.ds(top, height)
            pairs.append((h_refs[c].at[:, pl.ds(starts[c], width)], h_all.at[rows]))
            pairs.append((y_refs[c], y_all.at[rows]))
            top += height
        load_all(pairs, sem)

    block = out_ref.shape[0]
    h = h_all[:, pl.ds(pl.multiple_of(step * block, block), block)]
    out_ref[...] = over_rows(h, y_all[...]).astype(out_ref.dtype)


def row_grads(hs, ys, starts, part, parts, total, old):
    heights = [y.shape[0] for y in ys]
    tokens, features, width = sum(heights), ys[0].shape[1], total // parts
    block = 128
    steps = width // block
    anywhere = pl.BlockSpec(memory_space=pl.ANY)
    first = 2 * len(ys)
    return pl.pallas_call(
        functools.partial(rows_kernel, heights, starts, width, len(old)),
        grid=(steps,),
        out_shape=jax.ShapeDtypeStruct((total, features), jnp.bfloat16),
        in_specs=[anywhere] * (first + len(old)),
        out_specs=pl.BlockSpec((block, features), lambda i: (part * steps + i, 0)),
        scratch_shapes=[
            pltpu.VMEM((tokens, width), jnp.bfloat16),
            pltpu.VMEM((tokens, features), jnp.bfloat16),
            pltpu.SemaphoreType.DMA((first,)),
        ],
        input_output_aliases={first + i: i for i in range(len(old))},
        compiler_params=pltpu.CompilerParams(vmem_limit_bytes=20 * MIB),
        cost_estimate=pl.CostEstimate(
            flops=2 * tokens * features * width, bytes_accessed=2 * features * width, transcendentals=0
        ),
    )(*hs, *ys, *old)


def forward(x, dy, w_gate, w_up, w_down, cuts):
    parts = []
    for lower, upper in cuts:
        gate = rows_by_cols(x, w_gate[:, lower:upper]).astype(jnp.bfloat16)
        up = rows_by_cols(x, w_up[:, lower:upper]).astype(jnp.bfloat16)
        dhid = over_cols(dy, w_down[lower:upper]).astype(jnp.bfloat16)
        parts.append((gate, up, dhid))
    return parts


def piped(acts, grad_out, w_gate, w_up, w_down):
    unit = acts.shape[0] // sum(SIXTEENTHS)
    bounds = [0]
    for size in SIXTEENTHS:
        bounds.append(bounds[-1] + size * unit)
    spans = list(zip(bounds[:-1], bounds[1:]))
    last = len(spans) - 1
    total = w_gate.shape[1]
    whole, halves = [(0, total)], [(0, total // 2), (total // 2, total)]

    lower, upper = spans[0]
    ready = []
    for value in (acts[lower:upper], grad_out[lower:upper]):
        far = swapped(value, "hid", 2)
        near = swapped(jnp.concatenate([value, far], axis=1), "hid", 1)
        ready.append(own_first(arrange(value, far, near), "tok"))
    inputs = [tuple(ready)]
    sums = [forward(*ready, w_gate, w_up, w_down, whole)]
    anchor = sums[0][0]

    grads, backs = [], []

    def backward(index):
        results, back = [], None
        for (lower, upper), partial in zip(halves if index == last else whole, sums[index]):
            others = [shifted(part, "wid", 1) for part in partial]
            if index < last:
                others[0] = ordered(others[0], sums[index + 1][-1][2])
            gate, up, dhid = [
                part.astype(jnp.float32) + other.astype(jnp.float32) for part, other in zip(partial, others)
            ]
            hidden, d_gate, d_up = swiglu_grads(gate, up, dhid)
            term = over_cols(d_gate, w_gate[:, lower:upper]) + over_cols(d_up, w_up[:, lower:upper])
            back = term if back is None else back + term
            results.append((hidden, d_gate, d_up))
        grads.append(results)
        backs.append(scatter_cols(home_rows(back, "tok")))

    for index in range(1, len(spans)):
        lower, upper = spans[index]
        rows = upper - lower
        both = jnp.concatenate([acts[lower:upper], grad_out[lower:upper]], axis=0)
        both = ordered(both, anchor[0] if index == 1 else near)
        far = swapped(both, "hid", 2)
        far = ordered(far, anchor[2])
        near = swapped(jnp.concatenate([both, far], axis=1), "hid", 1)
        mixed = arrange(both, far, near)
        theirs = shifted(mixed, "tok", 1)
        x = jnp.concatenate([mixed[:rows], theirs[:rows]], axis=0)
        dy = jnp.concatenate([mixed[rows:], theirs[rows:]], axis=0)
        inputs.append((x, dy))
        sums.append(forward(x, dy, w_gate, w_up, w_down, halves if index == last else whole))
        anchor = sums[index][0]
    for index in range(len(spans)):
        backward(index)

    xs, dys = [x for x, _ in inputs], [dy for _, dy in inputs]
    columns, rows = (), ()
    for part in range(2):
        starts = [part * (total // 2)] * last + [0]
        hs, gs, us = [[g[0][i] for g in grads[:last]] + [grads[last][part][i]] for i in range(3)]
        columns = column_grads(xs, gs, us, starts, part, 2, total, columns)
        rows = (row_grads(hs, dys, starts, part, 2, total, rows),)
    return jnp.concatenate(backs, axis=0), columns[0], columns[1], rows[0]


def shards(acts, grad_out, w_gate, w_up, w_down):
    sizes = tuple(lax.axis_size(axis) for axis in ("hid", "wid", "tok"))
    aligned = acts.shape[0] % (16 * sum(SIXTEENTHS)) == 0 and acts.shape[1] % 128 == 0 and w_gate.shape[1] % 256 == 0
    if sizes == (4, 2, 2) and aligned:
        return piped(acts, grad_out, w_gate, w_up, w_down)
    return plain(acts, grad_out, w_gate, w_up, w_down)


def solution(mesh):
    placed = (
        P(("groups", "tok"), ("wid", "hid")),
        P(("groups", "tok"), ("wid", "hid")),
        P("wid", ("hid", "tok")),
        P("wid", ("hid", "tok")),
        P(("hid", "tok"), "wid"),
    )
    return jax.shard_map(
        shards,
        mesh=mesh,
        in_specs=placed,
        out_specs=(
            P(("groups", "tok"), ("wid", "hid")),
            P(("groups", "wid"), ("hid", "tok")),
            P(("groups", "wid"), ("hid", "tok")),
            P(("groups", "hid", "tok"), "wid"),
        ),
        check_vma=False,
    )
```

time: 290 us -> 223 us (0.77)
  waiting for transfers between devices: 108 us -> 34.3 us
  blocking collectives: 40.4 us -> 0 us
  starting transfers between devices: 0.39 us -> 40.7 us
  Pallas kernels: 0 us -> 27.3 us
  matrix products: 65.1 us -> 84.8 us
  other arithmetic: 42.1 us -> 22.8 us
  between operations: 13.9 us -> 1.66 us
  local copies, waits for them, and re-layouts: 20 us -> 10 us
    psum x1 -> x0, waiting for transfers between devices: 107 us -> none  [shards(): lax.psum(up_part.astype(jnp.bfloat16), 'wid').astype(jnp.float32)]
    ppermute x0 -> x42, starting transfers between devices: none -> 40.7 us  [the longest x18 24 us: swapped(): return lax.ppermute(value, axis, [(i, i ^ bit) for i in range(n)])]
    all_gather x2 -> x0, blocking collectives: 40.4 us -> none  [the longest x1 21.8 us: shards(): lax.all_gather(acts, 'hid', axis=1, tiled=True)]
    convert_element_type x3 -> x12, other arithmetic: 38.1 us -> 0.34 us  [the longest x4 0.2 us: scatter_cols(): theirs.astype(jnp.bfloat16)]
    ppermute x0 -> x42, waiting for transfers between devices: none -> 34.3 us  [the longest x18 29.4 us: swapped(): return lax.ppermute(value, axis, [(i, i ^ bit) for i in range(n)])]
    pallas_call x0 -> x13, Pallas kernels: none -> 27.3 us  [the longest x2 15.6 us: column_grads(): pl.pallas_call(functools.partial(columns_kernel, heights, starts, width,...]
    dot_general x11 -> x25, matrix products: 65.1 us -> 84.8 us  [dot(): lax.dot_general(left, right, (dims, ((), ())), preferred_element_type=jnp...]
    unnamed x18 -> x88, local copies, waits for them, and re-layouts: 20 us -> 3.72 us
  transfers between devices with their start and end apart: 5 -> 42, of which waited for: 1 -> 15; matrix products, arithmetic and copies ran while one was open for 36% -> 51% of each run, Pallas kernels for 0% -> 12%
where the time goes in v3:
time: 223 us; the launch traced here: 221 us
  matrix products  84.8 us (38%)
  starting transfers between devices  40.7 us (18%)
  waiting for transfers between devices  34.3 us (15%)
  Pallas kernels  27.3 us (12%)
  other arithmetic  22.8 us (10%)
  local copies, waits for them, and re-layouts  10 us (4%)
    dot_general x25, matrix products, dot(): lax.dot_general(left, right, (dims, ((), ())), preferred_element_type=jnp...  84.8 us
    ppermute x18, waiting for transfers between devices, swapped(): return lax.ppermute(value, axis, [(i, i ^ bit) for i in range(n)])  29.4 us
    ppermute x18, starting transfers between devices, swapped(): return lax.ppermute(value, axis, [(i, i ^ bit) for i in range(n)])  24 us
    ppermute x24, starting transfers between devices, shifted(): return lax.ppermute(value, axis, [(i, (i + step) % n) for i in range(n)])  16.7 us
    pallas_call x2, Pallas kernels, column_grads(): pl.pallas_call(functools.partial(columns_kernel, heights, starts, width,...  15.6 us
    pallas_call x2, Pallas kernels, row_grads(): pl.pallas_call(functools.partial(rows_kernel, heights, starts, width, len...  11.7 us
    convert_element_type x5, other arithmetic, swiglu_grads(): hidden = (gate * sig * up).astype(jnp.bfloat16)  7.98 us
    ppermute x24, waiting for transfers between devices, shifted(): return lax.ppermute(value, axis, [(i, (i + step) % n) for i in range(n)])  4.82 us
  transfers between devices with their start and end apart: 42, of which 15 were waited for; matrix products, arithmetic and copies ran while one was open for 51% of the time, Pallas kernels for 12%

profile of v3, /device:TPU:0, one launch (start us, length us, event | category | flops | bytes accessed | tf_op | source)
XLA Modules:
  0.0 221.5 jit_solution(1001620843873481011)
XLA Ops:
  1.4 4.0 %collective-permute-start.4 = (bf16[32,512]{1,0:T(8,128)(2,1)S(1)}, bf16[32,512]{1,0:T(8,128)(2,1)S(1)}, u32[]{:S(2)}, u32[]{:S(2)}) collective-permute-start(bf16[32,512]{1,0:T(8,128)(2,1)S(1)} %slice.211), channel_id=1, source_target_pairs={{0,8},{4,12},{8,0},{12,4},{1,9},{5,13},{9,1},{13,5},{2,10},{6,14},... | collective-permute-start | bytes 98312 | tf_op jit(solution)/shard_map/ppermute | solution.py:45
  11.5 2.0 collective-permute-start.5
  13.7 2.8 %collective-permute-done.5 = bf16[32,1024]{1,0:T(8,128)(2,1)S(1)} collective-permute-done((bf16[32,1024]{1,0:T(8,128)(2,1)S(1)}, bf16[32,1024]{1,0:T(8,128)(2,1)S(1)}, u32[]{:S(2)}, u32[]{:S(2)}) %collective-permute-start.5) | collective-permute-done | bytes 65568 | tf_op jit(solution)/shard_map/ppermute | solution.py:45
  18.8 5.1 %convolution_convert_fusion.6.refs_1_ = bf16[64,1792]{1,0:T(8,128)(2,1)} fusion(bf16[2048,1792]{1,0:T(8,128)(2,1)} %param.7, bf16[32,2048]{1,0:T(8,128)(2,1)S(1)} %collective-permute-done.6, bf16[32,512]{1,0:T(8,128)(2,1)S(1)} %get-tuple-element.76, bf16[32,512]{1,0:T(8,128)(2,1)S(1)} %get-tuple-element.75, bf16[32,512]{1,0:T(8,128)(2,1)S(1)} %get-tuple-element.74, ...), kind=kOutput, calls=%fused_computation.32 | convolution fusion | flops 471187456 | bytes 7831552 | tf_op jit(solution)/shard_map/dot_general | solution.py:15
  23.9 1.5 collective-permute-start.8
  25.4 2.6 %collective-permute-start.9 = (bf16[96,512]{1,0:T(8,128)(2,1)}, bf16[96,512]{1,0:T(8,128)(2,1)S(1)}, u32[]{:S(2)}, u32[]{:S(2)}) collective-permute-start(bf16[96,512]{1,0:T(8,128)(2,1)} %shard_map.84), channel_id=1, source_target_pairs={{0,8},{4,12},{8,0},{12,4},{1,9},{5,13},{9,1},{13,5},{2,10},{6,14},... | collective-permute-start | bytes 294920 | tf_op jit(solution)/shard_map/ppermute | solution.py:45
  28.0 4.5 %convolution_convert_fusion.7 = bf16[64,1792]{1,0:T(8,128)(2,1)S(1)} fusion(bf16[2048,1792]{1,0:T(8,128)(2,1)} %param.8, bf16[32,2048]{1,0:T(8,128)(2,1)S(1)} %collective-permute-done.6, bf16[32,512]{1,0:T(8,128)(2,1)S(1)} %get-tuple-element.76, bf16[32,512]{1,0:T(8,128)(2,1)S(1)} %get-tuple-element.75, bf16[32,512]{1,0:T(8,128)(2,1)S(1)} %get-tuple-element.74, ...), kind=kOutput, calls=%fused_computation.33 | convolution fusion | flops 471187456 | bytes 7831552 | tf_op jit(solution)/shard_map/dot_general | solution.py:15
  33.1 6.1 %convolution_convert_fusion.8.refs_1_ = bf16[64,1792]{1,0:T(8,128)(2,1)} fusion(bf16[1792,2048]{1,0:T(8,128)(2,1)} %param.9, bf16[32,2048]{1,0:T(8,128)(2,1)S(1)} %collective-permute-done.2, bf16[32,512]{1,0:T(8,128)(2,1)S(1)} %get-tuple-element.72, bf16[32,512]{1,0:T(8,128)(2,1)S(1)} %get-tuple-element.71, bf16[32,512]{1,0:T(8,128)(2,1)S(1)} %get-tuple-element.70, ...), kind=kOutput, calls=%fused_computation.34 | convolution fusion | flops 471187456 | bytes 7831552 | tf_op jit(solution)/shard_map/dot_general | solution.py:15
  39.2 1.5 collective-permute-start.3
  44.3 4.9 %collective-permute-done.10.refs_1_ = bf16[96,1024]{1,0:T(8,128)(2,1)S(1)} collective-permute-done((bf16[96,1024]{1,0:T(8,128)(2,1)S(1)}, bf16[96,1024]{1,0:T(8,128)(2,1)S(1)}, u32[]{:S(2)}, u32[]{:S(2)}) %collective-permute-start.10) | collective-permute-done | bytes 196640 | tf_op jit(solution)/shard_map/ppermute | solution.py:45
  51.4 1.7 collective-permute-done.11
  53.1 4.5 %convolution_convert_fusion.4 = bf16[96,1792]{1,0:T(8,128)(2,1)S(1)} fusion(bf16[2048,1792]{1,0:T(8,128)(2,1)} %param.8, bf16[48,2048]{1,0:T(8,128)(2,1)S(1)} %get-tuple-element.53, bf16[48,2048]{1,0:T(8,128)(2,1)S(1)} %get-tuple-element.51), kind=kOutput, calls=%fused_computation.29 | convolution fusion | flops 705601536 | bytes 8077312 | tf_op jit(solution)/shard_map/dot_general | solution.py:15
  57.6 4.5 %convolution_convert_fusion.3 = bf16[96,1792]{1,0:T(8,128)(2,1)S(1)} fusion(bf16[2048,1792]{1,0:T(8,128)(2,1)} %param.7, bf16[48,2048]{1,0:T(8,128)(2,1)S(1)} %get-tuple-element.53, bf16[48,2048]{1,0:T(8,128)(2,1)S(1)} %get-tuple-element.51), kind=kOutput, calls=%fused_computation.28 | convolution fusion | flops 705601536 | bytes 8077312 | tf_op jit(solution)/shard_map/dot_general | solution.py:15
  62.2 3.1 %convolution_convert_fusion.5.refs_1_ = bf16[96,1792]{1,0:T(8,128)(2,1)} fusion(bf16[1792,2048]{1,0:T(8,128)(2,1)S(1)} %bitcast.36, bf16[48,2048]{1,0:T(8,128)(2,1)S(1)} %get-tuple-element.54, bf16[48,2048]{1,0:T(8,128)(2,1)S(1)} %get-tuple-element.52), kind=kOutput, calls=%fused_computation.30 | convolution fusion | flops 705601536 | bytes 8077312 | tf_op jit(solution)/shard_map/dot_general | solution.py:15
  66.5 1.6 pad_maximum_fusion.11
  69.7 1.7 multiply_convert_fusion.6
  71.4 5.4 %fusion.55 = f32[64,2048]{1,0:T(8,128)S(1)} fusion(bf16[64,1792]{1,0:T(8,128)(2,1)S(1)} %get-tuple-element.31.refs_4_, bf16[2048,1792]{1,0:T(8,128)(2,1)} %param.7), kind=kOutput, calls=%fused_computation.182 | convolution fusion | flops 469762048 | bytes 8093696 | tf_op jit(solution)/shard_map/dot_general | solution.py:15
  76.8 5.4 %convolution_add_fusion.2 = f32[64,2048]{1,0:T(8,128)S(1)} fusion(f32[64,2048]{1,0:T(8,128)S(1)} %fusion.55, bf16[64,1792]{1,0:T(8,128)(2,1)S(1)} %get-tuple-element.32.refs_8_, bf16[2048,1792]{1,0:T(8,128)(2,1)} %param.8), kind=kOutput, calls=%fused_computation.31 | convolution fusion | flops 469893120 | bytes 8617984 | tf_op jit(solution)/shard_map/dot_general | solution.py:15
  85.0 1.6 collective-permute-start.16
  88.2 2.7 %collective-permute-start.14 = (bf16[32,512]{1,0:T(8,128)(2,1)S(1)}, bf16[32,512]{1,0:T(8,128)(2,1)S(1)}, u32[]{:S(2)}, u32[]{:S(2)}) collective-permute-start(bf16[32,512]{1,0:T(8,128)(2,1)S(1)} %get-tuple-element.12), channel_id=1, source_target_pairs={{0,8},{4,12},{8,0},{12,4},{1,9},{5,13},{9,1},{13,5},{2,10},{6,14},... | collective-permute-start | bytes 98312 | tf_op jit(solution)/shard_map/ppermute | solution.py:45
  91.2 1.8 collective-permute-done.14
  93.1 2.7 %collective-permute-start.27 = (bf16[96,512]{1,0:T(8,128)(2,1)}, bf16[96,512]{1,0:T(8,128)(2,1)S(1)}, u32[]{:S(2)}, u32[]{:S(2)}) collective-permute-start(bf16[96,512]{1,0:T(8,128)(2,1)} %shard_map.90), channel_id=1, source_target_pairs={{0,8},{4,12},{8,0},{12,4},{1,9},{5,13},{9,1},{13,5},{2,10},{6,14},... | collective-permute-start | bytes 294920 | tf_op jit(solution)/shard_map/ppermute | solution.py:45
  97.1 5.4 %convolution_convert_fusion.1 = bf16[128,1792]{1,0:T(8,128)(2,1)} fusion(bf16[2048,1792]{1,0:T(8,128)(2,1)} %param.8, bf16[64,2048]{1,0:T(8,128)(2,1)S(1)} %get-tuple-element.43, bf16[64,2048]{1,0:T(8,128)(2,1)S(1)} %get-tuple-element.41), kind=kOutput, calls=%fused_computation.25 | convolution fusion | flops 940802048 | bytes 8323072 | tf_op jit(solution)/shard_map/dot_general | solution.py:15
  102.5 2.0 convolution_convert_fusion
  104.5 3.3 %convolution_convert_fusion.2.refs_1_ = bf16[128,1792]{1,0:T(8,128)(2,1)} fusion(bf16[1792,2048]{1,0:T(8,128)(2,1)S(1)} %bitcast.38, bf16[64,2048]{1,0:T(8,128)(2,1)S(1)} %get-tuple-element.44, bf16[64,2048]{1,0:T(8,128)(2,1)S(1)} %get-tuple-element.42), kind=kOutput, calls=%fused_computation.26 | convolution fusion | flops 940802048 | bytes 8323072 | tf_op jit(solution)/shard_map/dot_general | solution.py:15
  107.8 1.5 collective-permute-start.24
  110.0 1.6 pad_maximum_fusion.13
  115.8 1.9 multiply_convert_fusion.3
  117.7 5.5 %fusion.56 = f32[96,2048]{1,0:T(8,128)S(1)} fusion(bf16[96,1792]{1,0:T(8,128)(2,1)S(1)} %get-tuple-element.28.refs_5_, bf16[2048,1792]{1,0:T(8,128)(2,1)} %param.7), kind=kOutput, calls=%fused_computation.183 | convolution fusion | flops 704643072 | bytes 8470528 | tf_op jit(solution)/shard_map/dot_general | solution.py:15
  123.2 5.6 %convolution_add_fusion.1 = f32[96,2048]{1,0:T(8,128)S(1)} fusion(f32[96,2048]{1,0:T(8,128)S(1)} %fusion.56, bf16[96,1792]{1,0:T(8,128)(2,1)S(1)} %get-tuple-element.29.refs_9_, bf16[2048,1792]{1,0:T(8,128)(2,1)} %param.8), kind=kOutput, calls=%fused_computation.27 | convolution fusion | flops 704839680 | bytes 9256960 | tf_op jit(solution)/shard_map/dot_general | solution.py:15
  132.5 2.8 %collective-permute-done.22 = bf16[48,1024]{1,0:T(8,128)(2,1)S(1)} collective-permute-done((bf16[48,1024]{1,0:T(8,128)(2,1)S(1)}, bf16[48,1024]{1,0:T(8,128)(2,1)S(1)}, u32[]{:S(2)}, u32[]{:S(2)}) %collective-permute-start.22) | collective-permute-done | bytes 98336 | tf_op jit(solution)/shard_map/ppermute | solution.py:45
  135.9 5.1 %collective-permute-done.23 = bf16[48,512]{1,0:T(8,128)(2,1)S(1)} collective-permute-done((bf16[48,512]{1,0:T(8,128)(2,1)S(1)}, bf16[48,512]{1,0:T(8,128)(2,1)S(1)}, u32[]{:S(2)}, u32[]{:S(2)}) %collective-permute-start.23) | collective-permute-done | bytes 49184 | tf_op jit(solution)/shard_map/ppermute | solution.py:45
  145.3 1.4 fusion.32
  148.7 1.9 fusion.41.refs_1_
  152.4 3.8 %fusion.44 = bf16[96,896]{1,0:T(8,128)(2,1)S(1)} fusion(bf16[1792,2048]{1,0:T(8,128)(2,1)} %param.9, bf16[48,2048]{1,0:T(8,128)(2,1)} %copy-done.22, bf16[48,2048]{1,0:T(8,128)(2,1)} %copy-done.20), kind=kOutput, calls=%fused_computation.40 | convolution fusion | flops 353193984 | bytes 4235264 | tf_op jit(solution)/shard_map/dot_general | solution.py:15
  158.4 2.4 %multiply_convert_fusion = (bf16[128,1792]{1,0:T(8,128)(2,1)S(1)}, bf16[128,1792]{1,0:T(8,128)(2,1)S(1)}, bf16[128,1792]{1,0:T(8,128)(2,1)S(1)}) fusion(bf16[128,1792]{1,0:T(8,128)(2,1)} %collective-permute-done.25, bf16[128,1792]{1,0:T(8,128)(2,1)} %convolution_convert_fusion.1, bf16[128,1792]{1,0:T(8,128)(2,1)} %shard_map.92, ...), kind=kLoop, calls=%fused_computation.41 | loop fusion | flops 5734400 | bytes 4128768 | tf_op jit(solution)/shard_map/convert_element_type | solution.py:32
  160.8 5.7 %fusion.57 = f32[128,2048]{1,0:T(8,128)S(1)} fusion(bf16[128,1792]{1,0:T(8,128)(2,1)S(1)} %get-tuple-element.25.refs_6_, bf16[2048,1792]{1,0:T(8,128)(2,1)} %param.7), kind=kOutput, calls=%fused_computation.184 | convolution fusion | flops 939524096 | bytes 8847360 | tf_op jit(solution)/shard_map/dot_general | solution.py:15
  166.6 2.5 %convolution_add_fusion = f32[128,2048]{1,0:T(8,128)S(1)} fusion(f32[128,2048]{1,0:T(8,128)S(1)} %fusion.57, bf16[128,1792]{1,0:T(8,128)(2,1)S(1)} %get-tuple-element.26.refs_10_, bf16[2048,1792]{1,0:T(8,128)(2,1)S(1)} %bitcast.28), kind=kOutput, calls=%fused_computation.20 | convolution fusion | flops 939786240 | bytes 9895936 | tf_op jit(solution)/shard_map/dot_general | solution.py:15
  170.6 1.6 multiply_convert_fusion.10
  178.8 5.9 %shard_map.95.refs_8_ = bf16[1792,2048]{1,0:T(8,128)(2,1)} custom-call(bf16[64,1792]{1,0:T(8,128)(2,1)S(1)} %get-tuple-element.30.refs_0_, bf16[96,1792]{1,0:T(8,128)(2,1)S(1)} %get-tuple-element.27.refs_1_, bf16[128,1792]{1,0:T(8,128)(2,1)S(1)} %get-tuple-element.24.refs_2_, bf16[96,896]{1,0:T(8,128)(2,1)S(1)} %get-tuple-element.33.refs_3_, ...), custom_call_target="tpu_custom_call" | custom-call | flops 1409286144 | bytes 3670016 | tf_op jit(solution)/shard_map/pallas_call | solution.py:216
  184.7 5.9 %shard_map.96 = bf16[1792,2048]{1,0:T(8,128)(2,1)} custom-call(bf16[64,1792]{1,0:T(8,128)(2,1)S(1)} %get-tuple-element.30.refs_0_, bf16[96,1792]{1,0:T(8,128)(2,1)S(1)} %get-tuple-element.27.refs_1_, bf16[128,1792]{1,0:T(8,128)(2,1)S(1)} %get-tuple-element.24.refs_2_, bf16[96,896]{1,0:T(8,128)(2,1)S(1)} %get-tuple-element.36.refs_3_, ...), custom_call_target="tpu_custom_call", output_to_operand_aliasing={{}: (8, {})} | custom-call | flops 1409286144 | bytes 3670016 | tf_op jit(solution)/shard_map/pallas_call | solution.py:216
  190.6 7.8 %shard_map.93 = (bf16[2048,1792]{1,0:T(8,128)(2,1)}, bf16[2048,1792]{1,0:T(8,128)(2,1)}) custom-call(bf16[64,2048]{1,0:T(8,128)(2,1)S(1)} %copy-done.1, bf16[96,2048]{1,0:T(8,128)(2,1)S(1)} %copy-done, bf16[128,2048]{1,0:T(8,128)(2,1)S(1)} %pad_maximum_fusion.2.refs_2_, bf16[96,2048]{1,0:T(8,128)(2,1)S(1)} %pad_maximum_fusion.8.refs_3_, ...), custom_call_target="tpu_custom_call" | custom-call | flops 2818572288 | bytes 7340032 | tf_op jit(solution)/shard_map/pallas_call | solution.py:168
  198.4 7.8 %shard_map.94 = (bf16[2048,1792]{1,0:T(8,128)(2,1)}, bf16[2048,1792]{1,0:T(8,128)(2,1)}) custom-call(bf16[64,2048]{1,0:T(8,128)(2,1)S(1)} %copy-done.1, bf16[96,2048]{1,0:T(8,128)(2,1)S(1)} %copy-done, bf16[128,2048]{1,0:T(8,128)(2,1)S(1)} %pad_maximum_fusion.2.refs_2_, ...), custom_call_target="tpu_custom_call", output_to_operand_aliasing={{0}: (12, {}), {1}: (13, {})} | custom-call | flops 2818572288 | bytes 7340032 | tf_op jit(solution)/shard_map/pallas_call | solution.py:168
  207.0 1.6 collective-permute-start.40
  208.6 4.1 %collective-permute-done.31 = bf16[64,1024]{1,0:T(8,128)(2,1)S(1)} collective-permute-done((bf16[64,1024]{1,0:T(8,128)(2,1)S(1)}, bf16[64,1024]{1,0:T(8,128)(2,1)S(1)}, u32[]{:S(2)}, u32[]{:S(2)}) %collective-permute-start.31) | collective-permute-done | bytes 131104 | tf_op jit(solution)/shard_map/ppermute | solution.py:45
  212.9 1.5 collective-permute-done.40
  214.5 1.5 collective-permute-start.41
  215.9 4.3 %collective-permute-done.32 = bf16[64,512]{1,0:T(8,128)(2,1)S(1)} collective-permute-done((bf16[64,512]{1,0:T(8,128)(2,1)S(1)}, bf16[64,512]{1,0:T(8,128)(2,1)S(1)}, u32[]{:S(2)}, u32[]{:S(2)}) %collective-permute-start.32) | collective-permute-done | bytes 65568 | tf_op jit(solution)/shard_map/ppermute | solution.py:45
  (242 shorter events, 53.7 us)
Async XLA Ops:
  1.4 10.1 %collective-permute-start.4 = (bf16[32,512]{1,0:T(8,128)(2,1)S(1)}, bf16[32,512]{1,0:T(8,128)(2,1)S(1)}, u32[]{:S(2)}, u32[]{:S(2)}) collective-permute-start(bf16[32,512]{1,0:T(8,128)(2,1)S(1)} %slice.211), channel_id=1, source_target_pairs={{0,8},{4,12},{8,0},{12,4},{1,9},{5,13},{9,1},{13,5},{2,10},{6,14},... | collective-permute-start | bytes 98312 | tf_op jit(solution)/shard_map/ppermute | solution.py:45
  6.2 7.3 %collective-permute-start = (bf16[32,512]{1,0:T(8,128)(2,1)S(1)}, bf16[32,512]{1,0:T(8,128)(2,1)S(1)}, u32[]{:S(2)}, u32[]{:S(2)}) collective-permute-start(bf16[32,512]{1,0:T(8,128)(2,1)S(1)} %slice.208), channel_id=1, source_target_pairs={{0,8},{4,12},{8,0},{12,4},{1,9},{5,13},{9,1},{13,5},{2,10},{6,14},... | collective-permute-start | bytes 98312 | tf_op jit(solution)/shard_map/ppermute | solution.py:45
  11.5 5.0 %collective-permute-start.5 = (bf16[32,1024]{1,0:T(8,128)(2,1)S(1)}, bf16[32,1024]{1,0:T(8,128)(2,1)S(1)}, u32[]{:S(2)}, u32[]{:S(2)}) collective-permute-start(bf16[32,1024]{1,0:T(8,128)(2,1)S(1)} %pad_maximum_fusion.24), channel_id=1, source_target_pairs={{0,4},{4,0},{8,12},{12,8},{1,5},{5,1},{9,13},{13,9},{2,6},{6,2},{1... | collective-permute-start | bytes 196616 | tf_op jit(solution)/shard_map/ppermute | solution.py:45
  13.5 4.3 %collective-permute-start.1 = (bf16[32,1024]{1,0:T(8,128)(2,1)S(1)}, bf16[32,1024]{1,0:T(8,128)(2,1)S(1)}, u32[]{:S(2)}, u32[]{:S(2)}) collective-permute-start(bf16[32,1024]{1,0:T(8,128)(2,1)S(1)} %pad_maximum_fusion.23), channel_id=1, source_target_pairs={{0,4},{4,0},{8,12},{12,8},{1,5},{5,1},{9,13},{13,9},{2,6},{6,2},{1... | collective-permute-start | bytes 196616 | tf_op jit(solution)/shard_map/ppermute | solution.py:45
  17.3 1.4 collective-permute-start.6
  18.6 14.5 %collective-permute-start.2 = (bf16[32,2048]{1,0:T(8,128)(2,1)S(1)}, bf16[32,2048]{1,0:T(8,128)(2,1)S(1)}, u32[]{:S(2)}, u32[]{:S(2)}) collective-permute-start(bf16[32,2048]{1,0:T(8,128)(2,1)S(1)} %pad_maximum_fusion.15), channel_id=1, source_target_pairs={{0,1},{1,0},{2,3},{3,2},{4,5},{5,4},{6,7},{7,6},{8,9},{9,8},{10,11... | collective-permute-start | bytes 393224 | tf_op jit(solution)/shard_map/ppermute | solution.py:40
  23.9 45.1 %collective-permute-start.8 = (bf16[64,1792]{1,0:T(8,128)(2,1)}, bf16[64,1792]{1,0:T(8,128)(2,1)S(1)}, u32[]{:S(2)}, u32[]{:S(2)}) collective-permute-start(bf16[64,1792]{1,0:T(8,128)(2,1)} %convolution_convert_fusion.6.refs_1_), channel_id=1, source_target_pairs={{0,2},{2,0},{1,3},{3,1},{4,6},{6,4},{5,7},{7,5},{8,10},{10,8},{9,1... | collective-permute-start | bytes 688136 | tf_op jit(solution)/shard_map/ppermute | solution.py:40
  25.4 16.0 %collective-permute-start.9 = (bf16[96,512]{1,0:T(8,128)(2,1)}, bf16[96,512]{1,0:T(8,128)(2,1)S(1)}, u32[]{:S(2)}, u32[]{:S(2)}) collective-permute-start(bf16[96,512]{1,0:T(8,128)(2,1)} %shard_map.84), channel_id=1, source_target_pairs={{0,8},{4,12},{8,0},{12,4},{1,9},{5,13},{9,1},{13,5},{2,10},{6,14},... | collective-permute-start | bytes 294920 | tf_op jit(solution)/shard_map/ppermute | solution.py:45
  32.5 37.2 %collective-permute-start.7 = (bf16[64,1792]{1,0:T(8,128)(2,1)S(1)}, bf16[64,1792]{1,0:T(8,128)(2,1)}, u32[]{:S(2)}, u32[]{:S(2)}) collective-permute-start(bf16[64,1792]{1,0:T(8,128)(2,1)S(1)} %convolution_convert_fusion.7), channel_id=1, source_target_pairs={{0,2},{2,0},{1,3},{3,1},{4,6},{6,4},{5,7},{7,5},{8,10},{10,8},{9,1... | collective-permute-start | bytes 688136 | tf_op jit(solution)/shard_map/ppermute | solution.py:40
  39.2 30.5 %collective-permute-start.3 = (bf16[64,1792]{1,0:T(8,128)(2,1)}, bf16[64,1792]{1,0:T(8,128)(2,1)}, u32[]{:S(2)}, u32[]{:S(2)}) collective-permute-start(bf16[64,1792]{1,0:T(8,128)(2,1)} %convolution_convert_fusion.8.refs_1_), channel_id=1, source_target_pairs={{0,2},{2,0},{1,3},{3,1},{4,6},{6,4},{5,7},{7,5},{8,10},{10,8},{9,1... | collective-permute-start | bytes 688136 | tf_op jit(solution)/shard_map/ppermute | solution.py:40
  43.0 6.2 %collective-permute-start.10 = (bf16[96,1024]{1,0:T(8,128)(2,1)S(1)}, bf16[96,1024]{1,0:T(8,128)(2,1)S(1)}, u32[]{:S(2)}, u32[]{:S(2)}) collective-permute-start(bf16[96,1024]{1,0:T(8,128)(2,1)S(1)} %pad_maximum_fusion.12), channel_id=1, source_target_pairs={{0,4},{4,0},{8,12},{12,8},{1,5},{5,1},{9,13},{13,9},{2,6},{6,2},{1... | collective-permute-start | bytes 589832 | tf_op jit(solution)/shard_map/ppermute | solution.py:45
  49.9 16.0 %collective-permute-start.18 = (bf16[128,512]{1,0:T(8,128)(2,1)}, bf16[128,512]{1,0:T(8,128)(2,1)S(1)}, u32[]{:S(2)}, u32[]{:S(2)}) collective-permute-start(bf16[128,512]{1,0:T(8,128)(2,1)} %shard_map.87), channel_id=1, source_target_pairs={{0,8},{4,12},{8,0},{12,4},{1,9},{5,13},{9,1},{13,5},{2,10},{6,14},... | collective-permute-start | bytes 393224 | tf_op jit(solution)/shard_map/ppermute | solution.py:45
  51.3 1.8 collective-permute-start.11
  62.2 24.4 %copy-start.9 = (bf16[96,1792]{1,0:T(8,128)(2,1)}, bf16[96,1792]{1,0:T(8,128)(2,1)S(1)}, u32[]{:S(2)}) copy-start(bf16[96,1792]{1,0:T(8,128)(2,1)S(1)} %convolution_convert_fusion.3) | copy-start | bytes 1032196
  65.3 50.5 %collective-permute-start.15 = (bf16[96,1792]{1,0:T(8,128)(2,1)}, bf16[96,1792]{1,0:T(8,128)(2,1)}, u32[]{:S(2)}, u32[]{:S(2)}) collective-permute-start(bf16[96,1792]{1,0:T(8,128)(2,1)} %convolution_convert_fusion.5.refs_1_), channel_id=1, source_target_pairs={{0,2},{2,0},{1,3},{3,1},{4,6},{6,4},{5,7},{7,5},{8,10},{10,8},{9,1... | collective-permute-start | bytes 1032200 | tf_op jit(solution)/shard_map/ppermute | solution.py:40
  68.1 22.7 %collective-permute-start.19 = (bf16[128,1024]{1,0:T(8,128)(2,1)}, bf16[128,1024]{1,0:T(8,128)(2,1)S(1)}, u32[]{:S(2)}, u32[]{:S(2)}) collective-permute-start(bf16[128,1024]{1,0:T(8,128)(2,1)} %pad_maximum_fusion.11), channel_id=1, source_target_pairs={{0,4},{4,0},{8,12},{12,8},{1,5},{5,1},{9,13},{13,9},{2,6},{6,2},{1... | collective-permute-start | bytes 786440 | tf_op jit(solution)/shard_map/ppermute | solution.py:45
  76.8 14.0 %copy-start.12 = (bf16[128,512]{1,0:T(8,128)(2,1)S(1)}, bf16[128,512]{1,0:T(8,128)(2,1)}, u32[]{:S(2)}) copy-start(bf16[128,512]{1,0:T(8,128)(2,1)} %shard_map.88) | copy-start | bytes 393220
  82.3 1.4 collective-permute-start.12
  83.8 4.3 %collective-permute-start.13 = (bf16[32,1024]{1,0:T(8,128)(2,1)S(1)}, bf16[32,1024]{1,0:T(8,128)(2,1)S(1)}, u32[]{:S(2)}, u32[]{:S(2)}) collective-permute-start(bf16[32,1024]{1,0:T(8,128)(2,1)S(1)} %pad_maximum_fusion.25), channel_id=1, source_target_pairs={{0,4},{4,0},{8,12},{12,8},{1,5},{5,1},{9,13},{13,9},{2,6},{6,2},{1... | collective-permute-start | bytes 196616 | tf_op jit(solution)/shard_map/ppermute | solution.py:45
  85.0 29.4 %collective-permute-start.16 = (bf16[96,1792]{1,0:T(8,128)(2,1)S(1)}, bf16[96,1792]{1,0:T(8,128)(2,1)}, u32[]{:S(2)}, u32[]{:S(2)}) collective-permute-start(bf16[96,1792]{1,0:T(8,128)(2,1)S(1)} %convolution_convert_fusion.4), channel_id=1, source_target_pairs={{0,2},{2,0},{1,3},{3,1},{4,6},{6,4},{5,7},{7,5},{8,10},{10,8},{9,1... | collective-permute-start | bytes 1032200 | tf_op jit(solution)/shard_map/ppermute | solution.py:40
  86.6 26.1 %collective-permute-start.17 = (bf16[96,1792]{1,0:T(8,128)(2,1)S(1)}, bf16[96,1792]{1,0:T(8,128)(2,1)S(1)}, u32[]{:S(2)}, u32[]{:S(2)}) collective-permute-start(bf16[96,1792]{1,0:T(8,128)(2,1)S(1)} %convolution_convert_fusion.3), channel_id=1, source_target_pairs={{0,2},{2,0},{1,3},{3,1},{4,6},{6,4},{5,7},{7,5},{8,10},{10,8},{9,1... | collective-permute-start | bytes 1032200 | tf_op jit(solution)/shard_map/ppermute | solution.py:40
  88.2 4.9 %collective-permute-start.14 = (bf16[32,512]{1,0:T(8,128)(2,1)S(1)}, bf16[32,512]{1,0:T(8,128)(2,1)S(1)}, u32[]{:S(2)}, u32[]{:S(2)}) collective-permute-start(bf16[32,512]{1,0:T(8,128)(2,1)S(1)} %get-tuple-element.12), channel_id=1, source_target_pairs={{0,8},{4,12},{8,0},{12,4},{1,9},{5,13},{9,1},{13,5},{2,10},{6,14},... | collective-permute-start | bytes 98312 | tf_op jit(solution)/shard_map/ppermute | solution.py:45
  90.9 4.9 %collective-permute-start.20 = (bf16[128,2048]{1,0:T(8,128)(2,1)S(1)}, bf16[128,2048]{1,0:T(8,128)(2,1)}, u32[]{:S(2)}, u32[]{:S(2)}) collective-permute-start(bf16[128,2048]{1,0:T(8,128)(2,1)S(1)} %pad_maximum_fusion), channel_id=1, source_target_pairs={{0,1},{1,0},{2,3},{3,2},{4,5},{5,4},{6,7},{7,6},{8,9},{9,8},{10,11... | collective-permute-start | bytes 1572872 | tf_op jit(solution)/shard_map/ppermute | solution.py:40
  93.1 16.2 %collective-permute-start.27 = (bf16[96,512]{1,0:T(8,128)(2,1)}, bf16[96,512]{1,0:T(8,128)(2,1)S(1)}, u32[]{:S(2)}, u32[]{:S(2)}) collective-permute-start(bf16[96,512]{1,0:T(8,128)(2,1)} %shard_map.90), channel_id=1, source_target_pairs={{0,8},{4,12},{8,0},{12,4},{1,9},{5,13},{9,1},{13,5},{2,10},{6,14},... | collective-permute-start | bytes 294920 | tf_op jit(solution)/shard_map/ppermute | solution.py:45
  107.8 49.8 %collective-permute-start.24 = (bf16[128,1792]{1,0:T(8,128)(2,1)}, bf16[128,1792]{1,0:T(8,128)(2,1)}, u32[]{:S(2)}, u32[]{:S(2)}) collective-permute-start(bf16[128,1792]{1,0:T(8,128)(2,1)} %convolution_convert_fusion.2.refs_1_), channel_id=1, source_target_pairs={{0,2},{2,0},{1,3},{3,1},{4,6},{6,4},{5,7},{7,5},{8,10},{10,8},{9,1... | collective-permute-start | bytes 1376264 | tf_op jit(solution)/shard_map/ppermute | solution.py:40
  111.6 19.9 %collective-permute-start.28 = (bf16[96,1024]{1,0:T(8,128)(2,1)}, bf16[96,1024]{1,0:T(8,128)(2,1)}, u32[]{:S(2)}, u32[]{:S(2)}) collective-permute-start(bf16[96,1024]{1,0:T(8,128)(2,1)} %pad_maximum_fusion.13), channel_id=1, source_target_pairs={{0,4},{4,0},{8,12},{12,8},{1,5},{5,1},{9,13},{13,9},{2,6},{6,2},{1... | collective-permute-start | bytes 589832 | tf_op jit(solution)/shard_map/ppermute | solution.py:45
  112.7 43.6 %collective-permute-start.25 = (bf16[128,1792]{1,0:T(8,128)(2,1)}, bf16[128,1792]{1,0:T(8,128)(2,1)}, u32[]{:S(2)}, u32[]{:S(2)}) collective-permute-start(bf16[128,1792]{1,0:T(8,128)(2,1)} %convolution_convert_fusion.1), channel_id=1, source_target_pairs={{0,2},{2,0},{1,3},{3,1},{4,6},{6,4},{5,7},{7,5},{8,10},{10,8},{9,1... | collective-permute-start | bytes 1376264 | tf_op jit(solution)/shard_map/ppermute | solution.py:40
  114.4 36.3 %collective-permute-start.26 = (bf16[128,1792]{1,0:T(8,128)(2,1)}, bf16[128,1792]{1,0:T(8,128)(2,1)}, u32[]{:S(2)}, u32[]{:S(2)}) collective-permute-start(bf16[128,1792]{1,0:T(8,128)(2,1)} %convolution_convert_fusion), channel_id=1, source_target_pairs={{0,2},{2,0},{1,3},{3,1},{4,6},{6,4},{5,7},{7,5},{8,10},{10,8},{9,1... | collective-permute-start | bytes 1376264 | tf_op jit(solution)/shard_map/ppermute | solution.py:40
  123.2 17.9 %slice-start = ((s8[7340032]{0:T(1024)(128)(4,1)}), s8[4194304]{0:T(1024)(128)(4,1)S(1)}, s32[]{:S(2)}) async-start(s8[7340032]{0:T(1024)(128)(4,1)} %bitcast.25), calls=%async_computation | async-start | bytes 8388608
  123.2 17.9 %slice-start.1 = ((s8[7340032]{0:T(1024)(128)(4,1)}), s8[3145728]{0:T(1024)(128)(4,1)S(1)}, s32[]{:S(2)}) async-start(s8[7340032]{0:T(1024)(128)(4,1)} %bitcast.25), calls=%async_computation.1 | async-start | bytes 6291456
  123.2 19.3 %slice-start.6 = ((s8[7340032]{0:T(1024)(128)(4,1)}), s8[4194304]{0:T(1024)(128)(4,1)S(1)}, s32[]{:S(2)}) async-start(s8[7340032]{0:T(1024)(128)(4,1)} %bitcast.31), calls=%async_computation.6 | async-start | bytes 8388608
  128.8 1.5 collective-permute-start.21
  130.4 4.9 %collective-permute-start.22 = (bf16[48,1024]{1,0:T(8,128)(2,1)S(1)}, bf16[48,1024]{1,0:T(8,128)(2,1)S(1)}, u32[]{:S(2)}, u32[]{:S(2)}) collective-permute-start(bf16[48,1024]{1,0:T(8,128)(2,1)S(1)} %pad_maximum_fusion.20), channel_id=1, source_target_pairs={{0,4},{4,0},{8,12},{12,8},{1,5},{5,1},{9,13},{13,9},{2,6},{6,2},{1... | collective-permute-start | bytes 294920 | tf_op jit(solution)/shard_map/ppermute | solution.py:45
  132.4 8.6 %collective-permute-start.29 = (bf16[96,2048]{1,0:T(8,128)(2,1)S(1)}, bf16[96,2048]{1,0:T(8,128)(2,1)S(1)}, u32[]{:S(2)}, u32[]{:S(2)}) collective-permute-start(bf16[96,2048]{1,0:T(8,128)(2,1)S(1)} %pad_maximum_fusion.6), channel_id=1, source_target_pairs={{0,1},{1,0},{2,3},{3,2},{4,5},{5,4},{6,7},{7,6},{8,9},{9,8},{10,11... | collective-permute-start | bytes 1179656 | tf_op jit(solution)/shard_map/ppermute | solution.py:40
  135.4 5.6 %collective-permute-start.23 = (bf16[48,512]{1,0:T(8,128)(2,1)S(1)}, bf16[48,512]{1,0:T(8,128)(2,1)S(1)}, u32[]{:S(2)}, u32[]{:S(2)}) collective-permute-start(bf16[48,512]{1,0:T(8,128)(2,1)S(1)} %get-tuple-element.15), channel_id=1, source_target_pairs={{0,8},{4,12},{8,0},{12,4},{1,9},{5,13},{9,1},{13,5},{2,10},{6,14},... | collective-permute-start | bytes 147464 | tf_op jit(solution)/shard_map/ppermute | solution.py:45
  146.7 22.5 %collective-permute-start.37 = (bf16[96,896]{1,0:T(8,128)(2,1)}, bf16[96,896]{1,0:T(8,128)(2,1)}, u32[]{:S(2)}, u32[]{:S(2)}) collective-permute-start(bf16[96,896]{1,0:T(8,128)(2,1)} %fusion.35), channel_id=1, source_target_pairs={{0,2},{2,0},{1,3},{3,1},{4,6},{6,4},{5,7},{7,5},{8,10},{10,8},{9,1... | collective-permute-start | bytes 516104 | tf_op jit(solution)/shard_map/ppermute | solution.py:40
  147.4 23.2 %collective-permute-start.38 = (bf16[96,896]{1,0:T(8,128)(2,1)}, bf16[96,896]{1,0:T(8,128)(2,1)}, u32[]{:S(2)}, u32[]{:S(2)}) collective-permute-start(bf16[96,896]{1,0:T(8,128)(2,1)} %fusion.38), channel_id=1, source_target_pairs={{0,2},{2,0},{1,3},{3,1},{4,6},{6,4},{5,7},{7,5},{8,10},{10,8},{9,1... | collective-permute-start | bytes 516104 | tf_op jit(solution)/shard_map/ppermute | solution.py:40
  150.7 19.9 %collective-permute-start.36 = (bf16[96,896]{1,0:T(8,128)(2,1)}, bf16[96,896]{1,0:T(8,128)(2,1)}, u32[]{:S(2)}, u32[]{:S(2)}) collective-permute-start(bf16[96,896]{1,0:T(8,128)(2,1)} %fusion.41.refs_1_), channel_id=1, source_target_pairs={{0,2},{2,0},{1,3},{3,1},{4,6},{6,4},{5,7},{7,5},{8,10},{10,8},{9,1... | collective-permute-start | bytes 516104 | tf_op jit(solution)/shard_map/ppermute | solution.py:40
  152.4 14.1 %slice-start.2 = ((s8[7340032]{0:T(1024)(128)(4,1)}), s8[4194304]{0:T(1024)(128)(4,1)S(1)}, s32[]{:S(2)}) async-start(s8[7340032]{0:T(1024)(128)(4,1)} %bitcast.27), calls=%async_computation.2 | async-start | bytes 8388608
  156.3 17.2 %collective-permute-start.34 = (bf16[96,896]{1,0:T(8,128)(2,1)}, bf16[96,896]{1,0:T(8,128)(2,1)S(1)}, u32[]{:S(2)}, u32[]{:S(2)}) collective-permute-start(bf16[96,896]{1,0:T(8,128)(2,1)} %fusion.29), channel_id=1, source_target_pairs={{0,2},{2,0},{1,3},{3,1},{4,6},{6,4},{5,7},{7,5},{8,10},{10,8},{9,1... | collective-permute-start | bytes 516104 | tf_op jit(solution)/shard_map/ppermute | solution.py:40
  157.7 15.8 %collective-permute-start.35 = (bf16[96,896]{1,0:T(8,128)(2,1)}, bf16[96,896]{1,0:T(8,128)(2,1)S(1)}, u32[]{:S(2)}, u32[]{:S(2)}) collective-permute-start(bf16[96,896]{1,0:T(8,128)(2,1)} %fusion.32), channel_id=1, source_target_pairs={{0,2},{2,0},{1,3},{3,1},{4,6},{6,4},{5,7},{7,5},{8,10},{10,8},{9,1... | collective-permute-start | bytes 516104 | tf_op jit(solution)/shard_map/ppermute | solution.py:40
  169.2 5.5 %collective-permute-start.33 = (bf16[96,896]{1,0:T(8,128)(2,1)S(1)}, bf16[96,896]{1,0:T(8,128)(2,1)S(1)}, u32[]{:S(2)}, u32[]{:S(2)}) collective-permute-start(bf16[96,896]{1,0:T(8,128)(2,1)S(1)} %fusion.44), channel_id=1, source_target_pairs={{0,2},{2,0},{1,3},{3,1},{4,6},{6,4},{5,7},{7,5},{8,10},{10,8},{9,1... | collective-permute-start | bytes 516104 | tf_op jit(solution)/shard_map/ppermute | solution.py:40
  170.6 35.6 %collective-permute-start.30 = (bf16[64,2048]{1,0:T(8,128)(2,1)S(1)}, bf16[64,2048]{1,0:T(8,128)(2,1)S(1)}, u32[]{:S(2)}, u32[]{:S(2)}) collective-permute-start(bf16[64,2048]{1,0:T(8,128)(2,1)S(1)} %slice.524), channel_id=1, source_target_pairs={{0,1},{1,0},{2,3},{3,2},{4,5},{5,4},{6,7},{7,6},{8,9},{9,8},{10,11... | collective-permute-start | bytes 786440 | tf_op jit(solution)/shard_map/ppermute | solution.py:40
  178.8 28.1 %collective-permute-start.39 = (bf16[48,2048]{1,0:T(8,128)(2,1)S(1)}, bf16[48,2048]{1,0:T(8,128)(2,1)S(1)}, u32[]{:S(2)}, u32[]{:S(2)}) collective-permute-start(bf16[48,2048]{1,0:T(8,128)(2,1)S(1)} %slice.525), channel_id=1, source_target_pairs={{0,1},{1,0},{2,3},{3,2},{4,5},{5,4},{6,7},{7,6},{8,9},{9,8},{10,11... | collective-permute-start | bytes 589832 | tf_op jit(solution)/shard_map/ppermute | solution.py:40
  206.4 6.4 %collective-permute-start.31 = (bf16[64,1024]{1,0:T(8,128)(2,1)S(1)}, bf16[64,1024]{1,0:T(8,128)(2,1)S(1)}, u32[]{:S(2)}, u32[]{:S(2)}) collective-permute-start(bf16[64,1024]{1,0:T(8,128)(2,1)S(1)} %pad_maximum_fusion.18), channel_id=1, source_target_pairs={{0,4},{4,0},{8,12},{12,8},{1,5},{5,1},{9,13},{13,9},{2,6},{6,2},{1... | collective-permute-start | bytes 393224 | tf_op jit(solution)/shard_map/ppermute | solution.py:45
  207.0 7.4 %collective-permute-start.40 = (bf16[48,1024]{1,0:T(8,128)(2,1)S(1)}, bf16[48,1024]{1,0:T(8,128)(2,1)S(1)}, u32[]{:S(2)}, u32[]{:S(2)}) collective-permute-start(bf16[48,1024]{1,0:T(8,128)(2,1)S(1)} %pad_maximum_fusion.22), channel_id=1, source_target_pairs={{0,4},{4,0},{8,12},{12,8},{1,5},{5,1},{9,13},{13,9},{2,6},{6,2},{1... | collective-permute-start | bytes 294920 | tf_op jit(solution)/shard_map/ppermute | solution.py:45
  212.8 7.4 %collective-permute-start.32 = (bf16[64,512]{1,0:T(8,128)(2,1)S(1)}, bf16[64,512]{1,0:T(8,128)(2,1)S(1)}, u32[]{:S(2)}, u32[]{:S(2)}) collective-permute-start(bf16[64,512]{1,0:T(8,128)(2,1)S(1)} %get-tuple-element.18), channel_id=1, source_target_pairs={{0,8},{4,12},{8,0},{12,4},{1,9},{5,13},{9,1},{13,5},{2,10},{6,14},... | collective-permute-start | bytes 196616 | tf_op jit(solution)/shard_map/ppermute | solution.py:45
  214.5 6.3 %collective-permute-start.41 = (bf16[48,512]{1,0:T(8,128)(2,1)S(1)}, bf16[48,512]{1,0:T(8,128)(2,1)S(1)}, u32[]{:S(2)}, u32[]{:S(2)}) collective-permute-start(bf16[48,512]{1,0:T(8,128)(2,1)S(1)} %get-tuple-element.21), channel_id=1, source_target_pairs={{0,8},{4,12},{8,0},{12,4},{1,9},{5,13},{9,1},{13,5},{2,10},{6,14},... | collective-permute-start | bytes 147464 | tf_op jit(solution)/shard_map/ppermute | solution.py:45
  (38 other events, 236.8 us)

commit v4 on v3

--- a/solution.py
+++ b/solution.py
@@ -96,6 +96,7 @@
         in_specs=[anywhere] * (1 + len(after)),
         out_specs=anywhere,
         input_output_aliases={0: 0},
+        compiler_params=pltpu.CompilerParams(vmem_limit_bytes=MIB // 4),
     )(value, *after)
 
 
@@ -178,7 +179,7 @@
             pltpu.SemaphoreType.DMA((first,)),
         ],
         input_output_aliases={first + i: i for i in range(len(old))},
-        compiler_params=pltpu.CompilerParams(vmem_limit_bytes=20 * MIB),
+        compiler_params=pltpu.CompilerParams(vmem_limit_bytes=12 * MIB),
         cost_estimate=pl.CostEstimate(
             flops=4 * tokens * features * width, bytes_accessed=4 * features * width, transcendentals=0
         ),
@@ -225,7 +226,7 @@
             pltpu.SemaphoreType.DMA((first,)),
         ],
         input_output_aliases={first + i: i for i in range(len(old))},
-        compiler_params=pltpu.CompilerParams(vmem_limit_bytes=20 * MIB),
+        compiler_params=pltpu.CompilerParams(vmem_limit_bytes=12 * MIB),
         cost_estimate=pl.CostEstimate(
             flops=2 * tokens * features * width, bytes_accessed=2 * features * width, transcendentals=0
         ),

time: 223 us -> 176 us (0.79)
  matrix products: 84.8 us -> 48.7 us
  other arithmetic: 22.8 us -> 5.67 us
  waiting for transfers between devices: 34.3 us -> 44.3 us
  local copies, waits for them, and re-layouts: 10 us -> 5.76 us
    dot_general x25, matrix products: 84.8 us -> 48.7 us  [dot(): lax.dot_general(left, right, (dims, ((), ())), preferred_element_type=jnp...]
    ppermute x24, waiting for transfers between devices: 4.82 us -> 14.6 us  [shifted(): return lax.ppermute(value, axis, [(i, (i + step) % n) for i in range(n)])]
    convert_element_type x5, other arithmetic: 7.98 us -> 2.26 us  [swiglu_grads(): hidden = (gate * sig * up).astype(jnp.bfloat16)]
    concatenate x3, other arithmetic: 4.12 us -> 0.05 us  [piped(): near = swapped(jnp.concatenate([both, far], axis=1), 'hid', 1)]
    unnamed x88 -> x16, local copies, waits for them, and re-layouts: 3.72 us -> 0.61 us
    concatenate x3, other arithmetic: 2.82 us -> 0.09 us  [piped(): x = jnp.concatenate([mixed[:rows], theirs[:rows]], axis=0)]
  transfers between devices with their start and end apart: 42 -> 42, of which waited for: 15 -> 17; matrix products, arithmetic and copies ran while one was open for 51% -> 33% of each run, Pallas kernels for 12% -> 16%
where the time goes in v4:
time: 176 us
  matrix products  48.7 us (28%)
  waiting for transfers between devices  44.3 us (25%)
  starting transfers between devices  42.4 us (24%)
  Pallas kernels  27.3 us (16%)
  local copies, waits for them, and re-layouts  5.76 us (3%)
  other arithmetic  5.67 us (3%)
    dot_general x25, matrix products, dot(): lax.dot_general(left, right, (dims, ((), ())), preferred_element_type=jnp...  48.7 us
    ppermute x18, waiting for transfers between devices, swapped(): return lax.ppermute(value, axis, [(i, i ^ bit) for i in range(n)])  29.7 us
    ppermute x18, starting transfers between devices, swapped(): return lax.ppermute(value, axis, [(i, i ^ bit) for i in range(n)])  25.2 us
    ppermute x24, starting transfers between devices, shifted(): return lax.ppermute(value, axis, [(i, (i + step) % n) for i in range(n)])  17.2 us
    pallas_call x2, Pallas kernels, column_grads(): pl.pallas_call(functools.partial(columns_kernel, heights, starts, width,...  15.6 us
    ppermute x24, waiting for transfers between devices, shifted(): return lax.ppermute(value, axis, [(i, (i + step) % n) for i in range(n)])  14.6 us
    pallas_call x2, Pallas kernels, row_grads(): pl.pallas_call(functools.partial(rows_kernel, heights, starts, width, len...  11.7 us
  transfers between devices with their start and end apart: 42, of which 17 were waited for; matrix products, arithmetic and copies ran while one was open for 33% of the time, Pallas kernels for 16%

profile of v4, /device:TPU:0, one launch (start us, length us, event | category | flops | bytes accessed | tf_op | source)
XLA Modules:
  0.0 175.6 jit_solution(1493458732218874083)
XLA Ops:
  1.4 4.0 %collective-permute-start.4 = (bf16[32,512]{1,0:T(8,128)(2,1)S(1)}, bf16[32,512]{1,0:T(8,128)(2,1)S(1)}, u32[]{:S(2)}, u32[]{:S(2)}) collective-permute-start(bf16[32,512]{1,0:T(8,128)(2,1)S(1)} %slice.211), channel_id=1, source_target_pairs={{0,8},{4,12},{8,0},{12,4},{1,9},{5,13},{9,1},{13,5},{2,10},{6,14},... | collective-permute-start | bytes 98312 | tf_op jit(solution)/shard_map/ppermute | solution.py:45
  9.6 2.0 %collective-permute-start.5 = (bf16[32,1024]{1,0:T(8,128)(2,1)S(1)}, bf16[32,1024]{1,0:T(8,128)(2,1)S(1)}, u32[]{:S(2)}, u32[]{:S(2)}) collective-permute-start(bf16[32,1024]{1,0:T(8,128)(2,1)S(1)} %pad_maximum_fusion.24), channel_id=1, source_target_pairs={{0,4},{4,0},{8,12},{12,8},{1,5},{5,1},{9,13},{13,9},{2,6},{6,2},{1... | collective-permute-start | bytes 196616 | tf_op jit(solution)/shard_map/ppermute | solution.py:45
  12.6 2.0 %collective-permute-done.5 = bf16[32,1024]{1,0:T(8,128)(2,1)S(1)} collective-permute-done((bf16[32,1024]{1,0:T(8,128)(2,1)S(1)}, bf16[32,1024]{1,0:T(8,128)(2,1)S(1)}, u32[]{:S(2)}, u32[]{:S(2)}) %collective-permute-start.5) | collective-permute-done | bytes 65568 | tf_op jit(solution)/shard_map/ppermute | solution.py:45
  16.9 4.6 %convolution_convert_fusion.6.refs_1_ = bf16[64,1792]{1,0:T(8,128)(2,1)S(1)} fusion(bf16[2048,1792]{1,0:T(8,128)(2,1)} %param.7, bf16[32,2048]{1,0:T(8,128)(2,1)S(1)} %collective-permute-done.6, bf16[32,512]{1,0:T(8,128)(2,1)S(1)} %get-tuple-element.76, bf16[32,512]{1,0:T(8,128)(2,1)S(1)} %get-tuple-element.75, bf16[32,512]{1,0:T(8,128)(2,1)S(1)} %get-tuple-element.74, ...), kind=kOutput, calls=%fused_computation.32 | convolution fusion | flops 471187456 | bytes 7831552 | tf_op jit(solution)/shard_map/dot_general | solution.py:15
  21.5 1.6 collective-permute-start.8
  23.1 2.6 %collective-permute-start.9 = (bf16[96,512]{1,0:T(8,128)(2,1)S(1)}, bf16[96,512]{1,0:T(8,128)(2,1)S(1)}, u32[]{:S(2)}, u32[]{:S(2)}) collective-permute-start(bf16[96,512]{1,0:T(8,128)(2,1)S(1)} %shard_map.84), channel_id=1, source_target_pairs={{0,8},{4,12},{8,0},{12,4},{1,9},{5,13},{9,1},{13,5},{2,10},{6,14},... | collective-permute-start | bytes 294920 | tf_op jit(solution)/shard_map/ppermute | solution.py:45
  25.7 1.4 convolution_convert_fusion.7
  27.7 2.3 %convolution_convert_fusion.8.refs_1_ = bf16[64,1792]{1,0:T(8,128)(2,1)S(1)} fusion(bf16[1792,2048]{1,0:T(8,128)(2,1)S(1)} %bitcast.30, bf16[32,2048]{1,0:T(8,128)(2,1)S(1)} %collective-permute-done.2, bf16[32,512]{1,0:T(8,128)(2,1)S(1)} %get-tuple-element.72, bf16[32,512]{1,0:T(8,128)(2,1)S(1)} %get-tuple-element.71, ...), kind=kOutput, calls=%fused_computation.34 | convolution fusion | flops 471187456 | bytes 7831552 | tf_op jit(solution)/shard_map/dot_general | solution.py:15
  30.1 1.6 collective-permute-start.3
  31.7 1.4 collective-permute-start.10
  33.1 4.8 %collective-permute-done.10.refs_1_ = bf16[96,1024]{1,0:T(8,128)(2,1)S(1)} collective-permute-done((bf16[96,1024]{1,0:T(8,128)(2,1)S(1)}, bf16[96,1024]{1,0:T(8,128)(2,1)S(1)}, u32[]{:S(2)}, u32[]{:S(2)}) %collective-permute-start.10) | collective-permute-done | bytes 196640 | tf_op jit(solution)/shard_map/ppermute | solution.py:45
  39.1 1.7 collective-permute-done.11
  40.8 1.3 convolution_convert_fusion.4
  42.7 1.3 convolution_convert_fusion.3
  44.0 5.5 %convolution_convert_fusion.5.refs_1_ = bf16[96,1792]{1,0:T(8,128)(2,1)S(1)} fusion(bf16[1792,2048]{1,0:T(8,128)(2,1)} %param.9, bf16[48,2048]{1,0:T(8,128)(2,1)S(1)} %get-tuple-element.54, bf16[48,2048]{1,0:T(8,128)(2,1)S(1)} %get-tuple-element.52), kind=kOutput, calls=%fused_computation.30 | convolution fusion | flops 705601536 | bytes 8077312 | tf_op jit(solution)/shard_map/dot_general | solution.py:15
  50.1 1.8 %collective-permute-start.19 = (bf16[128,1024]{1,0:T(8,128)(2,1)S(1)}, bf16[128,1024]{1,0:T(8,128)(2,1)S(1)}, u32[]{:S(2)}, u32[]{:S(2)}) collective-permute-start(bf16[128,1024]{1,0:T(8,128)(2,1)S(1)} %pad_maximum_fusion.11), channel_id=1, source_target_pairs={{0,4},{4,0},{8,12},{12,8},{1,5},{5,1},{9,13},{13,9},{2,6},{6,2},{1... | collective-permute-start | bytes 786440 | tf_op jit(solution)/shard_map/ppermute | solution.py:45
  52.3 2.3 %fusion.55 = f32[64,2048]{1,0:T(8,128)S(1)} fusion(bf16[64,1792]{1,0:T(8,128)(2,1)S(1)} %get-tuple-element.31.refs_4_, bf16[2048,1792]{1,0:T(8,128)(2,1)S(1)} %bitcast.28), kind=kOutput, calls=%fused_computation.182 | convolution fusion | flops 469762048 | bytes 8093696 | tf_op jit(solution)/shard_map/dot_general | solution.py:15
  54.6 2.3 %convolution_add_fusion.2 = f32[64,2048]{1,0:T(8,128)S(1)} fusion(f32[64,2048]{1,0:T(8,128)S(1)} %fusion.55, bf16[64,1792]{1,0:T(8,128)(2,1)S(1)} %get-tuple-element.32.refs_8_, bf16[2048,1792]{1,0:T(8,128)(2,1)S(1)} %bitcast.26), kind=kOutput, calls=%fused_computation.31 | convolution fusion | flops 469893120 | bytes 8617984 | tf_op jit(solution)/shard_map/dot_general | solution.py:15
  57.0 1.3 collective-permute-done.12
  58.8 1.6 collective-permute-start.16
  60.9 1.9 %collective-permute-done.13 = bf16[32,1024]{1,0:T(8,128)(2,1)S(1)} collective-permute-done((bf16[32,1024]{1,0:T(8,128)(2,1)S(1)}, bf16[32,1024]{1,0:T(8,128)(2,1)S(1)}, u32[]{:S(2)}, u32[]{:S(2)}) %collective-permute-start.13) | collective-permute-done | bytes 65568 | tf_op jit(solution)/shard_map/ppermute | solution.py:45
  64.1 3.6 %collective-permute-done.14 = bf16[32,512]{1,0:T(8,128)(2,1)S(1)} collective-permute-done((bf16[32,512]{1,0:T(8,128)(2,1)S(1)}, bf16[32,512]{1,0:T(8,128)(2,1)S(1)}, u32[]{:S(2)}, u32[]{:S(2)}) %collective-permute-start.14) | collective-permute-done | bytes 32800 | tf_op jit(solution)/shard_map/ppermute | solution.py:45
  71.3 5.6 %convolution_convert_fusion.2.refs_1_ = bf16[128,1792]{1,0:T(8,128)(2,1)S(1)} fusion(bf16[1792,2048]{1,0:T(8,128)(2,1)} %param.9, bf16[64,2048]{1,0:T(8,128)(2,1)S(1)} %get-tuple-element.44, bf16[64,2048]{1,0:T(8,128)(2,1)S(1)} %get-tuple-element.42), kind=kOutput, calls=%fused_computation.26 | convolution fusion | flops 940802048 | bytes 8323072 | tf_op jit(solution)/shard_map/dot_general | solution.py:15
  77.0 1.6 collective-permute-start.24
  80.3 1.6 collective-permute-start.26
  82.4 2.3 %fusion.56 = f32[96,2048]{1,0:T(8,128)S(1)} fusion(bf16[96,1792]{1,0:T(8,128)(2,1)S(1)} %get-tuple-element.28.refs_5_, bf16[2048,1792]{1,0:T(8,128)(2,1)S(1)} %bitcast.28), kind=kOutput, calls=%fused_computation.183 | convolution fusion | flops 704643072 | bytes 8470528 | tf_op jit(solution)/shard_map/dot_general | solution.py:15
  84.8 2.3 %convolution_add_fusion.1 = f32[96,2048]{1,0:T(8,128)S(1)} fusion(f32[96,2048]{1,0:T(8,128)S(1)} %fusion.56, bf16[96,1792]{1,0:T(8,128)(2,1)S(1)} %get-tuple-element.29.refs_9_, bf16[2048,1792]{1,0:T(8,128)(2,1)S(1)} %bitcast.26), kind=kOutput, calls=%fused_computation.27 | convolution fusion | flops 704839680 | bytes 9256960 | tf_op jit(solution)/shard_map/dot_general | solution.py:15
  87.3 1.4 collective-permute-done.21
  89.9 3.8 %collective-permute-done.22 = bf16[48,1024]{1,0:T(8,128)(2,1)S(1)} collective-permute-done((bf16[48,1024]{1,0:T(8,128)(2,1)S(1)}, bf16[48,1024]{1,0:T(8,128)(2,1)S(1)}, u32[]{:S(2)}, u32[]{:S(2)}) %collective-permute-start.22) | collective-permute-done | bytes 98336 | tf_op jit(solution)/shard_map/ppermute | solution.py:45
  94.8 4.5 %collective-permute-done.23 = bf16[48,512]{1,0:T(8,128)(2,1)S(1)} collective-permute-done((bf16[48,512]{1,0:T(8,128)(2,1)S(1)}, bf16[48,512]{1,0:T(8,128)(2,1)S(1)}, u32[]{:S(2)}, u32[]{:S(2)}) %collective-permute-start.23) | collective-permute-done | bytes 49184 | tf_op jit(solution)/shard_map/ppermute | solution.py:45
  102.8 1.5 collective-permute-start.38
  105.6 4.6 %collective-permute-done.26.refs_0_ = bf16[128,1792]{1,0:T(8,128)(2,1)S(1)} collective-permute-done((bf16[128,1792]{1,0:T(8,128)(2,1)S(1)}, bf16[128,1792]{1,0:T(8,128)(2,1)S(1)}, u32[]{:S(2)}, u32[]{:S(2)}) %collective-permute-start.26) | collective-permute-done | bytes 458784 | tf_op jit(solution)/shard_map/ppermute | solution.py:40
  110.2 1.5 collective-permute-start.36
  113.7 1.5 collective-permute-start.35
  116.0 2.5 %fusion.57 = f32[128,2048]{1,0:T(8,128)S(1)} fusion(bf16[128,1792]{1,0:T(8,128)(2,1)S(1)} %get-tuple-element.25.refs_6_, bf16[2048,1792]{1,0:T(8,128)(2,1)S(1)} %bitcast.28), kind=kOutput, calls=%fused_computation.184 | convolution fusion | flops 939524096 | bytes 8847360 | tf_op jit(solution)/shard_map/dot_general | solution.py:15
  118.5 2.5 %convolution_add_fusion = f32[128,2048]{1,0:T(8,128)S(1)} fusion(f32[128,2048]{1,0:T(8,128)S(1)} %fusion.57, bf16[128,1792]{1,0:T(8,128)(2,1)S(1)} %get-tuple-element.26.refs_10_, bf16[2048,1792]{1,0:T(8,128)(2,1)S(1)} %bitcast.26), kind=kOutput, calls=%fused_computation.20 | convolution fusion | flops 939786240 | bytes 9895936 | tf_op jit(solution)/shard_map/dot_general | solution.py:15
  123.2 1.7 collective-permute-done.34
  124.9 2.1 %collective-permute-done.35 = bf16[96,896]{1,0:T(8,128)(2,1)S(1)} collective-permute-done((bf16[96,896]{1,0:T(8,128)(2,1)S(1)}, bf16[96,896]{1,0:T(8,128)(2,1)S(1)}, u32[]{:S(2)}, u32[]{:S(2)}) %collective-permute-start.35) | collective-permute-done | bytes 172064 | tf_op jit(solution)/shard_map/ppermute | solution.py:40
  127.0 1.8 %collective-permute-done.33 = bf16[96,896]{1,0:T(8,128)(2,1)S(1)} collective-permute-done((bf16[96,896]{1,0:T(8,128)(2,1)S(1)}, bf16[96,896]{1,0:T(8,128)(2,1)S(1)}, u32[]{:S(2)}, u32[]{:S(2)}) %collective-permute-start.33) | collective-permute-done | bytes 172064 | tf_op jit(solution)/shard_map/ppermute | solution.py:40
  130.3 1.3 fusion.26
  133.0 5.9 %shard_map.95.refs_8_ = bf16[1792,2048]{1,0:T(8,128)(2,1)} custom-call(bf16[64,1792]{1,0:T(8,128)(2,1)S(1)} %get-tuple-element.30.refs_0_, bf16[96,1792]{1,0:T(8,128)(2,1)S(1)} %get-tuple-element.27.refs_1_, bf16[128,1792]{1,0:T(8,128)(2,1)S(1)} %get-tuple-element.24.refs_2_, bf16[96,896]{1,0:T(8,128)(2,1)S(1)} %get-tuple-element.33.refs_3_, ...), custom_call_target="tpu_custom_call" | custom-call | flops 1409286144 | bytes 3670016 | tf_op jit(solution)/shard_map/pallas_call | solution.py:217
  138.8 5.9 %shard_map.96 = bf16[1792,2048]{1,0:T(8,128)(2,1)} custom-call(bf16[64,1792]{1,0:T(8,128)(2,1)S(1)} %get-tuple-element.30.refs_0_, bf16[96,1792]{1,0:T(8,128)(2,1)S(1)} %get-tuple-element.27.refs_1_, bf16[128,1792]{1,0:T(8,128)(2,1)S(1)} %get-tuple-element.24.refs_2_, bf16[96,896]{1,0:T(8,128)(2,1)S(1)} %get-tuple-element.36.refs_3_, ...), custom_call_target="tpu_custom_call", output_to_operand_aliasing={{}: (8, {})} | custom-call | flops 1409286144 | bytes 3670016 | tf_op jit(solution)/shard_map/pallas_call | solution.py:217
  144.7 7.8 %shard_map.93 = (bf16[2048,1792]{1,0:T(8,128)(2,1)}, bf16[2048,1792]{1,0:T(8,128)(2,1)}) custom-call(bf16[64,2048]{1,0:T(8,128)(2,1)S(1)} %pad_maximum_fusion.10.refs_0_, bf16[96,2048]{1,0:T(8,128)(2,1)S(1)} %pad_maximum_fusion.5.refs_1_, bf16[128,2048]{1,0:T(8,128)(2,1)S(1)} %pad_maximum_fusion.2.refs_2_, bf16[96,2048]{1,0:T(8,128)(2,1)S(1)} %pad_maximum_fusion.8.refs_3_, ...), custom_call_target="tpu_custom_call" | custom-call | flops 2818572288 | bytes 7340032 | tf_op jit(solution)/shard_map/pallas_call | solution.py:169
  152.5 7.8 %shard_map.94 = (bf16[2048,1792]{1,0:T(8,128)(2,1)}, bf16[2048,1792]{1,0:T(8,128)(2,1)}) custom-call(bf16[64,2048]{1,0:T(8,128)(2,1)S(1)} %pad_maximum_fusion.10.refs_0_, bf16[96,2048]{1,0:T(8,128)(2,1)S(1)} %pad_maximum_fusion.5.refs_1_, bf16[128,2048]{1,0:T(8,128)(2,1)S(1)} %pad_maximum_fusion.2.refs_2_, ...), custom_call_target="tpu_custom_call", output_to_operand_aliasing={{0}: (12, {}), {1}: (13, {})} | custom-call | flops 2818572288 | bytes 7340032 | tf_op jit(solution)/shard_map/pallas_call | solution.py:169
  162.7 4.1 %collective-permute-done.31 = bf16[64,1024]{1,0:T(8,128)(2,1)S(1)} collective-permute-done((bf16[64,1024]{1,0:T(8,128)(2,1)S(1)}, bf16[64,1024]{1,0:T(8,128)(2,1)S(1)}, u32[]{:S(2)}, u32[]{:S(2)}) %collective-permute-start.31) | collective-permute-done | bytes 131104 | tf_op jit(solution)/shard_map/ppermute | solution.py:45
  166.9 1.9 %collective-permute-start.32 = (bf16[64,512]{1,0:T(8,128)(2,1)S(1)}, bf16[64,512]{1,0:T(8,128)(2,1)S(1)}, u32[]{:S(2)}, u32[]{:S(2)}) collective-permute-start(bf16[64,512]{1,0:T(8,128)(2,1)S(1)} %get-tuple-element.18), channel_id=1, source_target_pairs={{0,8},{4,12},{8,0},{12,4},{1,9},{5,13},{9,1},{13,5},{2,10},{6,14},... | collective-permute-start | bytes 196616 | tf_op jit(solution)/shard_map/ppermute | solution.py:45
  168.8 1.6 collective-permute-start.41
  170.4 3.8 %collective-permute-done.32 = bf16[64,512]{1,0:T(8,128)(2,1)S(1)} collective-permute-done((bf16[64,512]{1,0:T(8,128)(2,1)S(1)}, bf16[64,512]{1,0:T(8,128)(2,1)S(1)}, u32[]{:S(2)}, u32[]{:S(2)}) %collective-permute-start.32) | collective-permute-done | bytes 65568 | tf_op jit(solution)/shard_map/ppermute | solution.py:45
  (166 shorter events, 38.7 us)
Async XLA Ops:
  1.4 8.2 %collective-permute-start.4 = (bf16[32,512]{1,0:T(8,128)(2,1)S(1)}, bf16[32,512]{1,0:T(8,128)(2,1)S(1)}, u32[]{:S(2)}, u32[]{:S(2)}) collective-permute-start(bf16[32,512]{1,0:T(8,128)(2,1)S(1)} %slice.211), channel_id=1, source_target_pairs={{0,8},{4,12},{8,0},{12,4},{1,9},{5,13},{9,1},{13,5},{2,10},{6,14},... | collective-permute-start | bytes 98312 | tf_op jit(solution)/shard_map/ppermute | solution.py:45
  6.2 5.4 %collective-permute-start = (bf16[32,512]{1,0:T(8,128)(2,1)S(1)}, bf16[32,512]{1,0:T(8,128)(2,1)S(1)}, u32[]{:S(2)}, u32[]{:S(2)}) collective-permute-start(bf16[32,512]{1,0:T(8,128)(2,1)S(1)} %slice.208), channel_id=1, source_target_pairs={{0,8},{4,12},{8,0},{12,4},{1,9},{5,13},{9,1},{13,5},{2,10},{6,14},... | collective-permute-start | bytes 98312 | tf_op jit(solution)/shard_map/ppermute | solution.py:45
  9.6 5.0 %collective-permute-start.5 = (bf16[32,1024]{1,0:T(8,128)(2,1)S(1)}, bf16[32,1024]{1,0:T(8,128)(2,1)S(1)}, u32[]{:S(2)}, u32[]{:S(2)}) collective-permute-start(bf16[32,1024]{1,0:T(8,128)(2,1)S(1)} %pad_maximum_fusion.24), channel_id=1, source_target_pairs={{0,4},{4,0},{8,12},{12,8},{1,5},{5,1},{9,13},{13,9},{2,6},{6,2},{1... | collective-permute-start | bytes 196616 | tf_op jit(solution)/shard_map/ppermute | solution.py:45
  11.6 4.3 %collective-permute-start.1 = (bf16[32,1024]{1,0:T(8,128)(2,1)S(1)}, bf16[32,1024]{1,0:T(8,128)(2,1)S(1)}, u32[]{:S(2)}, u32[]{:S(2)}) collective-permute-start(bf16[32,1024]{1,0:T(8,128)(2,1)S(1)} %pad_maximum_fusion.23), channel_id=1, source_target_pairs={{0,4},{4,0},{8,12},{12,8},{1,5},{5,1},{9,13},{13,9},{2,6},{6,2},{1... | collective-permute-start | bytes 196616 | tf_op jit(solution)/shard_map/ppermute | solution.py:45
  15.4 1.5 collective-permute-start.6
  16.7 9.0 %slice-start = ((s8[7340032]{0:T(1024)(128)(4,1)}), s8[4194304]{0:T(1024)(128)(4,1)S(1)}, s32[]{:S(2)}) async-start(s8[7340032]{0:T(1024)(128)(4,1)} %bitcast.25), calls=%async_computation | async-start | bytes 8388608
  16.7 9.0 %slice-start.1 = ((s8[7340032]{0:T(1024)(128)(4,1)}), s8[3145728]{0:T(1024)(128)(4,1)S(1)}, s32[]{:S(2)}) async-start(s8[7340032]{0:T(1024)(128)(4,1)} %bitcast.25), calls=%async_computation.1 | async-start | bytes 6291456
  16.8 10.9 %collective-permute-start.2 = (bf16[32,2048]{1,0:T(8,128)(2,1)S(1)}, bf16[32,2048]{1,0:T(8,128)(2,1)S(1)}, u32[]{:S(2)}, u32[]{:S(2)}) collective-permute-start(bf16[32,2048]{1,0:T(8,128)(2,1)S(1)} %pad_maximum_fusion.15), channel_id=1, source_target_pairs={{0,1},{1,0},{2,3},{3,2},{4,5},{5,4},{6,7},{7,6},{8,9},{9,8},{10,11... | collective-permute-start | bytes 393224 | tf_op jit(solution)/shard_map/ppermute | solution.py:40
  21.5 6.2 %slice-start.4 = ((s8[7340032]{0:T(1024)(128)(4,1)}), s8[4194304]{0:T(1024)(128)(4,1)S(1)}, s32[]{:S(2)}) async-start(s8[7340032]{0:T(1024)(128)(4,1)} %bitcast.29), calls=%async_computation.4 | async-start | bytes 8388608
  21.5 30.3 %collective-permute-start.8 = (bf16[64,1792]{1,0:T(8,128)(2,1)S(1)}, bf16[64,1792]{1,0:T(8,128)(2,1)S(1)}, u32[]{:S(2)}, u32[]{:S(2)}) collective-permute-start(bf16[64,1792]{1,0:T(8,128)(2,1)S(1)} %convolution_convert_fusion.6.refs_1_), channel_id=1, source_target_pairs={{0,2},{2,0},{1,3},{3,1},{4,6},{6,4},{5,7},{7,5},{8,10},{10,8},{9,1... | collective-permute-start | bytes 688136 | tf_op jit(solution)/shard_map/ppermute | solution.py:40
  23.1 4.6 %slice-start.5 = ((s8[7340032]{0:T(1024)(128)(4,1)}), s8[3145728]{0:T(1024)(128)(4,1)S(1)}, s32[]{:S(2)}) async-start(s8[7340032]{0:T(1024)(128)(4,1)} %bitcast.29), calls=%async_computation.5 | async-start | bytes 6291456
  23.1 8.5 %collective-permute-start.9 = (bf16[96,512]{1,0:T(8,128)(2,1)S(1)}, bf16[96,512]{1,0:T(8,128)(2,1)S(1)}, u32[]{:S(2)}, u32[]{:S(2)}) collective-permute-start(bf16[96,512]{1,0:T(8,128)(2,1)S(1)} %shard_map.84), channel_id=1, source_target_pairs={{0,8},{4,12},{8,0},{12,4},{1,9},{5,13},{9,1},{13,5},{2,10},{6,14},... | collective-permute-start | bytes 294920 | tf_op jit(solution)/shard_map/ppermute | solution.py:45
  27.1 24.8 %collective-permute-start.7 = (bf16[64,1792]{1,0:T(8,128)(2,1)S(1)}, bf16[64,1792]{1,0:T(8,128)(2,1)S(1)}, u32[]{:S(2)}, u32[]{:S(2)}) collective-permute-start(bf16[64,1792]{1,0:T(8,128)(2,1)S(1)} %convolution_convert_fusion.7), channel_id=1, source_target_pairs={{0,2},{2,0},{1,3},{3,1},{4,6},{6,4},{5,7},{7,5},{8,10},{10,8},{9,1... | collective-permute-start | bytes 688136 | tf_op jit(solution)/shard_map/ppermute | solution.py:40
  30.1 12.0 %slice-start.2 = ((s8[7340032]{0:T(1024)(128)(4,1)}), s8[4194304]{0:T(1024)(128)(4,1)S(1)}, s32[]{:S(2)}) async-start(s8[7340032]{0:T(1024)(128)(4,1)} %bitcast.27), calls=%async_computation.2 | async-start | bytes 8388608
  30.1 21.8 %collective-permute-start.3 = (bf16[64,1792]{1,0:T(8,128)(2,1)S(1)}, bf16[64,1792]{1,0:T(8,128)(2,1)S(1)}, u32[]{:S(2)}, u32[]{:S(2)}) collective-permute-start(bf16[64,1792]{1,0:T(8,128)(2,1)S(1)} %convolution_convert_fusion.8.refs_1_), channel_id=1, source_target_pairs={{0,2},{2,0},{1,3},{3,1},{4,6},{6,4},{5,7},{7,5},{8,10},{10,8},{9,1... | collective-permute-start | bytes 688136 | tf_op jit(solution)/shard_map/ppermute | solution.py:40
  31.7 6.3 %collective-permute-start.10 = (bf16[96,1024]{1,0:T(8,128)(2,1)S(1)}, bf16[96,1024]{1,0:T(8,128)(2,1)S(1)}, u32[]{:S(2)}, u32[]{:S(2)}) collective-permute-start(bf16[96,1024]{1,0:T(8,128)(2,1)S(1)} %pad_maximum_fusion.12), channel_id=1, source_target_pairs={{0,4},{4,0},{8,12},{12,8},{1,5},{5,1},{9,13},{13,9},{2,6},{6,2},{1... | collective-permute-start | bytes 589832 | tf_op jit(solution)/shard_map/ppermute | solution.py:45
  38.0 12.1 %collective-permute-start.18 = (bf16[128,512]{1,0:T(8,128)(2,1)S(1)}, bf16[128,512]{1,0:T(8,128)(2,1)S(1)}, u32[]{:S(2)}, u32[]{:S(2)}) collective-permute-start(bf16[128,512]{1,0:T(8,128)(2,1)S(1)} %shard_map.87), channel_id=1, source_target_pairs={{0,8},{4,12},{8,0},{12,4},{1,9},{5,13},{9,1},{13,5},{2,10},{6,14},... | collective-permute-start | bytes 393224 | tf_op jit(solution)/shard_map/ppermute | solution.py:45
  38.9 1.8 %collective-permute-start.11 = (bf16[96,2048]{1,0:T(8,128)(2,1)S(1)}, bf16[96,2048]{1,0:T(8,128)(2,1)S(1)}, u32[]{:S(2)}, u32[]{:S(2)}) collective-permute-start(bf16[96,2048]{1,0:T(8,128)(2,1)S(1)} %pad_maximum_fusion.3), channel_id=1, source_target_pairs={{0,1},{1,0},{2,3},{3,2},{4,5},{5,4},{6,7},{7,6},{8,9},{9,8},{10,11... | collective-permute-start | bytes 1179656 | tf_op jit(solution)/shard_map/ppermute | solution.py:40
  49.4 32.4 %collective-permute-start.15 = (bf16[96,1792]{1,0:T(8,128)(2,1)S(1)}, bf16[96,1792]{1,0:T(8,128)(2,1)S(1)}, u32[]{:S(2)}, u32[]{:S(2)}) collective-permute-start(bf16[96,1792]{1,0:T(8,128)(2,1)S(1)} %convolution_convert_fusion.5.refs_1_), channel_id=1, source_target_pairs={{0,2},{2,0},{1,3},{3,1},{4,6},{6,4},{5,7},{7,5},{8,10},{10,8},{9,1... | collective-permute-start | bytes 1032200 | tf_op jit(solution)/shard_map/ppermute | solution.py:40
  50.1 13.9 %collective-permute-start.19 = (bf16[128,1024]{1,0:T(8,128)(2,1)S(1)}, bf16[128,1024]{1,0:T(8,128)(2,1)S(1)}, u32[]{:S(2)}, u32[]{:S(2)}) collective-permute-start(bf16[128,1024]{1,0:T(8,128)(2,1)S(1)} %pad_maximum_fusion.11), channel_id=1, source_target_pairs={{0,4},{4,0},{8,12},{12,8},{1,5},{5,1},{9,13},{13,9},{2,6},{6,2},{1... | collective-permute-start | bytes 786440 | tf_op jit(solution)/shard_map/ppermute | solution.py:45
  56.9 1.4 collective-permute-start.12
  58.4 4.3 %collective-permute-start.13 = (bf16[32,1024]{1,0:T(8,128)(2,1)S(1)}, bf16[32,1024]{1,0:T(8,128)(2,1)S(1)}, u32[]{:S(2)}, u32[]{:S(2)}) collective-permute-start(bf16[32,1024]{1,0:T(8,128)(2,1)S(1)} %pad_maximum_fusion.25), channel_id=1, source_target_pairs={{0,4},{4,0},{8,12},{12,8},{1,5},{5,1},{9,13},{13,9},{2,6},{6,2},{1... | collective-permute-start | bytes 196616 | tf_op jit(solution)/shard_map/ppermute | solution.py:45
  58.8 21.5 %collective-permute-start.16 = (bf16[96,1792]{1,0:T(8,128)(2,1)S(1)}, bf16[96,1792]{1,0:T(8,128)(2,1)S(1)}, u32[]{:S(2)}, u32[]{:S(2)}) collective-permute-start(bf16[96,1792]{1,0:T(8,128)(2,1)S(1)} %convolution_convert_fusion.4), channel_id=1, source_target_pairs={{0,2},{2,0},{1,3},{3,1},{4,6},{6,4},{5,7},{7,5},{8,10},{10,8},{9,1... | collective-permute-start | bytes 1032200 | tf_op jit(solution)/shard_map/ppermute | solution.py:40
  60.3 19.4 %collective-permute-start.17 = (bf16[96,1792]{1,0:T(8,128)(2,1)S(1)}, bf16[96,1792]{1,0:T(8,128)(2,1)S(1)}, u32[]{:S(2)}, u32[]{:S(2)}) collective-permute-start(bf16[96,1792]{1,0:T(8,128)(2,1)S(1)} %convolution_convert_fusion.3), channel_id=1, source_target_pairs={{0,2},{2,0},{1,3},{3,1},{4,6},{6,4},{5,7},{7,5},{8,10},{10,8},{9,1... | collective-permute-start | bytes 1032200 | tf_op jit(solution)/shard_map/ppermute | solution.py:40
  62.8 5.0 %collective-permute-start.14 = (bf16[32,512]{1,0:T(8,128)(2,1)S(1)}, bf16[32,512]{1,0:T(8,128)(2,1)S(1)}, u32[]{:S(2)}, u32[]{:S(2)}) collective-permute-start(bf16[32,512]{1,0:T(8,128)(2,1)S(1)} %get-tuple-element.12), channel_id=1, source_target_pairs={{0,8},{4,12},{8,0},{12,4},{1,9},{5,13},{9,1},{13,5},{2,10},{6,14},... | collective-permute-start | bytes 98312 | tf_op jit(solution)/shard_map/ppermute | solution.py:45
  64.1 4.9 %collective-permute-start.20 = (bf16[128,2048]{1,0:T(8,128)(2,1)S(1)}, bf16[128,2048]{1,0:T(8,128)(2,1)S(1)}, u32[]{:S(2)}, u32[]{:S(2)}) collective-permute-start(bf16[128,2048]{1,0:T(8,128)(2,1)S(1)} %pad_maximum_fusion), channel_id=1, source_target_pairs={{0,1},{1,0},{2,3},{3,2},{4,5},{5,4},{6,7},{7,6},{8,9},{9,8},{10,11... | collective-permute-start | bytes 1572872 | tf_op jit(solution)/shard_map/ppermute | solution.py:40
  67.8 10.8 %collective-permute-start.27 = (bf16[96,512]{1,0:T(8,128)(2,1)S(1)}, bf16[96,512]{1,0:T(8,128)(2,1)S(1)}, u32[]{:S(2)}, u32[]{:S(2)}) collective-permute-start(bf16[96,512]{1,0:T(8,128)(2,1)S(1)} %shard_map.90), channel_id=1, source_target_pairs={{0,8},{4,12},{8,0},{12,4},{1,9},{5,13},{9,1},{13,5},{2,10},{6,14},... | collective-permute-start | bytes 294920 | tf_op jit(solution)/shard_map/ppermute | solution.py:45
  77.0 36.8 %collective-permute-start.24 = (bf16[128,1792]{1,0:T(8,128)(2,1)S(1)}, bf16[128,1792]{1,0:T(8,128)(2,1)S(1)}, u32[]{:S(2)}, u32[]{:S(2)}) collective-permute-start(bf16[128,1792]{1,0:T(8,128)(2,1)S(1)} %convolution_convert_fusion.2.refs_1_), channel_id=1, source_target_pairs={{0,2},{2,0},{1,3},{3,1},{4,6},{6,4},{5,7},{7,5},{8,10},{10,8},{9,1... | collective-permute-start | bytes 1376264 | tf_op jit(solution)/shard_map/ppermute | solution.py:40
  78.6 11.2 %collective-permute-start.28 = (bf16[96,1024]{1,0:T(8,128)(2,1)S(1)}, bf16[96,1024]{1,0:T(8,128)(2,1)S(1)}, u32[]{:S(2)}, u32[]{:S(2)}) collective-permute-start(bf16[96,1024]{1,0:T(8,128)(2,1)S(1)} %pad_maximum_fusion.13), channel_id=1, source_target_pairs={{0,4},{4,0},{8,12},{12,8},{1,5},{5,1},{9,13},{13,9},{2,6},{6,2},{1... | collective-permute-start | bytes 589832 | tf_op jit(solution)/shard_map/ppermute | solution.py:45
  79.7 33.2 %collective-permute-start.25 = (bf16[128,1792]{1,0:T(8,128)(2,1)S(1)}, bf16[128,1792]{1,0:T(8,128)(2,1)S(1)}, u32[]{:S(2)}, u32[]{:S(2)}) collective-permute-start(bf16[128,1792]{1,0:T(8,128)(2,1)S(1)} %convolution_convert_fusion.1), channel_id=1, source_target_pairs={{0,2},{2,0},{1,3},{3,1},{4,6},{6,4},{5,7},{7,5},{8,10},{10,8},{9,1... | collective-permute-start | bytes 1376264 | tf_op jit(solution)/shard_map/ppermute | solution.py:40
  80.3 29.8 %collective-permute-start.26 = (bf16[128,1792]{1,0:T(8,128)(2,1)S(1)}, bf16[128,1792]{1,0:T(8,128)(2,1)S(1)}, u32[]{:S(2)}, u32[]{:S(2)}) collective-permute-start(bf16[128,1792]{1,0:T(8,128)(2,1)S(1)} %convolution_convert_fusion), channel_id=1, source_target_pairs={{0,2},{2,0},{1,3},{3,1},{4,6},{6,4},{5,7},{7,5},{8,10},{10,8},{9,1... | collective-permute-start | bytes 1376264 | tf_op jit(solution)/shard_map/ppermute | solution.py:40
  87.1 1.5 collective-permute-start.21
  88.7 4.9 %collective-permute-start.22 = (bf16[48,1024]{1,0:T(8,128)(2,1)S(1)}, bf16[48,1024]{1,0:T(8,128)(2,1)S(1)}, u32[]{:S(2)}, u32[]{:S(2)}) collective-permute-start(bf16[48,1024]{1,0:T(8,128)(2,1)S(1)} %pad_maximum_fusion.20), channel_id=1, source_target_pairs={{0,4},{4,0},{8,12},{12,8},{1,5},{5,1},{9,13},{13,9},{2,6},{6,2},{1... | collective-permute-start | bytes 294920 | tf_op jit(solution)/shard_map/ppermute | solution.py:45
  89.8 9.5 %collective-permute-start.29 = (bf16[96,2048]{1,0:T(8,128)(2,1)S(1)}, bf16[96,2048]{1,0:T(8,128)(2,1)S(1)}, u32[]{:S(2)}, u32[]{:S(2)}) collective-permute-start(bf16[96,2048]{1,0:T(8,128)(2,1)S(1)} %pad_maximum_fusion.6), channel_id=1, source_target_pairs={{0,1},{1,0},{2,3},{3,2},{4,5},{5,4},{6,7},{7,6},{8,9},{9,8},{10,11... | collective-permute-start | bytes 1179656 | tf_op jit(solution)/shard_map/ppermute | solution.py:40
  93.7 5.6 %collective-permute-start.23 = (bf16[48,512]{1,0:T(8,128)(2,1)S(1)}, bf16[48,512]{1,0:T(8,128)(2,1)S(1)}, u32[]{:S(2)}, u32[]{:S(2)}) collective-permute-start(bf16[48,512]{1,0:T(8,128)(2,1)S(1)} %get-tuple-element.15), channel_id=1, source_target_pairs={{0,8},{4,12},{8,0},{12,4},{1,9},{5,13},{9,1},{13,5},{2,10},{6,14},... | collective-permute-start | bytes 147464 | tf_op jit(solution)/shard_map/ppermute | solution.py:45
  100.1 4.3 %slice-start.6 = ((s8[7340032]{0:T(1024)(128)(4,1)}), s8[4194304]{0:T(1024)(128)(4,1)S(1)}, s32[]{:S(2)}) async-start(s8[7340032]{0:T(1024)(128)(4,1)} %bitcast.31), calls=%async_computation.6 | async-start | bytes 8388608
  102.2 18.8 %collective-permute-start.37 = (bf16[96,896]{1,0:T(8,128)(2,1)S(1)}, bf16[96,896]{1,0:T(8,128)(2,1)S(1)}, u32[]{:S(2)}, u32[]{:S(2)}) collective-permute-start(bf16[96,896]{1,0:T(8,128)(2,1)S(1)} %fusion.35), channel_id=1, source_target_pairs={{0,2},{2,0},{1,3},{3,1},{4,6},{6,4},{5,7},{7,5},{8,10},{10,8},{9,1... | collective-permute-start | bytes 516104 | tf_op jit(solution)/shard_map/ppermute | solution.py:40
  102.8 18.8 %collective-permute-start.38 = (bf16[96,896]{1,0:T(8,128)(2,1)S(1)}, bf16[96,896]{1,0:T(8,128)(2,1)S(1)}, u32[]{:S(2)}, u32[]{:S(2)}) collective-permute-start(bf16[96,896]{1,0:T(8,128)(2,1)S(1)} %fusion.38), channel_id=1, source_target_pairs={{0,2},{2,0},{1,3},{3,1},{4,6},{6,4},{5,7},{7,5},{8,10},{10,8},{9,1... | collective-permute-start | bytes 516104 | tf_op jit(solution)/shard_map/ppermute | solution.py:40
  110.2 11.5 %collective-permute-start.36 = (bf16[96,896]{1,0:T(8,128)(2,1)S(1)}, bf16[96,896]{1,0:T(8,128)(2,1)S(1)}, u32[]{:S(2)}, u32[]{:S(2)}) collective-permute-start(bf16[96,896]{1,0:T(8,128)(2,1)S(1)} %fusion.41.refs_1_), channel_id=1, source_target_pairs={{0,2},{2,0},{1,3},{3,1},{4,6},{6,4},{5,7},{7,5},{8,10},{10,8},{9,1... | collective-permute-start | bytes 516104 | tf_op jit(solution)/shard_map/ppermute | solution.py:40
  112.9 12.0 %collective-permute-start.34 = (bf16[96,896]{1,0:T(8,128)(2,1)S(1)}, bf16[96,896]{1,0:T(8,128)(2,1)S(1)}, u32[]{:S(2)}, u32[]{:S(2)}) collective-permute-start(bf16[96,896]{1,0:T(8,128)(2,1)S(1)} %fusion.29), channel_id=1, source_target_pairs={{0,2},{2,0},{1,3},{3,1},{4,6},{6,4},{5,7},{7,5},{8,10},{10,8},{9,1... | collective-permute-start | bytes 516104 | tf_op jit(solution)/shard_map/ppermute | solution.py:40
  113.7 13.2 %collective-permute-start.35 = (bf16[96,896]{1,0:T(8,128)(2,1)S(1)}, bf16[96,896]{1,0:T(8,128)(2,1)S(1)}, u32[]{:S(2)}, u32[]{:S(2)}) collective-permute-start(bf16[96,896]{1,0:T(8,128)(2,1)S(1)} %fusion.32), channel_id=1, source_target_pairs={{0,2},{2,0},{1,3},{3,1},{4,6},{6,4},{5,7},{7,5},{8,10},{10,8},{9,1... | collective-permute-start | bytes 516104 | tf_op jit(solution)/shard_map/ppermute | solution.py:40
  121.0 7.8 %collective-permute-start.33 = (bf16[96,896]{1,0:T(8,128)(2,1)S(1)}, bf16[96,896]{1,0:T(8,128)(2,1)S(1)}, u32[]{:S(2)}, u32[]{:S(2)}) collective-permute-start(bf16[96,896]{1,0:T(8,128)(2,1)S(1)} %fusion.44), channel_id=1, source_target_pairs={{0,2},{2,0},{1,3},{3,1},{4,6},{6,4},{5,7},{7,5},{8,10},{10,8},{9,1... | collective-permute-start | bytes 516104 | tf_op jit(solution)/shard_map/ppermute | solution.py:40
  121.6 38.7 %collective-permute-start.30 = (bf16[64,2048]{1,0:T(8,128)(2,1)S(1)}, bf16[64,2048]{1,0:T(8,128)(2,1)S(1)}, u32[]{:S(2)}, u32[]{:S(2)}) collective-permute-start(bf16[64,2048]{1,0:T(8,128)(2,1)S(1)} %slice.524), channel_id=1, source_target_pairs={{0,1},{1,0},{2,3},{3,2},{4,5},{5,4},{6,7},{7,6},{8,9},{9,8},{10,11... | collective-permute-start | bytes 786440 | tf_op jit(solution)/shard_map/ppermute | solution.py:40
  132.9 28.7 %collective-permute-start.39 = (bf16[48,2048]{1,0:T(8,128)(2,1)S(1)}, bf16[48,2048]{1,0:T(8,128)(2,1)S(1)}, u32[]{:S(2)}, u32[]{:S(2)}) collective-permute-start(bf16[48,2048]{1,0:T(8,128)(2,1)S(1)} %slice.525), channel_id=1, source_target_pairs={{0,1},{1,0},{2,3},{3,2},{4,5},{5,4},{6,7},{7,6},{8,9},{9,8},{10,11... | collective-permute-start | bytes 589832 | tf_op jit(solution)/shard_map/ppermute | solution.py:40
  160.4 6.4 %collective-permute-start.31 = (bf16[64,1024]{1,0:T(8,128)(2,1)S(1)}, bf16[64,1024]{1,0:T(8,128)(2,1)S(1)}, u32[]{:S(2)}, u32[]{:S(2)}) collective-permute-start(bf16[64,1024]{1,0:T(8,128)(2,1)S(1)} %pad_maximum_fusion.18), channel_id=1, source_target_pairs={{0,4},{4,0},{8,12},{12,8},{1,5},{5,1},{9,13},{13,9},{2,6},{6,2},{1... | collective-permute-start | bytes 393224 | tf_op jit(solution)/shard_map/ppermute | solution.py:45
  161.7 7.1 %collective-permute-start.40 = (bf16[48,1024]{1,0:T(8,128)(2,1)S(1)}, bf16[48,1024]{1,0:T(8,128)(2,1)S(1)}, u32[]{:S(2)}, u32[]{:S(2)}) collective-permute-start(bf16[48,1024]{1,0:T(8,128)(2,1)S(1)} %pad_maximum_fusion.22), channel_id=1, source_target_pairs={{0,4},{4,0},{8,12},{12,8},{1,5},{5,1},{9,13},{13,9},{2,6},{6,2},{1... | collective-permute-start | bytes 294920 | tf_op jit(solution)/shard_map/ppermute | solution.py:45
  166.9 7.3 %collective-permute-start.32 = (bf16[64,512]{1,0:T(8,128)(2,1)S(1)}, bf16[64,512]{1,0:T(8,128)(2,1)S(1)}, u32[]{:S(2)}, u32[]{:S(2)}) collective-permute-start(bf16[64,512]{1,0:T(8,128)(2,1)S(1)} %get-tuple-element.18), channel_id=1, source_target_pairs={{0,8},{4,12},{8,0},{12,4},{1,9},{5,13},{9,1},{13,5},{2,10},{6,14},... | collective-permute-start | bytes 196616 | tf_op jit(solution)/shard_map/ppermute | solution.py:45
  168.8 6.1 %collective-permute-start.41 = (bf16[48,512]{1,0:T(8,128)(2,1)S(1)}, bf16[48,512]{1,0:T(8,128)(2,1)S(1)}, u32[]{:S(2)}, u32[]{:S(2)}) collective-permute-start(bf16[48,512]{1,0:T(8,128)(2,1)S(1)} %get-tuple-element.21), channel_id=1, source_target_pairs={{0,8},{4,12},{8,0},{12,4},{1,9},{5,13},{9,1},{13,5},{2,10},{6,14},... | collective-permute-start | bytes 147464 | tf_op jit(solution)/shard_map/ppermute | solution.py:45
  (2 other events, 5.4 us)

commit v5 on v0

v5 whole, which is shorter than its diff:
```python
import functools

import jax
import jax.numpy as jnp
from jax import lax
from jax.experimental import pallas as pl
from jax.experimental.pallas import tpu as pltpu
from jax.sharding import PartitionSpec as P

PIECES = (1, 2, 1)
MIB = 1 << 20


def dot(left, right, dims):
    return lax.dot_general(left, right, (dims, ((), ())), preferred_element_type=jnp.float32)


def rows_by_cols(left, right):
    return dot(left, right, ((1,), (0,)))


def over_cols(left, right):
    return dot(left, right, ((1,), (1,)))


def over_rows(left, right):
    return dot(left, right, ((0,), (0,)))


def swiglu_grads(gate, up, dhid):
    sig = jax.nn.sigmoid(gate)
    hidden = (gate * sig * up).astype(jnp.bfloat16)
    d_gate = (dhid * up * sig * (1.0 + gate * (1.0 - sig))).astype(jnp.bfloat16)
    d_up = (dhid * gate * sig).astype(jnp.bfloat16)
    return hidden, d_gate, d_up


def shifted(value, axis, step):
    n = lax.axis_size(axis)
    return lax.ppermute(value, axis, [(i, (i + step) % n) for i in range(n)])


def swapped(value, axis, bit):
    n = lax.axis_size(axis)
    return lax.ppermute(value, axis, [(i, i ^ bit) for i in range(n)])


def summed(value, axis):
    total = value.astype(jnp.float32)
    for step in range(1, lax.axis_size(axis)):
        total = total + shifted(value, axis, step).astype(jnp.float32)
    return total


def own_first(value, axis):
    return jnp.concatenate([value] + [shifted(value, axis, step) for step in range(1, lax.axis_size(axis))], axis=0)


def home_rows(back, axis):
    n = lax.axis_size(axis)
    rows = back.shape[0] // n
    sent = back.astype(jnp.bfloat16)
    total = back[:rows]
    for step in range(1, n):
        block = sent[step * rows : (step + 1) * rows]
        total = total + shifted(block, axis, n - step).astype(jnp.float32)
    return total


def plain(acts, grad_out, w_gate, w_up, w_down):
    x = own_first(lax.all_gather(acts, "hid", axis=1, tiled=True), "tok")
    dy = own_first(lax.all_gather(grad_out, "hid", axis=1, tiled=True), "tok")
    gate = summed(rows_by_cols(x, w_gate).astype(jnp.bfloat16), "wid")
    up = summed(rows_by_cols(x, w_up).astype(jnp.bfloat16), "wid")
    dhid = summed(over_cols(dy, w_down).astype(jnp.bfloat16), "wid")
    hidden, d_gate, d_up = swiglu_grads(gate, up, dhid)
    back = home_rows(over_cols(d_gate, w_gate) + over_cols(d_up, w_up), "tok").astype(jnp.bfloat16)
    back = lax.psum_scatter(back, "hid", scatter_dimension=1, tiled=True)
    return (
        back,
        over_rows(x, d_gate).astype(jnp.bfloat16),
        over_rows(x, d_up).astype(jnp.bfloat16),
        over_rows(hidden, dy).astype(jnp.bfloat16),
    )


VMEM = pl.BlockSpec(memory_space=pltpu.VMEM)
ANYWHERE = pl.BlockSpec(memory_space=pl.ANY)


def local(kernel, outs, args, after=(), flops=0, moved=0, limit=8, scratch=(), out_specs=None):
    def body(*refs):
        kernel(refs[: len(args)], refs[len(args) + len(after) :])

    shapes = [jax.ShapeDtypeStruct(shape, dtype) for shape, dtype in outs]
    return pl.pallas_call(
        body,
        out_shape=shapes,
        in_specs=[VMEM] * len(args) + [ANYWHERE] * len(after),
        out_specs=out_specs if out_specs else [VMEM] * len(outs),
        scratch_shapes=list(scratch),
        compiler_params=pltpu.CompilerParams(vmem_limit_bytes=limit * MIB),
        cost_estimate=pl.CostEstimate(flops=flops, bytes_accessed=moved, transcendentals=0),
    )(*args, *after)


def lanes(index, width):
    return pl.ds(pl.multiple_of(index * width, width), width)


def cut_piece(acts, grad_out, lower, upper, after):
    rows, width = upper - lower, acts.shape[1]

    def kernel(ins, outs):
        outs[0][:rows] = ins[0][lower:upper]
        outs[0][rows:] = ins[1][lower:upper]

    return local(kernel, [((2 * rows, width), acts.dtype)], (acts, grad_out), after, limit=1)[0]


def pack(value, far, after=()):
    rows, width = value.shape

    def kernel(ins, outs):
        outs[0][:, :width] = ins[0][...]
        outs[0][:, width:] = ins[1][...]

    return local(kernel, [((rows, 2 * width), value.dtype)], (value, far), after, limit=1)[0]


def arrange(pair, near, after=()):
    rows, width = pair.shape[0], pair.shape[1] // 2

    def kernel(ins, outs):
        me = lax.axis_index("hid")
        for step, (source, at) in enumerate(((0, 0), (1, 0), (0, 1), (1, 1))):
            outs[0][:, lanes(me ^ step, width)] = ins[source][:, at * width : (at + 1) * width]

    return local(kernel, [((rows, 4 * width), pair.dtype)], (pair, near), after, limit=1)[0]


def blocks_of(width):
    full = width // 256
    return full, width - full * 256


def over_blocks(width, body):
    full, rest = blocks_of(width)

    @pl.loop(0, full)
    def _(j):
        body(lambda base: pl.ds(pl.multiple_of(base + j * 256, 128), 256))

    if rest:
        body(lambda base: pl.ds(base + full * 256, rest))


def forward(sources, weights, span, rows, after=()):
    lower, upper = span
    width, features, tokens = upper - lower, sources[0][0].shape[1], 2 * rows
    arrays = [array for own, theirs, _, _ in sources for array in (own, theirs)]

    def kernel(ins, refs):
        out, held = refs
        loaded = None
        for k, (_, _, first, down) in enumerate(sources):
            if loaded is None or arrays[2 * k] is not arrays[2 * loaded] or first != sources[loaded][2]:
                held[:rows] = ins[2 * k][first : first + rows]
                held[rows:] = ins[2 * k + 1][first : first + rows]
                loaded = k
            weight = ins[len(arrays) + k]
            top = k * tokens

            def product(at, weight=weight, top=top, down=down):
                if down:
                    value = over_cols(held[...], weight[at(lower), :])
                else:
                    value = rows_by_cols(held[...], weight[:, at(lower)])
                out[top : top + tokens, at(0)] = value.astype(out.dtype)

            over_blocks(width, product)

    return local(
        kernel,
        [((len(sources) * tokens, width), jnp.bfloat16)],
        (*arrays, *weights),
        after,
        flops=2 * len(sources) * tokens * features * width,
        scratch=[pltpu.VMEM((tokens, features), jnp.bfloat16)],
    )[0]


def backward(own, other, where, weights, span, rows, before, final, after=()):
    lower, upper = span
    width, features, tokens = upper - lower, weights[0].shape[0], 2 * rows
    count = len(own)
    ins_all = (*own, *other, *weights, *(() if before is None else (before,)))
    outs_all = [((tokens, width), jnp.bfloat16)] * 3
    outs_all += [((rows, features), jnp.float32), ((rows, features), jnp.bfloat16)] if final else [((tokens, features), jnp.float32)]

    def kernel(ins, outs):
        step = width // 7

        @pl.loop(0, 7)
        def _(j):
            at = lanes(j, step)

            def total(k):
                array, top = where[k]
                mine = ins[array][top : top + tokens, at].astype(jnp.float32)
                return mine + ins[count + array][top : top + tokens, at].astype(jnp.float32)

            for ref, value in zip(outs[:3], swiglu_grads(total(0), total(1), total(2))):
                ref[:, at] = value

        @pl.loop(0, features // 256)
        def _(j):
            at = lanes(j, 256)
            value = over_cols(outs[1][...], ins[2 * count][at, lower:upper])
            value = value + over_cols(outs[2][...], ins[2 * count + 1][at, lower:upper])
            if before is not None:
                value = value + ins[2 * count + 2][:, at]
            if final:
                outs[3][:, at] = value[:rows]
                outs[4][:, at] = value[rows:].astype(jnp.bfloat16)
            else:
                outs[3][:, at] = value

    return local(kernel, outs_all, ins_all, after, flops=4 * tokens * features * width)


def fold_near(value, theirs):
    rows, width = value.shape[0], value.shape[1] // 4

    def kernel(ins, outs):
        odd = lax.rem(lax.axis_index("hid"), 2)
        for i in range(2):
            at = slice(i * width, (i + 1) * width)
            for block, out in ((2 * i + odd, outs[0]), (2 * i + 1 - odd, outs[1])):
                source = lanes(block, width)
                out[:, at] = (ins[0][:, source] + ins[1][:, source].astype(jnp.float32)).astype(out.dtype)

    outs = [((rows, 2 * width), jnp.float32), ((rows, 2 * width), jnp.bfloat16)]
    return local(kernel, outs, (value, theirs), limit=4)


def fold_far(value, theirs):
    rows, width = value.shape[0], value.shape[1] // 2

    def kernel(ins, outs):
        upper = lax.div(lax.axis_index("hid"), 2)
        for block, out in ((upper, outs[0]), (1 - upper, outs[1])):
            source = lanes(block, width)
            out[...] = (ins[0][:, source] + ins[1][:, source].astype(jnp.float32)).astype(out.dtype)

    outs = [((rows, width), jnp.float32), ((rows, width), jnp.bfloat16)]
    return local(kernel, outs, (value, theirs), limit=4)


def fold_last(pairs):
    heights = [mine.shape[0] for mine, _ in pairs]
    width = pairs[0][0].shape[1]

    def kernel(ins, outs):
        top = 0
        for c, height in enumerate(heights):
            value = ins[2 * c][...] + ins[2 * c + 1][...].astype(jnp.float32)
            outs[0][top : top + height] = value.astype(jnp.bfloat16)
            top += height

    return local(
        kernel,
        [((sum(heights), width), jnp.bfloat16)],
        [array for pair in pairs for array in pair],
        limit=4,
        out_specs=[pl.BlockSpec((sum(heights), width), lambda: (0, 0))],
    )[0]


def scatter(mine, sent):
    keep, give = fold_near(mine, shifted(sent, "tok", 1))
    mine, give_far = fold_far(keep, swapped(give, "hid", 1))
    return keep, (mine, swapped(give_far, "hid", 2))


def stack(target, pieces, refs, at=None):
    top = 0
    for index, first, rows, column in pieces:
        width = target.shape[1]
        target[top : top + rows] = refs[index][first : first + rows, column : column + width]
        top += rows


def gradients(kernel, outs, arrays, old, grid, specs, scratch, after, flops, moved):
    def body(*refs):
        kernel(refs[: len(arrays)], refs[len(arrays) + len(old) + len(after) :])

    return pl.pallas_call(
        body,
        grid=grid,
        out_shape=[jax.ShapeDtypeStruct(shape, jnp.bfloat16) for shape in outs],
        in_specs=[VMEM] * len(arrays) + [ANYWHERE] * (len(old) + len(after)),
        out_specs=specs,
        scratch_shapes=scratch,
        input_output_aliases={len(arrays) + i: i for i in range(len(old))},
        compiler_params=pltpu.CompilerParams(vmem_limit_bytes=14 * MIB),
        cost_estimate=pl.CostEstimate(flops=flops, bytes_accessed=moved, transcendentals=0),
    )(*arrays, *old, *after)


def column_grads(xs, gs, us, part, parts, total, old, after=()):
    arrays = [p[0] for p in (*xs, *gs, *us)]
    n_x, n_g = len(xs), len(gs)
    tokens, features, width = sum(p[2] for p in xs), xs[0][0].shape[1], total // parts
    block = 512

    def kernel(ins, refs):
        gate_out, up_out, g_all, u_all = refs
        step = pl.program_id(0)

        @pl.when(step == 0)
        def _():
            stack(g_all, [(n_x + i, *p[1:]) for i, p in enumerate(gs)], ins)
            stack(u_all, [(n_x + n_g + i, *p[1:]) for i, p in enumerate(us)], ins)

        at = lanes(step, block)
        x = jnp.concatenate([ins[i][p[1] : p[1] + p[2], at] for i, p in enumerate(xs)], axis=0).T
        gate_out[...] = rows_by_cols(x, g_all[...]).astype(gate_out.dtype)
        up_out[...] = rows_by_cols(x, u_all[...]).astype(up_out.dtype)

    spec = pl.BlockSpec((block, width), lambda i: (i, part))
    scratch = [pltpu.VMEM((tokens, width), jnp.bfloat16)] * 2
    return gradients(
        kernel, [(features, total)] * 2, arrays, old, (features // block,), [spec, spec], scratch, after,
        4 * tokens * features * width, 4 * features * width,
    )


def row_grads(hs, ys, part, parts, total, old, after=()):
    arrays = [p[0] for p in (*hs, *ys)]
    n_h = len(hs)
    tokens, features, width = sum(p[2] for p in ys), ys[0][0].shape[1], total // parts
    block = 256

    def kernel(ins, refs):
        out, h_all = refs
        step = pl.program_id(0)

        @pl.when(step == 0)
        def _():
            pieces = [ins[i][p[1] : p[1] + p[2], p[3] : p[3] + width] for i, p in enumerate(hs)]
            h_all[...] = jnp.concatenate(pieces, axis=0).T

        at = lanes(step, block)
        y = jnp.concatenate([ins[n_h + i][p[1] : p[1] + p[2], at] for i, p in enumerate(ys)], axis=0)
        out[...] = rows_by_cols(h_all[...], y).astype(out.dtype)

    spec = pl.BlockSpec((width, block), lambda i: (part, i))
    scratch = [pltpu.VMEM((width, tokens), jnp.bfloat16)]
    return gradients(
        kernel, [(total, features)], arrays, old, (features // block,), [spec], scratch, after,
        2 * tokens * features * width, 2 * features * width,
    )


def piped(acts, grad_out, w_gate, w_up, w_down):
    unit = acts.shape[0] // sum(PIECES)
    bounds = [0]
    for size in PIECES:
        bounds.append(bounds[-1] + size * unit)
    spans = list(zip(bounds[:-1], bounds[1:]))
    heights = [upper - lower for lower, upper in spans]
    last = len(spans) - 1
    total = w_gate.shape[1]
    whole, halves = (0, total), ((0, total // 2), (total // 2, total))
    back_weights = (w_gate, w_up)

    lower, upper = spans[0]
    rows = heights[0]
    mixed, theirs = [], []
    for value in (acts[lower:upper], grad_out[lower:upper]):
        pair = pack(value, swapped(value, "hid", 2))
        mixed.append(arrange(pair, swapped(pair, "hid", 1)))
        theirs.append(shifted(mixed[-1], "tok", 1))
    x, dy = [(mixed[i], theirs[i], 0) for i in range(2)]
    gate = forward([(*x, False)], (w_gate,), whole, rows)
    rest = forward([(*x, False), (*dy, True)], (w_up, w_down), whole, rows, (gate,))
    tokens = 2 * rows
    inputs = [(x, dy)]
    sums = [[((gate, rest), ((0, 0), (1, 0), (1, tokens)))]]
    anchor, cut_after = rest, mixed[1]

    grads, scattered = [None] * len(spans), [None] * len(spans)

    def backward_piece(index, after):
        (own, where), = sums[index]
        other = [shifted(part, "wid", 1) for part in own]
        hidden, d_gate, d_up, mine, sent = backward(
            own, other, where, back_weights, whole, heights[index], None, True, after
        )
        grads[index] = (hidden, d_gate, d_up)
        return scatter(mine, sent)[1]

    for index in range(1, len(spans)):
        rows = heights[index]
        tokens = 2 * rows
        both = cut_piece(acts, grad_out, *spans[index], (cut_after,))
        pair = pack(both, swapped(both, "hid", 2), (anchor,))
        cut_after = pair
        own = arrange(pair, swapped(pair, "hid", 1))
        other = shifted(own, "tok", 1)
        x, dy = (own, other, 0), (own, other, rows)
        inputs.append((x, dy))
        sources = [(*x, False), (*x, False), (*dy, True)]
        where = ((0, 0), (0, tokens), (0, 2 * tokens))
        done, after = [], ()
        for span in halves if index == last else (whole,):
            part = forward(sources, (w_gate, w_up, w_down), span, rows, after)
            done.append(((part,), where))
            after = (part,)
        sums.append(done)
        anchor = after[0]
        scattered[index - 1] = backward_piece(index - 1, (anchor,))

    rows = heights[last]
    xs, ys = [], []
    for index, (x, dy) in enumerate(inputs):
        for pieces, (own, other, first) in ((xs, x), (ys, dy)):
            pieces.append((own, first, heights[index], 0))
            pieces.append((other, first, heights[index], 0))
    before, after, columns, downs = None, (), (), ()
    for part, (own, where) in enumerate(sums[last]):
        other = [shifted(value, "wid", 1) for value in own]
        results = backward(own, other, where, back_weights, halves[part], rows, before, part == 1, after)
        before = results[3]
        hs, gs, us = [
            [(grads[c][k], 0, 2 * heights[c], halves[part][0]) for c in range(last)] + [(results[k], 0, 2 * rows, 0)]
            for k in range(3)
        ]
        downs = row_grads(hs, ys, part, 2, total, downs)
        if part == 1:
            keep, scattered[last] = scatter(*results[3:])
            after = (keep,)
        columns = column_grads(xs, gs, us, part, 2, total, columns, after if part == 1 else ())
        after = (downs[0], columns[0])
    return fold_last(scattered), columns[0], columns[1], downs[0]


def shards(acts, grad_out, w_gate, w_up, w_down):
    sizes = tuple(lax.axis_size(axis) for axis in ("hid", "wid", "tok"))
    aligned = acts.shape[0] % (16 * sum(PIECES)) == 0 and acts.shape[1] % 128 == 0 and w_gate.shape[0] % 512 == 0 and w_gate.shape[1] % 1792 == 0
    if sizes == (4, 2, 2) and aligned:
        return piped(acts, grad_out, w_gate, w_up, w_down)
    return plain(acts, grad_out, w_gate, w_up, w_down)


def solution(mesh):
    placed = (
        P(("groups", "tok"), ("wid", "hid")),
        P(("groups", "tok"), ("wid", "hid")),
        P("wid", ("hid", "tok")),
        P("wid", ("hid", "tok")),
        P(("hid", "tok"), "wid"),
    )
    return jax.shard_map(
        shards,
        mesh=mesh,
        in_specs=placed,
        out_specs=(
            P(("groups", "tok"), ("wid", "hid")),
            P(("groups", "wid"), ("hid", "tok")),
            P(("groups", "wid"), ("hid", "tok")),
            P(("groups", "hid", "tok"), "wid"),
        ),
        check_vma=False,
    )
```

time: 290 us -> 197 us (0.68)
  Pallas kernels: 0 us -> 69.3 us
  matrix products: 65.1 us -> 0 us
  other arithmetic: 42.1 us -> 0.01 us
  blocking collectives: 40.4 us -> 0 us
  starting transfers between devices: 0.39 us -> 24.6 us
  waiting for transfers between devices: 108 us -> 88.4 us
  between operations: 13.9 us -> 0.95 us
  local copies, waits for them, and re-layouts: 20 us -> 13.1 us
    psum x1 -> x0, waiting for transfers between devices: 107 us -> none  [shards(): lax.psum(up_part.astype(jnp.bfloat16), 'wid').astype(jnp.float32)]
    ppermute x0 -> x26, waiting for transfers between devices: none -> 88.4 us  [the longest x12 49.5 us: shifted(): return lax.ppermute(value, axis, [(i, (i + step) % n) for i in range(n)])]
    pallas_call x0 -> x30, Pallas kernels: none -> 69.3 us  [the longest x26 46.7 us: local(): pl.pallas_call(body, out_shape=shapes, in_specs=[VMEM] * len(args) + [ANY...]
    dot_general x11 -> x0, matrix products: 65.1 us -> none  [the longest x6 32.3 us: over_rows(): lax.dot_general(left, right, (((0,), (0,)), ((), ())), preferred_element_...]
    convert_element_type x4 -> x0, other arithmetic: 42.1 us -> none  [the longest x3 38.1 us: blockwise(): return total.astype(jnp.bfloat16)]
    all_gather x2 -> x0, blocking collectives: 40.4 us -> none  [the longest x1 21.8 us: shards(): lax.all_gather(acts, 'hid', axis=1, tiled=True)]
    ppermute x0 -> x26, starting transfers between devices: none -> 24.6 us  [the longest x14 17.8 us: swapped(): return lax.ppermute(value, axis, [(i, i ^ bit) for i in range(n)])]
    unnamed x18 -> x26, local copies, waits for them, and re-layouts: 20 us -> 11.3 us
  transfers between devices with their start and end apart: 5 -> 26, of which waited for: 1 -> 11; matrix products, arithmetic and copies ran while one was open for 36% -> 0% of each run, Pallas kernels for 0% -> 30%
where the time goes in v5:
time: 197 us; the launch traced here: 196 us
  waiting for transfers between devices  88.4 us (45%)
  Pallas kernels  69.3 us (35%)
  starting transfers between devices  24.6 us (12%)
  local copies, waits for them, and re-layouts  13.1 us (7%)
    ppermute x12, waiting for transfers between devices, shifted(): return lax.ppermute(value, axis, [(i, (i + step) % n) for i in range(n)])  49.5 us
    pallas_call x26, Pallas kernels, local(): pl.pallas_call(body, out_shape=shapes, in_specs=[VMEM] * len(args) + [ANY...  46.7 us
    ppermute x14, waiting for transfers between devices, swapped(): return lax.ppermute(value, axis, [(i, i ^ bit) for i in range(n)])  38.9 us
    pallas_call x4, Pallas kernels, gradients(): pl.pallas_call(body, grid=grid, out_shape=[jax.ShapeDtypeStruct(shape, jn...  22.6 us
    ppermute x14, starting transfers between devices, swapped(): return lax.ppermute(value, axis, [(i, i ^ bit) for i in range(n)])  17.8 us
    unnamed x26, local copies, waits for them, and re-layouts  11.3 us
    ppermute x12, starting transfers between devices, shifted(): return lax.ppermute(value, axis, [(i, (i + step) % n) for i in range(n)])  6.8 us
  transfers between devices with their start and end apart: 26, of which 11 were waited for; matrix products, arithmetic and copies ran while one was open for 0% of the time, Pallas kernels for 30%

profile of v5, /device:TPU:0, one launch (start us, length us, event | category | flops | bytes accessed | tf_op | source)
XLA Modules:
  0.0 196.3 jit_solution(10156047539684227483)
XLA Ops:
  0.6 1.0 slice.6.refs_0_
  1.6 4.0 %collective-permute-start = (bf16[48,512]{1,0:T(8,128)(2,1)S(1)}, bf16[48,512]{1,0:T(8,128)(2,1)S(1)}, u32[]{:S(2)}, u32[]{:S(2)}) collective-permute-start(bf16[48,512]{1,0:T(8,128)(2,1)S(1)} %slice.6.refs_0_), channel_id=1, source_target_pairs={{0,8},{4,12},{8,0},{12,4},{1,9},{5,13},{9,1},{13,5},{2,10},{6,14},... | collective-permute-start | bytes 147464 | tf_op jit(solution)/shard_map/ppermute | solution.py:45
  5.6 2.6 %collective-permute-done.refs_1_ = bf16[48,512]{1,0:T(8,128)(2,1)S(1)} collective-permute-done((bf16[48,512]{1,0:T(8,128)(2,1)S(1)}, bf16[48,512]{1,0:T(8,128)(2,1)S(1)}, u32[]{:S(2)}, u32[]{:S(2)}) %collective-permute-start) | collective-permute-done | bytes 49184 | tf_op jit(solution)/shard_map/ppermute | solution.py:45
  8.2 1.4 collective-permute-start.1
  9.7 0.8 slice.7.refs_0_
  10.5 3.0 %collective-permute-start.3 = (bf16[48,512]{1,0:T(8,128)(2,1)S(1)}, bf16[48,512]{1,0:T(8,128)(2,1)S(1)}, u32[]{:S(2)}, u32[]{:S(2)}) collective-permute-start(bf16[48,512]{1,0:T(8,128)(2,1)S(1)} %slice.7.refs_0_), channel_id=1, source_target_pairs={{0,8},{4,12},{8,0},{12,4},{1,9},{5,13},{9,1},{13,5},{2,10},{6,14},... | collective-permute-start | bytes 147464 | tf_op jit(solution)/shard_map/ppermute | solution.py:45
  13.5 2.6 %collective-permute-done.3.refs_1_ = bf16[48,512]{1,0:T(8,128)(2,1)S(1)} collective-permute-done((bf16[48,512]{1,0:T(8,128)(2,1)S(1)}, bf16[48,512]{1,0:T(8,128)(2,1)S(1)}, u32[]{:S(2)}, u32[]{:S(2)}) %collective-permute-start.3) | collective-permute-done | bytes 49184 | tf_op jit(solution)/shard_map/ppermute | solution.py:45
  16.4 4.4 %collective-permute-done.4.refs_1_ = bf16[48,1024]{1,0:T(8,128)(2,1)S(1)} collective-permute-done((bf16[48,1024]{1,0:T(8,128)(2,1)S(1)}, bf16[48,1024]{1,0:T(8,128)(2,1)S(1)}, u32[]{:S(2)}, u32[]{:S(2)}) %collective-permute-start.4) | collective-permute-done | bytes 98336 | tf_op jit(solution)/shard_map/ppermute | solution.py:45
  20.9 0.9 copy-done.5
  21.8 0.9 copy-done.7
  22.8 2.9 %collective-permute-start.8 = (bf16[192,512]{1,0:T(8,128)(2,1)S(1)}, bf16[192,512]{1,0:T(8,128)(2,1)S(1)}, u32[]{:S(2)}, u32[]{:S(2)}) collective-permute-start(bf16[192,512]{1,0:T(8,128)(2,1)S(1)} %shard_map.90.refs_0_), channel_id=1, source_target_pairs={{0,8},{4,12},{8,0},{12,4},{1,9},{5,13},{9,1},{13,5},{2,10},{6,14},... | collective-permute-start | bytes 589832 | tf_op jit(solution)/shard_map/ppermute | solution.py:45
  25.7 3.1 %copy-done.1 = bf16[2048,1792]{1,0:T(8,128)(2,1)S(1)} copy-done((bf16[2048,1792]{1,0:T(8,128)(2,1)S(1)}, bf16[2048,1792]{1,0:T(8,128)(2,1)}, u32[]{:S(2)}) %copy-start.1) | copy-done | bytes 7340056
  28.8 2.2 %shard_map.86.refs_6_.refs_0_ = bf16[96,1792]{1,0:T(8,128)(2,1)S(1)} custom-call(bf16[48,2048]{1,0:T(8,128)(2,1)S(1)} %shard_map.85.refs_0_, bf16[48,2048]{1,0:T(8,128)(2,1)S(1)} %collective-permute-done.2.refs_1_, bf16[2048,1792]{1,0:T(8,128)(2,1)S(1)} %copy-done.1), custom_call_target="tpu_custom_call" | custom-call | flops 704643072 | tf_op jit(solution)/shard_map/pallas_call | solution.py:96
  31.1 3.2 %copy-done.2 = bf16[1792,2048]{1,0:T(8,128)(2,1)S(1)} copy-done((bf16[1792,2048]{1,0:T(8,128)(2,1)S(1)}, bf16[1792,2048]{1,0:T(8,128)(2,1)}, u32[]{:S(2)}) %copy-start.2) | copy-done | bytes 7340056
  34.3 5.5 %shard_map.89.refs_2_.refs_1_ = bf16[192,1792]{1,0:T(8,128)(2,1)S(1)} custom-call(bf16[48,2048]{1,0:T(8,128)(2,1)S(1)} %shard_map.85.refs_0_, bf16[48,2048]{1,0:T(8,128)(2,1)S(1)} %collective-permute-done.2.refs_1_, bf16[48,2048]{1,0:T(8,128)(2,1)S(1)} %shard_map.88.refs_2_.refs_3_, bf16[48,2048]{1,0:T(8,128)(2,1)S(1)} %collective-permute-done.5.refs_3_.refs_4_, ...), custom_call_target="tpu_custom_call" | custom-call | flops 1409286144 | tf_op jit(solution)/shard_map/pallas_call | solution.py:96
  39.9 11.2 %collective-permute-done.9.refs_1_ = bf16[192,1024]{1,0:T(8,128)(2,1)S(1)} collective-permute-done((bf16[192,1024]{1,0:T(8,128)(2,1)S(1)}, bf16[192,1024]{1,0:T(8,128)(2,1)S(1)}, u32[]{:S(2)}, u32[]{:S(2)}) %collective-permute-start.9) | collective-permute-done | bytes 393248 | tf_op jit(solution)/shard_map/ppermute | solution.py:45
  51.3 2.3 %collective-permute-done.10.refs_1_.refs_3_.refs_5_.refs_6_ = bf16[192,2048]{1,0:T(8,128)(2,1)S(1)} collective-permute-done((bf16[192,2048]{1,0:T(8,128)(2,1)S(1)}, bf16[192,2048]{1,0:T(8,128)(2,1)S(1)}, u32[]{:S(2)}, u32[]{:S(2)}) %collective-permute-start.10) | collective-permute-done | bytes 786464 | tf_op jit(solution)/shard_map/ppermute | solution.py:40
  53.6 9.2 %shard_map.93.refs_6_.refs_2_.refs_0_ = bf16[576,1792]{1,0:T(8,128)(2,1)S(1)} custom-call(bf16[192,2048]{1,0:T(8,128)(2,1)S(1)} %shard_map.92.refs_0_.refs_2_.refs_4_.refs_5_, bf16[192,2048]{1,0:T(8,128)(2,1)S(1)} %collective-permute-done.10.refs_1_.refs_3_.refs_5_.refs_6_, bf16[192,2048]{1,0:T(8,128)(2,1)S(1)} %shard_map.92.refs_0_.refs_2_.refs_4_.refs_5_, ...), custom_call_target="tpu_custom_call" | custom-call | flops 4227858432 | tf_op jit(solution)/shard_map/pallas_call | solution.py:96
  62.8 1.6 collective-permute-start.14
  64.4 0.4 collective-permute-start.15
  64.7 7.0 %collective-permute-done.15.refs_1_ = bf16[96,512]{1,0:T(8,128)(2,1)S(1)} collective-permute-done((bf16[96,512]{1,0:T(8,128)(2,1)S(1)}, bf16[96,512]{1,0:T(8,128)(2,1)S(1)}, u32[]{:S(2)}, u32[]{:S(2)}) %collective-permute-start.15) | collective-permute-done | bytes 98336 | tf_op jit(solution)/shard_map/ppermute | solution.py:45
  71.8 6.8 %collective-permute-done.16.refs_1_ = bf16[96,1024]{1,0:T(8,128)(2,1)S(1)} collective-permute-done((bf16[96,1024]{1,0:T(8,128)(2,1)S(1)}, bf16[96,1024]{1,0:T(8,128)(2,1)S(1)}, u32[]{:S(2)}, u32[]{:S(2)}) %collective-permute-start.16) | collective-permute-done | bytes 196640 | tf_op jit(solution)/shard_map/ppermute | solution.py:45
  78.7 0.6 collective-permute-start.7
  79.4 1.5 collective-permute-start.6
  80.8 4.1 %shard_map.100.refs_9_.refs_0_ = bf16[288,896]{1,0:T(8,128)(2,1)S(1)} custom-call(bf16[96,2048]{1,0:T(8,128)(2,1)S(1)} %shard_map.99.refs_0_.refs_2_.refs_4_.refs_7_, bf16[96,2048]{1,0:T(8,128)(2,1)S(1)} %collective-permute-done.17.refs_1_.refs_3_.refs_5_.refs_8_, bf16[96,2048]{1,0:T(8,128)(2,1)S(1)} %shard_map.99.refs_0_.refs_2_.refs_4_.refs_7_, ...), custom_call_target="tpu_custom_call" | custom-call | flops 1056964608 | tf_op jit(solution)/shard_map/pallas_call | solution.py:96
  84.9 0.6 collective-permute-start.22
  85.5 47.2 %collective-permute-done.6.refs_2_ = bf16[96,1792]{1,0:T(8,128)(2,1)S(1)} collective-permute-done((bf16[96,1792]{1,0:T(8,128)(2,1)S(1)}, bf16[96,1792]{1,0:T(8,128)(2,1)S(1)}, u32[]{:S(2)}, u32[]{:S(2)}) %collective-permute-start.6) | collective-permute-done | bytes 344096 | tf_op jit(solution)/shard_map/ppermute | solution.py:40
  132.8 6.1 %shard_map.94 = (bf16[96,1792]{1,0:T(8,128)(2,1)S(1)}, bf16[96,1792]{1,0:T(8,128)(2,1)S(1)}, bf16[96,1792]{1,0:T(8,128)(2,1)S(1)}, f32[48,2048]{1,0:T(8,128)S(1)}, bf16[48,2048]{1,0:T(8,128)(2,1)S(1)}) custom-call(bf16[96,1792]{1,0:T(8,128)(2,1)S(1)} %shard_map.86.refs_6_.refs_0_, bf16[192,1792]{1,0:T(8,128)(2,1)S(1)} %shard_map.89.refs_2_.refs_1_, ...), custom_call_target="tpu_custom_call" | custom-call | flops 1409286144 | tf_op jit(solution)/shard_map/pallas_call | solution.py:96
  139.0 4.1 %shard_map.101.refs_4_.refs_0_ = bf16[288,896]{1,0:T(8,128)(2,1)S(1)} custom-call(bf16[96,2048]{1,0:T(8,128)(2,1)S(1)} %shard_map.99.refs_0_.refs_2_.refs_4_.refs_7_, bf16[96,2048]{1,0:T(8,128)(2,1)S(1)} %collective-permute-done.17.refs_1_.refs_3_.refs_5_.refs_8_, bf16[96,2048]{1,0:T(8,128)(2,1)S(1)} %shard_map.99.refs_0_.refs_2_.refs_4_.refs_7_, ...), custom_call_target="tpu_custom_call" | custom-call | flops 1056964608 | tf_op jit(solution)/shard_map/pallas_call | solution.py:96
  143.1 1.6 collective-permute-start.21
  144.7 3.6 %shard_map.105 = (bf16[96,896]{1,0:T(8,128)(2,1)S(1)}, bf16[96,896]{1,0:T(8,128)(2,1)S(1)}, bf16[96,896]{1,0:T(8,128)(2,1)S(1)}, f32[96,2048]{1,0:T(8,128)S(1)}) custom-call(bf16[288,896]{1,0:T(8,128)(2,1)S(1)} %shard_map.100.refs_9_.refs_0_, bf16[288,896]{1,0:T(8,128)(2,1)S(1)} %collective-permute-done.22.refs_1_, bf16[2048,1792]{1,0:T(8,128)(2,1)S(1)} %bitcast.1, ...), custom_call_target="tpu_custom_call" | custom-call | flops 704643072 | tf_op jit(solution)/shard_map/pallas_call | solution.py:96
  148.3 7.0 %shard_map.102 = (bf16[192,1792]{1,0:T(8,128)(2,1)S(1)}, bf16[192,1792]{1,0:T(8,128)(2,1)S(1)}, bf16[192,1792]{1,0:T(8,128)(2,1)S(1)}, f32[96,2048]{1,0:T(8,128)S(1)}, bf16[96,2048]{1,0:T(8,128)(2,1)S(1)}) custom-call(bf16[576,1792]{1,0:T(8,128)(2,1)S(1)} %shard_map.93.refs_6_.refs_2_.refs_0_, bf16[576,1792]{1,0:T(8,128)(2,1)S(1)} %collective-permute-done.14.refs_1_, ...), custom_call_target="tpu_custom_call" | custom-call | flops 2818572288 | tf_op jit(solution)/shard_map/pallas_call | solution.py:96
  155.3 0.3 collective-permute-start.18
  155.6 6.0 %shard_map.107 = (bf16[2048,1792]{1,0:T(8,128)(2,1)}, bf16[2048,1792]{1,0:T(8,128)(2,1)}) custom-call(bf16[48,2048]{1,0:T(8,128)(2,1)S(1)} %shard_map.85.refs_0_, bf16[48,2048]{1,0:T(8,128)(2,1)S(1)} %collective-permute-done.2.refs_1_, bf16[192,2048]{1,0:T(8,128)(2,1)S(1)} %shard_map.92.refs_0_.refs_2_.refs_4_.refs_5_, ...), custom_call_target="tpu_custom_call" | custom-call | flops 2818572288 | bytes 7340032 | tf_op jit(solution)/shard_map/pallas_call | solution.py:298
  161.6 5.3 %shard_map.106.refs_5_.refs_9_ = bf16[1792,2048]{1,0:T(8,128)(2,1)} custom-call(bf16[96,1792]{1,0:T(8,128)(2,1)S(1)} %get-tuple-element.52.refs_0_, bf16[192,1792]{1,0:T(8,128)(2,1)S(1)} %get-tuple-element.53.refs_1_, bf16[96,896]{1,0:T(8,128)(2,1)S(1)} %get-tuple-element.54.refs_2_, bf16[48,2048]{1,0:T(8,128)(2,1)S(1)} %shard_map.88.refs_2_.refs_3_, ...), custom_call_target="tpu_custom_call" | custom-call | flops 1409286144 | bytes 3670016 | tf_op jit(solution)/shard_map/pallas_call | solution.py:298
  166.9 3.1 %copy-done.3 = bf16[1792,2048]{1,0:T(8,128)(2,1)S(1)} copy-done((bf16[1792,2048]{1,0:T(8,128)(2,1)S(1)}, bf16[1792,2048]{1,0:T(8,128)(2,1)}, u32[]{:S(2)}) %copy-start.3) | copy-done | bytes 7340056
  170.0 3.7 %shard_map.108 = (bf16[96,896]{1,0:T(8,128)(2,1)S(1)}, bf16[96,896]{1,0:T(8,128)(2,1)S(1)}, bf16[96,896]{1,0:T(8,128)(2,1)S(1)}, f32[48,2048]{1,0:T(8,128)S(1)}, bf16[48,2048]{1,0:T(8,128)(2,1)S(1)}) custom-call(bf16[288,896]{1,0:T(8,128)(2,1)S(1)} %shard_map.101.refs_4_.refs_0_, bf16[288,896]{1,0:T(8,128)(2,1)S(1)} %collective-permute-done.21.refs_1_, ...), custom_call_target="tpu_custom_call" | custom-call | flops 704643072 | tf_op jit(solution)/shard_map/pallas_call | solution.py:96
  173.6 0.4 collective-permute-start.23
  174.1 0.3 collective-permute-start.12
  174.5 1.8 collective-permute-start.19
  176.3 3.5 %collective-permute-done.12.refs_1_ = bf16[48,1024]{1,0:T(8,128)(2,1)S(1)} collective-permute-done((bf16[48,1024]{1,0:T(8,128)(2,1)S(1)}, bf16[48,1024]{1,0:T(8,128)(2,1)S(1)}, u32[]{:S(2)}, u32[]{:S(2)}) %collective-permute-start.12) | collective-permute-done | bytes 98336 | tf_op jit(solution)/shard_map/ppermute | solution.py:45
  179.8 0.4 collective-permute-start.13
  180.4 5.3 %shard_map.113 = bf16[1792,2048]{1,0:T(8,128)(2,1)} custom-call(bf16[96,1792]{1,0:T(8,128)(2,1)S(1)} %get-tuple-element.52.refs_0_, bf16[192,1792]{1,0:T(8,128)(2,1)S(1)} %get-tuple-element.53.refs_1_, bf16[96,896]{1,0:T(8,128)(2,1)S(1)} %get-tuple-element.73.refs_2_, ...), custom_call_target="tpu_custom_call", output_to_operand_aliasing={{}: (9, {})} | custom-call | flops 1409286144 | bytes 3670016 | tf_op jit(solution)/shard_map/pallas_call | solution.py:298
  185.7 0.7 collective-permute-done.24.refs_1_
  186.4 1.9 collective-permute-start.25
  188.4 1.1 collective-permute-start.20
  189.5 6.0 %shard_map.112 = (bf16[2048,1792]{1,0:T(8,128)(2,1)}, bf16[2048,1792]{1,0:T(8,128)(2,1)}) custom-call(bf16[48,2048]{1,0:T(8,128)(2,1)S(1)} %shard_map.85.refs_0_, bf16[48,2048]{1,0:T(8,128)(2,1)S(1)} %collective-permute-done.2.refs_1_, ...), custom_call_target="tpu_custom_call", output_to_operand_aliasing={{0}: (12, {}), {1}: (13, {})} | custom-call | flops 2818572288 | bytes 7340032 | tf_op jit(solution)/shard_map/pallas_call | solution.py:298
  195.6 0.7 shard_map.111
  (64 shorter events, 1.4 us)
Async XLA Ops:
  0.6 30.4 %copy-start = (bf16[2048,1792]{1,0:T(8,128)(2,1)S(1)}, bf16[2048,1792]{1,0:T(8,128)(2,1)}, u32[]{:S(2)}) copy-start(bf16[2048,1792]{1,0:T(8,128)(2,1)} %refs_3_.5) | copy-start | bytes 22020100
  1.6 6.6 %collective-permute-start = (bf16[48,512]{1,0:T(8,128)(2,1)S(1)}, bf16[48,512]{1,0:T(8,128)(2,1)S(1)}, u32[]{:S(2)}, u32[]{:S(2)}) collective-permute-start(bf16[48,512]{1,0:T(8,128)(2,1)S(1)} %slice.6.refs_0_), channel_id=1, source_target_pairs={{0,8},{4,12},{8,0},{12,4},{1,9},{5,13},{9,1},{13,5},{2,10},{6,14},... | collective-permute-start | bytes 147464 | tf_op jit(solution)/shard_map/ppermute | solution.py:45
  8.2 8.0 %collective-permute-start.1 = (bf16[48,1024]{1,0:T(8,128)(2,1)S(1)}, bf16[48,1024]{1,0:T(8,128)(2,1)S(1)}, u32[]{:S(2)}, u32[]{:S(2)}) collective-permute-start(bf16[48,1024]{1,0:T(8,128)(2,1)S(1)} %shard_map.84.refs_0_), channel_id=1, source_target_pairs={{0,4},{4,0},{8,12},{12,8},{1,5},{5,1},{9,13},{13,9},{2,6},{6,2},{1... | collective-permute-start | bytes 294920 | tf_op jit(solution)/shard_map/ppermute | solution.py:45
  10.5 5.6 %collective-permute-start.3 = (bf16[48,512]{1,0:T(8,128)(2,1)S(1)}, bf16[48,512]{1,0:T(8,128)(2,1)S(1)}, u32[]{:S(2)}, u32[]{:S(2)}) collective-permute-start(bf16[48,512]{1,0:T(8,128)(2,1)S(1)} %slice.7.refs_0_), channel_id=1, source_target_pairs={{0,8},{4,12},{8,0},{12,4},{1,9},{5,13},{9,1},{13,5},{2,10},{6,14},... | collective-permute-start | bytes 147464 | tf_op jit(solution)/shard_map/ppermute | solution.py:45
  16.1 4.7 %collective-permute-start.4 = (bf16[48,1024]{1,0:T(8,128)(2,1)S(1)}, bf16[48,1024]{1,0:T(8,128)(2,1)S(1)}, u32[]{:S(2)}, u32[]{:S(2)}) collective-permute-start(bf16[48,1024]{1,0:T(8,128)(2,1)S(1)} %shard_map.87.refs_0_), channel_id=1, source_target_pairs={{0,4},{4,0},{8,12},{12,8},{1,5},{5,1},{9,13},{13,9},{2,6},{6,2},{1... | collective-permute-start | bytes 294920 | tf_op jit(solution)/shard_map/ppermute | solution.py:45
  16.3 9.4 %collective-permute-start.2 = (bf16[48,2048]{1,0:T(8,128)(2,1)S(1)}, bf16[48,2048]{1,0:T(8,128)(2,1)S(1)}, u32[]{:S(2)}, u32[]{:S(2)}) collective-permute-start(bf16[48,2048]{1,0:T(8,128)(2,1)S(1)} %shard_map.85.refs_0_), channel_id=1, source_target_pairs={{0,1},{1,0},{2,3},{3,2},{4,5},{5,4},{6,7},{7,6},{8,9},{9,8},{10,11... | collective-permute-start | bytes 589832 | tf_op jit(solution)/shard_map/ppermute | solution.py:40
  20.8 10.2 %collective-permute-start.5 = (bf16[48,2048]{1,0:T(8,128)(2,1)S(1)}, bf16[48,2048]{1,0:T(8,128)(2,1)S(1)}, u32[]{:S(2)}, u32[]{:S(2)}) collective-permute-start(bf16[48,2048]{1,0:T(8,128)(2,1)S(1)} %shard_map.88.refs_2_.refs_3_), channel_id=1, source_target_pairs={{0,1},{1,0},{2,3},{3,2},{4,5},{5,4},{6,7},{7,6},{8,9},{9,8},{10,11... | collective-permute-start | bytes 589832 | tf_op jit(solution)/shard_map/ppermute | solution.py:40
  20.9 0.9 copy-start.5
  21.8 0.9 copy-start.7
  22.8 17.0 %collective-permute-start.8 = (bf16[192,512]{1,0:T(8,128)(2,1)S(1)}, bf16[192,512]{1,0:T(8,128)(2,1)S(1)}, u32[]{:S(2)}, u32[]{:S(2)}) collective-permute-start(bf16[192,512]{1,0:T(8,128)(2,1)S(1)} %shard_map.90.refs_0_), channel_id=1, source_target_pairs={{0,8},{4,12},{8,0},{12,4},{1,9},{5,13},{9,1},{13,5},{2,10},{6,14},... | collective-permute-start | bytes 589832 | tf_op jit(solution)/shard_map/ppermute | solution.py:45
  25.7 3.1 %copy-start.1 = (bf16[2048,1792]{1,0:T(8,128)(2,1)S(1)}, bf16[2048,1792]{1,0:T(8,128)(2,1)}, u32[]{:S(2)}) copy-start(bf16[2048,1792]{1,0:T(8,128)(2,1)} %refs_2_.7) | copy-start | bytes 22020100
  28.8 24.8 %slice-start = ((s8[7340032]{0:T(1024)(128)(4,1)}), s8[4194304]{0:T(1024)(128)(4,1)S(1)}, s32[]{:S(2)}) async-start(s8[7340032]{0:T(1024)(128)(4,1)} %bitcast), calls=%async_computation | async-start | bytes 8388608
  31.0 22.5 %slice-start.1 = ((s8[7340032]{0:T(1024)(128)(4,1)}), s8[3145728]{0:T(1024)(128)(4,1)S(1)}, s32[]{:S(2)}) async-start(s8[7340032]{0:T(1024)(128)(4,1)} %bitcast), calls=%async_computation.1 | async-start | bytes 6291456
  31.1 3.2 %copy-start.2 = (bf16[1792,2048]{1,0:T(8,128)(2,1)S(1)}, bf16[1792,2048]{1,0:T(8,128)(2,1)}, u32[]{:S(2)}) copy-start(bf16[1792,2048]{1,0:T(8,128)(2,1)} %refs_8_.5) | copy-start | bytes 22020100
  39.8 11.3 %collective-permute-start.9 = (bf16[192,1024]{1,0:T(8,128)(2,1)S(1)}, bf16[192,1024]{1,0:T(8,128)(2,1)S(1)}, u32[]{:S(2)}, u32[]{:S(2)}) collective-permute-start(bf16[192,1024]{1,0:T(8,128)(2,1)S(1)} %shard_map.91.refs_0_.refs_2_), channel_id=1, source_target_pairs={{0,4},{4,0},{8,12},{12,8},{1,5},{5,1},{9,13},{13,9},{2,6},{6,2},{1... | collective-permute-start | bytes 1179656 | tf_op jit(solution)/shard_map/ppermute | solution.py:45
  51.2 13.2 %copy-start.6 = (bf16[192,512]{1,0:T(8,128)(2,1)S(1)}, bf16[192,512]{1,0:T(8,128)(2,1)}, u32[]{:S(2)}) copy-start(bf16[192,512]{1,0:T(8,128)(2,1)} %refs_0_.3) | copy-start | bytes 589828
  51.2 13.1 %copy-start.8 = (bf16[192,512]{1,0:T(8,128)(2,1)S(1)}, bf16[192,512]{1,0:T(8,128)(2,1)}, u32[]{:S(2)}) copy-start(bf16[192,512]{1,0:T(8,128)(2,1)} %refs_1_.3) | copy-start | bytes 589828
  51.2 2.4 %collective-permute-start.10 = (bf16[192,2048]{1,0:T(8,128)(2,1)S(1)}, bf16[192,2048]{1,0:T(8,128)(2,1)S(1)}, u32[]{:S(2)}, u32[]{:S(2)}) collective-permute-start(bf16[192,2048]{1,0:T(8,128)(2,1)S(1)} %shard_map.92.refs_0_.refs_2_.refs_4_.refs_5_), channel_id=1, source_target_pairs={{0,1},{1,0},{2,3},{3,2},{4,5},{5,4},{6,7},{7,6},{8,9},{9,8},{10,11... | collective-permute-start | bytes 2359304 | tf_op jit(solution)/shard_map/ppermute | solution.py:40
  62.8 85.5 %collective-permute-start.14 = (bf16[576,1792]{1,0:T(8,128)(2,1)S(1)}, bf16[576,1792]{1,0:T(8,128)(2,1)S(1)}, u32[]{:S(2)}, u32[]{:S(2)}) collective-permute-start(bf16[576,1792]{1,0:T(8,128)(2,1)S(1)} %shard_map.93.refs_6_.refs_2_.refs_0_), channel_id=1, source_target_pairs={{0,2},{2,0},{1,3},{3,1},{4,6},{6,4},{5,7},{7,5},{8,10},{10,8},{9,1... | collective-permute-start | bytes 6193160 | tf_op jit(solution)/shard_map/ppermute | solution.py:40
  64.4 7.3 %collective-permute-start.15 = (bf16[96,512]{1,0:T(8,128)(2,1)S(1)}, bf16[96,512]{1,0:T(8,128)(2,1)S(1)}, u32[]{:S(2)}, u32[]{:S(2)}) collective-permute-start(bf16[96,512]{1,0:T(8,128)(2,1)S(1)} %shard_map.97.refs_0_), channel_id=1, source_target_pairs={{0,8},{4,12},{8,0},{12,4},{1,9},{5,13},{9,1},{13,5},{2,10},{6,14},... | collective-permute-start | bytes 294920 | tf_op jit(solution)/shard_map/ppermute | solution.py:45
  71.7 67.3 %slice-start.2 = ((s8[7340032]{0:T(1024)(128)(4,1)}), s8[4194304]{0:T(1024)(128)(4,1)S(1)}, s32[]{:S(2)}) async-start(s8[7340032]{0:T(1024)(128)(4,1)} %bitcast.2), calls=%async_computation.2 | async-start | bytes 8388608
  71.7 6.9 %collective-permute-start.16 = (bf16[96,1024]{1,0:T(8,128)(2,1)S(1)}, bf16[96,1024]{1,0:T(8,128)(2,1)S(1)}, u32[]{:S(2)}, u32[]{:S(2)}) collective-permute-start(bf16[96,1024]{1,0:T(8,128)(2,1)S(1)} %shard_map.98.refs_0_), channel_id=1, source_target_pairs={{0,4},{4,0},{8,12},{12,8},{1,5},{5,1},{9,13},{13,9},{2,6},{6,2},{1... | collective-permute-start | bytes 589832 | tf_op jit(solution)/shard_map/ppermute | solution.py:45
  78.7 60.3 %slice-start.3 = ((s8[7340032]{0:T(1024)(128)(4,1)}), s8[3145728]{0:T(1024)(128)(4,1)S(1)}, s32[]{:S(2)}) async-start(s8[7340032]{0:T(1024)(128)(4,1)} %bitcast.2), calls=%async_computation.3 | async-start | bytes 6291456
  78.7 2.2 %collective-permute-start.17 = (bf16[96,2048]{1,0:T(8,128)(2,1)S(1)}, bf16[96,2048]{1,0:T(8,128)(2,1)S(1)}, u32[]{:S(2)}, u32[]{:S(2)}) collective-permute-start(bf16[96,2048]{1,0:T(8,128)(2,1)S(1)} %shard_map.99.refs_0_.refs_2_.refs_4_.refs_7_), channel_id=1, source_target_pairs={{0,1},{1,0},{2,3},{3,2},{4,5},{5,4},{6,7},{7,6},{8,9},{9,8},{10,11... | collective-permute-start | bytes 1179656 | tf_op jit(solution)/shard_map/ppermute | solution.py:40
  78.7 54.0 %collective-permute-start.7 = (bf16[192,1792]{1,0:T(8,128)(2,1)S(1)}, bf16[192,1792]{1,0:T(8,128)(2,1)S(1)}, u32[]{:S(2)}, u32[]{:S(2)}) collective-permute-start(bf16[192,1792]{1,0:T(8,128)(2,1)S(1)} %shard_map.89.refs_2_.refs_1_), channel_id=1, source_target_pairs={{0,2},{2,0},{1,3},{3,1},{4,6},{6,4},{5,7},{7,5},{8,10},{10,8},{9,1... | collective-permute-start | bytes 2064392 | tf_op jit(solution)/shard_map/ppermute | solution.py:40
  79.4 53.4 %collective-permute-start.6 = (bf16[96,1792]{1,0:T(8,128)(2,1)S(1)}, bf16[96,1792]{1,0:T(8,128)(2,1)S(1)}, u32[]{:S(2)}, u32[]{:S(2)}) collective-permute-start(bf16[96,1792]{1,0:T(8,128)(2,1)S(1)} %shard_map.86.refs_6_.refs_0_), channel_id=1, source_target_pairs={{0,2},{2,0},{1,3},{3,1},{4,6},{6,4},{5,7},{7,5},{8,10},{10,8},{9,1... | collective-permute-start | bytes 1032200 | tf_op jit(solution)/shard_map/ppermute | solution.py:40
  84.9 59.8 %collective-permute-start.22 = (bf16[288,896]{1,0:T(8,128)(2,1)S(1)}, bf16[288,896]{1,0:T(8,128)(2,1)S(1)}, u32[]{:S(2)}, u32[]{:S(2)}) collective-permute-start(bf16[288,896]{1,0:T(8,128)(2,1)S(1)} %shard_map.100.refs_9_.refs_0_), channel_id=1, source_target_pairs={{0,2},{2,0},{1,3},{3,1},{4,6},{6,4},{5,7},{7,5},{8,10},{10,8},{9,1... | collective-permute-start | bytes 1548296 | tf_op jit(solution)/shard_map/ppermute | solution.py:40
  138.9 35.1 %collective-permute-start.11 = (bf16[48,2048]{1,0:T(8,128)(2,1)S(1)}, bf16[48,2048]{1,0:T(8,128)(2,1)S(1)}, u32[]{:S(2)}, u32[]{:S(2)}) collective-permute-start(bf16[48,2048]{1,0:T(8,128)(2,1)S(1)} %get-tuple-element.40), channel_id=1, source_target_pairs={{0,1},{1,0},{2,3},{3,2},{4,5},{5,4},{6,7},{7,6},{8,9},{9,8},{10,11... | collective-permute-start | bytes 589832 | tf_op jit(solution)/shard_map/ppermute | solution.py:40
  143.1 23.8 %collective-permute-start.21 = (bf16[288,896]{1,0:T(8,128)(2,1)S(1)}, bf16[288,896]{1,0:T(8,128)(2,1)S(1)}, u32[]{:S(2)}, u32[]{:S(2)}) collective-permute-start(bf16[288,896]{1,0:T(8,128)(2,1)S(1)} %shard_map.101.refs_4_.refs_0_), channel_id=1, source_target_pairs={{0,2},{2,0},{1,3},{3,1},{4,6},{6,4},{5,7},{7,5},{8,10},{10,8},{9,1... | collective-permute-start | bytes 1548296 | tf_op jit(solution)/shard_map/ppermute | solution.py:40
  155.3 19.1 %collective-permute-start.18 = (bf16[96,2048]{1,0:T(8,128)(2,1)S(1)}, bf16[96,2048]{1,0:T(8,128)(2,1)S(1)}, u32[]{:S(2)}, u32[]{:S(2)}) collective-permute-start(bf16[96,2048]{1,0:T(8,128)(2,1)S(1)} %get-tuple-element.46), channel_id=1, source_target_pairs={{0,1},{1,0},{2,3},{3,2},{4,5},{5,4},{6,7},{7,6},{8,9},{9,8},{10,11... | collective-permute-start | bytes 1179656 | tf_op jit(solution)/shard_map/ppermute | solution.py:40
  161.6 5.3 %copy-start.4 = (bf16[2048,1792]{1,0:T(8,128)(2,1)S(1)}, bf16[2048,1792]{1,0:T(8,128)(2,1)}, u32[]{:S(2)}) copy-start(bf16[2048,1792]{1,0:T(8,128)(2,1)} %get-tuple-element.61.refs_6_.refs_12_) | copy-start | bytes 22020100
  166.9 3.1 %copy-start.3 = (bf16[1792,2048]{1,0:T(8,128)(2,1)S(1)}, bf16[1792,2048]{1,0:T(8,128)(2,1)}, u32[]{:S(2)}) copy-start(bf16[1792,2048]{1,0:T(8,128)(2,1)} %shard_map.106.refs_5_.refs_9_) | copy-start | bytes 22020100
  173.6 6.5 %collective-permute-start.23 = (bf16[48,2048]{1,0:T(8,128)(2,1)S(1)}, bf16[48,2048]{1,0:T(8,128)(2,1)S(1)}, u32[]{:S(2)}, u32[]{:S(2)}) collective-permute-start(bf16[48,2048]{1,0:T(8,128)(2,1)S(1)} %get-tuple-element.63), channel_id=1, source_target_pairs={{0,1},{1,0},{2,3},{3,2},{4,5},{5,4},{6,7},{7,6},{8,9},{9,8},{10,11... | collective-permute-start | bytes 589832 | tf_op jit(solution)/shard_map/ppermute | solution.py:40
  174.1 5.7 %collective-permute-start.12 = (bf16[48,1024]{1,0:T(8,128)(2,1)S(1)}, bf16[48,1024]{1,0:T(8,128)(2,1)S(1)}, u32[]{:S(2)}, u32[]{:S(2)}) collective-permute-start(bf16[48,1024]{1,0:T(8,128)(2,1)S(1)} %get-tuple-element.42), channel_id=1, source_target_pairs={{0,4},{4,0},{8,12},{12,8},{1,5},{5,1},{9,13},{13,9},{2,6},{6,2},{1... | collective-permute-start | bytes 294920 | tf_op jit(solution)/shard_map/ppermute | solution.py:45
  174.5 13.9 %collective-permute-start.19 = (bf16[96,1024]{1,0:T(8,128)(2,1)S(1)}, bf16[96,1024]{1,0:T(8,128)(2,1)S(1)}, u32[]{:S(2)}, u32[]{:S(2)}) collective-permute-start(bf16[96,1024]{1,0:T(8,128)(2,1)S(1)} %get-tuple-element.48), channel_id=1, source_target_pairs={{0,4},{4,0},{8,12},{12,8},{1,5},{5,1},{9,13},{13,9},{2,6},{6,2},{1... | collective-permute-start | bytes 589832 | tf_op jit(solution)/shard_map/ppermute | solution.py:45
  179.8 15.7 %collective-permute-start.13 = (bf16[48,512]{1,0:T(8,128)(2,1)S(1)}, bf16[48,512]{1,0:T(8,128)(2,1)S(1)}, u32[]{:S(2)}, u32[]{:S(2)}) collective-permute-start(bf16[48,512]{1,0:T(8,128)(2,1)S(1)} %get-tuple-element.44), channel_id=1, source_target_pairs={{0,8},{4,12},{8,0},{12,4},{1,9},{5,13},{9,1},{13,5},{2,10},{6,14},... | collective-permute-start | bytes 147464 | tf_op jit(solution)/shard_map/ppermute | solution.py:45
  180.2 6.2 %collective-permute-start.24 = (bf16[48,1024]{1,0:T(8,128)(2,1)S(1)}, bf16[48,1024]{1,0:T(8,128)(2,1)S(1)}, u32[]{:S(2)}, u32[]{:S(2)}) collective-permute-start(bf16[48,1024]{1,0:T(8,128)(2,1)S(1)} %get-tuple-element.65), channel_id=1, source_target_pairs={{0,4},{4,0},{8,12},{12,8},{1,5},{5,1},{9,13},{13,9},{2,6},{6,2},{1... | collective-permute-start | bytes 294920 | tf_op jit(solution)/shard_map/ppermute | solution.py:45
  186.4 9.1 %collective-permute-start.25 = (bf16[48,512]{1,0:T(8,128)(2,1)S(1)}, bf16[48,512]{1,0:T(8,128)(2,1)S(1)}, u32[]{:S(2)}, u32[]{:S(2)}) collective-permute-start(bf16[48,512]{1,0:T(8,128)(2,1)S(1)} %get-tuple-element.67), channel_id=1, source_target_pairs={{0,8},{4,12},{8,0},{12,4},{1,9},{5,13},{9,1},{13,5},{2,10},{6,14},... | collective-permute-start | bytes 147464 | tf_op jit(solution)/shard_map/ppermute | solution.py:45
  188.4 7.1 %collective-permute-start.20 = (bf16[96,512]{1,0:T(8,128)(2,1)S(1)}, bf16[96,512]{1,0:T(8,128)(2,1)S(1)}, u32[]{:S(2)}, u32[]{:S(2)}) collective-permute-start(bf16[96,512]{1,0:T(8,128)(2,1)S(1)} %get-tuple-element.50), channel_id=1, source_target_pairs={{0,8},{4,12},{8,0},{12,4},{1,9},{5,13},{9,1},{13,5},{2,10},{6,14},... | collective-permute-start | bytes 294920 | tf_op jit(solution)/shard_map/ppermute | solution.py:45

commit v6 on v5

--- a/solution.py
+++ b/solution.py
@@ -7,7 +7,7 @@
 from jax.experimental.pallas import tpu as pltpu
 from jax.sharding import PartitionSpec as P
 
-PIECES = (1, 2, 1)
+PIECES = (1, 1, 1)
 MIB = 1 << 20
 
 
@@ -88,20 +88,26 @@
 ANYWHERE = pl.BlockSpec(memory_space=pl.ANY)
 
 
-def local(kernel, outs, args, after=(), flops=0, moved=0, limit=8, scratch=(), out_specs=None):
+def declared(cost):
+    return pl.CostEstimate(flops=int(cost * 1.15e9), bytes_accessed=0, transcendentals=0)
+
+
+def local(kernel, outs, args, after=(), limit=12, scratch=(), out_specs=None, resident=(), cost=0.1):
+    waits = len(resident) + len(after)
+
     def body(*refs):
-        kernel(refs[: len(args)], refs[len(args) + len(after) :])
+        kernel(refs[: len(args)], refs[len(args) + waits :])
 
     shapes = [jax.ShapeDtypeStruct(shape, dtype) for shape, dtype in outs]
     return pl.pallas_call(
         body,
         out_shape=shapes,
-        in_specs=[VMEM] * len(args) + [ANYWHERE] * len(after),
+        in_specs=[VMEM] * (len(args) + len(resident)) + [ANYWHERE] * len(after),
         out_specs=out_specs if out_specs else [VMEM] * len(outs),
         scratch_shapes=list(scratch),
         compiler_params=pltpu.CompilerParams(vmem_limit_bytes=limit * MIB),
-        cost_estimate=pl.CostEstimate(flops=flops, bytes_accessed=moved, transcendentals=0),
-    )(*args, *after)
+        cost_estimate=declared(cost),
+    )(*args, *resident, *after)
 
 
 def lanes(index, width):
@@ -118,17 +124,17 @@
     return local(kernel, [((2 * rows, width), acts.dtype)], (acts, grad_out), after, limit=1)[0]
 
 
-def pack(value, far, after=()):
+def pack(value, far, after=(), resident=(), cost=0.1):
     rows, width = value.shape
 
     def kernel(ins, outs):
         outs[0][:, :width] = ins[0][...]
         outs[0][:, width:] = ins[1][...]
 
-    return local(kernel, [((rows, 2 * width), value.dtype)], (value, far), after, limit=1)[0]
-
-
-def arrange(pair, near, after=()):
+    return local(kernel, [((rows, 2 * width), value.dtype)], (value, far), after, 1, resident=resident, cost=cost)[0]
+
+
+def arrange(pair, near, resident=(), cost=0.1):
     rows, width = pair.shape[0], pair.shape[1] // 2
 
     def kernel(ins, outs):
@@ -136,26 +142,15 @@
         for step, (source, at) in enumerate(((0, 0), (1, 0), (0, 1), (1, 1))):
             outs[0][:, lanes(me ^ step, width)] = ins[source][:, at * width : (at + 1) * width]
 
-    return local(kernel, [((rows, 4 * width), pair.dtype)], (pair, near), after, limit=1)[0]
-
-
-def blocks_of(width):
-    full = width // 256
-    return full, width - full * 256
-
-
-def over_blocks(width, body):
-    full, rest = blocks_of(width)
-
-    @pl.loop(0, full)
-    def _(j):
-        body(lambda base: pl.ds(pl.multiple_of(base + j * 256, 128), 256))
-
-    if rest:
-        body(lambda base: pl.ds(base + full * 256, rest))
-
-
-def forward(sources, weights, span, rows, after=()):
+    return local(kernel, [((rows, 4 * width), pair.dtype)], (pair, near), (), 1, resident=resident, cost=cost)[0]
+
+
+def over_blocks(width, step, body):
+    for base in range(0, width, step):
+        body(base, min(step, width - base))
+
+
+def forward(sources, weights, span, rows, after=(), cost=0.3):
     lower, upper = span
     width, features, tokens = upper - lower, sources[0][0].shape[1], 2 * rows
     arrays = [array for own, theirs, _, _ in sources for array in (own, theirs)]
@@ -171,26 +166,27 @@
             weight = ins[len(arrays) + k]
             top = k * tokens
 
-            def product(at, weight=weight, top=top, down=down):
+            def product(base, size, weight=weight, top=top, down=down):
+                at = slice(lower + base, lower + base + size)
                 if down:
-                    value = over_cols(held[...], weight[at(lower), :])
+                    value = over_cols(held[...], weight[at, :])
                 else:
-                    value = rows_by_cols(held[...], weight[:, at(lower)])
-                out[top : top + tokens, at(0)] = value.astype(out.dtype)
-
-            over_blocks(width, product)
+                    value = rows_by_cols(held[...], weight[:, at])
+                out[top : top + tokens, base : base + size] = value.astype(out.dtype)
+
+            over_blocks(width, 896, product)
 
     return local(
         kernel,
         [((len(sources) * tokens, width), jnp.bfloat16)],
         (*arrays, *weights),
         after,
-        flops=2 * len(sources) * tokens * features * width,
         scratch=[pltpu.VMEM((tokens, features), jnp.bfloat16)],
+        cost=cost,
     )[0]
 
 
-def backward(own, other, where, weights, span, rows, before, final, after=()):
+def backward(own, other, where, weights, span, rows, before, final, after=(), cost=1.0):
     lower, upper = span
     width, features, tokens = upper - lower, weights[0].shape[0], 2 * rows
     count = len(own)
@@ -213,9 +209,8 @@
             for ref, value in zip(outs[:3], swiglu_grads(total(0), total(1), total(2))):
                 ref[:, at] = value
 
-        @pl.loop(0, features // 256)
-        def _(j):
-            at = lanes(j, 256)
+        def product(base, size):
+            at = slice(base, base + size)
             value = over_cols(outs[1][...], ins[2 * count][at, lower:upper])
             value = value + over_cols(outs[2][...], ins[2 * count + 1][at, lower:upper])
             if before is not None:
@@ -226,7 +221,9 @@
             else:
                 outs[3][:, at] = value
 
-    return local(kernel, outs_all, ins_all, after, flops=4 * tokens * features * width)
+        over_blocks(features, 1024, product)
+
+    return local(kernel, outs_all, ins_all, after, cost=cost)
 
 
 def fold_near(value, theirs):
@@ -257,30 +254,20 @@
     return local(kernel, outs, (value, theirs), limit=4)
 
 
-def fold_last(pairs):
-    heights = [mine.shape[0] for mine, _ in pairs]
-    width = pairs[0][0].shape[1]
+def fold_last(mine, theirs, earlier=()):
+    heights = [piece.shape[0] for piece in earlier]
+    rows, width = mine.shape
+    shape = (sum(heights) + rows, width)
 
     def kernel(ins, outs):
         top = 0
         for c, height in enumerate(heights):
-            value = ins[2 * c][...] + ins[2 * c + 1][...].astype(jnp.float32)
-            outs[0][top : top + height] = value.astype(jnp.bfloat16)
+            outs[0][top : top + height] = ins[2 + c][...]
             top += height
-
-    return local(
-        kernel,
-        [((sum(heights), width), jnp.bfloat16)],
-        [array for pair in pairs for array in pair],
-        limit=4,
-        out_specs=[pl.BlockSpec((sum(heights), width), lambda: (0, 0))],
-    )[0]
-
-
-def scatter(mine, sent):
-    keep, give = fold_near(mine, shifted(sent, "tok", 1))
-    mine, give_far = fold_far(keep, swapped(give, "hid", 1))
-    return keep, (mine, swapped(give_far, "hid", 2))
+        outs[0][top:] = (ins[0][...] + ins[1][...].astype(jnp.float32)).astype(jnp.bfloat16)
+
+    specs = [pl.BlockSpec(shape, lambda: (0, 0))] if earlier else None
+    return local(kernel, [(shape, jnp.bfloat16)], (mine, theirs, *earlier), limit=4, out_specs=specs)[0]
 
 
 def stack(target, pieces, refs, at=None):
@@ -291,10 +278,11 @@
         top += rows
 
 
-def gradients(kernel, outs, arrays, old, grid, specs, scratch, after, flops, moved):
+def gradients(kernel, outs, arrays, old, grid, specs, scratch, after, cost):
     def body(*refs):
         kernel(refs[: len(arrays)], refs[len(arrays) + len(old) + len(after) :])
 
+    outs, specs = [*outs, (16, 128)], [*specs, VMEM]
     return pl.pallas_call(
         body,
         grid=grid,
@@ -304,7 +292,7 @@
         scratch_shapes=scratch,
         input_output_aliases={len(arrays) + i: i for i in range(len(old))},
         compiler_params=pltpu.CompilerParams(vmem_limit_bytes=14 * MIB),
-        cost_estimate=pl.CostEstimate(flops=flops, bytes_accessed=moved, transcendentals=0),
+        cost_estimate=declared(cost),
     )(*arrays, *old, *after)
 
 
@@ -315,11 +303,12 @@
     block = 512
 
     def kernel(ins, refs):
-        gate_out, up_out, g_all, u_all = refs
+        gate_out, up_out, token, g_all, u_all = refs
         step = pl.program_id(0)
 
         @pl.when(step == 0)
         def _():
+            token[...] = jnp.zeros_like(token)
             stack(g_all, [(n_x + i, *p[1:]) for i, p in enumerate(gs)], ins)
             stack(u_all, [(n_x + n_g + i, *p[1:]) for i, p in enumerate(us)], ins)
 
@@ -331,8 +320,7 @@
     spec = pl.BlockSpec((block, width), lambda i: (i, part))
     scratch = [pltpu.VMEM((tokens, width), jnp.bfloat16)] * 2
     return gradients(
-        kernel, [(features, total)] * 2, arrays, old, (features // block,), [spec, spec], scratch, after,
-        4 * tokens * features * width, 4 * features * width,
+        kernel, [(features, total)] * 2, arrays, old, (features // block,), [spec, spec], scratch, after, 5.0
     )
 
 
@@ -343,11 +331,12 @@
     block = 256
 
     def kernel(ins, refs):
-        out, h_all = refs
+        out, token, h_all = refs
         step = pl.program_id(0)
 
         @pl.when(step == 0)
         def _():
+            token[...] = jnp.zeros_like(token)
             pieces = [ins[i][p[1] : p[1] + p[2], p[3] : p[3] + width] for i, p in enumerate(hs)]
             h_all[...] = jnp.concatenate(pieces, axis=0).T
 
@@ -358,8 +347,7 @@
     spec = pl.BlockSpec((width, block), lambda i: (part, i))
     scratch = [pltpu.VMEM((width, tokens), jnp.bfloat16)]
     return gradients(
-        kernel, [(total, features)], arrays, old, (features // block,), [spec], scratch, after,
-        2 * tokens * features * width, 2 * features * width,
+        kernel, [(total, features)], arrays, old, (features // block,), [spec], scratch, after, 3.0
     )
 
 
@@ -378,72 +366,90 @@
     lower, upper = spans[0]
     rows = heights[0]
     mixed, theirs = [], []
-    for value in (acts[lower:upper], grad_out[lower:upper]):
-        pair = pack(value, swapped(value, "hid", 2))
-        mixed.append(arrange(pair, swapped(pair, "hid", 1)))
+    for value in (acts, grad_out):
+        value = value[lower:upper]
+        pair = pack(value, swapped(value, "hid", 2), cost=3.0)
+        mixed.append(arrange(pair, swapped(pair, "hid", 1), cost=3.0))
         theirs.append(shifted(mixed[-1], "tok", 1))
     x, dy = [(mixed[i], theirs[i], 0) for i in range(2)]
-    gate = forward([(*x, False)], (w_gate,), whole, rows)
-    rest = forward([(*x, False), (*dy, True)], (w_up, w_down), whole, rows, (gate,))
-    tokens = 2 * rows
+    gate_up = forward([(*x, False), (*x, False)], (w_gate, w_up), whole, rows)
+    dhid = forward([(*dy, True)], (w_down,), whole, rows, (gate_up,))
     inputs = [(x, dy)]
-    sums = [[((gate, rest), ((0, 0), (1, 0), (1, tokens)))]]
-    anchor, cut_after = rest, mixed[1]
-
-    grads, scattered = [None] * len(spans), [None] * len(spans)
-
-    def backward_piece(index, after):
-        (own, where), = sums[index]
-        other = [shifted(part, "wid", 1) for part in own]
-        hidden, d_gate, d_up, mine, sent = backward(
-            own, other, where, back_weights, whole, heights[index], None, True, after
-        )
-        grads[index] = (hidden, d_gate, d_up)
-        return scatter(mine, sent)[1]
-
-    for index in range(1, len(spans)):
+    sums = [[((gate_up, dhid), ((0, 0), (0, 2 * rows), (1, 0)))]]
+
+    def gather_piece(index, cut_after, pack_after):
         rows = heights[index]
-        tokens = 2 * rows
-        both = cut_piece(acts, grad_out, *spans[index], (cut_after,))
-        pair = pack(both, swapped(both, "hid", 2), (anchor,))
-        cut_after = pair
+        both = cut_piece(acts, grad_out, *spans[index], cut_after)
+        pair = pack(both, swapped(both, "hid", 2), pack_after)
         own = arrange(pair, swapped(pair, "hid", 1))
         other = shifted(own, "tok", 1)
-        x, dy = (own, other, 0), (own, other, rows)
-        inputs.append((x, dy))
-        sources = [(*x, False), (*x, False), (*dy, True)]
-        where = ((0, 0), (0, tokens), (0, 2 * tokens))
-        done, after = [], ()
+        inputs.append(((own, other, 0), (own, other, rows)))
+        return pair
+
+    def forward_piece(index, after):
+        x, dy = inputs[index]
+        rows = heights[index]
+        where = ((0, 0), (0, 2 * rows), (0, 4 * rows))
+        done = []
         for span in halves if index == last else (whole,):
-            part = forward(sources, (w_gate, w_up, w_down), span, rows, after)
+            part = forward([(*x, False), (*x, False), (*dy, True)], (w_gate, w_up, w_down), span, rows, after)
             done.append(((part,), where))
             after = (part,)
         sums.append(done)
-        anchor = after[0]
-        scattered[index - 1] = backward_piece(index - 1, (anchor,))
-
-    rows = heights[last]
+        return after
+
+    def backward_piece(index, part, before, final, after):
+        own, where = sums[index][part]
+        span = halves[part] if index == last else whole
+        other = [shifted(value, "wid", 1) for value in own]
+        cost = 1.0 if index == last else 60.0
+        return backward(own, other, where, back_weights, span, heights[index], before, final, after, cost)
+
+    def near_step(results):
+        return fold_near(results[3], shifted(results[4], "tok", 1))
+
+    def far_step(near):
+        return fold_far(near[0], swapped(near[1], "hid", 1))
+
+    def end_step(far, earlier=()):
+        return fold_last(far[0], swapped(far[1], "hid", 2), earlier)
+
+    pair = gather_piece(1, (mixed[1],), (dhid,))
+    done = forward_piece(1, ())
+    grads = [backward_piece(0, 0, None, True, done)]
+    gather_piece(2, (pair,), (grads[0][0],))
+    near = near_step(grads[0])
+    done = forward_piece(2, (near[0],))
+    far = far_step(near)
+    grads.append(backward_piece(1, 0, None, True, (*done, far[0])))
+    finished = [end_step(far)]
+
     xs, ys = [], []
     for index, (x, dy) in enumerate(inputs):
         for pieces, (own, other, first) in ((xs, x), (ys, dy)):
             pieces.append((own, first, heights[index], 0))
             pieces.append((other, first, heights[index], 0))
-    before, after, columns, downs = None, (), (), ()
-    for part, (own, where) in enumerate(sums[last]):
-        other = [shifted(value, "wid", 1) for value in own]
-        results = backward(own, other, where, back_weights, halves[part], rows, before, part == 1, after)
-        before = results[3]
-        hs, gs, us = [
-            [(grads[c][k], 0, 2 * heights[c], halves[part][0]) for c in range(last)] + [(results[k], 0, 2 * rows, 0)]
-            for k in range(3)
-        ]
-        downs = row_grads(hs, ys, part, 2, total, downs)
-        if part == 1:
-            keep, scattered[last] = scatter(*results[3:])
-            after = (keep,)
-        columns = column_grads(xs, gs, us, part, 2, total, columns, after if part == 1 else ())
-        after = (downs[0], columns[0])
-    return fold_last(scattered), columns[0], columns[1], downs[0]
+
+    def with_last(results, k, part):
+        pieces = [(grads[c][k], 0, 2 * heights[c], halves[part][0]) for c in range(last)]
+        return pieces + [(results[k], 0, 2 * heights[last], 0)]
+
+    first = backward_piece(last, 0, None, False, (grads[1][0], finished[0]))
+    near = near_step(grads[1])
+    down, down_token = row_grads(with_last(first, 0, 0), ys, 0, 2, total, (), (near[0],))
+    far = far_step(near)
+    gate, up, token = column_grads(
+        xs, with_last(first, 1, 0), with_last(first, 2, 0), 0, 2, total, (), (far[0], down_token)
+    )
+    finished.append(end_step(far))
+    second = backward_piece(last, 1, first[3], True, (token, finished[1]))
+    near = near_step(second)
+    down, down_token = row_grads(with_last(second, 0, 1), ys, 1, 2, total, (down,), ())
+    far = far_step(near)
+    gate, up, _ = column_grads(
+        xs, with_last(second, 1, 1), with_last(second, 2, 1), 1, 2, total, (gate, up), (near[0], down_token)
+    )
+    return end_step(far, finished), gate, up, down
 
 
 def shards(acts, grad_out, w_gate, w_up, w_down):

time: 197 us -> 137 us (0.70)
  waiting for transfers between devices: 88.4 us -> 44.7 us
  Pallas kernels: 69.3 us -> 54.9 us
  local copies, waits for them, and re-layouts: 13.1 us -> 1.79 us
  starting transfers between devices: 24.6 us -> 34.7 us
    ppermute x12, waiting for transfers between devices: 49.5 us -> 18.6 us  [shifted(): return lax.ppermute(value, axis, [(i, (i + step) % n) for i in range(n)])]
    pallas_call x26 -> x28, Pallas kernels: 46.7 us -> 32.2 us  [local(): pl.pallas_call(body, out_shape=shapes, in_specs=[VMEM] * (len(args) + len...]
    ppermute x14, waiting for transfers between devices: 38.9 us -> 26.1 us  [swapped(): return lax.ppermute(value, axis, [(i, i ^ bit) for i in range(n)])]
    unnamed x26 -> x40, local copies, waits for them, and re-layouts: 11.3 us -> 0.1 us
    ppermute x14, starting transfers between devices: 17.8 us -> 26.7 us  [swapped(): return lax.ppermute(value, axis, [(i, i ^ bit) for i in range(n)])]
  transfers between devices with their start and end apart: 26 -> 26, of which waited for: 11 -> 15; matrix products, arithmetic and copies ran while one was open for 0% -> 1% of each run, Pallas kernels for 30% -> 37%
where the time goes in v6:
time: 137 us
  Pallas kernels  54.9 us (40%)
  waiting for transfers between devices  44.7 us (33%)
  starting transfers between devices  34.7 us (25%)
  local copies, waits for them, and re-layouts  1.79 us (1%)
    pallas_call x28, Pallas kernels, local(): pl.pallas_call(body, out_shape=shapes, in_specs=[VMEM] * (len(args) + len...  32.2 us
    ppermute x14, starting transfers between devices, swapped(): return lax.ppermute(value, axis, [(i, i ^ bit) for i in range(n)])  26.7 us
    ppermute x14, waiting for transfers between devices, swapped(): return lax.ppermute(value, axis, [(i, i ^ bit) for i in range(n)])  26.1 us
    pallas_call x4, Pallas kernels, gradients(): pl.pallas_call(body, grid=grid, out_shape=[jax.ShapeDtypeStruct(shape, jn...  22.7 us
    ppermute x12, waiting for transfers between devices, shifted(): return lax.ppermute(value, axis, [(i, (i + step) % n) for i in range(n)])  18.6 us
    ppermute x12, starting transfers between devices, shifted(): return lax.ppermute(value, axis, [(i, (i + step) % n) for i in range(n)])  7.91 us
  transfers between devices with their start and end apart: 26, of which 15 were waited for; matrix products, arithmetic and copies ran while one was open for 1% of the time, Pallas kernels for 37%

profile of v6, /device:TPU:0, one launch (start us, length us, event | category | flops | bytes accessed | tf_op | source)
XLA Modules:
  0.0 137.1 jit_solution(410908995291037589)
XLA Ops:
  0.6 0.8 slice.7.refs_0_
  1.5 4.0 %collective-permute-start.4 = (bf16[64,512]{1,0:T(8,128)(2,1)S(1)}, bf16[64,512]{1,0:T(8,128)(2,1)S(1)}, u32[]{:S(2)}, u32[]{:S(2)}) collective-permute-start(bf16[64,512]{1,0:T(8,128)(2,1)S(1)} %slice.7.refs_0_), channel_id=1, source_target_pairs={{0,8},{4,12},{8,0},{12,4},{1,9},{5,13},{9,1},{13,5},{2,10},{6,14},... | collective-permute-start | bytes 196616 | tf_op jit(solution)/shard_map/ppermute | solution.py:45
  5.5 0.8 slice.6.refs_0_
  6.4 2.8 %collective-permute-done.4.refs_1_ = bf16[64,512]{1,0:T(8,128)(2,1)S(1)} collective-permute-done((bf16[64,512]{1,0:T(8,128)(2,1)S(1)}, bf16[64,512]{1,0:T(8,128)(2,1)S(1)}, u32[]{:S(2)}, u32[]{:S(2)}) %collective-permute-start.4) | collective-permute-done | bytes 65568 | tf_op jit(solution)/shard_map/ppermute | solution.py:45
  9.2 2.2 %collective-permute-start.5 = (bf16[64,1024]{1,0:T(8,128)(2,1)S(1)}, bf16[64,1024]{1,0:T(8,128)(2,1)S(1)}, u32[]{:S(2)}, u32[]{:S(2)}) collective-permute-start(bf16[64,1024]{1,0:T(8,128)(2,1)S(1)} %shard_map.87.refs_0_), channel_id=1, source_target_pairs={{0,4},{4,0},{8,12},{12,8},{1,5},{5,1},{9,13},{13,9},{2,6},{6,2},{1... | collective-permute-start | bytes 393224 | tf_op jit(solution)/shard_map/ppermute | solution.py:45
  11.4 0.5 collective-permute-done.refs_1_
  11.8 1.3 collective-permute-start.1
  13.2 2.5 %collective-permute-done.5.refs_1_ = bf16[64,1024]{1,0:T(8,128)(2,1)S(1)} collective-permute-done((bf16[64,1024]{1,0:T(8,128)(2,1)S(1)}, bf16[64,1024]{1,0:T(8,128)(2,1)S(1)}, u32[]{:S(2)}, u32[]{:S(2)}) %collective-permute-start.5) | collective-permute-done | bytes 131104 | tf_op jit(solution)/shard_map/ppermute | solution.py:45
  15.9 1.8 %collective-permute-done.1.refs_1_ = bf16[64,1024]{1,0:T(8,128)(2,1)S(1)} collective-permute-done((bf16[64,1024]{1,0:T(8,128)(2,1)S(1)}, bf16[64,1024]{1,0:T(8,128)(2,1)S(1)}, u32[]{:S(2)}, u32[]{:S(2)}) %collective-permute-start.1) | collective-permute-done | bytes 131104 | tf_op jit(solution)/shard_map/ppermute | solution.py:45
  17.8 3.4 %collective-permute-start.2 = (bf16[128,512]{1,0:T(8,128)(2,1)S(1)}, bf16[128,512]{1,0:T(8,128)(2,1)S(1)}, u32[]{:S(2)}, u32[]{:S(2)}) collective-permute-start(bf16[128,512]{1,0:T(8,128)(2,1)S(1)} %shard_map.86.refs_0_), channel_id=1, source_target_pairs={{0,8},{4,12},{8,0},{12,4},{1,9},{5,13},{9,1},{13,5},{2,10},{6,14},... | collective-permute-start | bytes 393224 | tf_op jit(solution)/shard_map/ppermute | solution.py:45
  21.3 2.4 %shard_map.89.refs_3_.refs_0_ = bf16[256,1792]{1,0:T(8,128)(2,1)S(1)} custom-call(bf16[64,2048]{1,0:T(8,128)(2,1)S(1)} %shard_map.88.refs_0_.refs_2_, bf16[64,2048]{1,0:T(8,128)(2,1)S(1)} %collective-permute-done.6.refs_1_.refs_3_, bf16[64,2048]{1,0:T(8,128)(2,1)S(1)} %shard_map.88.refs_0_.refs_2_, ...), custom_call_target="tpu_custom_call" | custom-call | flops 345000000 | tf_op jit(solution)/shard_map/pallas_call | solution.py:102
  23.7 1.6 %collective-permute-start.8 = (bf16[256,1792]{1,0:T(8,128)(2,1)S(1)}, bf16[256,1792]{1,0:T(8,128)(2,1)S(1)}, u32[]{:S(2)}, u32[]{:S(2)}) collective-permute-start(bf16[256,1792]{1,0:T(8,128)(2,1)S(1)} %shard_map.89.refs_3_.refs_0_), channel_id=1, source_target_pairs={{0,2},{2,0},{1,3},{3,1},{4,6},{6,4},{5,7},{7,5},{8,10},{10,8},{9,1... | collective-permute-start | bytes 2752520 | tf_op jit(solution)/shard_map/ppermute | solution.py:40
  25.4 2.4 %shard_map.90.refs_2_.refs_1_ = bf16[128,1792]{1,0:T(8,128)(2,1)S(1)} custom-call(bf16[64,2048]{1,0:T(8,128)(2,1)S(1)} %shard_map.85.refs_2_.refs_0_.refs_3_, bf16[64,2048]{1,0:T(8,128)(2,1)S(1)} %collective-permute-done.3.refs_1_.refs_4_, bf16[1792,2048]{1,0:T(8,128)(2,1)S(1)} %bitcast.5, bf16[256,1792]{1,0:T(8,128)(2,1)S(1)} %shard_map.89.refs_3_.refs_0_), custom_call_target="tpu_custom_call" | custom-call | flops 345000000 | tf_op jit(solution)/shard_map/pallas_call | solution.py:102
  27.8 0.4 collective-permute-done.2.refs_1_
  28.2 1.7 %collective-permute-start.10 = (bf16[128,1024]{1,0:T(8,128)(2,1)S(1)}, bf16[128,1024]{1,0:T(8,128)(2,1)S(1)}, u32[]{:S(2)}, u32[]{:S(2)}) collective-permute-start(bf16[128,1024]{1,0:T(8,128)(2,1)S(1)} %shard_map.91.refs_2_.refs_0_), channel_id=1, source_target_pairs={{0,4},{4,0},{8,12},{12,8},{1,5},{5,1},{9,13},{13,9},{2,6},{6,2},{1... | collective-permute-start | bytes 786440 | tf_op jit(solution)/shard_map/ppermute | solution.py:45
  29.9 6.5 %collective-permute-done.10.refs_1_ = bf16[128,1024]{1,0:T(8,128)(2,1)S(1)} collective-permute-done((bf16[128,1024]{1,0:T(8,128)(2,1)S(1)}, bf16[128,1024]{1,0:T(8,128)(2,1)S(1)}, u32[]{:S(2)}, u32[]{:S(2)}) %collective-permute-start.10) | collective-permute-done | bytes 262176 | tf_op jit(solution)/shard_map/ppermute | solution.py:45
  36.6 1.5 %collective-permute-start.9 = (bf16[128,1792]{1,0:T(8,128)(2,1)S(1)}, bf16[128,1792]{1,0:T(8,128)(2,1)S(1)}, u32[]{:S(2)}, u32[]{:S(2)}) collective-permute-start(bf16[128,1792]{1,0:T(8,128)(2,1)S(1)} %shard_map.90.refs_2_.refs_1_), channel_id=1, source_target_pairs={{0,2},{2,0},{1,3},{3,1},{4,6},{6,4},{5,7},{7,5},{8,10},{10,8},{9,1... | collective-permute-start | bytes 1376264 | tf_op jit(solution)/shard_map/ppermute | solution.py:40
  38.1 2.6 %collective-permute-start.7 = (bf16[128,512]{1,0:T(8,128)(2,1)S(1)}, bf16[128,512]{1,0:T(8,128)(2,1)S(1)}, u32[]{:S(2)}, u32[]{:S(2)}) collective-permute-start(bf16[128,512]{1,0:T(8,128)(2,1)S(1)} %shard_map.92.refs_0_), channel_id=1, source_target_pairs={{0,8},{4,12},{8,0},{12,4},{1,9},{5,13},{9,1},{13,5},{2,10},{6,14},... | collective-permute-start | bytes 393224 | tf_op jit(solution)/shard_map/ppermute | solution.py:45
  40.7 4.6 %shard_map.94.refs_6_.refs_0_ = bf16[384,1792]{1,0:T(8,128)(2,1)S(1)} custom-call(bf16[128,2048]{1,0:T(8,128)(2,1)S(1)} %shard_map.93.refs_0_.refs_2_.refs_4_.refs_5_, bf16[128,2048]{1,0:T(8,128)(2,1)S(1)} %collective-permute-done.11.refs_1_.refs_3_.refs_5_.refs_6_, bf16[128,2048]{1,0:T(8,128)(2,1)S(1)} %shard_map.93.refs_0_.refs_2_.refs_4_.refs_5_, ...), custom_call_target="tpu_custom_call" | custom-call | flops 345000000 | tf_op jit(solution)/shard_map/pallas_call | solution.py:102
  45.3 0.7 collective-permute-start.17
  46.0 10.8 %collective-permute-done.9.refs_3_ = bf16[128,1792]{1,0:T(8,128)(2,1)S(1)} collective-permute-done((bf16[128,1792]{1,0:T(8,128)(2,1)S(1)}, bf16[128,1792]{1,0:T(8,128)(2,1)S(1)}, u32[]{:S(2)}, u32[]{:S(2)}) %collective-permute-start.9) | collective-permute-done | bytes 458784 | tf_op jit(solution)/shard_map/ppermute | solution.py:40
  56.8 5.5 %shard_map.95 = (bf16[128,1792]{1,0:T(8,128)(2,1)S(1)}, bf16[128,1792]{1,0:T(8,128)(2,1)S(1)}, bf16[128,1792]{1,0:T(8,128)(2,1)S(1)}, f32[64,2048]{1,0:T(8,128)S(1)}, bf16[64,2048]{1,0:T(8,128)(2,1)S(1)}) custom-call(bf16[256,1792]{1,0:T(8,128)(2,1)S(1)} %shard_map.89.refs_3_.refs_0_, bf16[128,1792]{1,0:T(8,128)(2,1)S(1)} %shard_map.90.refs_2_.refs_1_, ...), custom_call_target="tpu_custom_call" | custom-call | flops 69000003584 | tf_op jit(solution)/shard_map/pallas_call | solution.py:102
  62.4 2.1 %collective-permute-start.12 = (bf16[128,1024]{1,0:T(8,128)(2,1)S(1)}, bf16[128,1024]{1,0:T(8,128)(2,1)S(1)}, u32[]{:S(2)}, u32[]{:S(2)}) collective-permute-start(bf16[128,1024]{1,0:T(8,128)(2,1)S(1)} %shard_map.96.refs_0_), channel_id=1, source_target_pairs={{0,4},{4,0},{8,12},{12,8},{1,5},{5,1},{9,13},{13,9},{2,6},{6,2},{1... | collective-permute-start | bytes 786440 | tf_op jit(solution)/shard_map/ppermute | solution.py:45
  64.5 4.8 %collective-permute-done.12.refs_1_ = bf16[128,1024]{1,0:T(8,128)(2,1)S(1)} collective-permute-done((bf16[128,1024]{1,0:T(8,128)(2,1)S(1)}, bf16[128,1024]{1,0:T(8,128)(2,1)S(1)}, u32[]{:S(2)}, u32[]{:S(2)}) %collective-permute-start.12) | collective-permute-done | bytes 262176 | tf_op jit(solution)/shard_map/ppermute | solution.py:45
  69.4 0.5 collective-permute-start.14
  69.9 1.8 %collective-permute-done.14.refs_1_ = bf16[64,2048]{1,0:T(8,128)(2,1)S(1)} collective-permute-done((bf16[64,2048]{1,0:T(8,128)(2,1)S(1)}, bf16[64,2048]{1,0:T(8,128)(2,1)S(1)}, u32[]{:S(2)}, u32[]{:S(2)}) %collective-permute-start.14) | collective-permute-done | bytes 262176 | tf_op jit(solution)/shard_map/ppermute | solution.py:40
  71.7 1.7 %collective-permute-start.18 = (bf16[64,1024]{1,0:T(8,128)(2,1)S(1)}, bf16[64,1024]{1,0:T(8,128)(2,1)S(1)}, u32[]{:S(2)}, u32[]{:S(2)}) collective-permute-start(bf16[64,1024]{1,0:T(8,128)(2,1)S(1)} %get-tuple-element.48), channel_id=1, source_target_pairs={{0,4},{4,0},{8,12},{12,8},{1,5},{5,1},{9,13},{13,9},{2,6},{6,2},{1... | collective-permute-start | bytes 393224 | tf_op jit(solution)/shard_map/ppermute | solution.py:45
  73.4 3.9 %collective-permute-done.18.refs_1_ = bf16[64,1024]{1,0:T(8,128)(2,1)S(1)} collective-permute-done((bf16[64,1024]{1,0:T(8,128)(2,1)S(1)}, bf16[64,1024]{1,0:T(8,128)(2,1)S(1)}, u32[]{:S(2)}, u32[]{:S(2)}) %collective-permute-start.18) | collective-permute-done | bytes 131104 | tf_op jit(solution)/shard_map/ppermute | solution.py:45
  77.4 2.4 %shard_map.99.refs_9_.refs_0_ = bf16[384,896]{1,0:T(8,128)(2,1)S(1)} custom-call(bf16[128,2048]{1,0:T(8,128)(2,1)S(1)} %shard_map.97.refs_0_.refs_2_.refs_4_.refs_7_, bf16[128,2048]{1,0:T(8,128)(2,1)S(1)} %collective-permute-done.13.refs_1_.refs_3_.refs_5_.refs_8_, bf16[128,2048]{1,0:T(8,128)(2,1)S(1)} %shard_map.97.refs_0_.refs_2_.refs_4_.refs_7_, ...), custom_call_target="tpu_custom_call" | custom-call | flops 345000000 | tf_op jit(solution)/shard_map/pallas_call | solution.py:102
  79.8 1.5 %collective-permute-start.16 = (bf16[384,896]{1,0:T(8,128)(2,1)S(1)}, bf16[384,896]{1,0:T(8,128)(2,1)S(1)}, u32[]{:S(2)}, u32[]{:S(2)}) collective-permute-start(bf16[384,896]{1,0:T(8,128)(2,1)S(1)} %shard_map.99.refs_9_.refs_0_), channel_id=1, source_target_pairs={{0,2},{2,0},{1,3},{3,1},{4,6},{6,4},{5,7},{7,5},{8,10},{10,8},{9,1... | collective-permute-start | bytes 2064392 | tf_op jit(solution)/shard_map/ppermute | solution.py:40
  81.3 2.4 %shard_map.100.refs_4_.refs_0_ = bf16[384,896]{1,0:T(8,128)(2,1)S(1)} custom-call(bf16[128,2048]{1,0:T(8,128)(2,1)S(1)} %shard_map.97.refs_0_.refs_2_.refs_4_.refs_7_, bf16[128,2048]{1,0:T(8,128)(2,1)S(1)} %collective-permute-done.13.refs_1_.refs_3_.refs_5_.refs_8_, bf16[128,2048]{1,0:T(8,128)(2,1)S(1)} %shard_map.97.refs_0_.refs_2_.refs_4_.refs_7_, ...), custom_call_target="tpu_custom_call" | custom-call | flops 345000000 | tf_op jit(solution)/shard_map/pallas_call | solution.py:102
  83.7 2.6 %collective-permute-done.17.refs_1_ = bf16[384,1792]{1,0:T(8,128)(2,1)S(1)} collective-permute-done((bf16[384,1792]{1,0:T(8,128)(2,1)S(1)}, bf16[384,1792]{1,0:T(8,128)(2,1)S(1)}, u32[]{:S(2)}, u32[]{:S(2)}) %collective-permute-start.17) | collective-permute-done | bytes 1376288 | tf_op jit(solution)/shard_map/ppermute | solution.py:40
  86.3 5.5 %shard_map.102 = (bf16[128,1792]{1,0:T(8,128)(2,1)S(1)}, bf16[128,1792]{1,0:T(8,128)(2,1)S(1)}, bf16[128,1792]{1,0:T(8,128)(2,1)S(1)}, f32[64,2048]{1,0:T(8,128)S(1)}, bf16[64,2048]{1,0:T(8,128)(2,1)S(1)}) custom-call(bf16[384,1792]{1,0:T(8,128)(2,1)S(1)} %shard_map.94.refs_6_.refs_0_, bf16[384,1792]{1,0:T(8,128)(2,1)S(1)} %collective-permute-done.17.refs_1_, ...), custom_call_target="tpu_custom_call" | custom-call | flops 69000003584 | tf_op jit(solution)/shard_map/pallas_call | solution.py:102
  91.9 2.6 %collective-permute-start.19 = (bf16[64,512]{1,0:T(8,128)(2,1)S(1)}, bf16[64,512]{1,0:T(8,128)(2,1)S(1)}, u32[]{:S(2)}, u32[]{:S(2)}) collective-permute-start(bf16[64,512]{1,0:T(8,128)(2,1)S(1)} %get-tuple-element.51), channel_id=1, source_target_pairs={{0,8},{4,12},{8,0},{12,4},{1,9},{5,13},{9,1},{13,5},{2,10},{6,14},... | collective-permute-start | bytes 196616 | tf_op jit(solution)/shard_map/ppermute | solution.py:45
  94.5 2.8 %collective-permute-done.19.refs_1_ = bf16[64,512]{1,0:T(8,128)(2,1)S(1)} collective-permute-done((bf16[64,512]{1,0:T(8,128)(2,1)S(1)}, bf16[64,512]{1,0:T(8,128)(2,1)S(1)}, u32[]{:S(2)}, u32[]{:S(2)}) %collective-permute-start.19) | collective-permute-done | bytes 65568 | tf_op jit(solution)/shard_map/ppermute | solution.py:45
  97.3 1.7 %collective-permute-start.15 = (bf16[384,896]{1,0:T(8,128)(2,1)S(1)}, bf16[384,896]{1,0:T(8,128)(2,1)S(1)}, u32[]{:S(2)}, u32[]{:S(2)}) collective-permute-start(bf16[384,896]{1,0:T(8,128)(2,1)S(1)} %shard_map.100.refs_4_.refs_0_), channel_id=1, source_target_pairs={{0,2},{2,0},{1,3},{3,1},{4,6},{6,4},{5,7},{7,5},{8,10},{10,8},{9,1... | collective-permute-start | bytes 2064392 | tf_op jit(solution)/shard_map/ppermute | solution.py:40
  99.0 1.9 %collective-permute-done.16.refs_1_ = bf16[384,896]{1,0:T(8,128)(2,1)S(1)} collective-permute-done((bf16[384,896]{1,0:T(8,128)(2,1)S(1)}, bf16[384,896]{1,0:T(8,128)(2,1)S(1)}, u32[]{:S(2)}, u32[]{:S(2)}) %collective-permute-start.16) | collective-permute-done | bytes 688160 | tf_op jit(solution)/shard_map/ppermute | solution.py:40
  100.9 2.9 %shard_map.104 = (bf16[128,896]{1,0:T(8,128)(2,1)S(1)}, bf16[128,896]{1,0:T(8,128)(2,1)S(1)}, bf16[128,896]{1,0:T(8,128)(2,1)S(1)}, f32[128,2048]{1,0:T(8,128)S(1)}) custom-call(bf16[384,896]{1,0:T(8,128)(2,1)S(1)} %shard_map.99.refs_9_.refs_0_, bf16[384,896]{1,0:T(8,128)(2,1)S(1)} %collective-permute-done.16.refs_1_, bf16[2048,1792]{1,0:T(8,128)(2,1)S(1)} %bitcast.1, ...), custom_call_target="tpu_custom_call" | custom-call | flops 1150000000 | tf_op jit(solution)/shard_map/pallas_call | solution.py:102
  103.9 1.3 collective-permute-start.21
  105.1 5.3 %shard_map.107 = (bf16[1792,2048]{1,0:T(8,128)(2,1)}, bf16[16,128]{1,0:T(8,128)(2,1)S(1)}) custom-call(bf16[128,1792]{1,0:T(8,128)(2,1)S(1)} %get-tuple-element.44.refs_2_.refs_0_, bf16[128,1792]{1,0:T(8,128)(2,1)S(1)} %get-tuple-element.50.refs_4_.refs_1_, bf16[128,896]{1,0:T(8,128)(2,1)S(1)} %get-tuple-element.64.refs_2_, bf16[64,2048]{1,0:T(8,128)(2,1)S(1)} %copy-done.11, ...), custom_call_target="tpu_custom_call" | custom-call | flops 3449999872 | tf_op jit(solution)/shard_map/pallas_call | solution.py:286
  110.5 1.8 %collective-permute-start.22 = (bf16[64,512]{1,0:T(8,128)(2,1)S(1)}, bf16[64,512]{1,0:T(8,128)(2,1)S(1)}, u32[]{:S(2)}, u32[]{:S(2)}) collective-permute-start(bf16[64,512]{1,0:T(8,128)(2,1)S(1)} %get-tuple-element.67), channel_id=1, source_target_pairs={{0,8},{4,12},{8,0},{12,4},{1,9},{5,13},{9,1},{13,5},{2,10},{6,14},... | collective-permute-start | bytes 196616 | tf_op jit(solution)/shard_map/ppermute | solution.py:45
  112.3 6.0 %shard_map.108 = (bf16[2048,1792]{1,0:T(8,128)(2,1)}, bf16[2048,1792]{1,0:T(8,128)(2,1)}, bf16[16,128]{1,0:T(8,128)(2,1)S(1)}) custom-call(bf16[64,2048]{1,0:T(8,128)(2,1)S(1)} %copy-done.7, bf16[64,2048]{1,0:T(8,128)(2,1)S(1)} %copy-done.9, bf16[128,2048]{1,0:T(8,128)(2,1)S(1)} %copy-done.1, bf16[128,2048]{1,0:T(8,128)(2,1)S(1)} %copy-done.3, ...), custom_call_target="tpu_custom_call" | custom-call | flops 5750000128 | tf_op jit(solution)/shard_map/pallas_call | solution.py:286
  118.4 2.9 %shard_map.110 = (bf16[128,896]{1,0:T(8,128)(2,1)S(1)}, bf16[128,896]{1,0:T(8,128)(2,1)S(1)}, bf16[128,896]{1,0:T(8,128)(2,1)S(1)}, f32[64,2048]{1,0:T(8,128)S(1)}, bf16[64,2048]{1,0:T(8,128)(2,1)S(1)}) custom-call(bf16[384,896]{1,0:T(8,128)(2,1)S(1)} %shard_map.100.refs_4_.refs_0_, bf16[384,896]{1,0:T(8,128)(2,1)S(1)} %collective-permute-done.15.refs_1_, ...), custom_call_target="tpu_custom_call" | custom-call | flops 1150000000 | tf_op jit(solution)/shard_map/pallas_call | solution.py:102
  121.3 1.5 %collective-permute-done.23.refs_1_ = bf16[64,2048]{1,0:T(8,128)(2,1)S(1)} collective-permute-done((bf16[64,2048]{1,0:T(8,128)(2,1)S(1)}, bf16[64,2048]{1,0:T(8,128)(2,1)S(1)}, u32[]{:S(2)}, u32[]{:S(2)}) %collective-permute-start.23) | collective-permute-done | bytes 262176 | tf_op jit(solution)/shard_map/ppermute | solution.py:40
  123.1 5.3 %shard_map.114 = (bf16[1792,2048]{1,0:T(8,128)(2,1)}, bf16[16,128]{1,0:T(8,128)(2,1)S(1)}) custom-call(bf16[128,1792]{1,0:T(8,128)(2,1)S(1)} %get-tuple-element.44.refs_2_.refs_0_, bf16[128,1792]{1,0:T(8,128)(2,1)S(1)} %get-tuple-element.50.refs_4_.refs_1_, bf16[128,896]{1,0:T(8,128)(2,1)S(1)} %get-tuple-element.78.refs_2_, ...), custom_call_target="tpu_custom_call", output_to_operand_aliasing={{0}: (9, {})} | custom-call | flops 3449999872 | tf_op jit(solution)/shard_map/pallas_call | solution.py:286
  128.6 1.9 %collective-permute-start.25 = (bf16[64,512]{1,0:T(8,128)(2,1)S(1)}, bf16[64,512]{1,0:T(8,128)(2,1)S(1)}, u32[]{:S(2)}, u32[]{:S(2)}) collective-permute-start(bf16[64,512]{1,0:T(8,128)(2,1)S(1)} %get-tuple-element.73), channel_id=1, source_target_pairs={{0,8},{4,12},{8,0},{12,4},{1,9},{5,13},{9,1},{13,5},{2,10},{6,14},... | collective-permute-start | bytes 196616 | tf_op jit(solution)/shard_map/ppermute | solution.py:45
  130.4 6.0 %shard_map.115 = (bf16[2048,1792]{1,0:T(8,128)(2,1)}, bf16[2048,1792]{1,0:T(8,128)(2,1)}, bf16[16,128]{1,0:T(8,128)(2,1)}) custom-call(bf16[64,2048]{1,0:T(8,128)(2,1)S(1)} %copy-done.7, bf16[64,2048]{1,0:T(8,128)(2,1)S(1)} %copy-done.9, bf16[128,2048]{1,0:T(8,128)(2,1)S(1)} %copy-done.1, ...), custom_call_target="tpu_custom_call", output_to_operand_aliasing={{0}: (12, {}), {1}: (13, {})} | custom-call | flops 5750000128 | tf_op jit(solution)/shard_map/pallas_call | solution.py:286
  136.4 0.7 shard_map.113
  (81 shorter events, 1.4 us)
Async XLA Ops:
  1.5 7.7 %collective-permute-start.4 = (bf16[64,512]{1,0:T(8,128)(2,1)S(1)}, bf16[64,512]{1,0:T(8,128)(2,1)S(1)}, u32[]{:S(2)}, u32[]{:S(2)}) collective-permute-start(bf16[64,512]{1,0:T(8,128)(2,1)S(1)} %slice.7.refs_0_), channel_id=1, source_target_pairs={{0,8},{4,12},{8,0},{12,4},{1,9},{5,13},{9,1},{13,5},{2,10},{6,14},... | collective-permute-start | bytes 196616 | tf_op jit(solution)/shard_map/ppermute | solution.py:45
  6.4 5.5 %collective-permute-start = (bf16[64,512]{1,0:T(8,128)(2,1)S(1)}, bf16[64,512]{1,0:T(8,128)(2,1)S(1)}, u32[]{:S(2)}, u32[]{:S(2)}) collective-permute-start(bf16[64,512]{1,0:T(8,128)(2,1)S(1)} %slice.6.refs_0_), channel_id=1, source_target_pairs={{0,8},{4,12},{8,0},{12,4},{1,9},{5,13},{9,1},{13,5},{2,10},{6,14},... | collective-permute-start | bytes 196616 | tf_op jit(solution)/shard_map/ppermute | solution.py:45
  9.2 6.5 %collective-permute-start.5 = (bf16[64,1024]{1,0:T(8,128)(2,1)S(1)}, bf16[64,1024]{1,0:T(8,128)(2,1)S(1)}, u32[]{:S(2)}, u32[]{:S(2)}) collective-permute-start(bf16[64,1024]{1,0:T(8,128)(2,1)S(1)} %shard_map.87.refs_0_), channel_id=1, source_target_pairs={{0,4},{4,0},{8,12},{12,8},{1,5},{5,1},{9,13},{13,9},{2,6},{6,2},{1... | collective-permute-start | bytes 393224 | tf_op jit(solution)/shard_map/ppermute | solution.py:45
  11.8 5.8 %collective-permute-start.1 = (bf16[64,1024]{1,0:T(8,128)(2,1)S(1)}, bf16[64,1024]{1,0:T(8,128)(2,1)S(1)}, u32[]{:S(2)}, u32[]{:S(2)}) collective-permute-start(bf16[64,1024]{1,0:T(8,128)(2,1)S(1)} %shard_map.84.refs_0_), channel_id=1, source_target_pairs={{0,4},{4,0},{8,12},{12,8},{1,5},{5,1},{9,13},{13,9},{2,6},{6,2},{1... | collective-permute-start | bytes 393224 | tf_op jit(solution)/shard_map/ppermute | solution.py:45
  15.7 5.6 %slice-start = ((s8[7340032]{0:T(1024)(128)(4,1)}), s8[4194304]{0:T(1024)(128)(4,1)S(1)}, s32[]{:S(2)}) async-start(s8[7340032]{0:T(1024)(128)(4,1)} %bitcast), calls=%async_computation | async-start | bytes 8388608
  15.7 5.6 %slice-start.2 = ((s8[7340032]{0:T(1024)(128)(4,1)}), s8[4194304]{0:T(1024)(128)(4,1)S(1)}, s32[]{:S(2)}) async-start(s8[7340032]{0:T(1024)(128)(4,1)} %bitcast.2), calls=%async_computation.2 | async-start | bytes 8388608
  15.7 8.0 %copy-start.6 = (bf16[64,2048]{1,0:T(8,128)(2,1)}, bf16[64,2048]{1,0:T(8,128)(2,1)S(1)}, u32[]{:S(2)}) copy-start(bf16[64,2048]{1,0:T(8,128)(2,1)S(1)} %shard_map.88.refs_0_.refs_2_) | copy-start | bytes 786436
  15.7 2.0 %copy-start.4 = (bf16[192,512]{1,0:T(8,128)(2,1)S(1)}, bf16[192,512]{1,0:T(8,128)(2,1)}, u32[]{:S(2)}) copy-start(bf16[192,512]{1,0:T(8,128)(2,1)} %refs_0_.3) | copy-start | bytes 589828
  15.7 2.0 %copy-start.5 = (bf16[192,512]{1,0:T(8,128)(2,1)S(1)}, bf16[192,512]{1,0:T(8,128)(2,1)}, u32[]{:S(2)}) copy-start(bf16[192,512]{1,0:T(8,128)(2,1)} %refs_1_.3) | copy-start | bytes 589828
  15.8 5.5 %slice-start.1 = ((s8[7340032]{0:T(1024)(128)(4,1)}), s8[3145728]{0:T(1024)(128)(4,1)S(1)}, s32[]{:S(2)}) async-start(s8[7340032]{0:T(1024)(128)(4,1)} %bitcast), calls=%async_computation.1 | async-start | bytes 6291456
  15.8 5.5 %slice-start.3 = ((s8[7340032]{0:T(1024)(128)(4,1)}), s8[3145728]{0:T(1024)(128)(4,1)S(1)}, s32[]{:S(2)}) async-start(s8[7340032]{0:T(1024)(128)(4,1)} %bitcast.2), calls=%async_computation.3 | async-start | bytes 6291456
  15.8 5.5 %collective-permute-start.6 = (bf16[64,2048]{1,0:T(8,128)(2,1)S(1)}, bf16[64,2048]{1,0:T(8,128)(2,1)S(1)}, u32[]{:S(2)}, u32[]{:S(2)}) collective-permute-start(bf16[64,2048]{1,0:T(8,128)(2,1)S(1)} %shard_map.88.refs_0_.refs_2_), channel_id=1, source_target_pairs={{0,1},{1,0},{2,3},{3,2},{4,5},{5,4},{6,7},{7,6},{8,9},{9,8},{10,11... | collective-permute-start | bytes 786440 | tf_op jit(solution)/shard_map/ppermute | solution.py:40
  17.7 7.7 %copy-start.10 = (bf16[64,2048]{1,0:T(8,128)(2,1)}, bf16[64,2048]{1,0:T(8,128)(2,1)S(1)}, u32[]{:S(2)}) copy-start(bf16[64,2048]{1,0:T(8,128)(2,1)S(1)} %shard_map.85.refs_2_.refs_0_.refs_3_) | copy-start | bytes 786436
  17.7 7.7 %collective-permute-start.3 = (bf16[64,2048]{1,0:T(8,128)(2,1)S(1)}, bf16[64,2048]{1,0:T(8,128)(2,1)S(1)}, u32[]{:S(2)}, u32[]{:S(2)}) collective-permute-start(bf16[64,2048]{1,0:T(8,128)(2,1)S(1)} %shard_map.85.refs_2_.refs_0_.refs_3_), channel_id=1, source_target_pairs={{0,1},{1,0},{2,3},{3,2},{4,5},{5,4},{6,7},{7,6},{8,9},{9,8},{10,11... | collective-permute-start | bytes 786440 | tf_op jit(solution)/shard_map/ppermute | solution.py:40
  17.8 7.6 %slice-start.4 = ((s8[7340032]{0:T(1024)(128)(4,1)}), s8[4194304]{0:T(1024)(128)(4,1)S(1)}, s32[]{:S(2)}) async-start(s8[7340032]{0:T(1024)(128)(4,1)} %bitcast.4), calls=%async_computation.4 | async-start | bytes 8388608
  17.8 7.6 %slice-start.5 = ((s8[7340032]{0:T(1024)(128)(4,1)}), s8[3145728]{0:T(1024)(128)(4,1)S(1)}, s32[]{:S(2)}) async-start(s8[7340032]{0:T(1024)(128)(4,1)} %bitcast.4), calls=%async_computation.5 | async-start | bytes 6291456
  17.8 10.4 %collective-permute-start.2 = (bf16[128,512]{1,0:T(8,128)(2,1)S(1)}, bf16[128,512]{1,0:T(8,128)(2,1)S(1)}, u32[]{:S(2)}, u32[]{:S(2)}) collective-permute-start(bf16[128,512]{1,0:T(8,128)(2,1)S(1)} %shard_map.86.refs_0_), channel_id=1, source_target_pairs={{0,8},{4,12},{8,0},{12,4},{1,9},{5,13},{9,1},{13,5},{2,10},{6,14},... | collective-permute-start | bytes 393224 | tf_op jit(solution)/shard_map/ppermute | solution.py:45
  21.3 2.4 %copy-start.8 = (bf16[64,2048]{1,0:T(8,128)(2,1)}, bf16[64,2048]{1,0:T(8,128)(2,1)S(1)}, u32[]{:S(2)}) copy-start(bf16[64,2048]{1,0:T(8,128)(2,1)S(1)} %collective-permute-done.6.refs_1_.refs_3_) | copy-start | bytes 786436
  23.7 33.1 %collective-permute-start.8 = (bf16[256,1792]{1,0:T(8,128)(2,1)S(1)}, bf16[256,1792]{1,0:T(8,128)(2,1)S(1)}, u32[]{:S(2)}, u32[]{:S(2)}) collective-permute-start(bf16[256,1792]{1,0:T(8,128)(2,1)S(1)} %shard_map.89.refs_3_.refs_0_), channel_id=1, source_target_pairs={{0,2},{2,0},{1,3},{3,1},{4,6},{6,4},{5,7},{7,5},{8,10},{10,8},{9,1... | collective-permute-start | bytes 2752520 | tf_op jit(solution)/shard_map/ppermute | solution.py:40
  25.4 11.0 %copy-start.12 = (bf16[64,2048]{1,0:T(8,128)(2,1)}, bf16[64,2048]{1,0:T(8,128)(2,1)S(1)}, u32[]{:S(2)}) copy-start(bf16[64,2048]{1,0:T(8,128)(2,1)S(1)} %collective-permute-done.3.refs_1_.refs_4_) | copy-start | bytes 786436
  28.2 8.2 %collective-permute-start.10 = (bf16[128,1024]{1,0:T(8,128)(2,1)S(1)}, bf16[128,1024]{1,0:T(8,128)(2,1)S(1)}, u32[]{:S(2)}, u32[]{:S(2)}) collective-permute-start(bf16[128,1024]{1,0:T(8,128)(2,1)S(1)} %shard_map.91.refs_2_.refs_0_), channel_id=1, source_target_pairs={{0,4},{4,0},{8,12},{12,8},{1,5},{5,1},{9,13},{13,9},{2,6},{6,2},{1... | collective-permute-start | bytes 786440 | tf_op jit(solution)/shard_map/ppermute | solution.py:45
  36.5 8.8 %copy-start = (bf16[128,2048]{1,0:T(8,128)(2,1)}, bf16[128,2048]{1,0:T(8,128)(2,1)S(1)}, u32[]{:S(2)}) copy-start(bf16[128,2048]{1,0:T(8,128)(2,1)S(1)} %shard_map.93.refs_0_.refs_2_.refs_4_.refs_5_) | copy-start | bytes 1572868
  36.5 4.2 %collective-permute-start.11 = (bf16[128,2048]{1,0:T(8,128)(2,1)S(1)}, bf16[128,2048]{1,0:T(8,128)(2,1)S(1)}, u32[]{:S(2)}, u32[]{:S(2)}) collective-permute-start(bf16[128,2048]{1,0:T(8,128)(2,1)S(1)} %shard_map.93.refs_0_.refs_2_.refs_4_.refs_5_), channel_id=1, source_target_pairs={{0,1},{1,0},{2,3},{3,2},{4,5},{5,4},{6,7},{7,6},{8,9},{9,8},{10,11... | collective-permute-start | bytes 1572872 | tf_op jit(solution)/shard_map/ppermute | solution.py:40
  36.6 20.2 %collective-permute-start.9 = (bf16[128,1792]{1,0:T(8,128)(2,1)S(1)}, bf16[128,1792]{1,0:T(8,128)(2,1)S(1)}, u32[]{:S(2)}, u32[]{:S(2)}) collective-permute-start(bf16[128,1792]{1,0:T(8,128)(2,1)S(1)} %shard_map.90.refs_2_.refs_1_), channel_id=1, source_target_pairs={{0,2},{2,0},{1,3},{3,1},{4,6},{6,4},{5,7},{7,5},{8,10},{10,8},{9,1... | collective-permute-start | bytes 1376264 | tf_op jit(solution)/shard_map/ppermute | solution.py:40
  38.1 24.3 %collective-permute-start.7 = (bf16[128,512]{1,0:T(8,128)(2,1)S(1)}, bf16[128,512]{1,0:T(8,128)(2,1)S(1)}, u32[]{:S(2)}, u32[]{:S(2)}) collective-permute-start(bf16[128,512]{1,0:T(8,128)(2,1)S(1)} %shard_map.92.refs_0_), channel_id=1, source_target_pairs={{0,8},{4,12},{8,0},{12,4},{1,9},{5,13},{9,1},{13,5},{2,10},{6,14},... | collective-permute-start | bytes 393224 | tf_op jit(solution)/shard_map/ppermute | solution.py:45
  40.7 4.6 %copy-start.2 = (bf16[128,2048]{1,0:T(8,128)(2,1)}, bf16[128,2048]{1,0:T(8,128)(2,1)S(1)}, u32[]{:S(2)}) copy-start(bf16[128,2048]{1,0:T(8,128)(2,1)S(1)} %collective-permute-done.11.refs_1_.refs_3_.refs_5_.refs_6_) | copy-start | bytes 1572868
  45.3 41.0 %collective-permute-start.17 = (bf16[384,1792]{1,0:T(8,128)(2,1)S(1)}, bf16[384,1792]{1,0:T(8,128)(2,1)S(1)}, u32[]{:S(2)}, u32[]{:S(2)}) collective-permute-start(bf16[384,1792]{1,0:T(8,128)(2,1)S(1)} %shard_map.94.refs_6_.refs_0_), channel_id=1, source_target_pairs={{0,2},{2,0},{1,3},{3,1},{4,6},{6,4},{5,7},{7,5},{8,10},{10,8},{9,1... | collective-permute-start | bytes 4128776 | tf_op jit(solution)/shard_map/ppermute | solution.py:40
  62.4 6.9 %collective-permute-start.12 = (bf16[128,1024]{1,0:T(8,128)(2,1)S(1)}, bf16[128,1024]{1,0:T(8,128)(2,1)S(1)}, u32[]{:S(2)}, u32[]{:S(2)}) collective-permute-start(bf16[128,1024]{1,0:T(8,128)(2,1)S(1)} %shard_map.96.refs_0_), channel_id=1, source_target_pairs={{0,4},{4,0},{8,12},{12,8},{1,5},{5,1},{9,13},{13,9},{2,6},{6,2},{1... | collective-permute-start | bytes 786440 | tf_op jit(solution)/shard_map/ppermute | solution.py:45
  69.3 8.0 %collective-permute-start.13 = (bf16[128,2048]{1,0:T(8,128)(2,1)S(1)}, bf16[128,2048]{1,0:T(8,128)(2,1)S(1)}, u32[]{:S(2)}, u32[]{:S(2)}) collective-permute-start(bf16[128,2048]{1,0:T(8,128)(2,1)S(1)} %shard_map.97.refs_0_.refs_2_.refs_4_.refs_7_), channel_id=1, source_target_pairs={{0,1},{1,0},{2,3},{3,2},{4,5},{5,4},{6,7},{7,6},{8,9},{9,8},{10,11... | collective-permute-start | bytes 1572872 | tf_op jit(solution)/shard_map/ppermute | solution.py:40
  69.4 2.3 %collective-permute-start.14 = (bf16[64,2048]{1,0:T(8,128)(2,1)S(1)}, bf16[64,2048]{1,0:T(8,128)(2,1)S(1)}, u32[]{:S(2)}, u32[]{:S(2)}) collective-permute-start(bf16[64,2048]{1,0:T(8,128)(2,1)S(1)} %get-tuple-element.46), channel_id=1, source_target_pairs={{0,1},{1,0},{2,3},{3,2},{4,5},{5,4},{6,7},{7,6},{8,9},{9,8},{10,11... | collective-permute-start | bytes 786440 | tf_op jit(solution)/shard_map/ppermute | solution.py:40
  71.7 5.6 %collective-permute-start.18 = (bf16[64,1024]{1,0:T(8,128)(2,1)S(1)}, bf16[64,1024]{1,0:T(8,128)(2,1)S(1)}, u32[]{:S(2)}, u32[]{:S(2)}) collective-permute-start(bf16[64,1024]{1,0:T(8,128)(2,1)S(1)} %get-tuple-element.48), channel_id=1, source_target_pairs={{0,4},{4,0},{8,12},{12,8},{1,5},{5,1},{9,13},{13,9},{2,6},{6,2},{1... | collective-permute-start | bytes 393224 | tf_op jit(solution)/shard_map/ppermute | solution.py:45
  79.8 21.1 %collective-permute-start.16 = (bf16[384,896]{1,0:T(8,128)(2,1)S(1)}, bf16[384,896]{1,0:T(8,128)(2,1)S(1)}, u32[]{:S(2)}, u32[]{:S(2)}) collective-permute-start(bf16[384,896]{1,0:T(8,128)(2,1)S(1)} %shard_map.99.refs_9_.refs_0_), channel_id=1, source_target_pairs={{0,2},{2,0},{1,3},{3,1},{4,6},{6,4},{5,7},{7,5},{8,10},{10,8},{9,1... | collective-permute-start | bytes 2064392 | tf_op jit(solution)/shard_map/ppermute | solution.py:40
  91.8 11.9 %collective-permute-start.20 = (bf16[64,2048]{1,0:T(8,128)(2,1)S(1)}, bf16[64,2048]{1,0:T(8,128)(2,1)S(1)}, u32[]{:S(2)}, u32[]{:S(2)}) collective-permute-start(bf16[64,2048]{1,0:T(8,128)(2,1)S(1)} %get-tuple-element.60), channel_id=1, source_target_pairs={{0,1},{1,0},{2,3},{3,2},{4,5},{5,4},{6,7},{7,6},{8,9},{9,8},{10,11... | collective-permute-start | bytes 786440 | tf_op jit(solution)/shard_map/ppermute | solution.py:40
  91.9 5.4 %collective-permute-start.19 = (bf16[64,512]{1,0:T(8,128)(2,1)S(1)}, bf16[64,512]{1,0:T(8,128)(2,1)S(1)}, u32[]{:S(2)}, u32[]{:S(2)}) collective-permute-start(bf16[64,512]{1,0:T(8,128)(2,1)S(1)} %get-tuple-element.51), channel_id=1, source_target_pairs={{0,8},{4,12},{8,0},{12,4},{1,9},{5,13},{9,1},{13,5},{2,10},{6,14},... | collective-permute-start | bytes 196616 | tf_op jit(solution)/shard_map/ppermute | solution.py:45
  97.3 21.0 %collective-permute-start.15 = (bf16[384,896]{1,0:T(8,128)(2,1)S(1)}, bf16[384,896]{1,0:T(8,128)(2,1)S(1)}, u32[]{:S(2)}, u32[]{:S(2)}) collective-permute-start(bf16[384,896]{1,0:T(8,128)(2,1)S(1)} %shard_map.100.refs_4_.refs_0_), channel_id=1, source_target_pairs={{0,2},{2,0},{1,3},{3,1},{4,6},{6,4},{5,7},{7,5},{8,10},{10,8},{9,1... | collective-permute-start | bytes 2064392 | tf_op jit(solution)/shard_map/ppermute | solution.py:40
  100.9 4.3 %copy-start.1 = (bf16[128,2048]{1,0:T(8,128)(2,1)S(1)}, bf16[128,2048]{1,0:T(8,128)(2,1)}, u32[]{:S(2)}) copy-start(bf16[128,2048]{1,0:T(8,128)(2,1)} %copy-done) | copy-start | bytes 1572868
  100.9 4.3 %copy-start.3 = (bf16[128,2048]{1,0:T(8,128)(2,1)S(1)}, bf16[128,2048]{1,0:T(8,128)(2,1)}, u32[]{:S(2)}) copy-start(bf16[128,2048]{1,0:T(8,128)(2,1)} %copy-done.2) | copy-start | bytes 1572868
  100.9 4.3 %copy-start.11 = (bf16[64,2048]{1,0:T(8,128)(2,1)S(1)}, bf16[64,2048]{1,0:T(8,128)(2,1)}, u32[]{:S(2)}) copy-start(bf16[64,2048]{1,0:T(8,128)(2,1)} %copy-done.10) | copy-start | bytes 786436
  100.9 4.3 %copy-start.13 = (bf16[64,2048]{1,0:T(8,128)(2,1)S(1)}, bf16[64,2048]{1,0:T(8,128)(2,1)}, u32[]{:S(2)}) copy-start(bf16[64,2048]{1,0:T(8,128)(2,1)} %copy-done.12) | copy-start | bytes 786436
  103.7 8.6 %copy-start.7 = (bf16[64,2048]{1,0:T(8,128)(2,1)S(1)}, bf16[64,2048]{1,0:T(8,128)(2,1)}, u32[]{:S(2)}) copy-start(bf16[64,2048]{1,0:T(8,128)(2,1)} %copy-done.6) | copy-start | bytes 786436
  103.8 8.6 %copy-start.9 = (bf16[64,2048]{1,0:T(8,128)(2,1)S(1)}, bf16[64,2048]{1,0:T(8,128)(2,1)}, u32[]{:S(2)}) copy-start(bf16[64,2048]{1,0:T(8,128)(2,1)} %copy-done.8) | copy-start | bytes 786436
  103.9 6.6 %collective-permute-start.21 = (bf16[64,1024]{1,0:T(8,128)(2,1)S(1)}, bf16[64,1024]{1,0:T(8,128)(2,1)S(1)}, u32[]{:S(2)}, u32[]{:S(2)}) collective-permute-start(bf16[64,1024]{1,0:T(8,128)(2,1)S(1)} %get-tuple-element.62), channel_id=1, source_target_pairs={{0,4},{4,0},{8,12},{12,8},{1,5},{5,1},{9,13},{13,9},{2,6},{6,2},{1... | collective-permute-start | bytes 393224 | tf_op jit(solution)/shard_map/ppermute | solution.py:45
  110.5 7.8 %collective-permute-start.22 = (bf16[64,512]{1,0:T(8,128)(2,1)S(1)}, bf16[64,512]{1,0:T(8,128)(2,1)S(1)}, u32[]{:S(2)}, u32[]{:S(2)}) collective-permute-start(bf16[64,512]{1,0:T(8,128)(2,1)S(1)} %get-tuple-element.67), channel_id=1, source_target_pairs={{0,8},{4,12},{8,0},{12,4},{1,9},{5,13},{9,1},{13,5},{2,10},{6,14},... | collective-permute-start | bytes 196616 | tf_op jit(solution)/shard_map/ppermute | solution.py:45
  121.3 1.6 %collective-permute-start.23 = (bf16[64,2048]{1,0:T(8,128)(2,1)S(1)}, bf16[64,2048]{1,0:T(8,128)(2,1)S(1)}, u32[]{:S(2)}, u32[]{:S(2)}) collective-permute-start(bf16[64,2048]{1,0:T(8,128)(2,1)S(1)} %get-tuple-element.69), channel_id=1, source_target_pairs={{0,1},{1,0},{2,3},{3,2},{4,5},{5,4},{6,7},{7,6},{8,9},{9,8},{10,11... | collective-permute-start | bytes 786440 | tf_op jit(solution)/shard_map/ppermute | solution.py:40
  122.9 5.6 %collective-permute-start.24 = (bf16[64,1024]{1,0:T(8,128)(2,1)S(1)}, bf16[64,1024]{1,0:T(8,128)(2,1)S(1)}, u32[]{:S(2)}, u32[]{:S(2)}) collective-permute-start(bf16[64,1024]{1,0:T(8,128)(2,1)S(1)} %get-tuple-element.71), channel_id=1, source_target_pairs={{0,4},{4,0},{8,12},{12,8},{1,5},{5,1},{9,13},{13,9},{2,6},{6,2},{1... | collective-permute-start | bytes 393224 | tf_op jit(solution)/shard_map/ppermute | solution.py:45
  128.6 7.8 %collective-permute-start.25 = (bf16[64,512]{1,0:T(8,128)(2,1)S(1)}, bf16[64,512]{1,0:T(8,128)(2,1)S(1)}, u32[]{:S(2)}, u32[]{:S(2)}) collective-permute-start(bf16[64,512]{1,0:T(8,128)(2,1)S(1)} %get-tuple-element.73), channel_id=1, source_target_pairs={{0,8},{4,12},{8,0},{12,4},{1,9},{5,13},{9,1},{13,5},{2,10},{6,14},... | collective-permute-start | bytes 196616 | tf_op jit(solution)/shard_map/ppermute | solution.py:45

commit v7 on v6

--- a/solution.py
+++ b/solution.py
@@ -174,7 +174,7 @@
                     value = rows_by_cols(held[...], weight[:, at])
                 out[top : top + tokens, base : base + size] = value.astype(out.dtype)
 
-            over_blocks(width, 896, product)
+            over_blocks(width, 1024, product)
 
     return local(
         kernel,
@@ -191,23 +191,21 @@
     width, features, tokens = upper - lower, weights[0].shape[0], 2 * rows
     count = len(own)
     ins_all = (*own, *other, *weights, *(() if before is None else (before,)))
-    outs_all = [((tokens, width), jnp.bfloat16)] * 3
+    outs_all = [((width, tokens), jnp.bfloat16)] + [((tokens, width), jnp.bfloat16)] * 2
     outs_all += [((rows, features), jnp.float32), ((rows, features), jnp.bfloat16)] if final else [((tokens, features), jnp.float32)]
 
     def kernel(ins, outs):
-        step = width // 7
-
-        @pl.loop(0, 7)
+        @pl.loop(0, width // 256)
         def _(j):
-            at = lanes(j, step)
+            at = lanes(j, 256)
 
             def total(k):
                 array, top = where[k]
                 mine = ins[array][top : top + tokens, at].astype(jnp.float32)
                 return mine + ins[count + array][top : top + tokens, at].astype(jnp.float32)
 
-            for ref, value in zip(outs[:3], swiglu_grads(total(0), total(1), total(2))):
-                ref[:, at] = value
+            hidden, outs[1][:, at], outs[2][:, at] = swiglu_grads(total(0), total(1), total(2))
+            outs[0][at, :] = hidden.T
 
         def product(base, size):
             at = slice(base, base + size)
@@ -270,12 +268,17 @@
     return local(kernel, [(shape, jnp.bfloat16)], (mine, theirs, *earlier), limit=4, out_specs=specs)[0]
 
 
-def stack(target, pieces, refs, at=None):
-    top = 0
-    for index, first, rows, column in pieces:
-        width = target.shape[1]
-        target[top : top + rows] = refs[index][first : first + rows, column : column + width]
-        top += rows
+def turned(own, theirs, first, rows, after=()):
+    features = own.shape[1]
+
+    def kernel(ins, outs):
+        @pl.loop(0, features // 512)
+        def _(j):
+            at = lanes(j, 512)
+            both = jnp.concatenate([ref[first : first + rows, at] for ref in ins], axis=0)
+            outs[0][at, :] = both.T
+
+    return local(kernel, [((features, 2 * rows), own.dtype)], (own, theirs), after, limit=4)[0]
 
 
 def gradients(kernel, outs, arrays, old, grid, specs, scratch, after, cost):
@@ -296,10 +299,14 @@
     )(*arrays, *old, *after)
 
 
-def column_grads(xs, gs, us, part, parts, total, old, after=()):
-    arrays = [p[0] for p in (*xs, *gs, *us)]
-    n_x, n_g = len(xs), len(gs)
-    tokens, features, width = sum(p[2] for p in xs), xs[0][0].shape[1], total // parts
+def placed(rows, columns, where):
+    return pl.BlockSpec((pl.Element(rows), pl.Element(columns)), where)
+
+
+def column_grads(xs, gs, us, span, total, old, after=()):
+    arrays = [*xs, *(p[0] for p in (*gs, *us))]
+    count, lower, width = len(xs), span[0], span[1] - span[0]
+    tokens, features = sum(x.shape[1] for x in xs), xs[0].shape[0]
     block = 512
 
     def kernel(ins, refs):
@@ -309,26 +316,28 @@
         @pl.when(step == 0)
         def _():
             token[...] = jnp.zeros_like(token)
-            stack(g_all, [(n_x + i, *p[1:]) for i, p in enumerate(gs)], ins)
-            stack(u_all, [(n_x + n_g + i, *p[1:]) for i, p in enumerate(us)], ins)
+            for first, pieces, target in ((count, gs, g_all), (2 * count, us, u_all)):
+                top = 0
+                for i, (piece, column) in enumerate(pieces):
+                    rows = piece.shape[0]
+                    target[top : top + rows] = ins[first + i][:, column : column + width]
+                    top += rows
 
         at = lanes(step, block)
-        x = jnp.concatenate([ins[i][p[1] : p[1] + p[2], at] for i, p in enumerate(xs)], axis=0).T
+        x = jnp.concatenate([ins[i][at, :] for i in range(count)], axis=1)
         gate_out[...] = rows_by_cols(x, g_all[...]).astype(gate_out.dtype)
         up_out[...] = rows_by_cols(x, u_all[...]).astype(up_out.dtype)
 
-    spec = pl.BlockSpec((block, width), lambda i: (i, part))
+    spec = placed(block, width, lambda i: (i * block, lower))
     scratch = [pltpu.VMEM((tokens, width), jnp.bfloat16)] * 2
-    return gradients(
-        kernel, [(features, total)] * 2, arrays, old, (features // block,), [spec, spec], scratch, after, 5.0
-    )
-
-
-def row_grads(hs, ys, part, parts, total, old, after=()):
+    return gradients(kernel, [(features, total)] * 2, arrays, old, (features // block,), [spec, spec], scratch, after, 5.0)
+
+
+def row_grads(hs, ys, span, total, old, after=()):
     arrays = [p[0] for p in (*hs, *ys)]
-    n_h = len(hs)
-    tokens, features, width = sum(p[2] for p in ys), ys[0][0].shape[1], total // parts
-    block = 256
+    count, lower, width = len(hs), span[0], span[1] - span[0]
+    tokens, features = sum(p[0].shape[1] for p in hs), ys[0][0].shape[1]
+    block = 512
 
     def kernel(ins, refs):
         out, token, h_all = refs
@@ -337,18 +346,18 @@
         @pl.when(step == 0)
         def _():
             token[...] = jnp.zeros_like(token)
-            pieces = [ins[i][p[1] : p[1] + p[2], p[3] : p[3] + width] for i, p in enumerate(hs)]
-            h_all[...] = jnp.concatenate(pieces, axis=0).T
+            left = 0
+            for i, (piece, row) in enumerate(hs):
+                h_all[:, left : left + piece.shape[1]] = ins[i][row : row + width]
+                left += piece.shape[1]
 
         at = lanes(step, block)
-        y = jnp.concatenate([ins[n_h + i][p[1] : p[1] + p[2], at] for i, p in enumerate(ys)], axis=0)
+        y = jnp.concatenate([ins[count + i][top : top + rows, at] for i, (_, top, rows) in enumerate(ys)], axis=0)
         out[...] = rows_by_cols(h_all[...], y).astype(out.dtype)
 
-    spec = pl.BlockSpec((width, block), lambda i: (part, i))
+    spec = placed(width, block, lambda i: (lower, i * block))
     scratch = [pltpu.VMEM((width, tokens), jnp.bfloat16)]
-    return gradients(
-        kernel, [(total, features)], arrays, old, (features // block,), [spec], scratch, after, 3.0
-    )
+    return gradients(kernel, [(total, features)], arrays, old, (features // block,), [spec], scratch, after, 3.0)
 
 
 def piped(acts, grad_out, w_gate, w_up, w_down):
@@ -360,7 +369,8 @@
     heights = [upper - lower for lower, upper in spans]
     last = len(spans) - 1
     total = w_gate.shape[1]
-    whole, halves = (0, total), ((0, total // 2), (total // 2, total))
+    cut = total // 7 * 4
+    whole, halves = (0, total), ((0, cut), (cut, total))
     back_weights = (w_gate, w_up)
 
     lower, upper = spans[0]
@@ -414,47 +424,44 @@
     def end_step(far, earlier=()):
         return fold_last(far[0], swapped(far[1], "hid", 2), earlier)
 
-    pair = gather_piece(1, (mixed[1],), (dhid,))
+    pair = gather_piece(1, (dhid,), ())
     done = forward_piece(1, ())
-    grads = [backward_piece(0, 0, None, True, done)]
-    gather_piece(2, (pair,), (grads[0][0],))
+    xs = [turned(*x, rows, done) for (x, _), rows in zip(inputs, heights)]
+    grads = [backward_piece(0, 0, None, True, (*done, *xs))]
+    gather_piece(2, (pair,), (grads[0][1],))
     near = near_step(grads[0])
     done = forward_piece(2, (near[0],))
+    xs.append(turned(*inputs[last][0], heights[last], done))
     far = far_step(near)
-    grads.append(backward_piece(1, 0, None, True, (*done, far[0])))
+    grads.append(backward_piece(1, 0, None, True, (*done, xs[last], far[0])))
     finished = [end_step(far)]
 
-    xs, ys = [], []
-    for index, (x, dy) in enumerate(inputs):
-        for pieces, (own, other, first) in ((xs, x), (ys, dy)):
-            pieces.append((own, first, heights[index], 0))
-            pieces.append((other, first, heights[index], 0))
+    ys = [(array, y[2], rows) for (_, y), rows in zip(inputs, heights) for array in y[:2]]
 
     def with_last(results, k, part):
-        pieces = [(grads[c][k], 0, 2 * heights[c], halves[part][0]) for c in range(last)]
-        return pieces + [(results[k], 0, 2 * heights[last], 0)]
-
-    first = backward_piece(last, 0, None, False, (grads[1][0], finished[0]))
+        return [(grads[c][k], halves[part][0]) for c in range(last)] + [(results[k], 0)]
+
+    first = backward_piece(last, 0, None, False, (grads[1][1], finished[0]))
     near = near_step(grads[1])
-    down, down_token = row_grads(with_last(first, 0, 0), ys, 0, 2, total, (), (near[0],))
+    down, down_token = row_grads(with_last(first, 0, 0), ys, halves[0], total, (), (near[0],))
     far = far_step(near)
     gate, up, token = column_grads(
-        xs, with_last(first, 1, 0), with_last(first, 2, 0), 0, 2, total, (), (far[0], down_token)
+        xs, with_last(first, 1, 0), with_last(first, 2, 0), halves[0], total, (), (far[0], down_token)
     )
     finished.append(end_step(far))
     second = backward_piece(last, 1, first[3], True, (token, finished[1]))
     near = near_step(second)
-    down, down_token = row_grads(with_last(second, 0, 1), ys, 1, 2, total, (down,), ())
+    down, down_token = row_grads(with_last(second, 0, 1), ys, halves[1], total, (down,), ())
     far = far_step(near)
     gate, up, _ = column_grads(
-        xs, with_last(second, 1, 1), with_last(second, 2, 1), 1, 2, total, (gate, up), (near[0], down_token)
+        xs, with_last(second, 1, 1), with_last(second, 2, 1), halves[1], total, (gate, up), (near[0], down_token)
     )
     return end_step(far, finished), gate, up, down
 
 
 def shards(acts, grad_out, w_gate, w_up, w_down):
     sizes = tuple(lax.axis_size(axis) for axis in ("hid", "wid", "tok"))
-    aligned = acts.shape[0] % (16 * sum(PIECES)) == 0 and acts.shape[1] % 128 == 0 and w_gate.shape[0] % 512 == 0 and w_gate.shape[1] % 1792 == 0
+    aligned = acts.shape[0] % (64 * sum(PIECES)) == 0 and acts.shape[1] % 128 == 0 and w_gate.shape[0] % 512 == 0 and w_gate.shape[1] % 1792 == 0
     if sizes == (4, 2, 2) and aligned:
         return piped(acts, grad_out, w_gate, w_up, w_down)
     return plain(acts, grad_out, w_gate, w_up, w_down)

time: 137 us -> 141 us (1.029)
  waiting for transfers between devices: 44.7 us -> 49.1 us
  local copies, waits for them, and re-layouts: 1.79 us -> 5.13 us
  Pallas kernels: 54.9 us -> 52.8 us
  starting transfers between devices: 34.7 us -> 33.2 us
    ppermute x14, waiting for transfers between devices: 26.1 us -> 31.3 us  [swapped(): return lax.ppermute(value, axis, [(i, i ^ bit) for i in range(n)])]
    pallas_call x4, Pallas kernels: 22.7 us -> 19.3 us  [gradients(): pl.pallas_call(body, grid=grid, out_shape=[jax.ShapeDtypeStruct(shape, jn...]
    unnamed x40 -> x32, local copies, waits for them, and re-layouts: 0.1 us -> 3.44 us
    ppermute x14, starting transfers between devices: 26.7 us -> 24.9 us  [swapped(): return lax.ppermute(value, axis, [(i, i ^ bit) for i in range(n)])]
    pallas_call x28 -> x31, Pallas kernels: 32.2 us -> 33.5 us  [local(): pl.pallas_call(body, out_shape=shapes, in_specs=[VMEM] * (len(args) + len...]
  transfers between devices with their start and end apart: 26 -> 26, of which waited for: 15 -> 15; matrix products, arithmetic and copies ran while one was open for 1% -> 1% of each run, Pallas kernels for 37% -> 33%
where the time goes in v7:
time: 141 us
  Pallas kernels  52.8 us (37%)
  waiting for transfers between devices  49.1 us (35%)
  starting transfers between devices  33.2 us (24%)
  local copies, waits for them, and re-layouts  5.13 us (4%)
    pallas_call x31, Pallas kernels, local(): pl.pallas_call(body, out_shape=shapes, in_specs=[VMEM] * (len(args) + len...  33.5 us
    ppermute x14, waiting for transfers between devices, swapped(): return lax.ppermute(value, axis, [(i, i ^ bit) for i in range(n)])  31.3 us
    ppermute x14, starting transfers between devices, swapped(): return lax.ppermute(value, axis, [(i, i ^ bit) for i in range(n)])  24.9 us
    pallas_call x4, Pallas kernels, gradients(): pl.pallas_call(body, grid=grid, out_shape=[jax.ShapeDtypeStruct(shape, jn...  19.3 us
    ppermute x12, waiting for transfers between devices, shifted(): return lax.ppermute(value, axis, [(i, (i + step) % n) for i in range(n)])  17.8 us
    ppermute x12, starting transfers between devices, shifted(): return lax.ppermute(value, axis, [(i, (i + step) % n) for i in range(n)])  8.28 us
    unnamed x32, local copies, waits for them, and re-layouts  3.44 us
  transfers between devices with their start and end apart: 26, of which 15 were waited for; matrix products, arithmetic and copies ran while one was open for 1% of the time, Pallas kernels for 33%

profile of v7, /device:TPU:0, one launch (start us, length us, event | category | flops | bytes accessed | tf_op | source)
XLA Modules:
  0.0 141.2 jit_solution(4812065078487785414)
XLA Ops:
  0.6 0.8 slice.7.refs_0_
  1.5 4.0 %collective-permute-start.3 = (bf16[64,512]{1,0:T(8,128)(2,1)S(1)}, bf16[64,512]{1,0:T(8,128)(2,1)S(1)}, u32[]{:S(2)}, u32[]{:S(2)}) collective-permute-start(bf16[64,512]{1,0:T(8,128)(2,1)S(1)} %slice.7.refs_0_), channel_id=1, source_target_pairs={{0,8},{4,12},{8,0},{12,4},{1,9},{5,13},{9,1},{13,5},{2,10},{6,14},... | collective-permute-start | bytes 196616 | tf_op jit(solution)/shard_map/ppermute | solution.py:45
  5.5 0.8 slice.6.refs_0_
  6.4 2.8 %collective-permute-done.3.refs_1_ = bf16[64,512]{1,0:T(8,128)(2,1)S(1)} collective-permute-done((bf16[64,512]{1,0:T(8,128)(2,1)S(1)}, bf16[64,512]{1,0:T(8,128)(2,1)S(1)}, u32[]{:S(2)}, u32[]{:S(2)}) %collective-permute-start.3) | collective-permute-done | bytes 65568 | tf_op jit(solution)/shard_map/ppermute | solution.py:45
  9.2 2.2 %collective-permute-start.4 = (bf16[64,1024]{1,0:T(8,128)(2,1)S(1)}, bf16[64,1024]{1,0:T(8,128)(2,1)S(1)}, u32[]{:S(2)}, u32[]{:S(2)}) collective-permute-start(bf16[64,1024]{1,0:T(8,128)(2,1)S(1)} %shard_map.86.refs_0_), channel_id=1, source_target_pairs={{0,4},{4,0},{8,12},{12,8},{1,5},{5,1},{9,13},{13,9},{2,6},{6,2},{1... | collective-permute-start | bytes 393224 | tf_op jit(solution)/shard_map/ppermute | solution.py:45
  11.8 1.3 collective-permute-start.1
  13.2 2.5 %collective-permute-done.4.refs_1_ = bf16[64,1024]{1,0:T(8,128)(2,1)S(1)} collective-permute-done((bf16[64,1024]{1,0:T(8,128)(2,1)S(1)}, bf16[64,1024]{1,0:T(8,128)(2,1)S(1)}, u32[]{:S(2)}, u32[]{:S(2)}) %collective-permute-start.4) | collective-permute-done | bytes 131104 | tf_op jit(solution)/shard_map/ppermute | solution.py:45
  15.8 1.8 %collective-permute-done.1.refs_1_ = bf16[64,1024]{1,0:T(8,128)(2,1)S(1)} collective-permute-done((bf16[64,1024]{1,0:T(8,128)(2,1)S(1)}, bf16[64,1024]{1,0:T(8,128)(2,1)S(1)}, u32[]{:S(2)}, u32[]{:S(2)}) %collective-permute-start.1) | collective-permute-done | bytes 131104 | tf_op jit(solution)/shard_map/ppermute | solution.py:45
  17.9 1.4 slice-done.2
  19.2 0.9 slice-done.1
  20.2 0.9 slice-done.3
  21.1 2.1 %shard_map.88.refs_3_.refs_0_ = bf16[256,1792]{1,0:T(8,128)(2,1)S(1)} custom-call(bf16[64,2048]{1,0:T(8,128)(2,1)S(1)} %shard_map.87.refs_0_.refs_2_, bf16[64,2048]{1,0:T(8,128)(2,1)S(1)} %collective-permute-done.5.refs_1_.refs_3_, bf16[64,2048]{1,0:T(8,128)(2,1)S(1)} %shard_map.87.refs_0_.refs_2_, ...), custom_call_target="tpu_custom_call" | custom-call | flops 345000000 | tf_op jit(solution)/shard_map/pallas_call | solution.py:102
  23.3 2.5 %shard_map.89.refs_2_.refs_1_ = bf16[128,1792]{1,0:T(8,128)(2,1)S(1)} custom-call(bf16[64,2048]{1,0:T(8,128)(2,1)S(1)} %shard_map.85.refs_0_.refs_3_, bf16[64,2048]{1,0:T(8,128)(2,1)S(1)} %collective-permute-done.2.refs_1_.refs_4_, bf16[1792,2048]{1,0:T(8,128)(2,1)S(1)} %bitcast.5, bf16[256,1792]{1,0:T(8,128)(2,1)S(1)} %shard_map.88.refs_3_.refs_0_), custom_call_target="tpu_custom_call" | custom-call | flops 345000000 | tf_op jit(solution)/shard_map/pallas_call | solution.py:102
  25.9 3.4 %collective-permute-start.6 = (bf16[128,512]{1,0:T(8,128)(2,1)S(1)}, bf16[128,512]{1,0:T(8,128)(2,1)S(1)}, u32[]{:S(2)}, u32[]{:S(2)}) collective-permute-start(bf16[128,512]{1,0:T(8,128)(2,1)S(1)} %shard_map.90.refs_0_), channel_id=1, source_target_pairs={{0,8},{4,12},{8,0},{12,4},{1,9},{5,13},{9,1},{13,5},{2,10},{6,14},... | collective-permute-start | bytes 393224 | tf_op jit(solution)/shard_map/ppermute | solution.py:45
  29.3 1.6 %collective-permute-start.8 = (bf16[256,1792]{1,0:T(8,128)(2,1)S(1)}, bf16[256,1792]{1,0:T(8,128)(2,1)S(1)}, u32[]{:S(2)}, u32[]{:S(2)}) collective-permute-start(bf16[256,1792]{1,0:T(8,128)(2,1)S(1)} %shard_map.88.refs_3_.refs_0_), channel_id=1, source_target_pairs={{0,2},{2,0},{1,3},{3,1},{4,6},{6,4},{5,7},{7,5},{8,10},{10,8},{9,1... | collective-permute-start | bytes 2752520 | tf_op jit(solution)/shard_map/ppermute | solution.py:40
  30.9 3.4 %collective-permute-done.6.refs_1_ = bf16[128,512]{1,0:T(8,128)(2,1)S(1)} collective-permute-done((bf16[128,512]{1,0:T(8,128)(2,1)S(1)}, bf16[128,512]{1,0:T(8,128)(2,1)S(1)}, u32[]{:S(2)}, u32[]{:S(2)}) %collective-permute-start.6) | collective-permute-done | bytes 131104 | tf_op jit(solution)/shard_map/ppermute | solution.py:45
  34.2 0.7 collective-permute-start.10
  35.0 5.7 %collective-permute-done.10.refs_1_ = bf16[128,1024]{1,0:T(8,128)(2,1)S(1)} collective-permute-done((bf16[128,1024]{1,0:T(8,128)(2,1)S(1)}, bf16[128,1024]{1,0:T(8,128)(2,1)S(1)}, u32[]{:S(2)}, u32[]{:S(2)}) %collective-permute-start.10) | collective-permute-done | bytes 262176 | tf_op jit(solution)/shard_map/ppermute | solution.py:45
  40.8 1.4 collective-permute-start.9
  42.2 2.1 %collective-permute-start.7 = (bf16[128,512]{1,0:T(8,128)(2,1)S(1)}, bf16[128,512]{1,0:T(8,128)(2,1)S(1)}, u32[]{:S(2)}, u32[]{:S(2)}) collective-permute-start(bf16[128,512]{1,0:T(8,128)(2,1)S(1)} %shard_map.92.refs_0_), channel_id=1, source_target_pairs={{0,8},{4,12},{8,0},{12,4},{1,9},{5,13},{9,1},{13,5},{2,10},{6,14},... | collective-permute-start | bytes 393224 | tf_op jit(solution)/shard_map/ppermute | solution.py:45
  44.4 4.4 %shard_map.94.refs_2_.refs_6_.refs_0_ = bf16[384,1792]{1,0:T(8,128)(2,1)S(1)} custom-call(bf16[128,2048]{1,0:T(8,128)(2,1)S(1)} %shard_map.93.refs_0_.refs_2_.refs_4_.refs_5_, bf16[128,2048]{1,0:T(8,128)(2,1)S(1)} %collective-permute-done.11.refs_1_.refs_3_.refs_5_.refs_6_, bf16[128,2048]{1,0:T(8,128)(2,1)S(1)} %shard_map.93.refs_0_.refs_2_.refs_4_.refs_5_, ...), custom_call_target="tpu_custom_call" | custom-call | flops 345000000 | tf_op jit(solution)/shard_map/pallas_call | solution.py:102
  48.8 1.7 %collective-permute-start.17 = (bf16[384,1792]{1,0:T(8,128)(2,1)S(1)}, bf16[384,1792]{1,0:T(8,128)(2,1)S(1)}, u32[]{:S(2)}, u32[]{:S(2)}) collective-permute-start(bf16[384,1792]{1,0:T(8,128)(2,1)S(1)} %shard_map.94.refs_2_.refs_6_.refs_0_), channel_id=1, source_target_pairs={{0,2},{2,0},{1,3},{3,1},{4,6},{6,4},{5,7},{7,5},{8,10},{10,8},{9,1... | collective-permute-start | bytes 4128776 | tf_op jit(solution)/shard_map/ppermute | solution.py:40
  51.2 11.2 %collective-permute-done.9.refs_3_ = bf16[128,1792]{1,0:T(8,128)(2,1)S(1)} collective-permute-done((bf16[128,1792]{1,0:T(8,128)(2,1)S(1)}, bf16[128,1792]{1,0:T(8,128)(2,1)S(1)}, u32[]{:S(2)}, u32[]{:S(2)}) %collective-permute-start.9) | collective-permute-done | bytes 458784 | tf_op jit(solution)/shard_map/ppermute | solution.py:40
  62.4 5.8 %shard_map.97 = (bf16[1792,128]{1,0:T(8,128)(2,1)S(1)}, bf16[128,1792]{1,0:T(8,128)(2,1)S(1)}, bf16[128,1792]{1,0:T(8,128)(2,1)S(1)}, f32[64,2048]{1,0:T(8,128)S(1)}, bf16[64,2048]{1,0:T(8,128)(2,1)S(1)}) custom-call(bf16[256,1792]{1,0:T(8,128)(2,1)S(1)} %shard_map.88.refs_3_.refs_0_, bf16[128,1792]{1,0:T(8,128)(2,1)S(1)} %shard_map.89.refs_2_.refs_1_, ...), custom_call_target="tpu_custom_call" | custom-call | flops 69000003584 | tf_op jit(solution)/shard_map/pallas_call | solution.py:102
  68.3 2.1 %collective-permute-start.12 = (bf16[128,1024]{1,0:T(8,128)(2,1)S(1)}, bf16[128,1024]{1,0:T(8,128)(2,1)S(1)}, u32[]{:S(2)}, u32[]{:S(2)}) collective-permute-start(bf16[128,1024]{1,0:T(8,128)(2,1)S(1)} %shard_map.98.refs_0_), channel_id=1, source_target_pairs={{0,4},{4,0},{8,12},{12,8},{1,5},{5,1},{9,13},{13,9},{2,6},{6,2},{1... | collective-permute-start | bytes 786440 | tf_op jit(solution)/shard_map/ppermute | solution.py:45
  70.4 4.4 %collective-permute-done.12.refs_1_ = bf16[128,1024]{1,0:T(8,128)(2,1)S(1)} collective-permute-done((bf16[128,1024]{1,0:T(8,128)(2,1)S(1)}, bf16[128,1024]{1,0:T(8,128)(2,1)S(1)}, u32[]{:S(2)}, u32[]{:S(2)}) %collective-permute-start.12) | collective-permute-done | bytes 262176 | tf_op jit(solution)/shard_map/ppermute | solution.py:45
  75.4 1.8 %collective-permute-done.14.refs_1_ = bf16[64,2048]{1,0:T(8,128)(2,1)S(1)} collective-permute-done((bf16[64,2048]{1,0:T(8,128)(2,1)S(1)}, bf16[64,2048]{1,0:T(8,128)(2,1)S(1)}, u32[]{:S(2)}, u32[]{:S(2)}) %collective-permute-start.14) | collective-permute-done | bytes 262176 | tf_op jit(solution)/shard_map/ppermute | solution.py:40
  77.2 2.1 %collective-permute-start.18 = (bf16[64,1024]{1,0:T(8,128)(2,1)S(1)}, bf16[64,1024]{1,0:T(8,128)(2,1)S(1)}, u32[]{:S(2)}, u32[]{:S(2)}) collective-permute-start(bf16[64,1024]{1,0:T(8,128)(2,1)S(1)} %get-tuple-element.48), channel_id=1, source_target_pairs={{0,4},{4,0},{8,12},{12,8},{1,5},{5,1},{9,13},{13,9},{2,6},{6,2},{1... | collective-permute-start | bytes 393224 | tf_op jit(solution)/shard_map/ppermute | solution.py:45
  79.3 3.8 %collective-permute-done.18.refs_1_ = bf16[64,1024]{1,0:T(8,128)(2,1)S(1)} collective-permute-done((bf16[64,1024]{1,0:T(8,128)(2,1)S(1)}, bf16[64,1024]{1,0:T(8,128)(2,1)S(1)}, u32[]{:S(2)}, u32[]{:S(2)}) %collective-permute-start.18) | collective-permute-done | bytes 131104 | tf_op jit(solution)/shard_map/ppermute | solution.py:45
  83.1 2.6 %shard_map.101.refs_9_.refs_0_ = bf16[384,1024]{1,0:T(8,128)(2,1)S(1)} custom-call(bf16[128,2048]{1,0:T(8,128)(2,1)S(1)} %shard_map.99.refs_0_.refs_2_.refs_4_.refs_7_, bf16[128,2048]{1,0:T(8,128)(2,1)S(1)} %collective-permute-done.13.refs_1_.refs_3_.refs_5_.refs_8_, bf16[128,2048]{1,0:T(8,128)(2,1)S(1)} %shard_map.99.refs_0_.refs_2_.refs_4_.refs_7_, ...), custom_call_target="tpu_custom_call" | custom-call | flops 345000000 | tf_op jit(solution)/shard_map/pallas_call | solution.py:102
  85.7 1.6 %collective-permute-start.16 = (bf16[384,1024]{1,0:T(8,128)(2,1)S(1)}, bf16[384,1024]{1,0:T(8,128)(2,1)S(1)}, u32[]{:S(2)}, u32[]{:S(2)}) collective-permute-start(bf16[384,1024]{1,0:T(8,128)(2,1)S(1)} %shard_map.101.refs_9_.refs_0_), channel_id=1, source_target_pairs={{0,2},{2,0},{1,3},{3,1},{4,6},{6,4},{5,7},{7,5},{8,10},{10,8},{9,1... | collective-permute-start | bytes 2359304 | tf_op jit(solution)/shard_map/ppermute | solution.py:40
  87.4 2.0 %shard_map.102.refs_2_.refs_4_.refs_0_ = bf16[384,768]{1,0:T(8,128)(2,1)S(1)} custom-call(bf16[128,2048]{1,0:T(8,128)(2,1)S(1)} %shard_map.99.refs_0_.refs_2_.refs_4_.refs_7_, bf16[128,2048]{1,0:T(8,128)(2,1)S(1)} %collective-permute-done.13.refs_1_.refs_3_.refs_5_.refs_8_, bf16[128,2048]{1,0:T(8,128)(2,1)S(1)} %shard_map.99.refs_0_.refs_2_.refs_4_.refs_7_, ...), custom_call_target="tpu_custom_call" | custom-call | flops 345000000 | tf_op jit(solution)/shard_map/pallas_call | solution.py:102
  90.0 5.8 %shard_map.105 = (bf16[1792,128]{1,0:T(8,128)(2,1)S(1)}, bf16[128,1792]{1,0:T(8,128)(2,1)S(1)}, bf16[128,1792]{1,0:T(8,128)(2,1)S(1)}, f32[64,2048]{1,0:T(8,128)S(1)}, bf16[64,2048]{1,0:T(8,128)(2,1)S(1)}) custom-call(bf16[384,1792]{1,0:T(8,128)(2,1)S(1)} %shard_map.94.refs_2_.refs_6_.refs_0_, bf16[384,1792]{1,0:T(8,128)(2,1)S(1)} %collective-permute-done.17.refs_1_, ...), custom_call_target="tpu_custom_call" | custom-call | flops 69000003584 | tf_op jit(solution)/shard_map/pallas_call | solution.py:102
  95.9 1.0 collective-permute-start.19
  96.9 5.8 %collective-permute-done.19.refs_1_ = bf16[64,512]{1,0:T(8,128)(2,1)S(1)} collective-permute-done((bf16[64,512]{1,0:T(8,128)(2,1)S(1)}, bf16[64,512]{1,0:T(8,128)(2,1)S(1)}, u32[]{:S(2)}, u32[]{:S(2)}) %collective-permute-start.19) | collective-permute-done | bytes 65568 | tf_op jit(solution)/shard_map/ppermute | solution.py:45
  102.7 1.1 collective-permute-start.15
  103.8 3.0 %collective-permute-done.16.refs_1_ = bf16[384,1024]{1,0:T(8,128)(2,1)S(1)} collective-permute-done((bf16[384,1024]{1,0:T(8,128)(2,1)S(1)}, bf16[384,1024]{1,0:T(8,128)(2,1)S(1)}, u32[]{:S(2)}, u32[]{:S(2)}) %collective-permute-start.16) | collective-permute-done | bytes 786464 | tf_op jit(solution)/shard_map/ppermute | solution.py:40
  106.9 3.4 %shard_map.107 = (bf16[1024,128]{1,0:T(8,128)(2,1)S(1)}, bf16[128,1024]{1,0:T(8,128)(2,1)S(1)}, bf16[128,1024]{1,0:T(8,128)(2,1)S(1)}, f32[128,2048]{1,0:T(8,128)S(1)}) custom-call(bf16[384,1024]{1,0:T(8,128)(2,1)S(1)} %shard_map.101.refs_9_.refs_0_, bf16[384,1024]{1,0:T(8,128)(2,1)S(1)} %collective-permute-done.16.refs_1_, bf16[2048,1792]{1,0:T(8,128)(2,1)S(1)} %bitcast.1, ...), custom_call_target="tpu_custom_call" | custom-call | flops 1150000000 | tf_op jit(solution)/shard_map/pallas_call | solution.py:102
  110.3 1.5 %collective-permute-start.21 = (bf16[64,1024]{1,0:T(8,128)(2,1)S(1)}, bf16[64,1024]{1,0:T(8,128)(2,1)S(1)}, u32[]{:S(2)}, u32[]{:S(2)}) collective-permute-start(bf16[64,1024]{1,0:T(8,128)(2,1)S(1)} %get-tuple-element.60), channel_id=1, source_target_pairs={{0,4},{4,0},{8,12},{12,8},{1,5},{5,1},{9,13},{13,9},{2,6},{6,2},{1... | collective-permute-start | bytes 393224 | tf_op jit(solution)/shard_map/ppermute | solution.py:45
  111.8 4.2 %shard_map.110 = (bf16[1792,2048]{1,0:T(8,128)(2,1)}, bf16[16,128]{1,0:T(8,128)(2,1)S(1)}) custom-call(bf16[1792,128]{1,0:T(8,128)(2,1)S(1)} %get-tuple-element.62.refs_0_, bf16[1792,128]{1,0:T(8,128)(2,1)S(1)} %get-tuple-element.63.refs_1_, bf16[1024,128]{1,0:T(8,128)(2,1)S(1)} %get-tuple-element.64.refs_2_, bf16[64,2048]{1,0:T(8,128)(2,1)S(1)} %copy-done.7, ...), custom_call_target="tpu_custom_call" | custom-call | flops 3449999872 | tf_op jit(solution)/shard_map/pallas_call | solution.py:289
  116.4 6.4 %shard_map.111 = (bf16[2048,1792]{1,0:T(8,128)(2,1)}, bf16[2048,1792]{1,0:T(8,128)(2,1)}, bf16[16,128]{1,0:T(8,128)(2,1)S(1)}) custom-call(bf16[2048,128]{1,0:T(8,128)(2,1)S(1)} %shard_map.95.refs_7_.refs_0_, bf16[2048,128]{1,0:T(8,128)(2,1)S(1)} %shard_map.96.refs_8_.refs_1_, bf16[2048,128]{1,0:T(8,128)(2,1)S(1)} %shard_map.103.refs_5_.refs_2_, ...), custom_call_target="tpu_custom_call" | custom-call | flops 5750000128 | tf_op jit(solution)/shard_map/pallas_call | solution.py:289
  122.8 2.6 %shard_map.113 = (bf16[768,128]{1,0:T(8,128)(2,1)S(1)}, bf16[128,768]{1,0:T(8,128)(2,1)S(1)}, bf16[128,768]{1,0:T(8,128)(2,1)S(1)}, f32[64,2048]{1,0:T(8,128)S(1)}, bf16[64,2048]{1,0:T(8,128)(2,1)S(1)}) custom-call(bf16[384,768]{1,0:T(8,128)(2,1)S(1)} %shard_map.102.refs_2_.refs_4_.refs_0_, bf16[384,768]{1,0:T(8,128)(2,1)S(1)} %collective-permute-done.15.refs_1_, ...), custom_call_target="tpu_custom_call" | custom-call | flops 1150000000 | tf_op jit(solution)/shard_map/pallas_call | solution.py:102
  125.5 1.5 %collective-permute-done.23.refs_1_ = bf16[64,2048]{1,0:T(8,128)(2,1)S(1)} collective-permute-done((bf16[64,2048]{1,0:T(8,128)(2,1)S(1)}, bf16[64,2048]{1,0:T(8,128)(2,1)S(1)}, u32[]{:S(2)}, u32[]{:S(2)}) %collective-permute-start.23) | collective-permute-done | bytes 262176 | tf_op jit(solution)/shard_map/ppermute | solution.py:40
  127.1 1.3 collective-permute-start.24
  128.4 3.6 %shard_map.117 = (bf16[1792,2048]{1,0:T(8,128)(2,1)}, bf16[16,128]{1,0:T(8,128)(2,1)S(1)}) custom-call(bf16[1792,128]{1,0:T(8,128)(2,1)S(1)} %get-tuple-element.62.refs_0_, bf16[1792,128]{1,0:T(8,128)(2,1)S(1)} %get-tuple-element.63.refs_1_, bf16[768,128]{1,0:T(8,128)(2,1)S(1)} %get-tuple-element.78.refs_2_, ...), custom_call_target="tpu_custom_call", output_to_operand_aliasing={{0}: (9, {})} | custom-call | flops 3449999872 | tf_op jit(solution)/shard_map/pallas_call | solution.py:289
  132.7 2.7 %collective-permute-start.25 = (bf16[64,512]{1,0:T(8,128)(2,1)S(1)}, bf16[64,512]{1,0:T(8,128)(2,1)S(1)}, u32[]{:S(2)}, u32[]{:S(2)}) collective-permute-start(bf16[64,512]{1,0:T(8,128)(2,1)S(1)} %get-tuple-element.73), channel_id=1, source_target_pairs={{0,8},{4,12},{8,0},{12,4},{1,9},{5,13},{9,1},{13,5},{2,10},{6,14},... | collective-permute-start | bytes 196616 | tf_op jit(solution)/shard_map/ppermute | solution.py:45
  135.4 5.1 %shard_map.118 = (bf16[2048,1792]{1,0:T(8,128)(2,1)}, bf16[2048,1792]{1,0:T(8,128)(2,1)}, bf16[16,128]{1,0:T(8,128)(2,1)}) custom-call(bf16[2048,128]{1,0:T(8,128)(2,1)S(1)} %shard_map.95.refs_7_.refs_0_, bf16[2048,128]{1,0:T(8,128)(2,1)S(1)} %shard_map.96.refs_8_.refs_1_, ...), custom_call_target="tpu_custom_call", output_to_operand_aliasing={{0}: (9, {}), {1}: (10, {})} | custom-call | flops 5750000128 | tf_op jit(solution)/shard_map/pallas_call | solution.py:289
  140.5 0.7 shard_map.116
  (76 shorter events, 4.5 us)
Async XLA Ops:
  1.5 7.7 %collective-permute-start.3 = (bf16[64,512]{1,0:T(8,128)(2,1)S(1)}, bf16[64,512]{1,0:T(8,128)(2,1)S(1)}, u32[]{:S(2)}, u32[]{:S(2)}) collective-permute-start(bf16[64,512]{1,0:T(8,128)(2,1)S(1)} %slice.7.refs_0_), channel_id=1, source_target_pairs={{0,8},{4,12},{8,0},{12,4},{1,9},{5,13},{9,1},{13,5},{2,10},{6,14},... | collective-permute-start | bytes 196616 | tf_op jit(solution)/shard_map/ppermute | solution.py:45
  6.4 5.5 %collective-permute-start = (bf16[64,512]{1,0:T(8,128)(2,1)S(1)}, bf16[64,512]{1,0:T(8,128)(2,1)S(1)}, u32[]{:S(2)}, u32[]{:S(2)}) collective-permute-start(bf16[64,512]{1,0:T(8,128)(2,1)S(1)} %slice.6.refs_0_), channel_id=1, source_target_pairs={{0,8},{4,12},{8,0},{12,4},{1,9},{5,13},{9,1},{13,5},{2,10},{6,14},... | collective-permute-start | bytes 196616 | tf_op jit(solution)/shard_map/ppermute | solution.py:45
  9.2 6.5 %collective-permute-start.4 = (bf16[64,1024]{1,0:T(8,128)(2,1)S(1)}, bf16[64,1024]{1,0:T(8,128)(2,1)S(1)}, u32[]{:S(2)}, u32[]{:S(2)}) collective-permute-start(bf16[64,1024]{1,0:T(8,128)(2,1)S(1)} %shard_map.86.refs_0_), channel_id=1, source_target_pairs={{0,4},{4,0},{8,12},{12,8},{1,5},{5,1},{9,13},{13,9},{2,6},{6,2},{1... | collective-permute-start | bytes 393224 | tf_op jit(solution)/shard_map/ppermute | solution.py:45
  11.8 5.8 %collective-permute-start.1 = (bf16[64,1024]{1,0:T(8,128)(2,1)S(1)}, bf16[64,1024]{1,0:T(8,128)(2,1)S(1)}, u32[]{:S(2)}, u32[]{:S(2)}) collective-permute-start(bf16[64,1024]{1,0:T(8,128)(2,1)S(1)} %shard_map.84.refs_0_), channel_id=1, source_target_pairs={{0,4},{4,0},{8,12},{12,8},{1,5},{5,1},{9,13},{13,9},{2,6},{6,2},{1... | collective-permute-start | bytes 393224 | tf_op jit(solution)/shard_map/ppermute | solution.py:45
  15.7 2.2 %slice-start = ((s8[7340032]{0:T(1024)(128)(4,1)}), s8[4194304]{0:T(1024)(128)(4,1)S(1)}, s32[]{:S(2)}) async-start(s8[7340032]{0:T(1024)(128)(4,1)} %bitcast), calls=%async_computation | async-start | bytes 8388608
  15.7 3.6 %slice-start.2 = ((s8[7340032]{0:T(1024)(128)(4,1)}), s8[4194304]{0:T(1024)(128)(4,1)S(1)}, s32[]{:S(2)}) async-start(s8[7340032]{0:T(1024)(128)(4,1)} %bitcast.2), calls=%async_computation.2 | async-start | bytes 8388608
  15.7 4.4 %slice-start.1 = ((s8[7340032]{0:T(1024)(128)(4,1)}), s8[3145728]{0:T(1024)(128)(4,1)S(1)}, s32[]{:S(2)}) async-start(s8[7340032]{0:T(1024)(128)(4,1)} %bitcast), calls=%async_computation.1 | async-start | bytes 6291456
  15.7 5.3 %slice-start.3 = ((s8[7340032]{0:T(1024)(128)(4,1)}), s8[3145728]{0:T(1024)(128)(4,1)S(1)}, s32[]{:S(2)}) async-start(s8[7340032]{0:T(1024)(128)(4,1)} %bitcast.2), calls=%async_computation.3 | async-start | bytes 6291456
  15.8 2.0 %collective-permute-start.5 = (bf16[64,2048]{1,0:T(8,128)(2,1)S(1)}, bf16[64,2048]{1,0:T(8,128)(2,1)S(1)}, u32[]{:S(2)}, u32[]{:S(2)}) collective-permute-start(bf16[64,2048]{1,0:T(8,128)(2,1)S(1)} %shard_map.87.refs_0_.refs_2_), channel_id=1, source_target_pairs={{0,1},{1,0},{2,3},{3,2},{4,5},{5,4},{6,7},{7,6},{8,9},{9,8},{10,11... | collective-permute-start | bytes 786440 | tf_op jit(solution)/shard_map/ppermute | solution.py:40
  17.7 5.5 %slice-start.4 = ((s8[7340032]{0:T(1024)(128)(4,1)}), s8[4194304]{0:T(1024)(128)(4,1)S(1)}, s32[]{:S(2)}) async-start(s8[7340032]{0:T(1024)(128)(4,1)} %bitcast.4), calls=%async_computation.4 | async-start | bytes 8388608
  17.7 5.5 %copy-start.6 = (bf16[64,2048]{1,0:T(8,128)(2,1)}, bf16[64,2048]{1,0:T(8,128)(2,1)S(1)}, u32[]{:S(2)}) copy-start(bf16[64,2048]{1,0:T(8,128)(2,1)S(1)} %shard_map.85.refs_0_.refs_3_) | copy-start | bytes 786436
  17.7 5.6 %slice-start.5 = ((s8[7340032]{0:T(1024)(128)(4,1)}), s8[3145728]{0:T(1024)(128)(4,1)S(1)}, s32[]{:S(2)}) async-start(s8[7340032]{0:T(1024)(128)(4,1)} %bitcast.4), calls=%async_computation.5 | async-start | bytes 6291456
  17.7 5.4 %collective-permute-start.2 = (bf16[64,2048]{1,0:T(8,128)(2,1)S(1)}, bf16[64,2048]{1,0:T(8,128)(2,1)S(1)}, u32[]{:S(2)}, u32[]{:S(2)}) collective-permute-start(bf16[64,2048]{1,0:T(8,128)(2,1)S(1)} %shard_map.85.refs_0_.refs_3_), channel_id=1, source_target_pairs={{0,1},{1,0},{2,3},{3,2},{4,5},{5,4},{6,7},{7,6},{8,9},{9,8},{10,11... | collective-permute-start | bytes 786440 | tf_op jit(solution)/shard_map/ppermute | solution.py:40
  23.1 2.7 %copy-start.4 = (bf16[192,512]{1,0:T(8,128)(2,1)S(1)}, bf16[192,512]{1,0:T(8,128)(2,1)}, u32[]{:S(2)}) copy-start(bf16[192,512]{1,0:T(8,128)(2,1)} %refs_0_.3) | copy-start | bytes 589828
  23.1 2.7 %copy-start.5 = (bf16[192,512]{1,0:T(8,128)(2,1)S(1)}, bf16[192,512]{1,0:T(8,128)(2,1)}, u32[]{:S(2)}) copy-start(bf16[192,512]{1,0:T(8,128)(2,1)} %refs_1_.3) | copy-start | bytes 589828
  23.3 11.7 %copy-start.8 = (bf16[64,2048]{1,0:T(8,128)(2,1)}, bf16[64,2048]{1,0:T(8,128)(2,1)S(1)}, u32[]{:S(2)}) copy-start(bf16[64,2048]{1,0:T(8,128)(2,1)S(1)} %collective-permute-done.2.refs_1_.refs_4_) | copy-start | bytes 786436
  25.9 8.4 %collective-permute-start.6 = (bf16[128,512]{1,0:T(8,128)(2,1)S(1)}, bf16[128,512]{1,0:T(8,128)(2,1)S(1)}, u32[]{:S(2)}, u32[]{:S(2)}) collective-permute-start(bf16[128,512]{1,0:T(8,128)(2,1)S(1)} %shard_map.90.refs_0_), channel_id=1, source_target_pairs={{0,8},{4,12},{8,0},{12,4},{1,9},{5,13},{9,1},{13,5},{2,10},{6,14},... | collective-permute-start | bytes 393224 | tf_op jit(solution)/shard_map/ppermute | solution.py:45
  29.3 33.1 %collective-permute-start.8 = (bf16[256,1792]{1,0:T(8,128)(2,1)S(1)}, bf16[256,1792]{1,0:T(8,128)(2,1)S(1)}, u32[]{:S(2)}, u32[]{:S(2)}) collective-permute-start(bf16[256,1792]{1,0:T(8,128)(2,1)S(1)} %shard_map.88.refs_3_.refs_0_), channel_id=1, source_target_pairs={{0,2},{2,0},{1,3},{3,1},{4,6},{6,4},{5,7},{7,5},{8,10},{10,8},{9,1... | collective-permute-start | bytes 2752520 | tf_op jit(solution)/shard_map/ppermute | solution.py:40
  34.2 6.4 %collective-permute-start.10 = (bf16[128,1024]{1,0:T(8,128)(2,1)S(1)}, bf16[128,1024]{1,0:T(8,128)(2,1)S(1)}, u32[]{:S(2)}, u32[]{:S(2)}) collective-permute-start(bf16[128,1024]{1,0:T(8,128)(2,1)S(1)} %shard_map.91.refs_2_.refs_0_), channel_id=1, source_target_pairs={{0,4},{4,0},{8,12},{12,8},{1,5},{5,1},{9,13},{13,9},{2,6},{6,2},{1... | collective-permute-start | bytes 786440 | tf_op jit(solution)/shard_map/ppermute | solution.py:45
  40.7 10.1 %copy-start = (bf16[128,2048]{1,0:T(8,128)(2,1)}, bf16[128,2048]{1,0:T(8,128)(2,1)S(1)}, u32[]{:S(2)}) copy-start(bf16[128,2048]{1,0:T(8,128)(2,1)S(1)} %shard_map.93.refs_0_.refs_2_.refs_4_.refs_5_) | copy-start | bytes 1572868
  40.7 3.6 %collective-permute-start.11 = (bf16[128,2048]{1,0:T(8,128)(2,1)S(1)}, bf16[128,2048]{1,0:T(8,128)(2,1)S(1)}, u32[]{:S(2)}, u32[]{:S(2)}) collective-permute-start(bf16[128,2048]{1,0:T(8,128)(2,1)S(1)} %shard_map.93.refs_0_.refs_2_.refs_4_.refs_5_), channel_id=1, source_target_pairs={{0,1},{1,0},{2,3},{3,2},{4,5},{5,4},{6,7},{7,6},{8,9},{9,8},{10,11... | collective-permute-start | bytes 1572872 | tf_op jit(solution)/shard_map/ppermute | solution.py:40
  40.8 21.6 %collective-permute-start.9 = (bf16[128,1792]{1,0:T(8,128)(2,1)S(1)}, bf16[128,1792]{1,0:T(8,128)(2,1)S(1)}, u32[]{:S(2)}, u32[]{:S(2)}) collective-permute-start(bf16[128,1792]{1,0:T(8,128)(2,1)S(1)} %shard_map.89.refs_2_.refs_1_), channel_id=1, source_target_pairs={{0,2},{2,0},{1,3},{3,1},{4,6},{6,4},{5,7},{7,5},{8,10},{10,8},{9,1... | collective-permute-start | bytes 1376264 | tf_op jit(solution)/shard_map/ppermute | solution.py:40
  42.2 26.0 %collective-permute-start.7 = (bf16[128,512]{1,0:T(8,128)(2,1)S(1)}, bf16[128,512]{1,0:T(8,128)(2,1)S(1)}, u32[]{:S(2)}, u32[]{:S(2)}) collective-permute-start(bf16[128,512]{1,0:T(8,128)(2,1)S(1)} %shard_map.92.refs_0_), channel_id=1, source_target_pairs={{0,8},{4,12},{8,0},{12,4},{1,9},{5,13},{9,1},{13,5},{2,10},{6,14},... | collective-permute-start | bytes 393224 | tf_op jit(solution)/shard_map/ppermute | solution.py:45
  44.4 6.5 %copy-start.2 = (bf16[128,2048]{1,0:T(8,128)(2,1)}, bf16[128,2048]{1,0:T(8,128)(2,1)S(1)}, u32[]{:S(2)}) copy-start(bf16[128,2048]{1,0:T(8,128)(2,1)S(1)} %collective-permute-done.11.refs_1_.refs_3_.refs_5_.refs_6_) | copy-start | bytes 1572868
  48.8 41.2 %collective-permute-start.17 = (bf16[384,1792]{1,0:T(8,128)(2,1)S(1)}, bf16[384,1792]{1,0:T(8,128)(2,1)S(1)}, u32[]{:S(2)}, u32[]{:S(2)}) collective-permute-start(bf16[384,1792]{1,0:T(8,128)(2,1)S(1)} %shard_map.94.refs_2_.refs_6_.refs_0_), channel_id=1, source_target_pairs={{0,2},{2,0},{1,3},{3,1},{4,6},{6,4},{5,7},{7,5},{8,10},{10,8},{9,1... | collective-permute-start | bytes 4128776 | tf_op jit(solution)/shard_map/ppermute | solution.py:40
  68.3 6.5 %collective-permute-start.12 = (bf16[128,1024]{1,0:T(8,128)(2,1)S(1)}, bf16[128,1024]{1,0:T(8,128)(2,1)S(1)}, u32[]{:S(2)}, u32[]{:S(2)}) collective-permute-start(bf16[128,1024]{1,0:T(8,128)(2,1)S(1)} %shard_map.98.refs_0_), channel_id=1, source_target_pairs={{0,4},{4,0},{8,12},{12,8},{1,5},{5,1},{9,13},{13,9},{2,6},{6,2},{1... | collective-permute-start | bytes 786440 | tf_op jit(solution)/shard_map/ppermute | solution.py:45
  74.8 8.3 %collective-permute-start.13 = (bf16[128,2048]{1,0:T(8,128)(2,1)S(1)}, bf16[128,2048]{1,0:T(8,128)(2,1)S(1)}, u32[]{:S(2)}, u32[]{:S(2)}) collective-permute-start(bf16[128,2048]{1,0:T(8,128)(2,1)S(1)} %shard_map.99.refs_0_.refs_2_.refs_4_.refs_7_), channel_id=1, source_target_pairs={{0,1},{1,0},{2,3},{3,2},{4,5},{5,4},{6,7},{7,6},{8,9},{9,8},{10,11... | collective-permute-start | bytes 1572872 | tf_op jit(solution)/shard_map/ppermute | solution.py:40
  74.9 2.3 %collective-permute-start.14 = (bf16[64,2048]{1,0:T(8,128)(2,1)S(1)}, bf16[64,2048]{1,0:T(8,128)(2,1)S(1)}, u32[]{:S(2)}, u32[]{:S(2)}) collective-permute-start(bf16[64,2048]{1,0:T(8,128)(2,1)S(1)} %get-tuple-element.46), channel_id=1, source_target_pairs={{0,1},{1,0},{2,3},{3,2},{4,5},{5,4},{6,7},{7,6},{8,9},{9,8},{10,11... | collective-permute-start | bytes 786440 | tf_op jit(solution)/shard_map/ppermute | solution.py:40
  77.2 5.9 %collective-permute-start.18 = (bf16[64,1024]{1,0:T(8,128)(2,1)S(1)}, bf16[64,1024]{1,0:T(8,128)(2,1)S(1)}, u32[]{:S(2)}, u32[]{:S(2)}) collective-permute-start(bf16[64,1024]{1,0:T(8,128)(2,1)S(1)} %get-tuple-element.48), channel_id=1, source_target_pairs={{0,4},{4,0},{8,12},{12,8},{1,5},{5,1},{9,13},{13,9},{2,6},{6,2},{1... | collective-permute-start | bytes 393224 | tf_op jit(solution)/shard_map/ppermute | solution.py:45
  85.7 21.1 %collective-permute-start.16 = (bf16[384,1024]{1,0:T(8,128)(2,1)S(1)}, bf16[384,1024]{1,0:T(8,128)(2,1)S(1)}, u32[]{:S(2)}, u32[]{:S(2)}) collective-permute-start(bf16[384,1024]{1,0:T(8,128)(2,1)S(1)} %shard_map.101.refs_9_.refs_0_), channel_id=1, source_target_pairs={{0,2},{2,0},{1,3},{3,1},{4,6},{6,4},{5,7},{7,5},{8,10},{10,8},{9,1... | collective-permute-start | bytes 2359304 | tf_op jit(solution)/shard_map/ppermute | solution.py:40
  95.8 14.5 %collective-permute-start.20 = (bf16[64,2048]{1,0:T(8,128)(2,1)S(1)}, bf16[64,2048]{1,0:T(8,128)(2,1)S(1)}, u32[]{:S(2)}, u32[]{:S(2)}) collective-permute-start(bf16[64,2048]{1,0:T(8,128)(2,1)S(1)} %get-tuple-element.58), channel_id=1, source_target_pairs={{0,1},{1,0},{2,3},{3,2},{4,5},{5,4},{6,7},{7,6},{8,9},{9,8},{10,11... | collective-permute-start | bytes 786440 | tf_op jit(solution)/shard_map/ppermute | solution.py:40
  95.9 6.8 %collective-permute-start.19 = (bf16[64,512]{1,0:T(8,128)(2,1)S(1)}, bf16[64,512]{1,0:T(8,128)(2,1)S(1)}, u32[]{:S(2)}, u32[]{:S(2)}) collective-permute-start(bf16[64,512]{1,0:T(8,128)(2,1)S(1)} %get-tuple-element.51), channel_id=1, source_target_pairs={{0,8},{4,12},{8,0},{12,4},{1,9},{5,13},{9,1},{13,5},{2,10},{6,14},... | collective-permute-start | bytes 196616 | tf_op jit(solution)/shard_map/ppermute | solution.py:45
  102.7 20.1 %collective-permute-start.15 = (bf16[384,768]{1,0:T(8,128)(2,1)S(1)}, bf16[384,768]{1,0:T(8,128)(2,1)S(1)}, u32[]{:S(2)}, u32[]{:S(2)}) collective-permute-start(bf16[384,768]{1,0:T(8,128)(2,1)S(1)} %shard_map.102.refs_2_.refs_4_.refs_0_), channel_id=1, source_target_pairs={{0,2},{2,0},{1,3},{3,1},{4,6},{6,4},{5,7},{7,5},{8,10},{10,8},{9,1... | collective-permute-start | bytes 1769480 | tf_op jit(solution)/shard_map/ppermute | solution.py:40
  106.8 5.0 %copy-start.1 = (bf16[128,2048]{1,0:T(8,128)(2,1)S(1)}, bf16[128,2048]{1,0:T(8,128)(2,1)}, u32[]{:S(2)}) copy-start(bf16[128,2048]{1,0:T(8,128)(2,1)} %copy-done) | copy-start | bytes 1572868
  106.8 5.0 %copy-start.3 = (bf16[128,2048]{1,0:T(8,128)(2,1)S(1)}, bf16[128,2048]{1,0:T(8,128)(2,1)}, u32[]{:S(2)}) copy-start(bf16[128,2048]{1,0:T(8,128)(2,1)} %copy-done.2) | copy-start | bytes 1572868
  106.9 5.0 %copy-start.7 = (bf16[64,2048]{1,0:T(8,128)(2,1)S(1)}, bf16[64,2048]{1,0:T(8,128)(2,1)}, u32[]{:S(2)}) copy-start(bf16[64,2048]{1,0:T(8,128)(2,1)} %copy-done.6) | copy-start | bytes 786436
  106.9 5.0 %copy-start.9 = (bf16[64,2048]{1,0:T(8,128)(2,1)S(1)}, bf16[64,2048]{1,0:T(8,128)(2,1)}, u32[]{:S(2)}) copy-start(bf16[64,2048]{1,0:T(8,128)(2,1)} %copy-done.8) | copy-start | bytes 786436
  110.3 5.8 %collective-permute-start.21 = (bf16[64,1024]{1,0:T(8,128)(2,1)S(1)}, bf16[64,1024]{1,0:T(8,128)(2,1)S(1)}, u32[]{:S(2)}, u32[]{:S(2)}) collective-permute-start(bf16[64,1024]{1,0:T(8,128)(2,1)S(1)} %get-tuple-element.60), channel_id=1, source_target_pairs={{0,4},{4,0},{8,12},{12,8},{1,5},{5,1},{9,13},{13,9},{2,6},{6,2},{1... | collective-permute-start | bytes 393224 | tf_op jit(solution)/shard_map/ppermute | solution.py:45
  116.1 6.7 %collective-permute-start.22 = (bf16[64,512]{1,0:T(8,128)(2,1)S(1)}, bf16[64,512]{1,0:T(8,128)(2,1)S(1)}, u32[]{:S(2)}, u32[]{:S(2)}) collective-permute-start(bf16[64,512]{1,0:T(8,128)(2,1)S(1)} %get-tuple-element.67), channel_id=1, source_target_pairs={{0,8},{4,12},{8,0},{12,4},{1,9},{5,13},{9,1},{13,5},{2,10},{6,14},... | collective-permute-start | bytes 196616 | tf_op jit(solution)/shard_map/ppermute | solution.py:45
  125.4 1.6 %collective-permute-start.23 = (bf16[64,2048]{1,0:T(8,128)(2,1)S(1)}, bf16[64,2048]{1,0:T(8,128)(2,1)S(1)}, u32[]{:S(2)}, u32[]{:S(2)}) collective-permute-start(bf16[64,2048]{1,0:T(8,128)(2,1)S(1)} %get-tuple-element.69), channel_id=1, source_target_pairs={{0,1},{1,0},{2,3},{3,2},{4,5},{5,4},{6,7},{7,6},{8,9},{9,8},{10,11... | collective-permute-start | bytes 786440 | tf_op jit(solution)/shard_map/ppermute | solution.py:40
  127.1 5.6 %collective-permute-start.24 = (bf16[64,1024]{1,0:T(8,128)(2,1)S(1)}, bf16[64,1024]{1,0:T(8,128)(2,1)S(1)}, u32[]{:S(2)}, u32[]{:S(2)}) collective-permute-start(bf16[64,1024]{1,0:T(8,128)(2,1)S(1)} %get-tuple-element.71), channel_id=1, source_target_pairs={{0,4},{4,0},{8,12},{12,8},{1,5},{5,1},{9,13},{13,9},{2,6},{6,2},{1... | collective-permute-start | bytes 393224 | tf_op jit(solution)/shard_map/ppermute | solution.py:45
  132.7 7.8 %collective-permute-start.25 = (bf16[64,512]{1,0:T(8,128)(2,1)S(1)}, bf16[64,512]{1,0:T(8,128)(2,1)S(1)}, u32[]{:S(2)}, u32[]{:S(2)}) collective-permute-start(bf16[64,512]{1,0:T(8,128)(2,1)S(1)} %get-tuple-element.73), channel_id=1, source_target_pairs={{0,8},{4,12},{8,0},{12,4},{1,9},{5,13},{9,1},{13,5},{2,10},{6,14},... | collective-permute-start | bytes 196616 | tf_op jit(solution)/shard_map/ppermute | solution.py:45

commit v8 on v7

--- a/solution.py
+++ b/solution.py
@@ -92,57 +92,79 @@
     return pl.CostEstimate(flops=int(cost * 1.15e9), bytes_accessed=0, transcendentals=0)
 
 
-def local(kernel, outs, args, after=(), limit=12, scratch=(), out_specs=None, resident=(), cost=0.1):
-    waits = len(resident) + len(after)
-
+def local(kernel, outs, args, after=(), limit=12, scratch=(), out_specs=None, cost=0.1):
     def body(*refs):
-        kernel(refs[: len(args)], refs[len(args) + waits :])
+        kernel(refs[: len(args)], refs[len(args) + len(after) :])
 
     shapes = [jax.ShapeDtypeStruct(shape, dtype) for shape, dtype in outs]
     return pl.pallas_call(
         body,
         out_shape=shapes,
-        in_specs=[VMEM] * (len(args) + len(resident)) + [ANYWHERE] * len(after),
+        in_specs=[VMEM] * len(args) + [ANYWHERE] * len(after),
         out_specs=out_specs if out_specs else [VMEM] * len(outs),
         scratch_shapes=list(scratch),
         compiler_params=pltpu.CompilerParams(vmem_limit_bytes=limit * MIB),
         cost_estimate=declared(cost),
-    )(*args, *resident, *after)
+    )(*args, *after)
 
 
 def lanes(index, width):
     return pl.ds(pl.multiple_of(index * width, width), width)
 
 
-def cut_piece(acts, grad_out, lower, upper, after):
-    rows, width = upper - lower, acts.shape[1]
-
-    def kernel(ins, outs):
-        outs[0][:rows] = ins[0][lower:upper]
-        outs[0][rows:] = ins[1][lower:upper]
-
-    return local(kernel, [((2 * rows, width), acts.dtype)], (acts, grad_out), after, limit=1)[0]
-
-
-def pack(value, far, after=(), resident=(), cost=0.1):
+def cut_rows(acts, grad_out, wanted, after=(), cost=0.1):
+    width = acts.shape[1]
+    height = sum(rows for _, _, rows in wanted)
+
+    def kernel(ins, outs):
+        top = 0
+        for array, first, rows in wanted:
+            outs[0][top : top + rows] = ins[array][first : first + rows]
+            top += rows
+
+    return local(kernel, [((height, width), acts.dtype)], (acts, grad_out), after, 1, cost=cost)[0]
+
+
+def first_rows(value, rows):
+    shape = (rows, value.shape[1])
+
+    def kernel(source, out):
+        out[...] = source[...]
+
+    return pl.pallas_call(
+        kernel,
+        grid=(1,),
+        out_shape=jax.ShapeDtypeStruct(shape, value.dtype),
+        in_specs=[pl.BlockSpec(shape, lambda i: (0, 0))],
+        out_specs=VMEM,
+        compiler_params=pltpu.CompilerParams(vmem_limit_bytes=MIB),
+        cost_estimate=declared(20.0),
+    )(value)
+
+
+def pack(value, far, after=()):
     rows, width = value.shape
 
     def kernel(ins, outs):
         outs[0][:, :width] = ins[0][...]
         outs[0][:, width:] = ins[1][...]
 
-    return local(kernel, [((rows, 2 * width), value.dtype)], (value, far), after, 1, resident=resident, cost=cost)[0]
-
-
-def arrange(pair, near, resident=(), cost=0.1):
-    rows, width = pair.shape[0], pair.shape[1] // 2
+    return local(kernel, [((rows, 2 * width), value.dtype)], (value, far), after, 1)[0]
+
+
+def arrange(pair, near, heights):
+    width = pair.shape[1] // 2
 
     def kernel(ins, outs):
         me = lax.axis_index("hid")
-        for step, (source, at) in enumerate(((0, 0), (1, 0), (0, 1), (1, 1))):
-            outs[0][:, lanes(me ^ step, width)] = ins[source][:, at * width : (at + 1) * width]
-
-    return local(kernel, [((rows, 4 * width), pair.dtype)], (pair, near), (), 1, resident=resident, cost=cost)[0]
+        top = 0
+        for out, height in zip(outs, heights):
+            for step, (source, at) in enumerate(((0, 0), (1, 0), (0, 1), (1, 1))):
+                block = ins[source][top : top + height, at * width : (at + 1) * width]
+                out[:, lanes(me ^ step, width)] = block
+            top += height
+
+    return local(kernel, [((height, 4 * width), pair.dtype) for height in heights], (pair, near), (), 1)
 
 
 def over_blocks(width, step, body):
@@ -268,17 +290,21 @@
     return local(kernel, [(shape, jnp.bfloat16)], (mine, theirs, *earlier), limit=4, out_specs=specs)[0]
 
 
-def turned(own, theirs, first, rows, after=()):
-    features = own.shape[1]
+def joined(pieces, turn, after=()):
+    tokens, features = sum(p[2] for p in pieces), pieces[0][0].shape[1]
 
     def kernel(ins, outs):
         @pl.loop(0, features // 512)
         def _(j):
             at = lanes(j, 512)
-            both = jnp.concatenate([ref[first : first + rows, at] for ref in ins], axis=0)
-            outs[0][at, :] = both.T
-
-    return local(kernel, [((features, 2 * rows), own.dtype)], (own, theirs), after, limit=4)[0]
+            rows = jnp.concatenate([ins[i][p[1] : p[1] + p[2], at] for i, p in enumerate(pieces)], axis=0)
+            if turn:
+                outs[0][at, :] = rows.T
+            else:
+                outs[0][:, at] = rows
+
+    shape = (features, tokens) if turn else (tokens, features)
+    return local(kernel, [(shape, jnp.bfloat16)], [p[0] for p in pieces], after, limit=4)[0]
 
 
 def gradients(kernel, outs, arrays, old, grid, specs, scratch, after, cost):
@@ -303,11 +329,11 @@
     return pl.BlockSpec((pl.Element(rows), pl.Element(columns)), where)
 
 
-def column_grads(xs, gs, us, span, total, old, after=()):
-    arrays = [*xs, *(p[0] for p in (*gs, *us))]
-    count, lower, width = len(xs), span[0], span[1] - span[0]
-    tokens, features = sum(x.shape[1] for x in xs), xs[0].shape[0]
-    block = 512
+def column_grads(x, gs, us, span, total, old, after=()):
+    arrays = [x, *(p[0] for p in (*gs, *us))]
+    count, lower, width = len(gs), span[0], span[1] - span[0]
+    features, tokens = x.shape
+    block = 256
 
     def kernel(ins, refs):
         gate_out, up_out, token, g_all, u_all = refs
@@ -316,48 +342,43 @@
         @pl.when(step == 0)
         def _():
             token[...] = jnp.zeros_like(token)
-            for first, pieces, target in ((count, gs, g_all), (2 * count, us, u_all)):
+            for first, pieces, target in ((1, gs, g_all), (1 + count, us, u_all)):
                 top = 0
                 for i, (piece, column) in enumerate(pieces):
                     rows = piece.shape[0]
                     target[top : top + rows] = ins[first + i][:, column : column + width]
                     top += rows
 
-        at = lanes(step, block)
-        x = jnp.concatenate([ins[i][at, :] for i in range(count)], axis=1)
-        gate_out[...] = rows_by_cols(x, g_all[...]).astype(gate_out.dtype)
-        up_out[...] = rows_by_cols(x, u_all[...]).astype(up_out.dtype)
-
-    spec = placed(block, width, lambda i: (i * block, lower))
+        rows = ins[0][lanes(step, block), :]
+        gate_out[...] = rows_by_cols(rows, g_all[...]).astype(gate_out.dtype)
+        up_out[...] = rows_by_cols(rows, u_all[...]).astype(up_out.dtype)
+
+    spec = placed(block, width, lambda i: (pl.multiple_of(i * block, block), lower))
     scratch = [pltpu.VMEM((tokens, width), jnp.bfloat16)] * 2
     return gradients(kernel, [(features, total)] * 2, arrays, old, (features // block,), [spec, spec], scratch, after, 5.0)
 
 
-def row_grads(hs, ys, span, total, old, after=()):
-    arrays = [p[0] for p in (*hs, *ys)]
+def row_grads(hs, y, span, total, old, after=()):
+    arrays = [*(p[0] for p in hs), y]
     count, lower, width = len(hs), span[0], span[1] - span[0]
-    tokens, features = sum(p[0].shape[1] for p in hs), ys[0][0].shape[1]
-    block = 512
+    features = y.shape[1]
+    block = 256
 
     def kernel(ins, refs):
-        out, token, h_all = refs
+        out, token = refs
         step = pl.program_id(0)
 
         @pl.when(step == 0)
         def _():
             token[...] = jnp.zeros_like(token)
-            left = 0
-            for i, (piece, row) in enumerate(hs):
-                h_all[:, left : left + piece.shape[1]] = ins[i][row : row + width]
-                left += piece.shape[1]
-
-        at = lanes(step, block)
-        y = jnp.concatenate([ins[count + i][top : top + rows, at] for i, (_, top, rows) in enumerate(ys)], axis=0)
-        out[...] = rows_by_cols(h_all[...], y).astype(out.dtype)
-
-    spec = placed(width, block, lambda i: (lower, i * block))
-    scratch = [pltpu.VMEM((width, tokens), jnp.bfloat16)]
-    return gradients(kernel, [(total, features)], arrays, old, (features // block,), [spec], scratch, after, 3.0)
+
+        rows = []
+        for i, (_, row) in enumerate(hs):
+            rows.append(ins[i][pl.ds(pl.multiple_of(row + step * block, block), block), :])
+        out[...] = rows_by_cols(jnp.concatenate(rows, axis=1), ins[count][...]).astype(out.dtype)
+
+    spec = placed(block, features, lambda i: (pl.multiple_of(lower + i * block, block), 0))
+    return gradients(kernel, [(total, features)], arrays, old, (width // block,), [spec], [], after, 3.0)
 
 
 def piped(acts, grad_out, w_gate, w_up, w_down):
@@ -373,28 +394,23 @@
     whole, halves = (0, total), ((0, cut), (cut, total))
     back_weights = (w_gate, w_up)
 
-    lower, upper = spans[0]
+    def gather(value, parts, early=()):
+        pair = pack(value, swapped(value, "hid", 2), early)
+        own = arrange(pair, swapped(pair, "hid", 1), [value.shape[0] // parts] * parts)
+        return [(array, shifted(array, "tok", 1), 0) for array in own]
+
+    def gather_both(index, after, early=()):
+        lower, upper = spans[index]
+        mixed = cut_rows(acts, grad_out, [(0, lower, upper - lower), (1, lower, upper - lower)], after)
+        return gather(mixed, 2, early)
+
     rows = heights[0]
-    mixed, theirs = [], []
-    for value in (acts, grad_out):
-        value = value[lower:upper]
-        pair = pack(value, swapped(value, "hid", 2), cost=3.0)
-        mixed.append(arrange(pair, swapped(pair, "hid", 1), cost=3.0))
-        theirs.append(shifted(mixed[-1], "tok", 1))
-    x, dy = [(mixed[i], theirs[i], 0) for i in range(2)]
+    x, = gather(first_rows(acts, rows), 1)
+    dy, = gather(cut_rows(acts, grad_out, [(1, 0, rows)]), 1)
+    inputs = [(x, dy), gather_both(1, (dy[0],))]
     gate_up = forward([(*x, False), (*x, False)], (w_gate, w_up), whole, rows)
     dhid = forward([(*dy, True)], (w_down,), whole, rows, (gate_up,))
-    inputs = [(x, dy)]
     sums = [[((gate_up, dhid), ((0, 0), (0, 2 * rows), (1, 0)))]]
-
-    def gather_piece(index, cut_after, pack_after):
-        rows = heights[index]
-        both = cut_piece(acts, grad_out, *spans[index], cut_after)
-        pair = pack(both, swapped(both, "hid", 2), pack_after)
-        own = arrange(pair, swapped(pair, "hid", 1))
-        other = shifted(own, "tok", 1)
-        inputs.append(((own, other, 0), (own, other, rows)))
-        return pair
 
     def forward_piece(index, after):
         x, dy = inputs[index]
@@ -424,37 +440,36 @@
     def end_step(far, earlier=()):
         return fold_last(far[0], swapped(far[1], "hid", 2), earlier)
 
-    pair = gather_piece(1, (dhid,), ())
-    done = forward_piece(1, ())
-    xs = [turned(*x, rows, done) for (x, _), rows in zip(inputs, heights)]
-    grads = [backward_piece(0, 0, None, True, (*done, *xs))]
-    gather_piece(2, (pair,), (grads[0][1],))
+    done = forward_piece(1, (dhid,))
+    grads = [backward_piece(0, 0, None, True, done)]
+    inputs.append(gather_both(last, (inputs[1][0][0],), (grads[0][1],)))
     near = near_step(grads[0])
-    done = forward_piece(2, (near[0],))
-    xs.append(turned(*inputs[last][0], heights[last], done))
+    done = forward_piece(last, (near[0],))
+    all_x, all_y = [
+        joined([(array, p[k][2], rows) for p, rows in zip(inputs, heights) for array in p[k][:2]], k == 0, done)
+        for k in range(2)
+    ]
     far = far_step(near)
-    grads.append(backward_piece(1, 0, None, True, (*done, xs[last], far[0])))
+    grads.append(backward_piece(1, 0, None, True, (all_x, all_y, far[0])))
     finished = [end_step(far)]
-
-    ys = [(array, y[2], rows) for (_, y), rows in zip(inputs, heights) for array in y[:2]]
 
     def with_last(results, k, part):
         return [(grads[c][k], halves[part][0]) for c in range(last)] + [(results[k], 0)]
 
     first = backward_piece(last, 0, None, False, (grads[1][1], finished[0]))
     near = near_step(grads[1])
-    down, down_token = row_grads(with_last(first, 0, 0), ys, halves[0], total, (), (near[0],))
+    down, down_token = row_grads(with_last(first, 0, 0), all_y, halves[0], total, (), (near[0],))
     far = far_step(near)
     gate, up, token = column_grads(
-        xs, with_last(first, 1, 0), with_last(first, 2, 0), halves[0], total, (), (far[0], down_token)
+        all_x, with_last(first, 1, 0), with_last(first, 2, 0), halves[0], total, (), (far[0], down_token)
     )
     finished.append(end_step(far))
     second = backward_piece(last, 1, first[3], True, (token, finished[1]))
     near = near_step(second)
-    down, down_token = row_grads(with_last(second, 0, 1), ys, halves[1], total, (down,), ())
+    down, down_token = row_grads(with_last(second, 0, 1), all_y, halves[1], total, (down,), ())
     far = far_step(near)
     gate, up, _ = column_grads(
-        xs, with_last(second, 1, 1), with_last(second, 2, 1), halves[1], total, (gate, up), (near[0], down_token)
+        all_x, with_last(second, 1, 1), with_last(second, 2, 1), halves[1], total, (gate, up), (near[0], down_token)
     )
     return end_step(far, finished), gate, up, down
 

time: 141 us -> 137 us (0.972)
  local copies, waits for them, and re-layouts: 5.13 us -> 1.1 us
    ppermute x12 -> x14, waiting for transfers between devices: 17.8 us -> 8.68 us  [shifted(): return lax.ppermute(value, axis, [(i, (i + step) % n) for i in range(n)])]
    ppermute x14, waiting for transfers between devices: 31.3 us -> 40.3 us  [swapped(): return lax.ppermute(value, axis, [(i, i ^ bit) for i in range(n)])]
    unnamed x32 -> x14, local copies, waits for them, and re-layouts: 3.44 us -> 1.1 us
    slice x2 -> x0, local copies, waits for them, and re-layouts: 1.69 us -> none  [piped(): value = value[lower:upper]]
    pallas_call x31 -> x32, Pallas kernels: 33.5 us -> 33.2 us  [the longest x31 33.2 us: local(): pl.pallas_call(body, out_shape=shapes, in_specs=[VMEM] * len(args) + [ANY...]
    ppermute x12 -> x14, starting transfers between devices: 8.28 us -> 8.25 us  [shifted(): return lax.ppermute(value, axis, [(i, (i + step) % n) for i in range(n)])]
  transfers between devices with their start and end apart: 26 -> 28, of which waited for: 15 -> 13; matrix products, arithmetic and copies ran while one was open for 1% -> 0% of each run, Pallas kernels for 33% -> 37%
where the time goes in v8:
time: 137 us; the launch traced here: 136 us
  Pallas kernels  53.6 us (39%)
  waiting for transfers between devices  49 us (36%)
  starting transfers between devices  31.8 us (23%)
    ppermute x14, waiting for transfers between devices, swapped(): return lax.ppermute(value, axis, [(i, i ^ bit) for i in range(n)])  40.3 us
    pallas_call x31, Pallas kernels, local(): pl.pallas_call(body, out_shape=shapes, in_specs=[VMEM] * len(args) + [ANY...  33.2 us
    ppermute x14, starting transfers between devices, swapped(): return lax.ppermute(value, axis, [(i, i ^ bit) for i in range(n)])  23.6 us
    pallas_call x4, Pallas kernels, gradients(): pl.pallas_call(body, grid=grid, out_shape=[jax.ShapeDtypeStruct(shape, jn...  20.4 us
    ppermute x14, waiting for transfers between devices, shifted(): return lax.ppermute(value, axis, [(i, (i + step) % n) for i in range(n)])  8.68 us
    ppermute x14, starting transfers between devices, shifted(): return lax.ppermute(value, axis, [(i, (i + step) % n) for i in range(n)])  8.25 us
  transfers between devices with their start and end apart: 28, of which 13 were waited for; matrix products, arithmetic and copies ran while one was open for 0% of the time, Pallas kernels for 37%

profile of v8, /device:TPU:0, one launch (start us, length us, event | category | flops | bytes accessed | tf_op | source)
XLA Modules:
  0.0 136.4 jit_solution(9280983260596682247)
XLA Ops:
  0.7 1.1 copy-done.2
  1.7 4.1 %collective-permute-start.5 = (bf16[64,512]{1,0:T(8,128)(2,1)S(1)}, bf16[64,512]{1,0:T(8,128)(2,1)S(1)}, u32[]{:S(2)}, u32[]{:S(2)}) collective-permute-start(bf16[64,512]{1,0:T(8,128)(2,1)S(1)} %shard_map.91.refs_0_), channel_id=1, source_target_pairs={{0,8},{4,12},{8,0},{12,4},{1,9},{5,13},{9,1},{13,5},{2,10},{6,14},... | collective-permute-start | bytes 196616 | tf_op jit(solution)/shard_map/ppermute | solution.py:45
  5.8 3.6 %collective-permute-done.5.refs_1_ = bf16[64,512]{1,0:T(8,128)(2,1)S(1)} collective-permute-done((bf16[64,512]{1,0:T(8,128)(2,1)S(1)}, bf16[64,512]{1,0:T(8,128)(2,1)S(1)}, u32[]{:S(2)}, u32[]{:S(2)}) %collective-permute-start.5) | collective-permute-done | bytes 65568 | tf_op jit(solution)/shard_map/ppermute | solution.py:45
  9.5 0.6 collective-permute-start.6
  10.1 4.4 %collective-permute-done.6.refs_1_ = bf16[64,1024]{1,0:T(8,128)(2,1)S(1)} collective-permute-done((bf16[64,1024]{1,0:T(8,128)(2,1)S(1)}, bf16[64,1024]{1,0:T(8,128)(2,1)S(1)}, u32[]{:S(2)}, u32[]{:S(2)}) %collective-permute-start.6) | collective-permute-done | bytes 131104 | tf_op jit(solution)/shard_map/ppermute | solution.py:45
  14.7 2.4 %collective-permute-start = (bf16[64,512]{1,0:T(8,128)(2,1)S(1)}, bf16[64,512]{1,0:T(8,128)(2,1)S(1)}, u32[]{:S(2)}, u32[]{:S(2)}) collective-permute-start(bf16[64,512]{1,0:T(8,128)(2,1)S(1)} %shard_map.84.refs_0_), channel_id=1, source_target_pairs={{0,8},{4,12},{8,0},{12,4},{1,9},{5,13},{9,1},{13,5},{2,10},{6,14},... | collective-permute-start | bytes 196616 | tf_op jit(solution)/shard_map/ppermute | solution.py:45
  17.1 2.1 %shard_map.94.refs_3_.refs_0_ = bf16[256,1792]{1,0:T(8,128)(2,1)S(1)} custom-call(bf16[64,2048]{1,0:T(8,128)(2,1)S(1)} %shard_map.93.refs_0_.refs_2_, bf16[64,2048]{1,0:T(8,128)(2,1)S(1)} %collective-permute-done.7.refs_1_.refs_3_, bf16[64,2048]{1,0:T(8,128)(2,1)S(1)} %shard_map.93.refs_0_.refs_2_, ...), custom_call_target="tpu_custom_call" | custom-call | flops 345000000 | tf_op jit(solution)/shard_map/pallas_call | solution.py:100
  19.2 1.6 %collective-permute-start.9 = (bf16[256,1792]{1,0:T(8,128)(2,1)S(1)}, bf16[256,1792]{1,0:T(8,128)(2,1)S(1)}, u32[]{:S(2)}, u32[]{:S(2)}) collective-permute-start(bf16[256,1792]{1,0:T(8,128)(2,1)S(1)} %shard_map.94.refs_3_.refs_0_), channel_id=1, source_target_pairs={{0,2},{2,0},{1,3},{3,1},{4,6},{6,4},{5,7},{7,5},{8,10},{10,8},{9,1... | collective-permute-start | bytes 2752520 | tf_op jit(solution)/shard_map/ppermute | solution.py:40
  20.7 0.8 collective-permute-done.refs_1_
  21.6 1.0 collective-permute-start.1
  22.6 4.1 %collective-permute-done.1.refs_1_ = bf16[64,1024]{1,0:T(8,128)(2,1)S(1)} collective-permute-done((bf16[64,1024]{1,0:T(8,128)(2,1)S(1)}, bf16[64,1024]{1,0:T(8,128)(2,1)S(1)}, u32[]{:S(2)}, u32[]{:S(2)}) %collective-permute-start.1) | collective-permute-done | bytes 131104 | tf_op jit(solution)/shard_map/ppermute | solution.py:45
  26.8 2.5 %collective-permute-start.2 = (bf16[128,512]{1,0:T(8,128)(2,1)S(1)}, bf16[128,512]{1,0:T(8,128)(2,1)S(1)}, u32[]{:S(2)}, u32[]{:S(2)}) collective-permute-start(bf16[128,512]{1,0:T(8,128)(2,1)S(1)} %shard_map.87.refs_0_), channel_id=1, source_target_pairs={{0,8},{4,12},{8,0},{12,4},{1,9},{5,13},{9,1},{13,5},{2,10},{6,14},... | collective-permute-start | bytes 393224 | tf_op jit(solution)/shard_map/ppermute | solution.py:45
  29.3 7.2 %collective-permute-done.2.refs_1_ = bf16[128,512]{1,0:T(8,128)(2,1)S(1)} collective-permute-done((bf16[128,512]{1,0:T(8,128)(2,1)S(1)}, bf16[128,512]{1,0:T(8,128)(2,1)S(1)}, u32[]{:S(2)}, u32[]{:S(2)}) %collective-permute-start.2) | collective-permute-done | bytes 131104 | tf_op jit(solution)/shard_map/ppermute | solution.py:45
  36.5 0.6 collective-permute-start.3
  37.1 2.5 %shard_map.95.refs_9_.refs_1_ = bf16[128,1792]{1,0:T(8,128)(2,1)S(1)} custom-call(bf16[64,2048]{1,0:T(8,128)(2,1)S(1)} %shard_map.86.refs_2_.refs_0_, bf16[64,2048]{1,0:T(8,128)(2,1)S(1)} %collective-permute-done.8.refs_1_, bf16[1792,2048]{1,0:T(8,128)(2,1)S(1)} %bitcast.1, bf16[256,1792]{1,0:T(8,128)(2,1)S(1)} %shard_map.94.refs_3_.refs_0_), custom_call_target="tpu_custom_call" | custom-call | flops 345000000 | tf_op jit(solution)/shard_map/pallas_call | solution.py:100
  39.6 1.6 %collective-permute-start.10 = (bf16[128,1792]{1,0:T(8,128)(2,1)S(1)}, bf16[128,1792]{1,0:T(8,128)(2,1)S(1)}, u32[]{:S(2)}, u32[]{:S(2)}) collective-permute-start(bf16[128,1792]{1,0:T(8,128)(2,1)S(1)} %shard_map.95.refs_9_.refs_1_), channel_id=1, source_target_pairs={{0,2},{2,0},{1,3},{3,1},{4,6},{6,4},{5,7},{7,5},{8,10},{10,8},{9,1... | collective-permute-start | bytes 1376264 | tf_op jit(solution)/shard_map/ppermute | solution.py:40
  41.2 3.3 %collective-permute-done.3.refs_1_ = bf16[128,1024]{1,0:T(8,128)(2,1)S(1)} collective-permute-done((bf16[128,1024]{1,0:T(8,128)(2,1)S(1)}, bf16[128,1024]{1,0:T(8,128)(2,1)S(1)}, u32[]{:S(2)}, u32[]{:S(2)}) %collective-permute-start.3) | collective-permute-done | bytes 262176 | tf_op jit(solution)/shard_map/ppermute | solution.py:45
  44.6 0.5 collective-permute-start.12
  45.1 2.6 %collective-permute-start.4 = (bf16[128,512]{1,0:T(8,128)(2,1)S(1)}, bf16[128,512]{1,0:T(8,128)(2,1)S(1)}, u32[]{:S(2)}, u32[]{:S(2)}) collective-permute-start(bf16[128,512]{1,0:T(8,128)(2,1)S(1)} %shard_map.90.refs_0_), channel_id=1, source_target_pairs={{0,8},{4,12},{8,0},{12,4},{1,9},{5,13},{9,1},{13,5},{2,10},{6,14},... | collective-permute-start | bytes 393224 | tf_op jit(solution)/shard_map/ppermute | solution.py:45
  47.7 4.4 %shard_map.96.refs_6_.refs_0_ = bf16[384,1792]{1,0:T(8,128)(2,1)S(1)} custom-call(bf16[64,2048]{1,0:T(8,128)(2,1)S(1)} %get-tuple-element.48.refs_2_.refs_0_, bf16[64,2048]{1,0:T(8,128)(2,1)S(1)} %collective-permute-done.11.refs_1_.refs_3_, bf16[64,2048]{1,0:T(8,128)(2,1)S(1)} %get-tuple-element.48.refs_2_.refs_0_, ...), custom_call_target="tpu_custom_call" | custom-call | flops 345000000 | tf_op jit(solution)/shard_map/pallas_call | solution.py:100
  52.2 1.6 %collective-permute-start.19 = (bf16[384,1792]{1,0:T(8,128)(2,1)S(1)}, bf16[384,1792]{1,0:T(8,128)(2,1)S(1)}, u32[]{:S(2)}, u32[]{:S(2)}) collective-permute-start(bf16[384,1792]{1,0:T(8,128)(2,1)S(1)} %shard_map.96.refs_6_.refs_0_), channel_id=1, source_target_pairs={{0,2},{2,0},{1,3},{3,1},{4,6},{6,4},{5,7},{7,5},{8,10},{10,8},{9,1... | collective-permute-start | bytes 4128776 | tf_op jit(solution)/shard_map/ppermute | solution.py:40
  53.7 5.8 %shard_map.97 = (bf16[1792,128]{1,0:T(8,128)(2,1)S(1)}, bf16[128,1792]{1,0:T(8,128)(2,1)S(1)}, bf16[128,1792]{1,0:T(8,128)(2,1)S(1)}, f32[64,2048]{1,0:T(8,128)S(1)}, bf16[64,2048]{1,0:T(8,128)(2,1)S(1)}) custom-call(bf16[256,1792]{1,0:T(8,128)(2,1)S(1)} %shard_map.94.refs_3_.refs_0_, bf16[128,1792]{1,0:T(8,128)(2,1)S(1)} %shard_map.95.refs_9_.refs_1_, ...), custom_call_target="tpu_custom_call" | custom-call | flops 69000003584 | tf_op jit(solution)/shard_map/pallas_call | solution.py:100
  59.6 1.8 %collective-permute-start.13 = (bf16[128,1024]{1,0:T(8,128)(2,1)S(1)}, bf16[128,1024]{1,0:T(8,128)(2,1)S(1)}, u32[]{:S(2)}, u32[]{:S(2)}) collective-permute-start(bf16[128,1024]{1,0:T(8,128)(2,1)S(1)} %shard_map.98.refs_0_), channel_id=1, source_target_pairs={{0,4},{4,0},{8,12},{12,8},{1,5},{5,1},{9,13},{13,9},{2,6},{6,2},{1... | collective-permute-start | bytes 786440 | tf_op jit(solution)/shard_map/ppermute | solution.py:45
  61.4 6.0 %collective-permute-done.13.refs_1_ = bf16[128,1024]{1,0:T(8,128)(2,1)S(1)} collective-permute-done((bf16[128,1024]{1,0:T(8,128)(2,1)S(1)}, bf16[128,1024]{1,0:T(8,128)(2,1)S(1)}, u32[]{:S(2)}, u32[]{:S(2)}) %collective-permute-start.13) | collective-permute-done | bytes 262176 | tf_op jit(solution)/shard_map/ppermute | solution.py:45
  68.1 1.8 %collective-permute-start.20 = (bf16[64,1024]{1,0:T(8,128)(2,1)S(1)}, bf16[64,1024]{1,0:T(8,128)(2,1)S(1)}, u32[]{:S(2)}, u32[]{:S(2)}) collective-permute-start(bf16[64,1024]{1,0:T(8,128)(2,1)S(1)} %get-tuple-element.56), channel_id=1, source_target_pairs={{0,4},{4,0},{8,12},{12,8},{1,5},{5,1},{9,13},{13,9},{2,6},{6,2},{1... | collective-permute-start | bytes 393224 | tf_op jit(solution)/shard_map/ppermute | solution.py:45
  69.9 3.7 %collective-permute-done.20.refs_1_ = bf16[64,1024]{1,0:T(8,128)(2,1)S(1)} collective-permute-done((bf16[64,1024]{1,0:T(8,128)(2,1)S(1)}, bf16[64,1024]{1,0:T(8,128)(2,1)S(1)}, u32[]{:S(2)}, u32[]{:S(2)}) %collective-permute-start.20) | collective-permute-done | bytes 131104 | tf_op jit(solution)/shard_map/ppermute | solution.py:45
  73.7 2.6 %shard_map.101.refs_9_.refs_0_ = bf16[384,1024]{1,0:T(8,128)(2,1)S(1)} custom-call(bf16[64,2048]{1,0:T(8,128)(2,1)S(1)} %get-tuple-element.51.refs_0_.refs_2_.refs_4_, bf16[64,2048]{1,0:T(8,128)(2,1)S(1)} %collective-permute-done.14.refs_1_.refs_3_.refs_5_, bf16[64,2048]{1,0:T(8,128)(2,1)S(1)} %get-tuple-element.51.refs_0_.refs_2_.refs_4_, ...), custom_call_target="tpu_custom_call" | custom-call | flops 345000000 | tf_op jit(solution)/shard_map/pallas_call | solution.py:100
  76.3 0.6 collective-permute-start.18
  76.9 2.0 %shard_map.102.refs_6_.refs_0_ = bf16[384,768]{1,0:T(8,128)(2,1)S(1)} custom-call(bf16[64,2048]{1,0:T(8,128)(2,1)S(1)} %get-tuple-element.51.refs_0_.refs_2_.refs_4_, bf16[64,2048]{1,0:T(8,128)(2,1)S(1)} %collective-permute-done.14.refs_1_.refs_3_.refs_5_, bf16[64,2048]{1,0:T(8,128)(2,1)S(1)} %get-tuple-element.51.refs_0_.refs_2_.refs_4_, ...), custom_call_target="tpu_custom_call" | custom-call | flops 345000000 | tf_op jit(solution)/shard_map/pallas_call | solution.py:100
  78.9 0.6 shard_map.103.refs_4_.refs_0_
  79.7 5.6 %collective-permute-done.19.refs_1_ = bf16[384,1792]{1,0:T(8,128)(2,1)S(1)} collective-permute-done((bf16[384,1792]{1,0:T(8,128)(2,1)S(1)}, bf16[384,1792]{1,0:T(8,128)(2,1)S(1)}, u32[]{:S(2)}, u32[]{:S(2)}) %collective-permute-start.19) | collective-permute-done | bytes 1376288 | tf_op jit(solution)/shard_map/ppermute | solution.py:40
  85.3 5.8 %shard_map.106 = (bf16[1792,128]{1,0:T(8,128)(2,1)S(1)}, bf16[128,1792]{1,0:T(8,128)(2,1)S(1)}, bf16[128,1792]{1,0:T(8,128)(2,1)S(1)}, f32[64,2048]{1,0:T(8,128)S(1)}, bf16[64,2048]{1,0:T(8,128)(2,1)S(1)}) custom-call(bf16[384,1792]{1,0:T(8,128)(2,1)S(1)} %shard_map.96.refs_6_.refs_0_, bf16[384,1792]{1,0:T(8,128)(2,1)S(1)} %collective-permute-done.19.refs_1_, ...), custom_call_target="tpu_custom_call" | custom-call | flops 69000003584 | tf_op jit(solution)/shard_map/pallas_call | solution.py:100
  91.2 1.5 %collective-permute-done.22.refs_1_ = bf16[64,2048]{1,0:T(8,128)(2,1)S(1)} collective-permute-done((bf16[64,2048]{1,0:T(8,128)(2,1)S(1)}, bf16[64,2048]{1,0:T(8,128)(2,1)S(1)}, u32[]{:S(2)}, u32[]{:S(2)}) %collective-permute-start.22) | collective-permute-done | bytes 262176 | tf_op jit(solution)/shard_map/ppermute | solution.py:40
  92.8 1.8 %collective-permute-start.23 = (bf16[64,1024]{1,0:T(8,128)(2,1)S(1)}, bf16[64,1024]{1,0:T(8,128)(2,1)S(1)}, u32[]{:S(2)}, u32[]{:S(2)}) collective-permute-start(bf16[64,1024]{1,0:T(8,128)(2,1)S(1)} %get-tuple-element.68), channel_id=1, source_target_pairs={{0,4},{4,0},{8,12},{12,8},{1,5},{5,1},{9,13},{13,9},{2,6},{6,2},{1... | collective-permute-start | bytes 393224 | tf_op jit(solution)/shard_map/ppermute | solution.py:45
  94.6 1.3 collective-permute-start.21
  95.9 4.9 %collective-permute-done.21.refs_1_ = bf16[64,512]{1,0:T(8,128)(2,1)S(1)} collective-permute-done((bf16[64,512]{1,0:T(8,128)(2,1)S(1)}, bf16[64,512]{1,0:T(8,128)(2,1)S(1)}, u32[]{:S(2)}, u32[]{:S(2)}) %collective-permute-start.21) | collective-permute-done | bytes 65568 | tf_op jit(solution)/shard_map/ppermute | solution.py:45
  100.8 1.6 %collective-permute-start.17 = (bf16[384,768]{1,0:T(8,128)(2,1)S(1)}, bf16[384,768]{1,0:T(8,128)(2,1)S(1)}, u32[]{:S(2)}, u32[]{:S(2)}) collective-permute-start(bf16[384,768]{1,0:T(8,128)(2,1)S(1)} %shard_map.102.refs_6_.refs_0_), channel_id=1, source_target_pairs={{0,2},{2,0},{1,3},{3,1},{4,6},{6,4},{5,7},{7,5},{8,10},{10,8},{9,1... | collective-permute-start | bytes 1769480 | tf_op jit(solution)/shard_map/ppermute | solution.py:40
  102.4 1.7 %collective-permute-start.24 = (bf16[64,512]{1,0:T(8,128)(2,1)S(1)}, bf16[64,512]{1,0:T(8,128)(2,1)S(1)}, u32[]{:S(2)}, u32[]{:S(2)}) collective-permute-start(bf16[64,512]{1,0:T(8,128)(2,1)S(1)} %get-tuple-element.75), channel_id=1, source_target_pairs={{0,8},{4,12},{8,0},{12,4},{1,9},{5,13},{9,1},{13,5},{2,10},{6,14},... | collective-permute-start | bytes 196616 | tf_op jit(solution)/shard_map/ppermute | solution.py:45
  104.1 3.4 %shard_map.108 = (bf16[1024,128]{1,0:T(8,128)(2,1)S(1)}, bf16[128,1024]{1,0:T(8,128)(2,1)S(1)}, bf16[128,1024]{1,0:T(8,128)(2,1)S(1)}, f32[128,2048]{1,0:T(8,128)S(1)}) custom-call(bf16[384,1024]{1,0:T(8,128)(2,1)S(1)} %shard_map.101.refs_9_.refs_0_, bf16[384,1024]{1,0:T(8,128)(2,1)S(1)} %collective-permute-done.18.refs_1_, bf16[2048,1792]{1,0:T(8,128)(2,1)S(1)} %copy-done, ...), custom_call_target="tpu_custom_call" | custom-call | flops 1150000000 | tf_op jit(solution)/shard_map/pallas_call | solution.py:100
  107.5 4.1 %shard_map.111 = (bf16[1792,2048]{1,0:T(8,128)(2,1)}, bf16[16,128]{1,0:T(8,128)(2,1)S(1)}) custom-call(bf16[1792,128]{1,0:T(8,128)(2,1)S(1)} %get-tuple-element.70.refs_0_, bf16[1792,128]{1,0:T(8,128)(2,1)S(1)} %get-tuple-element.71.refs_1_, bf16[1024,128]{1,0:T(8,128)(2,1)S(1)} %get-tuple-element.72.refs_2_, ...), custom_call_target="tpu_custom_call" | custom-call | flops 3449999872 | tf_op jit(solution)/shard_map/pallas_call | solution.py:315
  111.6 6.9 %shard_map.112 = (bf16[2048,1792]{1,0:T(8,128)(2,1)}, bf16[2048,1792]{1,0:T(8,128)(2,1)}, bf16[16,128]{1,0:T(8,128)(2,1)S(1)}) custom-call(bf16[2048,384]{1,0:T(8,128)(2,1)S(1)} %shard_map.103.refs_4_.refs_0_, bf16[128,1792]{1,0:T(8,128)(2,1)S(1)} %get-tuple-element.50.refs_2_.refs_1_, bf16[128,1792]{1,0:T(8,128)(2,1)S(1)} %get-tuple-element.58.refs_4_.refs_2_, ...), custom_call_target="tpu_custom_call" | custom-call | flops 5750000128 | tf_op jit(solution)/shard_map/pallas_call | solution.py:315
  118.5 2.6 %shard_map.114 = (bf16[768,128]{1,0:T(8,128)(2,1)S(1)}, bf16[128,768]{1,0:T(8,128)(2,1)S(1)}, bf16[128,768]{1,0:T(8,128)(2,1)S(1)}, f32[64,2048]{1,0:T(8,128)S(1)}, bf16[64,2048]{1,0:T(8,128)(2,1)S(1)}) custom-call(bf16[384,768]{1,0:T(8,128)(2,1)S(1)} %shard_map.102.refs_6_.refs_0_, bf16[384,768]{1,0:T(8,128)(2,1)S(1)} %collective-permute-done.17.refs_1_, ...), custom_call_target="tpu_custom_call" | custom-call | flops 1150000000 | tf_op jit(solution)/shard_map/pallas_call | solution.py:100
  121.2 1.5 %collective-permute-done.25.refs_1_ = bf16[64,2048]{1,0:T(8,128)(2,1)S(1)} collective-permute-done((bf16[64,2048]{1,0:T(8,128)(2,1)S(1)}, bf16[64,2048]{1,0:T(8,128)(2,1)S(1)}, u32[]{:S(2)}, u32[]{:S(2)}) %collective-permute-start.25) | collective-permute-done | bytes 262176 | tf_op jit(solution)/shard_map/ppermute | solution.py:40
  122.8 3.4 %shard_map.118 = (bf16[1792,2048]{1,0:T(8,128)(2,1)}, bf16[16,128]{1,0:T(8,128)(2,1)S(1)}) custom-call(bf16[1792,128]{1,0:T(8,128)(2,1)S(1)} %get-tuple-element.70.refs_0_, bf16[1792,128]{1,0:T(8,128)(2,1)S(1)} %get-tuple-element.71.refs_1_, bf16[768,128]{1,0:T(8,128)(2,1)S(1)} %get-tuple-element.86.refs_2_, ...), custom_call_target="tpu_custom_call", output_to_operand_aliasing={{0}: (4, {})} | custom-call | flops 3449999872 | tf_op jit(solution)/shard_map/pallas_call | solution.py:315
  126.2 2.1 %collective-permute-done.26.refs_1_ = bf16[64,1024]{1,0:T(8,128)(2,1)S(1)} collective-permute-done((bf16[64,1024]{1,0:T(8,128)(2,1)S(1)}, bf16[64,1024]{1,0:T(8,128)(2,1)S(1)}, u32[]{:S(2)}, u32[]{:S(2)}) %collective-permute-start.26) | collective-permute-done | bytes 131104 | tf_op jit(solution)/shard_map/ppermute | solution.py:45
  128.4 1.3 collective-permute-start.27
  129.7 6.0 %shard_map.119 = (bf16[2048,1792]{1,0:T(8,128)(2,1)}, bf16[2048,1792]{1,0:T(8,128)(2,1)}, bf16[16,128]{1,0:T(8,128)(2,1)}) custom-call(bf16[2048,384]{1,0:T(8,128)(2,1)S(1)} %shard_map.103.refs_4_.refs_0_, bf16[128,1792]{1,0:T(8,128)(2,1)S(1)} %get-tuple-element.50.refs_2_.refs_1_, ...), custom_call_target="tpu_custom_call", output_to_operand_aliasing={{0}: (7, {}), {1}: (8, {})} | custom-call | flops 5750000128 | tf_op jit(solution)/shard_map/pallas_call | solution.py:315
  135.7 0.7 shard_map.117
  (59 shorter events, 1.8 us)
Async XLA Ops:
  0.6 16.5 %copy-start = (bf16[2048,1792]{1,0:T(8,128)(2,1)S(1)}, bf16[2048,1792]{1,0:T(8,128)(2,1)}, u32[]{:S(2)}) copy-start(bf16[2048,1792]{1,0:T(8,128)(2,1)} %refs_2_.7) | copy-start | bytes 22020100
  0.6 16.5 %copy-start.1 = (bf16[2048,1792]{1,0:T(8,128)(2,1)S(1)}, bf16[2048,1792]{1,0:T(8,128)(2,1)}, u32[]{:S(2)}) copy-start(bf16[2048,1792]{1,0:T(8,128)(2,1)} %refs_3_.5) | copy-start | bytes 22020100
  0.7 1.1 copy-start.2
  1.7 12.9 %copy-start.3 = (bf16[192,512]{1,0:T(8,128)(2,1)S(1)}, bf16[192,512]{1,0:T(8,128)(2,1)}, u32[]{:S(2)}) copy-start(bf16[192,512]{1,0:T(8,128)(2,1)} %source.1) | copy-start | bytes 589828
  1.7 12.9 %copy-start.4 = (bf16[192,512]{1,0:T(8,128)(2,1)S(1)}, bf16[192,512]{1,0:T(8,128)(2,1)}, u32[]{:S(2)}) copy-start(bf16[192,512]{1,0:T(8,128)(2,1)} %refs_1_.5) | copy-start | bytes 589828
  1.7 7.8 %collective-permute-start.5 = (bf16[64,512]{1,0:T(8,128)(2,1)S(1)}, bf16[64,512]{1,0:T(8,128)(2,1)S(1)}, u32[]{:S(2)}, u32[]{:S(2)}) collective-permute-start(bf16[64,512]{1,0:T(8,128)(2,1)S(1)} %shard_map.91.refs_0_), channel_id=1, source_target_pairs={{0,8},{4,12},{8,0},{12,4},{1,9},{5,13},{9,1},{13,5},{2,10},{6,14},... | collective-permute-start | bytes 196616 | tf_op jit(solution)/shard_map/ppermute | solution.py:45
  9.5 5.0 %collective-permute-start.6 = (bf16[64,1024]{1,0:T(8,128)(2,1)S(1)}, bf16[64,1024]{1,0:T(8,128)(2,1)S(1)}, u32[]{:S(2)}, u32[]{:S(2)}) collective-permute-start(bf16[64,1024]{1,0:T(8,128)(2,1)S(1)} %shard_map.92.refs_0_), channel_id=1, source_target_pairs={{0,4},{4,0},{8,12},{12,8},{1,5},{5,1},{9,13},{13,9},{2,6},{6,2},{1... | collective-permute-start | bytes 393224 | tf_op jit(solution)/shard_map/ppermute | solution.py:45
  14.6 2.5 %collective-permute-start.7 = (bf16[64,2048]{1,0:T(8,128)(2,1)S(1)}, bf16[64,2048]{1,0:T(8,128)(2,1)S(1)}, u32[]{:S(2)}, u32[]{:S(2)}) collective-permute-start(bf16[64,2048]{1,0:T(8,128)(2,1)S(1)} %shard_map.93.refs_0_.refs_2_), channel_id=1, source_target_pairs={{0,1},{1,0},{2,3},{3,2},{4,5},{5,4},{6,7},{7,6},{8,9},{9,8},{10,11... | collective-permute-start | bytes 786440 | tf_op jit(solution)/shard_map/ppermute | solution.py:40
  14.7 22.4 %slice-start = ((s8[7340032]{0:T(1024)(128)(4,1)}), s8[4194304]{0:T(1024)(128)(4,1)S(1)}, s32[]{:S(2)}) async-start(s8[7340032]{0:T(1024)(128)(4,1)} %bitcast), calls=%async_computation | async-start | bytes 8388608
  14.7 22.4 %slice-start.1 = ((s8[7340032]{0:T(1024)(128)(4,1)}), s8[3145728]{0:T(1024)(128)(4,1)S(1)}, s32[]{:S(2)}) async-start(s8[7340032]{0:T(1024)(128)(4,1)} %bitcast), calls=%async_computation.1 | async-start | bytes 6291456
  14.7 6.8 %collective-permute-start = (bf16[64,512]{1,0:T(8,128)(2,1)S(1)}, bf16[64,512]{1,0:T(8,128)(2,1)S(1)}, u32[]{:S(2)}, u32[]{:S(2)}) collective-permute-start(bf16[64,512]{1,0:T(8,128)(2,1)S(1)} %shard_map.84.refs_0_), channel_id=1, source_target_pairs={{0,8},{4,12},{8,0},{12,4},{1,9},{5,13},{9,1},{13,5},{2,10},{6,14},... | collective-permute-start | bytes 196616 | tf_op jit(solution)/shard_map/ppermute | solution.py:45
  19.2 34.5 %collective-permute-start.9 = (bf16[256,1792]{1,0:T(8,128)(2,1)S(1)}, bf16[256,1792]{1,0:T(8,128)(2,1)S(1)}, u32[]{:S(2)}, u32[]{:S(2)}) collective-permute-start(bf16[256,1792]{1,0:T(8,128)(2,1)S(1)} %shard_map.94.refs_3_.refs_0_), channel_id=1, source_target_pairs={{0,2},{2,0},{1,3},{3,1},{4,6},{6,4},{5,7},{7,5},{8,10},{10,8},{9,1... | collective-permute-start | bytes 2752520 | tf_op jit(solution)/shard_map/ppermute | solution.py:40
  21.6 5.1 %collective-permute-start.1 = (bf16[64,1024]{1,0:T(8,128)(2,1)S(1)}, bf16[64,1024]{1,0:T(8,128)(2,1)S(1)}, u32[]{:S(2)}, u32[]{:S(2)}) collective-permute-start(bf16[64,1024]{1,0:T(8,128)(2,1)S(1)} %shard_map.85.refs_0_), channel_id=1, source_target_pairs={{0,4},{4,0},{8,12},{12,8},{1,5},{5,1},{9,13},{13,9},{2,6},{6,2},{1... | collective-permute-start | bytes 393224 | tf_op jit(solution)/shard_map/ppermute | solution.py:45
  26.7 10.4 %collective-permute-start.8 = (bf16[64,2048]{1,0:T(8,128)(2,1)S(1)}, bf16[64,2048]{1,0:T(8,128)(2,1)S(1)}, u32[]{:S(2)}, u32[]{:S(2)}) collective-permute-start(bf16[64,2048]{1,0:T(8,128)(2,1)S(1)} %shard_map.86.refs_2_.refs_0_), channel_id=1, source_target_pairs={{0,1},{1,0},{2,3},{3,2},{4,5},{5,4},{6,7},{7,6},{8,9},{9,8},{10,11... | collective-permute-start | bytes 786440 | tf_op jit(solution)/shard_map/ppermute | solution.py:40
  26.8 9.7 %collective-permute-start.2 = (bf16[128,512]{1,0:T(8,128)(2,1)S(1)}, bf16[128,512]{1,0:T(8,128)(2,1)S(1)}, u32[]{:S(2)}, u32[]{:S(2)}) collective-permute-start(bf16[128,512]{1,0:T(8,128)(2,1)S(1)} %shard_map.87.refs_0_), channel_id=1, source_target_pairs={{0,8},{4,12},{8,0},{12,4},{1,9},{5,13},{9,1},{13,5},{2,10},{6,14},... | collective-permute-start | bytes 393224 | tf_op jit(solution)/shard_map/ppermute | solution.py:45
  36.5 8.0 %collective-permute-start.3 = (bf16[128,1024]{1,0:T(8,128)(2,1)S(1)}, bf16[128,1024]{1,0:T(8,128)(2,1)S(1)}, u32[]{:S(2)}, u32[]{:S(2)}) collective-permute-start(bf16[128,1024]{1,0:T(8,128)(2,1)S(1)} %shard_map.88.refs_0_), channel_id=1, source_target_pairs={{0,4},{4,0},{8,12},{12,8},{1,5},{5,1},{9,13},{13,9},{2,6},{6,2},{1... | collective-permute-start | bytes 786440 | tf_op jit(solution)/shard_map/ppermute | solution.py:45
  39.6 14.1 %collective-permute-start.10 = (bf16[128,1792]{1,0:T(8,128)(2,1)S(1)}, bf16[128,1792]{1,0:T(8,128)(2,1)S(1)}, u32[]{:S(2)}, u32[]{:S(2)}) collective-permute-start(bf16[128,1792]{1,0:T(8,128)(2,1)S(1)} %shard_map.95.refs_9_.refs_1_), channel_id=1, source_target_pairs={{0,2},{2,0},{1,3},{3,1},{4,6},{6,4},{5,7},{7,5},{8,10},{10,8},{9,1... | collective-permute-start | bytes 1376264 | tf_op jit(solution)/shard_map/ppermute | solution.py:40
  44.6 3.2 %collective-permute-start.11 = (bf16[64,2048]{1,0:T(8,128)(2,1)S(1)}, bf16[64,2048]{1,0:T(8,128)(2,1)S(1)}, u32[]{:S(2)}, u32[]{:S(2)}) collective-permute-start(bf16[64,2048]{1,0:T(8,128)(2,1)S(1)} %get-tuple-element.48.refs_2_.refs_0_), channel_id=1, source_target_pairs={{0,1},{1,0},{2,3},{3,2},{4,5},{5,4},{6,7},{7,6},{8,9},{9,8},{10,11... | collective-permute-start | bytes 786440 | tf_op jit(solution)/shard_map/ppermute | solution.py:40
  44.6 3.1 %collective-permute-start.12 = (bf16[64,2048]{1,0:T(8,128)(2,1)S(1)}, bf16[64,2048]{1,0:T(8,128)(2,1)S(1)}, u32[]{:S(2)}, u32[]{:S(2)}) collective-permute-start(bf16[64,2048]{1,0:T(8,128)(2,1)S(1)} %get-tuple-element.49.refs_4_.refs_2_), channel_id=1, source_target_pairs={{0,1},{1,0},{2,3},{3,2},{4,5},{5,4},{6,7},{7,6},{8,9},{9,8},{10,11... | collective-permute-start | bytes 786440 | tf_op jit(solution)/shard_map/ppermute | solution.py:40
  45.1 14.4 %collective-permute-start.4 = (bf16[128,512]{1,0:T(8,128)(2,1)S(1)}, bf16[128,512]{1,0:T(8,128)(2,1)S(1)}, u32[]{:S(2)}, u32[]{:S(2)}) collective-permute-start(bf16[128,512]{1,0:T(8,128)(2,1)S(1)} %shard_map.90.refs_0_), channel_id=1, source_target_pairs={{0,8},{4,12},{8,0},{12,4},{1,9},{5,13},{9,1},{13,5},{2,10},{6,14},... | collective-permute-start | bytes 393224 | tf_op jit(solution)/shard_map/ppermute | solution.py:45
  52.2 33.1 %collective-permute-start.19 = (bf16[384,1792]{1,0:T(8,128)(2,1)S(1)}, bf16[384,1792]{1,0:T(8,128)(2,1)S(1)}, u32[]{:S(2)}, u32[]{:S(2)}) collective-permute-start(bf16[384,1792]{1,0:T(8,128)(2,1)S(1)} %shard_map.96.refs_6_.refs_0_), channel_id=1, source_target_pairs={{0,2},{2,0},{1,3},{3,1},{4,6},{6,4},{5,7},{7,5},{8,10},{10,8},{9,1... | collective-permute-start | bytes 4128776 | tf_op jit(solution)/shard_map/ppermute | solution.py:40
  59.6 7.8 %collective-permute-start.13 = (bf16[128,1024]{1,0:T(8,128)(2,1)S(1)}, bf16[128,1024]{1,0:T(8,128)(2,1)S(1)}, u32[]{:S(2)}, u32[]{:S(2)}) collective-permute-start(bf16[128,1024]{1,0:T(8,128)(2,1)S(1)} %shard_map.98.refs_0_), channel_id=1, source_target_pairs={{0,4},{4,0},{8,12},{12,8},{1,5},{5,1},{9,13},{13,9},{2,6},{6,2},{1... | collective-permute-start | bytes 786440 | tf_op jit(solution)/shard_map/ppermute | solution.py:45
  61.4 6.6 %collective-permute-start.16 = (bf16[64,2048]{1,0:T(8,128)(2,1)S(1)}, bf16[64,2048]{1,0:T(8,128)(2,1)S(1)}, u32[]{:S(2)}, u32[]{:S(2)}) collective-permute-start(bf16[64,2048]{1,0:T(8,128)(2,1)S(1)} %get-tuple-element.54), channel_id=1, source_target_pairs={{0,1},{1,0},{2,3},{3,2},{4,5},{5,4},{6,7},{7,6},{8,9},{9,8},{10,11... | collective-permute-start | bytes 786440 | tf_op jit(solution)/shard_map/ppermute | solution.py:40
  67.4 6.2 %collective-permute-start.14 = (bf16[64,2048]{1,0:T(8,128)(2,1)S(1)}, bf16[64,2048]{1,0:T(8,128)(2,1)S(1)}, u32[]{:S(2)}, u32[]{:S(2)}) collective-permute-start(bf16[64,2048]{1,0:T(8,128)(2,1)S(1)} %get-tuple-element.51.refs_0_.refs_2_.refs_4_), channel_id=1, source_target_pairs={{0,1},{1,0},{2,3},{3,2},{4,5},{5,4},{6,7},{7,6},{8,9},{9,8},{10,11... | collective-permute-start | bytes 786440 | tf_op jit(solution)/shard_map/ppermute | solution.py:40
  67.5 6.1 %collective-permute-start.15 = (bf16[64,2048]{1,0:T(8,128)(2,1)S(1)}, bf16[64,2048]{1,0:T(8,128)(2,1)S(1)}, u32[]{:S(2)}, u32[]{:S(2)}) collective-permute-start(bf16[64,2048]{1,0:T(8,128)(2,1)S(1)} %get-tuple-element.52.refs_4_), channel_id=1, source_target_pairs={{0,1},{1,0},{2,3},{3,2},{4,5},{5,4},{6,7},{7,6},{8,9},{9,8},{10,11... | collective-permute-start | bytes 786440 | tf_op jit(solution)/shard_map/ppermute | solution.py:40
  68.1 5.5 %collective-permute-start.20 = (bf16[64,1024]{1,0:T(8,128)(2,1)S(1)}, bf16[64,1024]{1,0:T(8,128)(2,1)S(1)}, u32[]{:S(2)}, u32[]{:S(2)}) collective-permute-start(bf16[64,1024]{1,0:T(8,128)(2,1)S(1)} %get-tuple-element.56), channel_id=1, source_target_pairs={{0,4},{4,0},{8,12},{12,8},{1,5},{5,1},{9,13},{13,9},{2,6},{6,2},{1... | collective-permute-start | bytes 393224 | tf_op jit(solution)/shard_map/ppermute | solution.py:45
  76.3 27.8 %collective-permute-start.18 = (bf16[384,1024]{1,0:T(8,128)(2,1)S(1)}, bf16[384,1024]{1,0:T(8,128)(2,1)S(1)}, u32[]{:S(2)}, u32[]{:S(2)}) collective-permute-start(bf16[384,1024]{1,0:T(8,128)(2,1)S(1)} %shard_map.101.refs_9_.refs_0_), channel_id=1, source_target_pairs={{0,2},{2,0},{1,3},{3,1},{4,6},{6,4},{5,7},{7,5},{8,10},{10,8},{9,1... | collective-permute-start | bytes 2359304 | tf_op jit(solution)/shard_map/ppermute | solution.py:40
  91.1 1.6 %collective-permute-start.22 = (bf16[64,2048]{1,0:T(8,128)(2,1)S(1)}, bf16[64,2048]{1,0:T(8,128)(2,1)S(1)}, u32[]{:S(2)}, u32[]{:S(2)}) collective-permute-start(bf16[64,2048]{1,0:T(8,128)(2,1)S(1)} %get-tuple-element.66), channel_id=1, source_target_pairs={{0,1},{1,0},{2,3},{3,2},{4,5},{5,4},{6,7},{7,6},{8,9},{9,8},{10,11... | collective-permute-start | bytes 786440 | tf_op jit(solution)/shard_map/ppermute | solution.py:40
  92.8 9.6 %collective-permute-start.23 = (bf16[64,1024]{1,0:T(8,128)(2,1)S(1)}, bf16[64,1024]{1,0:T(8,128)(2,1)S(1)}, u32[]{:S(2)}, u32[]{:S(2)}) collective-permute-start(bf16[64,1024]{1,0:T(8,128)(2,1)S(1)} %get-tuple-element.68), channel_id=1, source_target_pairs={{0,4},{4,0},{8,12},{12,8},{1,5},{5,1},{9,13},{13,9},{2,6},{6,2},{1... | collective-permute-start | bytes 393224 | tf_op jit(solution)/shard_map/ppermute | solution.py:45
  94.6 6.2 %collective-permute-start.21 = (bf16[64,512]{1,0:T(8,128)(2,1)S(1)}, bf16[64,512]{1,0:T(8,128)(2,1)S(1)}, u32[]{:S(2)}, u32[]{:S(2)}) collective-permute-start(bf16[64,512]{1,0:T(8,128)(2,1)S(1)} %get-tuple-element.59), channel_id=1, source_target_pairs={{0,8},{4,12},{8,0},{12,4},{1,9},{5,13},{9,1},{13,5},{2,10},{6,14},... | collective-permute-start | bytes 196616 | tf_op jit(solution)/shard_map/ppermute | solution.py:45
  100.8 17.7 %collective-permute-start.17 = (bf16[384,768]{1,0:T(8,128)(2,1)S(1)}, bf16[384,768]{1,0:T(8,128)(2,1)S(1)}, u32[]{:S(2)}, u32[]{:S(2)}) collective-permute-start(bf16[384,768]{1,0:T(8,128)(2,1)S(1)} %shard_map.102.refs_6_.refs_0_), channel_id=1, source_target_pairs={{0,2},{2,0},{1,3},{3,1},{4,6},{6,4},{5,7},{7,5},{8,10},{10,8},{9,1... | collective-permute-start | bytes 1769480 | tf_op jit(solution)/shard_map/ppermute | solution.py:40
  102.4 16.1 %collective-permute-start.24 = (bf16[64,512]{1,0:T(8,128)(2,1)S(1)}, bf16[64,512]{1,0:T(8,128)(2,1)S(1)}, u32[]{:S(2)}, u32[]{:S(2)}) collective-permute-start(bf16[64,512]{1,0:T(8,128)(2,1)S(1)} %get-tuple-element.75), channel_id=1, source_target_pairs={{0,8},{4,12},{8,0},{12,4},{1,9},{5,13},{9,1},{13,5},{2,10},{6,14},... | collective-permute-start | bytes 196616 | tf_op jit(solution)/shard_map/ppermute | solution.py:45
  121.1 1.6 %collective-permute-start.25 = (bf16[64,2048]{1,0:T(8,128)(2,1)S(1)}, bf16[64,2048]{1,0:T(8,128)(2,1)S(1)}, u32[]{:S(2)}, u32[]{:S(2)}) collective-permute-start(bf16[64,2048]{1,0:T(8,128)(2,1)S(1)} %get-tuple-element.77), channel_id=1, source_target_pairs={{0,1},{1,0},{2,3},{3,2},{4,5},{5,4},{6,7},{7,6},{8,9},{9,8},{10,11... | collective-permute-start | bytes 786440 | tf_op jit(solution)/shard_map/ppermute | solution.py:40
  122.7 5.6 %collective-permute-start.26 = (bf16[64,1024]{1,0:T(8,128)(2,1)S(1)}, bf16[64,1024]{1,0:T(8,128)(2,1)S(1)}, u32[]{:S(2)}, u32[]{:S(2)}) collective-permute-start(bf16[64,1024]{1,0:T(8,128)(2,1)S(1)} %get-tuple-element.79), channel_id=1, source_target_pairs={{0,4},{4,0},{8,12},{12,8},{1,5},{5,1},{9,13},{13,9},{2,6},{6,2},{1... | collective-permute-start | bytes 393224 | tf_op jit(solution)/shard_map/ppermute | solution.py:45
  128.4 7.4 %collective-permute-start.27 = (bf16[64,512]{1,0:T(8,128)(2,1)S(1)}, bf16[64,512]{1,0:T(8,128)(2,1)S(1)}, u32[]{:S(2)}, u32[]{:S(2)}) collective-permute-start(bf16[64,512]{1,0:T(8,128)(2,1)S(1)} %get-tuple-element.81), channel_id=1, source_target_pairs={{0,8},{4,12},{8,0},{12,4},{1,9},{5,13},{9,1},{13,5},{2,10},{6,14},... | collective-permute-start | bytes 196616 | tf_op jit(solution)/shard_map/ppermute | solution.py:45

commit v9 on v8

--- a/solution.py
+++ b/solution.py
@@ -142,17 +142,17 @@
     )(value)
 
 
-def pack(value, far, after=()):
+def pack(value, far, after=(), cost=0.1):
     rows, width = value.shape
 
     def kernel(ins, outs):
         outs[0][:, :width] = ins[0][...]
         outs[0][:, width:] = ins[1][...]
 
-    return local(kernel, [((rows, 2 * width), value.dtype)], (value, far), after, 1)[0]
-
-
-def arrange(pair, near, heights):
+    return local(kernel, [((rows, 2 * width), value.dtype)], (value, far), after, 1, cost=cost)[0]
+
+
+def arrange(pair, near, heights, cost=0.1):
     width = pair.shape[1] // 2
 
     def kernel(ins, outs):
@@ -164,7 +164,7 @@
                 out[:, lanes(me ^ step, width)] = block
             top += height
 
-    return local(kernel, [((height, 4 * width), pair.dtype) for height in heights], (pair, near), (), 1)
+    return local(kernel, [((height, 4 * width), pair.dtype) for height in heights], (pair, near), (), 1, cost=cost)
 
 
 def over_blocks(width, step, body):
@@ -325,6 +325,14 @@
     )(*arrays, *old, *after)
 
 
+def tiled(out, left, right):
+    height, width = out.shape
+    for top in range(0, height, 512):
+        for start in range(0, width, 256):
+            rows, columns = pl.ds(top, min(512, height - top)), pl.ds(start, min(256, width - start))
+            out[rows, columns] = rows_by_cols(left[rows, :], right[:, columns]).astype(out.dtype)
+
+
 def placed(rows, columns, where):
     return pl.BlockSpec((pl.Element(rows), pl.Element(columns)), where)
 
@@ -333,7 +341,7 @@
     arrays = [x, *(p[0] for p in (*gs, *us))]
     count, lower, width = len(gs), span[0], span[1] - span[0]
     features, tokens = x.shape
-    block = 256
+    block = 512
 
     def kernel(ins, refs):
         gate_out, up_out, token, g_all, u_all = refs
@@ -349,36 +357,38 @@
                     target[top : top + rows] = ins[first + i][:, column : column + width]
                     top += rows
 
-        rows = ins[0][lanes(step, block), :]
-        gate_out[...] = rows_by_cols(rows, g_all[...]).astype(gate_out.dtype)
-        up_out[...] = rows_by_cols(rows, u_all[...]).astype(up_out.dtype)
+        rows = ins[0].at[lanes(step, block), :]
+        tiled(gate_out, rows, g_all)
+        tiled(up_out, rows, u_all)
 
     spec = placed(block, width, lambda i: (pl.multiple_of(i * block, block), lower))
     scratch = [pltpu.VMEM((tokens, width), jnp.bfloat16)] * 2
-    return gradients(kernel, [(features, total)] * 2, arrays, old, (features // block,), [spec, spec], scratch, after, 5.0)
+    return gradients(kernel, [(features, total)] * 2, arrays, old, (features // block,), [spec, spec], scratch, after, 0.1)
 
 
 def row_grads(hs, y, span, total, old, after=()):
     arrays = [*(p[0] for p in hs), y]
     count, lower, width = len(hs), span[0], span[1] - span[0]
-    features = y.shape[1]
-    block = 256
+    tokens, features = y.shape
+    block = 512
 
     def kernel(ins, refs):
-        out, token = refs
+        out, token, h_all = refs
         step = pl.program_id(0)
 
         @pl.when(step == 0)
         def _():
             token[...] = jnp.zeros_like(token)
-
-        rows = []
-        for i, (_, row) in enumerate(hs):
-            rows.append(ins[i][pl.ds(pl.multiple_of(row + step * block, block), block), :])
-        out[...] = rows_by_cols(jnp.concatenate(rows, axis=1), ins[count][...]).astype(out.dtype)
-
-    spec = placed(block, features, lambda i: (pl.multiple_of(lower + i * block, block), 0))
-    return gradients(kernel, [(total, features)], arrays, old, (width // block,), [spec], [], after, 3.0)
+            left = 0
+            for i, (piece, row) in enumerate(hs):
+                h_all[:, left : left + piece.shape[1]] = ins[i][row : row + width]
+                left += piece.shape[1]
+
+        tiled(out, h_all, ins[count].at[:, lanes(step, block)])
+
+    spec = placed(width, block, lambda i: (lower, pl.multiple_of(i * block, block)))
+    scratch = [pltpu.VMEM((width, tokens), jnp.bfloat16)]
+    return gradients(kernel, [(total, features)], arrays, old, (features // block,), [spec], scratch, after, 0.1)
 
 
 def piped(acts, grad_out, w_gate, w_up, w_down):
@@ -394,9 +404,9 @@
     whole, halves = (0, total), ((0, cut), (cut, total))
     back_weights = (w_gate, w_up)
 
-    def gather(value, parts, early=()):
-        pair = pack(value, swapped(value, "hid", 2), early)
-        own = arrange(pair, swapped(pair, "hid", 1), [value.shape[0] // parts] * parts)
+    def gather(value, parts, early=(), costs=(0.1, 0.1)):
+        pair = pack(value, swapped(value, "hid", 2), early, costs[0])
+        own = arrange(pair, swapped(pair, "hid", 1), [value.shape[0] // parts] * parts, costs[1])
         return [(array, shifted(array, "tok", 1), 0) for array in own]
 
     def gather_both(index, after, early=()):
@@ -406,7 +416,7 @@
 
     rows = heights[0]
     x, = gather(first_rows(acts, rows), 1)
-    dy, = gather(cut_rows(acts, grad_out, [(1, 0, rows)]), 1)
+    dy, = gather(cut_rows(acts, grad_out, [(1, 0, rows)]), 1, costs=(1.2, 5.0))
     inputs = [(x, dy), gather_both(1, (dy[0],))]
     gate_up = forward([(*x, False), (*x, False)], (w_gate, w_up), whole, rows)
     dhid = forward([(*dy, True)], (w_down,), whole, rows, (gate_up,))

time: 137 us -> 135 us (0.985)
    ppermute x14, waiting for transfers between devices: 40.3 us -> 36.6 us  [swapped(): return lax.ppermute(value, axis, [(i, i ^ bit) for i in range(n)])]
    ppermute x14, waiting for transfers between devices: 8.68 us -> 11.4 us  [shifted(): return lax.ppermute(value, axis, [(i, (i + step) % n) for i in range(n)])]
  transfers between devices with their start and end apart: 28 -> 28, of which waited for: 13 -> 15; matrix products, arithmetic and copies ran while one was open for 0% -> 0% of each run, Pallas kernels for 37% -> 36%
where the time goes in v9:
time: 135 us
  Pallas kernels  52.3 us (39%)
  waiting for transfers between devices  48 us (36%)
  starting transfers between devices  32.6 us (24%)
    ppermute x14, waiting for transfers between devices, swapped(): return lax.ppermute(value, axis, [(i, i ^ bit) for i in range(n)])  36.6 us
    pallas_call x31, Pallas kernels, local(): pl.pallas_call(body, out_shape=shapes, in_specs=[VMEM] * len(args) + [ANY...  33.1 us
    ppermute x14, starting transfers between devices, swapped(): return lax.ppermute(value, axis, [(i, i ^ bit) for i in range(n)])  24.3 us
    pallas_call x4, Pallas kernels, gradients(): pl.pallas_call(body, grid=grid, out_shape=[jax.ShapeDtypeStruct(shape, jn...  19.2 us
    ppermute x14, waiting for transfers between devices, shifted(): return lax.ppermute(value, axis, [(i, (i + step) % n) for i in range(n)])  11.4 us
    ppermute x14, starting transfers between devices, shifted(): return lax.ppermute(value, axis, [(i, (i + step) % n) for i in range(n)])  8.32 us
  transfers between devices with their start and end apart: 28, of which 15 were waited for; matrix products, arithmetic and copies ran while one was open for 0% of the time, Pallas kernels for 36%

profile of v9, /device:TPU:0, one launch (start us, length us, event | category | flops | bytes accessed | tf_op | source)
XLA Modules:
  0.0 134.9 jit_solution(14327947456037518047)
XLA Ops:
  0.6 0.9 copy-done.2
  1.6 4.1 %collective-permute-start.5 = (bf16[64,512]{1,0:T(8,128)(2,1)S(1)}, bf16[64,512]{1,0:T(8,128)(2,1)S(1)}, u32[]{:S(2)}, u32[]{:S(2)}) collective-permute-start(bf16[64,512]{1,0:T(8,128)(2,1)S(1)} %shard_map.91.refs_0_), channel_id=1, source_target_pairs={{0,8},{4,12},{8,0},{12,4},{1,9},{5,13},{9,1},{13,5},{2,10},{6,14},... | collective-permute-start | bytes 196616 | tf_op jit(solution)/shard_map/ppermute | solution.py:45
  5.7 3.6 %collective-permute-done.5.refs_1_ = bf16[64,512]{1,0:T(8,128)(2,1)S(1)} collective-permute-done((bf16[64,512]{1,0:T(8,128)(2,1)S(1)}, bf16[64,512]{1,0:T(8,128)(2,1)S(1)}, u32[]{:S(2)}, u32[]{:S(2)}) %collective-permute-start.5) | collective-permute-done | bytes 65568 | tf_op jit(solution)/shard_map/ppermute | solution.py:45
  9.3 0.6 collective-permute-start.6
  10.0 3.4 %collective-permute-start = (bf16[64,512]{1,0:T(8,128)(2,1)S(1)}, bf16[64,512]{1,0:T(8,128)(2,1)S(1)}, u32[]{:S(2)}, u32[]{:S(2)}) collective-permute-start(bf16[64,512]{1,0:T(8,128)(2,1)S(1)} %shard_map.84.refs_0_), channel_id=1, source_target_pairs={{0,8},{4,12},{8,0},{12,4},{1,9},{5,13},{9,1},{13,5},{2,10},{6,14},... | collective-permute-start | bytes 196616 | tf_op jit(solution)/shard_map/ppermute | solution.py:45
  13.4 1.7 %collective-permute-done.6.refs_1_ = bf16[64,1024]{1,0:T(8,128)(2,1)S(1)} collective-permute-done((bf16[64,1024]{1,0:T(8,128)(2,1)S(1)}, bf16[64,1024]{1,0:T(8,128)(2,1)S(1)}, u32[]{:S(2)}, u32[]{:S(2)}) %collective-permute-start.6) | collective-permute-done | bytes 131104 | tf_op jit(solution)/shard_map/ppermute | solution.py:45
  15.2 1.1 collective-permute-done.refs_1_
  16.3 1.9 %collective-permute-start.1 = (bf16[64,1024]{1,0:T(8,128)(2,1)S(1)}, bf16[64,1024]{1,0:T(8,128)(2,1)S(1)}, u32[]{:S(2)}, u32[]{:S(2)}) collective-permute-start(bf16[64,1024]{1,0:T(8,128)(2,1)S(1)} %shard_map.85.refs_0_), channel_id=1, source_target_pairs={{0,4},{4,0},{8,12},{12,8},{1,5},{5,1},{9,13},{13,9},{2,6},{6,2},{1... | collective-permute-start | bytes 393224 | tf_op jit(solution)/shard_map/ppermute | solution.py:45
  18.2 2.1 %shard_map.94.refs_3_.refs_0_ = bf16[256,1792]{1,0:T(8,128)(2,1)S(1)} custom-call(bf16[64,2048]{1,0:T(8,128)(2,1)S(1)} %shard_map.93.refs_0_.refs_2_, bf16[64,2048]{1,0:T(8,128)(2,1)S(1)} %collective-permute-done.7.refs_1_.refs_3_, bf16[64,2048]{1,0:T(8,128)(2,1)S(1)} %shard_map.93.refs_0_.refs_2_, ...), custom_call_target="tpu_custom_call" | custom-call | flops 345000000 | tf_op jit(solution)/shard_map/pallas_call | solution.py:100
  20.3 1.6 %collective-permute-start.9 = (bf16[256,1792]{1,0:T(8,128)(2,1)S(1)}, bf16[256,1792]{1,0:T(8,128)(2,1)S(1)}, u32[]{:S(2)}, u32[]{:S(2)}) collective-permute-start(bf16[256,1792]{1,0:T(8,128)(2,1)S(1)} %shard_map.94.refs_3_.refs_0_), channel_id=1, source_target_pairs={{0,2},{2,0},{1,3},{3,1},{4,6},{6,4},{5,7},{7,5},{8,10},{10,8},{9,1... | collective-permute-start | bytes 2752520 | tf_op jit(solution)/shard_map/ppermute | solution.py:40
  22.0 2.4 %collective-permute-start.2 = (bf16[128,512]{1,0:T(8,128)(2,1)S(1)}, bf16[128,512]{1,0:T(8,128)(2,1)S(1)}, u32[]{:S(2)}, u32[]{:S(2)}) collective-permute-start(bf16[128,512]{1,0:T(8,128)(2,1)S(1)} %shard_map.87.refs_0_), channel_id=1, source_target_pairs={{0,8},{4,12},{8,0},{12,4},{1,9},{5,13},{9,1},{13,5},{2,10},{6,14},... | collective-permute-start | bytes 393224 | tf_op jit(solution)/shard_map/ppermute | solution.py:45
  24.4 7.3 %collective-permute-done.2.refs_1_ = bf16[128,512]{1,0:T(8,128)(2,1)S(1)} collective-permute-done((bf16[128,512]{1,0:T(8,128)(2,1)S(1)}, bf16[128,512]{1,0:T(8,128)(2,1)S(1)}, u32[]{:S(2)}, u32[]{:S(2)}) %collective-permute-start.2) | collective-permute-done | bytes 131104 | tf_op jit(solution)/shard_map/ppermute | solution.py:45
  31.7 0.5 collective-permute-start.3
  32.2 2.5 %shard_map.95.refs_9_.refs_1_ = bf16[128,1792]{1,0:T(8,128)(2,1)S(1)} custom-call(bf16[64,2048]{1,0:T(8,128)(2,1)S(1)} %shard_map.86.refs_2_.refs_0_, bf16[64,2048]{1,0:T(8,128)(2,1)S(1)} %collective-permute-done.8.refs_1_, bf16[1792,2048]{1,0:T(8,128)(2,1)S(1)} %bitcast.1, bf16[256,1792]{1,0:T(8,128)(2,1)S(1)} %shard_map.94.refs_3_.refs_0_), custom_call_target="tpu_custom_call" | custom-call | flops 345000000 | tf_op jit(solution)/shard_map/pallas_call | solution.py:100
  34.7 1.6 %collective-permute-start.10 = (bf16[128,1792]{1,0:T(8,128)(2,1)S(1)}, bf16[128,1792]{1,0:T(8,128)(2,1)S(1)}, u32[]{:S(2)}, u32[]{:S(2)}) collective-permute-start(bf16[128,1792]{1,0:T(8,128)(2,1)S(1)} %shard_map.95.refs_9_.refs_1_), channel_id=1, source_target_pairs={{0,2},{2,0},{1,3},{3,1},{4,6},{6,4},{5,7},{7,5},{8,10},{10,8},{9,1... | collective-permute-start | bytes 1376264 | tf_op jit(solution)/shard_map/ppermute | solution.py:40
  36.3 3.4 %collective-permute-done.3.refs_1_ = bf16[128,1024]{1,0:T(8,128)(2,1)S(1)} collective-permute-done((bf16[128,1024]{1,0:T(8,128)(2,1)S(1)}, bf16[128,1024]{1,0:T(8,128)(2,1)S(1)}, u32[]{:S(2)}, u32[]{:S(2)}) %collective-permute-start.3) | collective-permute-done | bytes 262176 | tf_op jit(solution)/shard_map/ppermute | solution.py:45
  39.8 0.5 collective-permute-start.12
  40.3 2.5 %collective-permute-start.4 = (bf16[128,512]{1,0:T(8,128)(2,1)S(1)}, bf16[128,512]{1,0:T(8,128)(2,1)S(1)}, u32[]{:S(2)}, u32[]{:S(2)}) collective-permute-start(bf16[128,512]{1,0:T(8,128)(2,1)S(1)} %shard_map.90.refs_0_), channel_id=1, source_target_pairs={{0,8},{4,12},{8,0},{12,4},{1,9},{5,13},{9,1},{13,5},{2,10},{6,14},... | collective-permute-start | bytes 393224 | tf_op jit(solution)/shard_map/ppermute | solution.py:45
  42.8 4.4 %shard_map.96.refs_6_.refs_0_ = bf16[384,1792]{1,0:T(8,128)(2,1)S(1)} custom-call(bf16[64,2048]{1,0:T(8,128)(2,1)S(1)} %get-tuple-element.48.refs_2_.refs_0_, bf16[64,2048]{1,0:T(8,128)(2,1)S(1)} %collective-permute-done.11.refs_1_.refs_3_, bf16[64,2048]{1,0:T(8,128)(2,1)S(1)} %get-tuple-element.48.refs_2_.refs_0_, ...), custom_call_target="tpu_custom_call" | custom-call | flops 345000000 | tf_op jit(solution)/shard_map/pallas_call | solution.py:100
  47.2 1.6 %collective-permute-start.19 = (bf16[384,1792]{1,0:T(8,128)(2,1)S(1)}, bf16[384,1792]{1,0:T(8,128)(2,1)S(1)}, u32[]{:S(2)}, u32[]{:S(2)}) collective-permute-start(bf16[384,1792]{1,0:T(8,128)(2,1)S(1)} %shard_map.96.refs_6_.refs_0_), channel_id=1, source_target_pairs={{0,2},{2,0},{1,3},{3,1},{4,6},{6,4},{5,7},{7,5},{8,10},{10,8},{9,1... | collective-permute-start | bytes 4128776 | tf_op jit(solution)/shard_map/ppermute | solution.py:40
  48.8 4.4 %collective-permute-done.10.refs_3_ = bf16[128,1792]{1,0:T(8,128)(2,1)S(1)} collective-permute-done((bf16[128,1792]{1,0:T(8,128)(2,1)S(1)}, bf16[128,1792]{1,0:T(8,128)(2,1)S(1)}, u32[]{:S(2)}, u32[]{:S(2)}) %collective-permute-start.10) | collective-permute-done | bytes 458784 | tf_op jit(solution)/shard_map/ppermute | solution.py:40
  53.2 5.8 %shard_map.97 = (bf16[1792,128]{1,0:T(8,128)(2,1)S(1)}, bf16[128,1792]{1,0:T(8,128)(2,1)S(1)}, bf16[128,1792]{1,0:T(8,128)(2,1)S(1)}, f32[64,2048]{1,0:T(8,128)S(1)}, bf16[64,2048]{1,0:T(8,128)(2,1)S(1)}) custom-call(bf16[256,1792]{1,0:T(8,128)(2,1)S(1)} %shard_map.94.refs_3_.refs_0_, bf16[128,1792]{1,0:T(8,128)(2,1)S(1)} %shard_map.95.refs_9_.refs_1_, ...), custom_call_target="tpu_custom_call" | custom-call | flops 69000003584 | tf_op jit(solution)/shard_map/pallas_call | solution.py:100
  59.2 6.3 %collective-permute-done.13.refs_1_ = bf16[128,1024]{1,0:T(8,128)(2,1)S(1)} collective-permute-done((bf16[128,1024]{1,0:T(8,128)(2,1)S(1)}, bf16[128,1024]{1,0:T(8,128)(2,1)S(1)}, u32[]{:S(2)}, u32[]{:S(2)}) %collective-permute-start.13) | collective-permute-done | bytes 262176 | tf_op jit(solution)/shard_map/ppermute | solution.py:45
  65.6 0.5 collective-permute-start.15
  66.3 5.5 %collective-permute-done.20.refs_1_ = bf16[64,1024]{1,0:T(8,128)(2,1)S(1)} collective-permute-done((bf16[64,1024]{1,0:T(8,128)(2,1)S(1)}, bf16[64,1024]{1,0:T(8,128)(2,1)S(1)}, u32[]{:S(2)}, u32[]{:S(2)}) %collective-permute-start.20) | collective-permute-done | bytes 131104 | tf_op jit(solution)/shard_map/ppermute | solution.py:45
  71.8 2.6 %shard_map.101.refs_9_.refs_0_ = bf16[384,1024]{1,0:T(8,128)(2,1)S(1)} custom-call(bf16[64,2048]{1,0:T(8,128)(2,1)S(1)} %get-tuple-element.51.refs_0_.refs_2_.refs_4_, bf16[64,2048]{1,0:T(8,128)(2,1)S(1)} %collective-permute-done.14.refs_1_.refs_3_.refs_5_, bf16[64,2048]{1,0:T(8,128)(2,1)S(1)} %get-tuple-element.51.refs_0_.refs_2_.refs_4_, ...), custom_call_target="tpu_custom_call" | custom-call | flops 345000000 | tf_op jit(solution)/shard_map/pallas_call | solution.py:100
  74.4 1.8 %collective-permute-start.18 = (bf16[384,1024]{1,0:T(8,128)(2,1)S(1)}, bf16[384,1024]{1,0:T(8,128)(2,1)S(1)}, u32[]{:S(2)}, u32[]{:S(2)}) collective-permute-start(bf16[384,1024]{1,0:T(8,128)(2,1)S(1)} %shard_map.101.refs_9_.refs_0_), channel_id=1, source_target_pairs={{0,2},{2,0},{1,3},{3,1},{4,6},{6,4},{5,7},{7,5},{8,10},{10,8},{9,1... | collective-permute-start | bytes 2359304 | tf_op jit(solution)/shard_map/ppermute | solution.py:40
  76.2 2.0 %shard_map.102.refs_6_.refs_0_ = bf16[384,768]{1,0:T(8,128)(2,1)S(1)} custom-call(bf16[64,2048]{1,0:T(8,128)(2,1)S(1)} %get-tuple-element.51.refs_0_.refs_2_.refs_4_, bf16[64,2048]{1,0:T(8,128)(2,1)S(1)} %collective-permute-done.14.refs_1_.refs_3_.refs_5_, bf16[64,2048]{1,0:T(8,128)(2,1)S(1)} %get-tuple-element.51.refs_0_.refs_2_.refs_4_, ...), custom_call_target="tpu_custom_call" | custom-call | flops 345000000 | tf_op jit(solution)/shard_map/pallas_call | solution.py:100
  78.5 0.6 shard_map.103.refs_4_.refs_0_
  79.3 3.4 %collective-permute-done.19.refs_1_ = bf16[384,1792]{1,0:T(8,128)(2,1)S(1)} collective-permute-done((bf16[384,1792]{1,0:T(8,128)(2,1)S(1)}, bf16[384,1792]{1,0:T(8,128)(2,1)S(1)}, u32[]{:S(2)}, u32[]{:S(2)}) %collective-permute-start.19) | collective-permute-done | bytes 1376288 | tf_op jit(solution)/shard_map/ppermute | solution.py:40
  82.7 5.8 %shard_map.106 = (bf16[1792,128]{1,0:T(8,128)(2,1)S(1)}, bf16[128,1792]{1,0:T(8,128)(2,1)S(1)}, bf16[128,1792]{1,0:T(8,128)(2,1)S(1)}, f32[64,2048]{1,0:T(8,128)S(1)}, bf16[64,2048]{1,0:T(8,128)(2,1)S(1)}) custom-call(bf16[384,1792]{1,0:T(8,128)(2,1)S(1)} %shard_map.96.refs_6_.refs_0_, bf16[384,1792]{1,0:T(8,128)(2,1)S(1)} %collective-permute-done.19.refs_1_, ...), custom_call_target="tpu_custom_call" | custom-call | flops 69000003584 | tf_op jit(solution)/shard_map/pallas_call | solution.py:100
  88.6 1.5 %collective-permute-done.22.refs_1_ = bf16[64,2048]{1,0:T(8,128)(2,1)S(1)} collective-permute-done((bf16[64,2048]{1,0:T(8,128)(2,1)S(1)}, bf16[64,2048]{1,0:T(8,128)(2,1)S(1)}, u32[]{:S(2)}, u32[]{:S(2)}) %collective-permute-start.22) | collective-permute-done | bytes 262176 | tf_op jit(solution)/shard_map/ppermute | solution.py:40
  90.2 3.4 %collective-permute-start.21 = (bf16[64,512]{1,0:T(8,128)(2,1)S(1)}, bf16[64,512]{1,0:T(8,128)(2,1)S(1)}, u32[]{:S(2)}, u32[]{:S(2)}) collective-permute-start(bf16[64,512]{1,0:T(8,128)(2,1)S(1)} %get-tuple-element.59), channel_id=1, source_target_pairs={{0,8},{4,12},{8,0},{12,4},{1,9},{5,13},{9,1},{13,5},{2,10},{6,14},... | collective-permute-start | bytes 196616 | tf_op jit(solution)/shard_map/ppermute | solution.py:45
  93.7 2.3 %collective-permute-done.21.refs_1_ = bf16[64,512]{1,0:T(8,128)(2,1)S(1)} collective-permute-done((bf16[64,512]{1,0:T(8,128)(2,1)S(1)}, bf16[64,512]{1,0:T(8,128)(2,1)S(1)}, u32[]{:S(2)}, u32[]{:S(2)}) %collective-permute-start.21) | collective-permute-done | bytes 65568 | tf_op jit(solution)/shard_map/ppermute | solution.py:45
  96.0 1.2 collective-permute-done.23.refs_1_
  97.2 1.8 %collective-permute-start.24 = (bf16[64,512]{1,0:T(8,128)(2,1)S(1)}, bf16[64,512]{1,0:T(8,128)(2,1)S(1)}, u32[]{:S(2)}, u32[]{:S(2)}) collective-permute-start(bf16[64,512]{1,0:T(8,128)(2,1)S(1)} %get-tuple-element.75), channel_id=1, source_target_pairs={{0,8},{4,12},{8,0},{12,4},{1,9},{5,13},{9,1},{13,5},{2,10},{6,14},... | collective-permute-start | bytes 196616 | tf_op jit(solution)/shard_map/ppermute | solution.py:45
  99.0 0.6 collective-permute-done.18.refs_1_
  99.5 3.4 %shard_map.108 = (bf16[1024,128]{1,0:T(8,128)(2,1)S(1)}, bf16[128,1024]{1,0:T(8,128)(2,1)S(1)}, bf16[128,1024]{1,0:T(8,128)(2,1)S(1)}, f32[128,2048]{1,0:T(8,128)S(1)}) custom-call(bf16[384,1024]{1,0:T(8,128)(2,1)S(1)} %shard_map.101.refs_9_.refs_0_, bf16[384,1024]{1,0:T(8,128)(2,1)S(1)} %collective-permute-done.18.refs_1_, bf16[2048,1792]{1,0:T(8,128)(2,1)S(1)} %copy-done, ...), custom_call_target="tpu_custom_call" | custom-call | flops 1150000000 | tf_op jit(solution)/shard_map/pallas_call | solution.py:100
  102.9 4.3 %shard_map.111 = (bf16[1792,2048]{1,0:T(8,128)(2,1)}, bf16[16,128]{1,0:T(8,128)(2,1)S(1)}) custom-call(bf16[1792,128]{1,0:T(8,128)(2,1)S(1)} %get-tuple-element.70.refs_0_, bf16[1792,128]{1,0:T(8,128)(2,1)S(1)} %get-tuple-element.71.refs_1_, bf16[1024,128]{1,0:T(8,128)(2,1)S(1)} %get-tuple-element.72.refs_2_, ...), custom_call_target="tpu_custom_call" | custom-call | flops 115000000 | tf_op jit(solution)/shard_map/pallas_call | solution.py:315
  107.2 6.3 %shard_map.112 = (bf16[2048,1792]{1,0:T(8,128)(2,1)}, bf16[2048,1792]{1,0:T(8,128)(2,1)}, bf16[16,128]{1,0:T(8,128)(2,1)S(1)}) custom-call(bf16[2048,384]{1,0:T(8,128)(2,1)S(1)} %shard_map.103.refs_4_.refs_0_, bf16[128,1792]{1,0:T(8,128)(2,1)S(1)} %get-tuple-element.50.refs_2_.refs_1_, bf16[128,1792]{1,0:T(8,128)(2,1)S(1)} %get-tuple-element.58.refs_4_.refs_2_, ...), custom_call_target="tpu_custom_call" | custom-call | flops 115000000 | tf_op jit(solution)/shard_map/pallas_call | solution.py:315
  113.5 2.6 %shard_map.114 = (bf16[768,128]{1,0:T(8,128)(2,1)S(1)}, bf16[128,768]{1,0:T(8,128)(2,1)S(1)}, bf16[128,768]{1,0:T(8,128)(2,1)S(1)}, f32[64,2048]{1,0:T(8,128)S(1)}, bf16[64,2048]{1,0:T(8,128)(2,1)S(1)}) custom-call(bf16[384,768]{1,0:T(8,128)(2,1)S(1)} %shard_map.102.refs_6_.refs_0_, bf16[384,768]{1,0:T(8,128)(2,1)S(1)} %collective-permute-done.17.refs_1_, ...), custom_call_target="tpu_custom_call" | custom-call | flops 1150000000 | tf_op jit(solution)/shard_map/pallas_call | solution.py:100
  116.2 1.5 %collective-permute-done.25.refs_1_ = bf16[64,2048]{1,0:T(8,128)(2,1)S(1)} collective-permute-done((bf16[64,2048]{1,0:T(8,128)(2,1)S(1)}, bf16[64,2048]{1,0:T(8,128)(2,1)S(1)}, u32[]{:S(2)}, u32[]{:S(2)}) %collective-permute-start.25) | collective-permute-done | bytes 262176 | tf_op jit(solution)/shard_map/ppermute | solution.py:40
  117.8 1.3 collective-permute-start.26
  119.1 4.3 %collective-permute-done.26.refs_1_ = bf16[64,1024]{1,0:T(8,128)(2,1)S(1)} collective-permute-done((bf16[64,1024]{1,0:T(8,128)(2,1)S(1)}, bf16[64,1024]{1,0:T(8,128)(2,1)S(1)}, u32[]{:S(2)}, u32[]{:S(2)}) %collective-permute-start.26) | collective-permute-done | bytes 131104 | tf_op jit(solution)/shard_map/ppermute | solution.py:45
  123.4 2.1 %collective-permute-start.27 = (bf16[64,512]{1,0:T(8,128)(2,1)S(1)}, bf16[64,512]{1,0:T(8,128)(2,1)S(1)}, u32[]{:S(2)}, u32[]{:S(2)}) collective-permute-start(bf16[64,512]{1,0:T(8,128)(2,1)S(1)} %get-tuple-element.81), channel_id=1, source_target_pairs={{0,8},{4,12},{8,0},{12,4},{1,9},{5,13},{9,1},{13,5},{2,10},{6,14},... | collective-permute-start | bytes 196616 | tf_op jit(solution)/shard_map/ppermute | solution.py:45
  125.5 3.6 %shard_map.118 = (bf16[1792,2048]{1,0:T(8,128)(2,1)}, bf16[16,128]{1,0:T(8,128)(2,1)S(1)}) custom-call(bf16[1792,128]{1,0:T(8,128)(2,1)S(1)} %get-tuple-element.70.refs_0_, bf16[1792,128]{1,0:T(8,128)(2,1)S(1)} %get-tuple-element.71.refs_1_, bf16[768,128]{1,0:T(8,128)(2,1)S(1)} %get-tuple-element.86.refs_2_, ...), custom_call_target="tpu_custom_call", output_to_operand_aliasing={{0}: (4, {})} | custom-call | flops 115000000 | tf_op jit(solution)/shard_map/pallas_call | solution.py:315
  129.1 5.1 %shard_map.119 = (bf16[2048,1792]{1,0:T(8,128)(2,1)}, bf16[2048,1792]{1,0:T(8,128)(2,1)}, bf16[16,128]{1,0:T(8,128)(2,1)}) custom-call(bf16[2048,384]{1,0:T(8,128)(2,1)S(1)} %shard_map.103.refs_4_.refs_0_, bf16[128,1792]{1,0:T(8,128)(2,1)S(1)} %get-tuple-element.50.refs_2_.refs_1_, ...), custom_call_target="tpu_custom_call", output_to_operand_aliasing={{0}: (7, {}), {1}: (8, {})} | custom-call | flops 115000000 | tf_op jit(solution)/shard_map/pallas_call | solution.py:315
  134.2 0.7 shard_map.117
  (59 shorter events, 1.7 us)
Async XLA Ops:
  0.6 0.9 copy-start.2
  1.6 8.4 %copy-start.3 = (bf16[192,512]{1,0:T(8,128)(2,1)S(1)}, bf16[192,512]{1,0:T(8,128)(2,1)}, u32[]{:S(2)}) copy-start(bf16[192,512]{1,0:T(8,128)(2,1)} %source.1) | copy-start | bytes 589828
  1.6 8.4 %copy-start.4 = (bf16[192,512]{1,0:T(8,128)(2,1)S(1)}, bf16[192,512]{1,0:T(8,128)(2,1)}, u32[]{:S(2)}) copy-start(bf16[192,512]{1,0:T(8,128)(2,1)} %refs_1_.5) | copy-start | bytes 589828
  1.6 16.6 %copy-start = (bf16[2048,1792]{1,0:T(8,128)(2,1)S(1)}, bf16[2048,1792]{1,0:T(8,128)(2,1)}, u32[]{:S(2)}) copy-start(bf16[2048,1792]{1,0:T(8,128)(2,1)} %refs_2_.7) | copy-start | bytes 22020100
  1.6 16.6 %copy-start.1 = (bf16[2048,1792]{1,0:T(8,128)(2,1)S(1)}, bf16[2048,1792]{1,0:T(8,128)(2,1)}, u32[]{:S(2)}) copy-start(bf16[2048,1792]{1,0:T(8,128)(2,1)} %refs_3_.5) | copy-start | bytes 22020100
  1.6 7.8 %collective-permute-start.5 = (bf16[64,512]{1,0:T(8,128)(2,1)S(1)}, bf16[64,512]{1,0:T(8,128)(2,1)S(1)}, u32[]{:S(2)}, u32[]{:S(2)}) collective-permute-start(bf16[64,512]{1,0:T(8,128)(2,1)S(1)} %shard_map.91.refs_0_), channel_id=1, source_target_pairs={{0,8},{4,12},{8,0},{12,4},{1,9},{5,13},{9,1},{13,5},{2,10},{6,14},... | collective-permute-start | bytes 196616 | tf_op jit(solution)/shard_map/ppermute | solution.py:45
  9.3 5.7 %collective-permute-start.6 = (bf16[64,1024]{1,0:T(8,128)(2,1)S(1)}, bf16[64,1024]{1,0:T(8,128)(2,1)S(1)}, u32[]{:S(2)}, u32[]{:S(2)}) collective-permute-start(bf16[64,1024]{1,0:T(8,128)(2,1)S(1)} %shard_map.92.refs_0_), channel_id=1, source_target_pairs={{0,4},{4,0},{8,12},{12,8},{1,5},{5,1},{9,13},{13,9},{2,6},{6,2},{1... | collective-permute-start | bytes 393224 | tf_op jit(solution)/shard_map/ppermute | solution.py:45
  10.0 6.3 %collective-permute-start = (bf16[64,512]{1,0:T(8,128)(2,1)S(1)}, bf16[64,512]{1,0:T(8,128)(2,1)S(1)}, u32[]{:S(2)}, u32[]{:S(2)}) collective-permute-start(bf16[64,512]{1,0:T(8,128)(2,1)S(1)} %shard_map.84.refs_0_), channel_id=1, source_target_pairs={{0,8},{4,12},{8,0},{12,4},{1,9},{5,13},{9,1},{13,5},{2,10},{6,14},... | collective-permute-start | bytes 196616 | tf_op jit(solution)/shard_map/ppermute | solution.py:45
  15.1 3.0 %collective-permute-start.7 = (bf16[64,2048]{1,0:T(8,128)(2,1)S(1)}, bf16[64,2048]{1,0:T(8,128)(2,1)S(1)}, u32[]{:S(2)}, u32[]{:S(2)}) collective-permute-start(bf16[64,2048]{1,0:T(8,128)(2,1)S(1)} %shard_map.93.refs_0_.refs_2_), channel_id=1, source_target_pairs={{0,1},{1,0},{2,3},{3,2},{4,5},{5,4},{6,7},{7,6},{8,9},{9,8},{10,11... | collective-permute-start | bytes 786440 | tf_op jit(solution)/shard_map/ppermute | solution.py:40
  16.3 5.6 %collective-permute-start.1 = (bf16[64,1024]{1,0:T(8,128)(2,1)S(1)}, bf16[64,1024]{1,0:T(8,128)(2,1)S(1)}, u32[]{:S(2)}, u32[]{:S(2)}) collective-permute-start(bf16[64,1024]{1,0:T(8,128)(2,1)S(1)} %shard_map.85.refs_0_), channel_id=1, source_target_pairs={{0,4},{4,0},{8,12},{12,8},{1,5},{5,1},{9,13},{13,9},{2,6},{6,2},{1... | collective-permute-start | bytes 393224 | tf_op jit(solution)/shard_map/ppermute | solution.py:45
  18.2 14.0 %slice-start = ((s8[7340032]{0:T(1024)(128)(4,1)}), s8[4194304]{0:T(1024)(128)(4,1)S(1)}, s32[]{:S(2)}) async-start(s8[7340032]{0:T(1024)(128)(4,1)} %bitcast), calls=%async_computation | async-start | bytes 8388608
  20.3 11.9 %slice-start.1 = ((s8[7340032]{0:T(1024)(128)(4,1)}), s8[3145728]{0:T(1024)(128)(4,1)S(1)}, s32[]{:S(2)}) async-start(s8[7340032]{0:T(1024)(128)(4,1)} %bitcast), calls=%async_computation.1 | async-start | bytes 6291456
  20.3 32.9 %collective-permute-start.9 = (bf16[256,1792]{1,0:T(8,128)(2,1)S(1)}, bf16[256,1792]{1,0:T(8,128)(2,1)S(1)}, u32[]{:S(2)}, u32[]{:S(2)}) collective-permute-start(bf16[256,1792]{1,0:T(8,128)(2,1)S(1)} %shard_map.94.refs_3_.refs_0_), channel_id=1, source_target_pairs={{0,2},{2,0},{1,3},{3,1},{4,6},{6,4},{5,7},{7,5},{8,10},{10,8},{9,1... | collective-permute-start | bytes 2752520 | tf_op jit(solution)/shard_map/ppermute | solution.py:40
  21.9 10.3 %collective-permute-start.8 = (bf16[64,2048]{1,0:T(8,128)(2,1)S(1)}, bf16[64,2048]{1,0:T(8,128)(2,1)S(1)}, u32[]{:S(2)}, u32[]{:S(2)}) collective-permute-start(bf16[64,2048]{1,0:T(8,128)(2,1)S(1)} %shard_map.86.refs_2_.refs_0_), channel_id=1, source_target_pairs={{0,1},{1,0},{2,3},{3,2},{4,5},{5,4},{6,7},{7,6},{8,9},{9,8},{10,11... | collective-permute-start | bytes 786440 | tf_op jit(solution)/shard_map/ppermute | solution.py:40
  22.0 9.7 %collective-permute-start.2 = (bf16[128,512]{1,0:T(8,128)(2,1)S(1)}, bf16[128,512]{1,0:T(8,128)(2,1)S(1)}, u32[]{:S(2)}, u32[]{:S(2)}) collective-permute-start(bf16[128,512]{1,0:T(8,128)(2,1)S(1)} %shard_map.87.refs_0_), channel_id=1, source_target_pairs={{0,8},{4,12},{8,0},{12,4},{1,9},{5,13},{9,1},{13,5},{2,10},{6,14},... | collective-permute-start | bytes 393224 | tf_op jit(solution)/shard_map/ppermute | solution.py:45
  31.7 8.0 %collective-permute-start.3 = (bf16[128,1024]{1,0:T(8,128)(2,1)S(1)}, bf16[128,1024]{1,0:T(8,128)(2,1)S(1)}, u32[]{:S(2)}, u32[]{:S(2)}) collective-permute-start(bf16[128,1024]{1,0:T(8,128)(2,1)S(1)} %shard_map.88.refs_0_), channel_id=1, source_target_pairs={{0,4},{4,0},{8,12},{12,8},{1,5},{5,1},{9,13},{13,9},{2,6},{6,2},{1... | collective-permute-start | bytes 786440 | tf_op jit(solution)/shard_map/ppermute | solution.py:45
  34.7 18.5 %collective-permute-start.10 = (bf16[128,1792]{1,0:T(8,128)(2,1)S(1)}, bf16[128,1792]{1,0:T(8,128)(2,1)S(1)}, u32[]{:S(2)}, u32[]{:S(2)}) collective-permute-start(bf16[128,1792]{1,0:T(8,128)(2,1)S(1)} %shard_map.95.refs_9_.refs_1_), channel_id=1, source_target_pairs={{0,2},{2,0},{1,3},{3,1},{4,6},{6,4},{5,7},{7,5},{8,10},{10,8},{9,1... | collective-permute-start | bytes 1376264 | tf_op jit(solution)/shard_map/ppermute | solution.py:40
  39.7 3.1 %collective-permute-start.11 = (bf16[64,2048]{1,0:T(8,128)(2,1)S(1)}, bf16[64,2048]{1,0:T(8,128)(2,1)S(1)}, u32[]{:S(2)}, u32[]{:S(2)}) collective-permute-start(bf16[64,2048]{1,0:T(8,128)(2,1)S(1)} %get-tuple-element.48.refs_2_.refs_0_), channel_id=1, source_target_pairs={{0,1},{1,0},{2,3},{3,2},{4,5},{5,4},{6,7},{7,6},{8,9},{9,8},{10,11... | collective-permute-start | bytes 786440 | tf_op jit(solution)/shard_map/ppermute | solution.py:40
  39.8 3.0 %collective-permute-start.12 = (bf16[64,2048]{1,0:T(8,128)(2,1)S(1)}, bf16[64,2048]{1,0:T(8,128)(2,1)S(1)}, u32[]{:S(2)}, u32[]{:S(2)}) collective-permute-start(bf16[64,2048]{1,0:T(8,128)(2,1)S(1)} %get-tuple-element.49.refs_4_.refs_2_), channel_id=1, source_target_pairs={{0,1},{1,0},{2,3},{3,2},{4,5},{5,4},{6,7},{7,6},{8,9},{9,8},{10,11... | collective-permute-start | bytes 786440 | tf_op jit(solution)/shard_map/ppermute | solution.py:40
  40.3 18.7 %collective-permute-start.4 = (bf16[128,512]{1,0:T(8,128)(2,1)S(1)}, bf16[128,512]{1,0:T(8,128)(2,1)S(1)}, u32[]{:S(2)}, u32[]{:S(2)}) collective-permute-start(bf16[128,512]{1,0:T(8,128)(2,1)S(1)} %shard_map.90.refs_0_), channel_id=1, source_target_pairs={{0,8},{4,12},{8,0},{12,4},{1,9},{5,13},{9,1},{13,5},{2,10},{6,14},... | collective-permute-start | bytes 393224 | tf_op jit(solution)/shard_map/ppermute | solution.py:45
  47.2 35.5 %collective-permute-start.19 = (bf16[384,1792]{1,0:T(8,128)(2,1)S(1)}, bf16[384,1792]{1,0:T(8,128)(2,1)S(1)}, u32[]{:S(2)}, u32[]{:S(2)}) collective-permute-start(bf16[384,1792]{1,0:T(8,128)(2,1)S(1)} %shard_map.96.refs_6_.refs_0_), channel_id=1, source_target_pairs={{0,2},{2,0},{1,3},{3,1},{4,6},{6,4},{5,7},{7,5},{8,10},{10,8},{9,1... | collective-permute-start | bytes 4128776 | tf_op jit(solution)/shard_map/ppermute | solution.py:40
  59.1 6.4 %collective-permute-start.13 = (bf16[128,1024]{1,0:T(8,128)(2,1)S(1)}, bf16[128,1024]{1,0:T(8,128)(2,1)S(1)}, u32[]{:S(2)}, u32[]{:S(2)}) collective-permute-start(bf16[128,1024]{1,0:T(8,128)(2,1)S(1)} %shard_map.98.refs_0_), channel_id=1, source_target_pairs={{0,4},{4,0},{8,12},{12,8},{1,5},{5,1},{9,13},{13,9},{2,6},{6,2},{1... | collective-permute-start | bytes 786440 | tf_op jit(solution)/shard_map/ppermute | solution.py:45
  59.1 7.0 %collective-permute-start.16 = (bf16[64,2048]{1,0:T(8,128)(2,1)S(1)}, bf16[64,2048]{1,0:T(8,128)(2,1)S(1)}, u32[]{:S(2)}, u32[]{:S(2)}) collective-permute-start(bf16[64,2048]{1,0:T(8,128)(2,1)S(1)} %get-tuple-element.54), channel_id=1, source_target_pairs={{0,1},{1,0},{2,3},{3,2},{4,5},{5,4},{6,7},{7,6},{8,9},{9,8},{10,11... | collective-permute-start | bytes 786440 | tf_op jit(solution)/shard_map/ppermute | solution.py:40
  65.5 6.2 %collective-permute-start.14 = (bf16[64,2048]{1,0:T(8,128)(2,1)S(1)}, bf16[64,2048]{1,0:T(8,128)(2,1)S(1)}, u32[]{:S(2)}, u32[]{:S(2)}) collective-permute-start(bf16[64,2048]{1,0:T(8,128)(2,1)S(1)} %get-tuple-element.51.refs_0_.refs_2_.refs_4_), channel_id=1, source_target_pairs={{0,1},{1,0},{2,3},{3,2},{4,5},{5,4},{6,7},{7,6},{8,9},{9,8},{10,11... | collective-permute-start | bytes 786440 | tf_op jit(solution)/shard_map/ppermute | solution.py:40
  65.6 6.1 %collective-permute-start.15 = (bf16[64,2048]{1,0:T(8,128)(2,1)S(1)}, bf16[64,2048]{1,0:T(8,128)(2,1)S(1)}, u32[]{:S(2)}, u32[]{:S(2)}) collective-permute-start(bf16[64,2048]{1,0:T(8,128)(2,1)S(1)} %get-tuple-element.52.refs_4_), channel_id=1, source_target_pairs={{0,1},{1,0},{2,3},{3,2},{4,5},{5,4},{6,7},{7,6},{8,9},{9,8},{10,11... | collective-permute-start | bytes 786440 | tf_op jit(solution)/shard_map/ppermute | solution.py:40
  66.2 5.5 %collective-permute-start.20 = (bf16[64,1024]{1,0:T(8,128)(2,1)S(1)}, bf16[64,1024]{1,0:T(8,128)(2,1)S(1)}, u32[]{:S(2)}, u32[]{:S(2)}) collective-permute-start(bf16[64,1024]{1,0:T(8,128)(2,1)S(1)} %get-tuple-element.56), channel_id=1, source_target_pairs={{0,4},{4,0},{8,12},{12,8},{1,5},{5,1},{9,13},{13,9},{2,6},{6,2},{1... | collective-permute-start | bytes 393224 | tf_op jit(solution)/shard_map/ppermute | solution.py:45
  74.4 25.2 %collective-permute-start.18 = (bf16[384,1024]{1,0:T(8,128)(2,1)S(1)}, bf16[384,1024]{1,0:T(8,128)(2,1)S(1)}, u32[]{:S(2)}, u32[]{:S(2)}) collective-permute-start(bf16[384,1024]{1,0:T(8,128)(2,1)S(1)} %shard_map.101.refs_9_.refs_0_), channel_id=1, source_target_pairs={{0,2},{2,0},{1,3},{3,1},{4,6},{6,4},{5,7},{7,5},{8,10},{10,8},{9,1... | collective-permute-start | bytes 2359304 | tf_op jit(solution)/shard_map/ppermute | solution.py:40
  78.2 35.3 %collective-permute-start.17 = (bf16[384,768]{1,0:T(8,128)(2,1)S(1)}, bf16[384,768]{1,0:T(8,128)(2,1)S(1)}, u32[]{:S(2)}, u32[]{:S(2)}) collective-permute-start(bf16[384,768]{1,0:T(8,128)(2,1)S(1)} %shard_map.102.refs_6_.refs_0_), channel_id=1, source_target_pairs={{0,2},{2,0},{1,3},{3,1},{4,6},{6,4},{5,7},{7,5},{8,10},{10,8},{9,1... | collective-permute-start | bytes 1769480 | tf_op jit(solution)/shard_map/ppermute | solution.py:40
  88.5 1.6 %collective-permute-start.22 = (bf16[64,2048]{1,0:T(8,128)(2,1)S(1)}, bf16[64,2048]{1,0:T(8,128)(2,1)S(1)}, u32[]{:S(2)}, u32[]{:S(2)}) collective-permute-start(bf16[64,2048]{1,0:T(8,128)(2,1)S(1)} %get-tuple-element.66), channel_id=1, source_target_pairs={{0,1},{1,0},{2,3},{3,2},{4,5},{5,4},{6,7},{7,6},{8,9},{9,8},{10,11... | collective-permute-start | bytes 786440 | tf_op jit(solution)/shard_map/ppermute | solution.py:40
  90.2 7.0 %collective-permute-start.23 = (bf16[64,1024]{1,0:T(8,128)(2,1)S(1)}, bf16[64,1024]{1,0:T(8,128)(2,1)S(1)}, u32[]{:S(2)}, u32[]{:S(2)}) collective-permute-start(bf16[64,1024]{1,0:T(8,128)(2,1)S(1)} %get-tuple-element.68), channel_id=1, source_target_pairs={{0,4},{4,0},{8,12},{12,8},{1,5},{5,1},{9,13},{13,9},{2,6},{6,2},{1... | collective-permute-start | bytes 393224 | tf_op jit(solution)/shard_map/ppermute | solution.py:45
  90.2 5.8 %collective-permute-start.21 = (bf16[64,512]{1,0:T(8,128)(2,1)S(1)}, bf16[64,512]{1,0:T(8,128)(2,1)S(1)}, u32[]{:S(2)}, u32[]{:S(2)}) collective-permute-start(bf16[64,512]{1,0:T(8,128)(2,1)S(1)} %get-tuple-element.59), channel_id=1, source_target_pairs={{0,8},{4,12},{8,0},{12,4},{1,9},{5,13},{9,1},{13,5},{2,10},{6,14},... | collective-permute-start | bytes 196616 | tf_op jit(solution)/shard_map/ppermute | solution.py:45
  97.2 16.3 %collective-permute-start.24 = (bf16[64,512]{1,0:T(8,128)(2,1)S(1)}, bf16[64,512]{1,0:T(8,128)(2,1)S(1)}, u32[]{:S(2)}, u32[]{:S(2)}) collective-permute-start(bf16[64,512]{1,0:T(8,128)(2,1)S(1)} %get-tuple-element.75), channel_id=1, source_target_pairs={{0,8},{4,12},{8,0},{12,4},{1,9},{5,13},{9,1},{13,5},{2,10},{6,14},... | collective-permute-start | bytes 196616 | tf_op jit(solution)/shard_map/ppermute | solution.py:45
  116.1 1.6 %collective-permute-start.25 = (bf16[64,2048]{1,0:T(8,128)(2,1)S(1)}, bf16[64,2048]{1,0:T(8,128)(2,1)S(1)}, u32[]{:S(2)}, u32[]{:S(2)}) collective-permute-start(bf16[64,2048]{1,0:T(8,128)(2,1)S(1)} %get-tuple-element.77), channel_id=1, source_target_pairs={{0,1},{1,0},{2,3},{3,2},{4,5},{5,4},{6,7},{7,6},{8,9},{9,8},{10,11... | collective-permute-start | bytes 786440 | tf_op jit(solution)/shard_map/ppermute | solution.py:40
  117.8 5.6 %collective-permute-start.26 = (bf16[64,1024]{1,0:T(8,128)(2,1)S(1)}, bf16[64,1024]{1,0:T(8,128)(2,1)S(1)}, u32[]{:S(2)}, u32[]{:S(2)}) collective-permute-start(bf16[64,1024]{1,0:T(8,128)(2,1)S(1)} %get-tuple-element.79), channel_id=1, source_target_pairs={{0,4},{4,0},{8,12},{12,8},{1,5},{5,1},{9,13},{13,9},{2,6},{6,2},{1... | collective-permute-start | bytes 393224 | tf_op jit(solution)/shard_map/ppermute | solution.py:45
  123.4 10.8 %collective-permute-start.27 = (bf16[64,512]{1,0:T(8,128)(2,1)S(1)}, bf16[64,512]{1,0:T(8,128)(2,1)S(1)}, u32[]{:S(2)}, u32[]{:S(2)}) collective-permute-start(bf16[64,512]{1,0:T(8,128)(2,1)S(1)} %get-tuple-element.81), channel_id=1, source_target_pairs={{0,8},{4,12},{8,0},{12,4},{1,9},{5,13},{9,1},{13,5},{2,10},{6,14},... | collective-permute-start | bytes 196616 | tf_op jit(solution)/shard_map/ppermute | solution.py:45

commit v10 on v9

--- a/solution.py
+++ b/solution.py
@@ -8,6 +8,7 @@
 from jax.sharding import PartitionSpec as P
 
 PIECES = (1, 1, 1)
+PARTS = (5, 5, 4)
 MIB = 1 << 20
 
 
@@ -217,9 +218,9 @@
     outs_all += [((rows, features), jnp.float32), ((rows, features), jnp.bfloat16)] if final else [((tokens, features), jnp.float32)]
 
     def kernel(ins, outs):
-        @pl.loop(0, width // 256)
+        @pl.loop(0, width // 128)
         def _(j):
-            at = lanes(j, 256)
+            at = lanes(j, 128)
 
             def total(k):
                 array, top = where[k]
@@ -337,7 +338,7 @@
     return pl.BlockSpec((pl.Element(rows), pl.Element(columns)), where)
 
 
-def column_grads(x, gs, us, span, total, old, after=()):
+def column_grads(x, gs, us, span, total, old, after=(), cost=0.1):
     arrays = [x, *(p[0] for p in (*gs, *us))]
     count, lower, width = len(gs), span[0], span[1] - span[0]
     features, tokens = x.shape
@@ -363,10 +364,10 @@
 
     spec = placed(block, width, lambda i: (pl.multiple_of(i * block, block), lower))
     scratch = [pltpu.VMEM((tokens, width), jnp.bfloat16)] * 2
-    return gradients(kernel, [(features, total)] * 2, arrays, old, (features // block,), [spec, spec], scratch, after, 0.1)
-
-
-def row_grads(hs, y, span, total, old, after=()):
+    return gradients(kernel, [(features, total)] * 2, arrays, old, (features // block,), [spec, spec], scratch, after, cost)
+
+
+def row_grads(hs, y, span, total, old, after=(), cost=0.1):
     arrays = [*(p[0] for p in hs), y]
     count, lower, width = len(hs), span[0], span[1] - span[0]
     tokens, features = y.shape
@@ -388,7 +389,7 @@
 
     spec = placed(width, block, lambda i: (lower, pl.multiple_of(i * block, block)))
     scratch = [pltpu.VMEM((width, tokens), jnp.bfloat16)]
-    return gradients(kernel, [(total, features)], arrays, old, (features // block,), [spec], scratch, after, 0.1)
+    return gradients(kernel, [(total, features)], arrays, old, (features // block,), [spec], scratch, after, cost)
 
 
 def piped(acts, grad_out, w_gate, w_up, w_down):
@@ -400,8 +401,9 @@
     heights = [upper - lower for lower, upper in spans]
     last = len(spans) - 1
     total = w_gate.shape[1]
-    cut = total // 7 * 4
-    whole, halves = (0, total), ((0, cut), (cut, total))
+    fraction = total // sum(PARTS)
+    edges = [sum(PARTS[:i]) * fraction for i in range(len(PARTS) + 1)]
+    whole, parts = (0, total), list(zip(edges[:-1], edges[1:]))
     back_weights = (w_gate, w_up)
 
     def gather(value, parts, early=(), costs=(0.1, 0.1)):
@@ -427,7 +429,7 @@
         rows = heights[index]
         where = ((0, 0), (0, 2 * rows), (0, 4 * rows))
         done = []
-        for span in halves if index == last else (whole,):
+        for span in parts if index == last else (whole,):
             part = forward([(*x, False), (*x, False), (*dy, True)], (w_gate, w_up, w_down), span, rows, after)
             done.append(((part,), where))
             after = (part,)
@@ -436,7 +438,7 @@
 
     def backward_piece(index, part, before, final, after):
         own, where = sums[index][part]
-        span = halves[part] if index == last else whole
+        span = parts[part] if index == last else whole
         other = [shifted(value, "wid", 1) for value in own]
         cost = 1.0 if index == last else 60.0
         return backward(own, other, where, back_weights, span, heights[index], before, final, after, cost)
@@ -464,24 +466,29 @@
     finished = [end_step(far)]
 
     def with_last(results, k, part):
-        return [(grads[c][k], halves[part][0]) for c in range(last)] + [(results[k], 0)]
-
-    first = backward_piece(last, 0, None, False, (grads[1][1], finished[0]))
-    near = near_step(grads[1])
-    down, down_token = row_grads(with_last(first, 0, 0), all_y, halves[0], total, (), (near[0],))
-    far = far_step(near)
-    gate, up, token = column_grads(
-        all_x, with_last(first, 1, 0), with_last(first, 2, 0), halves[0], total, (), (far[0], down_token)
-    )
-    finished.append(end_step(far))
-    second = backward_piece(last, 1, first[3], True, (token, finished[1]))
-    near = near_step(second)
-    down, down_token = row_grads(with_last(second, 0, 1), all_y, halves[1], total, (down,), ())
-    far = far_step(near)
-    gate, up, _ = column_grads(
-        all_x, with_last(second, 1, 1), with_last(second, 2, 1), halves[1], total, (gate, up), (near[0], down_token)
-    )
-    return end_step(far, finished), gate, up, down
+        return [(grads[c][k], parts[part][0]) for c in range(last)] + [(results[k], 0)]
+
+    down, columns, before, waits = (), (), None, (grads[1][1], finished[0])
+    for part in range(len(parts)):
+        final = part == len(parts) - 1
+        results = backward_piece(last, part, before, final, waits)
+        before = results[3]
+        near = near_step(results if final else grads[1]) if final or part == 0 else None
+        down, down_token = row_grads(
+            with_last(results, 0, part), all_y, parts[part], total, down, () if final or near is None else (near[0],),
+            3.0 if final else 0.1,
+        )
+        down = (down,)
+        far = far_step(near) if near is not None else None
+        ahead = () if near is None else (near[0],) if final else (far[0],)
+        *columns, token = column_grads(
+            all_x, with_last(results, 1, part), with_last(results, 2, part), parts[part], total, tuple(columns),
+            (*ahead, down_token), 5.0 if final else 0.1,
+        )
+        if part == 0:
+            finished.append(end_step(far))
+        waits = (token, finished[-1])
+    return end_step(far, finished), *columns, *down
 
 
 def shards(acts, grad_out, w_gate, w_up, w_down):

time: 135 us -> 138 us (1.022)
  Pallas kernels: 52.3 us -> 57.9 us
  waiting for transfers between devices: 48 us -> 43.6 us
  starting transfers between devices: 32.6 us -> 34 us
    pallas_call x4 -> x6, Pallas kernels: 19.2 us -> 22.9 us  [gradients(): pl.pallas_call(body, grid=grid, out_shape=[jax.ShapeDtypeStruct(shape, jn...]
    ppermute x14 -> x15, starting transfers between devices: 8.32 us -> 11.3 us  [shifted(): return lax.ppermute(value, axis, [(i, (i + step) % n) for i in range(n)])]
    ppermute x14 -> x15, waiting for transfers between devices: 11.4 us -> 8.81 us  [shifted(): return lax.ppermute(value, axis, [(i, (i + step) % n) for i in range(n)])]
    pallas_call x31 -> x33, Pallas kernels: 33.1 us -> 35 us  [local(): pl.pallas_call(body, out_shape=shapes, in_specs=[VMEM] * len(args) + [ANY...]
    ppermute x14, waiting for transfers between devices: 36.6 us -> 34.8 us  [swapped(): return lax.ppermute(value, axis, [(i, i ^ bit) for i in range(n)])]
    ppermute x14, starting transfers between devices: 24.3 us -> 22.7 us  [swapped(): return lax.ppermute(value, axis, [(i, i ^ bit) for i in range(n)])]
  transfers between devices with their start and end apart: 28 -> 29, of which waited for: 15 -> 13; matrix products, arithmetic and copies ran while one was open for 0% -> 0% of each run, Pallas kernels for 36% -> 40%
where the time goes in v10:
time: 138 us
  Pallas kernels  57.9 us (42%)
  waiting for transfers between devices  43.6 us (32%)
  starting transfers between devices  34 us (25%)
    pallas_call x33, Pallas kernels, local(): pl.pallas_call(body, out_shape=shapes, in_specs=[VMEM] * len(args) + [ANY...  35 us
    ppermute x14, waiting for transfers between devices, swapped(): return lax.ppermute(value, axis, [(i, i ^ bit) for i in range(n)])  34.8 us
    pallas_call x6, Pallas kernels, gradients(): pl.pallas_call(body, grid=grid, out_shape=[jax.ShapeDtypeStruct(shape, jn...  22.9 us
    ppermute x14, starting transfers between devices, swapped(): return lax.ppermute(value, axis, [(i, i ^ bit) for i in range(n)])  22.7 us
    ppermute x15, starting transfers between devices, shifted(): return lax.ppermute(value, axis, [(i, (i + step) % n) for i in range(n)])  11.3 us
    ppermute x15, waiting for transfers between devices, shifted(): return lax.ppermute(value, axis, [(i, (i + step) % n) for i in range(n)])  8.81 us
  transfers between devices with their start and end apart: 29, of which 13 were waited for; matrix products, arithmetic and copies ran while one was open for 0% of the time, Pallas kernels for 40%

profile of v10, /device:TPU:0, one launch (start us, length us, event | category | flops | bytes accessed | tf_op | source)
XLA Modules:
  0.0 137.6 jit_solution(7832519473988962006)
XLA Ops:
  0.6 0.9 copy-done.2
  1.6 4.1 %collective-permute-start.5 = (bf16[64,512]{1,0:T(8,128)(2,1)S(1)}, bf16[64,512]{1,0:T(8,128)(2,1)S(1)}, u32[]{:S(2)}, u32[]{:S(2)}) collective-permute-start(bf16[64,512]{1,0:T(8,128)(2,1)S(1)} %shard_map.91.refs_0_), channel_id=1, source_target_pairs={{0,8},{4,12},{8,0},{12,4},{1,9},{5,13},{9,1},{13,5},{2,10},{6,14},... | collective-permute-start | bytes 196616 | tf_op jit(solution)/shard_map/ppermute | solution.py:46
  5.7 3.6 %collective-permute-done.5.refs_1_ = bf16[64,512]{1,0:T(8,128)(2,1)S(1)} collective-permute-done((bf16[64,512]{1,0:T(8,128)(2,1)S(1)}, bf16[64,512]{1,0:T(8,128)(2,1)S(1)}, u32[]{:S(2)}, u32[]{:S(2)}) %collective-permute-start.5) | collective-permute-done | bytes 65568 | tf_op jit(solution)/shard_map/ppermute | solution.py:46
  9.3 0.6 collective-permute-start.6
  10.0 3.4 %collective-permute-start = (bf16[64,512]{1,0:T(8,128)(2,1)S(1)}, bf16[64,512]{1,0:T(8,128)(2,1)S(1)}, u32[]{:S(2)}, u32[]{:S(2)}) collective-permute-start(bf16[64,512]{1,0:T(8,128)(2,1)S(1)} %shard_map.84.refs_0_), channel_id=1, source_target_pairs={{0,8},{4,12},{8,0},{12,4},{1,9},{5,13},{9,1},{13,5},{2,10},{6,14},... | collective-permute-start | bytes 196616 | tf_op jit(solution)/shard_map/ppermute | solution.py:46
  13.4 1.7 %collective-permute-done.6.refs_1_ = bf16[64,1024]{1,0:T(8,128)(2,1)S(1)} collective-permute-done((bf16[64,1024]{1,0:T(8,128)(2,1)S(1)}, bf16[64,1024]{1,0:T(8,128)(2,1)S(1)}, u32[]{:S(2)}, u32[]{:S(2)}) %collective-permute-start.6) | collective-permute-done | bytes 131104 | tf_op jit(solution)/shard_map/ppermute | solution.py:46
  15.2 1.1 collective-permute-done.refs_1_
  16.3 1.9 %collective-permute-start.1 = (bf16[64,1024]{1,0:T(8,128)(2,1)S(1)}, bf16[64,1024]{1,0:T(8,128)(2,1)S(1)}, u32[]{:S(2)}, u32[]{:S(2)}) collective-permute-start(bf16[64,1024]{1,0:T(8,128)(2,1)S(1)} %shard_map.85.refs_0_), channel_id=1, source_target_pairs={{0,4},{4,0},{8,12},{12,8},{1,5},{5,1},{9,13},{13,9},{2,6},{6,2},{1... | collective-permute-start | bytes 393224 | tf_op jit(solution)/shard_map/ppermute | solution.py:46
  18.2 2.1 %shard_map.94.refs_3_.refs_0_ = bf16[256,1792]{1,0:T(8,128)(2,1)S(1)} custom-call(bf16[64,2048]{1,0:T(8,128)(2,1)S(1)} %shard_map.93.refs_0_.refs_2_, bf16[64,2048]{1,0:T(8,128)(2,1)S(1)} %collective-permute-done.7.refs_1_.refs_3_, bf16[64,2048]{1,0:T(8,128)(2,1)S(1)} %shard_map.93.refs_0_.refs_2_, ...), custom_call_target="tpu_custom_call" | custom-call | flops 345000000 | tf_op jit(solution)/shard_map/pallas_call | solution.py:101
  20.3 1.6 %collective-permute-start.9 = (bf16[256,1792]{1,0:T(8,128)(2,1)S(1)}, bf16[256,1792]{1,0:T(8,128)(2,1)S(1)}, u32[]{:S(2)}, u32[]{:S(2)}) collective-permute-start(bf16[256,1792]{1,0:T(8,128)(2,1)S(1)} %shard_map.94.refs_3_.refs_0_), channel_id=1, source_target_pairs={{0,2},{2,0},{1,3},{3,1},{4,6},{6,4},{5,7},{7,5},{8,10},{10,8},{9,1... | collective-permute-start | bytes 2752520 | tf_op jit(solution)/shard_map/ppermute | solution.py:41
  22.0 2.4 %collective-permute-start.2 = (bf16[128,512]{1,0:T(8,128)(2,1)S(1)}, bf16[128,512]{1,0:T(8,128)(2,1)S(1)}, u32[]{:S(2)}, u32[]{:S(2)}) collective-permute-start(bf16[128,512]{1,0:T(8,128)(2,1)S(1)} %shard_map.87.refs_0_), channel_id=1, source_target_pairs={{0,8},{4,12},{8,0},{12,4},{1,9},{5,13},{9,1},{13,5},{2,10},{6,14},... | collective-permute-start | bytes 393224 | tf_op jit(solution)/shard_map/ppermute | solution.py:46
  24.4 7.3 %collective-permute-done.2.refs_1_ = bf16[128,512]{1,0:T(8,128)(2,1)S(1)} collective-permute-done((bf16[128,512]{1,0:T(8,128)(2,1)S(1)}, bf16[128,512]{1,0:T(8,128)(2,1)S(1)}, u32[]{:S(2)}, u32[]{:S(2)}) %collective-permute-start.2) | collective-permute-done | bytes 131104 | tf_op jit(solution)/shard_map/ppermute | solution.py:46
  32.2 2.5 %shard_map.95.refs_9_.refs_1_ = bf16[128,1792]{1,0:T(8,128)(2,1)S(1)} custom-call(bf16[64,2048]{1,0:T(8,128)(2,1)S(1)} %shard_map.86.refs_2_.refs_0_, bf16[64,2048]{1,0:T(8,128)(2,1)S(1)} %collective-permute-done.8.refs_1_, bf16[1792,2048]{1,0:T(8,128)(2,1)S(1)} %bitcast.1, bf16[256,1792]{1,0:T(8,128)(2,1)S(1)} %shard_map.94.refs_3_.refs_0_), custom_call_target="tpu_custom_call" | custom-call | flops 345000000 | tf_op jit(solution)/shard_map/pallas_call | solution.py:101
  34.7 1.6 %collective-permute-start.10 = (bf16[128,1792]{1,0:T(8,128)(2,1)S(1)}, bf16[128,1792]{1,0:T(8,128)(2,1)S(1)}, u32[]{:S(2)}, u32[]{:S(2)}) collective-permute-start(bf16[128,1792]{1,0:T(8,128)(2,1)S(1)} %shard_map.95.refs_9_.refs_1_), channel_id=1, source_target_pairs={{0,2},{2,0},{1,3},{3,1},{4,6},{6,4},{5,7},{7,5},{8,10},{10,8},{9,1... | collective-permute-start | bytes 1376264 | tf_op jit(solution)/shard_map/ppermute | solution.py:41
  36.3 3.4 %collective-permute-done.3.refs_1_ = bf16[128,1024]{1,0:T(8,128)(2,1)S(1)} collective-permute-done((bf16[128,1024]{1,0:T(8,128)(2,1)S(1)}, bf16[128,1024]{1,0:T(8,128)(2,1)S(1)}, u32[]{:S(2)}, u32[]{:S(2)}) %collective-permute-start.3) | collective-permute-done | bytes 262176 | tf_op jit(solution)/shard_map/ppermute | solution.py:46
  40.3 2.5 %collective-permute-start.4 = (bf16[128,512]{1,0:T(8,128)(2,1)S(1)}, bf16[128,512]{1,0:T(8,128)(2,1)S(1)}, u32[]{:S(2)}, u32[]{:S(2)}) collective-permute-start(bf16[128,512]{1,0:T(8,128)(2,1)S(1)} %shard_map.90.refs_0_), channel_id=1, source_target_pairs={{0,8},{4,12},{8,0},{12,4},{1,9},{5,13},{9,1},{13,5},{2,10},{6,14},... | collective-permute-start | bytes 393224 | tf_op jit(solution)/shard_map/ppermute | solution.py:46
  42.8 4.4 %shard_map.96.refs_6_.refs_0_ = bf16[384,1792]{1,0:T(8,128)(2,1)S(1)} custom-call(bf16[64,2048]{1,0:T(8,128)(2,1)S(1)} %get-tuple-element.57.refs_2_.refs_0_, bf16[64,2048]{1,0:T(8,128)(2,1)S(1)} %collective-permute-done.11.refs_1_.refs_3_, bf16[64,2048]{1,0:T(8,128)(2,1)S(1)} %get-tuple-element.57.refs_2_.refs_0_, ...), custom_call_target="tpu_custom_call" | custom-call | flops 345000000 | tf_op jit(solution)/shard_map/pallas_call | solution.py:101
  47.2 1.6 %collective-permute-start.20 = (bf16[384,1792]{1,0:T(8,128)(2,1)S(1)}, bf16[384,1792]{1,0:T(8,128)(2,1)S(1)}, u32[]{:S(2)}, u32[]{:S(2)}) collective-permute-start(bf16[384,1792]{1,0:T(8,128)(2,1)S(1)} %shard_map.96.refs_6_.refs_0_), channel_id=1, source_target_pairs={{0,2},{2,0},{1,3},{3,1},{4,6},{6,4},{5,7},{7,5},{8,10},{10,8},{9,1... | collective-permute-start | bytes 4128776 | tf_op jit(solution)/shard_map/ppermute | solution.py:41
  48.8 4.4 %collective-permute-done.10.refs_3_ = bf16[128,1792]{1,0:T(8,128)(2,1)S(1)} collective-permute-done((bf16[128,1792]{1,0:T(8,128)(2,1)S(1)}, bf16[128,1792]{1,0:T(8,128)(2,1)S(1)}, u32[]{:S(2)}, u32[]{:S(2)}) %collective-permute-start.10) | collective-permute-done | bytes 458784 | tf_op jit(solution)/shard_map/ppermute | solution.py:41
  53.2 6.3 %shard_map.97 = (bf16[1792,128]{1,0:T(8,128)(2,1)S(1)}, bf16[128,1792]{1,0:T(8,128)(2,1)S(1)}, bf16[128,1792]{1,0:T(8,128)(2,1)S(1)}, f32[64,2048]{1,0:T(8,128)S(1)}, bf16[64,2048]{1,0:T(8,128)(2,1)S(1)}) custom-call(bf16[256,1792]{1,0:T(8,128)(2,1)S(1)} %shard_map.94.refs_3_.refs_0_, bf16[128,1792]{1,0:T(8,128)(2,1)S(1)} %shard_map.95.refs_9_.refs_1_, ...), custom_call_target="tpu_custom_call" | custom-call | flops 69000003584 | tf_op jit(solution)/shard_map/pallas_call | solution.py:101
  59.7 6.3 %collective-permute-done.13.refs_1_ = bf16[128,1024]{1,0:T(8,128)(2,1)S(1)} collective-permute-done((bf16[128,1024]{1,0:T(8,128)(2,1)S(1)}, bf16[128,1024]{1,0:T(8,128)(2,1)S(1)}, u32[]{:S(2)}, u32[]{:S(2)}) %collective-permute-start.13) | collective-permute-done | bytes 262176 | tf_op jit(solution)/shard_map/ppermute | solution.py:46
  66.8 5.5 %collective-permute-done.21.refs_1_ = bf16[64,1024]{1,0:T(8,128)(2,1)S(1)} collective-permute-done((bf16[64,1024]{1,0:T(8,128)(2,1)S(1)}, bf16[64,1024]{1,0:T(8,128)(2,1)S(1)}, u32[]{:S(2)}, u32[]{:S(2)}) %collective-permute-start.21) | collective-permute-done | bytes 131104 | tf_op jit(solution)/shard_map/ppermute | solution.py:46
  72.3 1.8 %shard_map.101.refs_9_.refs_0_ = bf16[384,640]{1,0:T(8,128)(2,1)S(1)} custom-call(bf16[64,2048]{1,0:T(8,128)(2,1)S(1)} %get-tuple-element.60.refs_0_.refs_2_.refs_4_, bf16[64,2048]{1,0:T(8,128)(2,1)S(1)} %collective-permute-done.14.refs_1_.refs_3_.refs_5_, bf16[64,2048]{1,0:T(8,128)(2,1)S(1)} %get-tuple-element.60.refs_0_.refs_2_.refs_4_, ...), custom_call_target="tpu_custom_call" | custom-call | flops 345000000 | tf_op jit(solution)/shard_map/pallas_call | solution.py:101
  74.1 1.8 %collective-permute-start.19 = (bf16[384,640]{1,0:T(8,128)(2,1)S(1)}, bf16[384,640]{1,0:T(8,128)(2,1)S(1)}, u32[]{:S(2)}, u32[]{:S(2)}) collective-permute-start(bf16[384,640]{1,0:T(8,128)(2,1)S(1)} %shard_map.101.refs_9_.refs_0_), channel_id=1, source_target_pairs={{0,2},{2,0},{1,3},{3,1},{4,6},{6,4},{5,7},{7,5},{8,10},{10,8},{9,1... | collective-permute-start | bytes 1474568 | tf_op jit(solution)/shard_map/ppermute | solution.py:41
  75.9 1.8 %shard_map.102.refs_9_.refs_0_ = bf16[384,640]{1,0:T(8,128)(2,1)S(1)} custom-call(bf16[64,2048]{1,0:T(8,128)(2,1)S(1)} %get-tuple-element.60.refs_0_.refs_2_.refs_4_, bf16[64,2048]{1,0:T(8,128)(2,1)S(1)} %collective-permute-done.14.refs_1_.refs_3_.refs_5_, bf16[64,2048]{1,0:T(8,128)(2,1)S(1)} %get-tuple-element.60.refs_0_.refs_2_.refs_4_, ...), custom_call_target="tpu_custom_call" | custom-call | flops 345000000 | tf_op jit(solution)/shard_map/pallas_call | solution.py:101
  77.7 1.4 %shard_map.103.refs_6_.refs_0_ = bf16[384,512]{1,0:T(8,128)(2,1)S(1)} custom-call(bf16[64,2048]{1,0:T(8,128)(2,1)S(1)} %get-tuple-element.60.refs_0_.refs_2_.refs_4_, bf16[64,2048]{1,0:T(8,128)(2,1)S(1)} %collective-permute-done.14.refs_1_.refs_3_.refs_5_, bf16[64,2048]{1,0:T(8,128)(2,1)S(1)} %get-tuple-element.60.refs_0_.refs_2_.refs_4_, ...), custom_call_target="tpu_custom_call" | custom-call | flops 345000000 | tf_op jit(solution)/shard_map/pallas_call | solution.py:101
  79.9 2.8 %collective-permute-done.20.refs_1_ = bf16[384,1792]{1,0:T(8,128)(2,1)S(1)} collective-permute-done((bf16[384,1792]{1,0:T(8,128)(2,1)S(1)}, bf16[384,1792]{1,0:T(8,128)(2,1)S(1)}, u32[]{:S(2)}, u32[]{:S(2)}) %collective-permute-start.20) | collective-permute-done | bytes 1376288 | tf_op jit(solution)/shard_map/ppermute | solution.py:41
  82.7 6.3 %shard_map.107 = (bf16[1792,128]{1,0:T(8,128)(2,1)S(1)}, bf16[128,1792]{1,0:T(8,128)(2,1)S(1)}, bf16[128,1792]{1,0:T(8,128)(2,1)S(1)}, f32[64,2048]{1,0:T(8,128)S(1)}, bf16[64,2048]{1,0:T(8,128)(2,1)S(1)}) custom-call(bf16[384,1792]{1,0:T(8,128)(2,1)S(1)} %shard_map.96.refs_6_.refs_0_, bf16[384,1792]{1,0:T(8,128)(2,1)S(1)} %collective-permute-done.20.refs_1_, ...), custom_call_target="tpu_custom_call" | custom-call | flops 69000003584 | tf_op jit(solution)/shard_map/pallas_call | solution.py:101
  89.1 1.8 %collective-permute-start.18 = (bf16[384,640]{1,0:T(8,128)(2,1)S(1)}, bf16[384,640]{1,0:T(8,128)(2,1)S(1)}, u32[]{:S(2)}, u32[]{:S(2)}) collective-permute-start(bf16[384,640]{1,0:T(8,128)(2,1)S(1)} %shard_map.102.refs_9_.refs_0_), channel_id=1, source_target_pairs={{0,2},{2,0},{1,3},{3,1},{4,6},{6,4},{5,7},{7,5},{8,10},{10,8},{9,1... | collective-permute-start | bytes 1474568 | tf_op jit(solution)/shard_map/ppermute | solution.py:41
  91.1 1.5 %collective-permute-start.17 = (bf16[384,512]{1,0:T(8,128)(2,1)S(1)}, bf16[384,512]{1,0:T(8,128)(2,1)S(1)}, u32[]{:S(2)}, u32[]{:S(2)}) collective-permute-start(bf16[384,512]{1,0:T(8,128)(2,1)S(1)} %shard_map.103.refs_6_.refs_0_), channel_id=1, source_target_pairs={{0,2},{2,0},{1,3},{3,1},{4,6},{6,4},{5,7},{7,5},{8,10},{10,8},{9,1... | collective-permute-start | bytes 1179656 | tf_op jit(solution)/shard_map/ppermute | solution.py:41
  92.6 3.1 %collective-permute-start.22 = (bf16[64,512]{1,0:T(8,128)(2,1)S(1)}, bf16[64,512]{1,0:T(8,128)(2,1)S(1)}, u32[]{:S(2)}, u32[]{:S(2)}) collective-permute-start(bf16[64,512]{1,0:T(8,128)(2,1)S(1)} %get-tuple-element.68), channel_id=1, source_target_pairs={{0,8},{4,12},{8,0},{12,4},{1,9},{5,13},{9,1},{13,5},{2,10},{6,14},... | collective-permute-start | bytes 196616 | tf_op jit(solution)/shard_map/ppermute | solution.py:46
  95.7 2.9 %collective-permute-done.22.refs_1_ = bf16[64,512]{1,0:T(8,128)(2,1)S(1)} collective-permute-done((bf16[64,512]{1,0:T(8,128)(2,1)S(1)}, bf16[64,512]{1,0:T(8,128)(2,1)S(1)}, u32[]{:S(2)}, u32[]{:S(2)}) %collective-permute-start.22) | collective-permute-done | bytes 65568 | tf_op jit(solution)/shard_map/ppermute | solution.py:46
  98.6 2.4 %collective-permute-start.25 = (bf16[64,512]{1,0:T(8,128)(2,1)S(1)}, bf16[64,512]{1,0:T(8,128)(2,1)S(1)}, u32[]{:S(2)}, u32[]{:S(2)}) collective-permute-start(bf16[64,512]{1,0:T(8,128)(2,1)S(1)} %get-tuple-element.84), channel_id=1, source_target_pairs={{0,8},{4,12},{8,0},{12,4},{1,9},{5,13},{9,1},{13,5},{2,10},{6,14},... | collective-permute-start | bytes 196616 | tf_op jit(solution)/shard_map/ppermute | solution.py:46
  101.0 2.3 %shard_map.109 = (bf16[640,128]{1,0:T(8,128)(2,1)S(1)}, bf16[128,640]{1,0:T(8,128)(2,1)S(1)}, bf16[128,640]{1,0:T(8,128)(2,1)S(1)}, f32[128,2048]{1,0:T(8,128)S(1)}) custom-call(bf16[384,640]{1,0:T(8,128)(2,1)S(1)} %shard_map.101.refs_9_.refs_0_, bf16[384,640]{1,0:T(8,128)(2,1)S(1)} %collective-permute-done.19.refs_1_, bf16[2048,1792]{1,0:T(8,128)(2,1)S(1)} %copy-done, ...), custom_call_target="tpu_custom_call" | custom-call | flops 1150000000 | tf_op jit(solution)/shard_map/pallas_call | solution.py:101
  103.3 3.3 %shard_map.112 = (bf16[1792,2048]{1,0:T(8,128)(2,1)}, bf16[16,128]{1,0:T(8,128)(2,1)S(1)}) custom-call(bf16[1792,128]{1,0:T(8,128)(2,1)S(1)} %get-tuple-element.79.refs_0_, bf16[1792,128]{1,0:T(8,128)(2,1)S(1)} %get-tuple-element.80.refs_1_, bf16[640,128]{1,0:T(8,128)(2,1)S(1)} %get-tuple-element.81.refs_2_, ...), custom_call_target="tpu_custom_call" | custom-call | flops 115000000 | tf_op jit(solution)/shard_map/pallas_call | solution.py:316
  106.6 4.7 %shard_map.113 = (bf16[2048,1792]{1,0:T(8,128)(2,1)}, bf16[2048,1792]{1,0:T(8,128)(2,1)}, bf16[16,128]{1,0:T(8,128)(2,1)S(1)}) custom-call(bf16[2048,384]{1,0:T(8,128)(2,1)S(1)} %shard_map.104.refs_4_.refs_0_, bf16[128,1792]{1,0:T(8,128)(2,1)S(1)} %get-tuple-element.59.refs_2_.refs_1_, bf16[128,1792]{1,0:T(8,128)(2,1)S(1)} %get-tuple-element.67.refs_4_.refs_2_, ...), custom_call_target="tpu_custom_call" | custom-call | flops 115000000 | tf_op jit(solution)/shard_map/pallas_call | solution.py:316
  111.4 2.3 %shard_map.115 = (bf16[640,128]{1,0:T(8,128)(2,1)S(1)}, bf16[128,640]{1,0:T(8,128)(2,1)S(1)}, bf16[128,640]{1,0:T(8,128)(2,1)S(1)}, f32[128,2048]{1,0:T(8,128)S(1)}) custom-call(bf16[384,640]{1,0:T(8,128)(2,1)S(1)} %shard_map.102.refs_9_.refs_0_, bf16[384,640]{1,0:T(8,128)(2,1)S(1)} %collective-permute-done.18.refs_1_, bf16[2048,1792]{1,0:T(8,128)(2,1)S(1)} %copy-done, ...), custom_call_target="tpu_custom_call" | custom-call | flops 1150000000 | tf_op jit(solution)/shard_map/pallas_call | solution.py:101
  113.7 3.3 %shard_map.116 = (bf16[1792,2048]{1,0:T(8,128)(2,1)}, bf16[16,128]{1,0:T(8,128)(2,1)S(1)}) custom-call(bf16[1792,128]{1,0:T(8,128)(2,1)S(1)} %get-tuple-element.79.refs_0_, bf16[1792,128]{1,0:T(8,128)(2,1)S(1)} %get-tuple-element.80.refs_1_, bf16[640,128]{1,0:T(8,128)(2,1)S(1)} %get-tuple-element.90.refs_2_, ...), custom_call_target="tpu_custom_call", output_to_operand_aliasing={{0}: (4, {})} | custom-call | flops 115000000 | tf_op jit(solution)/shard_map/pallas_call | solution.py:316
  117.0 4.7 %shard_map.117 = (bf16[2048,1792]{1,0:T(8,128)(2,1)}, bf16[2048,1792]{1,0:T(8,128)(2,1)}, bf16[16,128]{1,0:T(8,128)(2,1)S(1)}) custom-call(bf16[2048,384]{1,0:T(8,128)(2,1)S(1)} %shard_map.104.refs_4_.refs_0_, bf16[128,1792]{1,0:T(8,128)(2,1)S(1)} %get-tuple-element.59.refs_2_.refs_1_, ...), custom_call_target="tpu_custom_call", output_to_operand_aliasing={{0}: (7, {}), {1}: (8, {})} | custom-call | flops 115000000 | tf_op jit(solution)/shard_map/pallas_call | solution.py:316
  121.7 1.9 %shard_map.118 = (bf16[512,128]{1,0:T(8,128)(2,1)S(1)}, bf16[128,512]{1,0:T(8,128)(2,1)S(1)}, bf16[128,512]{1,0:T(8,128)(2,1)S(1)}, f32[64,2048]{1,0:T(8,128)S(1)}, bf16[64,2048]{1,0:T(8,128)(2,1)S(1)}) custom-call(bf16[384,512]{1,0:T(8,128)(2,1)S(1)} %shard_map.103.refs_6_.refs_0_, bf16[384,512]{1,0:T(8,128)(2,1)S(1)} %collective-permute-done.17.refs_1_, ...), custom_call_target="tpu_custom_call" | custom-call | flops 1150000000 | tf_op jit(solution)/shard_map/pallas_call | solution.py:101
  123.7 1.5 %collective-permute-done.26.refs_1_ = bf16[64,2048]{1,0:T(8,128)(2,1)S(1)} collective-permute-done((bf16[64,2048]{1,0:T(8,128)(2,1)S(1)}, bf16[64,2048]{1,0:T(8,128)(2,1)S(1)}, u32[]{:S(2)}, u32[]{:S(2)}) %collective-permute-start.26) | collective-permute-done | bytes 262176 | tf_op jit(solution)/shard_map/ppermute | solution.py:41
  125.3 0.8 collective-permute-start.27
  126.1 3.0 %shard_map.122 = (bf16[1792,2048]{1,0:T(8,128)(2,1)}, bf16[16,128]{1,0:T(8,128)(2,1)S(1)}) custom-call(bf16[1792,128]{1,0:T(8,128)(2,1)S(1)} %get-tuple-element.79.refs_0_, bf16[1792,128]{1,0:T(8,128)(2,1)S(1)} %get-tuple-element.80.refs_1_, bf16[512,128]{1,0:T(8,128)(2,1)S(1)} %get-tuple-element.104.refs_2_, ...), custom_call_target="tpu_custom_call", output_to_operand_aliasing={{0}: (4, {})} | custom-call | flops 3449999872 | tf_op jit(solution)/shard_map/pallas_call | solution.py:316
  129.1 1.8 %collective-permute-done.27.refs_1_ = bf16[64,1024]{1,0:T(8,128)(2,1)S(1)} collective-permute-done((bf16[64,1024]{1,0:T(8,128)(2,1)S(1)}, bf16[64,1024]{1,0:T(8,128)(2,1)S(1)}, u32[]{:S(2)}, u32[]{:S(2)}) %collective-permute-start.27) | collective-permute-done | bytes 131104 | tf_op jit(solution)/shard_map/ppermute | solution.py:46
  130.9 0.7 collective-permute-start.28
  131.6 3.8 %shard_map.123 = (bf16[2048,1792]{1,0:T(8,128)(2,1)}, bf16[2048,1792]{1,0:T(8,128)(2,1)}, bf16[16,128]{1,0:T(8,128)(2,1)}) custom-call(bf16[2048,384]{1,0:T(8,128)(2,1)S(1)} %shard_map.104.refs_4_.refs_0_, bf16[128,1792]{1,0:T(8,128)(2,1)S(1)} %get-tuple-element.59.refs_2_.refs_1_, ...), custom_call_target="tpu_custom_call", output_to_operand_aliasing={{0}: (7, {}), {1}: (8, {})} | custom-call | flops 5750000128 | tf_op jit(solution)/shard_map/pallas_call | solution.py:316
  135.4 1.4 %collective-permute-done.28.refs_1_ = bf16[64,512]{1,0:T(8,128)(2,1)S(1)} collective-permute-done((bf16[64,512]{1,0:T(8,128)(2,1)S(1)}, bf16[64,512]{1,0:T(8,128)(2,1)S(1)}, u32[]{:S(2)}, u32[]{:S(2)}) %collective-permute-start.28) | collective-permute-done | bytes 65568 | tf_op jit(solution)/shard_map/ppermute | solution.py:46
  136.9 0.7 shard_map.121
  (65 shorter events, 3.6 us)
Async XLA Ops:
  0.6 0.9 copy-start.2
  1.6 8.4 %copy-start.3 = (bf16[192,512]{1,0:T(8,128)(2,1)S(1)}, bf16[192,512]{1,0:T(8,128)(2,1)}, u32[]{:S(2)}) copy-start(bf16[192,512]{1,0:T(8,128)(2,1)} %source.1) | copy-start | bytes 589828
  1.6 8.4 %copy-start.4 = (bf16[192,512]{1,0:T(8,128)(2,1)S(1)}, bf16[192,512]{1,0:T(8,128)(2,1)}, u32[]{:S(2)}) copy-start(bf16[192,512]{1,0:T(8,128)(2,1)} %refs_1_.5) | copy-start | bytes 589828
  1.6 16.6 %copy-start = (bf16[2048,1792]{1,0:T(8,128)(2,1)S(1)}, bf16[2048,1792]{1,0:T(8,128)(2,1)}, u32[]{:S(2)}) copy-start(bf16[2048,1792]{1,0:T(8,128)(2,1)} %refs_2_.9) | copy-start | bytes 22020100
  1.6 16.6 %copy-start.1 = (bf16[2048,1792]{1,0:T(8,128)(2,1)S(1)}, bf16[2048,1792]{1,0:T(8,128)(2,1)}, u32[]{:S(2)}) copy-start(bf16[2048,1792]{1,0:T(8,128)(2,1)} %refs_3_.7) | copy-start | bytes 22020100
  1.6 7.8 %collective-permute-start.5 = (bf16[64,512]{1,0:T(8,128)(2,1)S(1)}, bf16[64,512]{1,0:T(8,128)(2,1)S(1)}, u32[]{:S(2)}, u32[]{:S(2)}) collective-permute-start(bf16[64,512]{1,0:T(8,128)(2,1)S(1)} %shard_map.91.refs_0_), channel_id=1, source_target_pairs={{0,8},{4,12},{8,0},{12,4},{1,9},{5,13},{9,1},{13,5},{2,10},{6,14},... | collective-permute-start | bytes 196616 | tf_op jit(solution)/shard_map/ppermute | solution.py:46
  9.3 5.7 %collective-permute-start.6 = (bf16[64,1024]{1,0:T(8,128)(2,1)S(1)}, bf16[64,1024]{1,0:T(8,128)(2,1)S(1)}, u32[]{:S(2)}, u32[]{:S(2)}) collective-permute-start(bf16[64,1024]{1,0:T(8,128)(2,1)S(1)} %shard_map.92.refs_0_), channel_id=1, source_target_pairs={{0,4},{4,0},{8,12},{12,8},{1,5},{5,1},{9,13},{13,9},{2,6},{6,2},{1... | collective-permute-start | bytes 393224 | tf_op jit(solution)/shard_map/ppermute | solution.py:46
  10.0 6.3 %collective-permute-start = (bf16[64,512]{1,0:T(8,128)(2,1)S(1)}, bf16[64,512]{1,0:T(8,128)(2,1)S(1)}, u32[]{:S(2)}, u32[]{:S(2)}) collective-permute-start(bf16[64,512]{1,0:T(8,128)(2,1)S(1)} %shard_map.84.refs_0_), channel_id=1, source_target_pairs={{0,8},{4,12},{8,0},{12,4},{1,9},{5,13},{9,1},{13,5},{2,10},{6,14},... | collective-permute-start | bytes 196616 | tf_op jit(solution)/shard_map/ppermute | solution.py:46
  15.1 3.0 %collective-permute-start.7 = (bf16[64,2048]{1,0:T(8,128)(2,1)S(1)}, bf16[64,2048]{1,0:T(8,128)(2,1)S(1)}, u32[]{:S(2)}, u32[]{:S(2)}) collective-permute-start(bf16[64,2048]{1,0:T(8,128)(2,1)S(1)} %shard_map.93.refs_0_.refs_2_), channel_id=1, source_target_pairs={{0,1},{1,0},{2,3},{3,2},{4,5},{5,4},{6,7},{7,6},{8,9},{9,8},{10,11... | collective-permute-start | bytes 786440 | tf_op jit(solution)/shard_map/ppermute | solution.py:41
  16.3 5.6 %collective-permute-start.1 = (bf16[64,1024]{1,0:T(8,128)(2,1)S(1)}, bf16[64,1024]{1,0:T(8,128)(2,1)S(1)}, u32[]{:S(2)}, u32[]{:S(2)}) collective-permute-start(bf16[64,1024]{1,0:T(8,128)(2,1)S(1)} %shard_map.85.refs_0_), channel_id=1, source_target_pairs={{0,4},{4,0},{8,12},{12,8},{1,5},{5,1},{9,13},{13,9},{2,6},{6,2},{1... | collective-permute-start | bytes 393224 | tf_op jit(solution)/shard_map/ppermute | solution.py:46
  18.2 14.0 %slice-start = ((s8[7340032]{0:T(1024)(128)(4,1)}), s8[4194304]{0:T(1024)(128)(4,1)S(1)}, s32[]{:S(2)}) async-start(s8[7340032]{0:T(1024)(128)(4,1)} %bitcast), calls=%async_computation | async-start | bytes 8388608
  20.3 11.9 %slice-start.1 = ((s8[7340032]{0:T(1024)(128)(4,1)}), s8[3145728]{0:T(1024)(128)(4,1)S(1)}, s32[]{:S(2)}) async-start(s8[7340032]{0:T(1024)(128)(4,1)} %bitcast), calls=%async_computation.1 | async-start | bytes 6291456
  20.3 32.9 %collective-permute-start.9 = (bf16[256,1792]{1,0:T(8,128)(2,1)S(1)}, bf16[256,1792]{1,0:T(8,128)(2,1)S(1)}, u32[]{:S(2)}, u32[]{:S(2)}) collective-permute-start(bf16[256,1792]{1,0:T(8,128)(2,1)S(1)} %shard_map.94.refs_3_.refs_0_), channel_id=1, source_target_pairs={{0,2},{2,0},{1,3},{3,1},{4,6},{6,4},{5,7},{7,5},{8,10},{10,8},{9,1... | collective-permute-start | bytes 2752520 | tf_op jit(solution)/shard_map/ppermute | solution.py:41
  21.9 10.3 %collective-permute-start.8 = (bf16[64,2048]{1,0:T(8,128)(2,1)S(1)}, bf16[64,2048]{1,0:T(8,128)(2,1)S(1)}, u32[]{:S(2)}, u32[]{:S(2)}) collective-permute-start(bf16[64,2048]{1,0:T(8,128)(2,1)S(1)} %shard_map.86.refs_2_.refs_0_), channel_id=1, source_target_pairs={{0,1},{1,0},{2,3},{3,2},{4,5},{5,4},{6,7},{7,6},{8,9},{9,8},{10,11... | collective-permute-start | bytes 786440 | tf_op jit(solution)/shard_map/ppermute | solution.py:41
  22.0 9.7 %collective-permute-start.2 = (bf16[128,512]{1,0:T(8,128)(2,1)S(1)}, bf16[128,512]{1,0:T(8,128)(2,1)S(1)}, u32[]{:S(2)}, u32[]{:S(2)}) collective-permute-start(bf16[128,512]{1,0:T(8,128)(2,1)S(1)} %shard_map.87.refs_0_), channel_id=1, source_target_pairs={{0,8},{4,12},{8,0},{12,4},{1,9},{5,13},{9,1},{13,5},{2,10},{6,14},... | collective-permute-start | bytes 393224 | tf_op jit(solution)/shard_map/ppermute | solution.py:46
  31.7 8.0 %collective-permute-start.3 = (bf16[128,1024]{1,0:T(8,128)(2,1)S(1)}, bf16[128,1024]{1,0:T(8,128)(2,1)S(1)}, u32[]{:S(2)}, u32[]{:S(2)}) collective-permute-start(bf16[128,1024]{1,0:T(8,128)(2,1)S(1)} %shard_map.88.refs_0_), channel_id=1, source_target_pairs={{0,4},{4,0},{8,12},{12,8},{1,5},{5,1},{9,13},{13,9},{2,6},{6,2},{1... | collective-permute-start | bytes 786440 | tf_op jit(solution)/shard_map/ppermute | solution.py:46
  34.7 18.5 %collective-permute-start.10 = (bf16[128,1792]{1,0:T(8,128)(2,1)S(1)}, bf16[128,1792]{1,0:T(8,128)(2,1)S(1)}, u32[]{:S(2)}, u32[]{:S(2)}) collective-permute-start(bf16[128,1792]{1,0:T(8,128)(2,1)S(1)} %shard_map.95.refs_9_.refs_1_), channel_id=1, source_target_pairs={{0,2},{2,0},{1,3},{3,1},{4,6},{6,4},{5,7},{7,5},{8,10},{10,8},{9,1... | collective-permute-start | bytes 1376264 | tf_op jit(solution)/shard_map/ppermute | solution.py:41
  39.7 3.1 %collective-permute-start.11 = (bf16[64,2048]{1,0:T(8,128)(2,1)S(1)}, bf16[64,2048]{1,0:T(8,128)(2,1)S(1)}, u32[]{:S(2)}, u32[]{:S(2)}) collective-permute-start(bf16[64,2048]{1,0:T(8,128)(2,1)S(1)} %get-tuple-element.57.refs_2_.refs_0_), channel_id=1, source_target_pairs={{0,1},{1,0},{2,3},{3,2},{4,5},{5,4},{6,7},{7,6},{8,9},{9,8},{10,11... | collective-permute-start | bytes 786440 | tf_op jit(solution)/shard_map/ppermute | solution.py:41
  39.8 3.0 %collective-permute-start.12 = (bf16[64,2048]{1,0:T(8,128)(2,1)S(1)}, bf16[64,2048]{1,0:T(8,128)(2,1)S(1)}, u32[]{:S(2)}, u32[]{:S(2)}) collective-permute-start(bf16[64,2048]{1,0:T(8,128)(2,1)S(1)} %get-tuple-element.58.refs_4_.refs_2_), channel_id=1, source_target_pairs={{0,1},{1,0},{2,3},{3,2},{4,5},{5,4},{6,7},{7,6},{8,9},{9,8},{10,11... | collective-permute-start | bytes 786440 | tf_op jit(solution)/shard_map/ppermute | solution.py:41
  40.3 19.2 %collective-permute-start.4 = (bf16[128,512]{1,0:T(8,128)(2,1)S(1)}, bf16[128,512]{1,0:T(8,128)(2,1)S(1)}, u32[]{:S(2)}, u32[]{:S(2)}) collective-permute-start(bf16[128,512]{1,0:T(8,128)(2,1)S(1)} %shard_map.90.refs_0_), channel_id=1, source_target_pairs={{0,8},{4,12},{8,0},{12,4},{1,9},{5,13},{9,1},{13,5},{2,10},{6,14},... | collective-permute-start | bytes 393224 | tf_op jit(solution)/shard_map/ppermute | solution.py:46
  47.2 35.5 %collective-permute-start.20 = (bf16[384,1792]{1,0:T(8,128)(2,1)S(1)}, bf16[384,1792]{1,0:T(8,128)(2,1)S(1)}, u32[]{:S(2)}, u32[]{:S(2)}) collective-permute-start(bf16[384,1792]{1,0:T(8,128)(2,1)S(1)} %shard_map.96.refs_6_.refs_0_), channel_id=1, source_target_pairs={{0,2},{2,0},{1,3},{3,1},{4,6},{6,4},{5,7},{7,5},{8,10},{10,8},{9,1... | collective-permute-start | bytes 4128776 | tf_op jit(solution)/shard_map/ppermute | solution.py:41
  59.6 6.4 %collective-permute-start.13 = (bf16[128,1024]{1,0:T(8,128)(2,1)S(1)}, bf16[128,1024]{1,0:T(8,128)(2,1)S(1)}, u32[]{:S(2)}, u32[]{:S(2)}) collective-permute-start(bf16[128,1024]{1,0:T(8,128)(2,1)S(1)} %shard_map.98.refs_0_), channel_id=1, source_target_pairs={{0,4},{4,0},{8,12},{12,8},{1,5},{5,1},{9,13},{13,9},{2,6},{6,2},{1... | collective-permute-start | bytes 786440 | tf_op jit(solution)/shard_map/ppermute | solution.py:46
  59.7 7.0 %collective-permute-start.16 = (bf16[64,2048]{1,0:T(8,128)(2,1)S(1)}, bf16[64,2048]{1,0:T(8,128)(2,1)S(1)}, u32[]{:S(2)}, u32[]{:S(2)}) collective-permute-start(bf16[64,2048]{1,0:T(8,128)(2,1)S(1)} %get-tuple-element.63), channel_id=1, source_target_pairs={{0,1},{1,0},{2,3},{3,2},{4,5},{5,4},{6,7},{7,6},{8,9},{9,8},{10,11... | collective-permute-start | bytes 786440 | tf_op jit(solution)/shard_map/ppermute | solution.py:41
  66.1 6.2 %collective-permute-start.14 = (bf16[64,2048]{1,0:T(8,128)(2,1)S(1)}, bf16[64,2048]{1,0:T(8,128)(2,1)S(1)}, u32[]{:S(2)}, u32[]{:S(2)}) collective-permute-start(bf16[64,2048]{1,0:T(8,128)(2,1)S(1)} %get-tuple-element.60.refs_0_.refs_2_.refs_4_), channel_id=1, source_target_pairs={{0,1},{1,0},{2,3},{3,2},{4,5},{5,4},{6,7},{7,6},{8,9},{9,8},{10,11... | collective-permute-start | bytes 786440 | tf_op jit(solution)/shard_map/ppermute | solution.py:41
  66.1 6.1 %collective-permute-start.15 = (bf16[64,2048]{1,0:T(8,128)(2,1)S(1)}, bf16[64,2048]{1,0:T(8,128)(2,1)S(1)}, u32[]{:S(2)}, u32[]{:S(2)}) collective-permute-start(bf16[64,2048]{1,0:T(8,128)(2,1)S(1)} %get-tuple-element.61.refs_4_), channel_id=1, source_target_pairs={{0,1},{1,0},{2,3},{3,2},{4,5},{5,4},{6,7},{7,6},{8,9},{9,8},{10,11... | collective-permute-start | bytes 786440 | tf_op jit(solution)/shard_map/ppermute | solution.py:41
  66.7 5.5 %collective-permute-start.21 = (bf16[64,1024]{1,0:T(8,128)(2,1)S(1)}, bf16[64,1024]{1,0:T(8,128)(2,1)S(1)}, u32[]{:S(2)}, u32[]{:S(2)}) collective-permute-start(bf16[64,1024]{1,0:T(8,128)(2,1)S(1)} %get-tuple-element.65), channel_id=1, source_target_pairs={{0,4},{4,0},{8,12},{12,8},{1,5},{5,1},{9,13},{13,9},{2,6},{6,2},{1... | collective-permute-start | bytes 393224 | tf_op jit(solution)/shard_map/ppermute | solution.py:46
  74.1 26.9 %collective-permute-start.19 = (bf16[384,640]{1,0:T(8,128)(2,1)S(1)}, bf16[384,640]{1,0:T(8,128)(2,1)S(1)}, u32[]{:S(2)}, u32[]{:S(2)}) collective-permute-start(bf16[384,640]{1,0:T(8,128)(2,1)S(1)} %shard_map.101.refs_9_.refs_0_), channel_id=1, source_target_pairs={{0,2},{2,0},{1,3},{3,1},{4,6},{6,4},{5,7},{7,5},{8,10},{10,8},{9,1... | collective-permute-start | bytes 1474568 | tf_op jit(solution)/shard_map/ppermute | solution.py:41
  89.0 1.9 %collective-permute-start.23 = (bf16[64,2048]{1,0:T(8,128)(2,1)S(1)}, bf16[64,2048]{1,0:T(8,128)(2,1)S(1)}, u32[]{:S(2)}, u32[]{:S(2)}) collective-permute-start(bf16[64,2048]{1,0:T(8,128)(2,1)S(1)} %get-tuple-element.75), channel_id=1, source_target_pairs={{0,1},{1,0},{2,3},{3,2},{4,5},{5,4},{6,7},{7,6},{8,9},{9,8},{10,11... | collective-permute-start | bytes 786440 | tf_op jit(solution)/shard_map/ppermute | solution.py:41
  89.1 22.2 %collective-permute-start.18 = (bf16[384,640]{1,0:T(8,128)(2,1)S(1)}, bf16[384,640]{1,0:T(8,128)(2,1)S(1)}, u32[]{:S(2)}, u32[]{:S(2)}) collective-permute-start(bf16[384,640]{1,0:T(8,128)(2,1)S(1)} %shard_map.102.refs_9_.refs_0_), channel_id=1, source_target_pairs={{0,2},{2,0},{1,3},{3,1},{4,6},{6,4},{5,7},{7,5},{8,10},{10,8},{9,1... | collective-permute-start | bytes 1474568 | tf_op jit(solution)/shard_map/ppermute | solution.py:41
  91.0 7.6 %collective-permute-start.24 = (bf16[64,1024]{1,0:T(8,128)(2,1)S(1)}, bf16[64,1024]{1,0:T(8,128)(2,1)S(1)}, u32[]{:S(2)}, u32[]{:S(2)}) collective-permute-start(bf16[64,1024]{1,0:T(8,128)(2,1)S(1)} %get-tuple-element.77), channel_id=1, source_target_pairs={{0,4},{4,0},{8,12},{12,8},{1,5},{5,1},{9,13},{13,9},{2,6},{6,2},{1... | collective-permute-start | bytes 393224 | tf_op jit(solution)/shard_map/ppermute | solution.py:46
  91.1 30.7 %collective-permute-start.17 = (bf16[384,512]{1,0:T(8,128)(2,1)S(1)}, bf16[384,512]{1,0:T(8,128)(2,1)S(1)}, u32[]{:S(2)}, u32[]{:S(2)}) collective-permute-start(bf16[384,512]{1,0:T(8,128)(2,1)S(1)} %shard_map.103.refs_6_.refs_0_), channel_id=1, source_target_pairs={{0,2},{2,0},{1,3},{3,1},{4,6},{6,4},{5,7},{7,5},{8,10},{10,8},{9,1... | collective-permute-start | bytes 1179656 | tf_op jit(solution)/shard_map/ppermute | solution.py:41
  92.6 6.0 %collective-permute-start.22 = (bf16[64,512]{1,0:T(8,128)(2,1)S(1)}, bf16[64,512]{1,0:T(8,128)(2,1)S(1)}, u32[]{:S(2)}, u32[]{:S(2)}) collective-permute-start(bf16[64,512]{1,0:T(8,128)(2,1)S(1)} %get-tuple-element.68), channel_id=1, source_target_pairs={{0,8},{4,12},{8,0},{12,4},{1,9},{5,13},{9,1},{13,5},{2,10},{6,14},... | collective-permute-start | bytes 196616 | tf_op jit(solution)/shard_map/ppermute | solution.py:46
  98.6 12.7 %collective-permute-start.25 = (bf16[64,512]{1,0:T(8,128)(2,1)S(1)}, bf16[64,512]{1,0:T(8,128)(2,1)S(1)}, u32[]{:S(2)}, u32[]{:S(2)}) collective-permute-start(bf16[64,512]{1,0:T(8,128)(2,1)S(1)} %get-tuple-element.84), channel_id=1, source_target_pairs={{0,8},{4,12},{8,0},{12,4},{1,9},{5,13},{9,1},{13,5},{2,10},{6,14},... | collective-permute-start | bytes 196616 | tf_op jit(solution)/shard_map/ppermute | solution.py:46
  123.6 1.6 %collective-permute-start.26 = (bf16[64,2048]{1,0:T(8,128)(2,1)S(1)}, bf16[64,2048]{1,0:T(8,128)(2,1)S(1)}, u32[]{:S(2)}, u32[]{:S(2)}) collective-permute-start(bf16[64,2048]{1,0:T(8,128)(2,1)S(1)} %get-tuple-element.95), channel_id=1, source_target_pairs={{0,1},{1,0},{2,3},{3,2},{4,5},{5,4},{6,7},{7,6},{8,9},{9,8},{10,11... | collective-permute-start | bytes 786440 | tf_op jit(solution)/shard_map/ppermute | solution.py:41
  125.3 5.6 %collective-permute-start.27 = (bf16[64,1024]{1,0:T(8,128)(2,1)S(1)}, bf16[64,1024]{1,0:T(8,128)(2,1)S(1)}, u32[]{:S(2)}, u32[]{:S(2)}) collective-permute-start(bf16[64,1024]{1,0:T(8,128)(2,1)S(1)} %get-tuple-element.97), channel_id=1, source_target_pairs={{0,4},{4,0},{8,12},{12,8},{1,5},{5,1},{9,13},{13,9},{2,6},{6,2},{1... | collective-permute-start | bytes 393224 | tf_op jit(solution)/shard_map/ppermute | solution.py:46
  130.9 5.9 %collective-permute-start.28 = (bf16[64,512]{1,0:T(8,128)(2,1)S(1)}, bf16[64,512]{1,0:T(8,128)(2,1)S(1)}, u32[]{:S(2)}, u32[]{:S(2)}) collective-permute-start(bf16[64,512]{1,0:T(8,128)(2,1)S(1)} %get-tuple-element.99), channel_id=1, source_target_pairs={{0,8},{4,12},{8,0},{12,4},{1,9},{5,13},{9,1},{13,5},{2,10},{6,14},... | collective-permute-start | bytes 196616 | tf_op jit(solution)/shard_map/ppermute | solution.py:46

commit v11 on v10

--- a/solution.py
+++ b/solution.py
@@ -8,7 +8,7 @@
 from jax.sharding import PartitionSpec as P
 
 PIECES = (1, 1, 1)
-PARTS = (5, 5, 4)
+PARTS = (4, 3)
 MIB = 1 << 20
 
 
@@ -209,15 +209,20 @@
     )[0]
 
 
-def backward(own, other, where, weights, span, rows, before, final, after=(), cost=1.0):
+def backward(own, other, where, weights, span, rows, before, final, after=(), cost=1.0, above=()):
     lower, upper = span
     width, features, tokens = upper - lower, weights[0].shape[0], 2 * rows
     count = len(own)
-    ins_all = (*own, *other, *weights, *(() if before is None else (before,)))
+    ins_all = (*own, *other, *weights, *(() if before is None else (before,)), *above)
+    upper_rows = above[0].shape[0] if above else 0
     outs_all = [((width, tokens), jnp.bfloat16)] + [((tokens, width), jnp.bfloat16)] * 2
-    outs_all += [((rows, features), jnp.float32), ((rows, features), jnp.bfloat16)] if final else [((tokens, features), jnp.float32)]
-
-    def kernel(ins, outs):
+    height = upper_rows + rows
+    outs_all += [((height, features), jnp.float32), ((height, features), jnp.bfloat16)] if final else [((tokens, features), jnp.float32)]
+
+    def kernel(ins, outs):
+        for k in range(len(above)):
+            outs[3 + k][:upper_rows] = ins[len(ins_all) - len(above) + k][...]
+
         @pl.loop(0, width // 128)
         def _(j):
             at = lanes(j, 128)
@@ -237,8 +242,8 @@
             if before is not None:
                 value = value + ins[2 * count + 2][:, at]
             if final:
-                outs[3][:, at] = value[:rows]
-                outs[4][:, at] = value[rows:].astype(jnp.bfloat16)
+                outs[3][upper_rows:, at] = value[:rows]
+                outs[4][upper_rows:, at] = value[rows:].astype(jnp.bfloat16)
             else:
                 outs[3][:, at] = value
 
@@ -262,7 +267,7 @@
     return local(kernel, outs, (value, theirs), limit=4)
 
 
-def fold_far(value, theirs):
+def fold_far(value, theirs, after=()):
     rows, width = value.shape[0], value.shape[1] // 2
 
     def kernel(ins, outs):
@@ -272,7 +277,7 @@
             out[...] = (ins[0][:, source] + ins[1][:, source].astype(jnp.float32)).astype(out.dtype)
 
     outs = [((rows, width), jnp.float32), ((rows, width), jnp.bfloat16)]
-    return local(kernel, outs, (value, theirs), limit=4)
+    return local(kernel, outs, (value, theirs), after, limit=4)
 
 
 def fold_last(mine, theirs, earlier=()):
@@ -436,18 +441,18 @@
         sums.append(done)
         return after
 
-    def backward_piece(index, part, before, final, after):
+    def backward_piece(index, part, before, final, after, above=()):
         own, where = sums[index][part]
         span = parts[part] if index == last else whole
         other = [shifted(value, "wid", 1) for value in own]
-        cost = 1.0 if index == last else 60.0
-        return backward(own, other, where, back_weights, span, heights[index], before, final, after, cost)
+        cost = 0.1 if index == last else 60.0
+        return backward(own, other, where, back_weights, span, heights[index], before, final, after, cost, above)
 
     def near_step(results):
         return fold_near(results[3], shifted(results[4], "tok", 1))
 
-    def far_step(near):
-        return fold_far(near[0], swapped(near[1], "hid", 1))
+    def far_step(near, after=()):
+        return fold_far(near[0], swapped(near[1], "hid", 1), after)
 
     def end_step(far, earlier=()):
         return fold_last(far[0], swapped(far[1], "hid", 2), earlier)
@@ -455,40 +460,32 @@
     done = forward_piece(1, (dhid,))
     grads = [backward_piece(0, 0, None, True, done)]
     inputs.append(gather_both(last, (inputs[1][0][0],), (grads[0][1],)))
-    near = near_step(grads[0])
-    done = forward_piece(last, (near[0],))
+    done = forward_piece(last, (grads[0][1],))
     all_x, all_y = [
         joined([(array, p[k][2], rows) for p, rows in zip(inputs, heights) for array in p[k][:2]], k == 0, done)
         for k in range(2)
     ]
-    far = far_step(near)
-    grads.append(backward_piece(1, 0, None, True, (all_x, all_y, far[0])))
-    finished = [end_step(far)]
+    grads.append(backward_piece(1, 0, None, True, (all_x, all_y), grads[0][3:]))
 
     def with_last(results, k, part):
         return [(grads[c][k], parts[part][0]) for c in range(last)] + [(results[k], 0)]
 
-    down, columns, before, waits = (), (), None, (grads[1][1], finished[0])
-    for part in range(len(parts)):
-        final = part == len(parts) - 1
-        results = backward_piece(last, part, before, final, waits)
-        before = results[3]
-        near = near_step(results if final else grads[1]) if final or part == 0 else None
-        down, down_token = row_grads(
-            with_last(results, 0, part), all_y, parts[part], total, down, () if final or near is None else (near[0],),
-            3.0 if final else 0.1,
-        )
-        down = (down,)
-        far = far_step(near) if near is not None else None
-        ahead = () if near is None else (near[0],) if final else (far[0],)
-        *columns, token = column_grads(
-            all_x, with_last(results, 1, part), with_last(results, 2, part), parts[part], total, tuple(columns),
-            (*ahead, down_token), 5.0 if final else 0.1,
-        )
-        if part == 0:
-            finished.append(end_step(far))
-        waits = (token, finished[-1])
-    return end_step(far, finished), *columns, *down
+    near = near_step(grads[1])
+    first = backward_piece(last, 0, None, False, (near[0],))
+    down, token = row_grads(with_last(first, 0, 0), all_y, parts[0], total, (), (), 2.0)
+    far = far_step(near, (token,))
+    gate, up, token = column_grads(
+        all_x, with_last(first, 1, 0), with_last(first, 2, 0), parts[0], total, (), (far[0], token)
+    )
+    finished = end_step(far)
+    second = backward_piece(last, 1, first[3], True, (token, finished))
+    near = near_step(second)
+    down, token = row_grads(with_last(second, 0, 1), all_y, parts[1], total, (down,), (), 3.0)
+    far = far_step(near)
+    gate, up, _ = column_grads(
+        all_x, with_last(second, 1, 1), with_last(second, 2, 1), parts[1], total, (gate, up), (near[0], token), 5.0
+    )
+    return end_step(far, (finished,)), gate, up, down
 
 
 def shards(acts, grad_out, w_gate, w_up, w_down):

time: 138 us -> 133 us (0.964)
  starting transfers between devices: 34 us -> 30 us
  Pallas kernels: 57.9 us -> 54 us
  waiting for transfers between devices: 43.6 us -> 47 us
    ppermute x15 -> x13, waiting for transfers between devices: 8.81 us -> 23.1 us  [shifted(): return lax.ppermute(value, axis, [(i, (i + step) % n) for i in range(n)])]
    ppermute x14 -> x12, waiting for transfers between devices: 34.8 us -> 23.9 us  [swapped(): return lax.ppermute(value, axis, [(i, i ^ bit) for i in range(n)])]
    pallas_call x6 -> x4, Pallas kernels: 22.9 us -> 19.3 us  [gradients(): pl.pallas_call(body, grid=grid, out_shape=[jax.ShapeDtypeStruct(shape, jn...]
    ppermute x14 -> x12, starting transfers between devices: 22.7 us -> 20.2 us  [swapped(): return lax.ppermute(value, axis, [(i, i ^ bit) for i in range(n)])]
    ppermute x15 -> x13, starting transfers between devices: 11.3 us -> 9.76 us  [shifted(): return lax.ppermute(value, axis, [(i, (i + step) % n) for i in range(n)])]
    pallas_call x33 -> x28, Pallas kernels: 35 us -> 34.7 us  [local(): pl.pallas_call(body, out_shape=shapes, in_specs=[VMEM] * len(args) + [ANY...]
  transfers between devices with their start and end apart: 29 -> 25, of which waited for: 13 -> 14; matrix products, arithmetic and copies ran while one was open for 0% -> 0% of each run, Pallas kernels for 40% -> 38%
where the time goes in v11:
time: 133 us
  Pallas kernels  54 us (41%)
  waiting for transfers between devices  47 us (35%)
  starting transfers between devices  30 us (23%)
    pallas_call x28, Pallas kernels, local(): pl.pallas_call(body, out_shape=shapes, in_specs=[VMEM] * len(args) + [ANY...  34.7 us
    ppermute x12, waiting for transfers between devices, swapped(): return lax.ppermute(value, axis, [(i, i ^ bit) for i in range(n)])  23.9 us
    ppermute x13, waiting for transfers between devices, shifted(): return lax.ppermute(value, axis, [(i, (i + step) % n) for i in range(n)])  23.1 us
    ppermute x12, starting transfers between devices, swapped(): return lax.ppermute(value, axis, [(i, i ^ bit) for i in range(n)])  20.2 us
    pallas_call x4, Pallas kernels, gradients(): pl.pallas_call(body, grid=grid, out_shape=[jax.ShapeDtypeStruct(shape, jn...  19.3 us
    ppermute x13, starting transfers between devices, shifted(): return lax.ppermute(value, axis, [(i, (i + step) % n) for i in range(n)])  9.76 us
  transfers between devices with their start and end apart: 25, of which 14 were waited for; matrix products, arithmetic and copies ran while one was open for 0% of the time, Pallas kernels for 38%

profile of v11, /device:TPU:0, one launch (start us, length us, event | category | flops | bytes accessed | tf_op | source)
XLA Modules:
  0.0 132.9 jit_solution(3575007651257209171)
XLA Ops:
  0.6 0.9 copy-done.2
  1.6 4.1 %collective-permute-start.5 = (bf16[64,512]{1,0:T(8,128)(2,1)S(1)}, bf16[64,512]{1,0:T(8,128)(2,1)S(1)}, u32[]{:S(2)}, u32[]{:S(2)}) collective-permute-start(bf16[64,512]{1,0:T(8,128)(2,1)S(1)} %shard_map.91.refs_0_), channel_id=1, source_target_pairs={{0,8},{4,12},{8,0},{12,4},{1,9},{5,13},{9,1},{13,5},{2,10},{6,14},... | collective-permute-start | bytes 196616 | tf_op jit(solution)/shard_map/ppermute | solution.py:46
  5.7 3.6 %collective-permute-done.5.refs_1_ = bf16[64,512]{1,0:T(8,128)(2,1)S(1)} collective-permute-done((bf16[64,512]{1,0:T(8,128)(2,1)S(1)}, bf16[64,512]{1,0:T(8,128)(2,1)S(1)}, u32[]{:S(2)}, u32[]{:S(2)}) %collective-permute-start.5) | collective-permute-done | bytes 65568 | tf_op jit(solution)/shard_map/ppermute | solution.py:46
  9.3 0.6 collective-permute-start.6
  10.0 3.4 %collective-permute-start = (bf16[64,512]{1,0:T(8,128)(2,1)S(1)}, bf16[64,512]{1,0:T(8,128)(2,1)S(1)}, u32[]{:S(2)}, u32[]{:S(2)}) collective-permute-start(bf16[64,512]{1,0:T(8,128)(2,1)S(1)} %shard_map.84.refs_0_), channel_id=1, source_target_pairs={{0,8},{4,12},{8,0},{12,4},{1,9},{5,13},{9,1},{13,5},{2,10},{6,14},... | collective-permute-start | bytes 196616 | tf_op jit(solution)/shard_map/ppermute | solution.py:46
  13.4 1.7 %collective-permute-done.6.refs_1_ = bf16[64,1024]{1,0:T(8,128)(2,1)S(1)} collective-permute-done((bf16[64,1024]{1,0:T(8,128)(2,1)S(1)}, bf16[64,1024]{1,0:T(8,128)(2,1)S(1)}, u32[]{:S(2)}, u32[]{:S(2)}) %collective-permute-start.6) | collective-permute-done | bytes 131104 | tf_op jit(solution)/shard_map/ppermute | solution.py:46
  15.2 1.1 collective-permute-done.refs_1_
  16.3 1.9 %collective-permute-start.1 = (bf16[64,1024]{1,0:T(8,128)(2,1)S(1)}, bf16[64,1024]{1,0:T(8,128)(2,1)S(1)}, u32[]{:S(2)}, u32[]{:S(2)}) collective-permute-start(bf16[64,1024]{1,0:T(8,128)(2,1)S(1)} %shard_map.85.refs_0_), channel_id=1, source_target_pairs={{0,4},{4,0},{8,12},{12,8},{1,5},{5,1},{9,13},{13,9},{2,6},{6,2},{1... | collective-permute-start | bytes 393224 | tf_op jit(solution)/shard_map/ppermute | solution.py:46
  18.2 2.1 %shard_map.94.refs_3_.refs_0_ = bf16[256,1792]{1,0:T(8,128)(2,1)S(1)} custom-call(bf16[64,2048]{1,0:T(8,128)(2,1)S(1)} %shard_map.93.refs_0_.refs_2_, bf16[64,2048]{1,0:T(8,128)(2,1)S(1)} %collective-permute-done.7.refs_1_.refs_3_, bf16[64,2048]{1,0:T(8,128)(2,1)S(1)} %shard_map.93.refs_0_.refs_2_, ...), custom_call_target="tpu_custom_call" | custom-call | flops 345000000 | tf_op jit(solution)/shard_map/pallas_call | solution.py:101
  20.3 1.6 %collective-permute-start.9 = (bf16[256,1792]{1,0:T(8,128)(2,1)S(1)}, bf16[256,1792]{1,0:T(8,128)(2,1)S(1)}, u32[]{:S(2)}, u32[]{:S(2)}) collective-permute-start(bf16[256,1792]{1,0:T(8,128)(2,1)S(1)} %shard_map.94.refs_3_.refs_0_), channel_id=1, source_target_pairs={{0,2},{2,0},{1,3},{3,1},{4,6},{6,4},{5,7},{7,5},{8,10},{10,8},{9,1... | collective-permute-start | bytes 2752520 | tf_op jit(solution)/shard_map/ppermute | solution.py:41
  22.0 2.4 %collective-permute-start.2 = (bf16[128,512]{1,0:T(8,128)(2,1)S(1)}, bf16[128,512]{1,0:T(8,128)(2,1)S(1)}, u32[]{:S(2)}, u32[]{:S(2)}) collective-permute-start(bf16[128,512]{1,0:T(8,128)(2,1)S(1)} %shard_map.87.refs_0_), channel_id=1, source_target_pairs={{0,8},{4,12},{8,0},{12,4},{1,9},{5,13},{9,1},{13,5},{2,10},{6,14},... | collective-permute-start | bytes 393224 | tf_op jit(solution)/shard_map/ppermute | solution.py:46
  24.4 7.3 %collective-permute-done.2.refs_1_ = bf16[128,512]{1,0:T(8,128)(2,1)S(1)} collective-permute-done((bf16[128,512]{1,0:T(8,128)(2,1)S(1)}, bf16[128,512]{1,0:T(8,128)(2,1)S(1)}, u32[]{:S(2)}, u32[]{:S(2)}) %collective-permute-start.2) | collective-permute-done | bytes 131104 | tf_op jit(solution)/shard_map/ppermute | solution.py:46
  31.7 0.5 collective-permute-start.3
  32.2 2.5 %shard_map.95.refs_9_.refs_1_ = bf16[128,1792]{1,0:T(8,128)(2,1)S(1)} custom-call(bf16[64,2048]{1,0:T(8,128)(2,1)S(1)} %shard_map.86.refs_2_.refs_0_, bf16[64,2048]{1,0:T(8,128)(2,1)S(1)} %collective-permute-done.8.refs_1_, bf16[1792,2048]{1,0:T(8,128)(2,1)S(1)} %bitcast.1, bf16[256,1792]{1,0:T(8,128)(2,1)S(1)} %shard_map.94.refs_3_.refs_0_), custom_call_target="tpu_custom_call" | custom-call | flops 345000000 | tf_op jit(solution)/shard_map/pallas_call | solution.py:101
  34.7 1.6 %collective-permute-start.10 = (bf16[128,1792]{1,0:T(8,128)(2,1)S(1)}, bf16[128,1792]{1,0:T(8,128)(2,1)S(1)}, u32[]{:S(2)}, u32[]{:S(2)}) collective-permute-start(bf16[128,1792]{1,0:T(8,128)(2,1)S(1)} %shard_map.95.refs_9_.refs_1_), channel_id=1, source_target_pairs={{0,2},{2,0},{1,3},{3,1},{4,6},{6,4},{5,7},{7,5},{8,10},{10,8},{9,1... | collective-permute-start | bytes 1376264 | tf_op jit(solution)/shard_map/ppermute | solution.py:41
  36.3 3.4 %collective-permute-done.3.refs_1_ = bf16[128,1024]{1,0:T(8,128)(2,1)S(1)} collective-permute-done((bf16[128,1024]{1,0:T(8,128)(2,1)S(1)}, bf16[128,1024]{1,0:T(8,128)(2,1)S(1)}, u32[]{:S(2)}, u32[]{:S(2)}) %collective-permute-start.3) | collective-permute-done | bytes 262176 | tf_op jit(solution)/shard_map/ppermute | solution.py:46
  39.8 0.5 collective-permute-start.12
  40.3 2.5 %collective-permute-start.4 = (bf16[128,512]{1,0:T(8,128)(2,1)S(1)}, bf16[128,512]{1,0:T(8,128)(2,1)S(1)}, u32[]{:S(2)}, u32[]{:S(2)}) collective-permute-start(bf16[128,512]{1,0:T(8,128)(2,1)S(1)} %shard_map.90.refs_0_), channel_id=1, source_target_pairs={{0,8},{4,12},{8,0},{12,4},{1,9},{5,13},{9,1},{13,5},{2,10},{6,14},... | collective-permute-start | bytes 393224 | tf_op jit(solution)/shard_map/ppermute | solution.py:46
  42.8 4.4 %shard_map.96.refs_6_.refs_0_ = bf16[384,1792]{1,0:T(8,128)(2,1)S(1)} custom-call(bf16[64,2048]{1,0:T(8,128)(2,1)S(1)} %get-tuple-element.44.refs_2_.refs_0_, bf16[64,2048]{1,0:T(8,128)(2,1)S(1)} %collective-permute-done.11.refs_1_.refs_3_, bf16[64,2048]{1,0:T(8,128)(2,1)S(1)} %get-tuple-element.44.refs_2_.refs_0_, ...), custom_call_target="tpu_custom_call" | custom-call | flops 345000000 | tf_op jit(solution)/shard_map/pallas_call | solution.py:101
  47.2 1.6 %collective-permute-start.18 = (bf16[384,1792]{1,0:T(8,128)(2,1)S(1)}, bf16[384,1792]{1,0:T(8,128)(2,1)S(1)}, u32[]{:S(2)}, u32[]{:S(2)}) collective-permute-start(bf16[384,1792]{1,0:T(8,128)(2,1)S(1)} %shard_map.96.refs_6_.refs_0_), channel_id=1, source_target_pairs={{0,2},{2,0},{1,3},{3,1},{4,6},{6,4},{5,7},{7,5},{8,10},{10,8},{9,1... | collective-permute-start | bytes 4128776 | tf_op jit(solution)/shard_map/ppermute | solution.py:41
  48.8 4.4 %collective-permute-done.10.refs_3_ = bf16[128,1792]{1,0:T(8,128)(2,1)S(1)} collective-permute-done((bf16[128,1792]{1,0:T(8,128)(2,1)S(1)}, bf16[128,1792]{1,0:T(8,128)(2,1)S(1)}, u32[]{:S(2)}, u32[]{:S(2)}) %collective-permute-start.10) | collective-permute-done | bytes 458784 | tf_op jit(solution)/shard_map/ppermute | solution.py:41
  53.2 6.3 %shard_map.97 = (bf16[1792,128]{1,0:T(8,128)(2,1)S(1)}, bf16[128,1792]{1,0:T(8,128)(2,1)S(1)}, bf16[128,1792]{1,0:T(8,128)(2,1)S(1)}, f32[64,2048]{1,0:T(8,128)S(1)}, bf16[64,2048]{1,0:T(8,128)(2,1)S(1)}) custom-call(bf16[256,1792]{1,0:T(8,128)(2,1)S(1)} %shard_map.94.refs_3_.refs_0_, bf16[128,1792]{1,0:T(8,128)(2,1)S(1)} %shard_map.95.refs_9_.refs_1_, ...), custom_call_target="tpu_custom_call" | custom-call | flops 69000003584 | tf_op jit(solution)/shard_map/pallas_call | solution.py:101
  59.7 6.4 %collective-permute-done.13.refs_1_ = bf16[128,1024]{1,0:T(8,128)(2,1)S(1)} collective-permute-done((bf16[128,1024]{1,0:T(8,128)(2,1)S(1)}, bf16[128,1024]{1,0:T(8,128)(2,1)S(1)}, u32[]{:S(2)}, u32[]{:S(2)}) %collective-permute-start.13) | collective-permute-done | bytes 262176 | tf_op jit(solution)/shard_map/ppermute | solution.py:46
  66.1 0.5 collective-permute-start.15
  66.6 1.0 collective-permute-done.14.refs_1_.refs_3_.refs_5_
  67.7 0.4 collective-permute-done.15.refs_5_
  68.0 2.6 %shard_map.100.refs_9_.refs_0_ = bf16[384,1024]{1,0:T(8,128)(2,1)S(1)} custom-call(bf16[64,2048]{1,0:T(8,128)(2,1)S(1)} %get-tuple-element.47.refs_0_.refs_2_.refs_4_, bf16[64,2048]{1,0:T(8,128)(2,1)S(1)} %collective-permute-done.14.refs_1_.refs_3_.refs_5_, bf16[64,2048]{1,0:T(8,128)(2,1)S(1)} %get-tuple-element.47.refs_0_.refs_2_.refs_4_, ...), custom_call_target="tpu_custom_call" | custom-call | flops 345000000 | tf_op jit(solution)/shard_map/pallas_call | solution.py:101
  70.6 1.8 %collective-permute-start.17 = (bf16[384,1024]{1,0:T(8,128)(2,1)S(1)}, bf16[384,1024]{1,0:T(8,128)(2,1)S(1)}, u32[]{:S(2)}, u32[]{:S(2)}) collective-permute-start(bf16[384,1024]{1,0:T(8,128)(2,1)S(1)} %shard_map.100.refs_9_.refs_0_), channel_id=1, source_target_pairs={{0,2},{2,0},{1,3},{3,1},{4,6},{6,4},{5,7},{7,5},{8,10},{10,8},{9,1... | collective-permute-start | bytes 2359304 | tf_op jit(solution)/shard_map/ppermute | solution.py:41
  72.5 2.0 %shard_map.101.refs_6_.refs_0_ = bf16[384,768]{1,0:T(8,128)(2,1)S(1)} custom-call(bf16[64,2048]{1,0:T(8,128)(2,1)S(1)} %get-tuple-element.47.refs_0_.refs_2_.refs_4_, bf16[64,2048]{1,0:T(8,128)(2,1)S(1)} %collective-permute-done.14.refs_1_.refs_3_.refs_5_, bf16[64,2048]{1,0:T(8,128)(2,1)S(1)} %get-tuple-element.47.refs_0_.refs_2_.refs_4_, ...), custom_call_target="tpu_custom_call" | custom-call | flops 345000000 | tf_op jit(solution)/shard_map/pallas_call | solution.py:101
  74.5 0.6 shard_map.102.refs_6_.refs_0_
  75.1 0.2 shard_map.103.refs_7_.refs_3_
  75.3 7.4 %collective-permute-done.18.refs_1_ = bf16[384,1792]{1,0:T(8,128)(2,1)S(1)} collective-permute-done((bf16[384,1792]{1,0:T(8,128)(2,1)S(1)}, bf16[384,1792]{1,0:T(8,128)(2,1)S(1)}, u32[]{:S(2)}, u32[]{:S(2)}) %collective-permute-start.18) | collective-permute-done | bytes 1376288 | tf_op jit(solution)/shard_map/ppermute | solution.py:41
  82.7 6.4 %shard_map.104 = (bf16[1792,128]{1,0:T(8,128)(2,1)S(1)}, bf16[128,1792]{1,0:T(8,128)(2,1)S(1)}, bf16[128,1792]{1,0:T(8,128)(2,1)S(1)}, f32[128,2048]{1,0:T(8,128)S(1)}, bf16[128,2048]{1,0:T(8,128)(2,1)S(1)}) custom-call(bf16[384,1792]{1,0:T(8,128)(2,1)S(1)} %shard_map.96.refs_6_.refs_0_, bf16[384,1792]{1,0:T(8,128)(2,1)S(1)} %collective-permute-done.18.refs_1_, ...), custom_call_target="tpu_custom_call" | custom-call | flops 69000003584 | tf_op jit(solution)/shard_map/pallas_call | solution.py:101
  89.2 1.8 %collective-permute-start.16 = (bf16[384,768]{1,0:T(8,128)(2,1)S(1)}, bf16[384,768]{1,0:T(8,128)(2,1)S(1)}, u32[]{:S(2)}, u32[]{:S(2)}) collective-permute-start(bf16[384,768]{1,0:T(8,128)(2,1)S(1)} %shard_map.101.refs_6_.refs_0_), channel_id=1, source_target_pairs={{0,2},{2,0},{1,3},{3,1},{4,6},{6,4},{5,7},{7,5},{8,10},{10,8},{9,1... | collective-permute-start | bytes 1769480 | tf_op jit(solution)/shard_map/ppermute | solution.py:41
  91.1 0.1 shard_map.105
  91.2 8.3 %collective-permute-done.17.refs_1_ = bf16[384,1024]{1,0:T(8,128)(2,1)S(1)} collective-permute-done((bf16[384,1024]{1,0:T(8,128)(2,1)S(1)}, bf16[384,1024]{1,0:T(8,128)(2,1)S(1)}, u32[]{:S(2)}, u32[]{:S(2)}) %collective-permute-start.17) | collective-permute-done | bytes 786464 | tf_op jit(solution)/shard_map/ppermute | solution.py:41
  99.5 3.7 %shard_map.106 = (bf16[1024,128]{1,0:T(8,128)(2,1)S(1)}, bf16[128,1024]{1,0:T(8,128)(2,1)S(1)}, bf16[128,1024]{1,0:T(8,128)(2,1)S(1)}, f32[128,2048]{1,0:T(8,128)S(1)}) custom-call(bf16[384,1024]{1,0:T(8,128)(2,1)S(1)} %shard_map.100.refs_9_.refs_0_, bf16[384,1024]{1,0:T(8,128)(2,1)S(1)} %collective-permute-done.17.refs_1_, bf16[2048,1792]{1,0:T(8,128)(2,1)S(1)} %copy-done, ...), custom_call_target="tpu_custom_call" | custom-call | flops 115000000 | tf_op jit(solution)/shard_map/pallas_call | solution.py:101
  103.2 4.3 %shard_map.107 = (bf16[1792,2048]{1,0:T(8,128)(2,1)}, bf16[16,128]{1,0:T(8,128)(2,1)S(1)}) custom-call(bf16[1792,128]{1,0:T(8,128)(2,1)S(1)} %get-tuple-element.61.refs_0_, bf16[1792,128]{1,0:T(8,128)(2,1)S(1)} %get-tuple-element.62.refs_1_, bf16[1024,128]{1,0:T(8,128)(2,1)S(1)} %get-tuple-element.63.refs_2_, bf16[384,2048]{1,0:T(8,128)(2,1)S(1)} %shard_map.103.refs_7_.refs_3_), custom_call_target="tpu_custom_call" | custom-call | flops 2300000000 | tf_op jit(solution)/shard_map/pallas_call | solution.py:321
  107.5 2.1 %collective-permute-start.21 = (bf16[128,512]{1,0:T(8,128)(2,1)S(1)}, bf16[128,512]{1,0:T(8,128)(2,1)S(1)}, u32[]{:S(2)}, u32[]{:S(2)}) collective-permute-start(bf16[128,512]{1,0:T(8,128)(2,1)S(1)} %get-tuple-element.67), channel_id=1, source_target_pairs={{0,8},{4,12},{8,0},{12,4},{1,9},{5,13},{9,1},{13,5},{2,10},{6,14},... | collective-permute-start | bytes 393224 | tf_op jit(solution)/shard_map/ppermute | solution.py:46
  109.6 6.3 %shard_map.109 = (bf16[2048,1792]{1,0:T(8,128)(2,1)}, bf16[2048,1792]{1,0:T(8,128)(2,1)}, bf16[16,128]{1,0:T(8,128)(2,1)S(1)}) custom-call(bf16[2048,384]{1,0:T(8,128)(2,1)S(1)} %shard_map.102.refs_6_.refs_0_, bf16[128,1792]{1,0:T(8,128)(2,1)S(1)} %get-tuple-element.46.refs_2_.refs_9_.refs_1_, bf16[128,1792]{1,0:T(8,128)(2,1)S(1)} %get-tuple-element.55.refs_2_, ...), custom_call_target="tpu_custom_call" | custom-call | flops 115000000 | tf_op jit(solution)/shard_map/pallas_call | solution.py:321
  116.0 2.8 %shard_map.111 = (bf16[768,128]{1,0:T(8,128)(2,1)S(1)}, bf16[128,768]{1,0:T(8,128)(2,1)S(1)}, bf16[128,768]{1,0:T(8,128)(2,1)S(1)}, f32[64,2048]{1,0:T(8,128)S(1)}, bf16[64,2048]{1,0:T(8,128)(2,1)S(1)}) custom-call(bf16[384,768]{1,0:T(8,128)(2,1)S(1)} %shard_map.101.refs_6_.refs_0_, bf16[384,768]{1,0:T(8,128)(2,1)S(1)} %collective-permute-done.16.refs_1_, ...), custom_call_target="tpu_custom_call" | custom-call | flops 115000000 | tf_op jit(solution)/shard_map/pallas_call | solution.py:101
  118.9 1.5 %collective-permute-done.22.refs_1_ = bf16[64,2048]{1,0:T(8,128)(2,1)S(1)} collective-permute-done((bf16[64,2048]{1,0:T(8,128)(2,1)S(1)}, bf16[64,2048]{1,0:T(8,128)(2,1)S(1)}, u32[]{:S(2)}, u32[]{:S(2)}) %collective-permute-start.22) | collective-permute-done | bytes 262176 | tf_op jit(solution)/shard_map/ppermute | solution.py:41
  120.5 1.5 %collective-permute-start.23 = (bf16[64,1024]{1,0:T(8,128)(2,1)S(1)}, bf16[64,1024]{1,0:T(8,128)(2,1)S(1)}, u32[]{:S(2)}, u32[]{:S(2)}) collective-permute-start(bf16[64,1024]{1,0:T(8,128)(2,1)S(1)} %get-tuple-element.71), channel_id=1, source_target_pairs={{0,4},{4,0},{8,12},{12,8},{1,5},{5,1},{9,13},{13,9},{2,6},{6,2},{1... | collective-permute-start | bytes 393224 | tf_op jit(solution)/shard_map/ppermute | solution.py:46
  122.0 3.6 %shard_map.115 = (bf16[1792,2048]{1,0:T(8,128)(2,1)}, bf16[16,128]{1,0:T(8,128)(2,1)S(1)}) custom-call(bf16[1792,128]{1,0:T(8,128)(2,1)S(1)} %get-tuple-element.61.refs_0_, bf16[1792,128]{1,0:T(8,128)(2,1)S(1)} %get-tuple-element.62.refs_1_, bf16[768,128]{1,0:T(8,128)(2,1)S(1)} %get-tuple-element.78.refs_2_, ...), custom_call_target="tpu_custom_call", output_to_operand_aliasing={{0}: (4, {})} | custom-call | flops 3449999872 | tf_op jit(solution)/shard_map/pallas_call | solution.py:321
  125.6 0.5 collective-permute-done.23.refs_1_
  126.1 1.0 collective-permute-start.24
  127.1 5.1 %shard_map.116 = (bf16[2048,1792]{1,0:T(8,128)(2,1)}, bf16[2048,1792]{1,0:T(8,128)(2,1)}, bf16[16,128]{1,0:T(8,128)(2,1)}) custom-call(bf16[2048,384]{1,0:T(8,128)(2,1)S(1)} %shard_map.102.refs_6_.refs_0_, bf16[128,1792]{1,0:T(8,128)(2,1)S(1)} %get-tuple-element.46.refs_2_.refs_9_.refs_1_, ...), custom_call_target="tpu_custom_call", output_to_operand_aliasing={{0}: (7, {}), {1}: (8, {})} | custom-call | flops 5750000128 | tf_op jit(solution)/shard_map/pallas_call | solution.py:321
  132.2 0.7 shard_map.114
  (50 shorter events, 1.1 us)
Async XLA Ops:
  0.6 0.9 copy-start.2
  1.6 8.4 %copy-start.3 = (bf16[192,512]{1,0:T(8,128)(2,1)S(1)}, bf16[192,512]{1,0:T(8,128)(2,1)}, u32[]{:S(2)}) copy-start(bf16[192,512]{1,0:T(8,128)(2,1)} %source.1) | copy-start | bytes 589828
  1.6 8.4 %copy-start.4 = (bf16[192,512]{1,0:T(8,128)(2,1)S(1)}, bf16[192,512]{1,0:T(8,128)(2,1)}, u32[]{:S(2)}) copy-start(bf16[192,512]{1,0:T(8,128)(2,1)} %refs_1_.5) | copy-start | bytes 589828
  1.6 16.6 %copy-start = (bf16[2048,1792]{1,0:T(8,128)(2,1)S(1)}, bf16[2048,1792]{1,0:T(8,128)(2,1)}, u32[]{:S(2)}) copy-start(bf16[2048,1792]{1,0:T(8,128)(2,1)} %refs_2_.7) | copy-start | bytes 22020100
  1.6 16.6 %copy-start.1 = (bf16[2048,1792]{1,0:T(8,128)(2,1)S(1)}, bf16[2048,1792]{1,0:T(8,128)(2,1)}, u32[]{:S(2)}) copy-start(bf16[2048,1792]{1,0:T(8,128)(2,1)} %refs_3_.5) | copy-start | bytes 22020100
  1.6 7.8 %collective-permute-start.5 = (bf16[64,512]{1,0:T(8,128)(2,1)S(1)}, bf16[64,512]{1,0:T(8,128)(2,1)S(1)}, u32[]{:S(2)}, u32[]{:S(2)}) collective-permute-start(bf16[64,512]{1,0:T(8,128)(2,1)S(1)} %shard_map.91.refs_0_), channel_id=1, source_target_pairs={{0,8},{4,12},{8,0},{12,4},{1,9},{5,13},{9,1},{13,5},{2,10},{6,14},... | collective-permute-start | bytes 196616 | tf_op jit(solution)/shard_map/ppermute | solution.py:46
  9.3 5.7 %collective-permute-start.6 = (bf16[64,1024]{1,0:T(8,128)(2,1)S(1)}, bf16[64,1024]{1,0:T(8,128)(2,1)S(1)}, u32[]{:S(2)}, u32[]{:S(2)}) collective-permute-start(bf16[64,1024]{1,0:T(8,128)(2,1)S(1)} %shard_map.92.refs_0_), channel_id=1, source_target_pairs={{0,4},{4,0},{8,12},{12,8},{1,5},{5,1},{9,13},{13,9},{2,6},{6,2},{1... | collective-permute-start | bytes 393224 | tf_op jit(solution)/shard_map/ppermute | solution.py:46
  10.0 6.3 %collective-permute-start = (bf16[64,512]{1,0:T(8,128)(2,1)S(1)}, bf16[64,512]{1,0:T(8,128)(2,1)S(1)}, u32[]{:S(2)}, u32[]{:S(2)}) collective-permute-start(bf16[64,512]{1,0:T(8,128)(2,1)S(1)} %shard_map.84.refs_0_), channel_id=1, source_target_pairs={{0,8},{4,12},{8,0},{12,4},{1,9},{5,13},{9,1},{13,5},{2,10},{6,14},... | collective-permute-start | bytes 196616 | tf_op jit(solution)/shard_map/ppermute | solution.py:46
  15.1 3.0 %collective-permute-start.7 = (bf16[64,2048]{1,0:T(8,128)(2,1)S(1)}, bf16[64,2048]{1,0:T(8,128)(2,1)S(1)}, u32[]{:S(2)}, u32[]{:S(2)}) collective-permute-start(bf16[64,2048]{1,0:T(8,128)(2,1)S(1)} %shard_map.93.refs_0_.refs_2_), channel_id=1, source_target_pairs={{0,1},{1,0},{2,3},{3,2},{4,5},{5,4},{6,7},{7,6},{8,9},{9,8},{10,11... | collective-permute-start | bytes 786440 | tf_op jit(solution)/shard_map/ppermute | solution.py:41
  16.3 5.6 %collective-permute-start.1 = (bf16[64,1024]{1,0:T(8,128)(2,1)S(1)}, bf16[64,1024]{1,0:T(8,128)(2,1)S(1)}, u32[]{:S(2)}, u32[]{:S(2)}) collective-permute-start(bf16[64,1024]{1,0:T(8,128)(2,1)S(1)} %shard_map.85.refs_0_), channel_id=1, source_target_pairs={{0,4},{4,0},{8,12},{12,8},{1,5},{5,1},{9,13},{13,9},{2,6},{6,2},{1... | collective-permute-start | bytes 393224 | tf_op jit(solution)/shard_map/ppermute | solution.py:46
  18.2 14.0 %slice-start = ((s8[7340032]{0:T(1024)(128)(4,1)}), s8[4194304]{0:T(1024)(128)(4,1)S(1)}, s32[]{:S(2)}) async-start(s8[7340032]{0:T(1024)(128)(4,1)} %bitcast), calls=%async_computation | async-start | bytes 8388608
  20.3 11.9 %slice-start.1 = ((s8[7340032]{0:T(1024)(128)(4,1)}), s8[3145728]{0:T(1024)(128)(4,1)S(1)}, s32[]{:S(2)}) async-start(s8[7340032]{0:T(1024)(128)(4,1)} %bitcast), calls=%async_computation.1 | async-start | bytes 6291456
  20.3 32.9 %collective-permute-start.9 = (bf16[256,1792]{1,0:T(8,128)(2,1)S(1)}, bf16[256,1792]{1,0:T(8,128)(2,1)S(1)}, u32[]{:S(2)}, u32[]{:S(2)}) collective-permute-start(bf16[256,1792]{1,0:T(8,128)(2,1)S(1)} %shard_map.94.refs_3_.refs_0_), channel_id=1, source_target_pairs={{0,2},{2,0},{1,3},{3,1},{4,6},{6,4},{5,7},{7,5},{8,10},{10,8},{9,1... | collective-permute-start | bytes 2752520 | tf_op jit(solution)/shard_map/ppermute | solution.py:41
  21.9 10.3 %collective-permute-start.8 = (bf16[64,2048]{1,0:T(8,128)(2,1)S(1)}, bf16[64,2048]{1,0:T(8,128)(2,1)S(1)}, u32[]{:S(2)}, u32[]{:S(2)}) collective-permute-start(bf16[64,2048]{1,0:T(8,128)(2,1)S(1)} %shard_map.86.refs_2_.refs_0_), channel_id=1, source_target_pairs={{0,1},{1,0},{2,3},{3,2},{4,5},{5,4},{6,7},{7,6},{8,9},{9,8},{10,11... | collective-permute-start | bytes 786440 | tf_op jit(solution)/shard_map/ppermute | solution.py:41
  22.0 9.7 %collective-permute-start.2 = (bf16[128,512]{1,0:T(8,128)(2,1)S(1)}, bf16[128,512]{1,0:T(8,128)(2,1)S(1)}, u32[]{:S(2)}, u32[]{:S(2)}) collective-permute-start(bf16[128,512]{1,0:T(8,128)(2,1)S(1)} %shard_map.87.refs_0_), channel_id=1, source_target_pairs={{0,8},{4,12},{8,0},{12,4},{1,9},{5,13},{9,1},{13,5},{2,10},{6,14},... | collective-permute-start | bytes 393224 | tf_op jit(solution)/shard_map/ppermute | solution.py:46
  31.7 8.0 %collective-permute-start.3 = (bf16[128,1024]{1,0:T(8,128)(2,1)S(1)}, bf16[128,1024]{1,0:T(8,128)(2,1)S(1)}, u32[]{:S(2)}, u32[]{:S(2)}) collective-permute-start(bf16[128,1024]{1,0:T(8,128)(2,1)S(1)} %shard_map.88.refs_0_), channel_id=1, source_target_pairs={{0,4},{4,0},{8,12},{12,8},{1,5},{5,1},{9,13},{13,9},{2,6},{6,2},{1... | collective-permute-start | bytes 786440 | tf_op jit(solution)/shard_map/ppermute | solution.py:46
  34.7 18.5 %collective-permute-start.10 = (bf16[128,1792]{1,0:T(8,128)(2,1)S(1)}, bf16[128,1792]{1,0:T(8,128)(2,1)S(1)}, u32[]{:S(2)}, u32[]{:S(2)}) collective-permute-start(bf16[128,1792]{1,0:T(8,128)(2,1)S(1)} %shard_map.95.refs_9_.refs_1_), channel_id=1, source_target_pairs={{0,2},{2,0},{1,3},{3,1},{4,6},{6,4},{5,7},{7,5},{8,10},{10,8},{9,1... | collective-permute-start | bytes 1376264 | tf_op jit(solution)/shard_map/ppermute | solution.py:41
  39.7 3.1 %collective-permute-start.11 = (bf16[64,2048]{1,0:T(8,128)(2,1)S(1)}, bf16[64,2048]{1,0:T(8,128)(2,1)S(1)}, u32[]{:S(2)}, u32[]{:S(2)}) collective-permute-start(bf16[64,2048]{1,0:T(8,128)(2,1)S(1)} %get-tuple-element.44.refs_2_.refs_0_), channel_id=1, source_target_pairs={{0,1},{1,0},{2,3},{3,2},{4,5},{5,4},{6,7},{7,6},{8,9},{9,8},{10,11... | collective-permute-start | bytes 786440 | tf_op jit(solution)/shard_map/ppermute | solution.py:41
  39.8 3.0 %collective-permute-start.12 = (bf16[64,2048]{1,0:T(8,128)(2,1)S(1)}, bf16[64,2048]{1,0:T(8,128)(2,1)S(1)}, u32[]{:S(2)}, u32[]{:S(2)}) collective-permute-start(bf16[64,2048]{1,0:T(8,128)(2,1)S(1)} %get-tuple-element.45.refs_4_.refs_2_), channel_id=1, source_target_pairs={{0,1},{1,0},{2,3},{3,2},{4,5},{5,4},{6,7},{7,6},{8,9},{9,8},{10,11... | collective-permute-start | bytes 786440 | tf_op jit(solution)/shard_map/ppermute | solution.py:41
  40.3 19.2 %collective-permute-start.4 = (bf16[128,512]{1,0:T(8,128)(2,1)S(1)}, bf16[128,512]{1,0:T(8,128)(2,1)S(1)}, u32[]{:S(2)}, u32[]{:S(2)}) collective-permute-start(bf16[128,512]{1,0:T(8,128)(2,1)S(1)} %shard_map.90.refs_0_), channel_id=1, source_target_pairs={{0,8},{4,12},{8,0},{12,4},{1,9},{5,13},{9,1},{13,5},{2,10},{6,14},... | collective-permute-start | bytes 393224 | tf_op jit(solution)/shard_map/ppermute | solution.py:46
  47.2 35.5 %collective-permute-start.18 = (bf16[384,1792]{1,0:T(8,128)(2,1)S(1)}, bf16[384,1792]{1,0:T(8,128)(2,1)S(1)}, u32[]{:S(2)}, u32[]{:S(2)}) collective-permute-start(bf16[384,1792]{1,0:T(8,128)(2,1)S(1)} %shard_map.96.refs_6_.refs_0_), channel_id=1, source_target_pairs={{0,2},{2,0},{1,3},{3,1},{4,6},{6,4},{5,7},{7,5},{8,10},{10,8},{9,1... | collective-permute-start | bytes 4128776 | tf_op jit(solution)/shard_map/ppermute | solution.py:41
  59.6 6.4 %collective-permute-start.13 = (bf16[128,1024]{1,0:T(8,128)(2,1)S(1)}, bf16[128,1024]{1,0:T(8,128)(2,1)S(1)}, u32[]{:S(2)}, u32[]{:S(2)}) collective-permute-start(bf16[128,1024]{1,0:T(8,128)(2,1)S(1)} %shard_map.98.refs_0_), channel_id=1, source_target_pairs={{0,4},{4,0},{8,12},{12,8},{1,5},{5,1},{9,13},{13,9},{2,6},{6,2},{1... | collective-permute-start | bytes 786440 | tf_op jit(solution)/shard_map/ppermute | solution.py:46
  66.1 1.6 %collective-permute-start.14 = (bf16[64,2048]{1,0:T(8,128)(2,1)S(1)}, bf16[64,2048]{1,0:T(8,128)(2,1)S(1)}, u32[]{:S(2)}, u32[]{:S(2)}) collective-permute-start(bf16[64,2048]{1,0:T(8,128)(2,1)S(1)} %get-tuple-element.47.refs_0_.refs_2_.refs_4_), channel_id=1, source_target_pairs={{0,1},{1,0},{2,3},{3,2},{4,5},{5,4},{6,7},{7,6},{8,9},{9,8},{10,11... | collective-permute-start | bytes 786440 | tf_op jit(solution)/shard_map/ppermute | solution.py:41
  66.1 1.9 %collective-permute-start.15 = (bf16[64,2048]{1,0:T(8,128)(2,1)S(1)}, bf16[64,2048]{1,0:T(8,128)(2,1)S(1)}, u32[]{:S(2)}, u32[]{:S(2)}) collective-permute-start(bf16[64,2048]{1,0:T(8,128)(2,1)S(1)} %get-tuple-element.48.refs_4_), channel_id=1, source_target_pairs={{0,1},{1,0},{2,3},{3,2},{4,5},{5,4},{6,7},{7,6},{8,9},{9,8},{10,11... | collective-permute-start | bytes 786440 | tf_op jit(solution)/shard_map/ppermute | solution.py:41
  70.6 28.9 %collective-permute-start.17 = (bf16[384,1024]{1,0:T(8,128)(2,1)S(1)}, bf16[384,1024]{1,0:T(8,128)(2,1)S(1)}, u32[]{:S(2)}, u32[]{:S(2)}) collective-permute-start(bf16[384,1024]{1,0:T(8,128)(2,1)S(1)} %shard_map.100.refs_9_.refs_0_), channel_id=1, source_target_pairs={{0,2},{2,0},{1,3},{3,1},{4,6},{6,4},{5,7},{7,5},{8,10},{10,8},{9,1... | collective-permute-start | bytes 2359304 | tf_op jit(solution)/shard_map/ppermute | solution.py:41
  89.1 2.0 %collective-permute-start.19 = (bf16[128,2048]{1,0:T(8,128)(2,1)S(1)}, bf16[128,2048]{1,0:T(8,128)(2,1)S(1)}, u32[]{:S(2)}, u32[]{:S(2)}) collective-permute-start(bf16[128,2048]{1,0:T(8,128)(2,1)S(1)} %get-tuple-element.52), channel_id=1, source_target_pairs={{0,1},{1,0},{2,3},{3,2},{4,5},{5,4},{6,7},{7,6},{8,9},{9,8},{10,11... | collective-permute-start | bytes 1572872 | tf_op jit(solution)/shard_map/ppermute | solution.py:41
  89.2 26.9 %collective-permute-start.16 = (bf16[384,768]{1,0:T(8,128)(2,1)S(1)}, bf16[384,768]{1,0:T(8,128)(2,1)S(1)}, u32[]{:S(2)}, u32[]{:S(2)}) collective-permute-start(bf16[384,768]{1,0:T(8,128)(2,1)S(1)} %shard_map.101.refs_6_.refs_0_), channel_id=1, source_target_pairs={{0,2},{2,0},{1,3},{3,1},{4,6},{6,4},{5,7},{7,5},{8,10},{10,8},{9,1... | collective-permute-start | bytes 1769480 | tf_op jit(solution)/shard_map/ppermute | solution.py:41
  91.1 16.3 %collective-permute-start.20 = (bf16[128,1024]{1,0:T(8,128)(2,1)S(1)}, bf16[128,1024]{1,0:T(8,128)(2,1)S(1)}, u32[]{:S(2)}, u32[]{:S(2)}) collective-permute-start(bf16[128,1024]{1,0:T(8,128)(2,1)S(1)} %get-tuple-element.60), channel_id=1, source_target_pairs={{0,4},{4,0},{8,12},{12,8},{1,5},{5,1},{9,13},{13,9},{2,6},{6,2},{1... | collective-permute-start | bytes 786440 | tf_op jit(solution)/shard_map/ppermute | solution.py:46
  107.5 8.4 %collective-permute-start.21 = (bf16[128,512]{1,0:T(8,128)(2,1)S(1)}, bf16[128,512]{1,0:T(8,128)(2,1)S(1)}, u32[]{:S(2)}, u32[]{:S(2)}) collective-permute-start(bf16[128,512]{1,0:T(8,128)(2,1)S(1)} %get-tuple-element.67), channel_id=1, source_target_pairs={{0,8},{4,12},{8,0},{12,4},{1,9},{5,13},{9,1},{13,5},{2,10},{6,14},... | collective-permute-start | bytes 393224 | tf_op jit(solution)/shard_map/ppermute | solution.py:46
  118.8 1.6 %collective-permute-start.22 = (bf16[64,2048]{1,0:T(8,128)(2,1)S(1)}, bf16[64,2048]{1,0:T(8,128)(2,1)S(1)}, u32[]{:S(2)}, u32[]{:S(2)}) collective-permute-start(bf16[64,2048]{1,0:T(8,128)(2,1)S(1)} %get-tuple-element.69), channel_id=1, source_target_pairs={{0,1},{1,0},{2,3},{3,2},{4,5},{5,4},{6,7},{7,6},{8,9},{9,8},{10,11... | collective-permute-start | bytes 786440 | tf_op jit(solution)/shard_map/ppermute | solution.py:41
  120.5 5.6 %collective-permute-start.23 = (bf16[64,1024]{1,0:T(8,128)(2,1)S(1)}, bf16[64,1024]{1,0:T(8,128)(2,1)S(1)}, u32[]{:S(2)}, u32[]{:S(2)}) collective-permute-start(bf16[64,1024]{1,0:T(8,128)(2,1)S(1)} %get-tuple-element.71), channel_id=1, source_target_pairs={{0,4},{4,0},{8,12},{12,8},{1,5},{5,1},{9,13},{13,9},{2,6},{6,2},{1... | collective-permute-start | bytes 393224 | tf_op jit(solution)/shard_map/ppermute | solution.py:46
  126.1 6.1 %collective-permute-start.24 = (bf16[64,512]{1,0:T(8,128)(2,1)S(1)}, bf16[64,512]{1,0:T(8,128)(2,1)S(1)}, u32[]{:S(2)}, u32[]{:S(2)}) collective-permute-start(bf16[64,512]{1,0:T(8,128)(2,1)S(1)} %get-tuple-element.73), channel_id=1, source_target_pairs={{0,8},{4,12},{8,0},{12,4},{1,9},{5,13},{9,1},{13,5},{2,10},{6,14},... | collective-permute-start | bytes 196616 | tf_op jit(solution)/shard_map/ppermute | solution.py:46

commit v12 on v11

--- a/solution.py
+++ b/solution.py
@@ -8,7 +8,7 @@
 from jax.sharding import PartitionSpec as P
 
 PIECES = (1, 1, 1)
-PARTS = (4, 3)
+PARTS = (1, 1)
 MIB = 1 << 20
 
 
@@ -223,9 +223,11 @@
         for k in range(len(above)):
             outs[3 + k][:upper_rows] = ins[len(ins_all) - len(above) + k][...]
 
-        @pl.loop(0, width // 128)
+        step = 256 if width % 256 == 0 else 128
+
+        @pl.loop(0, width // step)
         def _(j):
-            at = lanes(j, 128)
+            at = lanes(j, step)
 
             def total(k):
                 array, top = where[k]

time: 133 us -> 132 us (level)
  waiting for transfers between devices: 47 us -> 45.5 us
where the time goes in v12:
time: 132 us; the launch traced here: 131 us
  Pallas kernels  53.7 us (41%)
  waiting for transfers between devices  45.5 us (34%)
  starting transfers between devices  30.4 us (23%)
    pallas_call x28, Pallas kernels, local(): pl.pallas_call(body, out_shape=shapes, in_specs=[VMEM] * len(args) + [ANY...  33.8 us
    ppermute x12, waiting for transfers between devices, swapped(): return lax.ppermute(value, axis, [(i, i ^ bit) for i in range(n)])  23.6 us
    ppermute x13, waiting for transfers between devices, shifted(): return lax.ppermute(value, axis, [(i, (i + step) % n) for i in range(n)])  21.9 us
    ppermute x12, starting transfers between devices, swapped(): return lax.ppermute(value, axis, [(i, i ^ bit) for i in range(n)])  20.7 us
    pallas_call x4, Pallas kernels, gradients(): pl.pallas_call(body, grid=grid, out_shape=[jax.ShapeDtypeStruct(shape, jn...  19.8 us
    ppermute x13, starting transfers between devices, shifted(): return lax.ppermute(value, axis, [(i, (i + step) % n) for i in range(n)])  9.77 us
  transfers between devices with their start and end apart: 25, of which 14 were waited for; matrix products, arithmetic and copies ran while one was open for 0% of the time, Pallas kernels for 38%

profile of v12, /device:TPU:0, one launch (start us, length us, event | category | flops | bytes accessed | tf_op | source)
XLA Modules:
  0.0 131.4 jit_solution(10254590315605981226)
XLA Ops:
  0.6 0.9 copy-done.2
  1.6 4.1 %collective-permute-start.5 = (bf16[64,512]{1,0:T(8,128)(2,1)S(1)}, bf16[64,512]{1,0:T(8,128)(2,1)S(1)}, u32[]{:S(2)}, u32[]{:S(2)}) collective-permute-start(bf16[64,512]{1,0:T(8,128)(2,1)S(1)} %shard_map.91.refs_0_), channel_id=1, source_target_pairs={{0,8},{4,12},{8,0},{12,4},{1,9},{5,13},{9,1},{13,5},{2,10},{6,14},... | collective-permute-start | bytes 196616 | tf_op jit(solution)/shard_map/ppermute | solution.py:46
  5.7 3.6 %collective-permute-done.5.refs_1_ = bf16[64,512]{1,0:T(8,128)(2,1)S(1)} collective-permute-done((bf16[64,512]{1,0:T(8,128)(2,1)S(1)}, bf16[64,512]{1,0:T(8,128)(2,1)S(1)}, u32[]{:S(2)}, u32[]{:S(2)}) %collective-permute-start.5) | collective-permute-done | bytes 65568 | tf_op jit(solution)/shard_map/ppermute | solution.py:46
  9.3 0.6 collective-permute-start.6
  10.0 3.4 %collective-permute-start = (bf16[64,512]{1,0:T(8,128)(2,1)S(1)}, bf16[64,512]{1,0:T(8,128)(2,1)S(1)}, u32[]{:S(2)}, u32[]{:S(2)}) collective-permute-start(bf16[64,512]{1,0:T(8,128)(2,1)S(1)} %shard_map.84.refs_0_), channel_id=1, source_target_pairs={{0,8},{4,12},{8,0},{12,4},{1,9},{5,13},{9,1},{13,5},{2,10},{6,14},... | collective-permute-start | bytes 196616 | tf_op jit(solution)/shard_map/ppermute | solution.py:46
  13.4 1.7 %collective-permute-done.6.refs_1_ = bf16[64,1024]{1,0:T(8,128)(2,1)S(1)} collective-permute-done((bf16[64,1024]{1,0:T(8,128)(2,1)S(1)}, bf16[64,1024]{1,0:T(8,128)(2,1)S(1)}, u32[]{:S(2)}, u32[]{:S(2)}) %collective-permute-start.6) | collective-permute-done | bytes 131104 | tf_op jit(solution)/shard_map/ppermute | solution.py:46
  15.2 1.1 collective-permute-done.refs_1_
  16.3 1.9 %collective-permute-start.1 = (bf16[64,1024]{1,0:T(8,128)(2,1)S(1)}, bf16[64,1024]{1,0:T(8,128)(2,1)S(1)}, u32[]{:S(2)}, u32[]{:S(2)}) collective-permute-start(bf16[64,1024]{1,0:T(8,128)(2,1)S(1)} %shard_map.85.refs_0_), channel_id=1, source_target_pairs={{0,4},{4,0},{8,12},{12,8},{1,5},{5,1},{9,13},{13,9},{2,6},{6,2},{1... | collective-permute-start | bytes 393224 | tf_op jit(solution)/shard_map/ppermute | solution.py:46
  18.2 2.1 %shard_map.94.refs_3_.refs_0_ = bf16[256,1792]{1,0:T(8,128)(2,1)S(1)} custom-call(bf16[64,2048]{1,0:T(8,128)(2,1)S(1)} %shard_map.93.refs_0_.refs_2_, bf16[64,2048]{1,0:T(8,128)(2,1)S(1)} %collective-permute-done.7.refs_1_.refs_3_, bf16[64,2048]{1,0:T(8,128)(2,1)S(1)} %shard_map.93.refs_0_.refs_2_, ...), custom_call_target="tpu_custom_call" | custom-call | flops 345000000 | tf_op jit(solution)/shard_map/pallas_call | solution.py:101
  20.3 1.6 %collective-permute-start.9 = (bf16[256,1792]{1,0:T(8,128)(2,1)S(1)}, bf16[256,1792]{1,0:T(8,128)(2,1)S(1)}, u32[]{:S(2)}, u32[]{:S(2)}) collective-permute-start(bf16[256,1792]{1,0:T(8,128)(2,1)S(1)} %shard_map.94.refs_3_.refs_0_), channel_id=1, source_target_pairs={{0,2},{2,0},{1,3},{3,1},{4,6},{6,4},{5,7},{7,5},{8,10},{10,8},{9,1... | collective-permute-start | bytes 2752520 | tf_op jit(solution)/shard_map/ppermute | solution.py:41
  22.0 2.4 %collective-permute-start.2 = (bf16[128,512]{1,0:T(8,128)(2,1)S(1)}, bf16[128,512]{1,0:T(8,128)(2,1)S(1)}, u32[]{:S(2)}, u32[]{:S(2)}) collective-permute-start(bf16[128,512]{1,0:T(8,128)(2,1)S(1)} %shard_map.87.refs_0_), channel_id=1, source_target_pairs={{0,8},{4,12},{8,0},{12,4},{1,9},{5,13},{9,1},{13,5},{2,10},{6,14},... | collective-permute-start | bytes 393224 | tf_op jit(solution)/shard_map/ppermute | solution.py:46
  24.4 7.3 %collective-permute-done.2.refs_1_ = bf16[128,512]{1,0:T(8,128)(2,1)S(1)} collective-permute-done((bf16[128,512]{1,0:T(8,128)(2,1)S(1)}, bf16[128,512]{1,0:T(8,128)(2,1)S(1)}, u32[]{:S(2)}, u32[]{:S(2)}) %collective-permute-start.2) | collective-permute-done | bytes 131104 | tf_op jit(solution)/shard_map/ppermute | solution.py:46
  31.7 0.5 collective-permute-start.3
  32.2 2.5 %shard_map.95.refs_9_.refs_1_ = bf16[128,1792]{1,0:T(8,128)(2,1)S(1)} custom-call(bf16[64,2048]{1,0:T(8,128)(2,1)S(1)} %shard_map.86.refs_2_.refs_0_, bf16[64,2048]{1,0:T(8,128)(2,1)S(1)} %collective-permute-done.8.refs_1_, bf16[1792,2048]{1,0:T(8,128)(2,1)S(1)} %bitcast.1, bf16[256,1792]{1,0:T(8,128)(2,1)S(1)} %shard_map.94.refs_3_.refs_0_), custom_call_target="tpu_custom_call" | custom-call | flops 345000000 | tf_op jit(solution)/shard_map/pallas_call | solution.py:101
  34.7 1.6 %collective-permute-start.10 = (bf16[128,1792]{1,0:T(8,128)(2,1)S(1)}, bf16[128,1792]{1,0:T(8,128)(2,1)S(1)}, u32[]{:S(2)}, u32[]{:S(2)}) collective-permute-start(bf16[128,1792]{1,0:T(8,128)(2,1)S(1)} %shard_map.95.refs_9_.refs_1_), channel_id=1, source_target_pairs={{0,2},{2,0},{1,3},{3,1},{4,6},{6,4},{5,7},{7,5},{8,10},{10,8},{9,1... | collective-permute-start | bytes 1376264 | tf_op jit(solution)/shard_map/ppermute | solution.py:41
  36.3 3.4 %collective-permute-done.3.refs_1_ = bf16[128,1024]{1,0:T(8,128)(2,1)S(1)} collective-permute-done((bf16[128,1024]{1,0:T(8,128)(2,1)S(1)}, bf16[128,1024]{1,0:T(8,128)(2,1)S(1)}, u32[]{:S(2)}, u32[]{:S(2)}) %collective-permute-start.3) | collective-permute-done | bytes 262176 | tf_op jit(solution)/shard_map/ppermute | solution.py:46
  39.8 0.5 collective-permute-start.12
  40.3 2.5 %collective-permute-start.4 = (bf16[128,512]{1,0:T(8,128)(2,1)S(1)}, bf16[128,512]{1,0:T(8,128)(2,1)S(1)}, u32[]{:S(2)}, u32[]{:S(2)}) collective-permute-start(bf16[128,512]{1,0:T(8,128)(2,1)S(1)} %shard_map.90.refs_0_), channel_id=1, source_target_pairs={{0,8},{4,12},{8,0},{12,4},{1,9},{5,13},{9,1},{13,5},{2,10},{6,14},... | collective-permute-start | bytes 393224 | tf_op jit(solution)/shard_map/ppermute | solution.py:46
  42.8 4.4 %shard_map.96.refs_6_.refs_0_ = bf16[384,1792]{1,0:T(8,128)(2,1)S(1)} custom-call(bf16[64,2048]{1,0:T(8,128)(2,1)S(1)} %get-tuple-element.44.refs_2_.refs_0_, bf16[64,2048]{1,0:T(8,128)(2,1)S(1)} %collective-permute-done.11.refs_1_.refs_3_, bf16[64,2048]{1,0:T(8,128)(2,1)S(1)} %get-tuple-element.44.refs_2_.refs_0_, ...), custom_call_target="tpu_custom_call" | custom-call | flops 345000000 | tf_op jit(solution)/shard_map/pallas_call | solution.py:101
  47.2 1.6 %collective-permute-start.18 = (bf16[384,1792]{1,0:T(8,128)(2,1)S(1)}, bf16[384,1792]{1,0:T(8,128)(2,1)S(1)}, u32[]{:S(2)}, u32[]{:S(2)}) collective-permute-start(bf16[384,1792]{1,0:T(8,128)(2,1)S(1)} %shard_map.96.refs_6_.refs_0_), channel_id=1, source_target_pairs={{0,2},{2,0},{1,3},{3,1},{4,6},{6,4},{5,7},{7,5},{8,10},{10,8},{9,1... | collective-permute-start | bytes 4128776 | tf_op jit(solution)/shard_map/ppermute | solution.py:41
  48.8 4.4 %collective-permute-done.10.refs_3_ = bf16[128,1792]{1,0:T(8,128)(2,1)S(1)} collective-permute-done((bf16[128,1792]{1,0:T(8,128)(2,1)S(1)}, bf16[128,1792]{1,0:T(8,128)(2,1)S(1)}, u32[]{:S(2)}, u32[]{:S(2)}) %collective-permute-start.10) | collective-permute-done | bytes 458784 | tf_op jit(solution)/shard_map/ppermute | solution.py:41
  53.2 5.8 %shard_map.97 = (bf16[1792,128]{1,0:T(8,128)(2,1)S(1)}, bf16[128,1792]{1,0:T(8,128)(2,1)S(1)}, bf16[128,1792]{1,0:T(8,128)(2,1)S(1)}, f32[64,2048]{1,0:T(8,128)S(1)}, bf16[64,2048]{1,0:T(8,128)(2,1)S(1)}) custom-call(bf16[256,1792]{1,0:T(8,128)(2,1)S(1)} %shard_map.94.refs_3_.refs_0_, bf16[128,1792]{1,0:T(8,128)(2,1)S(1)} %shard_map.95.refs_9_.refs_1_, ...), custom_call_target="tpu_custom_call" | custom-call | flops 69000003584 | tf_op jit(solution)/shard_map/pallas_call | solution.py:101
  59.1 6.4 %collective-permute-done.13.refs_1_ = bf16[128,1024]{1,0:T(8,128)(2,1)S(1)} collective-permute-done((bf16[128,1024]{1,0:T(8,128)(2,1)S(1)}, bf16[128,1024]{1,0:T(8,128)(2,1)S(1)}, u32[]{:S(2)}, u32[]{:S(2)}) %collective-permute-start.13) | collective-permute-done | bytes 262176 | tf_op jit(solution)/shard_map/ppermute | solution.py:46
  65.6 0.5 collective-permute-start.15
  66.1 1.0 collective-permute-done.14.refs_1_.refs_3_.refs_5_
  67.1 0.4 collective-permute-done.15.refs_5_
  67.5 2.4 %shard_map.100.refs_9_.refs_0_ = bf16[384,896]{1,0:T(8,128)(2,1)S(1)} custom-call(bf16[64,2048]{1,0:T(8,128)(2,1)S(1)} %get-tuple-element.47.refs_0_.refs_2_.refs_4_, bf16[64,2048]{1,0:T(8,128)(2,1)S(1)} %collective-permute-done.14.refs_1_.refs_3_.refs_5_, bf16[64,2048]{1,0:T(8,128)(2,1)S(1)} %get-tuple-element.47.refs_0_.refs_2_.refs_4_, ...), custom_call_target="tpu_custom_call" | custom-call | flops 345000000 | tf_op jit(solution)/shard_map/pallas_call | solution.py:101
  69.9 1.8 %collective-permute-start.17 = (bf16[384,896]{1,0:T(8,128)(2,1)S(1)}, bf16[384,896]{1,0:T(8,128)(2,1)S(1)}, u32[]{:S(2)}, u32[]{:S(2)}) collective-permute-start(bf16[384,896]{1,0:T(8,128)(2,1)S(1)} %shard_map.100.refs_9_.refs_0_), channel_id=1, source_target_pairs={{0,2},{2,0},{1,3},{3,1},{4,6},{6,4},{5,7},{7,5},{8,10},{10,8},{9,1... | collective-permute-start | bytes 2064392 | tf_op jit(solution)/shard_map/ppermute | solution.py:41
  71.8 2.4 %shard_map.101.refs_6_.refs_0_ = bf16[384,896]{1,0:T(8,128)(2,1)S(1)} custom-call(bf16[64,2048]{1,0:T(8,128)(2,1)S(1)} %get-tuple-element.47.refs_0_.refs_2_.refs_4_, bf16[64,2048]{1,0:T(8,128)(2,1)S(1)} %collective-permute-done.14.refs_1_.refs_3_.refs_5_, bf16[64,2048]{1,0:T(8,128)(2,1)S(1)} %get-tuple-element.47.refs_0_.refs_2_.refs_4_, ...), custom_call_target="tpu_custom_call" | custom-call | flops 345000000 | tf_op jit(solution)/shard_map/pallas_call | solution.py:101
  74.2 0.6 shard_map.102.refs_6_.refs_0_
  74.8 0.2 shard_map.103.refs_7_.refs_3_
  75.0 7.7 %collective-permute-done.18.refs_1_ = bf16[384,1792]{1,0:T(8,128)(2,1)S(1)} collective-permute-done((bf16[384,1792]{1,0:T(8,128)(2,1)S(1)}, bf16[384,1792]{1,0:T(8,128)(2,1)S(1)}, u32[]{:S(2)}, u32[]{:S(2)}) %collective-permute-start.18) | collective-permute-done | bytes 1376288 | tf_op jit(solution)/shard_map/ppermute | solution.py:41
  82.7 5.8 %shard_map.104 = (bf16[1792,128]{1,0:T(8,128)(2,1)S(1)}, bf16[128,1792]{1,0:T(8,128)(2,1)S(1)}, bf16[128,1792]{1,0:T(8,128)(2,1)S(1)}, f32[128,2048]{1,0:T(8,128)S(1)}, bf16[128,2048]{1,0:T(8,128)(2,1)S(1)}) custom-call(bf16[384,1792]{1,0:T(8,128)(2,1)S(1)} %shard_map.96.refs_6_.refs_0_, bf16[384,1792]{1,0:T(8,128)(2,1)S(1)} %collective-permute-done.18.refs_1_, ...), custom_call_target="tpu_custom_call" | custom-call | flops 69000003584 | tf_op jit(solution)/shard_map/pallas_call | solution.py:101
  88.6 1.8 %collective-permute-start.16 = (bf16[384,896]{1,0:T(8,128)(2,1)S(1)}, bf16[384,896]{1,0:T(8,128)(2,1)S(1)}, u32[]{:S(2)}, u32[]{:S(2)}) collective-permute-start(bf16[384,896]{1,0:T(8,128)(2,1)S(1)} %shard_map.101.refs_6_.refs_0_), channel_id=1, source_target_pairs={{0,2},{2,0},{1,3},{3,1},{4,6},{6,4},{5,7},{7,5},{8,10},{10,8},{9,1... | collective-permute-start | bytes 2064392 | tf_op jit(solution)/shard_map/ppermute | solution.py:41
  90.5 0.1 shard_map.105
  90.7 6.7 %collective-permute-done.17.refs_1_ = bf16[384,896]{1,0:T(8,128)(2,1)S(1)} collective-permute-done((bf16[384,896]{1,0:T(8,128)(2,1)S(1)}, bf16[384,896]{1,0:T(8,128)(2,1)S(1)}, u32[]{:S(2)}, u32[]{:S(2)}) %collective-permute-start.17) | collective-permute-done | bytes 688160 | tf_op jit(solution)/shard_map/ppermute | solution.py:41
  97.4 3.2 %shard_map.106 = (bf16[896,128]{1,0:T(8,128)(2,1)S(1)}, bf16[128,896]{1,0:T(8,128)(2,1)S(1)}, bf16[128,896]{1,0:T(8,128)(2,1)S(1)}, f32[128,2048]{1,0:T(8,128)S(1)}) custom-call(bf16[384,896]{1,0:T(8,128)(2,1)S(1)} %shard_map.100.refs_9_.refs_0_, bf16[384,896]{1,0:T(8,128)(2,1)S(1)} %collective-permute-done.17.refs_1_, bf16[2048,1792]{1,0:T(8,128)(2,1)S(1)} %copy-done, ...), custom_call_target="tpu_custom_call" | custom-call | flops 115000000 | tf_op jit(solution)/shard_map/pallas_call | solution.py:101
  100.6 3.9 %shard_map.107 = (bf16[1792,2048]{1,0:T(8,128)(2,1)}, bf16[16,128]{1,0:T(8,128)(2,1)S(1)}) custom-call(bf16[1792,128]{1,0:T(8,128)(2,1)S(1)} %get-tuple-element.61.refs_0_, bf16[1792,128]{1,0:T(8,128)(2,1)S(1)} %get-tuple-element.62.refs_1_, bf16[896,128]{1,0:T(8,128)(2,1)S(1)} %get-tuple-element.63.refs_2_, bf16[384,2048]{1,0:T(8,128)(2,1)S(1)} %shard_map.103.refs_7_.refs_3_), custom_call_target="tpu_custom_call" | custom-call | flops 2300000000 | tf_op jit(solution)/shard_map/pallas_call | solution.py:323
  104.6 2.1 %collective-permute-start.21 = (bf16[128,512]{1,0:T(8,128)(2,1)S(1)}, bf16[128,512]{1,0:T(8,128)(2,1)S(1)}, u32[]{:S(2)}, u32[]{:S(2)}) collective-permute-start(bf16[128,512]{1,0:T(8,128)(2,1)S(1)} %get-tuple-element.67), channel_id=1, source_target_pairs={{0,8},{4,12},{8,0},{12,4},{1,9},{5,13},{9,1},{13,5},{2,10},{6,14},... | collective-permute-start | bytes 393224 | tf_op jit(solution)/shard_map/ppermute | solution.py:46
  106.7 6.0 %shard_map.109 = (bf16[2048,1792]{1,0:T(8,128)(2,1)}, bf16[2048,1792]{1,0:T(8,128)(2,1)}, bf16[16,128]{1,0:T(8,128)(2,1)S(1)}) custom-call(bf16[2048,384]{1,0:T(8,128)(2,1)S(1)} %shard_map.102.refs_6_.refs_0_, bf16[128,1792]{1,0:T(8,128)(2,1)S(1)} %get-tuple-element.46.refs_2_.refs_9_.refs_1_, bf16[128,1792]{1,0:T(8,128)(2,1)S(1)} %get-tuple-element.55.refs_2_, ...), custom_call_target="tpu_custom_call" | custom-call | flops 115000000 | tf_op jit(solution)/shard_map/pallas_call | solution.py:323
  112.8 3.2 %shard_map.111 = (bf16[896,128]{1,0:T(8,128)(2,1)S(1)}, bf16[128,896]{1,0:T(8,128)(2,1)S(1)}, bf16[128,896]{1,0:T(8,128)(2,1)S(1)}, f32[64,2048]{1,0:T(8,128)S(1)}, bf16[64,2048]{1,0:T(8,128)(2,1)S(1)}) custom-call(bf16[384,896]{1,0:T(8,128)(2,1)S(1)} %shard_map.101.refs_6_.refs_0_, bf16[384,896]{1,0:T(8,128)(2,1)S(1)} %collective-permute-done.16.refs_1_, ...), custom_call_target="tpu_custom_call" | custom-call | flops 115000000 | tf_op jit(solution)/shard_map/pallas_call | solution.py:101
  116.0 1.5 %collective-permute-done.22.refs_1_ = bf16[64,2048]{1,0:T(8,128)(2,1)S(1)} collective-permute-done((bf16[64,2048]{1,0:T(8,128)(2,1)S(1)}, bf16[64,2048]{1,0:T(8,128)(2,1)S(1)}, u32[]{:S(2)}, u32[]{:S(2)}) %collective-permute-start.22) | collective-permute-done | bytes 262176 | tf_op jit(solution)/shard_map/ppermute | solution.py:41
  117.6 1.5 %collective-permute-start.23 = (bf16[64,1024]{1,0:T(8,128)(2,1)S(1)}, bf16[64,1024]{1,0:T(8,128)(2,1)S(1)}, u32[]{:S(2)}, u32[]{:S(2)}) collective-permute-start(bf16[64,1024]{1,0:T(8,128)(2,1)S(1)} %get-tuple-element.71), channel_id=1, source_target_pairs={{0,4},{4,0},{8,12},{12,8},{1,5},{5,1},{9,13},{13,9},{2,6},{6,2},{1... | collective-permute-start | bytes 393224 | tf_op jit(solution)/shard_map/ppermute | solution.py:46
  119.1 3.9 %shard_map.115 = (bf16[1792,2048]{1,0:T(8,128)(2,1)}, bf16[16,128]{1,0:T(8,128)(2,1)S(1)}) custom-call(bf16[1792,128]{1,0:T(8,128)(2,1)S(1)} %get-tuple-element.61.refs_0_, bf16[1792,128]{1,0:T(8,128)(2,1)S(1)} %get-tuple-element.62.refs_1_, bf16[896,128]{1,0:T(8,128)(2,1)S(1)} %get-tuple-element.78.refs_2_, ...), custom_call_target="tpu_custom_call", output_to_operand_aliasing={{0}: (4, {})} | custom-call | flops 3449999872 | tf_op jit(solution)/shard_map/pallas_call | solution.py:323
  123.0 0.2 collective-permute-done.23.refs_1_
  123.3 1.5 %collective-permute-start.24 = (bf16[64,512]{1,0:T(8,128)(2,1)S(1)}, bf16[64,512]{1,0:T(8,128)(2,1)S(1)}, u32[]{:S(2)}, u32[]{:S(2)}) collective-permute-start(bf16[64,512]{1,0:T(8,128)(2,1)S(1)} %get-tuple-element.73), channel_id=1, source_target_pairs={{0,8},{4,12},{8,0},{12,4},{1,9},{5,13},{9,1},{13,5},{2,10},{6,14},... | collective-permute-start | bytes 196616 | tf_op jit(solution)/shard_map/ppermute | solution.py:46
  124.7 6.0 %shard_map.116 = (bf16[2048,1792]{1,0:T(8,128)(2,1)}, bf16[2048,1792]{1,0:T(8,128)(2,1)}, bf16[16,128]{1,0:T(8,128)(2,1)}) custom-call(bf16[2048,384]{1,0:T(8,128)(2,1)S(1)} %shard_map.102.refs_6_.refs_0_, bf16[128,1792]{1,0:T(8,128)(2,1)S(1)} %get-tuple-element.46.refs_2_.refs_9_.refs_1_, ...), custom_call_target="tpu_custom_call", output_to_operand_aliasing={{0}: (7, {}), {1}: (8, {})} | custom-call | flops 5750000128 | tf_op jit(solution)/shard_map/pallas_call | solution.py:323
  130.7 0.7 shard_map.114
  (50 shorter events, 1.1 us)
Async XLA Ops:
  0.6 0.9 copy-start.2
  1.6 8.4 %copy-start.3 = (bf16[192,512]{1,0:T(8,128)(2,1)S(1)}, bf16[192,512]{1,0:T(8,128)(2,1)}, u32[]{:S(2)}) copy-start(bf16[192,512]{1,0:T(8,128)(2,1)} %source.1) | copy-start | bytes 589828
  1.6 8.4 %copy-start.4 = (bf16[192,512]{1,0:T(8,128)(2,1)S(1)}, bf16[192,512]{1,0:T(8,128)(2,1)}, u32[]{:S(2)}) copy-start(bf16[192,512]{1,0:T(8,128)(2,1)} %refs_1_.5) | copy-start | bytes 589828
  1.6 16.6 %copy-start = (bf16[2048,1792]{1,0:T(8,128)(2,1)S(1)}, bf16[2048,1792]{1,0:T(8,128)(2,1)}, u32[]{:S(2)}) copy-start(bf16[2048,1792]{1,0:T(8,128)(2,1)} %refs_2_.7) | copy-start | bytes 22020100
  1.6 16.6 %copy-start.1 = (bf16[2048,1792]{1,0:T(8,128)(2,1)S(1)}, bf16[2048,1792]{1,0:T(8,128)(2,1)}, u32[]{:S(2)}) copy-start(bf16[2048,1792]{1,0:T(8,128)(2,1)} %refs_3_.5) | copy-start | bytes 22020100
  1.6 7.8 %collective-permute-start.5 = (bf16[64,512]{1,0:T(8,128)(2,1)S(1)}, bf16[64,512]{1,0:T(8,128)(2,1)S(1)}, u32[]{:S(2)}, u32[]{:S(2)}) collective-permute-start(bf16[64,512]{1,0:T(8,128)(2,1)S(1)} %shard_map.91.refs_0_), channel_id=1, source_target_pairs={{0,8},{4,12},{8,0},{12,4},{1,9},{5,13},{9,1},{13,5},{2,10},{6,14},... | collective-permute-start | bytes 196616 | tf_op jit(solution)/shard_map/ppermute | solution.py:46
  9.3 5.7 %collective-permute-start.6 = (bf16[64,1024]{1,0:T(8,128)(2,1)S(1)}, bf16[64,1024]{1,0:T(8,128)(2,1)S(1)}, u32[]{:S(2)}, u32[]{:S(2)}) collective-permute-start(bf16[64,1024]{1,0:T(8,128)(2,1)S(1)} %shard_map.92.refs_0_), channel_id=1, source_target_pairs={{0,4},{4,0},{8,12},{12,8},{1,5},{5,1},{9,13},{13,9},{2,6},{6,2},{1... | collective-permute-start | bytes 393224 | tf_op jit(solution)/shard_map/ppermute | solution.py:46
  10.0 6.3 %collective-permute-start = (bf16[64,512]{1,0:T(8,128)(2,1)S(1)}, bf16[64,512]{1,0:T(8,128)(2,1)S(1)}, u32[]{:S(2)}, u32[]{:S(2)}) collective-permute-start(bf16[64,512]{1,0:T(8,128)(2,1)S(1)} %shard_map.84.refs_0_), channel_id=1, source_target_pairs={{0,8},{4,12},{8,0},{12,4},{1,9},{5,13},{9,1},{13,5},{2,10},{6,14},... | collective-permute-start | bytes 196616 | tf_op jit(solution)/shard_map/ppermute | solution.py:46
  15.1 3.0 %collective-permute-start.7 = (bf16[64,2048]{1,0:T(8,128)(2,1)S(1)}, bf16[64,2048]{1,0:T(8,128)(2,1)S(1)}, u32[]{:S(2)}, u32[]{:S(2)}) collective-permute-start(bf16[64,2048]{1,0:T(8,128)(2,1)S(1)} %shard_map.93.refs_0_.refs_2_), channel_id=1, source_target_pairs={{0,1},{1,0},{2,3},{3,2},{4,5},{5,4},{6,7},{7,6},{8,9},{9,8},{10,11... | collective-permute-start | bytes 786440 | tf_op jit(solution)/shard_map/ppermute | solution.py:41
  16.3 5.6 %collective-permute-start.1 = (bf16[64,1024]{1,0:T(8,128)(2,1)S(1)}, bf16[64,1024]{1,0:T(8,128)(2,1)S(1)}, u32[]{:S(2)}, u32[]{:S(2)}) collective-permute-start(bf16[64,1024]{1,0:T(8,128)(2,1)S(1)} %shard_map.85.refs_0_), channel_id=1, source_target_pairs={{0,4},{4,0},{8,12},{12,8},{1,5},{5,1},{9,13},{13,9},{2,6},{6,2},{1... | collective-permute-start | bytes 393224 | tf_op jit(solution)/shard_map/ppermute | solution.py:46
  18.2 14.0 %slice-start = ((s8[7340032]{0:T(1024)(128)(4,1)}), s8[4194304]{0:T(1024)(128)(4,1)S(1)}, s32[]{:S(2)}) async-start(s8[7340032]{0:T(1024)(128)(4,1)} %bitcast), calls=%async_computation | async-start | bytes 8388608
  20.3 11.9 %slice-start.1 = ((s8[7340032]{0:T(1024)(128)(4,1)}), s8[3145728]{0:T(1024)(128)(4,1)S(1)}, s32[]{:S(2)}) async-start(s8[7340032]{0:T(1024)(128)(4,1)} %bitcast), calls=%async_computation.1 | async-start | bytes 6291456
  20.3 32.9 %collective-permute-start.9 = (bf16[256,1792]{1,0:T(8,128)(2,1)S(1)}, bf16[256,1792]{1,0:T(8,128)(2,1)S(1)}, u32[]{:S(2)}, u32[]{:S(2)}) collective-permute-start(bf16[256,1792]{1,0:T(8,128)(2,1)S(1)} %shard_map.94.refs_3_.refs_0_), channel_id=1, source_target_pairs={{0,2},{2,0},{1,3},{3,1},{4,6},{6,4},{5,7},{7,5},{8,10},{10,8},{9,1... | collective-permute-start | bytes 2752520 | tf_op jit(solution)/shard_map/ppermute | solution.py:41
  21.9 10.3 %collective-permute-start.8 = (bf16[64,2048]{1,0:T(8,128)(2,1)S(1)}, bf16[64,2048]{1,0:T(8,128)(2,1)S(1)}, u32[]{:S(2)}, u32[]{:S(2)}) collective-permute-start(bf16[64,2048]{1,0:T(8,128)(2,1)S(1)} %shard_map.86.refs_2_.refs_0_), channel_id=1, source_target_pairs={{0,1},{1,0},{2,3},{3,2},{4,5},{5,4},{6,7},{7,6},{8,9},{9,8},{10,11... | collective-permute-start | bytes 786440 | tf_op jit(solution)/shard_map/ppermute | solution.py:41
  22.0 9.7 %collective-permute-start.2 = (bf16[128,512]{1,0:T(8,128)(2,1)S(1)}, bf16[128,512]{1,0:T(8,128)(2,1)S(1)}, u32[]{:S(2)}, u32[]{:S(2)}) collective-permute-start(bf16[128,512]{1,0:T(8,128)(2,1)S(1)} %shard_map.87.refs_0_), channel_id=1, source_target_pairs={{0,8},{4,12},{8,0},{12,4},{1,9},{5,13},{9,1},{13,5},{2,10},{6,14},... | collective-permute-start | bytes 393224 | tf_op jit(solution)/shard_map/ppermute | solution.py:46
  31.7 8.0 %collective-permute-start.3 = (bf16[128,1024]{1,0:T(8,128)(2,1)S(1)}, bf16[128,1024]{1,0:T(8,128)(2,1)S(1)}, u32[]{:S(2)}, u32[]{:S(2)}) collective-permute-start(bf16[128,1024]{1,0:T(8,128)(2,1)S(1)} %shard_map.88.refs_0_), channel_id=1, source_target_pairs={{0,4},{4,0},{8,12},{12,8},{1,5},{5,1},{9,13},{13,9},{2,6},{6,2},{1... | collective-permute-start | bytes 786440 | tf_op jit(solution)/shard_map/ppermute | solution.py:46
  34.7 18.5 %collective-permute-start.10 = (bf16[128,1792]{1,0:T(8,128)(2,1)S(1)}, bf16[128,1792]{1,0:T(8,128)(2,1)S(1)}, u32[]{:S(2)}, u32[]{:S(2)}) collective-permute-start(bf16[128,1792]{1,0:T(8,128)(2,1)S(1)} %shard_map.95.refs_9_.refs_1_), channel_id=1, source_target_pairs={{0,2},{2,0},{1,3},{3,1},{4,6},{6,4},{5,7},{7,5},{8,10},{10,8},{9,1... | collective-permute-start | bytes 1376264 | tf_op jit(solution)/shard_map/ppermute | solution.py:41
  39.7 3.1 %collective-permute-start.11 = (bf16[64,2048]{1,0:T(8,128)(2,1)S(1)}, bf16[64,2048]{1,0:T(8,128)(2,1)S(1)}, u32[]{:S(2)}, u32[]{:S(2)}) collective-permute-start(bf16[64,2048]{1,0:T(8,128)(2,1)S(1)} %get-tuple-element.44.refs_2_.refs_0_), channel_id=1, source_target_pairs={{0,1},{1,0},{2,3},{3,2},{4,5},{5,4},{6,7},{7,6},{8,9},{9,8},{10,11... | collective-permute-start | bytes 786440 | tf_op jit(solution)/shard_map/ppermute | solution.py:41
  39.8 3.0 %collective-permute-start.12 = (bf16[64,2048]{1,0:T(8,128)(2,1)S(1)}, bf16[64,2048]{1,0:T(8,128)(2,1)S(1)}, u32[]{:S(2)}, u32[]{:S(2)}) collective-permute-start(bf16[64,2048]{1,0:T(8,128)(2,1)S(1)} %get-tuple-element.45.refs_4_.refs_2_), channel_id=1, source_target_pairs={{0,1},{1,0},{2,3},{3,2},{4,5},{5,4},{6,7},{7,6},{8,9},{9,8},{10,11... | collective-permute-start | bytes 786440 | tf_op jit(solution)/shard_map/ppermute | solution.py:41
  40.3 18.7 %collective-permute-start.4 = (bf16[128,512]{1,0:T(8,128)(2,1)S(1)}, bf16[128,512]{1,0:T(8,128)(2,1)S(1)}, u32[]{:S(2)}, u32[]{:S(2)}) collective-permute-start(bf16[128,512]{1,0:T(8,128)(2,1)S(1)} %shard_map.90.refs_0_), channel_id=1, source_target_pairs={{0,8},{4,12},{8,0},{12,4},{1,9},{5,13},{9,1},{13,5},{2,10},{6,14},... | collective-permute-start | bytes 393224 | tf_op jit(solution)/shard_map/ppermute | solution.py:46
  47.2 35.5 %collective-permute-start.18 = (bf16[384,1792]{1,0:T(8,128)(2,1)S(1)}, bf16[384,1792]{1,0:T(8,128)(2,1)S(1)}, u32[]{:S(2)}, u32[]{:S(2)}) collective-permute-start(bf16[384,1792]{1,0:T(8,128)(2,1)S(1)} %shard_map.96.refs_6_.refs_0_), channel_id=1, source_target_pairs={{0,2},{2,0},{1,3},{3,1},{4,6},{6,4},{5,7},{7,5},{8,10},{10,8},{9,1... | collective-permute-start | bytes 4128776 | tf_op jit(solution)/shard_map/ppermute | solution.py:41
  59.1 6.4 %collective-permute-start.13 = (bf16[128,1024]{1,0:T(8,128)(2,1)S(1)}, bf16[128,1024]{1,0:T(8,128)(2,1)S(1)}, u32[]{:S(2)}, u32[]{:S(2)}) collective-permute-start(bf16[128,1024]{1,0:T(8,128)(2,1)S(1)} %shard_map.98.refs_0_), channel_id=1, source_target_pairs={{0,4},{4,0},{8,12},{12,8},{1,5},{5,1},{9,13},{13,9},{2,6},{6,2},{1... | collective-permute-start | bytes 786440 | tf_op jit(solution)/shard_map/ppermute | solution.py:46
  65.5 1.6 %collective-permute-start.14 = (bf16[64,2048]{1,0:T(8,128)(2,1)S(1)}, bf16[64,2048]{1,0:T(8,128)(2,1)S(1)}, u32[]{:S(2)}, u32[]{:S(2)}) collective-permute-start(bf16[64,2048]{1,0:T(8,128)(2,1)S(1)} %get-tuple-element.47.refs_0_.refs_2_.refs_4_), channel_id=1, source_target_pairs={{0,1},{1,0},{2,3},{3,2},{4,5},{5,4},{6,7},{7,6},{8,9},{9,8},{10,11... | collective-permute-start | bytes 786440 | tf_op jit(solution)/shard_map/ppermute | solution.py:41
  65.6 1.9 %collective-permute-start.15 = (bf16[64,2048]{1,0:T(8,128)(2,1)S(1)}, bf16[64,2048]{1,0:T(8,128)(2,1)S(1)}, u32[]{:S(2)}, u32[]{:S(2)}) collective-permute-start(bf16[64,2048]{1,0:T(8,128)(2,1)S(1)} %get-tuple-element.48.refs_4_), channel_id=1, source_target_pairs={{0,1},{1,0},{2,3},{3,2},{4,5},{5,4},{6,7},{7,6},{8,9},{9,8},{10,11... | collective-permute-start | bytes 786440 | tf_op jit(solution)/shard_map/ppermute | solution.py:41
  69.9 27.5 %collective-permute-start.17 = (bf16[384,896]{1,0:T(8,128)(2,1)S(1)}, bf16[384,896]{1,0:T(8,128)(2,1)S(1)}, u32[]{:S(2)}, u32[]{:S(2)}) collective-permute-start(bf16[384,896]{1,0:T(8,128)(2,1)S(1)} %shard_map.100.refs_9_.refs_0_), channel_id=1, source_target_pairs={{0,2},{2,0},{1,3},{3,1},{4,6},{6,4},{5,7},{7,5},{8,10},{10,8},{9,1... | collective-permute-start | bytes 2064392 | tf_op jit(solution)/shard_map/ppermute | solution.py:41
  88.6 2.0 %collective-permute-start.19 = (bf16[128,2048]{1,0:T(8,128)(2,1)S(1)}, bf16[128,2048]{1,0:T(8,128)(2,1)S(1)}, u32[]{:S(2)}, u32[]{:S(2)}) collective-permute-start(bf16[128,2048]{1,0:T(8,128)(2,1)S(1)} %get-tuple-element.52), channel_id=1, source_target_pairs={{0,1},{1,0},{2,3},{3,2},{4,5},{5,4},{6,7},{7,6},{8,9},{9,8},{10,11... | collective-permute-start | bytes 1572872 | tf_op jit(solution)/shard_map/ppermute | solution.py:41
  88.6 24.1 %collective-permute-start.16 = (bf16[384,896]{1,0:T(8,128)(2,1)S(1)}, bf16[384,896]{1,0:T(8,128)(2,1)S(1)}, u32[]{:S(2)}, u32[]{:S(2)}) collective-permute-start(bf16[384,896]{1,0:T(8,128)(2,1)S(1)} %shard_map.101.refs_6_.refs_0_), channel_id=1, source_target_pairs={{0,2},{2,0},{1,3},{3,1},{4,6},{6,4},{5,7},{7,5},{8,10},{10,8},{9,1... | collective-permute-start | bytes 2064392 | tf_op jit(solution)/shard_map/ppermute | solution.py:41
  90.6 13.9 %collective-permute-start.20 = (bf16[128,1024]{1,0:T(8,128)(2,1)S(1)}, bf16[128,1024]{1,0:T(8,128)(2,1)S(1)}, u32[]{:S(2)}, u32[]{:S(2)}) collective-permute-start(bf16[128,1024]{1,0:T(8,128)(2,1)S(1)} %get-tuple-element.60), channel_id=1, source_target_pairs={{0,4},{4,0},{8,12},{12,8},{1,5},{5,1},{9,13},{13,9},{2,6},{6,2},{1... | collective-permute-start | bytes 786440 | tf_op jit(solution)/shard_map/ppermute | solution.py:46
  104.6 8.1 %collective-permute-start.21 = (bf16[128,512]{1,0:T(8,128)(2,1)S(1)}, bf16[128,512]{1,0:T(8,128)(2,1)S(1)}, u32[]{:S(2)}, u32[]{:S(2)}) collective-permute-start(bf16[128,512]{1,0:T(8,128)(2,1)S(1)} %get-tuple-element.67), channel_id=1, source_target_pairs={{0,8},{4,12},{8,0},{12,4},{1,9},{5,13},{9,1},{13,5},{2,10},{6,14},... | collective-permute-start | bytes 393224 | tf_op jit(solution)/shard_map/ppermute | solution.py:46
  116.0 1.6 %collective-permute-start.22 = (bf16[64,2048]{1,0:T(8,128)(2,1)S(1)}, bf16[64,2048]{1,0:T(8,128)(2,1)S(1)}, u32[]{:S(2)}, u32[]{:S(2)}) collective-permute-start(bf16[64,2048]{1,0:T(8,128)(2,1)S(1)} %get-tuple-element.69), channel_id=1, source_target_pairs={{0,1},{1,0},{2,3},{3,2},{4,5},{5,4},{6,7},{7,6},{8,9},{9,8},{10,11... | collective-permute-start | bytes 786440 | tf_op jit(solution)/shard_map/ppermute | solution.py:41
  117.6 5.6 %collective-permute-start.23 = (bf16[64,1024]{1,0:T(8,128)(2,1)S(1)}, bf16[64,1024]{1,0:T(8,128)(2,1)S(1)}, u32[]{:S(2)}, u32[]{:S(2)}) collective-permute-start(bf16[64,1024]{1,0:T(8,128)(2,1)S(1)} %get-tuple-element.71), channel_id=1, source_target_pairs={{0,4},{4,0},{8,12},{12,8},{1,5},{5,1},{9,13},{13,9},{2,6},{6,2},{1... | collective-permute-start | bytes 393224 | tf_op jit(solution)/shard_map/ppermute | solution.py:46
  123.3 7.5 %collective-permute-start.24 = (bf16[64,512]{1,0:T(8,128)(2,1)S(1)}, bf16[64,512]{1,0:T(8,128)(2,1)S(1)}, u32[]{:S(2)}, u32[]{:S(2)}) collective-permute-start(bf16[64,512]{1,0:T(8,128)(2,1)S(1)} %get-tuple-element.73), channel_id=1, source_target_pairs={{0,8},{4,12},{8,0},{12,4},{1,9},{5,13},{9,1},{13,5},{2,10},{6,14},... | collective-permute-start | bytes 196616 | tf_op jit(solution)/shard_map/ppermute | solution.py:46

commit v13 on v12

--- a/solution.py
+++ b/solution.py
@@ -333,12 +333,15 @@
     )(*arrays, *old, *after)
 
 
-def tiled(out, left, right):
+def tiled(out, left, right, above=None):
     height, width = out.shape
     for top in range(0, height, 512):
         for start in range(0, width, 256):
             rows, columns = pl.ds(top, min(512, height - top)), pl.ds(start, min(256, width - start))
-            out[rows, columns] = rows_by_cols(left[rows, :], right[:, columns]).astype(out.dtype)
+            value = rows_by_cols(left[rows, :], right[:, columns])
+            if above is not None:
+                value = value + above[rows, columns].astype(jnp.float32)
+            out[rows, columns] = value.astype(out.dtype)
 
 
 def placed(rows, columns, where):
@@ -397,6 +400,69 @@
     spec = placed(width, block, lambda i: (lower, pl.multiple_of(i * block, block)))
     scratch = [pltpu.VMEM((width, tokens), jnp.bfloat16)]
     return gradients(kernel, [(total, features)], arrays, old, (features // block,), [spec], scratch, after, cost)
+
+
+def early_terms(x, y, hs, gs, us, span, after=()):
+    count, lower, width = len(gs), span[0], span[1] - span[0]
+    tokens, features = sum(g.shape[0] for g in gs), x.shape[0]
+
+    def kernel(ins, refs):
+        gate, up, down, h_all, g_all, u_all = refs
+        top = 0
+        for i, piece in enumerate(gs):
+            rows = slice(top, top + piece.shape[0])
+            h_all[:, rows] = ins[2 + i][lower : lower + width]
+            g_all[rows] = ins[2 + count + i][:, lower : lower + width]
+            u_all[rows] = ins[2 + 2 * count + i][:, lower : lower + width]
+            top += piece.shape[0]
+        tiled(gate, ins[0].at[:, :tokens], g_all)
+        tiled(up, ins[0].at[:, :tokens], u_all)
+        tiled(down, h_all, ins[1].at[:tokens, :])
+
+    outs = [((features, width), jnp.bfloat16)] * 2 + [((width, features), jnp.bfloat16)]
+    scratch = [pltpu.VMEM((width, tokens), jnp.bfloat16)] + [pltpu.VMEM((tokens, width), jnp.bfloat16)] * 2
+    return local(kernel, outs, (x, y, *hs, *gs, *us), after, limit=6, scratch=scratch)
+
+
+def last_columns(x, first, g, u, terms, span, total, old, after, cost):
+    lower, width = span[0], span[1] - span[0]
+    features, block = x.shape[0], 512
+
+    def kernel(ins, refs):
+        gate_out, up_out, token = refs
+        step = pl.program_id(0)
+
+        @pl.when(step == 0)
+        def _():
+            token[...] = jnp.zeros_like(token)
+
+        at = lanes(step, block)
+        rows = ins[0].at[at, first:]
+        tiled(gate_out, rows, ins[1], ins[3].at[at, :])
+        tiled(up_out, rows, ins[2], ins[4].at[at, :])
+
+    spec = placed(block, width, lambda i: (pl.multiple_of(i * block, block), lower))
+    arrays = [x, g, u, *terms]
+    return gradients(kernel, [(features, total)] * 2, arrays, old, (features // block,), [spec, spec], [], after, cost)
+
+
+def last_rows(h, y, first, term, span, total, old, after, cost):
+    lower, width = span[0], span[1] - span[0]
+    features, block = y.shape[1], 512
+
+    def kernel(ins, refs):
+        out, token = refs
+        step = pl.program_id(0)
+
+        @pl.when(step == 0)
+        def _():
+            token[...] = jnp.zeros_like(token)
+
+        at = lanes(step, block)
+        tiled(out, ins[0], ins[1].at[first:, at], ins[2].at[:, at])
+
+    spec = placed(width, block, lambda i: (lower, pl.multiple_of(i * block, block)))
+    return gradients(kernel, [(total, features)], [h, y, term], old, (features // block,), [spec], [], after, cost)
 
 
 def piped(acts, grad_out, w_gate, w_up, w_down):
@@ -473,7 +539,8 @@
         return [(grads[c][k], parts[part][0]) for c in range(last)] + [(results[k], 0)]
 
     near = near_step(grads[1])
-    first = backward_piece(last, 0, None, False, (near[0],))
+    *terms, down_term = early_terms(all_x, all_y, *([g[k] for g in grads] for k in range(3)), parts[1], (near[0],))
+    first = backward_piece(last, 0, None, False, (down_term,))
     down, token = row_grads(with_last(first, 0, 0), all_y, parts[0], total, (), (), 2.0)
     far = far_step(near, (token,))
     gate, up, token = column_grads(
@@ -482,11 +549,12 @@
     finished = end_step(far)
     second = backward_piece(last, 1, first[3], True, (token, finished))
     near = near_step(second)
-    down, token = row_grads(with_last(second, 0, 1), all_y, parts[1], total, (down,), (), 3.0)
-    far = far_step(near)
-    gate, up, _ = column_grads(
-        all_x, with_last(second, 1, 1), with_last(second, 2, 1), parts[1], total, (gate, up), (near[0], token), 5.0
+    held = 2 * (heights[0] + heights[1])
+    gate, up, token = last_columns(
+        all_x, held, second[1], second[2], terms, parts[1], total, (gate, up), (near[0],), 5.0
     )
+    far = far_step(near, (token,))
+    down, _ = last_rows(second[0], all_y, held, down_term, parts[1], total, (down,), (far[0],), 3.0)
     return end_step(far, (finished,)), gate, up, down
 
 

time: 132 us -> 130 us (0.985)
  waiting for transfers between devices: 45.5 us -> 43.3 us
    pallas_call x28 -> x29, Pallas kernels: 33.8 us -> 37.4 us  [local(): pl.pallas_call(body, out_shape=shapes, in_specs=[VMEM] * len(args) + [ANY...]
    ppermute x13, waiting for transfers between devices: 21.9 us -> 18.3 us  [shifted(): return lax.ppermute(value, axis, [(i, (i + step) % n) for i in range(n)])]
    pallas_call x4, Pallas kernels: 19.8 us -> 17.1 us  [gradients(): pl.pallas_call(body, grid=grid, out_shape=[jax.ShapeDtypeStruct(shape, jn...]
    ppermute x12, waiting for transfers between devices: 23.6 us -> 24.9 us  [swapped(): return lax.ppermute(value, axis, [(i, i ^ bit) for i in range(n)])]
  transfers between devices with their start and end apart: 25 -> 25, of which waited for: 14 -> 14; matrix products, arithmetic and copies ran while one was open for 0% -> 0% of each run, Pallas kernels for 38% -> 39%
where the time goes in v13:
time: 130 us
  Pallas kernels  54.5 us (42%)
  waiting for transfers between devices  43.3 us (33%)
  starting transfers between devices  30.6 us (24%)
    pallas_call x29, Pallas kernels, local(): pl.pallas_call(body, out_shape=shapes, in_specs=[VMEM] * len(args) + [ANY...  37.4 us
    ppermute x12, waiting for transfers between devices, swapped(): return lax.ppermute(value, axis, [(i, i ^ bit) for i in range(n)])  24.9 us
    ppermute x12, starting transfers between devices, swapped(): return lax.ppermute(value, axis, [(i, i ^ bit) for i in range(n)])  20.8 us
    ppermute x13, waiting for transfers between devices, shifted(): return lax.ppermute(value, axis, [(i, (i + step) % n) for i in range(n)])  18.3 us
    pallas_call x4, Pallas kernels, gradients(): pl.pallas_call(body, grid=grid, out_shape=[jax.ShapeDtypeStruct(shape, jn...  17.1 us
    ppermute x13, starting transfers between devices, shifted(): return lax.ppermute(value, axis, [(i, (i + step) % n) for i in range(n)])  9.74 us
  transfers between devices with their start and end apart: 25, of which 14 were waited for; matrix products, arithmetic and copies ran while one was open for 0% of the time, Pallas kernels for 39%

profile of v13, /device:TPU:0, one launch (start us, length us, event | category | flops | bytes accessed | tf_op | source)
XLA Modules:
  0.0 130.2 jit_solution(16154831179526753207)
XLA Ops:
  0.6 0.9 copy-done.2
  1.6 4.1 %collective-permute-start.5 = (bf16[64,512]{1,0:T(8,128)(2,1)S(1)}, bf16[64,512]{1,0:T(8,128)(2,1)S(1)}, u32[]{:S(2)}, u32[]{:S(2)}) collective-permute-start(bf16[64,512]{1,0:T(8,128)(2,1)S(1)} %shard_map.91.refs_0_), channel_id=1, source_target_pairs={{0,8},{4,12},{8,0},{12,4},{1,9},{5,13},{9,1},{13,5},{2,10},{6,14},... | collective-permute-start | bytes 196616 | tf_op jit(solution)/shard_map/ppermute | solution.py:46
  5.7 3.6 %collective-permute-done.5.refs_1_ = bf16[64,512]{1,0:T(8,128)(2,1)S(1)} collective-permute-done((bf16[64,512]{1,0:T(8,128)(2,1)S(1)}, bf16[64,512]{1,0:T(8,128)(2,1)S(1)}, u32[]{:S(2)}, u32[]{:S(2)}) %collective-permute-start.5) | collective-permute-done | bytes 65568 | tf_op jit(solution)/shard_map/ppermute | solution.py:46
  9.3 0.6 collective-permute-start.6
  10.0 3.4 %collective-permute-start = (bf16[64,512]{1,0:T(8,128)(2,1)S(1)}, bf16[64,512]{1,0:T(8,128)(2,1)S(1)}, u32[]{:S(2)}, u32[]{:S(2)}) collective-permute-start(bf16[64,512]{1,0:T(8,128)(2,1)S(1)} %shard_map.84.refs_0_), channel_id=1, source_target_pairs={{0,8},{4,12},{8,0},{12,4},{1,9},{5,13},{9,1},{13,5},{2,10},{6,14},... | collective-permute-start | bytes 196616 | tf_op jit(solution)/shard_map/ppermute | solution.py:46
  13.4 1.7 %collective-permute-done.6.refs_1_ = bf16[64,1024]{1,0:T(8,128)(2,1)S(1)} collective-permute-done((bf16[64,1024]{1,0:T(8,128)(2,1)S(1)}, bf16[64,1024]{1,0:T(8,128)(2,1)S(1)}, u32[]{:S(2)}, u32[]{:S(2)}) %collective-permute-start.6) | collective-permute-done | bytes 131104 | tf_op jit(solution)/shard_map/ppermute | solution.py:46
  15.2 1.1 collective-permute-done.refs_1_
  16.3 1.9 %collective-permute-start.1 = (bf16[64,1024]{1,0:T(8,128)(2,1)S(1)}, bf16[64,1024]{1,0:T(8,128)(2,1)S(1)}, u32[]{:S(2)}, u32[]{:S(2)}) collective-permute-start(bf16[64,1024]{1,0:T(8,128)(2,1)S(1)} %shard_map.85.refs_0_), channel_id=1, source_target_pairs={{0,4},{4,0},{8,12},{12,8},{1,5},{5,1},{9,13},{13,9},{2,6},{6,2},{1... | collective-permute-start | bytes 393224 | tf_op jit(solution)/shard_map/ppermute | solution.py:46
  18.2 2.1 %shard_map.94.refs_3_.refs_0_ = bf16[256,1792]{1,0:T(8,128)(2,1)S(1)} custom-call(bf16[64,2048]{1,0:T(8,128)(2,1)S(1)} %shard_map.93.refs_0_.refs_2_, bf16[64,2048]{1,0:T(8,128)(2,1)S(1)} %collective-permute-done.7.refs_1_.refs_3_, bf16[64,2048]{1,0:T(8,128)(2,1)S(1)} %shard_map.93.refs_0_.refs_2_, ...), custom_call_target="tpu_custom_call" | custom-call | flops 345000000 | tf_op jit(solution)/shard_map/pallas_call | solution.py:101
  20.3 1.6 %collective-permute-start.9 = (bf16[256,1792]{1,0:T(8,128)(2,1)S(1)}, bf16[256,1792]{1,0:T(8,128)(2,1)S(1)}, u32[]{:S(2)}, u32[]{:S(2)}) collective-permute-start(bf16[256,1792]{1,0:T(8,128)(2,1)S(1)} %shard_map.94.refs_3_.refs_0_), channel_id=1, source_target_pairs={{0,2},{2,0},{1,3},{3,1},{4,6},{6,4},{5,7},{7,5},{8,10},{10,8},{9,1... | collective-permute-start | bytes 2752520 | tf_op jit(solution)/shard_map/ppermute | solution.py:41
  22.0 2.4 %collective-permute-start.2 = (bf16[128,512]{1,0:T(8,128)(2,1)S(1)}, bf16[128,512]{1,0:T(8,128)(2,1)S(1)}, u32[]{:S(2)}, u32[]{:S(2)}) collective-permute-start(bf16[128,512]{1,0:T(8,128)(2,1)S(1)} %shard_map.87.refs_0_), channel_id=1, source_target_pairs={{0,8},{4,12},{8,0},{12,4},{1,9},{5,13},{9,1},{13,5},{2,10},{6,14},... | collective-permute-start | bytes 393224 | tf_op jit(solution)/shard_map/ppermute | solution.py:46
  24.4 7.3 %collective-permute-done.2.refs_1_ = bf16[128,512]{1,0:T(8,128)(2,1)S(1)} collective-permute-done((bf16[128,512]{1,0:T(8,128)(2,1)S(1)}, bf16[128,512]{1,0:T(8,128)(2,1)S(1)}, u32[]{:S(2)}, u32[]{:S(2)}) %collective-permute-start.2) | collective-permute-done | bytes 131104 | tf_op jit(solution)/shard_map/ppermute | solution.py:46
  31.7 0.5 collective-permute-start.3
  32.2 2.5 %shard_map.95.refs_9_.refs_1_ = bf16[128,1792]{1,0:T(8,128)(2,1)S(1)} custom-call(bf16[64,2048]{1,0:T(8,128)(2,1)S(1)} %shard_map.86.refs_2_.refs_0_, bf16[64,2048]{1,0:T(8,128)(2,1)S(1)} %collective-permute-done.8.refs_1_, bf16[1792,2048]{1,0:T(8,128)(2,1)S(1)} %bitcast.1, bf16[256,1792]{1,0:T(8,128)(2,1)S(1)} %shard_map.94.refs_3_.refs_0_), custom_call_target="tpu_custom_call" | custom-call | flops 345000000 | tf_op jit(solution)/shard_map/pallas_call | solution.py:101
  34.7 1.6 %collective-permute-start.10 = (bf16[128,1792]{1,0:T(8,128)(2,1)S(1)}, bf16[128,1792]{1,0:T(8,128)(2,1)S(1)}, u32[]{:S(2)}, u32[]{:S(2)}) collective-permute-start(bf16[128,1792]{1,0:T(8,128)(2,1)S(1)} %shard_map.95.refs_9_.refs_1_), channel_id=1, source_target_pairs={{0,2},{2,0},{1,3},{3,1},{4,6},{6,4},{5,7},{7,5},{8,10},{10,8},{9,1... | collective-permute-start | bytes 1376264 | tf_op jit(solution)/shard_map/ppermute | solution.py:41
  36.3 3.4 %collective-permute-done.3.refs_1_ = bf16[128,1024]{1,0:T(8,128)(2,1)S(1)} collective-permute-done((bf16[128,1024]{1,0:T(8,128)(2,1)S(1)}, bf16[128,1024]{1,0:T(8,128)(2,1)S(1)}, u32[]{:S(2)}, u32[]{:S(2)}) %collective-permute-start.3) | collective-permute-done | bytes 262176 | tf_op jit(solution)/shard_map/ppermute | solution.py:46
  39.8 0.5 collective-permute-start.11
  40.3 2.5 %collective-permute-start.4 = (bf16[128,512]{1,0:T(8,128)(2,1)S(1)}, bf16[128,512]{1,0:T(8,128)(2,1)S(1)}, u32[]{:S(2)}, u32[]{:S(2)}) collective-permute-start(bf16[128,512]{1,0:T(8,128)(2,1)S(1)} %shard_map.90.refs_0_), channel_id=1, source_target_pairs={{0,8},{4,12},{8,0},{12,4},{1,9},{5,13},{9,1},{13,5},{2,10},{6,14},... | collective-permute-start | bytes 393224 | tf_op jit(solution)/shard_map/ppermute | solution.py:46
  42.8 4.4 %shard_map.96.refs_6_.refs_0_ = bf16[384,1792]{1,0:T(8,128)(2,1)S(1)} custom-call(bf16[64,2048]{1,0:T(8,128)(2,1)S(1)} %get-tuple-element.47.refs_2_.refs_0_, bf16[64,2048]{1,0:T(8,128)(2,1)S(1)} %collective-permute-done.11.refs_1_.refs_3_, bf16[64,2048]{1,0:T(8,128)(2,1)S(1)} %get-tuple-element.47.refs_2_.refs_0_, ...), custom_call_target="tpu_custom_call" | custom-call | flops 345000000 | tf_op jit(solution)/shard_map/pallas_call | solution.py:101
  47.2 1.6 %collective-permute-start.18 = (bf16[384,1792]{1,0:T(8,128)(2,1)S(1)}, bf16[384,1792]{1,0:T(8,128)(2,1)S(1)}, u32[]{:S(2)}, u32[]{:S(2)}) collective-permute-start(bf16[384,1792]{1,0:T(8,128)(2,1)S(1)} %shard_map.96.refs_6_.refs_0_), channel_id=1, source_target_pairs={{0,2},{2,0},{1,3},{3,1},{4,6},{6,4},{5,7},{7,5},{8,10},{10,8},{9,1... | collective-permute-start | bytes 4128776 | tf_op jit(solution)/shard_map/ppermute | solution.py:41
  48.8 4.4 %collective-permute-done.10.refs_3_ = bf16[128,1792]{1,0:T(8,128)(2,1)S(1)} collective-permute-done((bf16[128,1792]{1,0:T(8,128)(2,1)S(1)}, bf16[128,1792]{1,0:T(8,128)(2,1)S(1)}, u32[]{:S(2)}, u32[]{:S(2)}) %collective-permute-start.10) | collective-permute-done | bytes 458784 | tf_op jit(solution)/shard_map/ppermute | solution.py:41
  53.2 5.8 %shard_map.97 = (bf16[1792,128]{1,0:T(8,128)(2,1)S(1)}, bf16[128,1792]{1,0:T(8,128)(2,1)S(1)}, bf16[128,1792]{1,0:T(8,128)(2,1)S(1)}, f32[64,2048]{1,0:T(8,128)S(1)}, bf16[64,2048]{1,0:T(8,128)(2,1)S(1)}) custom-call(bf16[256,1792]{1,0:T(8,128)(2,1)S(1)} %shard_map.94.refs_3_.refs_0_, bf16[128,1792]{1,0:T(8,128)(2,1)S(1)} %shard_map.95.refs_9_.refs_1_, ...), custom_call_target="tpu_custom_call" | custom-call | flops 69000003584 | tf_op jit(solution)/shard_map/pallas_call | solution.py:101
  59.2 6.4 %collective-permute-done.13.refs_1_ = bf16[128,1024]{1,0:T(8,128)(2,1)S(1)} collective-permute-done((bf16[128,1024]{1,0:T(8,128)(2,1)S(1)}, bf16[128,1024]{1,0:T(8,128)(2,1)S(1)}, u32[]{:S(2)}, u32[]{:S(2)}) %collective-permute-start.13) | collective-permute-done | bytes 262176 | tf_op jit(solution)/shard_map/ppermute | solution.py:46
  65.6 0.5 collective-permute-start.15
  66.1 1.0 collective-permute-done.14.refs_1_.refs_3_.refs_5_
  67.2 0.4 collective-permute-done.15.refs_5_
  67.5 2.4 %shard_map.100.refs_9_.refs_0_ = bf16[384,896]{1,0:T(8,128)(2,1)S(1)} custom-call(bf16[64,2048]{1,0:T(8,128)(2,1)S(1)} %get-tuple-element.50.refs_0_.refs_2_.refs_4_, bf16[64,2048]{1,0:T(8,128)(2,1)S(1)} %collective-permute-done.14.refs_1_.refs_3_.refs_5_, bf16[64,2048]{1,0:T(8,128)(2,1)S(1)} %get-tuple-element.50.refs_0_.refs_2_.refs_4_, ...), custom_call_target="tpu_custom_call" | custom-call | flops 345000000 | tf_op jit(solution)/shard_map/pallas_call | solution.py:101
  70.0 1.8 %collective-permute-start.17 = (bf16[384,896]{1,0:T(8,128)(2,1)S(1)}, bf16[384,896]{1,0:T(8,128)(2,1)S(1)}, u32[]{:S(2)}, u32[]{:S(2)}) collective-permute-start(bf16[384,896]{1,0:T(8,128)(2,1)S(1)} %shard_map.100.refs_9_.refs_0_), channel_id=1, source_target_pairs={{0,2},{2,0},{1,3},{3,1},{4,6},{6,4},{5,7},{7,5},{8,10},{10,8},{9,1... | collective-permute-start | bytes 2064392 | tf_op jit(solution)/shard_map/ppermute | solution.py:41
  71.8 2.4 %shard_map.101.refs_6_.refs_0_ = bf16[384,896]{1,0:T(8,128)(2,1)S(1)} custom-call(bf16[64,2048]{1,0:T(8,128)(2,1)S(1)} %get-tuple-element.50.refs_0_.refs_2_.refs_4_, bf16[64,2048]{1,0:T(8,128)(2,1)S(1)} %collective-permute-done.14.refs_1_.refs_3_.refs_5_, bf16[64,2048]{1,0:T(8,128)(2,1)S(1)} %get-tuple-element.50.refs_0_.refs_2_.refs_4_, ...), custom_call_target="tpu_custom_call" | custom-call | flops 345000000 | tf_op jit(solution)/shard_map/pallas_call | solution.py:101
  74.2 0.2 shard_map.103.refs_7_.refs_1_.refs_3_
  74.4 0.6 shard_map.102.refs_6_.refs_0_
  75.0 7.7 %collective-permute-done.18.refs_1_ = bf16[384,1792]{1,0:T(8,128)(2,1)S(1)} collective-permute-done((bf16[384,1792]{1,0:T(8,128)(2,1)S(1)}, bf16[384,1792]{1,0:T(8,128)(2,1)S(1)}, u32[]{:S(2)}, u32[]{:S(2)}) %collective-permute-start.18) | collective-permute-done | bytes 1376288 | tf_op jit(solution)/shard_map/ppermute | solution.py:41
  82.7 6.1 %shard_map.104 = (bf16[1792,128]{1,0:T(8,128)(2,1)S(1)}, bf16[128,1792]{1,0:T(8,128)(2,1)S(1)}, bf16[128,1792]{1,0:T(8,128)(2,1)S(1)}, f32[128,2048]{1,0:T(8,128)S(1)}, bf16[128,2048]{1,0:T(8,128)(2,1)S(1)}) custom-call(bf16[384,1792]{1,0:T(8,128)(2,1)S(1)} %shard_map.96.refs_6_.refs_0_, bf16[384,1792]{1,0:T(8,128)(2,1)S(1)} %collective-permute-done.18.refs_1_, ...), custom_call_target="tpu_custom_call" | custom-call | flops 69000003584 | tf_op jit(solution)/shard_map/pallas_call | solution.py:101
  88.9 1.8 %collective-permute-start.16 = (bf16[384,896]{1,0:T(8,128)(2,1)S(1)}, bf16[384,896]{1,0:T(8,128)(2,1)S(1)}, u32[]{:S(2)}, u32[]{:S(2)}) collective-permute-start(bf16[384,896]{1,0:T(8,128)(2,1)S(1)} %shard_map.101.refs_6_.refs_0_), channel_id=1, source_target_pairs={{0,2},{2,0},{1,3},{3,1},{4,6},{6,4},{5,7},{7,5},{8,10},{10,8},{9,1... | collective-permute-start | bytes 2064392 | tf_op jit(solution)/shard_map/ppermute | solution.py:41
  91.0 3.3 %shard_map.106 = (bf16[2048,896]{1,0:T(8,128)(2,1)S(1)}, bf16[2048,896]{1,0:T(8,128)(2,1)S(1)}, bf16[896,2048]{1,0:T(8,128)(2,1)S(1)}) custom-call(bf16[2048,384]{1,0:T(8,128)(2,1)S(1)} %shard_map.102.refs_6_.refs_0_, bf16[384,2048]{1,0:T(8,128)(2,1)S(1)} %shard_map.103.refs_7_.refs_1_.refs_3_, bf16[1792,128]{1,0:T(8,128)(2,1)S(1)} %get-tuple-element.52.refs_2_.refs_0_, ...), custom_call_target="tpu_custom_call" | custom-call | flops 115000000 | tf_op jit(solution)/shard_map/pallas_call | solution.py:101
  94.3 3.2 %collective-permute-done.17.refs_1_ = bf16[384,896]{1,0:T(8,128)(2,1)S(1)} collective-permute-done((bf16[384,896]{1,0:T(8,128)(2,1)S(1)}, bf16[384,896]{1,0:T(8,128)(2,1)S(1)}, u32[]{:S(2)}, u32[]{:S(2)}) %collective-permute-start.17) | collective-permute-done | bytes 688160 | tf_op jit(solution)/shard_map/ppermute | solution.py:41
  97.5 3.2 %shard_map.107 = (bf16[896,128]{1,0:T(8,128)(2,1)S(1)}, bf16[128,896]{1,0:T(8,128)(2,1)S(1)}, bf16[128,896]{1,0:T(8,128)(2,1)S(1)}, f32[128,2048]{1,0:T(8,128)S(1)}) custom-call(bf16[384,896]{1,0:T(8,128)(2,1)S(1)} %shard_map.100.refs_9_.refs_0_, bf16[384,896]{1,0:T(8,128)(2,1)S(1)} %collective-permute-done.17.refs_1_, bf16[2048,1792]{1,0:T(8,128)(2,1)S(1)} %copy-done, ...), custom_call_target="tpu_custom_call" | custom-call | flops 115000000 | tf_op jit(solution)/shard_map/pallas_call | solution.py:101
  100.6 3.9 %shard_map.108 = (bf16[1792,2048]{1,0:T(8,128)(2,1)}, bf16[16,128]{1,0:T(8,128)(2,1)S(1)}) custom-call(bf16[1792,128]{1,0:T(8,128)(2,1)S(1)} %get-tuple-element.52.refs_2_.refs_0_, bf16[1792,128]{1,0:T(8,128)(2,1)S(1)} %get-tuple-element.55.refs_3_.refs_1_, bf16[896,128]{1,0:T(8,128)(2,1)S(1)} %get-tuple-element.67.refs_2_, ...), custom_call_target="tpu_custom_call" | custom-call | flops 2300000000 | tf_op jit(solution)/shard_map/pallas_call | solution.py:323
  104.6 2.1 %collective-permute-start.21 = (bf16[128,512]{1,0:T(8,128)(2,1)S(1)}, bf16[128,512]{1,0:T(8,128)(2,1)S(1)}, u32[]{:S(2)}, u32[]{:S(2)}) collective-permute-start(bf16[128,512]{1,0:T(8,128)(2,1)S(1)} %get-tuple-element.71), channel_id=1, source_target_pairs={{0,8},{4,12},{8,0},{12,4},{1,9},{5,13},{9,1},{13,5},{2,10},{6,14},... | collective-permute-start | bytes 393224 | tf_op jit(solution)/shard_map/ppermute | solution.py:46
  106.7 6.0 %shard_map.110 = (bf16[2048,1792]{1,0:T(8,128)(2,1)}, bf16[2048,1792]{1,0:T(8,128)(2,1)}, bf16[16,128]{1,0:T(8,128)(2,1)S(1)}) custom-call(bf16[2048,384]{1,0:T(8,128)(2,1)S(1)} %shard_map.102.refs_6_.refs_0_, bf16[128,1792]{1,0:T(8,128)(2,1)S(1)} %get-tuple-element.49.refs_2_.refs_9_.refs_4_.refs_1_, ...), custom_call_target="tpu_custom_call" | custom-call | flops 115000000 | tf_op jit(solution)/shard_map/pallas_call | solution.py:323
  112.8 3.2 %shard_map.112 = (bf16[896,128]{1,0:T(8,128)(2,1)S(1)}, bf16[128,896]{1,0:T(8,128)(2,1)S(1)}, bf16[128,896]{1,0:T(8,128)(2,1)S(1)}, f32[64,2048]{1,0:T(8,128)S(1)}, bf16[64,2048]{1,0:T(8,128)(2,1)S(1)}) custom-call(bf16[384,896]{1,0:T(8,128)(2,1)S(1)} %shard_map.101.refs_6_.refs_0_, bf16[384,896]{1,0:T(8,128)(2,1)S(1)} %collective-permute-done.16.refs_1_, ...), custom_call_target="tpu_custom_call" | custom-call | flops 115000000 | tf_op jit(solution)/shard_map/pallas_call | solution.py:101
  116.1 1.5 %collective-permute-done.22.refs_1_ = bf16[64,2048]{1,0:T(8,128)(2,1)S(1)} collective-permute-done((bf16[64,2048]{1,0:T(8,128)(2,1)S(1)}, bf16[64,2048]{1,0:T(8,128)(2,1)S(1)}, u32[]{:S(2)}, u32[]{:S(2)}) %collective-permute-start.22) | collective-permute-done | bytes 262176 | tf_op jit(solution)/shard_map/ppermute | solution.py:41
  117.7 1.5 %collective-permute-start.23 = (bf16[64,1024]{1,0:T(8,128)(2,1)S(1)}, bf16[64,1024]{1,0:T(8,128)(2,1)S(1)}, u32[]{:S(2)}, u32[]{:S(2)}) collective-permute-start(bf16[64,1024]{1,0:T(8,128)(2,1)S(1)} %get-tuple-element.75), channel_id=1, source_target_pairs={{0,4},{4,0},{8,12},{12,8},{1,5},{5,1},{9,13},{13,9},{2,6},{6,2},{1... | collective-permute-start | bytes 393224 | tf_op jit(solution)/shard_map/ppermute | solution.py:46
  119.2 4.1 %shard_map.114 = (bf16[2048,1792]{1,0:T(8,128)(2,1)}, bf16[2048,1792]{1,0:T(8,128)(2,1)}, bf16[16,128]{1,0:T(8,128)(2,1)S(1)}) custom-call(bf16[2048,384]{1,0:T(8,128)(2,1)S(1)} %shard_map.102.refs_6_.refs_0_, bf16[128,896]{1,0:T(8,128)(2,1)S(1)} %get-tuple-element.76.refs_1_, ...), custom_call_target="tpu_custom_call", output_to_operand_aliasing={{0}: (5, {}), {1}: (6, {})} | custom-call | flops 5750000128 | tf_op jit(solution)/shard_map/pallas_call | solution.py:323
  123.3 1.7 %collective-permute-start.24 = (bf16[64,512]{1,0:T(8,128)(2,1)S(1)}, bf16[64,512]{1,0:T(8,128)(2,1)S(1)}, u32[]{:S(2)}, u32[]{:S(2)}) collective-permute-start(bf16[64,512]{1,0:T(8,128)(2,1)S(1)} %get-tuple-element.84), channel_id=1, source_target_pairs={{0,8},{4,12},{8,0},{12,4},{1,9},{5,13},{9,1},{13,5},{2,10},{6,14},... | collective-permute-start | bytes 196616 | tf_op jit(solution)/shard_map/ppermute | solution.py:46
  125.0 3.0 %shard_map.117 = (bf16[1792,2048]{1,0:T(8,128)(2,1)}, bf16[16,128]{1,0:T(8,128)(2,1)}) custom-call(bf16[896,128]{1,0:T(8,128)(2,1)S(1)} %get-tuple-element.87.refs_0_, bf16[384,2048]{1,0:T(8,128)(2,1)S(1)} %shard_map.103.refs_7_.refs_1_.refs_3_, bf16[896,2048]{1,0:T(8,128)(2,1)S(1)} %get-tuple-element.62.refs_4_.refs_2_, ...), custom_call_target="tpu_custom_call", output_to_operand_aliasing={{0}: (3, {})} | custom-call | flops 3449999872 | tf_op jit(solution)/shard_map/pallas_call | solution.py:323
  128.0 1.5 %collective-permute-done.24.refs_1_ = bf16[64,512]{1,0:T(8,128)(2,1)S(1)} collective-permute-done((bf16[64,512]{1,0:T(8,128)(2,1)S(1)}, bf16[64,512]{1,0:T(8,128)(2,1)S(1)}, u32[]{:S(2)}, u32[]{:S(2)}) %collective-permute-start.24) | collective-permute-done | bytes 65568 | tf_op jit(solution)/shard_map/ppermute | solution.py:46
  129.5 0.7 shard_map.116
  (51 shorter events, 1.2 us)
Async XLA Ops:
  0.6 0.9 copy-start.2
  1.6 8.4 %copy-start.3 = (bf16[192,512]{1,0:T(8,128)(2,1)S(1)}, bf16[192,512]{1,0:T(8,128)(2,1)}, u32[]{:S(2)}) copy-start(bf16[192,512]{1,0:T(8,128)(2,1)} %source.1) | copy-start | bytes 589828
  1.6 8.4 %copy-start.4 = (bf16[192,512]{1,0:T(8,128)(2,1)S(1)}, bf16[192,512]{1,0:T(8,128)(2,1)}, u32[]{:S(2)}) copy-start(bf16[192,512]{1,0:T(8,128)(2,1)} %refs_1_.5) | copy-start | bytes 589828
  1.6 16.6 %copy-start = (bf16[2048,1792]{1,0:T(8,128)(2,1)S(1)}, bf16[2048,1792]{1,0:T(8,128)(2,1)}, u32[]{:S(2)}) copy-start(bf16[2048,1792]{1,0:T(8,128)(2,1)} %refs_2_.7) | copy-start | bytes 22020100
  1.6 16.6 %copy-start.1 = (bf16[2048,1792]{1,0:T(8,128)(2,1)S(1)}, bf16[2048,1792]{1,0:T(8,128)(2,1)}, u32[]{:S(2)}) copy-start(bf16[2048,1792]{1,0:T(8,128)(2,1)} %refs_3_.5) | copy-start | bytes 22020100
  1.6 7.8 %collective-permute-start.5 = (bf16[64,512]{1,0:T(8,128)(2,1)S(1)}, bf16[64,512]{1,0:T(8,128)(2,1)S(1)}, u32[]{:S(2)}, u32[]{:S(2)}) collective-permute-start(bf16[64,512]{1,0:T(8,128)(2,1)S(1)} %shard_map.91.refs_0_), channel_id=1, source_target_pairs={{0,8},{4,12},{8,0},{12,4},{1,9},{5,13},{9,1},{13,5},{2,10},{6,14},... | collective-permute-start | bytes 196616 | tf_op jit(solution)/shard_map/ppermute | solution.py:46
  9.3 5.7 %collective-permute-start.6 = (bf16[64,1024]{1,0:T(8,128)(2,1)S(1)}, bf16[64,1024]{1,0:T(8,128)(2,1)S(1)}, u32[]{:S(2)}, u32[]{:S(2)}) collective-permute-start(bf16[64,1024]{1,0:T(8,128)(2,1)S(1)} %shard_map.92.refs_0_), channel_id=1, source_target_pairs={{0,4},{4,0},{8,12},{12,8},{1,5},{5,1},{9,13},{13,9},{2,6},{6,2},{1... | collective-permute-start | bytes 393224 | tf_op jit(solution)/shard_map/ppermute | solution.py:46
  10.0 6.3 %collective-permute-start = (bf16[64,512]{1,0:T(8,128)(2,1)S(1)}, bf16[64,512]{1,0:T(8,128)(2,1)S(1)}, u32[]{:S(2)}, u32[]{:S(2)}) collective-permute-start(bf16[64,512]{1,0:T(8,128)(2,1)S(1)} %shard_map.84.refs_0_), channel_id=1, source_target_pairs={{0,8},{4,12},{8,0},{12,4},{1,9},{5,13},{9,1},{13,5},{2,10},{6,14},... | collective-permute-start | bytes 196616 | tf_op jit(solution)/shard_map/ppermute | solution.py:46
  15.1 3.0 %collective-permute-start.7 = (bf16[64,2048]{1,0:T(8,128)(2,1)S(1)}, bf16[64,2048]{1,0:T(8,128)(2,1)S(1)}, u32[]{:S(2)}, u32[]{:S(2)}) collective-permute-start(bf16[64,2048]{1,0:T(8,128)(2,1)S(1)} %shard_map.93.refs_0_.refs_2_), channel_id=1, source_target_pairs={{0,1},{1,0},{2,3},{3,2},{4,5},{5,4},{6,7},{7,6},{8,9},{9,8},{10,11... | collective-permute-start | bytes 786440 | tf_op jit(solution)/shard_map/ppermute | solution.py:41
  16.3 5.6 %collective-permute-start.1 = (bf16[64,1024]{1,0:T(8,128)(2,1)S(1)}, bf16[64,1024]{1,0:T(8,128)(2,1)S(1)}, u32[]{:S(2)}, u32[]{:S(2)}) collective-permute-start(bf16[64,1024]{1,0:T(8,128)(2,1)S(1)} %shard_map.85.refs_0_), channel_id=1, source_target_pairs={{0,4},{4,0},{8,12},{12,8},{1,5},{5,1},{9,13},{13,9},{2,6},{6,2},{1... | collective-permute-start | bytes 393224 | tf_op jit(solution)/shard_map/ppermute | solution.py:46
  18.2 14.0 %slice-start = ((s8[7340032]{0:T(1024)(128)(4,1)}), s8[4194304]{0:T(1024)(128)(4,1)S(1)}, s32[]{:S(2)}) async-start(s8[7340032]{0:T(1024)(128)(4,1)} %bitcast), calls=%async_computation | async-start | bytes 8388608
  20.3 11.9 %slice-start.1 = ((s8[7340032]{0:T(1024)(128)(4,1)}), s8[3145728]{0:T(1024)(128)(4,1)S(1)}, s32[]{:S(2)}) async-start(s8[7340032]{0:T(1024)(128)(4,1)} %bitcast), calls=%async_computation.1 | async-start | bytes 6291456
  20.3 32.9 %collective-permute-start.9 = (bf16[256,1792]{1,0:T(8,128)(2,1)S(1)}, bf16[256,1792]{1,0:T(8,128)(2,1)S(1)}, u32[]{:S(2)}, u32[]{:S(2)}) collective-permute-start(bf16[256,1792]{1,0:T(8,128)(2,1)S(1)} %shard_map.94.refs_3_.refs_0_), channel_id=1, source_target_pairs={{0,2},{2,0},{1,3},{3,1},{4,6},{6,4},{5,7},{7,5},{8,10},{10,8},{9,1... | collective-permute-start | bytes 2752520 | tf_op jit(solution)/shard_map/ppermute | solution.py:41
  21.9 10.3 %collective-permute-start.8 = (bf16[64,2048]{1,0:T(8,128)(2,1)S(1)}, bf16[64,2048]{1,0:T(8,128)(2,1)S(1)}, u32[]{:S(2)}, u32[]{:S(2)}) collective-permute-start(bf16[64,2048]{1,0:T(8,128)(2,1)S(1)} %shard_map.86.refs_2_.refs_0_), channel_id=1, source_target_pairs={{0,1},{1,0},{2,3},{3,2},{4,5},{5,4},{6,7},{7,6},{8,9},{9,8},{10,11... | collective-permute-start | bytes 786440 | tf_op jit(solution)/shard_map/ppermute | solution.py:41
  22.0 9.7 %collective-permute-start.2 = (bf16[128,512]{1,0:T(8,128)(2,1)S(1)}, bf16[128,512]{1,0:T(8,128)(2,1)S(1)}, u32[]{:S(2)}, u32[]{:S(2)}) collective-permute-start(bf16[128,512]{1,0:T(8,128)(2,1)S(1)} %shard_map.87.refs_0_), channel_id=1, source_target_pairs={{0,8},{4,12},{8,0},{12,4},{1,9},{5,13},{9,1},{13,5},{2,10},{6,14},... | collective-permute-start | bytes 393224 | tf_op jit(solution)/shard_map/ppermute | solution.py:46
  31.7 8.0 %collective-permute-start.3 = (bf16[128,1024]{1,0:T(8,128)(2,1)S(1)}, bf16[128,1024]{1,0:T(8,128)(2,1)S(1)}, u32[]{:S(2)}, u32[]{:S(2)}) collective-permute-start(bf16[128,1024]{1,0:T(8,128)(2,1)S(1)} %shard_map.88.refs_0_), channel_id=1, source_target_pairs={{0,4},{4,0},{8,12},{12,8},{1,5},{5,1},{9,13},{13,9},{2,6},{6,2},{1... | collective-permute-start | bytes 786440 | tf_op jit(solution)/shard_map/ppermute | solution.py:46
  34.7 18.5 %collective-permute-start.10 = (bf16[128,1792]{1,0:T(8,128)(2,1)S(1)}, bf16[128,1792]{1,0:T(8,128)(2,1)S(1)}, u32[]{:S(2)}, u32[]{:S(2)}) collective-permute-start(bf16[128,1792]{1,0:T(8,128)(2,1)S(1)} %shard_map.95.refs_9_.refs_1_), channel_id=1, source_target_pairs={{0,2},{2,0},{1,3},{3,1},{4,6},{6,4},{5,7},{7,5},{8,10},{10,8},{9,1... | collective-permute-start | bytes 1376264 | tf_op jit(solution)/shard_map/ppermute | solution.py:41
  39.7 3.1 %collective-permute-start.12 = (bf16[64,2048]{1,0:T(8,128)(2,1)S(1)}, bf16[64,2048]{1,0:T(8,128)(2,1)S(1)}, u32[]{:S(2)}, u32[]{:S(2)}) collective-permute-start(bf16[64,2048]{1,0:T(8,128)(2,1)S(1)} %get-tuple-element.48.refs_4_.refs_2_), channel_id=1, source_target_pairs={{0,1},{1,0},{2,3},{3,2},{4,5},{5,4},{6,7},{7,6},{8,9},{9,8},{10,11... | collective-permute-start | bytes 786440 | tf_op jit(solution)/shard_map/ppermute | solution.py:41
  39.8 3.0 %collective-permute-start.11 = (bf16[64,2048]{1,0:T(8,128)(2,1)S(1)}, bf16[64,2048]{1,0:T(8,128)(2,1)S(1)}, u32[]{:S(2)}, u32[]{:S(2)}) collective-permute-start(bf16[64,2048]{1,0:T(8,128)(2,1)S(1)} %get-tuple-element.47.refs_2_.refs_0_), channel_id=1, source_target_pairs={{0,1},{1,0},{2,3},{3,2},{4,5},{5,4},{6,7},{7,6},{8,9},{9,8},{10,11... | collective-permute-start | bytes 786440 | tf_op jit(solution)/shard_map/ppermute | solution.py:41
  40.3 18.7 %collective-permute-start.4 = (bf16[128,512]{1,0:T(8,128)(2,1)S(1)}, bf16[128,512]{1,0:T(8,128)(2,1)S(1)}, u32[]{:S(2)}, u32[]{:S(2)}) collective-permute-start(bf16[128,512]{1,0:T(8,128)(2,1)S(1)} %shard_map.90.refs_0_), channel_id=1, source_target_pairs={{0,8},{4,12},{8,0},{12,4},{1,9},{5,13},{9,1},{13,5},{2,10},{6,14},... | collective-permute-start | bytes 393224 | tf_op jit(solution)/shard_map/ppermute | solution.py:46
  47.2 35.5 %collective-permute-start.18 = (bf16[384,1792]{1,0:T(8,128)(2,1)S(1)}, bf16[384,1792]{1,0:T(8,128)(2,1)S(1)}, u32[]{:S(2)}, u32[]{:S(2)}) collective-permute-start(bf16[384,1792]{1,0:T(8,128)(2,1)S(1)} %shard_map.96.refs_6_.refs_0_), channel_id=1, source_target_pairs={{0,2},{2,0},{1,3},{3,1},{4,6},{6,4},{5,7},{7,5},{8,10},{10,8},{9,1... | collective-permute-start | bytes 4128776 | tf_op jit(solution)/shard_map/ppermute | solution.py:41
  59.1 6.4 %collective-permute-start.13 = (bf16[128,1024]{1,0:T(8,128)(2,1)S(1)}, bf16[128,1024]{1,0:T(8,128)(2,1)S(1)}, u32[]{:S(2)}, u32[]{:S(2)}) collective-permute-start(bf16[128,1024]{1,0:T(8,128)(2,1)S(1)} %shard_map.98.refs_0_), channel_id=1, source_target_pairs={{0,4},{4,0},{8,12},{12,8},{1,5},{5,1},{9,13},{13,9},{2,6},{6,2},{1... | collective-permute-start | bytes 786440 | tf_op jit(solution)/shard_map/ppermute | solution.py:46
  65.6 1.6 %collective-permute-start.14 = (bf16[64,2048]{1,0:T(8,128)(2,1)S(1)}, bf16[64,2048]{1,0:T(8,128)(2,1)S(1)}, u32[]{:S(2)}, u32[]{:S(2)}) collective-permute-start(bf16[64,2048]{1,0:T(8,128)(2,1)S(1)} %get-tuple-element.50.refs_0_.refs_2_.refs_4_), channel_id=1, source_target_pairs={{0,1},{1,0},{2,3},{3,2},{4,5},{5,4},{6,7},{7,6},{8,9},{9,8},{10,11... | collective-permute-start | bytes 786440 | tf_op jit(solution)/shard_map/ppermute | solution.py:41
  65.6 1.9 %collective-permute-start.15 = (bf16[64,2048]{1,0:T(8,128)(2,1)S(1)}, bf16[64,2048]{1,0:T(8,128)(2,1)S(1)}, u32[]{:S(2)}, u32[]{:S(2)}) collective-permute-start(bf16[64,2048]{1,0:T(8,128)(2,1)S(1)} %get-tuple-element.51.refs_4_), channel_id=1, source_target_pairs={{0,1},{1,0},{2,3},{3,2},{4,5},{5,4},{6,7},{7,6},{8,9},{9,8},{10,11... | collective-permute-start | bytes 786440 | tf_op jit(solution)/shard_map/ppermute | solution.py:41
  70.0 27.5 %collective-permute-start.17 = (bf16[384,896]{1,0:T(8,128)(2,1)S(1)}, bf16[384,896]{1,0:T(8,128)(2,1)S(1)}, u32[]{:S(2)}, u32[]{:S(2)}) collective-permute-start(bf16[384,896]{1,0:T(8,128)(2,1)S(1)} %shard_map.100.refs_9_.refs_0_), channel_id=1, source_target_pairs={{0,2},{2,0},{1,3},{3,1},{4,6},{6,4},{5,7},{7,5},{8,10},{10,8},{9,1... | collective-permute-start | bytes 2064392 | tf_op jit(solution)/shard_map/ppermute | solution.py:41
  88.8 2.0 %collective-permute-start.19 = (bf16[128,2048]{1,0:T(8,128)(2,1)S(1)}, bf16[128,2048]{1,0:T(8,128)(2,1)S(1)}, u32[]{:S(2)}, u32[]{:S(2)}) collective-permute-start(bf16[128,2048]{1,0:T(8,128)(2,1)S(1)} %get-tuple-element.60), channel_id=1, source_target_pairs={{0,1},{1,0},{2,3},{3,2},{4,5},{5,4},{6,7},{7,6},{8,9},{9,8},{10,11... | collective-permute-start | bytes 1572872 | tf_op jit(solution)/shard_map/ppermute | solution.py:41
  88.9 23.9 %collective-permute-start.16 = (bf16[384,896]{1,0:T(8,128)(2,1)S(1)}, bf16[384,896]{1,0:T(8,128)(2,1)S(1)}, u32[]{:S(2)}, u32[]{:S(2)}) collective-permute-start(bf16[384,896]{1,0:T(8,128)(2,1)S(1)} %shard_map.101.refs_6_.refs_0_), channel_id=1, source_target_pairs={{0,2},{2,0},{1,3},{3,1},{4,6},{6,4},{5,7},{7,5},{8,10},{10,8},{9,1... | collective-permute-start | bytes 2064392 | tf_op jit(solution)/shard_map/ppermute | solution.py:41
  90.9 13.7 %collective-permute-start.20 = (bf16[128,1024]{1,0:T(8,128)(2,1)S(1)}, bf16[128,1024]{1,0:T(8,128)(2,1)S(1)}, u32[]{:S(2)}, u32[]{:S(2)}) collective-permute-start(bf16[128,1024]{1,0:T(8,128)(2,1)S(1)} %get-tuple-element.66), channel_id=1, source_target_pairs={{0,4},{4,0},{8,12},{12,8},{1,5},{5,1},{9,13},{13,9},{2,6},{6,2},{1... | collective-permute-start | bytes 786440 | tf_op jit(solution)/shard_map/ppermute | solution.py:46
  104.6 8.1 %collective-permute-start.21 = (bf16[128,512]{1,0:T(8,128)(2,1)S(1)}, bf16[128,512]{1,0:T(8,128)(2,1)S(1)}, u32[]{:S(2)}, u32[]{:S(2)}) collective-permute-start(bf16[128,512]{1,0:T(8,128)(2,1)S(1)} %get-tuple-element.71), channel_id=1, source_target_pairs={{0,8},{4,12},{8,0},{12,4},{1,9},{5,13},{9,1},{13,5},{2,10},{6,14},... | collective-permute-start | bytes 393224 | tf_op jit(solution)/shard_map/ppermute | solution.py:46
  116.0 1.6 %collective-permute-start.22 = (bf16[64,2048]{1,0:T(8,128)(2,1)S(1)}, bf16[64,2048]{1,0:T(8,128)(2,1)S(1)}, u32[]{:S(2)}, u32[]{:S(2)}) collective-permute-start(bf16[64,2048]{1,0:T(8,128)(2,1)S(1)} %get-tuple-element.73), channel_id=1, source_target_pairs={{0,1},{1,0},{2,3},{3,2},{4,5},{5,4},{6,7},{7,6},{8,9},{9,8},{10,11... | collective-permute-start | bytes 786440 | tf_op jit(solution)/shard_map/ppermute | solution.py:41
  117.7 5.6 %collective-permute-start.23 = (bf16[64,1024]{1,0:T(8,128)(2,1)S(1)}, bf16[64,1024]{1,0:T(8,128)(2,1)S(1)}, u32[]{:S(2)}, u32[]{:S(2)}) collective-permute-start(bf16[64,1024]{1,0:T(8,128)(2,1)S(1)} %get-tuple-element.75), channel_id=1, source_target_pairs={{0,4},{4,0},{8,12},{12,8},{1,5},{5,1},{9,13},{13,9},{2,6},{6,2},{1... | collective-permute-start | bytes 393224 | tf_op jit(solution)/shard_map/ppermute | solution.py:46
  123.3 6.2 %collective-permute-start.24 = (bf16[64,512]{1,0:T(8,128)(2,1)S(1)}, bf16[64,512]{1,0:T(8,128)(2,1)S(1)}, u32[]{:S(2)}, u32[]{:S(2)}) collective-permute-start(bf16[64,512]{1,0:T(8,128)(2,1)S(1)} %get-tuple-element.84), channel_id=1, source_target_pairs={{0,8},{4,12},{8,0},{12,4},{1,9},{5,13},{9,1},{13,5},{2,10},{6,14},... | collective-permute-start | bytes 196616 | tf_op jit(solution)/shard_map/ppermute | solution.py:46

commit v14 on v13

--- a/solution.py
+++ b/solution.py
@@ -328,7 +328,7 @@
         out_specs=specs,
         scratch_shapes=scratch,
         input_output_aliases={len(arrays) + i: i for i in range(len(old))},
-        compiler_params=pltpu.CompilerParams(vmem_limit_bytes=14 * MIB),
+        compiler_params=pltpu.CompilerParams(vmem_limit_bytes=8 * MIB),
         cost_estimate=declared(cost),
     )(*arrays, *old, *after)
 
@@ -346,60 +346,6 @@
 
 def placed(rows, columns, where):
     return pl.BlockSpec((pl.Element(rows), pl.Element(columns)), where)
-
-
-def column_grads(x, gs, us, span, total, old, after=(), cost=0.1):
-    arrays = [x, *(p[0] for p in (*gs, *us))]
-    count, lower, width = len(gs), span[0], span[1] - span[0]
-    features, tokens = x.shape
-    block = 512
-
-    def kernel(ins, refs):
-        gate_out, up_out, token, g_all, u_all = refs
-        step = pl.program_id(0)
-
-        @pl.when(step == 0)
-        def _():
-            token[...] = jnp.zeros_like(token)
-            for first, pieces, target in ((1, gs, g_all), (1 + count, us, u_all)):
-                top = 0
-                for i, (piece, column) in enumerate(pieces):
-                    rows = piece.shape[0]
-                    target[top : top + rows] = ins[first + i][:, column : column + width]
-                    top += rows
-
-        rows = ins[0].at[lanes(step, block), :]
-        tiled(gate_out, rows, g_all)
-        tiled(up_out, rows, u_all)
-
-    spec = placed(block, width, lambda i: (pl.multiple_of(i * block, block), lower))
-    scratch = [pltpu.VMEM((tokens, width), jnp.bfloat16)] * 2
-    return gradients(kernel, [(features, total)] * 2, arrays, old, (features // block,), [spec, spec], scratch, after, cost)
-
-
-def row_grads(hs, y, span, total, old, after=(), cost=0.1):
-    arrays = [*(p[0] for p in hs), y]
-    count, lower, width = len(hs), span[0], span[1] - span[0]
-    tokens, features = y.shape
-    block = 512
-
-    def kernel(ins, refs):
-        out, token, h_all = refs
-        step = pl.program_id(0)
-
-        @pl.when(step == 0)
-        def _():
-            token[...] = jnp.zeros_like(token)
-            left = 0
-            for i, (piece, row) in enumerate(hs):
-                h_all[:, left : left + piece.shape[1]] = ins[i][row : row + width]
-                left += piece.shape[1]
-
-        tiled(out, h_all, ins[count].at[:, lanes(step, block)])
-
-    spec = placed(width, block, lambda i: (lower, pl.multiple_of(i * block, block)))
-    scratch = [pltpu.VMEM((width, tokens), jnp.bfloat16)]
-    return gradients(kernel, [(total, features)], arrays, old, (features // block,), [spec], scratch, after, cost)
 
 
 def early_terms(x, y, hs, gs, us, span, after=()):
@@ -535,21 +481,20 @@
     ]
     grads.append(backward_piece(1, 0, None, True, (all_x, all_y), grads[0][3:]))
 
-    def with_last(results, k, part):
-        return [(grads[c][k], parts[part][0]) for c in range(last)] + [(results[k], 0)]
-
     near = near_step(grads[1])
-    *terms, down_term = early_terms(all_x, all_y, *([g[k] for g in grads] for k in range(3)), parts[1], (near[0],))
-    first = backward_piece(last, 0, None, False, (down_term,))
-    down, token = row_grads(with_last(first, 0, 0), all_y, parts[0], total, (), (), 2.0)
+    held = 2 * (heights[0] + heights[1])
+    known = [[g[k] for g in grads] for k in range(3)]
+    *terms, down_term = early_terms(all_x, all_y, *known, parts[1], (near[0],))
+    *first_terms, first_down = early_terms(all_x, all_y, *known, parts[0], (down_term,))
+    first = backward_piece(last, 0, None, False, (first_down,))
+    down, token = last_rows(first[0], all_y, held, first_down, parts[0], total, (), (), 2.0)
     far = far_step(near, (token,))
-    gate, up, token = column_grads(
-        all_x, with_last(first, 1, 0), with_last(first, 2, 0), parts[0], total, (), (far[0], token)
+    gate, up, token = last_columns(
+        all_x, held, first[1], first[2], first_terms, parts[0], total, (), (far[0], token), 0.1
     )
     finished = end_step(far)
     second = backward_piece(last, 1, first[3], True, (token, finished))
     near = near_step(second)
-    held = 2 * (heights[0] + heights[1])
     gate, up, token = last_columns(
         all_x, held, second[1], second[2], terms, parts[1], total, (gate, up), (near[0],), 5.0
     )

time: 130 us -> 131 us (level)
    pallas_call x29 -> x30, Pallas kernels: 37.4 us -> 40.9 us  [local(): pl.pallas_call(body, out_shape=shapes, in_specs=[VMEM] * len(args) + [ANY...]
    ppermute x13, waiting for transfers between devices: 18.3 us -> 15.1 us  [shifted(): return lax.ppermute(value, axis, [(i, (i + step) % n) for i in range(n)])]
    ppermute x12, waiting for transfers between devices: 24.9 us -> 28.1 us  [swapped(): return lax.ppermute(value, axis, [(i, i ^ bit) for i in range(n)])]
    pallas_call x4, Pallas kernels: 17.1 us -> 14.3 us  [gradients(): pl.pallas_call(body, grid=grid, out_shape=[jax.ShapeDtypeStruct(shape, jn...]
  transfers between devices with their start and end apart: 25 -> 25, of which waited for: 14 -> 15; matrix products, arithmetic and copies ran while one was open for 0% -> 0% of each run, Pallas kernels for 39% -> 39%
where the time goes in v14:
time: 131 us
  Pallas kernels  55.2 us (42%)
  waiting for transfers between devices  43.2 us (33%)
  starting transfers between devices  30.8 us (24%)
    pallas_call x30, Pallas kernels, local(): pl.pallas_call(body, out_shape=shapes, in_specs=[VMEM] * len(args) + [ANY...  40.9 us
    ppermute x12, waiting for transfers between devices, swapped(): return lax.ppermute(value, axis, [(i, i ^ bit) for i in range(n)])  28.1 us
    ppermute x12, starting transfers between devices, swapped(): return lax.ppermute(value, axis, [(i, i ^ bit) for i in range(n)])  21.1 us
    ppermute x13, waiting for transfers between devices, shifted(): return lax.ppermute(value, axis, [(i, (i + step) % n) for i in range(n)])  15.1 us
    pallas_call x4, Pallas kernels, gradients(): pl.pallas_call(body, grid=grid, out_shape=[jax.ShapeDtypeStruct(shape, jn...  14.3 us
    ppermute x13, starting transfers between devices, shifted(): return lax.ppermute(value, axis, [(i, (i + step) % n) for i in range(n)])  9.74 us
  transfers between devices with their start and end apart: 25, of which 15 were waited for; matrix products, arithmetic and copies ran while one was open for 0% of the time, Pallas kernels for 39%

profile of v14, /device:TPU:0, one launch (start us, length us, event | category | flops | bytes accessed | tf_op | source)
XLA Modules:
  0.0 131.2 jit_solution(17919072888253473570)
XLA Ops:
  0.6 0.9 copy-done.4
  1.6 4.1 %collective-permute-start.5 = (bf16[64,512]{1,0:T(8,128)(2,1)S(1)}, bf16[64,512]{1,0:T(8,128)(2,1)S(1)}, u32[]{:S(2)}, u32[]{:S(2)}) collective-permute-start(bf16[64,512]{1,0:T(8,128)(2,1)S(1)} %shard_map.91.refs_0_), channel_id=1, source_target_pairs={{0,8},{4,12},{8,0},{12,4},{1,9},{5,13},{9,1},{13,5},{2,10},{6,14},... | collective-permute-start | bytes 196616 | tf_op jit(solution)/shard_map/ppermute | solution.py:46
  5.7 3.6 %collective-permute-done.5.refs_1_ = bf16[64,512]{1,0:T(8,128)(2,1)S(1)} collective-permute-done((bf16[64,512]{1,0:T(8,128)(2,1)S(1)}, bf16[64,512]{1,0:T(8,128)(2,1)S(1)}, u32[]{:S(2)}, u32[]{:S(2)}) %collective-permute-start.5) | collective-permute-done | bytes 65568 | tf_op jit(solution)/shard_map/ppermute | solution.py:46
  9.3 0.6 collective-permute-start.6
  10.0 3.4 %collective-permute-start = (bf16[64,512]{1,0:T(8,128)(2,1)S(1)}, bf16[64,512]{1,0:T(8,128)(2,1)S(1)}, u32[]{:S(2)}, u32[]{:S(2)}) collective-permute-start(bf16[64,512]{1,0:T(8,128)(2,1)S(1)} %shard_map.84.refs_0_), channel_id=1, source_target_pairs={{0,8},{4,12},{8,0},{12,4},{1,9},{5,13},{9,1},{13,5},{2,10},{6,14},... | collective-permute-start | bytes 196616 | tf_op jit(solution)/shard_map/ppermute | solution.py:46
  13.4 1.7 %collective-permute-done.6.refs_1_ = bf16[64,1024]{1,0:T(8,128)(2,1)S(1)} collective-permute-done((bf16[64,1024]{1,0:T(8,128)(2,1)S(1)}, bf16[64,1024]{1,0:T(8,128)(2,1)S(1)}, u32[]{:S(2)}, u32[]{:S(2)}) %collective-permute-start.6) | collective-permute-done | bytes 131104 | tf_op jit(solution)/shard_map/ppermute | solution.py:46
  15.2 1.1 collective-permute-done.refs_1_
  16.3 1.9 %collective-permute-start.1 = (bf16[64,1024]{1,0:T(8,128)(2,1)S(1)}, bf16[64,1024]{1,0:T(8,128)(2,1)S(1)}, u32[]{:S(2)}, u32[]{:S(2)}) collective-permute-start(bf16[64,1024]{1,0:T(8,128)(2,1)S(1)} %shard_map.85.refs_0_), channel_id=1, source_target_pairs={{0,4},{4,0},{8,12},{12,8},{1,5},{5,1},{9,13},{13,9},{2,6},{6,2},{1... | collective-permute-start | bytes 393224 | tf_op jit(solution)/shard_map/ppermute | solution.py:46
  18.2 2.1 %shard_map.94.refs_3_.refs_0_ = bf16[256,1792]{1,0:T(8,128)(2,1)S(1)} custom-call(bf16[64,2048]{1,0:T(8,128)(2,1)S(1)} %shard_map.93.refs_0_.refs_2_, bf16[64,2048]{1,0:T(8,128)(2,1)S(1)} %collective-permute-done.7.refs_1_.refs_3_, bf16[64,2048]{1,0:T(8,128)(2,1)S(1)} %shard_map.93.refs_0_.refs_2_, ...), custom_call_target="tpu_custom_call" | custom-call | flops 345000000 | tf_op jit(solution)/shard_map/pallas_call | solution.py:101
  20.3 1.6 %collective-permute-start.9 = (bf16[256,1792]{1,0:T(8,128)(2,1)S(1)}, bf16[256,1792]{1,0:T(8,128)(2,1)S(1)}, u32[]{:S(2)}, u32[]{:S(2)}) collective-permute-start(bf16[256,1792]{1,0:T(8,128)(2,1)S(1)} %shard_map.94.refs_3_.refs_0_), channel_id=1, source_target_pairs={{0,2},{2,0},{1,3},{3,1},{4,6},{6,4},{5,7},{7,5},{8,10},{10,8},{9,1... | collective-permute-start | bytes 2752520 | tf_op jit(solution)/shard_map/ppermute | solution.py:41
  22.0 2.4 %collective-permute-start.2 = (bf16[128,512]{1,0:T(8,128)(2,1)S(1)}, bf16[128,512]{1,0:T(8,128)(2,1)S(1)}, u32[]{:S(2)}, u32[]{:S(2)}) collective-permute-start(bf16[128,512]{1,0:T(8,128)(2,1)S(1)} %shard_map.87.refs_0_), channel_id=1, source_target_pairs={{0,8},{4,12},{8,0},{12,4},{1,9},{5,13},{9,1},{13,5},{2,10},{6,14},... | collective-permute-start | bytes 393224 | tf_op jit(solution)/shard_map/ppermute | solution.py:46
  24.4 7.3 %collective-permute-done.2.refs_1_ = bf16[128,512]{1,0:T(8,128)(2,1)S(1)} collective-permute-done((bf16[128,512]{1,0:T(8,128)(2,1)S(1)}, bf16[128,512]{1,0:T(8,128)(2,1)S(1)}, u32[]{:S(2)}, u32[]{:S(2)}) %collective-permute-start.2) | collective-permute-done | bytes 131104 | tf_op jit(solution)/shard_map/ppermute | solution.py:46
  31.7 0.5 collective-permute-start.3
  32.2 2.5 %shard_map.95.refs_9_.refs_1_ = bf16[128,1792]{1,0:T(8,128)(2,1)S(1)} custom-call(bf16[64,2048]{1,0:T(8,128)(2,1)S(1)} %shard_map.86.refs_2_.refs_0_, bf16[64,2048]{1,0:T(8,128)(2,1)S(1)} %collective-permute-done.8.refs_1_, bf16[1792,2048]{1,0:T(8,128)(2,1)S(1)} %bitcast.1, bf16[256,1792]{1,0:T(8,128)(2,1)S(1)} %shard_map.94.refs_3_.refs_0_), custom_call_target="tpu_custom_call" | custom-call | flops 345000000 | tf_op jit(solution)/shard_map/pallas_call | solution.py:101
  34.7 1.6 %collective-permute-start.10 = (bf16[128,1792]{1,0:T(8,128)(2,1)S(1)}, bf16[128,1792]{1,0:T(8,128)(2,1)S(1)}, u32[]{:S(2)}, u32[]{:S(2)}) collective-permute-start(bf16[128,1792]{1,0:T(8,128)(2,1)S(1)} %shard_map.95.refs_9_.refs_1_), channel_id=1, source_target_pairs={{0,2},{2,0},{1,3},{3,1},{4,6},{6,4},{5,7},{7,5},{8,10},{10,8},{9,1... | collective-permute-start | bytes 1376264 | tf_op jit(solution)/shard_map/ppermute | solution.py:41
  36.3 3.4 %collective-permute-done.3.refs_1_ = bf16[128,1024]{1,0:T(8,128)(2,1)S(1)} collective-permute-done((bf16[128,1024]{1,0:T(8,128)(2,1)S(1)}, bf16[128,1024]{1,0:T(8,128)(2,1)S(1)}, u32[]{:S(2)}, u32[]{:S(2)}) %collective-permute-start.3) | collective-permute-done | bytes 262176 | tf_op jit(solution)/shard_map/ppermute | solution.py:46
  39.8 0.5 collective-permute-start.11
  40.3 2.5 %collective-permute-start.4 = (bf16[128,512]{1,0:T(8,128)(2,1)S(1)}, bf16[128,512]{1,0:T(8,128)(2,1)S(1)}, u32[]{:S(2)}, u32[]{:S(2)}) collective-permute-start(bf16[128,512]{1,0:T(8,128)(2,1)S(1)} %shard_map.90.refs_0_), channel_id=1, source_target_pairs={{0,8},{4,12},{8,0},{12,4},{1,9},{5,13},{9,1},{13,5},{2,10},{6,14},... | collective-permute-start | bytes 393224 | tf_op jit(solution)/shard_map/ppermute | solution.py:46
  42.8 4.4 %shard_map.96.refs_6_.refs_0_ = bf16[384,1792]{1,0:T(8,128)(2,1)S(1)} custom-call(bf16[64,2048]{1,0:T(8,128)(2,1)S(1)} %get-tuple-element.50.refs_2_.refs_0_, bf16[64,2048]{1,0:T(8,128)(2,1)S(1)} %collective-permute-done.11.refs_1_.refs_3_, bf16[64,2048]{1,0:T(8,128)(2,1)S(1)} %get-tuple-element.50.refs_2_.refs_0_, ...), custom_call_target="tpu_custom_call" | custom-call | flops 345000000 | tf_op jit(solution)/shard_map/pallas_call | solution.py:101
  47.2 1.6 %collective-permute-start.18 = (bf16[384,1792]{1,0:T(8,128)(2,1)S(1)}, bf16[384,1792]{1,0:T(8,128)(2,1)S(1)}, u32[]{:S(2)}, u32[]{:S(2)}) collective-permute-start(bf16[384,1792]{1,0:T(8,128)(2,1)S(1)} %shard_map.96.refs_6_.refs_0_), channel_id=1, source_target_pairs={{0,2},{2,0},{1,3},{3,1},{4,6},{6,4},{5,7},{7,5},{8,10},{10,8},{9,1... | collective-permute-start | bytes 4128776 | tf_op jit(solution)/shard_map/ppermute | solution.py:41
  48.8 4.4 %collective-permute-done.10.refs_3_ = bf16[128,1792]{1,0:T(8,128)(2,1)S(1)} collective-permute-done((bf16[128,1792]{1,0:T(8,128)(2,1)S(1)}, bf16[128,1792]{1,0:T(8,128)(2,1)S(1)}, u32[]{:S(2)}, u32[]{:S(2)}) %collective-permute-start.10) | collective-permute-done | bytes 458784 | tf_op jit(solution)/shard_map/ppermute | solution.py:41
  53.2 5.8 %shard_map.97 = (bf16[1792,128]{1,0:T(8,128)(2,1)S(1)}, bf16[128,1792]{1,0:T(8,128)(2,1)S(1)}, bf16[128,1792]{1,0:T(8,128)(2,1)S(1)}, f32[64,2048]{1,0:T(8,128)S(1)}, bf16[64,2048]{1,0:T(8,128)(2,1)S(1)}) custom-call(bf16[256,1792]{1,0:T(8,128)(2,1)S(1)} %shard_map.94.refs_3_.refs_0_, bf16[128,1792]{1,0:T(8,128)(2,1)S(1)} %shard_map.95.refs_9_.refs_1_, ...), custom_call_target="tpu_custom_call" | custom-call | flops 69000003584 | tf_op jit(solution)/shard_map/pallas_call | solution.py:101
  59.1 6.4 %collective-permute-done.13.refs_1_ = bf16[128,1024]{1,0:T(8,128)(2,1)S(1)} collective-permute-done((bf16[128,1024]{1,0:T(8,128)(2,1)S(1)}, bf16[128,1024]{1,0:T(8,128)(2,1)S(1)}, u32[]{:S(2)}, u32[]{:S(2)}) %collective-permute-start.13) | collective-permute-done | bytes 262176 | tf_op jit(solution)/shard_map/ppermute | solution.py:46
  65.6 0.5 collective-permute-start.15
  66.1 1.0 collective-permute-done.14.refs_1_.refs_3_.refs_5_
  67.2 0.4 collective-permute-done.15.refs_5_
  67.5 2.4 %shard_map.100.refs_9_.refs_0_ = bf16[384,896]{1,0:T(8,128)(2,1)S(1)} custom-call(bf16[64,2048]{1,0:T(8,128)(2,1)S(1)} %get-tuple-element.53.refs_0_.refs_2_.refs_4_, bf16[64,2048]{1,0:T(8,128)(2,1)S(1)} %collective-permute-done.14.refs_1_.refs_3_.refs_5_, bf16[64,2048]{1,0:T(8,128)(2,1)S(1)} %get-tuple-element.53.refs_0_.refs_2_.refs_4_, ...), custom_call_target="tpu_custom_call" | custom-call | flops 345000000 | tf_op jit(solution)/shard_map/pallas_call | solution.py:101
  69.9 1.8 %collective-permute-start.17 = (bf16[384,896]{1,0:T(8,128)(2,1)S(1)}, bf16[384,896]{1,0:T(8,128)(2,1)S(1)}, u32[]{:S(2)}, u32[]{:S(2)}) collective-permute-start(bf16[384,896]{1,0:T(8,128)(2,1)S(1)} %shard_map.100.refs_9_.refs_0_), channel_id=1, source_target_pairs={{0,2},{2,0},{1,3},{3,1},{4,6},{6,4},{5,7},{7,5},{8,10},{10,8},{9,1... | collective-permute-start | bytes 2064392 | tf_op jit(solution)/shard_map/ppermute | solution.py:41
  71.8 2.4 %shard_map.101.refs_6_.refs_0_ = bf16[384,896]{1,0:T(8,128)(2,1)S(1)} custom-call(bf16[64,2048]{1,0:T(8,128)(2,1)S(1)} %get-tuple-element.53.refs_0_.refs_2_.refs_4_, bf16[64,2048]{1,0:T(8,128)(2,1)S(1)} %collective-permute-done.14.refs_1_.refs_3_.refs_5_, bf16[64,2048]{1,0:T(8,128)(2,1)S(1)} %get-tuple-element.53.refs_0_.refs_2_.refs_4_, ...), custom_call_target="tpu_custom_call" | custom-call | flops 345000000 | tf_op jit(solution)/shard_map/pallas_call | solution.py:101
  74.3 0.6 shard_map.102.refs_6_.refs_0_
  75.0 7.7 %collective-permute-done.18.refs_1_ = bf16[384,1792]{1,0:T(8,128)(2,1)S(1)} collective-permute-done((bf16[384,1792]{1,0:T(8,128)(2,1)S(1)}, bf16[384,1792]{1,0:T(8,128)(2,1)S(1)}, u32[]{:S(2)}, u32[]{:S(2)}) %collective-permute-start.18) | collective-permute-done | bytes 1376288 | tf_op jit(solution)/shard_map/ppermute | solution.py:41
  82.7 6.1 %shard_map.104 = (bf16[1792,128]{1,0:T(8,128)(2,1)S(1)}, bf16[128,1792]{1,0:T(8,128)(2,1)S(1)}, bf16[128,1792]{1,0:T(8,128)(2,1)S(1)}, f32[128,2048]{1,0:T(8,128)S(1)}, bf16[128,2048]{1,0:T(8,128)(2,1)S(1)}) custom-call(bf16[384,1792]{1,0:T(8,128)(2,1)S(1)} %shard_map.96.refs_6_.refs_0_, bf16[384,1792]{1,0:T(8,128)(2,1)S(1)} %collective-permute-done.18.refs_1_, ...), custom_call_target="tpu_custom_call" | custom-call | flops 69000003584 | tf_op jit(solution)/shard_map/pallas_call | solution.py:101
  88.8 1.8 %collective-permute-start.16 = (bf16[384,896]{1,0:T(8,128)(2,1)S(1)}, bf16[384,896]{1,0:T(8,128)(2,1)S(1)}, u32[]{:S(2)}, u32[]{:S(2)}) collective-permute-start(bf16[384,896]{1,0:T(8,128)(2,1)S(1)} %shard_map.101.refs_6_.refs_0_), channel_id=1, source_target_pairs={{0,2},{2,0},{1,3},{3,1},{4,6},{6,4},{5,7},{7,5},{8,10},{10,8},{9,1... | collective-permute-start | bytes 2064392 | tf_op jit(solution)/shard_map/ppermute | solution.py:41
  90.9 3.3 %shard_map.106 = (bf16[2048,896]{1,0:T(8,128)(2,1)S(1)}, bf16[2048,896]{1,0:T(8,128)(2,1)S(1)}, bf16[896,2048]{1,0:T(8,128)(2,1)S(1)}) custom-call(bf16[2048,384]{1,0:T(8,128)(2,1)S(1)} %shard_map.102.refs_6_.refs_0_, bf16[384,2048]{1,0:T(8,128)(2,1)S(1)} %shard_map.103.refs_7_.refs_1_, bf16[1792,128]{1,0:T(8,128)(2,1)S(1)} %get-tuple-element.55.refs_2_, ...), custom_call_target="tpu_custom_call" | custom-call | flops 115000000 | tf_op jit(solution)/shard_map/pallas_call | solution.py:101
  94.3 3.3 %shard_map.107 = (bf16[2048,896]{1,0:T(8,128)(2,1)S(1)}, bf16[2048,896]{1,0:T(8,128)(2,1)S(1)}, bf16[896,2048]{1,0:T(8,128)(2,1)S(1)}) custom-call(bf16[2048,384]{1,0:T(8,128)(2,1)S(1)} %shard_map.102.refs_6_.refs_0_, bf16[384,2048]{1,0:T(8,128)(2,1)S(1)} %shard_map.103.refs_7_.refs_1_, bf16[1792,128]{1,0:T(8,128)(2,1)S(1)} %get-tuple-element.55.refs_2_, ...), custom_call_target="tpu_custom_call" | custom-call | flops 115000000 | tf_op jit(solution)/shard_map/pallas_call | solution.py:101
  97.6 3.2 %shard_map.108 = (bf16[896,128]{1,0:T(8,128)(2,1)S(1)}, bf16[128,896]{1,0:T(8,128)(2,1)S(1)}, bf16[128,896]{1,0:T(8,128)(2,1)S(1)}, f32[128,2048]{1,0:T(8,128)S(1)}) custom-call(bf16[384,896]{1,0:T(8,128)(2,1)S(1)} %shard_map.100.refs_9_.refs_0_, bf16[384,896]{1,0:T(8,128)(2,1)S(1)} %collective-permute-done.17.refs_1_, bf16[2048,1792]{1,0:T(8,128)(2,1)S(1)} %copy-done, ...), custom_call_target="tpu_custom_call" | custom-call | flops 115000000 | tf_op jit(solution)/shard_map/pallas_call | solution.py:101
  100.8 3.1 %shard_map.109 = (bf16[1792,2048]{1,0:T(8,128)(2,1)}, bf16[16,128]{1,0:T(8,128)(2,1)S(1)}) custom-call(bf16[896,128]{1,0:T(8,128)(2,1)S(1)} %get-tuple-element.73.refs_0_, bf16[384,2048]{1,0:T(8,128)(2,1)S(1)} %shard_map.103.refs_7_.refs_1_, bf16[896,2048]{1,0:T(8,128)(2,1)S(1)} %get-tuple-element.66.refs_4_.refs_2_), custom_call_target="tpu_custom_call" | custom-call | flops 2300000000 | tf_op jit(solution)/shard_map/pallas_call | solution.py:323
  103.9 3.5 %collective-permute-start.21 = (bf16[128,512]{1,0:T(8,128)(2,1)S(1)}, bf16[128,512]{1,0:T(8,128)(2,1)S(1)}, u32[]{:S(2)}, u32[]{:S(2)}) collective-permute-start(bf16[128,512]{1,0:T(8,128)(2,1)S(1)} %get-tuple-element.77), channel_id=1, source_target_pairs={{0,8},{4,12},{8,0},{12,4},{1,9},{5,13},{9,1},{13,5},{2,10},{6,14},... | collective-permute-start | bytes 393224 | tf_op jit(solution)/shard_map/ppermute | solution.py:46
  107.5 4.1 %shard_map.111 = (bf16[2048,1792]{1,0:T(8,128)(2,1)}, bf16[2048,1792]{1,0:T(8,128)(2,1)}, bf16[16,128]{1,0:T(8,128)(2,1)S(1)}) custom-call(bf16[2048,384]{1,0:T(8,128)(2,1)S(1)} %shard_map.102.refs_6_.refs_0_, bf16[128,896]{1,0:T(8,128)(2,1)S(1)} %get-tuple-element.68.refs_1_, bf16[128,896]{1,0:T(8,128)(2,1)S(1)} %get-tuple-element.69.refs_2_, ...), custom_call_target="tpu_custom_call" | custom-call | flops 115000000 | tf_op jit(solution)/shard_map/pallas_call | solution.py:323
  111.5 2.2 %collective-permute-done.21.refs_1_ = bf16[128,512]{1,0:T(8,128)(2,1)S(1)} collective-permute-done((bf16[128,512]{1,0:T(8,128)(2,1)S(1)}, bf16[128,512]{1,0:T(8,128)(2,1)S(1)}, u32[]{:S(2)}, u32[]{:S(2)}) %collective-permute-start.21) | collective-permute-done | bytes 131104 | tf_op jit(solution)/shard_map/ppermute | solution.py:46
  113.8 3.4 %shard_map.113 = (bf16[896,128]{1,0:T(8,128)(2,1)S(1)}, bf16[128,896]{1,0:T(8,128)(2,1)S(1)}, bf16[128,896]{1,0:T(8,128)(2,1)S(1)}, f32[64,2048]{1,0:T(8,128)S(1)}, bf16[64,2048]{1,0:T(8,128)(2,1)S(1)}) custom-call(bf16[384,896]{1,0:T(8,128)(2,1)S(1)} %shard_map.101.refs_6_.refs_0_, bf16[384,896]{1,0:T(8,128)(2,1)S(1)} %collective-permute-done.16.refs_1_, ...), custom_call_target="tpu_custom_call" | custom-call | flops 115000000 | tf_op jit(solution)/shard_map/pallas_call | solution.py:101
  117.4 1.5 %collective-permute-done.22.refs_1_ = bf16[64,2048]{1,0:T(8,128)(2,1)S(1)} collective-permute-done((bf16[64,2048]{1,0:T(8,128)(2,1)S(1)}, bf16[64,2048]{1,0:T(8,128)(2,1)S(1)}, u32[]{:S(2)}, u32[]{:S(2)}) %collective-permute-start.22) | collective-permute-done | bytes 262176 | tf_op jit(solution)/shard_map/ppermute | solution.py:41
  119.0 4.1 %shard_map.115 = (bf16[2048,1792]{1,0:T(8,128)(2,1)}, bf16[2048,1792]{1,0:T(8,128)(2,1)}, bf16[16,128]{1,0:T(8,128)(2,1)S(1)}) custom-call(bf16[2048,384]{1,0:T(8,128)(2,1)S(1)} %shard_map.102.refs_6_.refs_0_, bf16[128,896]{1,0:T(8,128)(2,1)S(1)} %get-tuple-element.82.refs_1_, ...), custom_call_target="tpu_custom_call", output_to_operand_aliasing={{0}: (5, {}), {1}: (6, {})} | custom-call | flops 5750000128 | tf_op jit(solution)/shard_map/pallas_call | solution.py:323
  123.1 1.4 %collective-permute-done.23.refs_1_ = bf16[64,1024]{1,0:T(8,128)(2,1)S(1)} collective-permute-done((bf16[64,1024]{1,0:T(8,128)(2,1)S(1)}, bf16[64,1024]{1,0:T(8,128)(2,1)S(1)}, u32[]{:S(2)}, u32[]{:S(2)}) %collective-permute-start.23) | collective-permute-done | bytes 131104 | tf_op jit(solution)/shard_map/ppermute | solution.py:46
  124.6 1.9 %collective-permute-start.24 = (bf16[64,512]{1,0:T(8,128)(2,1)S(1)}, bf16[64,512]{1,0:T(8,128)(2,1)S(1)}, u32[]{:S(2)}, u32[]{:S(2)}) collective-permute-start(bf16[64,512]{1,0:T(8,128)(2,1)S(1)} %get-tuple-element.90), channel_id=1, source_target_pairs={{0,8},{4,12},{8,0},{12,4},{1,9},{5,13},{9,1},{13,5},{2,10},{6,14},... | collective-permute-start | bytes 196616 | tf_op jit(solution)/shard_map/ppermute | solution.py:46
  126.4 3.0 %shard_map.118 = (bf16[1792,2048]{1,0:T(8,128)(2,1)}, bf16[16,128]{1,0:T(8,128)(2,1)}) custom-call(bf16[896,128]{1,0:T(8,128)(2,1)S(1)} %get-tuple-element.93.refs_0_, bf16[384,2048]{1,0:T(8,128)(2,1)S(1)} %shard_map.103.refs_7_.refs_1_, bf16[896,2048]{1,0:T(8,128)(2,1)S(1)} %get-tuple-element.65.refs_8_.refs_2_, ...), custom_call_target="tpu_custom_call", output_to_operand_aliasing={{0}: (3, {})} | custom-call | flops 3449999872 | tf_op jit(solution)/shard_map/pallas_call | solution.py:323
  129.5 1.0 collective-permute-done.24.refs_1_
  130.5 0.7 shard_map.117
  (56 shorter events, 1.4 us)
Async XLA Ops:
  0.6 0.9 copy-start.4
  1.6 8.4 %copy-start.5 = (bf16[192,512]{1,0:T(8,128)(2,1)S(1)}, bf16[192,512]{1,0:T(8,128)(2,1)}, u32[]{:S(2)}) copy-start(bf16[192,512]{1,0:T(8,128)(2,1)} %source.1) | copy-start | bytes 589828
  1.6 8.4 %copy-start.6 = (bf16[192,512]{1,0:T(8,128)(2,1)S(1)}, bf16[192,512]{1,0:T(8,128)(2,1)}, u32[]{:S(2)}) copy-start(bf16[192,512]{1,0:T(8,128)(2,1)} %refs_1_.5) | copy-start | bytes 589828
  1.6 16.6 %copy-start = (bf16[2048,1792]{1,0:T(8,128)(2,1)S(1)}, bf16[2048,1792]{1,0:T(8,128)(2,1)}, u32[]{:S(2)}) copy-start(bf16[2048,1792]{1,0:T(8,128)(2,1)} %refs_2_.7) | copy-start | bytes 22020100
  1.6 16.6 %copy-start.1 = (bf16[2048,1792]{1,0:T(8,128)(2,1)S(1)}, bf16[2048,1792]{1,0:T(8,128)(2,1)}, u32[]{:S(2)}) copy-start(bf16[2048,1792]{1,0:T(8,128)(2,1)} %refs_3_.5) | copy-start | bytes 22020100
  1.6 7.8 %collective-permute-start.5 = (bf16[64,512]{1,0:T(8,128)(2,1)S(1)}, bf16[64,512]{1,0:T(8,128)(2,1)S(1)}, u32[]{:S(2)}, u32[]{:S(2)}) collective-permute-start(bf16[64,512]{1,0:T(8,128)(2,1)S(1)} %shard_map.91.refs_0_), channel_id=1, source_target_pairs={{0,8},{4,12},{8,0},{12,4},{1,9},{5,13},{9,1},{13,5},{2,10},{6,14},... | collective-permute-start | bytes 196616 | tf_op jit(solution)/shard_map/ppermute | solution.py:46
  9.3 5.7 %collective-permute-start.6 = (bf16[64,1024]{1,0:T(8,128)(2,1)S(1)}, bf16[64,1024]{1,0:T(8,128)(2,1)S(1)}, u32[]{:S(2)}, u32[]{:S(2)}) collective-permute-start(bf16[64,1024]{1,0:T(8,128)(2,1)S(1)} %shard_map.92.refs_0_), channel_id=1, source_target_pairs={{0,4},{4,0},{8,12},{12,8},{1,5},{5,1},{9,13},{13,9},{2,6},{6,2},{1... | collective-permute-start | bytes 393224 | tf_op jit(solution)/shard_map/ppermute | solution.py:46
  10.0 6.3 %collective-permute-start = (bf16[64,512]{1,0:T(8,128)(2,1)S(1)}, bf16[64,512]{1,0:T(8,128)(2,1)S(1)}, u32[]{:S(2)}, u32[]{:S(2)}) collective-permute-start(bf16[64,512]{1,0:T(8,128)(2,1)S(1)} %shard_map.84.refs_0_), channel_id=1, source_target_pairs={{0,8},{4,12},{8,0},{12,4},{1,9},{5,13},{9,1},{13,5},{2,10},{6,14},... | collective-permute-start | bytes 196616 | tf_op jit(solution)/shard_map/ppermute | solution.py:46
  15.1 3.0 %collective-permute-start.7 = (bf16[64,2048]{1,0:T(8,128)(2,1)S(1)}, bf16[64,2048]{1,0:T(8,128)(2,1)S(1)}, u32[]{:S(2)}, u32[]{:S(2)}) collective-permute-start(bf16[64,2048]{1,0:T(8,128)(2,1)S(1)} %shard_map.93.refs_0_.refs_2_), channel_id=1, source_target_pairs={{0,1},{1,0},{2,3},{3,2},{4,5},{5,4},{6,7},{7,6},{8,9},{9,8},{10,11... | collective-permute-start | bytes 786440 | tf_op jit(solution)/shard_map/ppermute | solution.py:41
  16.3 5.6 %collective-permute-start.1 = (bf16[64,1024]{1,0:T(8,128)(2,1)S(1)}, bf16[64,1024]{1,0:T(8,128)(2,1)S(1)}, u32[]{:S(2)}, u32[]{:S(2)}) collective-permute-start(bf16[64,1024]{1,0:T(8,128)(2,1)S(1)} %shard_map.85.refs_0_), channel_id=1, source_target_pairs={{0,4},{4,0},{8,12},{12,8},{1,5},{5,1},{9,13},{13,9},{2,6},{6,2},{1... | collective-permute-start | bytes 393224 | tf_op jit(solution)/shard_map/ppermute | solution.py:46
  18.2 14.0 %slice-start = ((s8[7340032]{0:T(1024)(128)(4,1)}), s8[4194304]{0:T(1024)(128)(4,1)S(1)}, s32[]{:S(2)}) async-start(s8[7340032]{0:T(1024)(128)(4,1)} %bitcast), calls=%async_computation | async-start | bytes 8388608
  20.3 11.9 %slice-start.1 = ((s8[7340032]{0:T(1024)(128)(4,1)}), s8[3145728]{0:T(1024)(128)(4,1)S(1)}, s32[]{:S(2)}) async-start(s8[7340032]{0:T(1024)(128)(4,1)} %bitcast), calls=%async_computation.1 | async-start | bytes 6291456
  20.3 32.9 %collective-permute-start.9 = (bf16[256,1792]{1,0:T(8,128)(2,1)S(1)}, bf16[256,1792]{1,0:T(8,128)(2,1)S(1)}, u32[]{:S(2)}, u32[]{:S(2)}) collective-permute-start(bf16[256,1792]{1,0:T(8,128)(2,1)S(1)} %shard_map.94.refs_3_.refs_0_), channel_id=1, source_target_pairs={{0,2},{2,0},{1,3},{3,1},{4,6},{6,4},{5,7},{7,5},{8,10},{10,8},{9,1... | collective-permute-start | bytes 2752520 | tf_op jit(solution)/shard_map/ppermute | solution.py:41
  21.9 10.3 %collective-permute-start.8 = (bf16[64,2048]{1,0:T(8,128)(2,1)S(1)}, bf16[64,2048]{1,0:T(8,128)(2,1)S(1)}, u32[]{:S(2)}, u32[]{:S(2)}) collective-permute-start(bf16[64,2048]{1,0:T(8,128)(2,1)S(1)} %shard_map.86.refs_2_.refs_0_), channel_id=1, source_target_pairs={{0,1},{1,0},{2,3},{3,2},{4,5},{5,4},{6,7},{7,6},{8,9},{9,8},{10,11... | collective-permute-start | bytes 786440 | tf_op jit(solution)/shard_map/ppermute | solution.py:41
  22.0 9.7 %collective-permute-start.2 = (bf16[128,512]{1,0:T(8,128)(2,1)S(1)}, bf16[128,512]{1,0:T(8,128)(2,1)S(1)}, u32[]{:S(2)}, u32[]{:S(2)}) collective-permute-start(bf16[128,512]{1,0:T(8,128)(2,1)S(1)} %shard_map.87.refs_0_), channel_id=1, source_target_pairs={{0,8},{4,12},{8,0},{12,4},{1,9},{5,13},{9,1},{13,5},{2,10},{6,14},... | collective-permute-start | bytes 393224 | tf_op jit(solution)/shard_map/ppermute | solution.py:46
  31.7 8.0 %collective-permute-start.3 = (bf16[128,1024]{1,0:T(8,128)(2,1)S(1)}, bf16[128,1024]{1,0:T(8,128)(2,1)S(1)}, u32[]{:S(2)}, u32[]{:S(2)}) collective-permute-start(bf16[128,1024]{1,0:T(8,128)(2,1)S(1)} %shard_map.88.refs_0_), channel_id=1, source_target_pairs={{0,4},{4,0},{8,12},{12,8},{1,5},{5,1},{9,13},{13,9},{2,6},{6,2},{1... | collective-permute-start | bytes 786440 | tf_op jit(solution)/shard_map/ppermute | solution.py:46
  34.7 18.5 %collective-permute-start.10 = (bf16[128,1792]{1,0:T(8,128)(2,1)S(1)}, bf16[128,1792]{1,0:T(8,128)(2,1)S(1)}, u32[]{:S(2)}, u32[]{:S(2)}) collective-permute-start(bf16[128,1792]{1,0:T(8,128)(2,1)S(1)} %shard_map.95.refs_9_.refs_1_), channel_id=1, source_target_pairs={{0,2},{2,0},{1,3},{3,1},{4,6},{6,4},{5,7},{7,5},{8,10},{10,8},{9,1... | collective-permute-start | bytes 1376264 | tf_op jit(solution)/shard_map/ppermute | solution.py:41
  39.7 3.1 %collective-permute-start.12 = (bf16[64,2048]{1,0:T(8,128)(2,1)S(1)}, bf16[64,2048]{1,0:T(8,128)(2,1)S(1)}, u32[]{:S(2)}, u32[]{:S(2)}) collective-permute-start(bf16[64,2048]{1,0:T(8,128)(2,1)S(1)} %get-tuple-element.51.refs_4_.refs_2_), channel_id=1, source_target_pairs={{0,1},{1,0},{2,3},{3,2},{4,5},{5,4},{6,7},{7,6},{8,9},{9,8},{10,11... | collective-permute-start | bytes 786440 | tf_op jit(solution)/shard_map/ppermute | solution.py:41
  39.8 3.0 %collective-permute-start.11 = (bf16[64,2048]{1,0:T(8,128)(2,1)S(1)}, bf16[64,2048]{1,0:T(8,128)(2,1)S(1)}, u32[]{:S(2)}, u32[]{:S(2)}) collective-permute-start(bf16[64,2048]{1,0:T(8,128)(2,1)S(1)} %get-tuple-element.50.refs_2_.refs_0_), channel_id=1, source_target_pairs={{0,1},{1,0},{2,3},{3,2},{4,5},{5,4},{6,7},{7,6},{8,9},{9,8},{10,11... | collective-permute-start | bytes 786440 | tf_op jit(solution)/shard_map/ppermute | solution.py:41
  40.3 18.7 %collective-permute-start.4 = (bf16[128,512]{1,0:T(8,128)(2,1)S(1)}, bf16[128,512]{1,0:T(8,128)(2,1)S(1)}, u32[]{:S(2)}, u32[]{:S(2)}) collective-permute-start(bf16[128,512]{1,0:T(8,128)(2,1)S(1)} %shard_map.90.refs_0_), channel_id=1, source_target_pairs={{0,8},{4,12},{8,0},{12,4},{1,9},{5,13},{9,1},{13,5},{2,10},{6,14},... | collective-permute-start | bytes 393224 | tf_op jit(solution)/shard_map/ppermute | solution.py:46
  47.2 35.5 %collective-permute-start.18 = (bf16[384,1792]{1,0:T(8,128)(2,1)S(1)}, bf16[384,1792]{1,0:T(8,128)(2,1)S(1)}, u32[]{:S(2)}, u32[]{:S(2)}) collective-permute-start(bf16[384,1792]{1,0:T(8,128)(2,1)S(1)} %shard_map.96.refs_6_.refs_0_), channel_id=1, source_target_pairs={{0,2},{2,0},{1,3},{3,1},{4,6},{6,4},{5,7},{7,5},{8,10},{10,8},{9,1... | collective-permute-start | bytes 4128776 | tf_op jit(solution)/shard_map/ppermute | solution.py:41
  59.1 6.4 %collective-permute-start.13 = (bf16[128,1024]{1,0:T(8,128)(2,1)S(1)}, bf16[128,1024]{1,0:T(8,128)(2,1)S(1)}, u32[]{:S(2)}, u32[]{:S(2)}) collective-permute-start(bf16[128,1024]{1,0:T(8,128)(2,1)S(1)} %shard_map.98.refs_0_), channel_id=1, source_target_pairs={{0,4},{4,0},{8,12},{12,8},{1,5},{5,1},{9,13},{13,9},{2,6},{6,2},{1... | collective-permute-start | bytes 786440 | tf_op jit(solution)/shard_map/ppermute | solution.py:46
  65.6 1.6 %collective-permute-start.14 = (bf16[64,2048]{1,0:T(8,128)(2,1)S(1)}, bf16[64,2048]{1,0:T(8,128)(2,1)S(1)}, u32[]{:S(2)}, u32[]{:S(2)}) collective-permute-start(bf16[64,2048]{1,0:T(8,128)(2,1)S(1)} %get-tuple-element.53.refs_0_.refs_2_.refs_4_), channel_id=1, source_target_pairs={{0,1},{1,0},{2,3},{3,2},{4,5},{5,4},{6,7},{7,6},{8,9},{9,8},{10,11... | collective-permute-start | bytes 786440 | tf_op jit(solution)/shard_map/ppermute | solution.py:41
  65.6 1.9 %collective-permute-start.15 = (bf16[64,2048]{1,0:T(8,128)(2,1)S(1)}, bf16[64,2048]{1,0:T(8,128)(2,1)S(1)}, u32[]{:S(2)}, u32[]{:S(2)}) collective-permute-start(bf16[64,2048]{1,0:T(8,128)(2,1)S(1)} %get-tuple-element.54.refs_4_), channel_id=1, source_target_pairs={{0,1},{1,0},{2,3},{3,2},{4,5},{5,4},{6,7},{7,6},{8,9},{9,8},{10,11... | collective-permute-start | bytes 786440 | tf_op jit(solution)/shard_map/ppermute | solution.py:41
  69.9 27.7 %collective-permute-start.17 = (bf16[384,896]{1,0:T(8,128)(2,1)S(1)}, bf16[384,896]{1,0:T(8,128)(2,1)S(1)}, u32[]{:S(2)}, u32[]{:S(2)}) collective-permute-start(bf16[384,896]{1,0:T(8,128)(2,1)S(1)} %shard_map.100.refs_9_.refs_0_), channel_id=1, source_target_pairs={{0,2},{2,0},{1,3},{3,1},{4,6},{6,4},{5,7},{7,5},{8,10},{10,8},{9,1... | collective-permute-start | bytes 2064392 | tf_op jit(solution)/shard_map/ppermute | solution.py:41
  88.8 2.0 %collective-permute-start.19 = (bf16[128,2048]{1,0:T(8,128)(2,1)S(1)}, bf16[128,2048]{1,0:T(8,128)(2,1)S(1)}, u32[]{:S(2)}, u32[]{:S(2)}) collective-permute-start(bf16[128,2048]{1,0:T(8,128)(2,1)S(1)} %get-tuple-element.63), channel_id=1, source_target_pairs={{0,1},{1,0},{2,3},{3,2},{4,5},{5,4},{6,7},{7,6},{8,9},{9,8},{10,11... | collective-permute-start | bytes 1572872 | tf_op jit(solution)/shard_map/ppermute | solution.py:41
  88.8 25.0 %collective-permute-start.16 = (bf16[384,896]{1,0:T(8,128)(2,1)S(1)}, bf16[384,896]{1,0:T(8,128)(2,1)S(1)}, u32[]{:S(2)}, u32[]{:S(2)}) collective-permute-start(bf16[384,896]{1,0:T(8,128)(2,1)S(1)} %shard_map.101.refs_6_.refs_0_), channel_id=1, source_target_pairs={{0,2},{2,0},{1,3},{3,1},{4,6},{6,4},{5,7},{7,5},{8,10},{10,8},{9,1... | collective-permute-start | bytes 2064392 | tf_op jit(solution)/shard_map/ppermute | solution.py:41
  90.8 13.0 %collective-permute-start.20 = (bf16[128,1024]{1,0:T(8,128)(2,1)S(1)}, bf16[128,1024]{1,0:T(8,128)(2,1)S(1)}, u32[]{:S(2)}, u32[]{:S(2)}) collective-permute-start(bf16[128,1024]{1,0:T(8,128)(2,1)S(1)} %get-tuple-element.72), channel_id=1, source_target_pairs={{0,4},{4,0},{8,12},{12,8},{1,5},{5,1},{9,13},{13,9},{2,6},{6,2},{1... | collective-permute-start | bytes 786440 | tf_op jit(solution)/shard_map/ppermute | solution.py:46
  94.3 3.3 %copy-start.2 = (bf16[2048,896]{1,0:T(8,128)(2,1)}, bf16[2048,896]{1,0:T(8,128)(2,1)S(1)}, u32[]{:S(2)}) copy-start(bf16[2048,896]{1,0:T(8,128)(2,1)S(1)} %get-tuple-element.85.refs_4_) | copy-start | bytes 11010052
  103.9 9.9 %collective-permute-start.21 = (bf16[128,512]{1,0:T(8,128)(2,1)S(1)}, bf16[128,512]{1,0:T(8,128)(2,1)S(1)}, u32[]{:S(2)}, u32[]{:S(2)}) collective-permute-start(bf16[128,512]{1,0:T(8,128)(2,1)S(1)} %get-tuple-element.77), channel_id=1, source_target_pairs={{0,8},{4,12},{8,0},{12,4},{1,9},{5,13},{9,1},{13,5},{2,10},{6,14},... | collective-permute-start | bytes 393224 | tf_op jit(solution)/shard_map/ppermute | solution.py:46
  113.8 5.2 %copy-start.3 = (bf16[2048,896]{1,0:T(8,128)(2,1)S(1)}, bf16[2048,896]{1,0:T(8,128)(2,1)}, u32[]{:S(2)}) copy-start(bf16[2048,896]{1,0:T(8,128)(2,1)} %copy-done.2) | copy-start | bytes 11010052
  117.3 1.6 %collective-permute-start.22 = (bf16[64,2048]{1,0:T(8,128)(2,1)S(1)}, bf16[64,2048]{1,0:T(8,128)(2,1)S(1)}, u32[]{:S(2)}, u32[]{:S(2)}) collective-permute-start(bf16[64,2048]{1,0:T(8,128)(2,1)S(1)} %get-tuple-element.79), channel_id=1, source_target_pairs={{0,1},{1,0},{2,3},{3,2},{4,5},{5,4},{6,7},{7,6},{8,9},{9,8},{10,11... | collective-permute-start | bytes 786440 | tf_op jit(solution)/shard_map/ppermute | solution.py:41
  118.9 5.6 %collective-permute-start.23 = (bf16[64,1024]{1,0:T(8,128)(2,1)S(1)}, bf16[64,1024]{1,0:T(8,128)(2,1)S(1)}, u32[]{:S(2)}, u32[]{:S(2)}) collective-permute-start(bf16[64,1024]{1,0:T(8,128)(2,1)S(1)} %get-tuple-element.81), channel_id=1, source_target_pairs={{0,4},{4,0},{8,12},{12,8},{1,5},{5,1},{9,13},{13,9},{2,6},{6,2},{1... | collective-permute-start | bytes 393224 | tf_op jit(solution)/shard_map/ppermute | solution.py:46
  124.6 5.9 %collective-permute-start.24 = (bf16[64,512]{1,0:T(8,128)(2,1)S(1)}, bf16[64,512]{1,0:T(8,128)(2,1)S(1)}, u32[]{:S(2)}, u32[]{:S(2)}) collective-permute-start(bf16[64,512]{1,0:T(8,128)(2,1)S(1)} %get-tuple-element.90), channel_id=1, source_target_pairs={{0,8},{4,12},{8,0},{12,4},{1,9},{5,13},{9,1},{13,5},{2,10},{6,14},... | collective-permute-start | bytes 196616 | tf_op jit(solution)/shard_map/ppermute | solution.py:46

commit v15 on v14

--- a/solution.py
+++ b/solution.py
@@ -459,7 +459,7 @@
         own, where = sums[index][part]
         span = parts[part] if index == last else whole
         other = [shifted(value, "wid", 1) for value in own]
-        cost = 0.1 if index == last else 60.0
+        cost = 2.0 if index == last else 60.0
         return backward(own, other, where, back_weights, span, heights[index], before, final, after, cost, above)
 
     def near_step(results):
@@ -487,10 +487,10 @@
     *terms, down_term = early_terms(all_x, all_y, *known, parts[1], (near[0],))
     *first_terms, first_down = early_terms(all_x, all_y, *known, parts[0], (down_term,))
     first = backward_piece(last, 0, None, False, (first_down,))
-    down, token = last_rows(first[0], all_y, held, first_down, parts[0], total, (), (), 2.0)
-    far = far_step(near, (token,))
+    far = far_step(near, (first[1],))
+    down, token = last_rows(first[0], all_y, held, first_down, parts[0], total, (), (far[0],), 2.0)
     gate, up, token = last_columns(
-        all_x, held, first[1], first[2], first_terms, parts[0], total, (), (far[0], token), 0.1
+        all_x, held, first[1], first[2], first_terms, parts[0], total, (), (token,), 0.1
     )
     finished = end_step(far)
     second = backward_piece(last, 1, first[3], True, (token, finished))

time: 131 us -> 129 us (0.985)
  waiting for transfers between devices: 43.2 us -> 40.3 us
    ppermute x12, waiting for transfers between devices: 28.1 us -> 25.2 us  [swapped(): return lax.ppermute(value, axis, [(i, i ^ bit) for i in range(n)])]
  transfers between devices with their start and end apart: 25 -> 25, of which waited for: 15 -> 14; matrix products, arithmetic and copies ran while one was open for 0% -> 0% of each run, Pallas kernels for 39% -> 39%
where the time goes in v15:
time: 129 us
  Pallas kernels  55.2 us (43%)
  waiting for transfers between devices  40.3 us (31%)
  starting transfers between devices  31.5 us (24%)
    pallas_call x30, Pallas kernels, local(): pl.pallas_call(body, out_shape=shapes, in_specs=[VMEM] * len(args) + [ANY...  40.9 us
    ppermute x12, waiting for transfers between devices, swapped(): return lax.ppermute(value, axis, [(i, i ^ bit) for i in range(n)])  25.2 us
    ppermute x12, starting transfers between devices, swapped(): return lax.ppermute(value, axis, [(i, i ^ bit) for i in range(n)])  21.8 us
    ppermute x13, waiting for transfers between devices, shifted(): return lax.ppermute(value, axis, [(i, (i + step) % n) for i in range(n)])  15.1 us
    pallas_call x4, Pallas kernels, gradients(): pl.pallas_call(body, grid=grid, out_shape=[jax.ShapeDtypeStruct(shape, jn...  14.2 us
    ppermute x13, starting transfers between devices, shifted(): return lax.ppermute(value, axis, [(i, (i + step) % n) for i in range(n)])  9.74 us
  transfers between devices with their start and end apart: 25, of which 14 were waited for; matrix products, arithmetic and copies ran while one was open for 0% of the time, Pallas kernels for 39%

profile of v15, /device:TPU:0, one launch (start us, length us, event | category | flops | bytes accessed | tf_op | source)
XLA Modules:
  0.0 129.0 jit_solution(11096754824834177319)
XLA Ops:
  0.6 0.9 copy-done.4
  1.6 4.1 %collective-permute-start.5 = (bf16[64,512]{1,0:T(8,128)(2,1)S(1)}, bf16[64,512]{1,0:T(8,128)(2,1)S(1)}, u32[]{:S(2)}, u32[]{:S(2)}) collective-permute-start(bf16[64,512]{1,0:T(8,128)(2,1)S(1)} %shard_map.91.refs_0_), channel_id=1, source_target_pairs={{0,8},{4,12},{8,0},{12,4},{1,9},{5,13},{9,1},{13,5},{2,10},{6,14},... | collective-permute-start | bytes 196616 | tf_op jit(solution)/shard_map/ppermute | solution.py:46
  5.7 3.6 %collective-permute-done.5.refs_1_ = bf16[64,512]{1,0:T(8,128)(2,1)S(1)} collective-permute-done((bf16[64,512]{1,0:T(8,128)(2,1)S(1)}, bf16[64,512]{1,0:T(8,128)(2,1)S(1)}, u32[]{:S(2)}, u32[]{:S(2)}) %collective-permute-start.5) | collective-permute-done | bytes 65568 | tf_op jit(solution)/shard_map/ppermute | solution.py:46
  9.3 0.6 collective-permute-start.6
  10.0 3.4 %collective-permute-start = (bf16[64,512]{1,0:T(8,128)(2,1)S(1)}, bf16[64,512]{1,0:T(8,128)(2,1)S(1)}, u32[]{:S(2)}, u32[]{:S(2)}) collective-permute-start(bf16[64,512]{1,0:T(8,128)(2,1)S(1)} %shard_map.84.refs_0_), channel_id=1, source_target_pairs={{0,8},{4,12},{8,0},{12,4},{1,9},{5,13},{9,1},{13,5},{2,10},{6,14},... | collective-permute-start | bytes 196616 | tf_op jit(solution)/shard_map/ppermute | solution.py:46
  13.4 1.7 %collective-permute-done.6.refs_1_ = bf16[64,1024]{1,0:T(8,128)(2,1)S(1)} collective-permute-done((bf16[64,1024]{1,0:T(8,128)(2,1)S(1)}, bf16[64,1024]{1,0:T(8,128)(2,1)S(1)}, u32[]{:S(2)}, u32[]{:S(2)}) %collective-permute-start.6) | collective-permute-done | bytes 131104 | tf_op jit(solution)/shard_map/ppermute | solution.py:46
  15.2 1.1 collective-permute-done.refs_1_
  16.3 1.9 %collective-permute-start.1 = (bf16[64,1024]{1,0:T(8,128)(2,1)S(1)}, bf16[64,1024]{1,0:T(8,128)(2,1)S(1)}, u32[]{:S(2)}, u32[]{:S(2)}) collective-permute-start(bf16[64,1024]{1,0:T(8,128)(2,1)S(1)} %shard_map.85.refs_0_), channel_id=1, source_target_pairs={{0,4},{4,0},{8,12},{12,8},{1,5},{5,1},{9,13},{13,9},{2,6},{6,2},{1... | collective-permute-start | bytes 393224 | tf_op jit(solution)/shard_map/ppermute | solution.py:46
  18.2 2.1 %shard_map.94.refs_3_.refs_0_ = bf16[256,1792]{1,0:T(8,128)(2,1)S(1)} custom-call(bf16[64,2048]{1,0:T(8,128)(2,1)S(1)} %shard_map.93.refs_0_.refs_2_, bf16[64,2048]{1,0:T(8,128)(2,1)S(1)} %collective-permute-done.7.refs_1_.refs_3_, bf16[64,2048]{1,0:T(8,128)(2,1)S(1)} %shard_map.93.refs_0_.refs_2_, ...), custom_call_target="tpu_custom_call" | custom-call | flops 345000000 | tf_op jit(solution)/shard_map/pallas_call | solution.py:101
  20.3 1.6 %collective-permute-start.9 = (bf16[256,1792]{1,0:T(8,128)(2,1)S(1)}, bf16[256,1792]{1,0:T(8,128)(2,1)S(1)}, u32[]{:S(2)}, u32[]{:S(2)}) collective-permute-start(bf16[256,1792]{1,0:T(8,128)(2,1)S(1)} %shard_map.94.refs_3_.refs_0_), channel_id=1, source_target_pairs={{0,2},{2,0},{1,3},{3,1},{4,6},{6,4},{5,7},{7,5},{8,10},{10,8},{9,1... | collective-permute-start | bytes 2752520 | tf_op jit(solution)/shard_map/ppermute | solution.py:41
  22.0 2.4 %collective-permute-start.2 = (bf16[128,512]{1,0:T(8,128)(2,1)S(1)}, bf16[128,512]{1,0:T(8,128)(2,1)S(1)}, u32[]{:S(2)}, u32[]{:S(2)}) collective-permute-start(bf16[128,512]{1,0:T(8,128)(2,1)S(1)} %shard_map.87.refs_0_), channel_id=1, source_target_pairs={{0,8},{4,12},{8,0},{12,4},{1,9},{5,13},{9,1},{13,5},{2,10},{6,14},... | collective-permute-start | bytes 393224 | tf_op jit(solution)/shard_map/ppermute | solution.py:46
  24.4 7.3 %collective-permute-done.2.refs_1_ = bf16[128,512]{1,0:T(8,128)(2,1)S(1)} collective-permute-done((bf16[128,512]{1,0:T(8,128)(2,1)S(1)}, bf16[128,512]{1,0:T(8,128)(2,1)S(1)}, u32[]{:S(2)}, u32[]{:S(2)}) %collective-permute-start.2) | collective-permute-done | bytes 131104 | tf_op jit(solution)/shard_map/ppermute | solution.py:46
  31.7 0.5 collective-permute-start.3
  32.2 2.5 %shard_map.95.refs_9_.refs_1_ = bf16[128,1792]{1,0:T(8,128)(2,1)S(1)} custom-call(bf16[64,2048]{1,0:T(8,128)(2,1)S(1)} %shard_map.86.refs_2_.refs_0_, bf16[64,2048]{1,0:T(8,128)(2,1)S(1)} %collective-permute-done.8.refs_1_, bf16[1792,2048]{1,0:T(8,128)(2,1)S(1)} %bitcast.1, bf16[256,1792]{1,0:T(8,128)(2,1)S(1)} %shard_map.94.refs_3_.refs_0_), custom_call_target="tpu_custom_call" | custom-call | flops 345000000 | tf_op jit(solution)/shard_map/pallas_call | solution.py:101
  34.7 1.6 %collective-permute-start.10 = (bf16[128,1792]{1,0:T(8,128)(2,1)S(1)}, bf16[128,1792]{1,0:T(8,128)(2,1)S(1)}, u32[]{:S(2)}, u32[]{:S(2)}) collective-permute-start(bf16[128,1792]{1,0:T(8,128)(2,1)S(1)} %shard_map.95.refs_9_.refs_1_), channel_id=1, source_target_pairs={{0,2},{2,0},{1,3},{3,1},{4,6},{6,4},{5,7},{7,5},{8,10},{10,8},{9,1... | collective-permute-start | bytes 1376264 | tf_op jit(solution)/shard_map/ppermute | solution.py:41
  36.3 3.4 %collective-permute-done.3.refs_1_ = bf16[128,1024]{1,0:T(8,128)(2,1)S(1)} collective-permute-done((bf16[128,1024]{1,0:T(8,128)(2,1)S(1)}, bf16[128,1024]{1,0:T(8,128)(2,1)S(1)}, u32[]{:S(2)}, u32[]{:S(2)}) %collective-permute-start.3) | collective-permute-done | bytes 262176 | tf_op jit(solution)/shard_map/ppermute | solution.py:46
  39.8 0.5 collective-permute-start.11
  40.3 2.5 %collective-permute-start.4 = (bf16[128,512]{1,0:T(8,128)(2,1)S(1)}, bf16[128,512]{1,0:T(8,128)(2,1)S(1)}, u32[]{:S(2)}, u32[]{:S(2)}) collective-permute-start(bf16[128,512]{1,0:T(8,128)(2,1)S(1)} %shard_map.90.refs_0_), channel_id=1, source_target_pairs={{0,8},{4,12},{8,0},{12,4},{1,9},{5,13},{9,1},{13,5},{2,10},{6,14},... | collective-permute-start | bytes 393224 | tf_op jit(solution)/shard_map/ppermute | solution.py:46
  42.8 4.4 %shard_map.96.refs_6_.refs_0_ = bf16[384,1792]{1,0:T(8,128)(2,1)S(1)} custom-call(bf16[64,2048]{1,0:T(8,128)(2,1)S(1)} %get-tuple-element.50.refs_2_.refs_0_, bf16[64,2048]{1,0:T(8,128)(2,1)S(1)} %collective-permute-done.11.refs_1_.refs_3_, bf16[64,2048]{1,0:T(8,128)(2,1)S(1)} %get-tuple-element.50.refs_2_.refs_0_, ...), custom_call_target="tpu_custom_call" | custom-call | flops 345000000 | tf_op jit(solution)/shard_map/pallas_call | solution.py:101
  47.2 1.6 %collective-permute-start.18 = (bf16[384,1792]{1,0:T(8,128)(2,1)S(1)}, bf16[384,1792]{1,0:T(8,128)(2,1)S(1)}, u32[]{:S(2)}, u32[]{:S(2)}) collective-permute-start(bf16[384,1792]{1,0:T(8,128)(2,1)S(1)} %shard_map.96.refs_6_.refs_0_), channel_id=1, source_target_pairs={{0,2},{2,0},{1,3},{3,1},{4,6},{6,4},{5,7},{7,5},{8,10},{10,8},{9,1... | collective-permute-start | bytes 4128776 | tf_op jit(solution)/shard_map/ppermute | solution.py:41
  48.8 4.4 %collective-permute-done.10.refs_3_ = bf16[128,1792]{1,0:T(8,128)(2,1)S(1)} collective-permute-done((bf16[128,1792]{1,0:T(8,128)(2,1)S(1)}, bf16[128,1792]{1,0:T(8,128)(2,1)S(1)}, u32[]{:S(2)}, u32[]{:S(2)}) %collective-permute-start.10) | collective-permute-done | bytes 458784 | tf_op jit(solution)/shard_map/ppermute | solution.py:41
  53.2 5.8 %shard_map.97 = (bf16[1792,128]{1,0:T(8,128)(2,1)S(1)}, bf16[128,1792]{1,0:T(8,128)(2,1)S(1)}, bf16[128,1792]{1,0:T(8,128)(2,1)S(1)}, f32[64,2048]{1,0:T(8,128)S(1)}, bf16[64,2048]{1,0:T(8,128)(2,1)S(1)}) custom-call(bf16[256,1792]{1,0:T(8,128)(2,1)S(1)} %shard_map.94.refs_3_.refs_0_, bf16[128,1792]{1,0:T(8,128)(2,1)S(1)} %shard_map.95.refs_9_.refs_1_, ...), custom_call_target="tpu_custom_call" | custom-call | flops 69000003584 | tf_op jit(solution)/shard_map/pallas_call | solution.py:101
  59.1 6.4 %collective-permute-done.13.refs_1_ = bf16[128,1024]{1,0:T(8,128)(2,1)S(1)} collective-permute-done((bf16[128,1024]{1,0:T(8,128)(2,1)S(1)}, bf16[128,1024]{1,0:T(8,128)(2,1)S(1)}, u32[]{:S(2)}, u32[]{:S(2)}) %collective-permute-start.13) | collective-permute-done | bytes 262176 | tf_op jit(solution)/shard_map/ppermute | solution.py:46
  65.6 0.5 collective-permute-start.15
  66.1 1.0 collective-permute-done.14.refs_1_.refs_3_.refs_5_
  67.2 0.4 collective-permute-done.15.refs_5_
  67.5 2.4 %shard_map.100.refs_9_.refs_0_ = bf16[384,896]{1,0:T(8,128)(2,1)S(1)} custom-call(bf16[64,2048]{1,0:T(8,128)(2,1)S(1)} %get-tuple-element.53.refs_0_.refs_2_.refs_4_, bf16[64,2048]{1,0:T(8,128)(2,1)S(1)} %collective-permute-done.14.refs_1_.refs_3_.refs_5_, bf16[64,2048]{1,0:T(8,128)(2,1)S(1)} %get-tuple-element.53.refs_0_.refs_2_.refs_4_, ...), custom_call_target="tpu_custom_call" | custom-call | flops 345000000 | tf_op jit(solution)/shard_map/pallas_call | solution.py:101
  69.9 1.8 %collective-permute-start.17 = (bf16[384,896]{1,0:T(8,128)(2,1)S(1)}, bf16[384,896]{1,0:T(8,128)(2,1)S(1)}, u32[]{:S(2)}, u32[]{:S(2)}) collective-permute-start(bf16[384,896]{1,0:T(8,128)(2,1)S(1)} %shard_map.100.refs_9_.refs_0_), channel_id=1, source_target_pairs={{0,2},{2,0},{1,3},{3,1},{4,6},{6,4},{5,7},{7,5},{8,10},{10,8},{9,1... | collective-permute-start | bytes 2064392 | tf_op jit(solution)/shard_map/ppermute | solution.py:41
  71.8 2.4 %shard_map.101.refs_6_.refs_0_ = bf16[384,896]{1,0:T(8,128)(2,1)S(1)} custom-call(bf16[64,2048]{1,0:T(8,128)(2,1)S(1)} %get-tuple-element.53.refs_0_.refs_2_.refs_4_, bf16[64,2048]{1,0:T(8,128)(2,1)S(1)} %collective-permute-done.14.refs_1_.refs_3_.refs_5_, bf16[64,2048]{1,0:T(8,128)(2,1)S(1)} %get-tuple-element.53.refs_0_.refs_2_.refs_4_, ...), custom_call_target="tpu_custom_call" | custom-call | flops 345000000 | tf_op jit(solution)/shard_map/pallas_call | solution.py:101
  74.3 0.6 shard_map.102.refs_6_.refs_0_
  75.0 7.7 %collective-permute-done.18.refs_1_ = bf16[384,1792]{1,0:T(8,128)(2,1)S(1)} collective-permute-done((bf16[384,1792]{1,0:T(8,128)(2,1)S(1)}, bf16[384,1792]{1,0:T(8,128)(2,1)S(1)}, u32[]{:S(2)}, u32[]{:S(2)}) %collective-permute-start.18) | collective-permute-done | bytes 1376288 | tf_op jit(solution)/shard_map/ppermute | solution.py:41
  82.7 6.1 %shard_map.104 = (bf16[1792,128]{1,0:T(8,128)(2,1)S(1)}, bf16[128,1792]{1,0:T(8,128)(2,1)S(1)}, bf16[128,1792]{1,0:T(8,128)(2,1)S(1)}, f32[128,2048]{1,0:T(8,128)S(1)}, bf16[128,2048]{1,0:T(8,128)(2,1)S(1)}) custom-call(bf16[384,1792]{1,0:T(8,128)(2,1)S(1)} %shard_map.96.refs_6_.refs_0_, bf16[384,1792]{1,0:T(8,128)(2,1)S(1)} %collective-permute-done.18.refs_1_, ...), custom_call_target="tpu_custom_call" | custom-call | flops 69000003584 | tf_op jit(solution)/shard_map/pallas_call | solution.py:101
  88.9 1.8 %collective-permute-start.16 = (bf16[384,896]{1,0:T(8,128)(2,1)S(1)}, bf16[384,896]{1,0:T(8,128)(2,1)S(1)}, u32[]{:S(2)}, u32[]{:S(2)}) collective-permute-start(bf16[384,896]{1,0:T(8,128)(2,1)S(1)} %shard_map.101.refs_6_.refs_0_), channel_id=1, source_target_pairs={{0,2},{2,0},{1,3},{3,1},{4,6},{6,4},{5,7},{7,5},{8,10},{10,8},{9,1... | collective-permute-start | bytes 2064392 | tf_op jit(solution)/shard_map/ppermute | solution.py:41
  90.9 3.3 %shard_map.106 = (bf16[2048,896]{1,0:T(8,128)(2,1)S(1)}, bf16[2048,896]{1,0:T(8,128)(2,1)S(1)}, bf16[896,2048]{1,0:T(8,128)(2,1)S(1)}) custom-call(bf16[2048,384]{1,0:T(8,128)(2,1)S(1)} %shard_map.102.refs_6_.refs_0_, bf16[384,2048]{1,0:T(8,128)(2,1)S(1)} %shard_map.103.refs_7_.refs_1_, bf16[1792,128]{1,0:T(8,128)(2,1)S(1)} %get-tuple-element.55.refs_2_, ...), custom_call_target="tpu_custom_call" | custom-call | flops 115000000 | tf_op jit(solution)/shard_map/pallas_call | solution.py:101
  94.3 3.3 %shard_map.107 = (bf16[2048,896]{1,0:T(8,128)(2,1)S(1)}, bf16[2048,896]{1,0:T(8,128)(2,1)S(1)}, bf16[896,2048]{1,0:T(8,128)(2,1)S(1)}) custom-call(bf16[2048,384]{1,0:T(8,128)(2,1)S(1)} %shard_map.102.refs_6_.refs_0_, bf16[384,2048]{1,0:T(8,128)(2,1)S(1)} %shard_map.103.refs_7_.refs_1_, bf16[1792,128]{1,0:T(8,128)(2,1)S(1)} %get-tuple-element.55.refs_2_, ...), custom_call_target="tpu_custom_call" | custom-call | flops 115000000 | tf_op jit(solution)/shard_map/pallas_call | solution.py:101
  97.6 3.2 %shard_map.108 = (bf16[896,128]{1,0:T(8,128)(2,1)S(1)}, bf16[128,896]{1,0:T(8,128)(2,1)S(1)}, bf16[128,896]{1,0:T(8,128)(2,1)S(1)}, f32[128,2048]{1,0:T(8,128)S(1)}) custom-call(bf16[384,896]{1,0:T(8,128)(2,1)S(1)} %shard_map.100.refs_9_.refs_0_, bf16[384,896]{1,0:T(8,128)(2,1)S(1)} %collective-permute-done.17.refs_1_, bf16[2048,1792]{1,0:T(8,128)(2,1)S(1)} %copy-done, ...), custom_call_target="tpu_custom_call" | custom-call | flops 2300000000 | tf_op jit(solution)/shard_map/pallas_call | solution.py:101
  100.9 3.5 %collective-permute-start.21 = (bf16[128,512]{1,0:T(8,128)(2,1)S(1)}, bf16[128,512]{1,0:T(8,128)(2,1)S(1)}, u32[]{:S(2)}, u32[]{:S(2)}) collective-permute-start(bf16[128,512]{1,0:T(8,128)(2,1)S(1)} %get-tuple-element.77), channel_id=1, source_target_pairs={{0,8},{4,12},{8,0},{12,4},{1,9},{5,13},{9,1},{13,5},{2,10},{6,14},... | collective-permute-start | bytes 393224 | tf_op jit(solution)/shard_map/ppermute | solution.py:46
  104.4 3.0 %shard_map.110 = (bf16[1792,2048]{1,0:T(8,128)(2,1)}, bf16[16,128]{1,0:T(8,128)(2,1)S(1)}) custom-call(bf16[896,128]{1,0:T(8,128)(2,1)S(1)} %get-tuple-element.72.refs_0_, bf16[384,2048]{1,0:T(8,128)(2,1)S(1)} %shard_map.103.refs_7_.refs_1_, bf16[896,2048]{1,0:T(8,128)(2,1)S(1)} %get-tuple-element.66.refs_4_.refs_2_, ...), custom_call_target="tpu_custom_call" | custom-call | flops 2300000000 | tf_op jit(solution)/shard_map/pallas_call | solution.py:323
  107.4 4.1 %shard_map.111 = (bf16[2048,1792]{1,0:T(8,128)(2,1)}, bf16[2048,1792]{1,0:T(8,128)(2,1)}, bf16[16,128]{1,0:T(8,128)(2,1)S(1)}) custom-call(bf16[2048,384]{1,0:T(8,128)(2,1)S(1)} %shard_map.102.refs_6_.refs_0_, bf16[128,896]{1,0:T(8,128)(2,1)S(1)} %get-tuple-element.68.refs_2_.refs_1_, bf16[128,896]{1,0:T(8,128)(2,1)S(1)} %get-tuple-element.69.refs_2_, ...), custom_call_target="tpu_custom_call" | custom-call | flops 115000000 | tf_op jit(solution)/shard_map/pallas_call | solution.py:323
  111.6 3.4 %shard_map.113 = (bf16[896,128]{1,0:T(8,128)(2,1)S(1)}, bf16[128,896]{1,0:T(8,128)(2,1)S(1)}, bf16[128,896]{1,0:T(8,128)(2,1)S(1)}, f32[64,2048]{1,0:T(8,128)S(1)}, bf16[64,2048]{1,0:T(8,128)(2,1)S(1)}) custom-call(bf16[384,896]{1,0:T(8,128)(2,1)S(1)} %shard_map.101.refs_6_.refs_0_, bf16[384,896]{1,0:T(8,128)(2,1)S(1)} %collective-permute-done.16.refs_1_, ...), custom_call_target="tpu_custom_call" | custom-call | flops 2300000000 | tf_op jit(solution)/shard_map/pallas_call | solution.py:101
  115.1 1.5 %collective-permute-done.22.refs_1_ = bf16[64,2048]{1,0:T(8,128)(2,1)S(1)} collective-permute-done((bf16[64,2048]{1,0:T(8,128)(2,1)S(1)}, bf16[64,2048]{1,0:T(8,128)(2,1)S(1)}, u32[]{:S(2)}, u32[]{:S(2)}) %collective-permute-start.22) | collective-permute-done | bytes 262176 | tf_op jit(solution)/shard_map/ppermute | solution.py:41
  116.7 0.7 collective-permute-start.23
  117.4 4.1 %shard_map.115 = (bf16[2048,1792]{1,0:T(8,128)(2,1)}, bf16[2048,1792]{1,0:T(8,128)(2,1)}, bf16[16,128]{1,0:T(8,128)(2,1)S(1)}) custom-call(bf16[2048,384]{1,0:T(8,128)(2,1)S(1)} %shard_map.102.refs_6_.refs_0_, bf16[128,896]{1,0:T(8,128)(2,1)S(1)} %get-tuple-element.82.refs_1_, ...), custom_call_target="tpu_custom_call", output_to_operand_aliasing={{0}: (5, {}), {1}: (6, {})} | custom-call | flops 5750000128 | tf_op jit(solution)/shard_map/pallas_call | solution.py:323
  121.4 0.9 collective-permute-done.23.refs_1_
  122.3 2.0 %collective-permute-start.24 = (bf16[64,512]{1,0:T(8,128)(2,1)S(1)}, bf16[64,512]{1,0:T(8,128)(2,1)S(1)}, u32[]{:S(2)}, u32[]{:S(2)}) collective-permute-start(bf16[64,512]{1,0:T(8,128)(2,1)S(1)} %get-tuple-element.90), channel_id=1, source_target_pairs={{0,8},{4,12},{8,0},{12,4},{1,9},{5,13},{9,1},{13,5},{2,10},{6,14},... | collective-permute-start | bytes 196616 | tf_op jit(solution)/shard_map/ppermute | solution.py:46
  124.3 3.0 %shard_map.118 = (bf16[1792,2048]{1,0:T(8,128)(2,1)}, bf16[16,128]{1,0:T(8,128)(2,1)}) custom-call(bf16[896,128]{1,0:T(8,128)(2,1)S(1)} %get-tuple-element.93.refs_0_, bf16[384,2048]{1,0:T(8,128)(2,1)S(1)} %shard_map.103.refs_7_.refs_1_, bf16[896,2048]{1,0:T(8,128)(2,1)S(1)} %get-tuple-element.65.refs_8_.refs_2_, ...), custom_call_target="tpu_custom_call", output_to_operand_aliasing={{0}: (3, {})} | custom-call | flops 3449999872 | tf_op jit(solution)/shard_map/pallas_call | solution.py:323
  127.3 0.9 collective-permute-done.24.refs_1_
  128.3 0.7 shard_map.117
  (56 shorter events, 1.4 us)
Async XLA Ops:
  0.6 0.9 copy-start.4
  1.6 8.4 %copy-start.5 = (bf16[192,512]{1,0:T(8,128)(2,1)S(1)}, bf16[192,512]{1,0:T(8,128)(2,1)}, u32[]{:S(2)}) copy-start(bf16[192,512]{1,0:T(8,128)(2,1)} %source.1) | copy-start | bytes 589828
  1.6 8.4 %copy-start.6 = (bf16[192,512]{1,0:T(8,128)(2,1)S(1)}, bf16[192,512]{1,0:T(8,128)(2,1)}, u32[]{:S(2)}) copy-start(bf16[192,512]{1,0:T(8,128)(2,1)} %refs_1_.5) | copy-start | bytes 589828
  1.6 16.6 %copy-start = (bf16[2048,1792]{1,0:T(8,128)(2,1)S(1)}, bf16[2048,1792]{1,0:T(8,128)(2,1)}, u32[]{:S(2)}) copy-start(bf16[2048,1792]{1,0:T(8,128)(2,1)} %refs_2_.7) | copy-start | bytes 22020100
  1.6 16.6 %copy-start.1 = (bf16[2048,1792]{1,0:T(8,128)(2,1)S(1)}, bf16[2048,1792]{1,0:T(8,128)(2,1)}, u32[]{:S(2)}) copy-start(bf16[2048,1792]{1,0:T(8,128)(2,1)} %refs_3_.5) | copy-start | bytes 22020100
  1.6 7.8 %collective-permute-start.5 = (bf16[64,512]{1,0:T(8,128)(2,1)S(1)}, bf16[64,512]{1,0:T(8,128)(2,1)S(1)}, u32[]{:S(2)}, u32[]{:S(2)}) collective-permute-start(bf16[64,512]{1,0:T(8,128)(2,1)S(1)} %shard_map.91.refs_0_), channel_id=1, source_target_pairs={{0,8},{4,12},{8,0},{12,4},{1,9},{5,13},{9,1},{13,5},{2,10},{6,14},... | collective-permute-start | bytes 196616 | tf_op jit(solution)/shard_map/ppermute | solution.py:46
  9.3 5.7 %collective-permute-start.6 = (bf16[64,1024]{1,0:T(8,128)(2,1)S(1)}, bf16[64,1024]{1,0:T(8,128)(2,1)S(1)}, u32[]{:S(2)}, u32[]{:S(2)}) collective-permute-start(bf16[64,1024]{1,0:T(8,128)(2,1)S(1)} %shard_map.92.refs_0_), channel_id=1, source_target_pairs={{0,4},{4,0},{8,12},{12,8},{1,5},{5,1},{9,13},{13,9},{2,6},{6,2},{1... | collective-permute-start | bytes 393224 | tf_op jit(solution)/shard_map/ppermute | solution.py:46
  10.0 6.3 %collective-permute-start = (bf16[64,512]{1,0:T(8,128)(2,1)S(1)}, bf16[64,512]{1,0:T(8,128)(2,1)S(1)}, u32[]{:S(2)}, u32[]{:S(2)}) collective-permute-start(bf16[64,512]{1,0:T(8,128)(2,1)S(1)} %shard_map.84.refs_0_), channel_id=1, source_target_pairs={{0,8},{4,12},{8,0},{12,4},{1,9},{5,13},{9,1},{13,5},{2,10},{6,14},... | collective-permute-start | bytes 196616 | tf_op jit(solution)/shard_map/ppermute | solution.py:46
  15.1 3.0 %collective-permute-start.7 = (bf16[64,2048]{1,0:T(8,128)(2,1)S(1)}, bf16[64,2048]{1,0:T(8,128)(2,1)S(1)}, u32[]{:S(2)}, u32[]{:S(2)}) collective-permute-start(bf16[64,2048]{1,0:T(8,128)(2,1)S(1)} %shard_map.93.refs_0_.refs_2_), channel_id=1, source_target_pairs={{0,1},{1,0},{2,3},{3,2},{4,5},{5,4},{6,7},{7,6},{8,9},{9,8},{10,11... | collective-permute-start | bytes 786440 | tf_op jit(solution)/shard_map/ppermute | solution.py:41
  16.3 5.6 %collective-permute-start.1 = (bf16[64,1024]{1,0:T(8,128)(2,1)S(1)}, bf16[64,1024]{1,0:T(8,128)(2,1)S(1)}, u32[]{:S(2)}, u32[]{:S(2)}) collective-permute-start(bf16[64,1024]{1,0:T(8,128)(2,1)S(1)} %shard_map.85.refs_0_), channel_id=1, source_target_pairs={{0,4},{4,0},{8,12},{12,8},{1,5},{5,1},{9,13},{13,9},{2,6},{6,2},{1... | collective-permute-start | bytes 393224 | tf_op jit(solution)/shard_map/ppermute | solution.py:46
  18.2 14.0 %slice-start = ((s8[7340032]{0:T(1024)(128)(4,1)}), s8[4194304]{0:T(1024)(128)(4,1)S(1)}, s32[]{:S(2)}) async-start(s8[7340032]{0:T(1024)(128)(4,1)} %bitcast), calls=%async_computation | async-start | bytes 8388608
  20.3 11.9 %slice-start.1 = ((s8[7340032]{0:T(1024)(128)(4,1)}), s8[3145728]{0:T(1024)(128)(4,1)S(1)}, s32[]{:S(2)}) async-start(s8[7340032]{0:T(1024)(128)(4,1)} %bitcast), calls=%async_computation.1 | async-start | bytes 6291456
  20.3 32.9 %collective-permute-start.9 = (bf16[256,1792]{1,0:T(8,128)(2,1)S(1)}, bf16[256,1792]{1,0:T(8,128)(2,1)S(1)}, u32[]{:S(2)}, u32[]{:S(2)}) collective-permute-start(bf16[256,1792]{1,0:T(8,128)(2,1)S(1)} %shard_map.94.refs_3_.refs_0_), channel_id=1, source_target_pairs={{0,2},{2,0},{1,3},{3,1},{4,6},{6,4},{5,7},{7,5},{8,10},{10,8},{9,1... | collective-permute-start | bytes 2752520 | tf_op jit(solution)/shard_map/ppermute | solution.py:41
  21.9 10.3 %collective-permute-start.8 = (bf16[64,2048]{1,0:T(8,128)(2,1)S(1)}, bf16[64,2048]{1,0:T(8,128)(2,1)S(1)}, u32[]{:S(2)}, u32[]{:S(2)}) collective-permute-start(bf16[64,2048]{1,0:T(8,128)(2,1)S(1)} %shard_map.86.refs_2_.refs_0_), channel_id=1, source_target_pairs={{0,1},{1,0},{2,3},{3,2},{4,5},{5,4},{6,7},{7,6},{8,9},{9,8},{10,11... | collective-permute-start | bytes 786440 | tf_op jit(solution)/shard_map/ppermute | solution.py:41
  22.0 9.7 %collective-permute-start.2 = (bf16[128,512]{1,0:T(8,128)(2,1)S(1)}, bf16[128,512]{1,0:T(8,128)(2,1)S(1)}, u32[]{:S(2)}, u32[]{:S(2)}) collective-permute-start(bf16[128,512]{1,0:T(8,128)(2,1)S(1)} %shard_map.87.refs_0_), channel_id=1, source_target_pairs={{0,8},{4,12},{8,0},{12,4},{1,9},{5,13},{9,1},{13,5},{2,10},{6,14},... | collective-permute-start | bytes 393224 | tf_op jit(solution)/shard_map/ppermute | solution.py:46
  31.7 8.0 %collective-permute-start.3 = (bf16[128,1024]{1,0:T(8,128)(2,1)S(1)}, bf16[128,1024]{1,0:T(8,128)(2,1)S(1)}, u32[]{:S(2)}, u32[]{:S(2)}) collective-permute-start(bf16[128,1024]{1,0:T(8,128)(2,1)S(1)} %shard_map.88.refs_0_), channel_id=1, source_target_pairs={{0,4},{4,0},{8,12},{12,8},{1,5},{5,1},{9,13},{13,9},{2,6},{6,2},{1... | collective-permute-start | bytes 786440 | tf_op jit(solution)/shard_map/ppermute | solution.py:46
  34.7 18.5 %collective-permute-start.10 = (bf16[128,1792]{1,0:T(8,128)(2,1)S(1)}, bf16[128,1792]{1,0:T(8,128)(2,1)S(1)}, u32[]{:S(2)}, u32[]{:S(2)}) collective-permute-start(bf16[128,1792]{1,0:T(8,128)(2,1)S(1)} %shard_map.95.refs_9_.refs_1_), channel_id=1, source_target_pairs={{0,2},{2,0},{1,3},{3,1},{4,6},{6,4},{5,7},{7,5},{8,10},{10,8},{9,1... | collective-permute-start | bytes 1376264 | tf_op jit(solution)/shard_map/ppermute | solution.py:41
  39.7 3.1 %collective-permute-start.12 = (bf16[64,2048]{1,0:T(8,128)(2,1)S(1)}, bf16[64,2048]{1,0:T(8,128)(2,1)S(1)}, u32[]{:S(2)}, u32[]{:S(2)}) collective-permute-start(bf16[64,2048]{1,0:T(8,128)(2,1)S(1)} %get-tuple-element.51.refs_4_.refs_2_), channel_id=1, source_target_pairs={{0,1},{1,0},{2,3},{3,2},{4,5},{5,4},{6,7},{7,6},{8,9},{9,8},{10,11... | collective-permute-start | bytes 786440 | tf_op jit(solution)/shard_map/ppermute | solution.py:41
  39.8 3.0 %collective-permute-start.11 = (bf16[64,2048]{1,0:T(8,128)(2,1)S(1)}, bf16[64,2048]{1,0:T(8,128)(2,1)S(1)}, u32[]{:S(2)}, u32[]{:S(2)}) collective-permute-start(bf16[64,2048]{1,0:T(8,128)(2,1)S(1)} %get-tuple-element.50.refs_2_.refs_0_), channel_id=1, source_target_pairs={{0,1},{1,0},{2,3},{3,2},{4,5},{5,4},{6,7},{7,6},{8,9},{9,8},{10,11... | collective-permute-start | bytes 786440 | tf_op jit(solution)/shard_map/ppermute | solution.py:41
  40.3 18.7 %collective-permute-start.4 = (bf16[128,512]{1,0:T(8,128)(2,1)S(1)}, bf16[128,512]{1,0:T(8,128)(2,1)S(1)}, u32[]{:S(2)}, u32[]{:S(2)}) collective-permute-start(bf16[128,512]{1,0:T(8,128)(2,1)S(1)} %shard_map.90.refs_0_), channel_id=1, source_target_pairs={{0,8},{4,12},{8,0},{12,4},{1,9},{5,13},{9,1},{13,5},{2,10},{6,14},... | collective-permute-start | bytes 393224 | tf_op jit(solution)/shard_map/ppermute | solution.py:46
  47.2 35.5 %collective-permute-start.18 = (bf16[384,1792]{1,0:T(8,128)(2,1)S(1)}, bf16[384,1792]{1,0:T(8,128)(2,1)S(1)}, u32[]{:S(2)}, u32[]{:S(2)}) collective-permute-start(bf16[384,1792]{1,0:T(8,128)(2,1)S(1)} %shard_map.96.refs_6_.refs_0_), channel_id=1, source_target_pairs={{0,2},{2,0},{1,3},{3,1},{4,6},{6,4},{5,7},{7,5},{8,10},{10,8},{9,1... | collective-permute-start | bytes 4128776 | tf_op jit(solution)/shard_map/ppermute | solution.py:41
  59.1 6.4 %collective-permute-start.13 = (bf16[128,1024]{1,0:T(8,128)(2,1)S(1)}, bf16[128,1024]{1,0:T(8,128)(2,1)S(1)}, u32[]{:S(2)}, u32[]{:S(2)}) collective-permute-start(bf16[128,1024]{1,0:T(8,128)(2,1)S(1)} %shard_map.98.refs_0_), channel_id=1, source_target_pairs={{0,4},{4,0},{8,12},{12,8},{1,5},{5,1},{9,13},{13,9},{2,6},{6,2},{1... | collective-permute-start | bytes 786440 | tf_op jit(solution)/shard_map/ppermute | solution.py:46
  65.6 1.6 %collective-permute-start.14 = (bf16[64,2048]{1,0:T(8,128)(2,1)S(1)}, bf16[64,2048]{1,0:T(8,128)(2,1)S(1)}, u32[]{:S(2)}, u32[]{:S(2)}) collective-permute-start(bf16[64,2048]{1,0:T(8,128)(2,1)S(1)} %get-tuple-element.53.refs_0_.refs_2_.refs_4_), channel_id=1, source_target_pairs={{0,1},{1,0},{2,3},{3,2},{4,5},{5,4},{6,7},{7,6},{8,9},{9,8},{10,11... | collective-permute-start | bytes 786440 | tf_op jit(solution)/shard_map/ppermute | solution.py:41
  65.6 1.9 %collective-permute-start.15 = (bf16[64,2048]{1,0:T(8,128)(2,1)S(1)}, bf16[64,2048]{1,0:T(8,128)(2,1)S(1)}, u32[]{:S(2)}, u32[]{:S(2)}) collective-permute-start(bf16[64,2048]{1,0:T(8,128)(2,1)S(1)} %get-tuple-element.54.refs_4_), channel_id=1, source_target_pairs={{0,1},{1,0},{2,3},{3,2},{4,5},{5,4},{6,7},{7,6},{8,9},{9,8},{10,11... | collective-permute-start | bytes 786440 | tf_op jit(solution)/shard_map/ppermute | solution.py:41
  69.9 27.7 %collective-permute-start.17 = (bf16[384,896]{1,0:T(8,128)(2,1)S(1)}, bf16[384,896]{1,0:T(8,128)(2,1)S(1)}, u32[]{:S(2)}, u32[]{:S(2)}) collective-permute-start(bf16[384,896]{1,0:T(8,128)(2,1)S(1)} %shard_map.100.refs_9_.refs_0_), channel_id=1, source_target_pairs={{0,2},{2,0},{1,3},{3,1},{4,6},{6,4},{5,7},{7,5},{8,10},{10,8},{9,1... | collective-permute-start | bytes 2064392 | tf_op jit(solution)/shard_map/ppermute | solution.py:41
  88.8 2.0 %collective-permute-start.19 = (bf16[128,2048]{1,0:T(8,128)(2,1)S(1)}, bf16[128,2048]{1,0:T(8,128)(2,1)S(1)}, u32[]{:S(2)}, u32[]{:S(2)}) collective-permute-start(bf16[128,2048]{1,0:T(8,128)(2,1)S(1)} %get-tuple-element.63), channel_id=1, source_target_pairs={{0,1},{1,0},{2,3},{3,2},{4,5},{5,4},{6,7},{7,6},{8,9},{9,8},{10,11... | collective-permute-start | bytes 1572872 | tf_op jit(solution)/shard_map/ppermute | solution.py:41
  88.9 22.7 %collective-permute-start.16 = (bf16[384,896]{1,0:T(8,128)(2,1)S(1)}, bf16[384,896]{1,0:T(8,128)(2,1)S(1)}, u32[]{:S(2)}, u32[]{:S(2)}) collective-permute-start(bf16[384,896]{1,0:T(8,128)(2,1)S(1)} %shard_map.101.refs_6_.refs_0_), channel_id=1, source_target_pairs={{0,2},{2,0},{1,3},{3,1},{4,6},{6,4},{5,7},{7,5},{8,10},{10,8},{9,1... | collective-permute-start | bytes 2064392 | tf_op jit(solution)/shard_map/ppermute | solution.py:41
  90.9 9.9 %collective-permute-start.20 = (bf16[128,1024]{1,0:T(8,128)(2,1)S(1)}, bf16[128,1024]{1,0:T(8,128)(2,1)S(1)}, u32[]{:S(2)}, u32[]{:S(2)}) collective-permute-start(bf16[128,1024]{1,0:T(8,128)(2,1)S(1)} %get-tuple-element.73), channel_id=1, source_target_pairs={{0,4},{4,0},{8,12},{12,8},{1,5},{5,1},{9,13},{13,9},{2,6},{6,2},{1... | collective-permute-start | bytes 786440 | tf_op jit(solution)/shard_map/ppermute | solution.py:46
  94.3 3.3 %copy-start.2 = (bf16[2048,896]{1,0:T(8,128)(2,1)}, bf16[2048,896]{1,0:T(8,128)(2,1)S(1)}, u32[]{:S(2)}) copy-start(bf16[2048,896]{1,0:T(8,128)(2,1)S(1)} %get-tuple-element.85.refs_4_) | copy-start | bytes 11010052
  100.9 10.7 %collective-permute-start.21 = (bf16[128,512]{1,0:T(8,128)(2,1)S(1)}, bf16[128,512]{1,0:T(8,128)(2,1)S(1)}, u32[]{:S(2)}, u32[]{:S(2)}) collective-permute-start(bf16[128,512]{1,0:T(8,128)(2,1)S(1)} %get-tuple-element.77), channel_id=1, source_target_pairs={{0,8},{4,12},{8,0},{12,4},{1,9},{5,13},{9,1},{13,5},{2,10},{6,14},... | collective-permute-start | bytes 393224 | tf_op jit(solution)/shard_map/ppermute | solution.py:46
  111.6 5.8 %copy-start.3 = (bf16[2048,896]{1,0:T(8,128)(2,1)S(1)}, bf16[2048,896]{1,0:T(8,128)(2,1)}, u32[]{:S(2)}) copy-start(bf16[2048,896]{1,0:T(8,128)(2,1)} %copy-done.2) | copy-start | bytes 11010052
  115.0 1.6 %collective-permute-start.22 = (bf16[64,2048]{1,0:T(8,128)(2,1)S(1)}, bf16[64,2048]{1,0:T(8,128)(2,1)S(1)}, u32[]{:S(2)}, u32[]{:S(2)}) collective-permute-start(bf16[64,2048]{1,0:T(8,128)(2,1)S(1)} %get-tuple-element.79), channel_id=1, source_target_pairs={{0,1},{1,0},{2,3},{3,2},{4,5},{5,4},{6,7},{7,6},{8,9},{9,8},{10,11... | collective-permute-start | bytes 786440 | tf_op jit(solution)/shard_map/ppermute | solution.py:41
  116.7 5.6 %collective-permute-start.23 = (bf16[64,1024]{1,0:T(8,128)(2,1)S(1)}, bf16[64,1024]{1,0:T(8,128)(2,1)S(1)}, u32[]{:S(2)}, u32[]{:S(2)}) collective-permute-start(bf16[64,1024]{1,0:T(8,128)(2,1)S(1)} %get-tuple-element.81), channel_id=1, source_target_pairs={{0,4},{4,0},{8,12},{12,8},{1,5},{5,1},{9,13},{13,9},{2,6},{6,2},{1... | collective-permute-start | bytes 393224 | tf_op jit(solution)/shard_map/ppermute | solution.py:46
  122.3 5.9 %collective-permute-start.24 = (bf16[64,512]{1,0:T(8,128)(2,1)S(1)}, bf16[64,512]{1,0:T(8,128)(2,1)S(1)}, u32[]{:S(2)}, u32[]{:S(2)}) collective-permute-start(bf16[64,512]{1,0:T(8,128)(2,1)S(1)} %get-tuple-element.90), channel_id=1, source_target_pairs={{0,8},{4,12},{8,0},{12,4},{1,9},{5,13},{9,1},{13,5},{2,10},{6,14},... | collective-permute-start | bytes 196616 | tf_op jit(solution)/shard_map/ppermute | solution.py:46
